TPU v7x, 32 devices: a whole 2x2x4 slice. The times are simulated.
32 devices in a mesh: expert: 8 (over y, x, core), tensor: 4 (over z).
Axes of the slice: x: 2, y: 2, z: 4, core: 2. Of those that a mesh axis runs over, the one named last changes fastest.
Arguments:
- tokens: bfloat16 [2048, 7168], P(('expert', 'tensor')), may hold values from -6 to 6
- expert_ids: int32 [2048, 2], P('expert'), may hold values from 0 to 2, all different within a row
- gate_scores: int32 [2048, 2], P('expert'), may hold values from 1 to 64
- gate_weight: bfloat16 [3, 7168, 2048], P(None, ('expert', 'tensor')), may hold values from -0.0625 to 0.0625
- up_weight: bfloat16 [3, 7168, 2048], P(None, ('expert', 'tensor')), may hold values from -0.0625 to 0.0625
- down_weight: bfloat16 [3, 7168, 2048], P(None, ('expert', 'tensor')), may hold values from -0.1875 to 0.1875
Outputs:
- mixed: bfloat16 [2048, 7168], P(('expert', 'tensor'))
Inputs may be any that keep to these rules, and one draw needn't show every extreme that they name: `expert_ids`: each row names 2 different experts.
All inputs are finite; a program needn't handle non-finite values.
Results may differ from a plain program's by a relative error of at most 0.015.
Values may be sent and summed in bfloat16 or wider, within the bound.
No kernel may reach another device: no remote copies, remote signals or barrier semaphores. Data moves between devices by JAX's collectives and lax.ppermute only.
A program may use at most 128 MiB of HBM per device.

v0:
```python
import jax
import jax.numpy as jnp
from jax import lax
from jax.sharding import PartitionSpec as P


def activate(gate_sum, up_sum, weight_col):
    return (jax.nn.silu(gate_sum) * up_sum * weight_col).astype(jnp.bfloat16)


def local(tokens, expert_ids, gate_scores, gate_weight, up_weight, down_weight):
    gathered = lax.all_gather(tokens, "tensor", axis=0, tiled=True)
    experts = gate_weight.shape[0]
    scores = gate_scores.astype(jnp.float32)
    score_sum = jnp.sum(scores, axis=1, keepdims=True)
    labels = jnp.arange(experts, dtype=jnp.int32)
    picked = (expert_ids[:, :, None] == labels[None, None, :]).astype(jnp.float32)
    combine = jnp.sum(scores[:, :, None] * picked, axis=1) / score_sum
    served_gate, served_up, served_down = (
        lax.all_to_all(gate_weight, "tensor", split_axis=2, concat_axis=1, tiled=True),
        lax.all_to_all(up_weight, "tensor", split_axis=2, concat_axis=1, tiled=True),
        lax.all_to_all(down_weight, "tensor", split_axis=2, concat_axis=1, tiled=True),
    )
    hiddens = []
    full_gate, full_up = (
        lax.all_gather(served_gate, "expert", axis=1, tiled=True),
        lax.all_gather(served_up, "expert", axis=1, tiled=True),
    )
    for which in range(experts):
        gate_sum = jnp.dot(gathered, full_gate[which], preferred_element_type=jnp.float32)
        up_sum = jnp.dot(gathered, full_up[which], preferred_element_type=jnp.float32)
        hiddens.append(activate(gate_sum, up_sum, combine[:, which : which + 1]))
    stacked = jnp.stack(hiddens)
    partial_sum = jnp.einsum(
        "etf,edf->td",
        stacked,
        lax.all_gather(served_down, "expert", axis=1, tiled=True),
        preferred_element_type=jnp.float32,
    )
    output_rows = lax.psum_scatter(
        partial_sum.astype(jnp.bfloat16), "tensor", scatter_dimension=0, tiled=True
    )
    return output_rows


def solution(mesh):
    return jax.shard_map(
        local,
        mesh=mesh,
        in_specs=(
            P(("expert", "tensor"), None),
            P("expert", None),
            P("expert", None),
            P(None, ("expert", "tensor"), None),
            P(None, ("expert", "tensor"), None),
            P(None, ("expert", "tensor"), None),
        ),
        out_specs=P(("expert", "tensor"), None),
        check_vma=False,
    )
```

profile of v0, /device:TPU:0, one launch (start us, length us, event | category | flops | bytes accessed | tf_op | source)
XLA Modules:
  0.0 605.2 jit_solution(7890234099564896453)
XLA Ops:
  6.5 0.0 all-gather.5.cloned.1.call-start
  6.5 0.7 all-gather.5.cloned.1.call-update
  7.3 0.0 all-gather.7.cloned.1.call-start
  7.3 7.1 %copy.28 = bf16[3,224,2048]{1,0,2:T(4,128)(2,1)} copy(bf16[3,224,2048]{2,1,0:T(8,128)(2,1)} %param.9) | data formatting | bytes 5505024 | tf_op args[3]
  14.4 158.5 %all_to_all.54 = bf16[3,224,2048]{1,0,2:T(4,128)(2,1)} all-to-all(bf16[3,224,2048]{1,0,2:T(4,128)(2,1)} %copy.28), channel_id=1, replica_groups=mesh['expert'=8,'tensor'=4] {'tensor'}, dimensions={2} | all-to-all | bytes 5505024 | tf_op jit(solution)/shard_map/all_to_all | solution.py:20
  172.9 0.0 copy-start
  172.9 7.2 %copy.30 = bf16[3,4,224,512]{3,2,1,0:T(8,128)(2,1)} copy(bf16[3,4,224,512]{2,0,3,1:T(4,128)(2,1)} %bitcast.76) | data formatting | bytes 5505024 | tf_op jit(solution)/shard_map/all_to_all | solution.py:20
  180.1 0.0 all-gather.7.cloned.1.call-update
  180.1 0.0 all-gather.9.cloned.1.call-start
  180.2 0.0 copy-done
  180.2 4.8 copy.31
  185.0 99.5 %all_to_all.55 = bf16[3,224,2048]{1,0,2:T(4,128)(2,1)} all-to-all(bf16[3,224,2048]{1,0,2:T(4,128)(2,1)} %copy.31), channel_id=1, replica_groups=mesh['expert'=8,'tensor'=4] {'tensor'}, dimensions={2} | all-to-all | bytes 5505024 | tf_op jit(solution)/shard_map/all_to_all | solution.py:21
  284.5 0.0 copy-start.1
  284.5 7.2 %copy.33 = bf16[3,4,224,512]{3,2,1,0:T(8,128)(2,1)} copy(bf16[3,4,224,512]{2,0,3,1:T(4,128)(2,1)} %bitcast.77) | data formatting | bytes 5505024 | tf_op jit(solution)/shard_map/all_to_all | solution.py:21
  291.7 0.0 all-gather.9.cloned.1.call-update
  291.7 0.0 all-gather.11.cloned.1.call-start
  291.7 0.0 copy-done.1
  291.8 4.8 copy.34
  296.6 98.6 %all_to_all.56 = bf16[3,224,2048]{1,0,2:T(4,128)(2,1)} all-to-all(bf16[3,224,2048]{1,0,2:T(4,128)(2,1)} %copy.34), channel_id=1, replica_groups=mesh['expert'=8,'tensor'=4] {'tensor'}, dimensions={2} | all-to-all | bytes 5505024 | tf_op jit(solution)/shard_map/all_to_all | solution.py:22
  395.2 0.0 copy-start.2
  395.2 0.0 copy-start.3
  395.2 7.1 %copy.35 = bf16[3,224,4,512]{3,1,2,0:T(8,128)(2,1)} copy(bf16[3,224,4,512]{1,0,3,2:T(4,128)(2,1)} %bitcast.78) | data formatting | bytes 5505024 | tf_op jit(solution)/shard_map/all_to_all | solution.py:22
  402.3 0.0 all-gather.11.cloned.1.call-update
  402.3 0.2 reduce-scatter.2.cloned.1.call-start
  402.5 0.0 copy-done.2
  402.6 0.0 copy-done.3
  402.6 0.0 all-gather.5.cloned.1.call-done
  402.7 0.0 all-gather.7.cloned.1.call-done
  402.7 0.0 copy-start.4
  402.7 6.4 %fusion.2 = f32[256,512]{1,0:T(8,128)S(1)} fusion(bf16[256,7168]{1,0:T(8,128)(2,1)} %all-gather.5.cloned.1.call-done, bf16[3,7168,512]{2,1,0:T(8,128)(2,1)} %all-gather.7.cloned.1.call-done), kind=kOutput, calls=%fused_computation.5 | convolution fusion | flops 1879048192 | bytes 11534336 | tf_op jit(solution)/shard_map/dot_general | solution.py:30
  409.1 0.0 copy-done.4
  409.1 5.2 fusion.4
  414.3 6.2 %fusion.6 = f32[256,512]{1,0:T(8,128)S(1)} fusion(bf16[256,7168]{1,0:T(8,128)(2,1)S(1)} %copy-done.4, bf16[3,7168,512]{2,1,0:T(8,128)(2,1)} %all-gather.7.cloned.1.call-done), kind=kOutput, calls=%fused_computation.13 | convolution fusion | flops 1879048192 | bytes 11534336 | tf_op jit(solution)/shard_map/dot_general | solution.py:30
  420.6 0.0 all-gather.9.cloned.1.call-done
  420.6 0.0 copy-start.5
  420.6 6.4 %fusion.18 = bf16[1,256,512]{2,1,0:T(8,128)(2,1)S(1)} fusion(bf16[256,7168]{1,0:T(8,128)(2,1)} %all-gather.5.cloned.1.call-done, bf16[3,7168,512]{2,1,0:T(8,128)(2,1)} %all-gather.9.cloned.1.call-done, f32[256,512]{1,0:T(8,128)S(1)} %fusion.2, f32[256]{0:T(256)S(1)} %bitcast.84), kind=kOutput, calls=%fused_computation.25 | convolution fusion | flops 1879965696 | bytes 11797504 | tf_op jit(solution)/shard_map/dot_general | solution.py:31
  427.1 0.0 copy-done.5
  427.1 5.3 fusion.17
  432.3 5.3 fusion.16
  437.6 80.9 %all-gather.11.cloned.1.call-done = bf16[3,7168,512]{2,1,0:T(8,128)(2,1)} async-done(((bf16[3,896,512]{2,1,0:T(8,128)(2,1)}), bf16[3,7168,512]{2,1,0:T(8,128)(2,1)}) %all-gather.11.cloned.1.call-update) | async-done | bytes 22020112 | tf_op jit(solution)/shard_map/all_gather | solution.py:37
  518.6 11.6 %fusion = bf16[256,7168]{1,0:T(8,128)(2,1)} fusion(bf16[3,7168,512]{2,1,0:T(8,128)(2,1)} %all-gather.11.cloned.1.call-done, bf16[1,256,512]{2,1,0:T(8,128)(2,1)S(1)} %fusion.18, bf16[1,256,512]{2,1,0:T(8,128)(2,1)S(1)} %fusion.17, bf16[1,256,512]{2,1,0:T(8,128)(2,1)S(1)} %fusion.16), kind=kOutput, calls=%fused_computation.1 | convolution fusion | flops 5639766016 | bytes 26476544 | tf_op jit(solution)/shard_map/etf,edf->td/dot_general | solution.py:34
  530.1 0.0 reduce-scatter.2.cloned.1.call-update
  530.2 68.6 %reduce-scatter.2.cloned.1.call-done = bf16[64,7168]{1,0:T(8,128)(2,1)} async-done(((bf16[256,7168]{1,0:T(8,128)(2,1)}), bf16[64,7168]{1,0:T(8,128)(2,1)}) %reduce-scatter.2.cloned.1.call-update) | async-done | bytes 917520 | tf_op jit(solution)/shard_map/reduce_scatter | solution.py:40
  (5 shorter events, 0.1 us)
Async XLA Ops:
  6.5 396.1 %all-gather.5.cloned.1.call-start = ((), (), s32[]{:S(2)}) async-start(), calls=%async_computation.4 | async-start | bytes 4587520 | tf_op jit(solution)/shard_map/all_gather | solution.py:12
  7.3 395.4 %all-gather.7.cloned.1.call-start = ((), (), s32[]{:S(2)}) async-start(), calls=%async_computation.5 | async-start | bytes 24772608 | tf_op jit(solution)/shard_map/all_gather | solution.py:26
  172.9 7.2 %copy-start = (bf16[3,224,2048]{2,1,0:T(8,128)(2,1)S(1)}, bf16[3,224,2048]{2,1,0:T(8,128)(2,1)}, u32[]{:S(2)}) copy-start(bf16[3,224,2048]{2,1,0:T(8,128)(2,1)} %param.10) | copy-start | bytes 8257540
  180.1 240.5 %all-gather.9.cloned.1.call-start = ((), (), s32[]{:S(2)}) async-start(), calls=%async_computation.6 | async-start | bytes 24772608 | tf_op jit(solution)/shard_map/all_gather | solution.py:27
  284.5 7.3 %copy-start.1 = (bf16[3,224,2048]{2,1,0:T(8,128)(2,1)S(1)}, bf16[3,224,2048]{2,1,0:T(8,128)(2,1)}, u32[]{:S(2)}) copy-start(bf16[3,224,2048]{2,1,0:T(8,128)(2,1)} %param.11) | copy-start | bytes 8257540
  291.7 226.9 %all-gather.11.cloned.1.call-start = ((), (), s32[]{:S(2)}) async-start(), calls=%async_computation.7 | async-start | bytes 24772608 | tf_op jit(solution)/shard_map/all_gather | solution.py:37
  395.2 7.4 %copy-start.2 = (s32[256,2]{0,1:T(2,128)S(1)}, s32[256,2]{0,1:T(2,128)}, u32[]{:S(2)}) copy-start(s32[256,2]{0,1:T(2,128)} %param.8) | copy-start | bytes 6148
  395.2 7.4 %copy-start.3 = (s32[256,2]{0,1:T(2,128)S(1)}, s32[256,2]{0,1:T(2,128)}, u32[]{:S(2)}) copy-start(s32[256,2]{0,1:T(2,128)} %param.7) | copy-start | bytes 6148
  402.3 196.4 %reduce-scatter.2.cloned.1.call-start = ((), (), s32[]{:S(2)}) async-start(), calls=%async_computation.8 | async-start | bytes 4587520 | tf_op jit(solution)/shard_map/reduce_scatter | solution.py:40
  402.7 6.4 %copy-start.4 = (bf16[256,7168]{1,0:T(8,128)(2,1)S(1)}, bf16[256,7168]{1,0:T(8,128)(2,1)}, u32[]{:S(2)}) copy-start(bf16[256,7168]{1,0:T(8,128)(2,1)} %all-gather.5.cloned.1.call-done) | copy-start | bytes 11010052
  420.6 6.4 %copy-start.5 = (bf16[256,7168]{1,0:T(8,128)(2,1)S(1)}, bf16[256,7168]{1,0:T(8,128)(2,1)}, u32[]{:S(2)}) copy-start(bf16[256,7168]{1,0:T(8,128)(2,1)} %all-gather.5.cloned.1.call-done) | copy-start | bytes 11010052
Sparse Core Ops, SparseCore 0:
  8.9 148.7 all-gather.4
  180.2 110.4 all-gather.6
  292.7 112.0 all-gather.8
  406.5 112.0 all-gather.10
  530.3 68.3 reduce-scatter.1
where the time goes:
time: 606 us; the launch traced here: 605 us
  blocking collectives  357 us (59%)
  waiting for transfers between devices  150 us (25%)
  matrix products  46.4 us (8%)
  local copies, waits for them, and re-layouts  38.2 us (6%)
  between operations  13.3 us (2%)
    all_to_all x1, blocking collectives, local(): lax.all_to_all(gate_weight, 'tensor', split_axis=2, concat_axis=1, tiled=...  159 us
    all_to_all x1, blocking collectives, local(): lax.all_to_all(up_weight, 'tensor', split_axis=2, concat_axis=1, tiled=True)  99.5 us
    all_to_all x1, blocking collectives, local(): lax.all_to_all(down_weight, 'tensor', split_axis=2, concat_axis=1, tiled=...  98.6 us
    all_gather x1, waiting for transfers between devices, local(): lax.all_gather(served_down, 'expert', axis=1, tiled=True)  80.9 us
    reduce_scatter x1, waiting for transfers between devices, local(): lax.psum_scatter(partial_sum.astype(jnp.bfloat16), 'tensor', scatter_dime...  68.6 us
    dot_general x3, matrix products, local(): jnp.dot(gathered, full_gate[which], preferred_element_type=jnp.float32)  17.9 us
    dot_general x3, matrix products, local(): jnp.dot(gathered, full_up[which], preferred_element_type=jnp.float32)  17 us
    unnamed x15, local copies, waits for them, and re-layouts  16.7 us
  transfers between devices with their start and end apart: 5, of which 2 were waited for; matrix products, arithmetic and copies ran while one was open for 12% of the time, Pallas kernels for 0%

commit v1 on v0

v1 whole, which is shorter than its diff:
```python
import jax
import jax.numpy as jnp
from jax import lax
from jax.experimental import pallas as pl
from jax.experimental.pallas import tpu as pltpu
from jax.sharding import PartitionSpec as P

VMEM_BYTES = 48 * 1024 * 1024


def pick_kernel(ids_ref, tok_ref, w_ref, out_ref):
    experts, _, width = w_ref.shape
    tok = tok_ref[...]
    sums = [
        jnp.dot(tok, w_ref[which], preferred_element_type=jnp.float32)
        for which in range(experts)
    ]
    for slot in range(ids_ref.shape[1]):
        chosen = ids_ref[:, slot : slot + 1]
        picked = sums[0]
        for which in range(1, experts):
            picked = jnp.where(chosen == which, sums[which], picked)
        out_ref[:, slot * width : (slot + 1) * width] = picked.astype(out_ref.dtype)


def picked_sums(ids, tok, weight):
    count, depth = tok.shape
    experts, _, width = weight.shape
    slots = ids.shape[1]
    tile = 256
    return pl.pallas_call(
        pick_kernel,
        grid=(count // tile,),
        in_specs=[
            pl.BlockSpec((tile, slots), lambda i: (i, 0)),
            pl.BlockSpec((tile, depth), lambda i: (i, 0)),
            pl.BlockSpec((experts, depth, width), lambda i: (0, 0, 0)),
        ],
        out_specs=pl.BlockSpec((tile, slots * width), lambda i: (i, 0)),
        out_shape=jax.ShapeDtypeStruct((count, slots * width), jnp.bfloat16),
        cost_estimate=pl.CostEstimate(
            flops=2 * count * depth * width * experts,
            bytes_accessed=2 * (count * depth + experts * depth * width + count * slots * width),
            transcendentals=0,
        ),
        compiler_params=pltpu.CompilerParams(vmem_limit_bytes=VMEM_BYTES),
    )(ids, tok, weight)


def down_kernel(ids_ref, hid_ref, w_ref, out_ref):
    experts, _, width = w_ref.shape
    total = None
    for which in range(experts):
        mine = jnp.zeros((hid_ref.shape[0], width), hid_ref.dtype)
        for slot in range(ids_ref.shape[1]):
            part = hid_ref[:, slot * width : (slot + 1) * width]
            mine = jnp.where(ids_ref[:, slot : slot + 1] == which, part, mine)
        term = lax.dot_general(
            mine, w_ref[which], (((1,), (1,)), ((), ())), preferred_element_type=jnp.float32
        )
        total = term if total is None else total + term
    out_ref[...] = total.astype(out_ref.dtype)


def down_sums(ids, hidden, weight):
    count = hidden.shape[0]
    experts, depth, width = weight.shape
    slots = ids.shape[1]
    tile = 256
    return pl.pallas_call(
        down_kernel,
        grid=(count // tile,),
        in_specs=[
            pl.BlockSpec((tile, slots), lambda i: (i, 0)),
            pl.BlockSpec((tile, slots * width), lambda i: (i, 0)),
            pl.BlockSpec((experts, depth, width), lambda i: (0, 0, 0)),
        ],
        out_specs=pl.BlockSpec((tile, depth), lambda i: (i, 0)),
        out_shape=jax.ShapeDtypeStruct((count, depth), jnp.bfloat16),
        cost_estimate=pl.CostEstimate(
            flops=2 * count * depth * width * experts,
            bytes_accessed=2 * (count * depth + experts * depth * width + count * slots * width),
            transcendentals=0,
        ),
        compiler_params=pltpu.CompilerParams(vmem_limit_bytes=VMEM_BYTES),
    )(ids, hidden, weight)


def local(tokens, expert_ids, gate_scores, gate_weight, up_weight, down_weight):
    n_expert, n_tensor = lax.axis_size("expert"), lax.axis_size("tensor")
    rows, model = tokens.shape
    depth = gate_weight.shape[1]
    cut = tokens.reshape(rows, n_expert, n_tensor, depth)
    cut = lax.all_to_all(cut, "tensor", split_axis=2, concat_axis=0, tiled=True)
    tok = lax.all_gather(
        cut.reshape(rows * n_tensor, n_expert * depth), "expert", axis=0, tiled=True
    )
    routing = lax.all_gather(
        jnp.concatenate([expert_ids, gate_scores], axis=1), "expert", axis=0, tiled=True
    )
    slots = expert_ids.shape[1]
    ids, scores = routing[:, :slots], routing[:, slots:].astype(jnp.float32)

    def serve(weight):
        return lax.all_to_all(weight, "expert", split_axis=2, concat_axis=1, tiled=True)

    gate_part = picked_sums(ids, tok, serve(gate_weight))
    gate_sum = lax.psum_scatter(gate_part, "tensor", scatter_dimension=0, tiled=True)
    up_part = picked_sums(ids, tok, serve(up_weight))
    up_sum = lax.psum_scatter(up_part, "tensor", scatter_dimension=0, tiled=True)

    count = gate_sum.shape[0]
    mine = lax.dynamic_slice_in_dim(scores, lax.axis_index("tensor") * count, count, 0)
    combine = mine / jnp.sum(mine, axis=1, keepdims=True)
    width = gate_sum.shape[1] // slots
    combine = jnp.repeat(combine, width, axis=1)
    hidden = (
        jax.nn.silu(gate_sum.astype(jnp.float32)) * up_sum.astype(jnp.float32) * combine
    ).astype(jnp.bfloat16)
    hidden = lax.all_gather(hidden, "tensor", axis=0, tiled=True)

    partial_sum = down_sums(ids, hidden, serve(down_weight))
    mixed = lax.psum_scatter(partial_sum, "expert", scatter_dimension=0, tiled=True)
    mixed = mixed.reshape(rows * n_tensor, n_expert, 1, depth)
    mixed = lax.all_to_all(mixed, "tensor", split_axis=0, concat_axis=2, tiled=True)
    return mixed.reshape(rows, model)


def solution(mesh):
    return jax.shard_map(
        local,
        mesh=mesh,
        in_specs=(
            P(("expert", "tensor"), None),
            P("expert", None),
            P("expert", None),
            P(None, ("expert", "tensor"), None),
            P(None, ("expert", "tensor"), None),
            P(None, ("expert", "tensor"), None),
        ),
        out_specs=P(("expert", "tensor"), None),
        check_vma=False,
    )
```

time: 606 us -> 466 us (0.77)
  blocking collectives: 357 us -> 248 us
  matrix products: 46.4 us -> 0 us
  waiting for transfers between devices: 150 us -> 105 us
  Pallas kernels: 0 us -> 27.4 us
  local copies, waits for them, and re-layouts: 38.2 us -> 60.5 us
    all_to_all x3 -> x4, blocking collectives: 357 us -> 169 us  [the longest x2 107 us: serve(): lax.all_to_all(weight, 'expert', split_axis=2, concat_axis=1, tiled=True)]
    all_gather x4 -> x2, waiting for transfers between devices: 81 us -> 0.04 us  [the longest x1 0.02 us: local(): lax.all_gather(cut.reshape(rows * n_tensor, n_expert * depth), 'expert',...]
    all_gather x0 -> x1, blocking collectives: none -> 79.4 us  [local(): lax.all_gather(jnp.concatenate([expert_ids, gate_scores], axis=1), 'exper...]
    dot_general x7 -> x0, matrix products: 46.4 us -> none  [the longest x3 17.9 us: local(): jnp.dot(gathered, full_gate[which], preferred_element_type=jnp.float32)]
    reduce_scatter x1 -> x3, waiting for transfers between devices: 68.6 us -> 105 us  [the longest x1 64.6 us: local(): lax.psum_scatter(partial_sum, 'expert', scatter_dimension=0, tiled=True)]
    pallas_call x0 -> x3, Pallas kernels: none -> 27.4 us  [the longest x2 18.7 us: picked_sums(): pl.pallas_call(pick_kernel, grid=(count // tile,), in_specs=[pl.BlockSpec...]
    unnamed x15 -> x20, local copies, waits for them, and re-layouts: 16.7 us -> 29.3 us
    reshape x0 -> x5, local copies, waits for them, and re-layouts: none -> 9.53 us  [the longest x2 3.69 us: local(): cut = tokens.reshape(rows, n_expert, n_tensor, depth)]
  transfers between devices with their start and end apart: 5 -> 6, of which waited for: 2 -> 2; matrix products, arithmetic and copies ran while one was open for 12% -> 9% of each run, Pallas kernels for 0% -> 2%
where the time goes in v1:
time: 466 us; the launch traced here: 464 us
  blocking collectives  248 us (53%)
  waiting for transfers between devices  105 us (23%)
  local copies, waits for them, and re-layouts  60.5 us (13%)
  Pallas kernels  27.4 us (6%)
  between operations  13.3 us (3%)
  starting transfers between devices  4.86 us (1%)
    all_to_all x2, blocking collectives, serve(): lax.all_to_all(weight, 'expert', split_axis=2, concat_axis=1, tiled=True)  107 us
    all_gather x1, blocking collectives, local(): lax.all_gather(jnp.concatenate([expert_ids, gate_scores], axis=1), 'exper...  79.4 us
    reduce_scatter x1, waiting for transfers between devices, local(): lax.psum_scatter(partial_sum, 'expert', scatter_dimension=0, tiled=True)  64.6 us
    reduce_scatter x1, waiting for transfers between devices, local(): lax.psum_scatter(up_part, 'tensor', scatter_dimension=0, tiled=True)  40.1 us
    all_to_all x1, blocking collectives, local(): cut = lax.all_to_all(cut, 'tensor', split_axis=2, concat_axis=0, tiled=True)  31.8 us
    all_to_all x1, blocking collectives, local(): lax.all_to_all(mixed, 'tensor', split_axis=0, concat_axis=2, tiled=True)  30.1 us
    unnamed x20, local copies, waits for them, and re-layouts  29.3 us
    pallas_call x2, Pallas kernels, picked_sums(): pl.pallas_call(pick_kernel, grid=(count // tile,), in_specs=[pl.BlockSpec...  18.7 us
  transfers between devices with their start and end apart: 6, of which 2 were waited for; matrix products, arithmetic and copies ran while one was open for 9% of the time, Pallas kernels for 2%

profile of v1, /device:TPU:0, one launch (start us, length us, event | category | flops | bytes accessed | tf_op | source)
XLA Modules:
  0.0 463.9 jit_solution(18441990758760057268)
XLA Ops:
  6.5 3.5 reshape.18
  10.1 0.1 copy.40
  10.2 31.8 %all_to_all.84 = bf16[64,8,4,224]{3,1,0,2:T(8,128)(2,1)S(1)} all-to-all(bf16[64,8,4,224]{3,1,0,2:T(8,128)(2,1)S(1)} %copy.40), channel_id=1, replica_groups=mesh['expert'=8,'tensor'=4] {'tensor'}, dimensions={2} | all-to-all | bytes 1835008 | tf_op jit(solution)/shard_map/all_to_all | solution.py:94
  42.1 2.2 reshape.19
  44.3 0.0 all-gather.3.cloned.1.call-update
  44.3 7.1 %copy.41 = bf16[3,224,2048]{1,0,2:T(4,128)(2,1)} copy(bf16[3,224,2048]{2,1,0:T(8,128)(2,1)} %param.9) | data formatting | bytes 5505024 | tf_op args[3]
  51.5 4.7 %all-to-all-start.1 = ((bf16[3,224,2048]{1,0,2:T(4,128)(2,1)}), bf16[3,224,2048]{1,0,2:T(4,128)(2,1)}, u32[]{:S(2)}, u32[]{:S(2)}) async-start(bf16[3,224,2048]{1,0,2:T(4,128)(2,1)} %copy.41), calls=%async_computation.1 | async-start | bytes 8388608 | tf_op jit(solution)/shard_map/all_to_all | solution.py:105
  56.2 0.0 reduce-scatter.4.cloned.1.call-start
  56.3 0.1 copy.39
  56.4 79.4 %all_gather.9 = s32[2048,4]{1,0:T(8,128)S(1)} all-gather(s32[256,4]{1,0:T(8,128)S(1)} %copy.39), channel_id=1, replica_groups=mesh['expert'=8,'tensor'=4] {'expert'}, dimensions={0}, use_global_device_ids=true | all-gather | bytes 36864 | tf_op jit(solution)/shard_map/all_gather | solution.py:98
  135.8 1.6 fusion.8
  137.4 5.5 %copy.42 = bf16[3,224,8,256]{3,1,2,0:T(8,128)(2,1)S(1)} copy(bf16[3,224,8,256]{1,0,3,2:T(4,128)(2,1)} %bitcast.2) | data formatting | bytes 5505024 | tf_op jit(solution)/shard_map/all_to_all | solution.py:105
  142.9 0.0 all-gather.3.cloned.1.call-done.tok_ref
  143.0 1.2 copy-done.2
  144.2 9.4 %shard_map.64 = bf16[2048,512]{1,0:T(8,128)(2,1)S(1)} custom-call(s32[2048,2]{1,0:T(8,128)S(1)} %copy-done.2, bf16[2048,1792]{1,0:T(8,128)(2,1)} %all-gather.3.cloned.1.call-done.tok_ref, bf16[3,1792,256]{2,1,0:T(8,128)(2,1)S(1)} %bitcast.28), custom_call_target="tpu_custom_call" | custom-call | flops 5637144576 | bytes 12189696 | tf_op jit(solution)/shard_map/pallas_call | solution.py:31
  153.6 1.3 copy-done
  154.8 0.0 reduce-scatter.4.cloned.1.call-update
  154.9 0.0 reduce-scatter.6.cloned.1.call-start
  154.9 7.1 %copy.43 = bf16[3,224,2048]{1,0,2:T(4,128)(2,1)} copy(bf16[3,224,2048]{2,1,0:T(8,128)(2,1)} %param.10) | data formatting | bytes 5505024 | tf_op args[4]
  162.0 53.5 %all_to_all.85 = bf16[3,224,2048]{1,0,2:T(4,128)(2,1)} all-to-all(bf16[3,224,2048]{1,0,2:T(4,128)(2,1)} %copy.43), channel_id=1, replica_groups=mesh['expert'=8,'tensor'=4] {'expert'}, dimensions={2} | all-to-all | bytes 5505024 | tf_op jit(solution)/shard_map/all_to_all | solution.py:105
  215.5 5.5 %copy.44 = bf16[3,224,8,256]{3,1,2,0:T(8,128)(2,1)S(1)} copy(bf16[3,224,8,256]{1,0,3,2:T(4,128)(2,1)} %bitcast.30) | data formatting | bytes 5505024 | tf_op jit(solution)/shard_map/all_to_all | solution.py:105
  221.1 1.2 copy-done.3
  222.3 9.4 %shard_map.65 = bf16[2048,512]{1,0:T(8,128)(2,1)S(1)} custom-call(s32[2048,2]{1,0:T(8,128)S(1)} %copy-done.3, bf16[2048,1792]{1,0:T(8,128)(2,1)} %all-gather.3.cloned.1.call-done.tok_ref, bf16[3,1792,256]{2,1,0:T(8,128)(2,1)S(1)} %bitcast.29), custom_call_target="tpu_custom_call" | custom-call | flops 5637144576 | bytes 12189696 | tf_op jit(solution)/shard_map/pallas_call | solution.py:31
  231.7 1.3 copy-done.1
  233.0 0.0 reduce-scatter.6.cloned.1.call-update
  233.0 0.0 all-gather.5.cloned.1.call-start
  233.1 1.1 fusion.6
  234.2 1.1 fusion.7
  235.3 0.6 broadcast_in_dim.4
  235.9 0.1 copy.50
  236.0 0.0 reduce-scatter.4.cloned.1.call-done
  236.0 40.1 %reduce-scatter.6.cloned.1.call-done = bf16[512,512]{1,0:T(8,128)(2,1)} async-done(((bf16[2048,512]{1,0:T(8,128)(2,1)}), bf16[512,512]{1,0:T(8,128)(2,1)}) %reduce-scatter.6.cloned.1.call-update) | async-done | bytes 524304 | tf_op jit(solution)/shard_map/reduce_scatter | solution.py:110
  276.1 2.3 fusion.5
  278.5 0.0 reduce-scatter.8.cloned.1.call-start
  278.5 7.1 %copy.45 = bf16[3,224,2048]{1,0,2:T(4,128)(2,1)} copy(bf16[3,224,2048]{2,1,0:T(8,128)(2,1)} %param.11) | data formatting | bytes 5505024 | tf_op args[5]
  285.6 53.5 %all_to_all.86 = bf16[3,224,2048]{1,0,2:T(4,128)(2,1)} all-to-all(bf16[3,224,2048]{1,0,2:T(4,128)(2,1)} %copy.45), channel_id=1, replica_groups=mesh['expert'=8,'tensor'=4] {'expert'}, dimensions={2} | all-to-all | bytes 5505024 | tf_op jit(solution)/shard_map/all_to_all | solution.py:105
  339.2 5.5 %copy.46 = bf16[3,224,8,256]{3,1,2,0:T(8,128)(2,1)S(1)} copy(bf16[3,224,8,256]{1,0,3,2:T(4,128)(2,1)} %bitcast.31) | data formatting | bytes 5505024 | tf_op jit(solution)/shard_map/all_to_all | solution.py:105
  344.7 0.0 all-gather.5.cloned.1.call-done.hid_ref
  344.7 1.2 copy-done.4
  345.9 1.6 copy-done.5
  347.5 8.6 %shard_map.66 = bf16[2048,1792]{1,0:T(8,128)(2,1)} custom-call(s32[2048,2]{1,0:T(8,128)S(1)} %copy-done.4, bf16[2048,512]{1,0:T(8,128)(2,1)S(1)} %copy-done.5, bf16[3,1792,256]{2,1,0:T(8,128)(2,1)S(1)} %bitcast.27), custom_call_target="tpu_custom_call" | custom-call | flops 5637144576 | bytes 12189696 | tf_op jit(solution)/shard_map/pallas_call | solution.py:70
  356.2 0.0 reduce-scatter.8.cloned.1.call-update
  356.2 64.6 %reduce-scatter.8.cloned.1.call-done = bf16[256,1792]{1,0:T(8,128)(2,1)} async-done(((bf16[2048,1792]{1,0:T(8,128)(2,1)}), bf16[256,1792]{1,0:T(8,128)(2,1)}) %reduce-scatter.8.cloned.1.call-update) | async-done | bytes 917520 | tf_op jit(solution)/shard_map/reduce_scatter | solution.py:123
  420.8 1.5 copy.47
  422.2 1.0 copy.48
  423.2 30.1 %all_to_all.87 = bf16[256,8,1,224]{3,1,2,0:T(8,128)(2,1)S(1)} all-to-all(bf16[256,8,1,224]{3,1,2,0:T(8,128)(2,1)S(1)} %copy.48), channel_id=1, replica_groups=mesh['expert'=8,'tensor'=4] {'tensor'}, dimensions={0} | all-to-all | bytes 1835008 | tf_op jit(solution)/shard_map/all_to_all | solution.py:125
  453.4 1.4 copy.49
  454.7 2.6 reshape.22
  (14 shorter events, 0.0 us)
Async XLA Ops:
  6.5 136.4 %all-gather.3.cloned.1.call-start = ((), (), s32[]{:S(2)}) async-start(), calls=%async_computation.8 | async-start | bytes 8257536 | tf_op jit(solution)/shard_map/all_gather | solution.py:95
  51.5 4.8 %copy-start.6 = (s32[256,2]{0,1:T(2,128)S(1)}, s32[256,2]{0,1:T(2,128)}, u32[]{:S(2)}) copy-start(s32[256,2]{0,1:T(2,128)} %param.8) | copy-start | bytes 6148
  51.5 4.8 %copy-start.7 = (s32[256,2]{0,1:T(2,128)S(1)}, s32[256,2]{0,1:T(2,128)}, u32[]{:S(2)}) copy-start(s32[256,2]{0,1:T(2,128)} %param.7) | copy-start | bytes 6148
  51.5 85.9 %all-to-all-start.1 = ((bf16[3,224,2048]{1,0,2:T(4,128)(2,1)}), bf16[3,224,2048]{1,0,2:T(4,128)(2,1)}, u32[]{:S(2)}, u32[]{:S(2)}) async-start(bf16[3,224,2048]{1,0,2:T(4,128)(2,1)} %copy.41), calls=%async_computation.1 | async-start | bytes 8388608 | tf_op jit(solution)/shard_map/all_to_all | solution.py:105
  56.2 179.8 %reduce-scatter.4.cloned.1.call-start = ((), (), s32[]{:S(2)}) async-start(), calls=%async_computation.9 | async-start | bytes 2621440 | tf_op jit(solution)/shard_map/reduce_scatter | solution.py:108
  142.9 1.2 copy-start.2
  153.5 1.3 copy-start
  154.9 121.2 %reduce-scatter.6.cloned.1.call-start = ((), (), s32[]{:S(2)}) async-start(), calls=%async_computation.10 | async-start | bytes 2621440 | tf_op jit(solution)/shard_map/reduce_scatter | solution.py:110
  221.1 1.2 copy-start.3
  231.7 1.3 copy-start.1
  233.0 111.7 %all-gather.5.cloned.1.call-start = ((), (), s32[]{:S(2)}) async-start(), calls=%async_computation.11 | async-start | bytes 2621440 | tf_op jit(solution)/shard_map/all_gather | solution.py:120
  278.5 142.3 %reduce-scatter.8.cloned.1.call-start = ((), (), s32[]{:S(2)}) async-start(), calls=%async_computation.12 | async-start | bytes 8257536 | tf_op jit(solution)/shard_map/reduce_scatter | solution.py:123
  344.7 1.2 copy-start.4
  345.9 1.6 copy-start.5
Sparse Core Ops, SparseCore 0:
  44.4 87.7 all-gather.2
  155.0 43.8 reduce-scatter.3
  233.1 42.9 reduce-scatter.5
  278.6 45.2 all-gather.4
  356.3 64.4 reduce-scatter.7

commit v2 on v1

v2 whole, which is shorter than its diff:
```python
import functools

import jax
import jax.numpy as jnp
from jax import lax
from jax.experimental import pallas as pl
from jax.experimental.pallas import tpu as pltpu
from jax.sharding import PartitionSpec as P

VMEM_BYTES = 48 * 1024 * 1024
CORES = 2


def fill(place_ref, own_ref, pieces, held, sems):
    experts, depth, _ = own_ref.shape
    width = held.shape[2]
    q, c = place_ref[0], place_ref[1]
    chips = len(pieces) // CORES
    copies = []
    for index in range(CORES * chips):
        side, step = index // chips, index % chips
        source = own_ref.at[:, :, pl.ds(pl.multiple_of(q * width, width), width)]
        if index > 0:
            source = pieces[index]
        block = jnp.bitwise_xor(q, step) * CORES + jnp.bitwise_xor(c, side)
        target = held.at[:, pl.ds(pl.multiple_of(block * depth, 16), depth), :]
        copies.append(pltpu.make_async_copy(source, target, sems.at[index]))
    for copy in copies:
        copy.start()
    for copy in copies:
        copy.wait()


def pick_kernel(count, place_ref, ids_ref, tok_ref, own_ref, *refs):
    pieces, (out_ref, held, sems) = (None,) + refs[: count - 1], refs[count - 1 :]

    @pl.when(pl.program_id(0) == 0)
    def _():
        fill(place_ref, own_ref, pieces, held, sems)

    experts, _, width = held.shape
    tok = tok_ref[...]
    sums = [
        jnp.dot(tok, held[which], preferred_element_type=jnp.float32)
        for which in range(experts)
    ]
    for slot in range(ids_ref.shape[1]):
        chosen = ids_ref[:, slot : slot + 1]
        picked = sums[0]
        for which in range(1, experts):
            picked = jnp.where(chosen == which, sums[which], picked)
        out_ref[:, slot * width : (slot + 1) * width] = picked.astype(out_ref.dtype)


def down_kernel(count, place_ref, ids_ref, hid_ref, own_ref, *refs):
    pieces, (out_ref, held, sems) = (None,) + refs[: count - 1], refs[count - 1 :]

    @pl.when(pl.program_id(0) == 0)
    def _():
        fill(place_ref, own_ref, pieces, held, sems)

    experts, _, width = held.shape
    total = None
    for which in range(experts):
        mine = jnp.zeros((hid_ref.shape[0], width), hid_ref.dtype)
        for slot in range(ids_ref.shape[1]):
            part = hid_ref[:, slot * width : (slot + 1) * width]
            mine = jnp.where(ids_ref[:, slot : slot + 1] == which, part, mine)
        term = lax.dot_general(
            mine, held[which], (((1,), (1,)), ((), ())), preferred_element_type=jnp.float32
        )
        total = term if total is None else total + term
    out_ref[...] = total.astype(out_ref.dtype)


def multiply(kernel, place, ids, left, own, pieces, out_width, width):
    count, slots = ids.shape
    experts, depth, _ = own.shape
    blocks = len(pieces) + 1
    tile = 256
    return pl.pallas_call(
        functools.partial(kernel, blocks),
        grid=(count // tile,),
        in_specs=[
            pl.BlockSpec(memory_space=pltpu.SMEM),
            pl.BlockSpec((tile, slots), lambda i: (i, 0)),
            pl.BlockSpec((tile, left.shape[1]), lambda i: (i, 0)),
        ]
        + [pl.BlockSpec(memory_space=pl.ANY)] * blocks,
        out_specs=pl.BlockSpec((tile, out_width), lambda i: (i, 0)),
        out_shape=jax.ShapeDtypeStruct((count, out_width), jnp.bfloat16),
        scratch_shapes=[
            pltpu.VMEM((experts, blocks * depth, width), jnp.bfloat16),
            pltpu.SemaphoreType.DMA((blocks,)),
        ],
        cost_estimate=pl.CostEstimate(
            flops=2 * count * blocks * depth * width * experts,
            bytes_accessed=2 * (left.size + experts * blocks * depth * width + count * out_width),
            transcendentals=0,
        ),
        compiler_params=pltpu.CompilerParams(vmem_limit_bytes=VMEM_BYTES),
    )(place, ids, left, own, *pieces)


def local(tokens, expert_ids, gate_scores, gate_weight, up_weight, down_weight):
    n_expert, n_tensor = lax.axis_size("expert"), lax.axis_size("tensor")
    chips = n_expert // CORES
    rows, model = tokens.shape
    experts, depth, units = gate_weight.shape
    slots = expert_ids.shape[1]
    width = units // chips
    spot, level = lax.axis_index("expert"), lax.axis_index("tensor")
    q, c = spot // CORES, spot % CORES
    place = jnp.stack([q, c])

    def to_chip(value, step):
        pairs = [(s, s ^ (step * CORES)) for s in range(n_expert)]
        return lax.ppermute(value, "expert", pairs)

    def to_core(value):
        return lax.ppermute(value, "expert", [(s, s ^ 1) for s in range(n_expert)])

    def to_level(value, step):
        return lax.ppermute(value, "tensor", [(s, s ^ step) for s in range(n_tensor)])

    def serve(weight):
        def block(step):
            return lax.dynamic_slice_in_dim(weight, (q ^ step) * width, width, 2)

        same = [to_chip(block(step), step) for step in range(1, chips)]
        other = [to_core(value) for value in [block(0)] + same]
        return same + other

    cut = tokens.reshape(rows, n_expert, n_tensor, depth).transpose(2, 0, 1, 3)
    cut = cut.reshape(n_tensor, rows, n_expert * depth)

    def level_piece(step):
        return lax.dynamic_index_in_dim(cut, level ^ step, 0, keepdims=False)

    got = [level_piece(0)] + [to_level(level_piece(s), s) for s in range(1, n_tensor)]
    group = jnp.zeros((n_tensor, rows, n_expert * depth), tokens.dtype)
    for step, value in enumerate(got):
        group = lax.dynamic_update_index_in_dim(group, value, level ^ step, 0)
    group = group.reshape(n_tensor * rows, n_expert * depth)
    tok = jnp.concatenate([group] + [to_chip(group, s) for s in range(1, chips)])
    routing = jnp.concatenate([expert_ids, gate_scores], axis=1)
    routing = jnp.concatenate([routing] + [to_chip(routing, s) for s in range(1, chips)])
    ids, scores = routing[:, :slots], routing[:, slots:].astype(jnp.float32)

    gate_pieces = serve(gate_weight)
    tok, up_weight = lax.optimization_barrier((tok, up_weight))
    up_pieces = serve(up_weight)
    up_pieces, down_weight = lax.optimization_barrier((up_pieces, down_weight))
    down_pieces = serve(down_weight)

    def picked_sums(weight, pieces):
        part = multiply(pick_kernel, place, ids, tok, weight, pieces, slots * width, width)
        return lax.psum_scatter(part, "tensor", scatter_dimension=0, tiled=True)

    gate_sum = picked_sums(gate_weight, gate_pieces)
    up_sum = picked_sums(up_weight, up_pieces)

    count = gate_sum.shape[0]
    mine = lax.dynamic_slice_in_dim(scores, level * count, count, 0)
    combine = mine / jnp.sum(mine, axis=1, keepdims=True)
    combine = jnp.repeat(combine, width, axis=1)
    hidden = (
        jax.nn.silu(gate_sum.astype(jnp.float32)) * up_sum.astype(jnp.float32) * combine
    ).astype(jnp.bfloat16)
    hidden = lax.all_gather(hidden, "tensor", axis=0, tiled=True)

    part = multiply(
        down_kernel, place, ids, hidden, down_weight, down_pieces, n_expert * depth, width
    )
    part = part.reshape(chips, n_tensor * rows, n_expert * depth)
    total = part[0].astype(jnp.float32)
    for step in range(1, chips):
        total = total + to_chip(part[step], step).astype(jnp.float32)
    total = total.astype(jnp.bfloat16).reshape(n_tensor, rows, n_expert, depth)

    def row_piece(step):
        return lax.dynamic_index_in_dim(total, level ^ step, 0, keepdims=False)

    back = [row_piece(0)] + [to_level(row_piece(s), s) for s in range(1, n_tensor)]
    mixed = jnp.zeros((n_tensor, rows, n_expert, depth), tokens.dtype)
    for step, value in enumerate(back):
        mixed = lax.dynamic_update_index_in_dim(mixed, value, level ^ step, 0)
    return mixed.transpose(1, 2, 0, 3).reshape(rows, model)


def solution(mesh):
    return jax.shard_map(
        local,
        mesh=mesh,
        in_specs=(
            P(("expert", "tensor"), None),
            P("expert", None),
            P("expert", None),
            P(None, ("expert", "tensor"), None),
            P(None, ("expert", "tensor"), None),
            P(None, ("expert", "tensor"), None),
        ),
        out_specs=P(("expert", "tensor"), None),
        check_vma=False,
    )
```

time: 466 us -> 380 us (0.82)
  blocking collectives: 248 us -> 0 us
  waiting for transfers between devices: 105 us -> 242 us
  starting transfers between devices: 4.86 us -> 34.7 us
  local copies, waits for them, and re-layouts: 60.5 us -> 51 us
    ppermute x0 -> x36, waiting for transfers between devices: none -> 192 us  [the longest x18 161 us: to_chip(): return lax.ppermute(value, 'expert', pairs)]
    all_to_all x4 -> x0, blocking collectives: 169 us -> none  [the longest x2 107 us: serve(): lax.all_to_all(weight, 'expert', split_axis=2, concat_axis=1, tiled=True)]
    all_gather x1 -> x0, blocking collectives: 79.4 us -> none  [local(): lax.all_gather(jnp.concatenate([expert_ids, gate_scores], axis=1), 'exper...]
    reduce_scatter x3 -> x2, waiting for transfers between devices: 105 us -> 43.9 us  [picked_sums(): return lax.psum_scatter(part, 'tensor', scatter_dimension=0, tiled=True)]
    ppermute x0 -> x36, starting transfers between devices: none -> 34.5 us  [the longest x18 22.4 us: to_chip(): return lax.ppermute(value, 'expert', pairs)]
    unnamed x20 -> x18, local copies, waits for them, and re-layouts: 29.3 us -> 6.29 us
    dynamic_update_slice x0 -> x7, local copies, waits for them, and re-layouts: none -> 23 us  [the longest x4 20.9 us: local(): mixed = lax.dynamic_update_index_in_dim(mixed, value, level ^ step, 0)]
    all_to_all x4 -> x0, local copies, waits for them, and re-layouts: 17.9 us -> none  [the longest x3 16.5 us: serve(): lax.all_to_all(weight, 'expert', split_axis=2, concat_axis=1, tiled=True)]
  transfers between devices with their start and end apart: 6 -> 39, of which waited for: 2 -> 20; matrix products, arithmetic and copies ran while one was open for 9% -> 4% of each run, Pallas kernels for 2% -> 3%
where the time goes in v2:
time: 380 us; the launch traced here: 379 us
  waiting for transfers between devices  242 us (64%)
  local copies, waits for them, and re-layouts  51 us (13%)
  starting transfers between devices  34.7 us (9%)
  Pallas kernels  30.4 us (8%)
  between operations  13.4 us (4%)
  other arithmetic  7.63 us (2%)
    ppermute x18, waiting for transfers between devices, to_chip(): return lax.ppermute(value, 'expert', pairs)  161 us
    reduce_scatter x2, waiting for transfers between devices, picked_sums(): return lax.psum_scatter(part, 'tensor', scatter_dimension=0, tiled=True)  43.9 us
    pallas_call x3, Pallas kernels, multiply(): pl.pallas_call(functools.partial(kernel, blocks), grid=(count // tile,),...  30.4 us
    ppermute x6, waiting for transfers between devices, to_level(): lax.ppermute(value, 'tensor', [(s, s ^ step) for s in range(n_tensor)])  26.5 us
    ppermute x18, starting transfers between devices, to_chip(): return lax.ppermute(value, 'expert', pairs)  22.4 us
    dynamic_update_slice x4, local copies, waits for them, and re-layouts, local(): mixed = lax.dynamic_update_index_in_dim(mixed, value, level ^ step, 0)  20.9 us
    ppermute x6, starting transfers between devices, to_level(): lax.ppermute(value, 'tensor', [(s, s ^ step) for s in range(n_tensor)])  10.1 us
  transfers between devices with their start and end apart: 39, of which 20 were waited for; matrix products, arithmetic and copies ran while one was open for 4% of the time, Pallas kernels for 3%

profile of v2, /device:TPU:0, one launch (start us, length us, event | category | flops | bytes accessed | tf_op | source)
XLA Modules:
  0.0 378.9 jit_solution(5556168801192020998)
XLA Ops:
  6.5 3.5 reshape.28
  10.2 1.3 reshape.29
  13.3 3.0 collective-permute-start.3
  16.3 2.6 collective-permute-start.4
  18.9 3.0 constant_dynamic-slice_fusion.9
  22.0 1.7 collective-permute-start.9
  23.7 2.4 collective-permute-done.3
  26.8 8.8 %collective-permute-done.4 = bf16[64,1792]{1,0:T(8,128)(2,1)S(1)} collective-permute-done((bf16[64,1792]{1,0:T(8,128)(2,1)S(1)}, bf16[64,1792]{1,0:T(8,128)(2,1)S(1)}, u32[]{:S(2)}, u32[]{:S(2)}) %collective-permute-start.4) | collective-permute-done | bytes 229408 | tf_op jit(solution)/shard_map/ppermute | solution.py:124
  37.0 1.5 collective-permute-start.6
  38.5 1.5 collective-permute-start.7
  41.1 17.3 %collective-permute-done = s32[256,4]{0,1:T(4,128)S(1)} collective-permute-done((s32[256,4]{0,1:T(4,128)S(1)}, s32[256,4]{0,1:T(4,128)S(1)}, u32[]{:S(2)}, u32[]{:S(2)}) %collective-permute-start) | collective-permute-done | bytes 4128 | tf_op jit(solution)/shard_map/ppermute | solution.py:118
  58.4 2.4 collective-permute-start.2
  61.3 1.6 collective-permute-done.2
  63.0 2.4 collective-permute-start.11
  66.0 44.2 %collective-permute-done.10.refs_1_ = bf16[3,224,512]{2,1,0:T(8,128)(2,1)S(1)} collective-permute-done((bf16[3,224,512]{2,1,0:T(8,128)(2,1)S(1)}, bf16[3,224,512]{2,1,0:T(8,128)(2,1)S(1)}, u32[]{:S(2)}, u32[]{:S(2)}) %collective-permute-start.10) | collective-permute-done | bytes 688160 | tf_op jit(solution)/shard_map/ppermute | solution.py:118
  111.5 3.4 pad_maximum_fusion.tok_ref
  115.5 10.5 %shard_map.64 = bf16[1024,1024]{1,0:T(8,128)(2,1)} custom-call(s32[2]{0:T(128)S(1)} %pad_add_fusion.2.place_ref, s32[1024,2]{1,0:T(8,128)S(1)} %copy.25.ids_ref, bf16[1024,1792]{1,0:T(8,128)(2,1)} %pad_maximum_fusion.tok_ref, bf16[3,224,2048]{2,1,0:T(8,128)(2,1)} %own_ref.1, bf16[3,224,512]{2,1,0:T(8,128)(2,1)S(1)} %collective-permute-done.9.refs_0_, ...), custom_call_target="tpu_custom_call" | custom-call | flops 5637144576 | bytes 11272192 | tf_op jit(solution)/shard_map/pallas_call | solution.py:81
  126.1 1.9 constant_dynamic-slice_fusion.5
  129.1 2.4 collective-permute-start.18
  131.5 14.8 %collective-permute-done.16.refs_0_ = bf16[3,224,512]{2,1,0:T(8,128)(2,1)S(1)} collective-permute-done((bf16[3,224,512]{2,1,0:T(8,128)(2,1)S(1)}, bf16[3,224,512]{2,1,0:T(8,128)(2,1)S(1)}, u32[]{:S(2)}, u32[]{:S(2)}) %collective-permute-start.16) | collective-permute-done | bytes 688160 | tf_op jit(solution)/shard_map/ppermute | solution.py:118
  146.3 14.2 %collective-permute-done.17.refs_1_ = bf16[3,224,512]{2,1,0:T(8,128)(2,1)S(1)} collective-permute-done((bf16[3,224,512]{2,1,0:T(8,128)(2,1)S(1)}, bf16[3,224,512]{2,1,0:T(8,128)(2,1)S(1)}, u32[]{:S(2)}, u32[]{:S(2)}) %collective-permute-start.17) | collective-permute-done | bytes 688160 | tf_op jit(solution)/shard_map/ppermute | solution.py:118
  161.1 1.6 collective-permute-done.21.refs_5_
  163.7 9.8 %shard_map.65 = bf16[1024,1024]{1,0:T(8,128)(2,1)} custom-call(s32[2]{0:T(128)S(1)} %pad_add_fusion.2.place_ref, s32[1024,2]{1,0:T(8,128)S(1)} %copy.25.ids_ref, bf16[1024,1792]{1,0:T(8,128)(2,1)} %pad_maximum_fusion.tok_ref, bf16[3,224,2048]{2,1,0:T(8,128)(2,1)} %own_ref.2, bf16[3,224,512]{2,1,0:T(8,128)(2,1)S(1)} %collective-permute-done.16.refs_0_, ...), custom_call_target="tpu_custom_call" | custom-call | flops 5637144576 | bytes 11272192 | tf_op jit(solution)/shard_map/pallas_call | solution.py:81
  174.5 43.9 %reduce-scatter.5.cloned.1.call-done = bf16[256,1024]{1,0:T(8,128)(2,1)} async-done(((bf16[1024,1024]{1,0:T(8,128)(2,1)}), bf16[256,1024]{1,0:T(8,128)(2,1)}) %reduce-scatter.5.cloned.1.call-update) | async-done | bytes 524304 | tf_op jit(solution)/shard_map/reduce_scatter | solution.py:158
  218.4 2.4 fusion.5
  220.8 2.1 constant_dynamic-slice_fusion
  222.9 1.5 collective-permute-start.23
  224.4 1.5 collective-permute-start.24
  226.5 14.9 %collective-permute-done.23.refs_0_ = bf16[3,224,512]{2,1,0:T(8,128)(2,1)S(1)} collective-permute-done((bf16[3,224,512]{2,1,0:T(8,128)(2,1)S(1)}, bf16[3,224,512]{2,1,0:T(8,128)(2,1)S(1)}, u32[]{:S(2)}, u32[]{:S(2)}) %collective-permute-start.23) | collective-permute-done | bytes 688160 | tf_op jit(solution)/shard_map/ppermute | solution.py:118
  241.3 14.6 %collective-permute-done.24.refs_1_ = bf16[3,224,512]{2,1,0:T(8,128)(2,1)S(1)} collective-permute-done((bf16[3,224,512]{2,1,0:T(8,128)(2,1)S(1)}, bf16[3,224,512]{2,1,0:T(8,128)(2,1)S(1)}, u32[]{:S(2)}, u32[]{:S(2)}) %collective-permute-start.24) | collective-permute-done | bytes 688160 | tf_op jit(solution)/shard_map/ppermute | solution.py:118
  259.9 6.3 %all-gather.2.cloned.1.call-done.hid_ref = bf16[1024,1024]{1,0:T(8,128)(2,1)} async-done(((bf16[256,1024]{1,0:T(8,128)(2,1)}), bf16[1024,1024]{1,0:T(8,128)(2,1)}) %all-gather.2.cloned.1.call-update) | async-done | bytes 2097168 | tf_op jit(solution)/shard_map/all_gather | solution.py:170
  269.5 10.0 %shard_map.66 = bf16[1024,1792]{1,0:T(8,128)(2,1)} custom-call(s32[2]{0:T(128)S(1)} %pad_add_fusion.2.place_ref, s32[1024,2]{1,0:T(8,128)S(1)} %copy.25.ids_ref, bf16[1024,1024]{1,0:T(8,128)(2,1)} %all-gather.2.cloned.1.call-done.hid_ref, bf16[3,224,2048]{2,1,0:T(8,128)(2,1)} %own_ref.3, bf16[3,224,512]{2,1,0:T(8,128)(2,1)S(1)} %collective-permute-done.23.refs_0_, ...), custom_call_target="tpu_custom_call" | custom-call | flops 5637144576 | bytes 11272192 | tf_op jit(solution)/shard_map/pallas_call | solution.py:81
  279.6 1.9 fusion.9
  281.5 1.5 collective-permute-start.30
  283.0 1.5 collective-permute-start.31
  285.0 19.8 %collective-permute-done.30 = bf16[256,1792]{1,0:T(8,128)(2,1)S(1)} collective-permute-done((bf16[256,1792]{1,0:T(8,128)(2,1)S(1)}, bf16[256,1792]{1,0:T(8,128)(2,1)S(1)}, u32[]{:S(2)}, u32[]{:S(2)}) %collective-permute-start.30) | collective-permute-done | bytes 917536 | tf_op jit(solution)/shard_map/ppermute | solution.py:118
  304.8 19.7 %collective-permute-done.31 = bf16[256,1792]{1,0:T(8,128)(2,1)S(1)} collective-permute-done((bf16[256,1792]{1,0:T(8,128)(2,1)S(1)}, bf16[256,1792]{1,0:T(8,128)(2,1)S(1)}, u32[]{:S(2)}, u32[]{:S(2)}) %collective-permute-start.31) | collective-permute-done | bytes 917536 | tf_op jit(solution)/shard_map/ppermute | solution.py:118
  324.5 1.7 add_convert_fusion
  326.2 1.5 reshape.32
  328.0 1.9 collective-permute-start.34
  329.9 2.5 collective-permute-start.35
  332.3 1.4 copy.21
  333.7 5.8 %collective-permute-done.33 = bf16[64,8,224]{2,1,0:T(8,128)(2,1)S(1)} collective-permute-done((bf16[64,8,224]{2,1,0:T(8,128)(2,1)S(1)}, bf16[64,8,224]{2,1,0:T(8,128)(2,1)S(1)}, u32[]{:S(2)}, u32[]{:S(2)}) %collective-permute-start.33) | collective-permute-done | bytes 229408 | tf_op jit(solution)/shard_map/ppermute | solution.py:124
  339.9 9.5 %collective-permute-done.34 = bf16[64,8,224]{2,1,0:T(8,128)(2,1)S(1)} collective-permute-done((bf16[64,8,224]{2,1,0:T(8,128)(2,1)S(1)}, bf16[64,8,224]{2,1,0:T(8,128)(2,1)S(1)}, u32[]{:S(2)}, u32[]{:S(2)}) %collective-permute-start.34) | collective-permute-done | bytes 229408 | tf_op jit(solution)/shard_map/ppermute | solution.py:124
  350.3 6.5 %dynamic_update_slice.31 = bf16[4,64,8,224]{3,0,2,1:T(4,128)(2,1)S(1)} dynamic-update-slice(bf16[4,64,8,224]{3,0,2,1:T(4,128)(2,1)S(1)} %copy.21, bf16[1,64,8,224]{3,0,2,1:T(2,128)(2,1)S(1)} %copy.22, s32[]{:T(128)S(6)} %select_n.65, s32[]{:T(128)} %constant.82.clone.1, s32[]{:T(128)} %constant.82.clone.1, s32[]{:T(128)} %constant.82.clone.1) | dynamic-update-slice | bytes 458756 | tf_op jit(solution)/shard_map/jit(dynamic_update_index_in_dim)/dynamic_update_slice | solution.py:187
  356.8 6.5 %dynamic_update_slice.32 = bf16[4,64,8,224]{3,0,2,1:T(4,128)(2,1)S(1)} dynamic-update-slice(bf16[4,64,8,224]{3,0,2,1:T(4,128)(2,1)S(1)} %dynamic_update_slice.31, bf16[1,64,8,224]{3,0,2,1:T(2,128)(2,1)S(1)} %copy.23, s32[]{:T(128)S(6)} %select_n.66, s32[]{:T(128)} %constant.82.clone.1, s32[]{:T(128)} %constant.82.clone.1, s32[]{:T(128)} %constant.82.clone.1) | dynamic-update-slice | bytes 458756 | tf_op jit(solution)/shard_map/jit(dynamic_update_index_in_dim)/dynamic_update_slice | solution.py:187
  363.3 6.5 %dynamic_update_slice.33 = bf16[4,64,8,224]{3,0,2,1:T(4,128)(2,1)S(1)} dynamic-update-slice(bf16[4,64,8,224]{3,0,2,1:T(4,128)(2,1)S(1)} %dynamic_update_slice.32, bf16[1,64,8,224]{3,0,2,1:T(2,128)(2,1)S(1)} %copy.24, s32[]{:T(128)S(6)} %select_n.67, s32[]{:T(128)} %constant.82.clone.1, s32[]{:T(128)} %constant.82.clone.1, s32[]{:T(128)} %constant.82.clone.1) | dynamic-update-slice | bytes 458756 | tf_op jit(solution)/shard_map/jit(dynamic_update_index_in_dim)/dynamic_update_slice | solution.py:187
  369.8 2.6 reshape.33
  (88 shorter events, 21.5 us)
Async XLA Ops:
  6.5 168.0 %reduce-scatter.3.cloned.1.call-start = ((), (), s32[]{:S(2)}) async-start(), calls=%async_computation.2 | async-start | bytes 2621440 | tf_op jit(solution)/shard_map/reduce_scatter | solution.py:158
  13.3 26.7 %copy-start.6 = (s32[256,2]{0,1:T(2,128)S(1)}, s32[256,2]{0,1:T(2,128)}, u32[]{:S(2)}) copy-start(s32[256,2]{0,1:T(2,128)} %param.8) | copy-start | bytes 6148
  13.3 26.7 %copy-start.7 = (s32[256,2]{0,1:T(2,128)S(1)}, s32[256,2]{0,1:T(2,128)}, u32[]{:S(2)}) copy-start(s32[256,2]{0,1:T(2,128)} %param.7) | copy-start | bytes 6148
  13.3 12.8 %collective-permute-start.3 = (bf16[64,1792]{1,0:T(8,128)(2,1)S(1)}, bf16[64,1792]{1,0:T(8,128)(2,1)S(1)}, u32[]{:S(2)}, u32[]{:S(2)}) collective-permute-start(bf16[64,1792]{1,0:T(8,128)(2,1)S(1)} %get-tuple-element.46), channel_id=1, source_target_pairs={{0,1},{1,0},{2,3},{3,2},{4,5},{5,4},{6,7},{7,6},{8,9},{9,8},{10,11... | collective-permute-start | bytes 688136 | tf_op jit(solution)/shard_map/ppermute | solution.py:124
  16.3 19.3 %collective-permute-start.4 = (bf16[64,1792]{1,0:T(8,128)(2,1)S(1)}, bf16[64,1792]{1,0:T(8,128)(2,1)S(1)}, u32[]{:S(2)}, u32[]{:S(2)}) collective-permute-start(bf16[64,1792]{1,0:T(8,128)(2,1)S(1)} %get-tuple-element.45), channel_id=1, source_target_pairs={{0,2},{1,3},{2,0},{3,1},{4,6},{5,7},{6,4},{7,5},{8,10},{9,11},{10,... | collective-permute-start | bytes 688136 | tf_op jit(solution)/shard_map/ppermute | solution.py:124
  18.9 17.4 %collective-permute-start.5 = (bf16[64,1792]{1,0:T(8,128)(2,1)S(1)}, bf16[64,1792]{1,0:T(8,128)(2,1)S(1)}, u32[]{:S(2)}, u32[]{:S(2)}) collective-permute-start(bf16[64,1792]{1,0:T(8,128)(2,1)S(1)} %get-tuple-element.44), channel_id=1, source_target_pairs={{0,3},{1,2},{2,1},{3,0},{4,7},{5,6},{6,5},{7,4},{8,11},{9,10},{10,... | collective-permute-start | bytes 688136 | tf_op jit(solution)/shard_map/ppermute | solution.py:124
  22.0 43.5 %collective-permute-start.9 = (bf16[3,224,512]{2,1,0:T(8,128)(2,1)S(1)}, bf16[3,224,512]{2,1,0:T(8,128)(2,1)S(1)}, u32[]{:S(2)}, u32[]{:S(2)}) collective-permute-start(bf16[3,224,512]{2,1,0:T(8,128)(2,1)S(1)} %get-tuple-element.35), channel_id=1, source_target_pairs={{0,8},{4,12},{8,0},{12,4},{16,24},{20,28},{24,16},{28,20},{1,9},{5... | collective-permute-start | bytes 2064392 | tf_op jit(solution)/shard_map/ppermute | solution.py:118
  37.0 73.8 %collective-permute-start.6 = (bf16[256,1792]{1,0:T(8,128)(2,1)}, bf16[256,1792]{1,0:T(8,128)(2,1)}, u32[]{:S(2)}, u32[]{:S(2)}) collective-permute-start(bf16[256,1792]{1,0:T(8,128)(2,1)} %bitcast.9), channel_id=1, source_target_pairs={{0,8},{4,12},{8,0},{12,4},{16,24},{20,28},{24,16},{28,20},{1,9},{5... | collective-permute-start | bytes 2752520 | tf_op jit(solution)/shard_map/ppermute | solution.py:118
  38.5 72.3 %collective-permute-start.7 = (bf16[256,1792]{1,0:T(8,128)(2,1)}, bf16[256,1792]{1,0:T(8,128)(2,1)}, u32[]{:S(2)}, u32[]{:S(2)}) collective-permute-start(bf16[256,1792]{1,0:T(8,128)(2,1)} %bitcast.9), channel_id=1, source_target_pairs={{0,16},{4,20},{8,24},{12,28},{16,0},{20,4},{24,8},{28,12},{1,17},{... | collective-permute-start | bytes 2752520 | tf_op jit(solution)/shard_map/ppermute | solution.py:118
  40.0 18.4 %collective-permute-start = (s32[256,4]{0,1:T(4,128)S(1)}, s32[256,4]{0,1:T(4,128)S(1)}, u32[]{:S(2)}, u32[]{:S(2)}) collective-permute-start(s32[256,4]{0,1:T(4,128)S(1)} %pad_add_fusion.1), channel_id=1, source_target_pairs={{0,8},{4,12},{8,0},{12,4},{16,24},{20,28},{24,16},{28,20},{1,9},{5... | collective-permute-start | bytes 12296 | tf_op jit(solution)/shard_map/ppermute | solution.py:118
  40.6 20.2 %collective-permute-start.1 = (s32[256,4]{0,1:T(4,128)S(1)}, s32[256,4]{0,1:T(4,128)S(1)}, u32[]{:S(2)}, u32[]{:S(2)}) collective-permute-start(s32[256,4]{0,1:T(4,128)S(1)} %pad_add_fusion.1), channel_id=1, source_target_pairs={{0,16},{4,20},{8,24},{12,28},{16,0},{20,4},{24,8},{28,12},{1,17},{... | collective-permute-start | bytes 12296 | tf_op jit(solution)/shard_map/ppermute | solution.py:118
  58.4 4.6 %collective-permute-start.2 = (s32[256,4]{0,1:T(4,128)S(1)}, s32[256,4]{0,1:T(4,128)S(1)}, u32[]{:S(2)}, u32[]{:S(2)}) collective-permute-start(s32[256,4]{0,1:T(4,128)S(1)} %pad_add_fusion.1), channel_id=1, source_target_pairs={{0,24},{4,28},{8,16},{12,20},{16,8},{20,12},{24,0},{28,4},{1,25},{... | collective-permute-start | bytes 12296 | tf_op jit(solution)/shard_map/ppermute | solution.py:118
  60.8 49.4 %collective-permute-start.10 = (bf16[3,224,512]{2,1,0:T(8,128)(2,1)S(1)}, bf16[3,224,512]{2,1,0:T(8,128)(2,1)S(1)}, u32[]{:S(2)}, u32[]{:S(2)}) collective-permute-start(bf16[3,224,512]{2,1,0:T(8,128)(2,1)S(1)} %get-tuple-element.34), channel_id=1, source_target_pairs={{0,16},{4,20},{8,24},{12,28},{16,0},{20,4},{24,8},{28,12},{1,17},{... | collective-permute-start | bytes 2064392 | tf_op jit(solution)/shard_map/ppermute | solution.py:118
  63.0 47.3 %collective-permute-start.11 = (bf16[3,224,512]{2,1,0:T(8,128)(2,1)}, bf16[3,224,512]{2,1,0:T(8,128)(2,1)S(1)}, u32[]{:S(2)}, u32[]{:S(2)}) collective-permute-start(bf16[3,224,512]{2,1,0:T(8,128)(2,1)} %get-tuple-element.33), channel_id=1, source_target_pairs={{0,24},{4,28},{8,16},{12,20},{16,8},{20,12},{24,0},{28,4},{1,25},{... | collective-permute-start | bytes 2064392 | tf_op jit(solution)/shard_map/ppermute | solution.py:118
  65.4 46.1 %collective-permute-start.8 = (bf16[256,1792]{1,0:T(8,128)(2,1)}, bf16[256,1792]{1,0:T(8,128)(2,1)}, u32[]{:S(2)}, u32[]{:S(2)}) collective-permute-start(bf16[256,1792]{1,0:T(8,128)(2,1)} %bitcast.9), channel_id=1, source_target_pairs={{0,24},{4,28},{8,16},{12,20},{16,8},{20,12},{24,0},{28,4},{1,25},{... | collective-permute-start | bytes 2752520 | tf_op jit(solution)/shard_map/ppermute | solution.py:118
  110.2 4.7 %collective-permute-start.12 = (bf16[3,224,512]{2,1,0:T(8,128)(2,1)}, bf16[3,224,512]{2,1,0:T(8,128)(2,1)S(1)}, u32[]{:S(2)}, u32[]{:S(2)}) collective-permute-start(bf16[3,224,512]{2,1,0:T(8,128)(2,1)} %get-tuple-element.32), channel_id=1, source_target_pairs={{0,4},{4,0},{8,12},{12,8},{16,20},{20,16},{24,28},{28,24},{1,5},{5... | collective-permute-start | bytes 2064392 | tf_op jit(solution)/shard_map/ppermute | solution.py:121
  110.2 4.7 %collective-permute-start.13 = (bf16[3,224,512]{2,1,0:T(8,128)(2,1)S(1)}, bf16[3,224,512]{2,1,0:T(8,128)(2,1)}, u32[]{:S(2)}, u32[]{:S(2)}) collective-permute-start(bf16[3,224,512]{2,1,0:T(8,128)(2,1)S(1)} %collective-permute-done.9.refs_0_), channel_id=1, source_target_pairs={{0,4},{4,0},{8,12},{12,8},{16,20},{20,16},{24,28},{28,24},{1,5},{5... | collective-permute-start | bytes 2064392 | tf_op jit(solution)/shard_map/ppermute | solution.py:121
  110.8 4.2 %collective-permute-start.14 = (bf16[3,224,512]{2,1,0:T(8,128)(2,1)S(1)}, bf16[3,224,512]{2,1,0:T(8,128)(2,1)}, u32[]{:S(2)}, u32[]{:S(2)}) collective-permute-start(bf16[3,224,512]{2,1,0:T(8,128)(2,1)S(1)} %collective-permute-done.10.refs_1_), channel_id=1, source_target_pairs={{0,4},{4,0},{8,12},{12,8},{16,20},{20,16},{24,28},{28,24},{1,5},{5... | collective-permute-start | bytes 2064392 | tf_op jit(solution)/shard_map/ppermute | solution.py:121
  110.8 4.6 %collective-permute-start.15 = (bf16[3,224,512]{2,1,0:T(8,128)(2,1)S(1)}, bf16[3,224,512]{2,1,0:T(8,128)(2,1)}, u32[]{:S(2)}, u32[]{:S(2)}) collective-permute-start(bf16[3,224,512]{2,1,0:T(8,128)(2,1)S(1)} %collective-permute-done.11.refs_2_), channel_id=1, source_target_pairs={{0,4},{4,0},{8,12},{12,8},{16,20},{20,16},{24,28},{28,24},{1,5},{5... | collective-permute-start | bytes 2064392 | tf_op jit(solution)/shard_map/ppermute | solution.py:121
  126.0 92.4 %reduce-scatter.5.cloned.1.call-start = ((), (), s32[]{:S(2)}) async-start(), calls=%async_computation.3 | async-start | bytes 2621440 | tf_op jit(solution)/shard_map/reduce_scatter | solution.py:158
  128.0 18.3 %collective-permute-start.16 = (bf16[3,224,512]{2,1,0:T(8,128)(2,1)S(1)}, bf16[3,224,512]{2,1,0:T(8,128)(2,1)S(1)}, u32[]{:S(2)}, u32[]{:S(2)}) collective-permute-start(bf16[3,224,512]{2,1,0:T(8,128)(2,1)S(1)} %get-tuple-element.39), channel_id=1, source_target_pairs={{0,8},{4,12},{8,0},{12,4},{16,24},{20,28},{24,16},{28,20},{1,9},{5... | collective-permute-start | bytes 2064392 | tf_op jit(solution)/shard_map/ppermute | solution.py:118
  128.6 31.9 %collective-permute-start.17 = (bf16[3,224,512]{2,1,0:T(8,128)(2,1)S(1)}, bf16[3,224,512]{2,1,0:T(8,128)(2,1)S(1)}, u32[]{:S(2)}, u32[]{:S(2)}) collective-permute-start(bf16[3,224,512]{2,1,0:T(8,128)(2,1)S(1)} %get-tuple-element.38), channel_id=1, source_target_pairs={{0,16},{4,20},{8,24},{12,28},{16,0},{20,4},{24,8},{28,12},{1,17},{... | collective-permute-start | bytes 2064392 | tf_op jit(solution)/shard_map/ppermute | solution.py:118
  129.1 31.4 %collective-permute-start.18 = (bf16[3,224,512]{2,1,0:T(8,128)(2,1)S(1)}, bf16[3,224,512]{2,1,0:T(8,128)(2,1)S(1)}, u32[]{:S(2)}, u32[]{:S(2)}) collective-permute-start(bf16[3,224,512]{2,1,0:T(8,128)(2,1)S(1)} %get-tuple-element.37), channel_id=1, source_target_pairs={{0,24},{4,28},{8,16},{12,20},{16,8},{20,12},{24,0},{28,4},{1,25},{... | collective-permute-start | bytes 2064392 | tf_op jit(solution)/shard_map/ppermute | solution.py:118
  131.5 29.5 %collective-permute-start.19 = (bf16[3,224,512]{2,1,0:T(8,128)(2,1)S(1)}, bf16[3,224,512]{2,1,0:T(8,128)(2,1)S(1)}, u32[]{:S(2)}, u32[]{:S(2)}) collective-permute-start(bf16[3,224,512]{2,1,0:T(8,128)(2,1)S(1)} %get-tuple-element.36), channel_id=1, source_target_pairs={{0,4},{4,0},{8,12},{12,8},{16,20},{20,16},{24,28},{28,24},{1,5},{5... | collective-permute-start | bytes 2064392 | tf_op jit(solution)/shard_map/ppermute | solution.py:121
  146.3 14.7 %collective-permute-start.20 = (bf16[3,224,512]{2,1,0:T(8,128)(2,1)S(1)}, bf16[3,224,512]{2,1,0:T(8,128)(2,1)S(1)}, u32[]{:S(2)}, u32[]{:S(2)}) collective-permute-start(bf16[3,224,512]{2,1,0:T(8,128)(2,1)S(1)} %collective-permute-done.16.refs_0_), channel_id=1, source_target_pairs={{0,4},{4,0},{8,12},{12,8},{16,20},{20,16},{24,28},{28,24},{1,5},{5... | collective-permute-start | bytes 2064392 | tf_op jit(solution)/shard_map/ppermute | solution.py:121
  160.5 2.1 collective-permute-start.21
  160.5 3.1 collective-permute-start.22
  173.5 92.7 %all-gather.2.cloned.1.call-start = ((), (), s32[]{:S(2)}) async-start(), calls=%async_computation.4 | async-start | bytes 2621440 | tf_op jit(solution)/shard_map/all_gather | solution.py:170
  222.9 18.4 %collective-permute-start.23 = (bf16[3,224,512]{2,1,0:T(8,128)(2,1)S(1)}, bf16[3,224,512]{2,1,0:T(8,128)(2,1)S(1)}, u32[]{:S(2)}, u32[]{:S(2)}) collective-permute-start(bf16[3,224,512]{2,1,0:T(8,128)(2,1)S(1)} %get-tuple-element.31), channel_id=1, source_target_pairs={{0,8},{4,12},{8,0},{12,4},{16,24},{20,28},{24,16},{28,20},{1,9},{5... | collective-permute-start | bytes 2064392 | tf_op jit(solution)/shard_map/ppermute | solution.py:118
  224.4 31.5 %collective-permute-start.24 = (bf16[3,224,512]{2,1,0:T(8,128)(2,1)S(1)}, bf16[3,224,512]{2,1,0:T(8,128)(2,1)S(1)}, u32[]{:S(2)}, u32[]{:S(2)}) collective-permute-start(bf16[3,224,512]{2,1,0:T(8,128)(2,1)S(1)} %get-tuple-element.30), channel_id=1, source_target_pairs={{0,16},{4,20},{8,24},{12,28},{16,0},{20,4},{24,8},{28,12},{1,17},{... | collective-permute-start | bytes 2064392 | tf_op jit(solution)/shard_map/ppermute | solution.py:118
  225.9 30.0 %collective-permute-start.25 = (bf16[3,224,512]{2,1,0:T(8,128)(2,1)S(1)}, bf16[3,224,512]{2,1,0:T(8,128)(2,1)S(1)}, u32[]{:S(2)}, u32[]{:S(2)}) collective-permute-start(bf16[3,224,512]{2,1,0:T(8,128)(2,1)S(1)} %get-tuple-element.29), channel_id=1, source_target_pairs={{0,24},{4,28},{8,16},{12,20},{16,8},{20,12},{24,0},{28,4},{1,25},{... | collective-permute-start | bytes 2064392 | tf_op jit(solution)/shard_map/ppermute | solution.py:118
  226.5 30.0 %collective-permute-start.26 = (bf16[3,224,512]{2,1,0:T(8,128)(2,1)S(1)}, bf16[3,224,512]{2,1,0:T(8,128)(2,1)S(1)}, u32[]{:S(2)}, u32[]{:S(2)}) collective-permute-start(bf16[3,224,512]{2,1,0:T(8,128)(2,1)S(1)} %get-tuple-element.28), channel_id=1, source_target_pairs={{0,4},{4,0},{8,12},{12,8},{16,20},{20,16},{24,28},{28,24},{1,5},{5... | collective-permute-start | bytes 2064392 | tf_op jit(solution)/shard_map/ppermute | solution.py:121
  241.3 15.1 %collective-permute-start.27 = (bf16[3,224,512]{2,1,0:T(8,128)(2,1)S(1)}, bf16[3,224,512]{2,1,0:T(8,128)(2,1)S(1)}, u32[]{:S(2)}, u32[]{:S(2)}) collective-permute-start(bf16[3,224,512]{2,1,0:T(8,128)(2,1)S(1)} %collective-permute-done.23.refs_0_), channel_id=1, source_target_pairs={{0,4},{4,0},{8,12},{12,8},{16,20},{20,16},{24,28},{28,24},{1,5},{5... | collective-permute-start | bytes 2064392 | tf_op jit(solution)/shard_map/ppermute | solution.py:121
  255.9 2.1 collective-permute-start.28
  255.9 3.1 collective-permute-start.29
  256.4 0.8 copy-start
  258.1 0.9 copy-start.2
  259.1 0.9 copy-start.4
  266.2 1.1 copy-start.1
  267.3 1.1 copy-start.3
  268.4 1.1 copy-start.5
  281.5 23.3 %collective-permute-start.30 = (bf16[256,1792]{1,0:T(8,128)(2,1)S(1)}, bf16[256,1792]{1,0:T(8,128)(2,1)S(1)}, u32[]{:S(2)}, u32[]{:S(2)}) collective-permute-start(bf16[256,1792]{1,0:T(8,128)(2,1)S(1)} %get-tuple-element.25), channel_id=1, source_target_pairs={{0,8},{4,12},{8,0},{12,4},{16,24},{20,28},{24,16},{28,20},{1,9},{5... | collective-permute-start | bytes 2752520 | tf_op jit(solution)/shard_map/ppermute | solution.py:118
  283.0 41.5 %collective-permute-start.31 = (bf16[256,1792]{1,0:T(8,128)(2,1)S(1)}, bf16[256,1792]{1,0:T(8,128)(2,1)S(1)}, u32[]{:S(2)}, u32[]{:S(2)}) collective-permute-start(bf16[256,1792]{1,0:T(8,128)(2,1)S(1)} %get-tuple-element.27), channel_id=1, source_target_pairs={{0,16},{4,20},{8,24},{12,28},{16,0},{20,4},{24,8},{28,12},{1,17},{... | collective-permute-start | bytes 2752520 | tf_op jit(solution)/shard_map/ppermute | solution.py:118
  284.5 40.0 %collective-permute-start.32 = (bf16[256,1792]{1,0:T(8,128)(2,1)S(1)}, bf16[256,1792]{1,0:T(8,128)(2,1)S(1)}, u32[]{:S(2)}, u32[]{:S(2)}) collective-permute-start(bf16[256,1792]{1,0:T(8,128)(2,1)S(1)} %get-tuple-element.26), channel_id=1, source_target_pairs={{0,24},{4,28},{8,16},{12,20},{16,8},{20,12},{24,0},{28,4},{1,25},{... | collective-permute-start | bytes 2752520 | tf_op jit(solution)/shard_map/ppermute | solution.py:118
  327.9 11.6 %collective-permute-start.33 = (bf16[64,8,224]{2,1,0:T(8,128)(2,1)S(1)}, bf16[64,8,224]{2,1,0:T(8,128)(2,1)S(1)}, u32[]{:S(2)}, u32[]{:S(2)}) collective-permute-start(bf16[64,8,224]{2,1,0:T(8,128)(2,1)S(1)} %get-tuple-element.42), channel_id=1, source_target_pairs={{0,1},{1,0},{2,3},{3,2},{4,5},{5,4},{6,7},{7,6},{8,9},{9,8},{10,11... | collective-permute-start | bytes 688136 | tf_op jit(solution)/shard_map/ppermute | solution.py:124
  328.0 21.4 %collective-permute-start.34 = (bf16[64,8,224]{2,1,0:T(8,128)(2,1)S(1)}, bf16[64,8,224]{2,1,0:T(8,128)(2,1)S(1)}, u32[]{:S(2)}, u32[]{:S(2)}) collective-permute-start(bf16[64,8,224]{2,1,0:T(8,128)(2,1)S(1)} %get-tuple-element.41), channel_id=1, source_target_pairs={{0,2},{1,3},{2,0},{3,1},{4,6},{5,7},{6,4},{7,5},{8,10},{9,11},{10,... | collective-permute-start | bytes 688136 | tf_op jit(solution)/shard_map/ppermute | solution.py:124
  329.9 20.0 %collective-permute-start.35 = (bf16[64,8,224]{2,1,0:T(8,128)(2,1)S(1)}, bf16[64,8,224]{2,1,0:T(8,128)(2,1)S(1)}, u32[]{:S(2)}, u32[]{:S(2)}) collective-permute-start(bf16[64,8,224]{2,1,0:T(8,128)(2,1)S(1)} %get-tuple-element.40), channel_id=1, source_target_pairs={{0,3},{1,2},{2,1},{3,0},{4,7},{5,6},{6,5},{7,4},{8,11},{9,10},{10,... | collective-permute-start | bytes 688136 | tf_op jit(solution)/shard_map/ppermute | solution.py:124
Sparse Core Ops, SparseCore 0:
  126.1 43.8 reduce-scatter.2
  173.7 44.7 reduce-scatter.4
  221.0 45.2 all-gather.1

commit v3 on v0

v3 whole, which is shorter than its diff:
```python
import functools

import jax
import jax.numpy as jnp
from jax import lax
from jax.experimental import pallas as pl
from jax.experimental.pallas import tpu as pltpu
from jax.sharding import PartitionSpec as P

VMEM_BYTES = 32 * 1024 * 1024
CORES = 2
HALVES = 2
TILE = 256
ROWS = 16

SMEM_SPEC = pl.BlockSpec(memory_space=pltpu.SMEM)
VMEM_SPEC = pl.BlockSpec(memory_space=pltpu.VMEM)
ANY_SPEC = pl.BlockSpec(memory_space=pl.ANY)
PARAMS = pltpu.CompilerParams(vmem_limit_bytes=VMEM_BYTES)


def bf16(*shape):
    return jax.ShapeDtypeStruct(shape, jnp.bfloat16)


def cut_kernel(depth, place_ref, tokens_ref, *refs):
    outs, held = refs[:-1], refs[-1]
    levels, _, wide = held.shape
    level = place_ref[2]
    tokens = tokens_ref[...]
    for other in range(levels):
        starts = [(block * levels + other) * depth for block in range(wide // depth)]
        piece = jnp.concatenate([tokens[:, s : s + depth] for s in starts], axis=1)
        held[jnp.bitwise_xor(level, other)] = piece
    for step, out_ref in enumerate(outs):
        out_ref[...] = held[step]


def cut_tokens(place, tokens, levels, depth):
    rows, model = tokens.shape
    shape = (rows, model // levels)
    return pl.pallas_call(
        functools.partial(cut_kernel, depth),
        in_specs=[SMEM_SPEC, VMEM_SPEC],
        out_specs=[VMEM_SPEC] * levels,
        out_shape=[bf16(*shape)] * levels,
        scratch_shapes=[pltpu.VMEM((levels,) + shape, jnp.bfloat16)],
        compiler_params=PARAMS,
    )(place, tokens)


def group_kernel(levels, place_ref, *refs):
    pieces, outs = refs[:levels], refs[levels:]
    rows = pieces[0].shape[0] // HALVES
    for step, piece in enumerate(pieces):
        start = pl.multiple_of(jnp.bitwise_xor(place_ref[2], step) * rows, rows)
        for half, out_ref in enumerate(outs):
            out_ref[pl.ds(start, rows), :] = piece[half * rows : (half + 1) * rows, :]


def group_tokens(place, pieces):
    rows, wide = pieces[0].shape
    levels = len(pieces)
    return pl.pallas_call(
        functools.partial(group_kernel, levels),
        in_specs=[SMEM_SPEC] + [VMEM_SPEC] * levels,
        out_specs=[VMEM_SPEC] * HALVES,
        out_shape=[bf16(levels * rows // HALVES, wide)] * HALVES,
        compiler_params=PARAMS,
    )(place, *pieces)


def finish_kernel(depth, levels, place_ref, *refs):
    pieces, (out_ref, held) = refs[:-2], refs[-2:]
    rows, wide = pieces[0].shape
    for index, piece in enumerate(pieces):
        half, step = index // levels, index % levels
        other = jnp.bitwise_xor(place_ref[2], step)
        held[other, half * rows : (half + 1) * rows, :] = piece[...]
    parts = []
    for block in range(wide // depth):
        for other in range(levels):
            parts.append(held[other, :, block * depth : (block + 1) * depth])
    out_ref[...] = jnp.concatenate(parts, axis=1)


def finish(place, pieces, levels, depth):
    rows, wide = pieces[0].shape
    rows = rows * HALVES
    return pl.pallas_call(
        functools.partial(finish_kernel, depth, levels),
        in_specs=[SMEM_SPEC] + [VMEM_SPEC] * len(pieces),
        out_specs=VMEM_SPEC,
        out_shape=bf16(rows, wide * levels),
        scratch_shapes=[pltpu.VMEM((levels, rows, wide), jnp.bfloat16)],
        compiler_params=PARAMS,
    )(place, *pieces)


def fill(place_ref, own_ref, pieces, held, sems, staged):
    experts, depth, _ = own_ref.shape
    width = held.shape[2]
    q, c = place_ref[0], place_ref[1]
    chips = (len(pieces) + 1) // CORES
    copies = []
    for which in range(experts):
        mine = []
        for index in range(CORES * chips):
            side, step = index // chips, index % chips
            if index == 0:
                columns = pl.ds(pl.multiple_of(q * width, width), width)
                source = own_ref.at[which, :, columns]
            else:
                source = pieces[index - 1].at[which]
            block = jnp.bitwise_xor(q, step) * CORES + jnp.bitwise_xor(c, side)
            if staged:
                target = staged[0].at[which, block]
            else:
                rows = pl.ds(pl.multiple_of(block * depth, ROWS), depth)
                target = held.at[which, rows, :]
            mine.append(pltpu.make_async_copy(source, target, sems.at[which, index]))
        copies.append(mine)
    for mine in copies:
        for copy in mine:
            copy.start()

    def ready(which):
        for copy in copies[which]:
            copy.wait()
        if staged:
            for block in range(CORES * chips):
                held[which, block * depth : (block + 1) * depth, :] = staged[0][which, block]

    return ready


def weight_scratch(experts, blocks, depth, width):
    scratch = [
        pltpu.VMEM((experts, blocks * depth, width), jnp.bfloat16),
        pltpu.SemaphoreType.DMA((experts, blocks)),
    ]
    if depth % ROWS:
        scratch.append(pltpu.VMEM((experts, blocks, depth, width), jnp.bfloat16))
    return scratch


def pick_kernel(chips, blocks, place_ref, ids_ref, *refs):
    toks, refs = refs[:chips], refs[chips:]
    own_ref, pieces, refs = refs[0], refs[1:blocks], refs[blocks:]
    out_ref, left, held, sems, *staged = refs
    ready = fill(place_ref, own_ref, pieces, held, sems, staged)
    rows = toks[0].shape[0]
    for step, tok in enumerate(toks):
        left[step * rows : (step + 1) * rows, :] = tok[...]
    experts, _, width = held.shape
    tile = min(TILE, width)
    for start in range(0, width, tile):
        sums = []
        for which in range(experts):
            if start == 0:
                ready(which)
            sums.append(
                jnp.dot(
                    left[...],
                    held[which, :, start : start + tile],
                    preferred_element_type=jnp.float32,
                )
            )
        for slot in range(ids_ref.shape[1]):
            chosen = ids_ref[:, slot : slot + 1]
            picked = sums[0]
            for which in range(1, experts):
                picked = jnp.where(chosen == which, sums[which], picked)
            first = slot * width + start
            out_ref[:, first : first + tile] = picked.astype(out_ref.dtype)


def picked_sums(place, ids, toks, own, pieces):
    count, slots = ids.shape
    experts, depth, _ = own.shape
    blocks = len(pieces) + 1
    width = pieces[0].shape[2]
    wide = blocks * depth
    return pl.pallas_call(
        functools.partial(pick_kernel, len(toks), blocks),
        in_specs=[SMEM_SPEC, VMEM_SPEC] + [VMEM_SPEC] * len(toks) + [ANY_SPEC] * blocks,
        out_specs=VMEM_SPEC,
        out_shape=bf16(count, slots * width),
        scratch_shapes=[
            pltpu.VMEM((count, wide), jnp.bfloat16),
            *weight_scratch(experts, blocks, depth, width),
        ],
        cost_estimate=pl.CostEstimate(
            flops=2 * count * wide * width * experts,
            bytes_accessed=2 * (count * wide + experts * wide * width + count * slots * width),
            transcendentals=0,
        ),
        compiler_params=PARAMS,
    )(place, ids, *toks, own, *pieces)


def down_kernel(chips, blocks, place_ref, ids_ref, hid_ref, *refs):
    own_ref, pieces, refs = refs[0], refs[1:blocks], refs[blocks:]
    outs, (left, held, sems, *staged) = refs[:chips], refs[chips:]
    ready = fill(place_ref, own_ref, pieces, held, sems, staged)
    experts, wide, width = held.shape
    for which in range(experts):
        mine = jnp.zeros((hid_ref.shape[0], width), hid_ref.dtype)
        for slot in range(ids_ref.shape[1]):
            part = hid_ref[:, slot * width : (slot + 1) * width]
            mine = jnp.where(ids_ref[:, slot : slot + 1] == which, part, mine)
        left[which] = mine
    for which in range(experts):
        ready(which)
    rows = outs[0].shape[0]
    for start in range(0, wide, TILE):
        tile = min(TILE, wide - start)
        total = None
        for which in range(experts):
            term = lax.dot_general(
                left[which],
                held[which, start : start + tile, :],
                (((1,), (1,)), ((), ())),
                preferred_element_type=jnp.float32,
            )
            total = term if total is None else total + term
        for step, out_ref in enumerate(outs):
            part = total[step * rows : (step + 1) * rows]
            out_ref[:, start : start + tile] = part.astype(out_ref.dtype)


def down_sums(place, ids, hidden, own, pieces):
    count = ids.shape[0]
    experts, depth, _ = own.shape
    blocks = len(pieces) + 1
    width = pieces[0].shape[2]
    wide, chips = blocks * depth, blocks // CORES
    return pl.pallas_call(
        functools.partial(down_kernel, chips, blocks),
        in_specs=[SMEM_SPEC, VMEM_SPEC, VMEM_SPEC] + [ANY_SPEC] * blocks,
        out_specs=[VMEM_SPEC] * chips,
        out_shape=[bf16(count // chips, wide)] * chips,
        scratch_shapes=[
            pltpu.VMEM((experts, count, width), jnp.bfloat16),
            *weight_scratch(experts, blocks, depth, width),
        ],
        cost_estimate=pl.CostEstimate(
            flops=2 * count * wide * width * experts,
            bytes_accessed=2 * (hidden.size + experts * wide * width + count * wide),
            transcendentals=0,
        ),
        compiler_params=PARAMS,
    )(place, ids, hidden, own, *pieces)


def after(values, others):
    return lax.optimization_barrier((values, others))[0]


def local(tokens, expert_ids, gate_scores, gate_weight, up_weight, down_weight):
    n_expert, n_tensor = lax.axis_size("expert"), lax.axis_size("tensor")
    chips = n_expert // CORES
    rows = tokens.shape[0]
    depth, units = gate_weight.shape[1:]
    slots = expert_ids.shape[1]
    width = units // chips
    spot, level = lax.axis_index("expert"), lax.axis_index("tensor")
    q, c = spot // CORES, spot % CORES
    place = jnp.stack([q, c, level])

    def to_chip(value, step):
        pairs = [(s, s ^ (step * CORES)) for s in range(n_expert)]
        return lax.ppermute(value, "expert", pairs)

    def to_core(value):
        return lax.ppermute(value, "expert", [(s, s ^ 1) for s in range(n_expert)])

    def to_level(value, step):
        return lax.ppermute(value, "tensor", [(s, s ^ step) for s in range(n_tensor)])

    def blocks_of(weight):
        return [
            lax.dynamic_slice_in_dim(weight, (q ^ step) * width, width, 2)
            for step in range(chips)
        ]

    def chip_exchange(blocks):
        return [to_chip(blocks[step], step) for step in range(1, chips)]

    def core_exchange(blocks, same):
        return same + [to_core(value) for value in [blocks[0]] + same]

    gate_blocks = blocks_of(gate_weight)
    gate_same = chip_exchange(gate_blocks)
    cut = cut_tokens(place, after(tokens, gate_blocks), n_tensor, depth)
    cut = [cut[0]] + [to_level(cut[step], step) for step in range(1, n_tensor)]
    groups = group_tokens(place, cut)
    gate_pieces = core_exchange(gate_blocks, gate_same)

    routing = jnp.concatenate([expert_ids, gate_scores], axis=1)
    routing = lax.all_gather(routing, "expert", axis=0)
    order = jnp.stack([(q ^ step) * CORES + c for step in range(chips)])
    routing = jnp.take(routing, order, axis=0)
    routing = routing.reshape(chips, n_tensor, HALVES, rows // HALVES, 2 * slots)
    routing = [routing[:, :, half].reshape(-1, 2 * slots) for half in range(HALVES)]

    toks, barrier = [], gate_same
    for half in range(HALVES):
        group = after(groups[half], barrier)
        toks.append([group] + [to_chip(group, step) for step in range(1, chips)])
        barrier = toks[-1][1:]
    up_blocks = after(blocks_of(up_weight), barrier)
    up_pieces = core_exchange(up_blocks, chip_exchange(up_blocks))
    down_blocks = after(blocks_of(down_weight), up_pieces)
    down_pieces = core_exchange(down_blocks, chip_exchange(down_blocks))

    sums, part = [], place
    for weight, pieces in ((gate_weight, gate_pieces), (up_weight, up_pieces)):
        for half in range(HALVES):
            ids = routing[half][:, :slots]
            part = picked_sums(place, ids, after(toks[half], part), weight, pieces)
            sums.append(lax.psum_scatter(part, "tensor", scatter_dimension=0, tiled=True))
    gate_sums, up_sums = sums[:HALVES], sums[HALVES:]

    hiddens = []
    for half in range(HALVES):
        count = gate_sums[half].shape[0]
        scores = routing[half][:, slots:].astype(jnp.float32)
        scores = lax.dynamic_slice_in_dim(scores, level * count, count, 0)
        combine = scores / jnp.sum(scores, axis=1, keepdims=True)
        combine = jnp.repeat(combine, width, axis=1)
        gate_sum = gate_sums[half].astype(jnp.float32)
        up_sum = up_sums[half].astype(jnp.float32)
        hidden = (jax.nn.silu(gate_sum) * up_sum * combine).astype(jnp.bfloat16)
        hiddens.append(lax.all_gather(hidden, "tensor", axis=0, tiled=True))

    backs = []
    for half in range(HALVES):
        ids = routing[half][:, :slots]
        parts = down_sums(place, ids, hiddens[half], down_weight, down_pieces)
        total = parts[0].astype(jnp.float32)
        for step in range(1, chips):
            total = total + to_chip(parts[step], step).astype(jnp.float32)
        total = total.astype(jnp.bfloat16).reshape(n_tensor, rows // HALVES, -1)
        for step in range(n_tensor):
            piece = lax.dynamic_index_in_dim(total, level ^ step, 0, keepdims=False)
            backs.append(to_level(piece, step) if step else piece)
    return finish(place, backs, n_tensor, depth)


def solution(mesh):
    return jax.shard_map(
        local,
        mesh=mesh,
        in_specs=(
            P(("expert", "tensor"), None),
            P("expert", None),
            P("expert", None),
            P(None, ("expert", "tensor"), None),
            P(None, ("expert", "tensor"), None),
            P(None, ("expert", "tensor"), None),
        ),
        out_specs=P(("expert", "tensor"), None),
        check_vma=False,
    )
```

time: 606 us -> 400 us (0.66)
  blocking collectives: 357 us -> 24.6 us
  Pallas kernels: 0 us -> 64.5 us
  matrix products: 46.4 us -> 0 us
  starting transfers between devices: 0.35 us -> 44.1 us
  waiting for transfers between devices: 150 us -> 191 us
  local copies, waits for them, and re-layouts: 38.2 us -> 53.2 us
  other arithmetic: 0.05 us -> 7.2 us
    all_to_all x3 -> x0, blocking collectives: 357 us -> none  [the longest x1 159 us: local(): lax.all_to_all(gate_weight, 'tensor', split_axis=2, concat_axis=1, tiled=...]
    ppermute x0 -> x42, waiting for transfers between devices: none -> 85.9 us  [the longest x21 62.3 us: to_chip(): return lax.ppermute(value, 'expert', pairs)]
    pallas_call x0 -> x9, Pallas kernels: none -> 64.5 us  [the longest x4 41.2 us: picked_sums(): pl.pallas_call(functools.partial(pick_kernel, len(toks), blocks), in_spec...]
    all_gather x4 -> x2, waiting for transfers between devices: 81 us -> 29.4 us  [local(): hiddens.append(lax.all_gather(hidden, 'tensor', axis=0, tiled=True))]
    dot_general x7 -> x0, matrix products: 46.4 us -> none  [the longest x3 17.9 us: local(): jnp.dot(gathered, full_gate[which], preferred_element_type=jnp.float32)]
    ppermute x0 -> x42, starting transfers between devices: none -> 43.5 us  [the longest x21 25.4 us: to_chip(): return lax.ppermute(value, 'expert', pairs)]
    all_gather x0 -> x1, blocking collectives: none -> 24.6 us  [local(): routing = lax.all_gather(routing, 'expert', axis=0)]
    unnamed x15 -> x106, local copies, waits for them, and re-layouts: 16.7 us -> 38.4 us
  transfers between devices with their start and end apart: 5 -> 48, of which waited for: 2 -> 25; matrix products, arithmetic and copies ran while one was open for 12% -> 5% of each run, Pallas kernels for 0% -> 14%
where the time goes in v3:
time: 400 us; the launch traced here: 399 us
  waiting for transfers between devices  191 us (48%)
  Pallas kernels  64.5 us (16%)
  local copies, waits for them, and re-layouts  53.2 us (13%)
  starting transfers between devices  44.1 us (11%)
  blocking collectives  24.6 us (6%)
  between operations  13.9 us (3%)
  other arithmetic  7.2 us (2%)
    reduce_scatter x4, waiting for transfers between devices, local(): lax.psum_scatter(part, 'tensor', scatter_dimension=0, tiled=True)  74.9 us
    ppermute x21, waiting for transfers between devices, to_chip(): return lax.ppermute(value, 'expert', pairs)  62.3 us
    pallas_call x4, Pallas kernels, picked_sums(): pl.pallas_call(functools.partial(pick_kernel, len(toks), blocks), in_spec...  41.2 us
    unnamed x106, local copies, waits for them, and re-layouts  38.4 us
    all_gather x2, waiting for transfers between devices, local(): hiddens.append(lax.all_gather(hidden, 'tensor', axis=0, tiled=True))  29.4 us
    ppermute x21, starting transfers between devices, to_chip(): return lax.ppermute(value, 'expert', pairs)  25.4 us
    all_gather x1, blocking collectives, local(): routing = lax.all_gather(routing, 'expert', axis=0)  24.6 us
    ppermute x9, waiting for transfers between devices, to_level(): lax.ppermute(value, 'tensor', [(s, s ^ step) for s in range(n_tensor)])  19.5 us
  transfers between devices with their start and end apart: 48, of which 25 were waited for; matrix products, arithmetic and copies ran while one was open for 5% of the time, Pallas kernels for 14%

profile of v3, /device:TPU:0, one launch (start us, length us, event | category | flops | bytes accessed | tf_op | source)
XLA Modules:
  0.0 399.0 jit_solution(9985584893596899242)
XLA Ops:
  6.5 3.4 constant_dynamic-slice_fusion.8
  10.0 3.9 collective-permute-start.5
  14.5 1.7 shard_map.64
  16.9 2.1 collective-permute-start
  18.9 2.6 collective-permute-start.1
  21.5 6.8 %collective-permute-done.refs_1_ = bf16[64,1792]{1,0:T(8,128)(2,1)S(1)} collective-permute-done((bf16[64,1792]{1,0:T(8,128)(2,1)S(1)}, bf16[64,1792]{1,0:T(8,128)(2,1)S(1)}, u32[]{:S(2)}, u32[]{:S(2)}) %collective-permute-start) | collective-permute-done | bytes 229408 | tf_op jit(solution)/shard_map/ppermute | solution.py:279
  29.0 2.6 collective-permute-start.2
  31.8 5.4 %collective-permute-done.2.refs_3_ = bf16[64,1792]{1,0:T(8,128)(2,1)} collective-permute-done((bf16[64,1792]{1,0:T(8,128)(2,1)}, bf16[64,1792]{1,0:T(8,128)(2,1)}, u32[]{:S(2)}, u32[]{:S(2)}) %collective-permute-start.2) | collective-permute-done | bytes 229408 | tf_op jit(solution)/shard_map/ppermute | solution.py:279
  39.1 1.9 shard_map.65
  41.8 2.5 collective-permute-done.4.refs_6_
  46.1 1.5 collective-permute-start.7
  47.6 24.6 %all-gather = s32[2048,4]{0,1:T(4,128)S(1)} all-gather(s32[256,4]{0,1:T(4,128)S(1)} %pad_add_fusion), channel_id=2, replica_groups=mesh['expert'=8,'tensor'=4] {'expert'}, dimensions={0}, use_global_device_ids=true | all-gather | bytes 36864 | tf_op jit(solution)/shard_map/all_gather | solution.py:301
  77.6 1.9 fusion.18
  79.5 8.3 %collective-permute-done.6.refs_1_ = bf16[128,1792]{1,0:T(8,128)(2,1)} collective-permute-done((bf16[128,1792]{1,0:T(8,128)(2,1)}, bf16[128,1792]{1,0:T(8,128)(2,1)}, u32[]{:S(2)}, u32[]{:S(2)}) %collective-permute-start.6) | collective-permute-done | bytes 458784 | tf_op jit(solution)/shard_map/ppermute | solution.py:273
  87.8 1.5 collective-permute-start.15
  89.6 1.7 collective-permute-start.13
  91.3 1.9 fusion.17
  93.3 7.5 %shard_map.66 = bf16[512,1024]{1,0:T(8,128)(2,1)S(1)} custom-call(s32[3]{0:T(128)S(1)} %pad_add_fusion.1.place_ref, s32[512,2]{1,0:T(8,128)S(1)} %get-tuple-element.110.ids_ref, bf16[128,1792]{1,0:T(8,128)(2,1)} %get-tuple-element.63.refs_0_, bf16[128,1792]{1,0:T(8,128)(2,1)} %collective-permute-done.6.refs_1_, ...), custom_call_target="tpu_custom_call" | custom-call | flops 2818572288 | bytes 8388608 | tf_op jit(solution)/shard_map/pallas_call | solution.py:184
  102.6 8.1 %collective-permute-done.14.refs_2_ = bf16[128,1792]{1,0:T(8,128)(2,1)} collective-permute-done((bf16[128,1792]{1,0:T(8,128)(2,1)}, bf16[128,1792]{1,0:T(8,128)(2,1)}, u32[]{:S(2)}, u32[]{:S(2)}) %collective-permute-start.14) | collective-permute-done | bytes 458784 | tf_op jit(solution)/shard_map/ppermute | solution.py:273
  112.6 7.4 %shard_map.67 = bf16[512,1024]{1,0:T(8,128)(2,1)S(1)} custom-call(s32[3]{0:T(128)S(1)} %pad_add_fusion.1.place_ref, s32[512,2]{1,0:T(8,128)S(1)} %copy-done.21, bf16[128,1792]{1,0:T(8,128)(2,1)S(1)} %copy-done.25, bf16[128,1792]{1,0:T(8,128)(2,1)} %collective-permute-done.13.refs_1_, bf16[128,1792]{1,0:T(8,128)(2,1)} %collective-permute-done.14.refs_2_, ...), custom_call_target="tpu_custom_call" | custom-call | flops 2818572288 | bytes 8388608 | tf_op jit(solution)/shard_map/pallas_call | solution.py:184
  121.3 2.2 constant_dynamic-slice_fusion.4
  127.1 14.8 %collective-permute-done.16.refs_5_ = bf16[3,224,512]{2,1,0:T(8,128)(2,1)S(1)} collective-permute-done((bf16[3,224,512]{2,1,0:T(8,128)(2,1)S(1)}, bf16[3,224,512]{2,1,0:T(8,128)(2,1)S(1)}, u32[]{:S(2)}, u32[]{:S(2)}) %collective-permute-start.16) | collective-permute-done | bytes 688160 | tf_op jit(solution)/shard_map/ppermute | solution.py:273
  141.9 13.1 %collective-permute-done.17.refs_6_ = bf16[3,224,512]{2,1,0:T(8,128)(2,1)S(1)} collective-permute-done((bf16[3,224,512]{2,1,0:T(8,128)(2,1)S(1)}, bf16[3,224,512]{2,1,0:T(8,128)(2,1)S(1)}, u32[]{:S(2)}, u32[]{:S(2)}) %collective-permute-start.17) | collective-permute-done | bytes 688160 | tf_op jit(solution)/shard_map/ppermute | solution.py:273
  158.2 13.7 %shard_map.68 = bf16[512,1024]{1,0:T(8,128)(2,1)} custom-call(s32[3]{0:T(128)S(1)} %pad_add_fusion.1.place_ref, s32[512,2]{1,0:T(8,128)S(1)} %copy-done.19, bf16[128,1792]{1,0:T(8,128)(2,1)} %get-tuple-element.63.refs_0_, bf16[128,1792]{1,0:T(8,128)(2,1)} %collective-permute-done.6.refs_1_, bf16[128,1792]{1,0:T(8,128)(2,1)} %collective-permute-done.7.refs_2_, ...), custom_call_target="tpu_custom_call" | custom-call | flops 2818572288 | bytes 8388608 | tf_op jit(solution)/shard_map/pallas_call | solution.py:184
  185.6 12.6 %shard_map.70 = bf16[512,1024]{1,0:T(8,128)(2,1)S(1)} custom-call(s32[3]{0:T(128)S(1)} %pad_add_fusion.1.place_ref, s32[512,2]{1,0:T(8,128)S(1)} %copy-done.22, bf16[128,1792]{1,0:T(8,128)(2,1)S(1)} %copy-done.26, bf16[128,1792]{1,0:T(8,128)(2,1)} %collective-permute-done.13.refs_1_, bf16[128,1792]{1,0:T(8,128)(2,1)} %collective-permute-done.14.refs_2_, ...), custom_call_target="tpu_custom_call" | custom-call | flops 2818572288 | bytes 8388608 | tf_op jit(solution)/shard_map/pallas_call | solution.py:184
  201.2 26.6 %reduce-scatter.11.cloned.1.call-done = bf16[128,1024]{1,0:T(8,128)(2,1)} async-done(((bf16[512,1024]{1,0:T(8,128)(2,1)}), bf16[128,1024]{1,0:T(8,128)(2,1)}) %reduce-scatter.11.cloned.1.call-update) | async-done | bytes 262160 | tf_op jit(solution)/shard_map/reduce_scatter | solution.py:322
  227.8 1.9 fusion.10
  230.2 1.7 constant_dynamic-slice_fusion
  233.3 1.5 collective-permute-start.24
  235.7 20.2 %reduce-scatter.5.cloned.1.call-done = bf16[128,1024]{1,0:T(8,128)(2,1)} async-done(((bf16[512,1024]{1,0:T(8,128)(2,1)}), bf16[128,1024]{1,0:T(8,128)(2,1)}) %reduce-scatter.5.cloned.1.call-update) | async-done | bytes 262160 | tf_op jit(solution)/shard_map/reduce_scatter | solution.py:322
  256.0 28.0 %reduce-scatter.7.cloned.1.call-done = bf16[128,1024]{1,0:T(8,128)(2,1)} async-done(((bf16[512,1024]{1,0:T(8,128)(2,1)}), bf16[128,1024]{1,0:T(8,128)(2,1)}) %reduce-scatter.7.cloned.1.call-update) | async-done | bytes 262160 | tf_op jit(solution)/shard_map/reduce_scatter | solution.py:322
  284.0 1.9 fusion.11
  292.2 19.8 %all-gather.6.cloned.1.call-done.hid_ref = bf16[512,1024]{1,0:T(8,128)(2,1)} async-done(((bf16[128,1024]{1,0:T(8,128)(2,1)}), bf16[512,1024]{1,0:T(8,128)(2,1)}) %all-gather.6.cloned.1.call-update) | async-done | bytes 1048592 | tf_op jit(solution)/shard_map/all_gather | solution.py:335
  317.7 9.5 %shard_map.71 = (bf16[128,1792]{1,0:T(8,128)(2,1)S(1)}, bf16[128,1792]{1,0:T(8,128)(2,1)}, bf16[128,1792]{1,0:T(8,128)(2,1)}, bf16[128,1792]{1,0:T(8,128)(2,1)}) custom-call(s32[3]{0:T(128)S(1)} %pad_add_fusion.1.place_ref, s32[512,2]{1,0:T(8,128)S(1)} %copy-done.23, bf16[512,1024]{1,0:T(8,128)(2,1)S(1)} %copy-done.35, bf16[3,224,2048]{2,1,0:T(8,128)(2,1)S(1)} %copy-done.5, ...), custom_call_target="tpu_custom_call" | custom-call | flops 2818572288 | bytes 8388608 | tf_op jit(solution)/shard_map/pallas_call | solution.py:238
  329.4 1.5 collective-permute-start.37
  331.4 9.5 %all-gather.4.cloned.1.call-done.hid_ref = bf16[512,1024]{1,0:T(8,128)(2,1)} async-done(((bf16[128,1024]{1,0:T(8,128)(2,1)}), bf16[512,1024]{1,0:T(8,128)(2,1)}) %all-gather.4.cloned.1.call-update) | async-done | bytes 1048592 | tf_op jit(solution)/shard_map/all_gather | solution.py:335
  346.6 8.4 %shard_map.69 = (bf16[128,1792]{1,0:T(8,128)(2,1)S(1)}, bf16[128,1792]{1,0:T(8,128)(2,1)S(1)}, bf16[128,1792]{1,0:T(8,128)(2,1)S(1)}, bf16[128,1792]{1,0:T(8,128)(2,1)S(1)}) custom-call(s32[3]{0:T(128)S(1)} %pad_add_fusion.1.place_ref, s32[512,2]{1,0:T(8,128)S(1)} %copy-done.20, bf16[512,1024]{1,0:T(8,128)(2,1)S(1)} %copy-done.34, ...), custom_call_target="tpu_custom_call" | custom-call | flops 2818572288 | bytes 8388608 | tf_op jit(solution)/shard_map/pallas_call | solution.py:238
  355.0 1.5 collective-permute-start.30
  356.5 1.5 collective-permute-start.31
  358.6 1.6 add_convert_fusion
  360.2 2.0 collective-permute-start.41
  363.2 5.3 %collective-permute-done.30 = bf16[128,1792]{1,0:T(8,128)(2,1)S(1)} collective-permute-done((bf16[128,1792]{1,0:T(8,128)(2,1)S(1)}, bf16[128,1792]{1,0:T(8,128)(2,1)S(1)}, u32[]{:S(2)}, u32[]{:S(2)}) %collective-permute-start.30) | collective-permute-done | bytes 458784 | tf_op jit(solution)/shard_map/ppermute | solution.py:273
  370.0 8.2 %collective-permute-done.31 = bf16[128,1792]{1,0:T(8,128)(2,1)S(1)} collective-permute-done((bf16[128,1792]{1,0:T(8,128)(2,1)S(1)}, bf16[128,1792]{1,0:T(8,128)(2,1)S(1)}, u32[]{:S(2)}, u32[]{:S(2)}) %collective-permute-start.31) | collective-permute-done | bytes 458784 | tf_op jit(solution)/shard_map/ppermute | solution.py:273
  378.5 2.3 collective-permute-start.35
  381.4 1.6 collective-permute-start.33
  383.0 3.4 collective-permute-done.35.refs_3_
  386.4 3.9 collective-permute-done.34.refs_2_
  390.3 1.8 shard_map.72
  (198 shorter events, 67.6 us)
Async XLA Ops:
  6.5 194.7 %reduce-scatter.9.cloned.1.call-start = ((), (), s32[]{:S(2)}) async-start(), calls=%async_computation.7 | async-start | bytes 1310720 | tf_op jit(solution)/shard_map/reduce_scatter | solution.py:322
  10.0 31.8 %collective-permute-start.5 = (bf16[3,224,512]{2,1,0:T(8,128)(2,1)}, bf16[3,224,512]{2,1,0:T(8,128)(2,1)S(1)}, u32[]{:S(2)}, u32[]{:S(2)}) collective-permute-start(bf16[3,224,512]{2,1,0:T(8,128)(2,1)} %get-tuple-element.95), channel_id=1, source_target_pairs={{0,24},{4,28},{8,16},{12,20},{16,8},{20,12},{24,0},{28,4},{1,25},{... | collective-permute-start | bytes 2064392 | tf_op jit(solution)/shard_map/ppermute | solution.py:273
  13.9 30.5 %collective-permute-start.4 = (bf16[3,224,512]{2,1,0:T(8,128)(2,1)}, bf16[3,224,512]{2,1,0:T(8,128)(2,1)}, u32[]{:S(2)}, u32[]{:S(2)}) collective-permute-start(bf16[3,224,512]{2,1,0:T(8,128)(2,1)} %get-tuple-element.96), channel_id=1, source_target_pairs={{0,16},{4,20},{8,24},{12,28},{16,0},{20,4},{24,8},{28,12},{1,17},{... | collective-permute-start | bytes 2064392 | tf_op jit(solution)/shard_map/ppermute | solution.py:273
  14.4 30.3 %collective-permute-start.3 = (bf16[3,224,512]{2,1,0:T(8,128)(2,1)}, bf16[3,224,512]{2,1,0:T(8,128)(2,1)}, u32[]{:S(2)}, u32[]{:S(2)}) collective-permute-start(bf16[3,224,512]{2,1,0:T(8,128)(2,1)} %get-tuple-element.97), channel_id=1, source_target_pairs={{0,8},{4,12},{8,0},{12,4},{16,24},{20,28},{24,16},{28,20},{1,9},{5... | collective-permute-start | bytes 2064392 | tf_op jit(solution)/shard_map/ppermute | solution.py:273
  16.9 11.4 %collective-permute-start = (bf16[64,1792]{1,0:T(8,128)(2,1)S(1)}, bf16[64,1792]{1,0:T(8,128)(2,1)S(1)}, u32[]{:S(2)}, u32[]{:S(2)}) collective-permute-start(bf16[64,1792]{1,0:T(8,128)(2,1)S(1)} %get-tuple-element.48), channel_id=1, source_target_pairs={{0,1},{1,0},{2,3},{3,2},{4,5},{5,4},{6,7},{7,6},{8,9},{9,8},{10,11... | collective-permute-start | bytes 688136 | tf_op jit(solution)/shard_map/ppermute | solution.py:279
  18.9 12.8 %collective-permute-start.1 = (bf16[64,1792]{1,0:T(8,128)(2,1)}, bf16[64,1792]{1,0:T(8,128)(2,1)}, u32[]{:S(2)}, u32[]{:S(2)}) collective-permute-start(bf16[64,1792]{1,0:T(8,128)(2,1)} %get-tuple-element.49), channel_id=1, source_target_pairs={{0,2},{1,3},{2,0},{3,1},{4,6},{5,7},{6,4},{7,5},{8,10},{9,11},{10,... | collective-permute-start | bytes 688136 | tf_op jit(solution)/shard_map/ppermute | solution.py:279
  29.0 8.2 %collective-permute-start.2 = (bf16[64,1792]{1,0:T(8,128)(2,1)}, bf16[64,1792]{1,0:T(8,128)(2,1)}, u32[]{:S(2)}, u32[]{:S(2)}) collective-permute-start(bf16[64,1792]{1,0:T(8,128)(2,1)} %get-tuple-element.50), channel_id=1, source_target_pairs={{0,3},{1,2},{2,1},{3,0},{4,7},{5,6},{6,5},{7,4},{8,11},{9,10},{10,... | collective-permute-start | bytes 688136 | tf_op jit(solution)/shard_map/ppermute | solution.py:279
  31.7 57.6 %collective-permute-start.9 = (bf16[3,224,512]{2,1,0:T(8,128)(2,1)}, bf16[3,224,512]{2,1,0:T(8,128)(2,1)}, u32[]{:S(2)}, u32[]{:S(2)}) collective-permute-start(bf16[3,224,512]{2,1,0:T(8,128)(2,1)} %get-tuple-element.98), channel_id=1, source_target_pairs={{0,4},{4,0},{8,12},{12,8},{16,20},{20,16},{24,28},{28,24},{1,5},{5... | collective-permute-start | bytes 2064392 | tf_op jit(solution)/shard_map/ppermute | solution.py:276
  44.7 30.6 %collective-permute-start.8 = (bf16[128,1792]{1,0:T(8,128)(2,1)}, bf16[128,1792]{1,0:T(8,128)(2,1)}, u32[]{:S(2)}, u32[]{:S(2)}) collective-permute-start(bf16[128,1792]{1,0:T(8,128)(2,1)} %get-tuple-element.63.refs_0_), channel_id=1, source_target_pairs={{0,24},{4,28},{8,16},{12,20},{16,8},{20,12},{24,0},{28,4},{1,25},{... | collective-permute-start | bytes 1376264 | tf_op jit(solution)/shard_map/ppermute | solution.py:273
  46.1 29.2 %collective-permute-start.7 = (bf16[128,1792]{1,0:T(8,128)(2,1)}, bf16[128,1792]{1,0:T(8,128)(2,1)}, u32[]{:S(2)}, u32[]{:S(2)}) collective-permute-start(bf16[128,1792]{1,0:T(8,128)(2,1)} %get-tuple-element.63.refs_0_), channel_id=1, source_target_pairs={{0,16},{4,20},{8,24},{12,28},{16,0},{20,4},{24,8},{28,12},{1,17},{... | collective-permute-start | bytes 1376264 | tf_op jit(solution)/shard_map/ppermute | solution.py:273
  73.6 16.1 %collective-permute-start.12 = (bf16[3,224,512]{2,1,0:T(8,128)(2,1)S(1)}, bf16[3,224,512]{2,1,0:T(8,128)(2,1)}, u32[]{:S(2)}, u32[]{:S(2)}) collective-permute-start(bf16[3,224,512]{2,1,0:T(8,128)(2,1)S(1)} %collective-permute-done.5.refs_7_), channel_id=1, source_target_pairs={{0,4},{4,0},{8,12},{12,8},{16,20},{20,16},{24,28},{28,24},{1,5},{5... | collective-permute-start | bytes 2064392 | tf_op jit(solution)/shard_map/ppermute | solution.py:276
  74.8 13.0 %collective-permute-start.6 = (bf16[128,1792]{1,0:T(8,128)(2,1)}, bf16[128,1792]{1,0:T(8,128)(2,1)}, u32[]{:S(2)}, u32[]{:S(2)}) collective-permute-start(bf16[128,1792]{1,0:T(8,128)(2,1)} %get-tuple-element.63.refs_0_), channel_id=1, source_target_pairs={{0,8},{4,12},{8,0},{12,4},{16,24},{20,28},{24,16},{28,20},{1,9},{5... | collective-permute-start | bytes 1376264 | tf_op jit(solution)/shard_map/ppermute | solution.py:273
  75.3 18.0 %collective-permute-start.11 = (bf16[3,224,512]{2,1,0:T(8,128)(2,1)}, bf16[3,224,512]{2,1,0:T(8,128)(2,1)}, u32[]{:S(2)}, u32[]{:S(2)}) collective-permute-start(bf16[3,224,512]{2,1,0:T(8,128)(2,1)} %collective-permute-done.4.refs_6_), channel_id=1, source_target_pairs={{0,4},{4,0},{8,12},{12,8},{16,20},{20,16},{24,28},{28,24},{1,5},{5... | collective-permute-start | bytes 2064392 | tf_op jit(solution)/shard_map/ppermute | solution.py:276
  75.3 18.0 %collective-permute-start.10 = (bf16[3,224,512]{2,1,0:T(8,128)(2,1)}, bf16[3,224,512]{2,1,0:T(8,128)(2,1)}, u32[]{:S(2)}, u32[]{:S(2)}) collective-permute-start(bf16[3,224,512]{2,1,0:T(8,128)(2,1)} %collective-permute-done.3.refs_5_), channel_id=1, source_target_pairs={{0,4},{4,0},{8,12},{12,8},{16,20},{20,16},{24,28},{28,24},{1,5},{5... | collective-permute-start | bytes 2064392 | tf_op jit(solution)/shard_map/ppermute | solution.py:276
  87.8 14.7 %collective-permute-start.15 = (bf16[128,1792]{1,0:T(8,128)(2,1)}, bf16[128,1792]{1,0:T(8,128)(2,1)}, u32[]{:S(2)}, u32[]{:S(2)}) collective-permute-start(bf16[128,1792]{1,0:T(8,128)(2,1)} %copy-done.24), channel_id=1, source_target_pairs={{0,24},{4,28},{8,16},{12,20},{16,8},{20,12},{24,0},{28,4},{1,25},{... | collective-permute-start | bytes 1376264 | tf_op jit(solution)/shard_map/ppermute | solution.py:273
  89.3 21.3 %collective-permute-start.14 = (bf16[128,1792]{1,0:T(8,128)(2,1)}, bf16[128,1792]{1,0:T(8,128)(2,1)}, u32[]{:S(2)}, u32[]{:S(2)}) collective-permute-start(bf16[128,1792]{1,0:T(8,128)(2,1)} %copy-done.24), channel_id=1, source_target_pairs={{0,16},{4,20},{8,24},{12,28},{16,0},{20,4},{24,8},{28,12},{1,17},{... | collective-permute-start | bytes 1376264 | tf_op jit(solution)/shard_map/ppermute | solution.py:273
  89.6 21.0 %collective-permute-start.13 = (bf16[128,1792]{1,0:T(8,128)(2,1)}, bf16[128,1792]{1,0:T(8,128)(2,1)}, u32[]{:S(2)}, u32[]{:S(2)}) collective-permute-start(bf16[128,1792]{1,0:T(8,128)(2,1)} %copy-done.24), channel_id=1, source_target_pairs={{0,8},{4,12},{8,0},{12,4},{16,24},{20,28},{24,16},{28,20},{1,9},{5... | collective-permute-start | bytes 1376264 | tf_op jit(solution)/shard_map/ppermute | solution.py:273
  121.1 106.8 %reduce-scatter.11.cloned.1.call-start = ((), (), s32[]{:S(2)}) async-start(), calls=%async_computation.8 | async-start | bytes 1310720 | tf_op jit(solution)/shard_map/reduce_scatter | solution.py:322
  123.5 18.4 %collective-permute-start.16 = (bf16[3,224,512]{2,1,0:T(8,128)(2,1)S(1)}, bf16[3,224,512]{2,1,0:T(8,128)(2,1)S(1)}, u32[]{:S(2)}, u32[]{:S(2)}) collective-permute-start(bf16[3,224,512]{2,1,0:T(8,128)(2,1)S(1)} %get-tuple-element.67), channel_id=1, source_target_pairs={{0,8},{4,12},{8,0},{12,4},{16,24},{20,28},{24,16},{28,20},{1,9},{5... | collective-permute-start | bytes 2064392 | tf_op jit(solution)/shard_map/ppermute | solution.py:273
  124.2 30.8 %collective-permute-start.17 = (bf16[3,224,512]{2,1,0:T(8,128)(2,1)S(1)}, bf16[3,224,512]{2,1,0:T(8,128)(2,1)S(1)}, u32[]{:S(2)}, u32[]{:S(2)}) collective-permute-start(bf16[3,224,512]{2,1,0:T(8,128)(2,1)S(1)} %get-tuple-element.68), channel_id=1, source_target_pairs={{0,16},{4,20},{8,24},{12,28},{16,0},{20,4},{24,8},{28,12},{1,17},{... | collective-permute-start | bytes 2064392 | tf_op jit(solution)/shard_map/ppermute | solution.py:273
  125.7 30.1 %collective-permute-start.18 = (bf16[3,224,512]{2,1,0:T(8,128)(2,1)S(1)}, bf16[3,224,512]{2,1,0:T(8,128)(2,1)S(1)}, u32[]{:S(2)}, u32[]{:S(2)}) collective-permute-start(bf16[3,224,512]{2,1,0:T(8,128)(2,1)S(1)} %get-tuple-element.69), channel_id=1, source_target_pairs={{0,24},{4,28},{8,16},{12,20},{16,8},{20,12},{24,0},{28,4},{1,25},{... | collective-permute-start | bytes 2064392 | tf_op jit(solution)/shard_map/ppermute | solution.py:273
  127.1 28.7 %collective-permute-start.19 = (bf16[3,224,512]{2,1,0:T(8,128)(2,1)S(1)}, bf16[3,224,512]{2,1,0:T(8,128)(2,1)S(1)}, u32[]{:S(2)}, u32[]{:S(2)}) collective-permute-start(bf16[3,224,512]{2,1,0:T(8,128)(2,1)S(1)} %get-tuple-element.70), channel_id=1, source_target_pairs={{0,4},{4,0},{8,12},{12,8},{16,20},{20,16},{24,28},{28,24},{1,5},{5... | collective-permute-start | bytes 2064392 | tf_op jit(solution)/shard_map/ppermute | solution.py:276
  141.9 13.9 %collective-permute-start.20 = (bf16[3,224,512]{2,1,0:T(8,128)(2,1)S(1)}, bf16[3,224,512]{2,1,0:T(8,128)(2,1)S(1)}, u32[]{:S(2)}, u32[]{:S(2)}) collective-permute-start(bf16[3,224,512]{2,1,0:T(8,128)(2,1)S(1)} %collective-permute-done.16.refs_5_), channel_id=1, source_target_pairs={{0,4},{4,0},{8,12},{12,8},{16,20},{20,16},{24,28},{28,24},{1,5},{5... | collective-permute-start | bytes 2064392 | tf_op jit(solution)/shard_map/ppermute | solution.py:276
  155.0 2.1 collective-permute-start.21
  155.8 2.4 collective-permute-start.22
  199.3 56.7 %reduce-scatter.5.cloned.1.call-start = ((), (), s32[]{:S(2)}) async-start(), calls=%async_computation.4 | async-start | bytes 1310720 | tf_op jit(solution)/shard_map/reduce_scatter | solution.py:322
  200.0 84.0 %reduce-scatter.7.cloned.1.call-start = ((), (), s32[]{:S(2)}) async-start(), calls=%async_computation.5 | async-start | bytes 1310720 | tf_op jit(solution)/shard_map/reduce_scatter | solution.py:322
  200.6 111.4 %all-gather.6.cloned.1.call-start = ((), (), s32[]{:S(2)}) async-start(), calls=%async_computation.9 | async-start | bytes 1310720 | tf_op jit(solution)/shard_map/all_gather | solution.py:335
  229.8 111.2 %all-gather.4.cloned.1.call-start = ((), (), s32[]{:S(2)}) async-start(), calls=%async_computation.6 | async-start | bytes 1310720 | tf_op jit(solution)/shard_map/all_gather | solution.py:335
  231.8 54.2 %collective-permute-start.23 = (bf16[3,224,512]{2,1,0:T(8,128)(2,1)}, bf16[3,224,512]{2,1,0:T(8,128)(2,1)}, u32[]{:S(2)}, u32[]{:S(2)}) collective-permute-start(bf16[3,224,512]{2,1,0:T(8,128)(2,1)} %get-tuple-element.71), channel_id=1, source_target_pairs={{0,8},{4,12},{8,0},{12,4},{16,24},{20,28},{24,16},{28,20},{1,9},{5... | collective-permute-start | bytes 2064392 | tf_op jit(solution)/shard_map/ppermute | solution.py:273
  233.3 53.2 %collective-permute-start.24 = (bf16[3,224,512]{2,1,0:T(8,128)(2,1)}, bf16[3,224,512]{2,1,0:T(8,128)(2,1)}, u32[]{:S(2)}, u32[]{:S(2)}) collective-permute-start(bf16[3,224,512]{2,1,0:T(8,128)(2,1)} %get-tuple-element.72), channel_id=1, source_target_pairs={{0,16},{4,20},{8,24},{12,28},{16,0},{20,4},{24,8},{28,12},{1,17},{... | collective-permute-start | bytes 2064392 | tf_op jit(solution)/shard_map/ppermute | solution.py:273
  234.8 51.8 %collective-permute-start.25 = (bf16[3,224,512]{2,1,0:T(8,128)(2,1)}, bf16[3,224,512]{2,1,0:T(8,128)(2,1)}, u32[]{:S(2)}, u32[]{:S(2)}) collective-permute-start(bf16[3,224,512]{2,1,0:T(8,128)(2,1)} %get-tuple-element.73), channel_id=1, source_target_pairs={{0,24},{4,28},{8,16},{12,20},{16,8},{20,12},{24,0},{28,4},{1,25},{... | collective-permute-start | bytes 2064392 | tf_op jit(solution)/shard_map/ppermute | solution.py:273
  286.0 2.4 collective-permute-start.26
  286.1 3.3 collective-permute-start.27
  286.6 3.8 collective-permute-start.28
  286.6 4.7 %collective-permute-start.29 = (bf16[3,224,512]{2,1,0:T(8,128)(2,1)}, bf16[3,224,512]{2,1,0:T(8,128)(2,1)S(1)}, u32[]{:S(2)}, u32[]{:S(2)}) collective-permute-start(bf16[3,224,512]{2,1,0:T(8,128)(2,1)} %collective-permute-done.25.refs_3_), channel_id=1, source_target_pairs={{0,4},{4,0},{8,12},{12,8},{16,20},{20,16},{24,28},{28,24},{1,5},{5... | collective-permute-start | bytes 2064392 | tf_op jit(solution)/shard_map/ppermute | solution.py:276
  327.9 30.1 %collective-permute-start.36 = (bf16[128,1792]{1,0:T(8,128)(2,1)}, bf16[128,1792]{1,0:T(8,128)(2,1)}, u32[]{:S(2)}, u32[]{:S(2)}) collective-permute-start(bf16[128,1792]{1,0:T(8,128)(2,1)} %get-tuple-element.84), channel_id=1, source_target_pairs={{0,8},{4,12},{8,0},{12,4},{16,24},{20,28},{24,16},{28,20},{1,9},{5... | collective-permute-start | bytes 1376264 | tf_op jit(solution)/shard_map/ppermute | solution.py:273
  329.4 29.2 %collective-permute-start.37 = (bf16[128,1792]{1,0:T(8,128)(2,1)}, bf16[128,1792]{1,0:T(8,128)(2,1)}, u32[]{:S(2)}, u32[]{:S(2)}) collective-permute-start(bf16[128,1792]{1,0:T(8,128)(2,1)} %get-tuple-element.85), channel_id=1, source_target_pairs={{0,16},{4,20},{8,24},{12,28},{16,0},{20,4},{24,8},{28,12},{1,17},{... | collective-permute-start | bytes 1376264 | tf_op jit(solution)/shard_map/ppermute | solution.py:273
  330.9 27.7 %collective-permute-start.38 = (bf16[128,1792]{1,0:T(8,128)(2,1)}, bf16[128,1792]{1,0:T(8,128)(2,1)}, u32[]{:S(2)}, u32[]{:S(2)}) collective-permute-start(bf16[128,1792]{1,0:T(8,128)(2,1)} %get-tuple-element.86), channel_id=1, source_target_pairs={{0,24},{4,28},{8,16},{12,20},{16,8},{20,12},{24,0},{28,4},{1,25},{... | collective-permute-start | bytes 1376264 | tf_op jit(solution)/shard_map/ppermute | solution.py:273
  355.0 13.5 %collective-permute-start.30 = (bf16[128,1792]{1,0:T(8,128)(2,1)S(1)}, bf16[128,1792]{1,0:T(8,128)(2,1)S(1)}, u32[]{:S(2)}, u32[]{:S(2)}) collective-permute-start(bf16[128,1792]{1,0:T(8,128)(2,1)S(1)} %get-tuple-element.76), channel_id=1, source_target_pairs={{0,8},{4,12},{8,0},{12,4},{16,24},{20,28},{24,16},{28,20},{1,9},{5... | collective-permute-start | bytes 1376264 | tf_op jit(solution)/shard_map/ppermute | solution.py:273
  356.5 21.7 %collective-permute-start.31 = (bf16[128,1792]{1,0:T(8,128)(2,1)S(1)}, bf16[128,1792]{1,0:T(8,128)(2,1)S(1)}, u32[]{:S(2)}, u32[]{:S(2)}) collective-permute-start(bf16[128,1792]{1,0:T(8,128)(2,1)S(1)} %get-tuple-element.77), channel_id=1, source_target_pairs={{0,16},{4,20},{8,24},{12,28},{16,0},{20,4},{24,8},{28,12},{1,17},{... | collective-permute-start | bytes 1376264 | tf_op jit(solution)/shard_map/ppermute | solution.py:273
  358.0 20.2 %collective-permute-start.32 = (bf16[128,1792]{1,0:T(8,128)(2,1)S(1)}, bf16[128,1792]{1,0:T(8,128)(2,1)S(1)}, u32[]{:S(2)}, u32[]{:S(2)}) collective-permute-start(bf16[128,1792]{1,0:T(8,128)(2,1)S(1)} %get-tuple-element.78), channel_id=1, source_target_pairs={{0,24},{4,28},{8,16},{12,20},{16,8},{20,12},{24,0},{28,4},{1,25},{... | collective-permute-start | bytes 1376264 | tf_op jit(solution)/shard_map/ppermute | solution.py:273
  360.2 21.2 %collective-permute-start.41 = (bf16[32,1792]{1,0:T(8,128)(2,1)S(1)}, bf16[32,1792]{1,0:T(8,128)(2,1)S(1)}, u32[]{:S(2)}, u32[]{:S(2)}) collective-permute-start(bf16[32,1792]{1,0:T(8,128)(2,1)S(1)} %get-tuple-element.99), channel_id=1, source_target_pairs={{0,3},{1,2},{2,1},{3,0},{4,7},{5,6},{6,5},{7,4},{8,11},{9,10},{10,... | collective-permute-start | bytes 344072 | tf_op jit(solution)/shard_map/ppermute | solution.py:279
  362.1 20.8 %collective-permute-start.40 = (bf16[32,1792]{1,0:T(8,128)(2,1)S(1)}, bf16[32,1792]{1,0:T(8,128)(2,1)S(1)}, u32[]{:S(2)}, u32[]{:S(2)}) collective-permute-start(bf16[32,1792]{1,0:T(8,128)(2,1)S(1)} %get-tuple-element.100), channel_id=1, source_target_pairs={{0,2},{1,3},{2,0},{3,1},{4,6},{5,7},{6,4},{7,5},{8,10},{9,11},{10,... | collective-permute-start | bytes 344072 | tf_op jit(solution)/shard_map/ppermute | solution.py:279
  368.5 14.5 %collective-permute-start.39 = (bf16[32,1792]{1,0:T(8,128)(2,1)S(1)}, bf16[32,1792]{1,0:T(8,128)(2,1)S(1)}, u32[]{:S(2)}, u32[]{:S(2)}) collective-permute-start(bf16[32,1792]{1,0:T(8,128)(2,1)S(1)} %get-tuple-element.101), channel_id=1, source_target_pairs={{0,1},{1,0},{2,3},{3,2},{4,5},{5,4},{6,7},{7,6},{8,9},{9,8},{10,11... | collective-permute-start | bytes 344072 | tf_op jit(solution)/shard_map/ppermute | solution.py:279
  378.5 7.9 %collective-permute-start.35 = (bf16[32,1792]{1,0:T(8,128)(2,1)S(1)}, bf16[32,1792]{1,0:T(8,128)(2,1)S(1)}, u32[]{:S(2)}, u32[]{:S(2)}) collective-permute-start(bf16[32,1792]{1,0:T(8,128)(2,1)S(1)} %get-tuple-element.103), channel_id=1, source_target_pairs={{0,3},{1,2},{2,1},{3,0},{4,7},{5,6},{6,5},{7,4},{8,11},{9,10},{10,... | collective-permute-start | bytes 344072 | tf_op jit(solution)/shard_map/ppermute | solution.py:279
  380.8 9.5 %collective-permute-start.34 = (bf16[32,1792]{1,0:T(8,128)(2,1)S(1)}, bf16[32,1792]{1,0:T(8,128)(2,1)S(1)}, u32[]{:S(2)}, u32[]{:S(2)}) collective-permute-start(bf16[32,1792]{1,0:T(8,128)(2,1)S(1)} %get-tuple-element.104), channel_id=1, source_target_pairs={{0,2},{1,3},{2,0},{3,1},{4,6},{5,7},{6,4},{7,5},{8,10},{9,11},{10,... | collective-permute-start | bytes 344072 | tf_op jit(solution)/shard_map/ppermute | solution.py:279
  381.4 8.9 %collective-permute-start.33 = (bf16[32,1792]{1,0:T(8,128)(2,1)S(1)}, bf16[32,1792]{1,0:T(8,128)(2,1)S(1)}, u32[]{:S(2)}, u32[]{:S(2)}) collective-permute-start(bf16[32,1792]{1,0:T(8,128)(2,1)S(1)} %get-tuple-element.105), channel_id=1, source_target_pairs={{0,1},{1,0},{2,3},{3,2},{4,5},{5,4},{6,7},{7,6},{8,9},{9,8},{10,11... | collective-permute-start | bytes 344072 | tf_op jit(solution)/shard_map/ppermute | solution.py:279
  (52 other events, 470.9 us)
Sparse Core Ops, SparseCore 0:
  121.2 27.4 reduce-scatter.8
  199.4 28.3 reduce-scatter.10
  230.1 25.7 reduce-scatter.4
  258.2 25.7 reduce-scatter.6
  285.4 26.5 all-gather.5
  313.5 27.4 all-gather.3

commit v4 on v3

--- a/solution.py
+++ b/solution.py
@@ -7,7 +7,7 @@
 from jax.experimental.pallas import tpu as pltpu
 from jax.sharding import PartitionSpec as P
 
-VMEM_BYTES = 32 * 1024 * 1024
+VMEM_BYTES = 22 * 1024 * 1024
 CORES = 2
 HALVES = 2
 TILE = 256
@@ -144,14 +144,19 @@
     return scratch
 
 
+def rows_of(block, rows):
+    return pl.ds(pl.multiple_of(block * rows, rows), rows)
+
+
 def pick_kernel(chips, blocks, place_ref, ids_ref, *refs):
     toks, refs = refs[:chips], refs[chips:]
     own_ref, pieces, refs = refs[0], refs[1:blocks], refs[blocks:]
-    out_ref, left, held, sems, *staged = refs
+    outs, (left, held, sems, *staged) = refs[:chips], refs[chips:]
     ready = fill(place_ref, own_ref, pieces, held, sems, staged)
-    rows = toks[0].shape[0]
+    level = place_ref[2]
+    rows, slots = ids_ref.shape[1], ids_ref.shape[2]
     for step, tok in enumerate(toks):
-        left[step * rows : (step + 1) * rows, :] = tok[...]
+        left[rows_of(jnp.bitwise_xor(step, level), rows), :] = tok[...]
     experts, _, width = held.shape
     tile = min(TILE, width)
     for start in range(0, width, tile):
@@ -166,26 +171,28 @@
                     preferred_element_type=jnp.float32,
                 )
             )
-        for slot in range(ids_ref.shape[1]):
-            chosen = ids_ref[:, slot : slot + 1]
-            picked = sums[0]
-            for which in range(1, experts):
-                picked = jnp.where(chosen == which, sums[which], picked)
-            first = slot * width + start
-            out_ref[:, first : first + tile] = picked.astype(out_ref.dtype)
+        for step, out_ref in enumerate(outs):
+            ids = ids_ref[jnp.bitwise_xor(step, level)]
+            for slot in range(slots):
+                picked = sums[0][step * rows : (step + 1) * rows]
+                for which in range(1, experts):
+                    other = sums[which][step * rows : (step + 1) * rows]
+                    picked = jnp.where(ids[:, slot : slot + 1] == which, other, picked)
+                first = slot * width + start
+                out_ref[:, first : first + tile] = picked.astype(out_ref.dtype)
 
 
 def picked_sums(place, ids, toks, own, pieces):
-    count, slots = ids.shape
+    chips, rows, slots = ids.shape
     experts, depth, _ = own.shape
     blocks = len(pieces) + 1
     width = pieces[0].shape[2]
-    wide = blocks * depth
-    return pl.pallas_call(
-        functools.partial(pick_kernel, len(toks), blocks),
-        in_specs=[SMEM_SPEC, VMEM_SPEC] + [VMEM_SPEC] * len(toks) + [ANY_SPEC] * blocks,
-        out_specs=VMEM_SPEC,
-        out_shape=bf16(count, slots * width),
+    wide, count = blocks * depth, chips * rows
+    return pl.pallas_call(
+        functools.partial(pick_kernel, chips, blocks),
+        in_specs=[SMEM_SPEC, VMEM_SPEC] + [VMEM_SPEC] * chips + [ANY_SPEC] * blocks,
+        out_specs=[VMEM_SPEC] * chips,
+        out_shape=[bf16(rows, slots * width)] * chips,
         scratch_shapes=[
             pltpu.VMEM((count, wide), jnp.bfloat16),
             *weight_scratch(experts, blocks, depth, width),
@@ -199,20 +206,48 @@
     )(place, ids, *toks, own, *pieces)
 
 
-def down_kernel(chips, blocks, place_ref, ids_ref, hid_ref, *refs):
+def hidden_kernel(terms, place_ref, scores_ref, *refs):
+    gates, ups, out_ref = refs[:terms], refs[terms : 2 * terms], refs[2 * terms]
+    scores = scores_ref[place_ref[2]].astype(jnp.float32)
+    slots = scores.shape[1]
+    combine = scores / jnp.sum(scores, axis=1, keepdims=True)
+    width = out_ref.shape[1] // slots
+    for slot in range(slots):
+        columns = slice(slot * width, (slot + 1) * width)
+        gate_sum = sum(ref[:, columns].astype(jnp.float32) for ref in gates)
+        up_sum = sum(ref[:, columns].astype(jnp.float32) for ref in ups)
+        value = gate_sum / (1.0 + jnp.exp(-gate_sum)) * up_sum * combine[:, slot : slot + 1]
+        out_ref[:, columns] = value.astype(out_ref.dtype)
+
+
+def hidden_rows(place, scores, gates, ups):
+    return pl.pallas_call(
+        functools.partial(hidden_kernel, len(gates)),
+        in_specs=[SMEM_SPEC] + [VMEM_SPEC] * (1 + 2 * len(gates)),
+        out_specs=VMEM_SPEC,
+        out_shape=bf16(*gates[0].shape),
+        compiler_params=PARAMS,
+    )(place, scores, *gates, *ups)
+
+
+def down_kernel(chips, blocks, place_ref, ids_ref, *refs):
+    hids, refs = refs[:chips], refs[chips:]
     own_ref, pieces, refs = refs[0], refs[1:blocks], refs[blocks:]
     outs, (left, held, sems, *staged) = refs[:chips], refs[chips:]
     ready = fill(place_ref, own_ref, pieces, held, sems, staged)
     experts, wide, width = held.shape
-    for which in range(experts):
-        mine = jnp.zeros((hid_ref.shape[0], width), hid_ref.dtype)
-        for slot in range(ids_ref.shape[1]):
-            part = hid_ref[:, slot * width : (slot + 1) * width]
-            mine = jnp.where(ids_ref[:, slot : slot + 1] == which, part, mine)
-        left[which] = mine
+    rows, slots = ids_ref.shape[1], ids_ref.shape[2]
+    for step, hid_ref in enumerate(hids):
+        block = jnp.bitwise_xor(step, place_ref[2])
+        ids = ids_ref[block]
+        for which in range(experts):
+            mine = jnp.zeros((rows, width), hid_ref.dtype)
+            for slot in range(slots):
+                part = hid_ref[:, slot * width : (slot + 1) * width]
+                mine = jnp.where(ids[:, slot : slot + 1] == which, part, mine)
+            left[which, rows_of(block, rows), :] = mine
     for which in range(experts):
         ready(which)
-    rows = outs[0].shape[0]
     for start in range(0, wide, TILE):
         tile = min(TILE, wide - start)
         total = None
@@ -229,28 +264,28 @@
             out_ref[:, start : start + tile] = part.astype(out_ref.dtype)
 
 
-def down_sums(place, ids, hidden, own, pieces):
-    count = ids.shape[0]
+def down_sums(place, ids, hids, own, pieces):
+    chips, rows, slots = ids.shape
     experts, depth, _ = own.shape
     blocks = len(pieces) + 1
     width = pieces[0].shape[2]
-    wide, chips = blocks * depth, blocks // CORES
+    wide, count = blocks * depth, chips * rows
     return pl.pallas_call(
         functools.partial(down_kernel, chips, blocks),
-        in_specs=[SMEM_SPEC, VMEM_SPEC, VMEM_SPEC] + [ANY_SPEC] * blocks,
+        in_specs=[SMEM_SPEC, VMEM_SPEC] + [VMEM_SPEC] * chips + [ANY_SPEC] * blocks,
         out_specs=[VMEM_SPEC] * chips,
-        out_shape=[bf16(count // chips, wide)] * chips,
+        out_shape=[bf16(rows, wide)] * chips,
         scratch_shapes=[
             pltpu.VMEM((experts, count, width), jnp.bfloat16),
             *weight_scratch(experts, blocks, depth, width),
         ],
         cost_estimate=pl.CostEstimate(
             flops=2 * count * wide * width * experts,
-            bytes_accessed=2 * (hidden.size + experts * wide * width + count * wide),
+            bytes_accessed=2 * (count * slots * width + experts * wide * width + count * wide),
             transcendentals=0,
         ),
         compiler_params=PARAMS,
-    )(place, ids, hidden, own, *pieces)
+    )(place, ids, *hids, own, *pieces)
 
 
 def after(values, others):
@@ -290,19 +325,37 @@
     def core_exchange(blocks, same):
         return same + [to_core(value) for value in [blocks[0]] + same]
 
-    gate_blocks = blocks_of(gate_weight)
-    gate_same = chip_exchange(gate_blocks)
-    cut = cut_tokens(place, after(tokens, gate_blocks), n_tensor, depth)
+    def level_sums(parts):
+        terms, bit = [[part] for part in parts], 1
+        while bit < n_tensor:
+            for step in range(n_tensor - bit, 0, -2 * bit):
+                value = terms[step][0]
+                if len(terms[step]) > 1:
+                    value = sum(term.astype(jnp.float32) for term in terms[step])
+                terms[step - bit].append(to_level(value.astype(jnp.bfloat16), bit))
+            bit *= 2
+        return terms[0]
+
+    def level_copies(value):
+        held, bit = {0: value}, n_tensor // 2
+        while bit:
+            for step in sorted(held):
+                held[step + bit] = to_level(held[step], bit)
+            bit //= 2
+        return [held[step] for step in range(n_tensor)]
+
+    routing = jnp.concatenate([expert_ids, gate_scores], axis=1)
+    routing = [routing] + [to_chip(routing, step) for step in range(1, chips)]
+    gate_blocks = after(blocks_of(gate_weight), routing)
+    routing = jnp.stack(routing).reshape(chips, n_tensor, HALVES, rows // HALVES, 2 * slots)
+    routing = routing.transpose(2, 0, 1, 3, 4).reshape(HALVES, chips, -1, 2 * slots)
+    ids, scores = routing[..., :slots], routing[..., slots:]
+
+    cut = cut_tokens(place, tokens, n_tensor, depth)
     cut = [cut[0]] + [to_level(cut[step], step) for step in range(1, n_tensor)]
     groups = group_tokens(place, cut)
+    gate_same = chip_exchange(gate_blocks)
     gate_pieces = core_exchange(gate_blocks, gate_same)
-
-    routing = jnp.concatenate([expert_ids, gate_scores], axis=1)
-    routing = lax.all_gather(routing, "expert", axis=0)
-    order = jnp.stack([(q ^ step) * CORES + c for step in range(chips)])
-    routing = jnp.take(routing, order, axis=0)
-    routing = routing.reshape(chips, n_tensor, HALVES, rows // HALVES, 2 * slots)
-    routing = [routing[:, :, half].reshape(-1, 2 * slots) for half in range(HALVES)]
 
     toks, barrier = [], gate_same
     for half in range(HALVES):
@@ -314,30 +367,21 @@
     down_blocks = after(blocks_of(down_weight), up_pieces)
     down_pieces = core_exchange(down_blocks, chip_exchange(down_blocks))
 
-    sums, part = [], place
+    sums, parts = [], place
     for weight, pieces in ((gate_weight, gate_pieces), (up_weight, up_pieces)):
         for half in range(HALVES):
-            ids = routing[half][:, :slots]
-            part = picked_sums(place, ids, after(toks[half], part), weight, pieces)
-            sums.append(lax.psum_scatter(part, "tensor", scatter_dimension=0, tiled=True))
-    gate_sums, up_sums = sums[:HALVES], sums[HALVES:]
+            left = after(toks[half], parts)
+            parts = picked_sums(place, ids[half], left, weight, pieces)
+            sums.append(level_sums(parts))
 
     hiddens = []
     for half in range(HALVES):
-        count = gate_sums[half].shape[0]
-        scores = routing[half][:, slots:].astype(jnp.float32)
-        scores = lax.dynamic_slice_in_dim(scores, level * count, count, 0)
-        combine = scores / jnp.sum(scores, axis=1, keepdims=True)
-        combine = jnp.repeat(combine, width, axis=1)
-        gate_sum = gate_sums[half].astype(jnp.float32)
-        up_sum = up_sums[half].astype(jnp.float32)
-        hidden = (jax.nn.silu(gate_sum) * up_sum * combine).astype(jnp.bfloat16)
-        hiddens.append(lax.all_gather(hidden, "tensor", axis=0, tiled=True))
+        hidden = hidden_rows(place, scores[half], sums[half], sums[HALVES + half])
+        hiddens.append(level_copies(hidden))
 
     backs = []
     for half in range(HALVES):
-        ids = routing[half][:, :slots]
-        parts = down_sums(place, ids, hiddens[half], down_weight, down_pieces)
+        parts = down_sums(place, ids[half], hiddens[half], down_weight, down_pieces)
         total = parts[0].astype(jnp.float32)
         for step in range(1, chips):
             total = total + to_chip(parts[step], step).astype(jnp.float32)

time: 400 us -> 318 us (0.80)
  waiting for transfers between devices: 191 us -> 149 us
  blocking collectives: 24.6 us -> 0 us
  starting transfers between devices: 44.1 us -> 68.3 us
  local copies, waits for them, and re-layouts: 53.2 us -> 31.7 us
  between operations: 13.9 us -> 0.54 us
    reduce_scatter x4 -> x0, waiting for transfers between devices: 74.9 us -> none  [local(): lax.psum_scatter(part, 'tensor', scatter_dimension=0, tiled=True)]
    ppermute x9 -> x27, waiting for transfers between devices: 19.5 us -> 83.2 us  [to_level(): lax.ppermute(value, 'tensor', [(s, s ^ step) for s in range(n_tensor)])]
    all_gather x2 -> x0, waiting for transfers between devices: 29.4 us -> none  [local(): hiddens.append(lax.all_gather(hidden, 'tensor', axis=0, tiled=True))]
    all_gather x1 -> x0, blocking collectives: 24.6 us -> none  [local(): routing = lax.all_gather(routing, 'expert', axis=0)]
    ppermute x9 -> x27, starting transfers between devices: 16.2 us -> 36.4 us  [to_level(): lax.ppermute(value, 'tensor', [(s, s ^ step) for s in range(n_tensor)])]
    unnamed x106 -> x88, local copies, waits for them, and re-layouts: 38.4 us -> 22.6 us
    pallas_call x2, Pallas kernels: 17.9 us -> 24.1 us  [down_sums(): pl.pallas_call(functools.partial(down_kernel, chips, blocks), in_specs=[S...]
    slice x5 -> x0, local copies, waits for them, and re-layouts: 5.66 us -> none  [the longest x2 3.86 us: local(): scores = routing[half][:, slots:].astype(jnp.float32)]
  transfers between devices with their start and end apart: 48 -> 63, of which waited for: 25 -> 23; matrix products, arithmetic and copies ran while one was open for 5% -> 4% of each run, Pallas kernels for 14% -> 20%
where the time goes in v4:
time: 318 us; the launch traced here: 317 us
  waiting for transfers between devices  149 us (47%)
  starting transfers between devices  68.3 us (21%)
  Pallas kernels  64.2 us (20%)
  local copies, waits for them, and re-layouts  31.7 us (10%)
  other arithmetic  3.56 us (1%)
    ppermute x27, waiting for transfers between devices, to_level(): lax.ppermute(value, 'tensor', [(s, s ^ step) for s in range(n_tensor)])  83.2 us
    ppermute x24, waiting for transfers between devices, to_chip(): return lax.ppermute(value, 'expert', pairs)  65.6 us
    ppermute x27, starting transfers between devices, to_level(): lax.ppermute(value, 'tensor', [(s, s ^ step) for s in range(n_tensor)])  36.4 us
    pallas_call x4, Pallas kernels, picked_sums(): pl.pallas_call(functools.partial(pick_kernel, chips, blocks), in_specs=[S...  34.8 us
    ppermute x24, starting transfers between devices, to_chip(): return lax.ppermute(value, 'expert', pairs)  29.7 us
    pallas_call x2, Pallas kernels, down_sums(): pl.pallas_call(functools.partial(down_kernel, chips, blocks), in_specs=[S...  24.1 us
    unnamed x88, local copies, waits for them, and re-layouts  22.6 us
  transfers between devices with their start and end apart: 63, of which 23 were waited for; matrix products, arithmetic and copies ran while one was open for 4% of the time, Pallas kernels for 20%

profile of v4, /device:TPU:0, one launch (start us, length us, event | category | flops | bytes accessed | tf_op | source)
XLA Modules:
  0.0 317.1 jit_solution(8894522912237661479)
XLA Ops:
  0.7 3.9 %collective-permute-start.2 = (s32[256,4]{0,1:T(4,128)S(1)}, s32[256,4]{0,1:T(4,128)S(1)}, u32[]{:S(2)}, u32[]{:S(2)}) collective-permute-start(s32[256,4]{0,1:T(4,128)S(1)} %pad_add_fusion), channel_id=1, source_target_pairs={{0,24},{4,28},{8,16},{12,20},{16,8},{20,12},{24,0},{28,4},{1,25},{... | collective-permute-start | bytes 12296 | tf_op jit(solution)/shard_map/ppermute | solution.py:308
  5.2 3.5 %constant_dynamic-slice_fusion.8 = (bf16[3,224,512]{2,1,0:T(8,128)(2,1)}, bf16[3,224,512]{2,1,0:T(8,128)(2,1)}, bf16[3,224,512]{2,1,0:T(8,128)(2,1)}, bf16[3,224,512]{2,1,0:T(8,128)(2,1)}) fusion(bf16[3,224,2048]{2,1,0:T(8,128)(2,1)} %refs_4_.7, s32[]{:T(128)S(6)} %select_n.53, s32[]{:T(128)S(6)} %select_n.52, s32[]{:T(128)S(6)} %select_n.51, s32[]{:T(128)S(6)} %select_n.50), kind=kLoop, calls=%fused_computation.27 | loop fusion | bytes 5505040 | tf_op jit(solution)/shard_map/dynamic_slice | solution.py:318
  8.8 2.0 collective-permute-start.6
  14.5 2.1 collective-permute-start.3
  16.6 2.6 collective-permute-start.4
  19.1 5.5 %collective-permute-done.3.refs_1_ = bf16[64,1792]{1,0:T(8,128)(2,1)S(1)} collective-permute-done((bf16[64,1792]{1,0:T(8,128)(2,1)S(1)}, bf16[64,1792]{1,0:T(8,128)(2,1)S(1)}, u32[]{:S(2)}, u32[]{:S(2)}) %collective-permute-start.3) | collective-permute-done | bytes 229408 | tf_op jit(solution)/shard_map/ppermute | solution.py:314
  24.6 3.2 %collective-permute-start.5 = (bf16[64,1792]{1,0:T(8,128)(2,1)S(1)}, bf16[64,1792]{1,0:T(8,128)(2,1)S(1)}, u32[]{:S(2)}, u32[]{:S(2)}) collective-permute-start(bf16[64,1792]{1,0:T(8,128)(2,1)S(1)} %get-tuple-element.68), channel_id=1, source_target_pairs={{0,3},{1,2},{2,1},{3,0},{4,7},{5,6},{6,5},{7,4},{8,11},{9,10},{10,... | collective-permute-start | bytes 688136 | tf_op jit(solution)/shard_map/ppermute | solution.py:314
  27.8 5.8 %collective-permute-done.4.refs_2_ = bf16[64,1792]{1,0:T(8,128)(2,1)S(1)} collective-permute-done((bf16[64,1792]{1,0:T(8,128)(2,1)S(1)}, bf16[64,1792]{1,0:T(8,128)(2,1)S(1)}, u32[]{:S(2)}, u32[]{:S(2)}) %collective-permute-start.4) | collective-permute-done | bytes 229408 | tf_op jit(solution)/shard_map/ppermute | solution.py:314
  34.3 7.5 %collective-permute-done.7.refs_6_ = bf16[3,224,512]{2,1,0:T(8,128)(2,1)} collective-permute-done((bf16[3,224,512]{2,1,0:T(8,128)(2,1)}, bf16[3,224,512]{2,1,0:T(8,128)(2,1)}, u32[]{:S(2)}, u32[]{:S(2)}) %collective-permute-start.7) | collective-permute-done | bytes 688160 | tf_op jit(solution)/shard_map/ppermute | solution.py:308
  45.3 10.9 %collective-permute-done.11.refs_3_ = bf16[128,1792]{1,0:T(8,128)(2,1)S(1)} collective-permute-done((bf16[128,1792]{1,0:T(8,128)(2,1)S(1)}, bf16[128,1792]{1,0:T(8,128)(2,1)S(1)}, u32[]{:S(2)}, u32[]{:S(2)}) %collective-permute-start.11) | collective-permute-done | bytes 458784 | tf_op jit(solution)/shard_map/ppermute | solution.py:308
  57.0 5.9 %collective-permute-done.10.refs_2_ = bf16[128,1792]{1,0:T(8,128)(2,1)S(1)} collective-permute-done((bf16[128,1792]{1,0:T(8,128)(2,1)S(1)}, bf16[128,1792]{1,0:T(8,128)(2,1)S(1)}, u32[]{:S(2)}, u32[]{:S(2)}) %collective-permute-start.10) | collective-permute-done | bytes 458784 | tf_op jit(solution)/shard_map/ppermute | solution.py:308
  68.5 10.3 %collective-permute-done.21.refs_3_ = bf16[128,1792]{1,0:T(8,128)(2,1)S(1)} collective-permute-done((bf16[128,1792]{1,0:T(8,128)(2,1)S(1)}, bf16[128,1792]{1,0:T(8,128)(2,1)S(1)}, u32[]{:S(2)}, u32[]{:S(2)}) %collective-permute-start.21) | collective-permute-done | bytes 458784 | tf_op jit(solution)/shard_map/ppermute | solution.py:308
  79.6 8.1 %collective-permute-done.20.refs_2_ = bf16[128,1792]{1,0:T(8,128)(2,1)S(1)} collective-permute-done((bf16[128,1792]{1,0:T(8,128)(2,1)S(1)}, bf16[128,1792]{1,0:T(8,128)(2,1)S(1)}, u32[]{:S(2)}, u32[]{:S(2)}) %collective-permute-start.20) | collective-permute-done | bytes 458784 | tf_op jit(solution)/shard_map/ppermute | solution.py:308
  88.4 1.7 constant_dynamic-slice_fusion.4
  106.8 8.2 %shard_map.66 = (bf16[128,1024]{1,0:T(8,128)(2,1)S(1)}, bf16[128,1024]{1,0:T(8,128)(2,1)S(1)}, bf16[128,1024]{1,0:T(8,128)(2,1)S(1)}, bf16[128,1024]{1,0:T(8,128)(2,1)S(1)}) custom-call(s32[3]{0:T(128)S(1)} %pad_add_fusion.1.place_ref, s32[4,128,2]{2,1,0:T(8,128)S(1)} %get-tuple-element.140.ids_ref, bf16[128,1792]{1,0:T(8,128)(2,1)S(1)} %copy-done.30, ...), custom_call_target="tpu_custom_call" | custom-call | flops 2818572288 | bytes 8388608 | tf_op jit(solution)/shard_map/pallas_call | solution.py:191
  115.0 1.6 collective-permute-start.17
  117.1 7.6 %collective-permute-done.23.refs_6_ = bf16[3,224,512]{2,1,0:T(8,128)(2,1)} collective-permute-done((bf16[3,224,512]{2,1,0:T(8,128)(2,1)}, bf16[3,224,512]{2,1,0:T(8,128)(2,1)}, u32[]{:S(2)}, u32[]{:S(2)}) %collective-permute-start.23) | collective-permute-done | bytes 688160 | tf_op jit(solution)/shard_map/ppermute | solution.py:308
  125.3 8.0 %shard_map.67 = (bf16[128,1024]{1,0:T(8,128)(2,1)S(1)}, bf16[128,1024]{1,0:T(8,128)(2,1)S(1)}, bf16[128,1024]{1,0:T(8,128)(2,1)S(1)}, bf16[128,1024]{1,0:T(8,128)(2,1)S(1)}) custom-call(s32[3]{0:T(128)S(1)} %pad_add_fusion.1.place_ref, s32[4,128,2]{2,1,0:T(8,128)S(1)} %get-tuple-element.138.ids_ref, bf16[128,1792]{1,0:T(8,128)(2,1)S(1)} %copy-done.28, ...), custom_call_target="tpu_custom_call" | custom-call | flops 2818572288 | bytes 8388608 | tf_op jit(solution)/shard_map/pallas_call | solution.py:191
  135.0 6.7 %collective-permute-done.49 = bf16[128,1024]{1,0:T(8,128)(2,1)S(1)} collective-permute-done((bf16[128,1024]{1,0:T(8,128)(2,1)S(1)}, bf16[128,1024]{1,0:T(8,128)(2,1)S(1)}, u32[]{:S(2)}, u32[]{:S(2)}) %collective-permute-start.49) | collective-permute-done | bytes 262176 | tf_op jit(solution)/shard_map/ppermute | solution.py:314
  143.8 2.5 collective-permute-start.18
  146.7 9.2 %shard_map.68 = (bf16[128,1024]{1,0:T(8,128)(2,1)S(1)}, bf16[128,1024]{1,0:T(8,128)(2,1)S(1)}, bf16[128,1024]{1,0:T(8,128)(2,1)S(1)}, bf16[128,1024]{1,0:T(8,128)(2,1)S(1)}) custom-call(s32[3]{0:T(128)S(1)} %pad_add_fusion.1.place_ref, s32[4,128,2]{2,1,0:T(8,128)S(1)} %get-tuple-element.140.ids_ref, bf16[128,1792]{1,0:T(8,128)(2,1)S(1)} %copy-done.30, ...), custom_call_target="tpu_custom_call" | custom-call | flops 2818572288 | bytes 8388608 | tf_op jit(solution)/shard_map/pallas_call | solution.py:191
  156.0 9.4 %shard_map.71 = (bf16[128,1024]{1,0:T(8,128)(2,1)S(1)}, bf16[128,1024]{1,0:T(8,128)(2,1)S(1)}, bf16[128,1024]{1,0:T(8,128)(2,1)S(1)}, bf16[128,1024]{1,0:T(8,128)(2,1)S(1)}) custom-call(s32[3]{0:T(128)S(1)} %pad_add_fusion.1.place_ref, s32[4,128,2]{2,1,0:T(8,128)S(1)} %get-tuple-element.138.ids_ref, bf16[128,1792]{1,0:T(8,128)(2,1)S(1)} %copy-done.28, ...), custom_call_target="tpu_custom_call" | custom-call | flops 2818572288 | bytes 8388608 | tf_op jit(solution)/shard_map/pallas_call | solution.py:191
  169.4 1.8 collective-permute-start.35
  171.7 3.1 collective-permute-done.51.refs_4_
  174.7 1.7 collective-permute-start.37
  176.5 3.9 %collective-permute-done.52 = bf16[128,1024]{1,0:T(8,128)(2,1)S(1)} collective-permute-done((bf16[128,1024]{1,0:T(8,128)(2,1)S(1)}, bf16[128,1024]{1,0:T(8,128)(2,1)S(1)}, u32[]{:S(2)}, u32[]{:S(2)}) %collective-permute-start.52) | collective-permute-done | bytes 262176 | tf_op jit(solution)/shard_map/ppermute | solution.py:314
  181.8 4.1 %collective-permute-done.29.refs_4_ = bf16[128,1024]{1,0:T(8,128)(2,1)S(1)} collective-permute-done((bf16[128,1024]{1,0:T(8,128)(2,1)S(1)}, bf16[128,1024]{1,0:T(8,128)(2,1)S(1)}, u32[]{:S(2)}, u32[]{:S(2)}) %collective-permute-start.29) | collective-permute-done | bytes 262176 | tf_op jit(solution)/shard_map/ppermute | solution.py:314
  186.0 3.1 collective-permute-done.30
  189.1 3.4 %collective-permute-start.53 = (bf16[128,1024]{1,0:T(8,128)(2,1)S(1)}, bf16[128,1024]{1,0:T(8,128)(2,1)S(1)}, u32[]{:S(2)}, u32[]{:S(2)}) collective-permute-start(bf16[128,1024]{1,0:T(8,128)(2,1)S(1)} %add_convert_fusion.2), channel_id=1, source_target_pairs={{0,2},{1,3},{2,0},{3,1},{4,6},{5,7},{6,4},{7,5},{8,10},{9,11},{10,... | collective-permute-start | bytes 786440 | tf_op jit(solution)/shard_map/ppermute | solution.py:314
  192.6 11.4 %collective-permute-done.53.refs_5_ = bf16[128,1024]{1,0:T(8,128)(2,1)S(1)} collective-permute-done((bf16[128,1024]{1,0:T(8,128)(2,1)S(1)}, bf16[128,1024]{1,0:T(8,128)(2,1)S(1)}, u32[]{:S(2)}, u32[]{:S(2)}) %collective-permute-start.53) | collective-permute-done | bytes 262176 | tf_op jit(solution)/shard_map/ppermute | solution.py:314
  205.7 11.9 %collective-permute-done.31.refs_5_ = bf16[128,1024]{1,0:T(8,128)(2,1)S(1)} collective-permute-done((bf16[128,1024]{1,0:T(8,128)(2,1)S(1)}, bf16[128,1024]{1,0:T(8,128)(2,1)S(1)}, u32[]{:S(2)}, u32[]{:S(2)}) %collective-permute-start.31) | collective-permute-done | bytes 262176 | tf_op jit(solution)/shard_map/ppermute | solution.py:314
  217.6 1.8 collective-permute-start.54
  220.3 10.0 %collective-permute-done.55.refs_2_ = bf16[128,1024]{1,0:T(8,128)(2,1)S(1)} collective-permute-done((bf16[128,1024]{1,0:T(8,128)(2,1)S(1)}, bf16[128,1024]{1,0:T(8,128)(2,1)S(1)}, u32[]{:S(2)}, u32[]{:S(2)}) %collective-permute-start.55) | collective-permute-done | bytes 262176 | tf_op jit(solution)/shard_map/ppermute | solution.py:314
  230.4 1.7 collective-permute-start.56
  232.0 11.7 %collective-permute-done.33.refs_2_ = bf16[128,1024]{1,0:T(8,128)(2,1)} collective-permute-done((bf16[128,1024]{1,0:T(8,128)(2,1)S(1)}, bf16[128,1024]{1,0:T(8,128)(2,1)}, u32[]{:S(2)}, u32[]{:S(2)}) %collective-permute-start.33) | collective-permute-done | bytes 262176 | tf_op jit(solution)/shard_map/ppermute | solution.py:314
  243.8 2.0 collective-permute-start.34
  245.8 12.2 %shard_map.73 = (bf16[128,1792]{1,0:T(8,128)(2,1)S(1)}, bf16[128,1792]{1,0:T(8,128)(2,1)}, bf16[128,1792]{1,0:T(8,128)(2,1)}, bf16[128,1792]{1,0:T(8,128)(2,1)}) custom-call(s32[3]{0:T(128)S(1)} %pad_add_fusion.1.place_ref, s32[4,128,2]{2,1,0:T(8,128)S(1)} %get-tuple-element.138.ids_ref, bf16[128,1024]{1,0:T(8,128)(2,1)S(1)} %shard_map.72.refs_0_, ...), custom_call_target="tpu_custom_call" | custom-call | flops 2818572288 | bytes 8388608 | tf_op jit(solution)/shard_map/pallas_call | solution.py:273
  258.1 1.8 collective-permute-start.57
  270.3 11.9 %shard_map.70 = (bf16[128,1792]{1,0:T(8,128)(2,1)S(1)}, bf16[128,1792]{1,0:T(8,128)(2,1)S(1)}, bf16[128,1792]{1,0:T(8,128)(2,1)S(1)}, bf16[128,1792]{1,0:T(8,128)(2,1)S(1)}) custom-call(s32[3]{0:T(128)S(1)} %pad_add_fusion.1.place_ref, s32[4,128,2]{2,1,0:T(8,128)S(1)} %copy-done.6, bf16[128,1024]{1,0:T(8,128)(2,1)S(1)} %shard_map.69.refs_0_, ...), custom_call_target="tpu_custom_call" | custom-call | flops 2818572288 | bytes 8388608 | tf_op jit(solution)/shard_map/pallas_call | solution.py:273
  282.2 1.8 collective-permute-start.42
  287.4 1.9 collective-permute-start.62
  289.3 6.5 %collective-permute-done.42 = bf16[128,1792]{1,0:T(8,128)(2,1)S(1)} collective-permute-done((bf16[128,1792]{1,0:T(8,128)(2,1)S(1)}, bf16[128,1792]{1,0:T(8,128)(2,1)S(1)}, u32[]{:S(2)}, u32[]{:S(2)}) %collective-permute-start.42) | collective-permute-done | bytes 458784 | tf_op jit(solution)/shard_map/ppermute | solution.py:308
  295.8 8.7 %collective-permute-done.43 = bf16[128,1792]{1,0:T(8,128)(2,1)S(1)} collective-permute-done((bf16[128,1792]{1,0:T(8,128)(2,1)S(1)}, bf16[128,1792]{1,0:T(8,128)(2,1)S(1)}, u32[]{:S(2)}, u32[]{:S(2)}) %collective-permute-start.43) | collective-permute-done | bytes 458784 | tf_op jit(solution)/shard_map/ppermute | solution.py:308
  304.8 1.9 collective-permute-start.47
  306.7 2.6 collective-permute-start.45
  309.3 2.5 collective-permute-done.47.refs_3_
  311.8 3.5 %collective-permute-done.46.refs_2_ = bf16[32,1792]{1,0:T(8,128)(2,1)S(1)} collective-permute-done((bf16[32,1792]{1,0:T(8,128)(2,1)S(1)}, bf16[32,1792]{1,0:T(8,128)(2,1)S(1)}, u32[]{:S(2)}, u32[]{:S(2)}) %collective-permute-start.46) | collective-permute-done | bytes 114720 | tf_op jit(solution)/shard_map/ppermute | solution.py:314
  315.2 1.8 shard_map.74
  (201 shorter events, 61.9 us)
Async XLA Ops:
  8.8 25.5 %collective-permute-start.6 = (bf16[3,224,512]{2,1,0:T(8,128)(2,1)}, bf16[3,224,512]{2,1,0:T(8,128)(2,1)S(1)}, u32[]{:S(2)}, u32[]{:S(2)}) collective-permute-start(bf16[3,224,512]{2,1,0:T(8,128)(2,1)} %get-tuple-element.70), channel_id=1, source_target_pairs={{0,8},{4,12},{8,0},{12,4},{16,24},{20,28},{24,16},{28,20},{1,9},{5... | collective-permute-start | bytes 2064392 | tf_op jit(solution)/shard_map/ppermute | solution.py:308
  10.7 31.1 %collective-permute-start.7 = (bf16[3,224,512]{2,1,0:T(8,128)(2,1)}, bf16[3,224,512]{2,1,0:T(8,128)(2,1)}, u32[]{:S(2)}, u32[]{:S(2)}) collective-permute-start(bf16[3,224,512]{2,1,0:T(8,128)(2,1)} %get-tuple-element.71), channel_id=1, source_target_pairs={{0,16},{4,20},{8,24},{12,28},{16,0},{20,4},{24,8},{28,12},{1,17},{... | collective-permute-start | bytes 2064392 | tf_op jit(solution)/shard_map/ppermute | solution.py:308
  12.2 29.6 %collective-permute-start.8 = (bf16[3,224,512]{2,1,0:T(8,128)(2,1)}, bf16[3,224,512]{2,1,0:T(8,128)(2,1)}, u32[]{:S(2)}, u32[]{:S(2)}) collective-permute-start(bf16[3,224,512]{2,1,0:T(8,128)(2,1)} %get-tuple-element.72), channel_id=1, source_target_pairs={{0,24},{4,28},{8,16},{12,20},{16,8},{20,12},{24,0},{28,4},{1,25},{... | collective-permute-start | bytes 2064392 | tf_op jit(solution)/shard_map/ppermute | solution.py:308
  16.6 17.1 %collective-permute-start.4 = (bf16[64,1792]{1,0:T(8,128)(2,1)S(1)}, bf16[64,1792]{1,0:T(8,128)(2,1)S(1)}, u32[]{:S(2)}, u32[]{:S(2)}) collective-permute-start(bf16[64,1792]{1,0:T(8,128)(2,1)S(1)} %get-tuple-element.67), channel_id=1, source_target_pairs={{0,2},{1,3},{2,0},{3,1},{4,6},{5,7},{6,4},{7,5},{8,10},{9,11},{10,... | collective-permute-start | bytes 688136 | tf_op jit(solution)/shard_map/ppermute | solution.py:314
  41.9 14.4 %collective-permute-start.11 = (bf16[128,1792]{1,0:T(8,128)(2,1)S(1)}, bf16[128,1792]{1,0:T(8,128)(2,1)S(1)}, u32[]{:S(2)}, u32[]{:S(2)}) collective-permute-start(bf16[128,1792]{1,0:T(8,128)(2,1)S(1)} %get-tuple-element.93.refs_0_), channel_id=1, source_target_pairs={{0,24},{4,28},{8,16},{12,20},{16,8},{20,12},{24,0},{28,4},{1,25},{... | collective-permute-start | bytes 1376264 | tf_op jit(solution)/shard_map/ppermute | solution.py:308
  43.3 19.5 %collective-permute-start.10 = (bf16[128,1792]{1,0:T(8,128)(2,1)S(1)}, bf16[128,1792]{1,0:T(8,128)(2,1)S(1)}, u32[]{:S(2)}, u32[]{:S(2)}) collective-permute-start(bf16[128,1792]{1,0:T(8,128)(2,1)S(1)} %get-tuple-element.93.refs_0_), channel_id=1, source_target_pairs={{0,16},{4,20},{8,24},{12,28},{16,0},{20,4},{24,8},{28,12},{1,17},{... | collective-permute-start | bytes 1376264 | tf_op jit(solution)/shard_map/ppermute | solution.py:308
  44.5 19.1 %collective-permute-start.9 = (bf16[128,1792]{1,0:T(8,128)(2,1)S(1)}, bf16[128,1792]{1,0:T(8,128)(2,1)S(1)}, u32[]{:S(2)}, u32[]{:S(2)}) collective-permute-start(bf16[128,1792]{1,0:T(8,128)(2,1)S(1)} %get-tuple-element.93.refs_0_), channel_id=1, source_target_pairs={{0,8},{4,12},{8,0},{12,4},{16,24},{20,28},{24,16},{28,20},{1,9},{5... | collective-permute-start | bytes 1376264 | tf_op jit(solution)/shard_map/ppermute | solution.py:308
  64.5 14.3 %collective-permute-start.21 = (bf16[128,1792]{1,0:T(8,128)(2,1)S(1)}, bf16[128,1792]{1,0:T(8,128)(2,1)S(1)}, u32[]{:S(2)}, u32[]{:S(2)}) collective-permute-start(bf16[128,1792]{1,0:T(8,128)(2,1)S(1)} %get-tuple-element.113.refs_0_), channel_id=1, source_target_pairs={{0,24},{4,28},{8,16},{12,20},{16,8},{20,12},{24,0},{28,4},{1,25},{... | collective-permute-start | bytes 1376264 | tf_op jit(solution)/shard_map/ppermute | solution.py:308
  65.9 21.7 %collective-permute-start.20 = (bf16[128,1792]{1,0:T(8,128)(2,1)S(1)}, bf16[128,1792]{1,0:T(8,128)(2,1)S(1)}, u32[]{:S(2)}, u32[]{:S(2)}) collective-permute-start(bf16[128,1792]{1,0:T(8,128)(2,1)S(1)} %get-tuple-element.113.refs_0_), channel_id=1, source_target_pairs={{0,16},{4,20},{8,24},{12,28},{16,0},{20,4},{24,8},{28,12},{1,17},{... | collective-permute-start | bytes 1376264 | tf_op jit(solution)/shard_map/ppermute | solution.py:308
  66.9 24.4 %collective-permute-start.12 = (bf16[3,224,512]{2,1,0:T(8,128)(2,1)}, bf16[3,224,512]{2,1,0:T(8,128)(2,1)S(1)}, u32[]{:S(2)}, u32[]{:S(2)}) collective-permute-start(bf16[3,224,512]{2,1,0:T(8,128)(2,1)} %get-tuple-element.78), channel_id=1, source_target_pairs={{0,4},{4,0},{8,12},{12,8},{16,20},{20,16},{24,28},{28,24},{1,5},{5... | collective-permute-start | bytes 2064392 | tf_op jit(solution)/shard_map/ppermute | solution.py:311
  66.9 26.9 %collective-permute-start.13 = (bf16[3,224,512]{2,1,0:T(8,128)(2,1)S(1)}, bf16[3,224,512]{2,1,0:T(8,128)(2,1)S(1)}, u32[]{:S(2)}, u32[]{:S(2)}) collective-permute-start(bf16[3,224,512]{2,1,0:T(8,128)(2,1)S(1)} %collective-permute-done.6.refs_5_), channel_id=1, source_target_pairs={{0,4},{4,0},{8,12},{12,8},{16,20},{20,16},{24,28},{28,24},{1,5},{5... | collective-permute-start | bytes 2064392 | tf_op jit(solution)/shard_map/ppermute | solution.py:311
  67.4 22.7 %collective-permute-start.19 = (bf16[128,1792]{1,0:T(8,128)(2,1)S(1)}, bf16[128,1792]{1,0:T(8,128)(2,1)S(1)}, u32[]{:S(2)}, u32[]{:S(2)}) collective-permute-start(bf16[128,1792]{1,0:T(8,128)(2,1)S(1)} %get-tuple-element.113.refs_0_), channel_id=1, source_target_pairs={{0,8},{4,12},{8,0},{12,4},{16,24},{20,28},{24,16},{28,20},{1,9},{5... | collective-permute-start | bytes 1376264 | tf_op jit(solution)/shard_map/ppermute | solution.py:308
  79.6 20.8 %collective-permute-start.14 = (bf16[3,224,512]{2,1,0:T(8,128)(2,1)}, bf16[3,224,512]{2,1,0:T(8,128)(2,1)}, u32[]{:S(2)}, u32[]{:S(2)}) collective-permute-start(bf16[3,224,512]{2,1,0:T(8,128)(2,1)} %collective-permute-done.7.refs_6_), channel_id=1, source_target_pairs={{0,4},{4,0},{8,12},{12,8},{16,20},{20,16},{24,28},{28,24},{1,5},{5... | collective-permute-start | bytes 2064392 | tf_op jit(solution)/shard_map/ppermute | solution.py:311
  90.9 25.7 %collective-permute-start.22 = (bf16[3,224,512]{2,1,0:T(8,128)(2,1)}, bf16[3,224,512]{2,1,0:T(8,128)(2,1)}, u32[]{:S(2)}, u32[]{:S(2)}) collective-permute-start(bf16[3,224,512]{2,1,0:T(8,128)(2,1)} %get-tuple-element.97), channel_id=1, source_target_pairs={{0,8},{4,12},{8,0},{12,4},{16,24},{20,28},{24,16},{28,20},{1,9},{5... | collective-permute-start | bytes 2064392 | tf_op jit(solution)/shard_map/ppermute | solution.py:308
  92.1 32.6 %collective-permute-start.23 = (bf16[3,224,512]{2,1,0:T(8,128)(2,1)}, bf16[3,224,512]{2,1,0:T(8,128)(2,1)}, u32[]{:S(2)}, u32[]{:S(2)}) collective-permute-start(bf16[3,224,512]{2,1,0:T(8,128)(2,1)} %get-tuple-element.98), channel_id=1, source_target_pairs={{0,16},{4,20},{8,24},{12,28},{16,0},{20,4},{24,8},{28,12},{1,17},{... | collective-permute-start | bytes 2064392 | tf_op jit(solution)/shard_map/ppermute | solution.py:308
  94.6 30.1 %collective-permute-start.24 = (bf16[3,224,512]{2,1,0:T(8,128)(2,1)}, bf16[3,224,512]{2,1,0:T(8,128)(2,1)}, u32[]{:S(2)}, u32[]{:S(2)}) collective-permute-start(bf16[3,224,512]{2,1,0:T(8,128)(2,1)} %get-tuple-element.99), channel_id=1, source_target_pairs={{0,24},{4,28},{8,16},{12,20},{16,8},{20,12},{24,0},{28,4},{1,25},{... | collective-permute-start | bytes 2064392 | tf_op jit(solution)/shard_map/ppermute | solution.py:308
  115.0 18.4 %collective-permute-start.17 = (bf16[128,1024]{1,0:T(8,128)(2,1)S(1)}, bf16[128,1024]{1,0:T(8,128)(2,1)S(1)}, u32[]{:S(2)}, u32[]{:S(2)}) collective-permute-start(bf16[128,1024]{1,0:T(8,128)(2,1)S(1)} %get-tuple-element.82), channel_id=1, source_target_pairs={{0,1},{1,0},{2,3},{3,2},{4,5},{5,4},{6,7},{7,6},{8,9},{9,8},{10,11... | collective-permute-start | bytes 786440 | tf_op jit(solution)/shard_map/ppermute | solution.py:314
  116.6 26.6 %collective-permute-start.25 = (bf16[3,224,512]{2,1,0:T(8,128)(2,1)S(1)}, bf16[3,224,512]{2,1,0:T(8,128)(2,1)S(1)}, u32[]{:S(2)}, u32[]{:S(2)}) collective-permute-start(bf16[3,224,512]{2,1,0:T(8,128)(2,1)S(1)} %copy-done.43), channel_id=1, source_target_pairs={{0,4},{4,0},{8,12},{12,8},{16,20},{20,16},{24,28},{28,24},{1,5},{5... | collective-permute-start | bytes 2064392 | tf_op jit(solution)/shard_map/ppermute | solution.py:311
  116.6 27.2 %collective-permute-start.26 = (bf16[3,224,512]{2,1,0:T(8,128)(2,1)}, bf16[3,224,512]{2,1,0:T(8,128)(2,1)S(1)}, u32[]{:S(2)}, u32[]{:S(2)}) collective-permute-start(bf16[3,224,512]{2,1,0:T(8,128)(2,1)} %collective-permute-done.22.refs_5_), channel_id=1, source_target_pairs={{0,4},{4,0},{8,12},{12,8},{16,20},{20,16},{24,28},{28,24},{1,5},{5... | collective-permute-start | bytes 2064392 | tf_op jit(solution)/shard_map/ppermute | solution.py:311
  124.7 21.6 %collective-permute-start.27 = (bf16[3,224,512]{2,1,0:T(8,128)(2,1)}, bf16[3,224,512]{2,1,0:T(8,128)(2,1)S(1)}, u32[]{:S(2)}, u32[]{:S(2)}) collective-permute-start(bf16[3,224,512]{2,1,0:T(8,128)(2,1)} %collective-permute-done.23.refs_6_), channel_id=1, source_target_pairs={{0,4},{4,0},{8,12},{12,8},{16,20},{20,16},{24,28},{28,24},{1,5},{5... | collective-permute-start | bytes 2064392 | tf_op jit(solution)/shard_map/ppermute | solution.py:311
  124.7 22.0 %collective-permute-start.28 = (bf16[3,224,512]{2,1,0:T(8,128)(2,1)}, bf16[3,224,512]{2,1,0:T(8,128)(2,1)S(1)}, u32[]{:S(2)}, u32[]{:S(2)}) collective-permute-start(bf16[3,224,512]{2,1,0:T(8,128)(2,1)} %collective-permute-done.24.refs_7_), channel_id=1, source_target_pairs={{0,4},{4,0},{8,12},{12,8},{16,20},{20,16},{24,28},{28,24},{1,5},{5... | collective-permute-start | bytes 2064392 | tf_op jit(solution)/shard_map/ppermute | solution.py:311
  141.6 25.4 %collective-permute-start.16 = (bf16[128,1024]{1,0:T(8,128)(2,1)S(1)}, bf16[128,1024]{1,0:T(8,128)(2,1)S(1)}, u32[]{:S(2)}, u32[]{:S(2)}) collective-permute-start(bf16[128,1024]{1,0:T(8,128)(2,1)S(1)} %get-tuple-element.80), channel_id=1, source_target_pairs={{0,1},{1,0},{2,3},{3,2},{4,5},{5,4},{6,7},{7,6},{8,9},{9,8},{10,11... | collective-permute-start | bytes 786440 | tf_op jit(solution)/shard_map/ppermute | solution.py:314
  143.2 24.3 %collective-permute-start.48 = (bf16[128,1024]{1,0:T(8,128)(2,1)S(1)}, bf16[128,1024]{1,0:T(8,128)(2,1)S(1)}, u32[]{:S(2)}, u32[]{:S(2)}) collective-permute-start(bf16[128,1024]{1,0:T(8,128)(2,1)S(1)} %get-tuple-element.90), channel_id=1, source_target_pairs={{0,1},{1,0},{2,3},{3,2},{4,5},{5,4},{6,7},{7,6},{8,9},{9,8},{10,11... | collective-permute-start | bytes 786440 | tf_op jit(solution)/shard_map/ppermute | solution.py:314
  143.8 25.6 %collective-permute-start.18 = (bf16[128,1024]{1,0:T(8,128)(2,1)S(1)}, bf16[128,1024]{1,0:T(8,128)(2,1)S(1)}, u32[]{:S(2)}, u32[]{:S(2)}) collective-permute-start(bf16[128,1024]{1,0:T(8,128)(2,1)S(1)} %add_convert_fusion.5), channel_id=1, source_target_pairs={{0,2},{1,3},{2,0},{3,1},{4,6},{5,7},{6,4},{7,5},{8,10},{9,11},{10,... | collective-permute-start | bytes 786440 | tf_op jit(solution)/shard_map/ppermute | solution.py:314
  146.3 24.8 %collective-permute-start.50 = (bf16[128,1024]{1,0:T(8,128)(2,1)S(1)}, bf16[128,1024]{1,0:T(8,128)(2,1)S(1)}, u32[]{:S(2)}, u32[]{:S(2)}) collective-permute-start(bf16[128,1024]{1,0:T(8,128)(2,1)S(1)} %add_convert_fusion.3), channel_id=1, source_target_pairs={{0,2},{1,3},{2,0},{3,1},{4,6},{5,7},{6,4},{7,5},{8,10},{9,11},{10,... | collective-permute-start | bytes 786440 | tf_op jit(solution)/shard_map/ppermute | solution.py:314
  167.5 18.4 %collective-permute-start.29 = (bf16[128,1024]{1,0:T(8,128)(2,1)S(1)}, bf16[128,1024]{1,0:T(8,128)(2,1)S(1)}, u32[]{:S(2)}, u32[]{:S(2)}) collective-permute-start(bf16[128,1024]{1,0:T(8,128)(2,1)S(1)} %get-tuple-element.102), channel_id=1, source_target_pairs={{0,1},{1,0},{2,3},{3,2},{4,5},{5,4},{6,7},{7,6},{8,9},{9,8},{10,11... | collective-permute-start | bytes 786440 | tf_op jit(solution)/shard_map/ppermute | solution.py:314
  169.4 34.7 %collective-permute-start.35 = (bf16[3,224,512]{2,1,0:T(8,128)(2,1)S(1)}, bf16[3,224,512]{2,1,0:T(8,128)(2,1)S(1)}, u32[]{:S(2)}, u32[]{:S(2)}) collective-permute-start(bf16[3,224,512]{2,1,0:T(8,128)(2,1)S(1)} %get-tuple-element.105), channel_id=1, source_target_pairs={{0,8},{4,12},{8,0},{12,4},{16,24},{20,28},{24,16},{28,20},{1,9},{5... | collective-permute-start | bytes 2064392 | tf_op jit(solution)/shard_map/ppermute | solution.py:308
  171.2 33.0 %collective-permute-start.36 = (bf16[3,224,512]{2,1,0:T(8,128)(2,1)S(1)}, bf16[3,224,512]{2,1,0:T(8,128)(2,1)S(1)}, u32[]{:S(2)}, u32[]{:S(2)}) collective-permute-start(bf16[3,224,512]{2,1,0:T(8,128)(2,1)S(1)} %get-tuple-element.106), channel_id=1, source_target_pairs={{0,16},{4,20},{8,24},{12,28},{16,0},{20,4},{24,8},{28,12},{1,17},{... | collective-permute-start | bytes 2064392 | tf_op jit(solution)/shard_map/ppermute | solution.py:308
  174.7 29.9 %collective-permute-start.37 = (bf16[3,224,512]{2,1,0:T(8,128)(2,1)S(1)}, bf16[3,224,512]{2,1,0:T(8,128)(2,1)S(1)}, u32[]{:S(2)}, u32[]{:S(2)}) collective-permute-start(bf16[3,224,512]{2,1,0:T(8,128)(2,1)S(1)} %get-tuple-element.107), channel_id=1, source_target_pairs={{0,24},{4,28},{8,16},{12,20},{16,8},{20,12},{24,0},{28,4},{1,25},{... | collective-permute-start | bytes 2064392 | tf_op jit(solution)/shard_map/ppermute | solution.py:308
  186.0 31.6 %collective-permute-start.38 = (bf16[3,224,512]{2,1,0:T(8,128)(2,1)S(1)}, bf16[3,224,512]{2,1,0:T(8,128)(2,1)S(1)}, u32[]{:S(2)}, u32[]{:S(2)}) collective-permute-start(bf16[3,224,512]{2,1,0:T(8,128)(2,1)S(1)} %get-tuple-element.108), channel_id=1, source_target_pairs={{0,4},{4,0},{8,12},{12,8},{16,20},{20,16},{24,28},{28,24},{1,5},{5... | collective-permute-start | bytes 2064392 | tf_op jit(solution)/shard_map/ppermute | solution.py:311
  189.1 14.9 %collective-permute-start.53 = (bf16[128,1024]{1,0:T(8,128)(2,1)S(1)}, bf16[128,1024]{1,0:T(8,128)(2,1)S(1)}, u32[]{:S(2)}, u32[]{:S(2)}) collective-permute-start(bf16[128,1024]{1,0:T(8,128)(2,1)S(1)} %add_convert_fusion.2), channel_id=1, source_target_pairs={{0,2},{1,3},{2,0},{3,1},{4,6},{5,7},{6,4},{7,5},{8,10},{9,11},{10,... | collective-permute-start | bytes 786440 | tf_op jit(solution)/shard_map/ppermute | solution.py:314
  204.0 13.5 %collective-permute-start.31 = (bf16[128,1024]{1,0:T(8,128)(2,1)S(1)}, bf16[128,1024]{1,0:T(8,128)(2,1)S(1)}, u32[]{:S(2)}, u32[]{:S(2)}) collective-permute-start(bf16[128,1024]{1,0:T(8,128)(2,1)S(1)} %add_convert_fusion.4), channel_id=1, source_target_pairs={{0,2},{1,3},{2,0},{3,1},{4,6},{5,7},{6,4},{7,5},{8,10},{9,11},{10,... | collective-permute-start | bytes 786440 | tf_op jit(solution)/shard_map/ppermute | solution.py:314
  204.0 41.8 %collective-permute-start.39 = (bf16[3,224,512]{2,1,0:T(8,128)(2,1)S(1)}, bf16[3,224,512]{2,1,0:T(8,128)(2,1)S(1)}, u32[]{:S(2)}, u32[]{:S(2)}) collective-permute-start(bf16[3,224,512]{2,1,0:T(8,128)(2,1)S(1)} %collective-permute-done.35.refs_5_), channel_id=1, source_target_pairs={{0,4},{4,0},{8,12},{12,8},{16,20},{20,16},{24,28},{28,24},{1,5},{5... | collective-permute-start | bytes 2064392 | tf_op jit(solution)/shard_map/ppermute | solution.py:311
  204.1 41.7 %collective-permute-start.40 = (bf16[3,224,512]{2,1,0:T(8,128)(2,1)S(1)}, bf16[3,224,512]{2,1,0:T(8,128)(2,1)S(1)}, u32[]{:S(2)}, u32[]{:S(2)}) collective-permute-start(bf16[3,224,512]{2,1,0:T(8,128)(2,1)S(1)} %collective-permute-done.36.refs_6_), channel_id=1, source_target_pairs={{0,4},{4,0},{8,12},{12,8},{16,20},{20,16},{24,28},{28,24},{1,5},{5... | collective-permute-start | bytes 2064392 | tf_op jit(solution)/shard_map/ppermute | solution.py:311
  204.6 41.2 %collective-permute-start.41 = (bf16[3,224,512]{2,1,0:T(8,128)(2,1)S(1)}, bf16[3,224,512]{2,1,0:T(8,128)(2,1)S(1)}, u32[]{:S(2)}, u32[]{:S(2)}) collective-permute-start(bf16[3,224,512]{2,1,0:T(8,128)(2,1)S(1)} %collective-permute-done.37.refs_7_), channel_id=1, source_target_pairs={{0,4},{4,0},{8,12},{12,8},{16,20},{20,16},{24,28},{28,24},{1,5},{5... | collective-permute-start | bytes 2064392 | tf_op jit(solution)/shard_map/ppermute | solution.py:311
  230.3 13.4 %collective-permute-start.33 = (bf16[128,1024]{1,0:T(8,128)(2,1)S(1)}, bf16[128,1024]{1,0:T(8,128)(2,1)}, u32[]{:S(2)}, u32[]{:S(2)}) collective-permute-start(bf16[128,1024]{1,0:T(8,128)(2,1)S(1)} %shard_map.69.refs_0_), channel_id=1, source_target_pairs={{0,2},{1,3},{2,0},{3,1},{4,6},{5,7},{6,4},{7,5},{8,10},{9,11},{10,... | collective-permute-start | bytes 786440 | tf_op jit(solution)/shard_map/ppermute | solution.py:314
  230.4 13.4 %collective-permute-start.56 = (bf16[128,1024]{1,0:T(8,128)(2,1)S(1)}, bf16[128,1024]{1,0:T(8,128)(2,1)S(1)}, u32[]{:S(2)}, u32[]{:S(2)}) collective-permute-start(bf16[128,1024]{1,0:T(8,128)(2,1)S(1)} %collective-permute-done.55.refs_2_), channel_id=1, source_target_pairs={{0,1},{1,0},{2,3},{3,2},{4,5},{5,4},{6,7},{7,6},{8,9},{9,8},{10,11... | collective-permute-start | bytes 786440 | tf_op jit(solution)/shard_map/ppermute | solution.py:314
  243.7 17.9 %collective-permute-start.32 = (bf16[128,1024]{1,0:T(8,128)(2,1)S(1)}, bf16[128,1024]{1,0:T(8,128)(2,1)}, u32[]{:S(2)}, u32[]{:S(2)}) collective-permute-start(bf16[128,1024]{1,0:T(8,128)(2,1)S(1)} %shard_map.69.refs_0_), channel_id=1, source_target_pairs={{0,1},{1,0},{2,3},{3,2},{4,5},{5,4},{6,7},{7,6},{8,9},{9,8},{10,11... | collective-permute-start | bytes 786440 | tf_op jit(solution)/shard_map/ppermute | solution.py:314
  243.8 17.8 %collective-permute-start.34 = (bf16[128,1024]{1,0:T(8,128)(2,1)}, bf16[128,1024]{1,0:T(8,128)(2,1)}, u32[]{:S(2)}, u32[]{:S(2)}) collective-permute-start(bf16[128,1024]{1,0:T(8,128)(2,1)} %collective-permute-done.33.refs_2_), channel_id=1, source_target_pairs={{0,1},{1,0},{2,3},{3,2},{4,5},{5,4},{6,7},{7,6},{8,9},{9,8},{10,11... | collective-permute-start | bytes 786440 | tf_op jit(solution)/shard_map/ppermute | solution.py:314
  258.1 26.4 %collective-permute-start.57 = (bf16[128,1792]{1,0:T(8,128)(2,1)}, bf16[128,1792]{1,0:T(8,128)(2,1)}, u32[]{:S(2)}, u32[]{:S(2)}) collective-permute-start(bf16[128,1792]{1,0:T(8,128)(2,1)} %get-tuple-element.122), channel_id=1, source_target_pairs={{0,8},{4,12},{8,0},{12,4},{16,24},{20,28},{24,16},{28,20},{1,9},{5... | collective-permute-start | bytes 1376264 | tf_op jit(solution)/shard_map/ppermute | solution.py:308
  259.9 25.9 %collective-permute-start.58 = (bf16[128,1792]{1,0:T(8,128)(2,1)}, bf16[128,1792]{1,0:T(8,128)(2,1)}, u32[]{:S(2)}, u32[]{:S(2)}) collective-permute-start(bf16[128,1792]{1,0:T(8,128)(2,1)} %get-tuple-element.123), channel_id=1, source_target_pairs={{0,16},{4,20},{8,24},{12,28},{16,0},{20,4},{24,8},{28,12},{1,17},{... | collective-permute-start | bytes 1376264 | tf_op jit(solution)/shard_map/ppermute | solution.py:308
  260.4 25.4 %collective-permute-start.59 = (bf16[128,1792]{1,0:T(8,128)(2,1)}, bf16[128,1792]{1,0:T(8,128)(2,1)}, u32[]{:S(2)}, u32[]{:S(2)}) collective-permute-start(bf16[128,1792]{1,0:T(8,128)(2,1)} %get-tuple-element.124), channel_id=1, source_target_pairs={{0,24},{4,28},{8,16},{12,20},{16,8},{20,12},{24,0},{28,4},{1,25},{... | collective-permute-start | bytes 1376264 | tf_op jit(solution)/shard_map/ppermute | solution.py:308
  282.2 13.5 %collective-permute-start.42 = (bf16[128,1792]{1,0:T(8,128)(2,1)S(1)}, bf16[128,1792]{1,0:T(8,128)(2,1)S(1)}, u32[]{:S(2)}, u32[]{:S(2)}) collective-permute-start(bf16[128,1792]{1,0:T(8,128)(2,1)S(1)} %get-tuple-element.110), channel_id=1, source_target_pairs={{0,8},{4,12},{8,0},{12,4},{16,24},{20,28},{24,16},{28,20},{1,9},{5... | collective-permute-start | bytes 1376264 | tf_op jit(solution)/shard_map/ppermute | solution.py:308
  284.0 20.5 %collective-permute-start.43 = (bf16[128,1792]{1,0:T(8,128)(2,1)S(1)}, bf16[128,1792]{1,0:T(8,128)(2,1)S(1)}, u32[]{:S(2)}, u32[]{:S(2)}) collective-permute-start(bf16[128,1792]{1,0:T(8,128)(2,1)S(1)} %get-tuple-element.111), channel_id=1, source_target_pairs={{0,16},{4,20},{8,24},{12,28},{16,0},{20,4},{24,8},{28,12},{1,17},{... | collective-permute-start | bytes 1376264 | tf_op jit(solution)/shard_map/ppermute | solution.py:308
  284.5 20.0 %collective-permute-start.44 = (bf16[128,1792]{1,0:T(8,128)(2,1)S(1)}, bf16[128,1792]{1,0:T(8,128)(2,1)S(1)}, u32[]{:S(2)}, u32[]{:S(2)}) collective-permute-start(bf16[128,1792]{1,0:T(8,128)(2,1)S(1)} %get-tuple-element.112), channel_id=1, source_target_pairs={{0,24},{4,28},{8,16},{12,20},{16,8},{20,12},{24,0},{28,4},{1,25},{... | collective-permute-start | bytes 1376264 | tf_op jit(solution)/shard_map/ppermute | solution.py:308
  287.4 19.3 %collective-permute-start.62 = (bf16[32,1792]{1,0:T(8,128)(2,1)S(1)}, bf16[32,1792]{1,0:T(8,128)(2,1)S(1)}, u32[]{:S(2)}, u32[]{:S(2)}) collective-permute-start(bf16[32,1792]{1,0:T(8,128)(2,1)S(1)} %get-tuple-element.141), channel_id=1, source_target_pairs={{0,3},{1,2},{2,1},{3,0},{4,7},{5,6},{6,5},{7,4},{8,11},{9,10},{10,... | collective-permute-start | bytes 344072 | tf_op jit(solution)/shard_map/ppermute | solution.py:314
  289.3 20.0 %collective-permute-start.61 = (bf16[32,1792]{1,0:T(8,128)(2,1)S(1)}, bf16[32,1792]{1,0:T(8,128)(2,1)S(1)}, u32[]{:S(2)}, u32[]{:S(2)}) collective-permute-start(bf16[32,1792]{1,0:T(8,128)(2,1)S(1)} %get-tuple-element.142), channel_id=1, source_target_pairs={{0,2},{1,3},{2,0},{3,1},{4,6},{5,7},{6,4},{7,5},{8,10},{9,11},{10,... | collective-permute-start | bytes 344072 | tf_op jit(solution)/shard_map/ppermute | solution.py:314
  295.7 13.6 %collective-permute-start.60 = (bf16[32,1792]{1,0:T(8,128)(2,1)S(1)}, bf16[32,1792]{1,0:T(8,128)(2,1)S(1)}, u32[]{:S(2)}, u32[]{:S(2)}) collective-permute-start(bf16[32,1792]{1,0:T(8,128)(2,1)S(1)} %get-tuple-element.143), channel_id=1, source_target_pairs={{0,1},{1,0},{2,3},{3,2},{4,5},{5,4},{6,7},{7,6},{8,9},{9,8},{10,11... | collective-permute-start | bytes 344072 | tf_op jit(solution)/shard_map/ppermute | solution.py:314
  (59 other events, 804.4 us)

commit v5 on v0

v5 whole, which is shorter than its diff:
```python
import functools

import jax
import jax.numpy as jnp
from jax import lax
from jax.experimental import pallas as pl
from jax.experimental.pallas import tpu as pltpu
from jax.sharding import PartitionSpec as P

VMEM_BYTES = 22 * 1024 * 1024
CORES = 2
HALVES = 2
TILE = 256
LANES = 128

SMEM_SPEC = pl.BlockSpec(memory_space=pltpu.SMEM)
VMEM_SPEC = pl.BlockSpec(memory_space=pltpu.VMEM)
ANY_SPEC = pl.BlockSpec(memory_space=pl.ANY)
PARAMS = pltpu.CompilerParams(vmem_limit_bytes=VMEM_BYTES)


def bf16(*shape):
    return jax.ShapeDtypeStruct(shape, jnp.bfloat16)


def cost(flops, elements):
    return pl.CostEstimate(flops=flops, bytes_accessed=2 * elements, transcendentals=0)


def rows_of(block, rows):
    return pl.ds(pl.multiple_of(block * rows, rows), rows)


def cut_kernel(depth, place_ref, tokens_ref, *refs):
    outs, held = refs[:-1], refs[-1]
    levels, _, wide = held.shape
    core, level = place_ref[1], place_ref[2]
    tokens = tokens_ref[...]
    for other in range(levels):
        sides = []
        for side in range(CORES):
            blocks = range(side, wide // depth, CORES)
            starts = [(block * levels + other) * depth for block in blocks]
            sides.append(jnp.concatenate([tokens[:, s : s + depth] for s in starts], axis=1))
        swapped = jnp.concatenate(sides[::-1], axis=1)
        piece = jnp.where(core == 0, jnp.concatenate(sides, axis=1), swapped)
        held[jnp.bitwise_xor(level, other)] = piece
    for step, out_ref in enumerate(outs):
        out_ref[...] = held[step]


def cut_tokens(place, tokens, levels, depth):
    rows, model = tokens.shape
    shape = (rows, model // levels)
    return pl.pallas_call(
        functools.partial(cut_kernel, depth),
        in_specs=[SMEM_SPEC, VMEM_SPEC],
        out_specs=[VMEM_SPEC] * levels,
        out_shape=[bf16(*shape)] * levels,
        scratch_shapes=[pltpu.VMEM((levels,) + shape, jnp.bfloat16)],
        compiler_params=PARAMS,
    )(place, tokens)


def group_kernel(levels, place_ref, routing_ref, *refs):
    pieces, outs = refs[:levels], refs[levels:]
    wide = pieces[0].shape[1]
    rows = pieces[0].shape[0] // HALVES
    for step, piece in enumerate(pieces):
        target = rows_of(jnp.bitwise_xor(place_ref[2], step), rows)
        for half, out_ref in enumerate(outs):
            out_ref[target, :wide] = piece[half * rows : (half + 1) * rows, :]
    for level in range(levels):
        for half, out_ref in enumerate(outs):
            first = (level * HALVES + half) * rows
            out_ref[level * rows : (level + 1) * rows, wide:] = routing_ref[first : first + rows, :]


def group_tokens(place, routing, pieces):
    rows, wide = pieces[0].shape
    levels = len(pieces)
    return pl.pallas_call(
        functools.partial(group_kernel, levels),
        in_specs=[SMEM_SPEC, VMEM_SPEC] + [VMEM_SPEC] * levels,
        out_specs=[VMEM_SPEC] * HALVES,
        out_shape=[bf16(levels * rows // HALVES, wide + LANES)] * HALVES,
        compiler_params=PARAMS,
    )(place, routing, *pieces)


def finish_kernel(depth, levels, place_ref, *refs):
    pieces, (out_ref, held) = refs[:-2], refs[-2:]
    rows, wide = pieces[0].shape
    for index, piece in enumerate(pieces):
        half, step = index // levels, index % levels
        other = jnp.bitwise_xor(place_ref[2], step)
        held[other, half * rows : (half + 1) * rows, :] = piece[...]
    chips = wide // depth // CORES
    first, second = [], []
    for chip in range(chips):
        for side in range(CORES):
            for other in range(levels):
                for parts, place in ((first, side), (second, 1 - side)):
                    start = (place * chips + chip) * depth
                    parts.append(held[other, :, start : start + depth])
    first, second = jnp.concatenate(first, axis=1), jnp.concatenate(second, axis=1)
    out_ref[...] = jnp.where(place_ref[1] == 0, first, second)


def finish(place, pieces, levels, depth):
    rows, wide = pieces[0].shape
    rows = rows * HALVES
    return pl.pallas_call(
        functools.partial(finish_kernel, depth, levels),
        in_specs=[SMEM_SPEC] + [VMEM_SPEC] * len(pieces),
        out_specs=VMEM_SPEC,
        out_shape=bf16(rows, wide * levels),
        scratch_shapes=[pltpu.VMEM((levels, rows, wide), jnp.bfloat16)],
        compiler_params=PARAMS,
    )(place, *pieces)


def join_kernel(chips, place_ref, own_ref, *refs):
    pieces, (out_ref, sems) = refs[: chips - 1], refs[chips - 1 :]
    width = out_ref.shape[3]
    chip = place_ref[0]
    columns = pl.ds(pl.multiple_of(chip * width, width), width)
    sources = [own_ref.at[:, :, columns]] + list(pieces)
    copies = [
        pltpu.make_async_copy(source, out_ref.at[:, jnp.bitwise_xor(chip, step)], sems.at[step])
        for step, source in enumerate(sources)
    ]
    for copy in copies:
        copy.start()
    for copy in copies:
        copy.wait()


def join_blocks(place, own, pieces):
    experts, depth, units = own.shape
    chips = len(pieces) + 1
    shape = (experts, chips, depth, units // chips)
    return pl.pallas_call(
        functools.partial(join_kernel, chips),
        in_specs=[SMEM_SPEC] + [ANY_SPEC] * chips,
        out_specs=VMEM_SPEC,
        out_shape=bf16(*shape),
        scratch_shapes=[pltpu.SemaphoreType.DMA((chips,))],
        cost_estimate=cost(0, 2 * own.size),
        compiler_params=PARAMS,
    )(place, own, *pieces)


def pick_kernel(chips, place_ref, *refs):
    toks, refs = refs[:chips], refs[chips:]
    weights, (keep_ref, send_ref, routing_ref, left) = refs[:CORES], refs[CORES:]
    experts, depth, width = weights[0].shape
    rows = toks[0].shape[0]
    for step, tok in enumerate(toks):
        block = jnp.bitwise_xor(step, place_ref[2])
        left[rows_of(block, rows), :] = tok[:, : CORES * depth]
        routing_ref[block] = tok[:, CORES * depth :]
    slots = keep_ref.shape[2] // width
    tile = min(TILE, width)
    for start in range(0, width, tile):
        sums = []
        for which in range(experts):
            total = None
            for side, weight in enumerate(weights):
                term = jnp.dot(
                    left[:, side * depth : (side + 1) * depth],
                    weight[which, :, start : start + tile],
                    preferred_element_type=jnp.float32,
                )
                total = term if total is None else total + term
            sums.append(total)
        for step in range(chips):
            out_ref = (keep_ref, send_ref)[step % 2]
            ids = routing_ref[step].astype(jnp.float32)
            for slot in range(slots):
                chosen = ids[:, slot : slot + 1]
                picked = sums[0][step * rows : (step + 1) * rows]
                for which in range(1, experts):
                    other = sums[which][step * rows : (step + 1) * rows]
                    picked = jnp.where(chosen == which, other, picked)
                first = slot * width + start
                out_ref[step // 2, :, first : first + tile] = picked.astype(out_ref.dtype)


def picked_sums(place, toks, weights, slots):
    chips, rows = len(toks), toks[0].shape[0]
    experts, depth, width = weights[0].shape
    wide = CORES * depth
    count = chips * rows
    return pl.pallas_call(
        functools.partial(pick_kernel, chips),
        in_specs=[SMEM_SPEC] + [VMEM_SPEC] * (chips + CORES),
        out_specs=[VMEM_SPEC] * 3,
        out_shape=[bf16(chips // 2, rows, slots * width)] * 2 + [bf16(chips, rows, LANES)],
        scratch_shapes=[pltpu.VMEM((count, wide), jnp.bfloat16)],
        cost_estimate=cost(
            2 * count * wide * width * experts,
            count * wide + experts * wide * width + count * slots * width,
        ),
        compiler_params=PARAMS,
    )(place, *toks, *weights)


def hidden_kernel(terms, slots, routing_ref, *refs):
    gates, ups, out_ref = refs[:terms], refs[terms : 2 * terms], refs[2 * terms]
    scores = routing_ref[0].astype(jnp.float32)[:, slots : 2 * slots]
    combine = scores / jnp.sum(scores, axis=1, keepdims=True)
    width = out_ref.shape[1] // slots
    for slot in range(slots):
        columns = slice(slot * width, (slot + 1) * width)
        gate_sum = sum(ref[0, :, columns].astype(jnp.float32) for ref in gates)
        up_sum = sum(ref[0, :, columns].astype(jnp.float32) for ref in ups)
        value = gate_sum / (1.0 + jnp.exp(-gate_sum)) * up_sum * combine[:, slot : slot + 1]
        out_ref[:, columns] = value.astype(out_ref.dtype)


def hidden_rows(routing, gates, ups, slots):
    return pl.pallas_call(
        functools.partial(hidden_kernel, len(gates), slots),
        in_specs=[VMEM_SPEC] * (1 + 2 * len(gates)),
        out_specs=VMEM_SPEC,
        out_shape=bf16(*gates[0].shape[1:]),
        compiler_params=PARAMS,
    )(routing, *gates, *ups)


def down_kernel(step, slots, routing_ref, hid_ref, *refs):
    weights, (out_ref,) = refs[:CORES], refs[CORES:]
    experts, depth, width = weights[0].shape
    ids = routing_ref[step].astype(jnp.float32)
    lefts = []
    for which in range(experts):
        mine = jnp.zeros((hid_ref.shape[0], width), jnp.float32)
        for slot in range(slots):
            part = hid_ref[:, slot * width : (slot + 1) * width].astype(jnp.float32)
            mine = jnp.where(ids[:, slot : slot + 1] == which, part, mine)
        lefts.append(mine.astype(hid_ref.dtype))
    for side, weight in enumerate(weights):
        total = None
        for which in range(experts):
            term = lax.dot_general(
                lefts[which],
                weight[which],
                (((1,), (1,)), ((), ())),
                preferred_element_type=jnp.float32,
            )
            total = term if total is None else total + term
        out_ref[:, side * depth : (side + 1) * depth] = total.astype(out_ref.dtype)


def down_sums(routing, hidden, weights, step, slots):
    rows = hidden.shape[0]
    experts, depth, width = weights[0].shape
    wide = CORES * depth
    return pl.pallas_call(
        functools.partial(down_kernel, step, slots),
        in_specs=[VMEM_SPEC] * (2 + CORES),
        out_specs=VMEM_SPEC,
        out_shape=bf16(rows, wide),
        cost_estimate=cost(
            2 * rows * wide * width * experts,
            rows * slots * width + experts * wide * width + rows * wide,
        ),
        compiler_params=PARAMS,
    )(routing, hidden, *weights)


def after(values, others):
    return lax.optimization_barrier((values, others))[0]


def local(tokens, expert_ids, gate_scores, gate_weight, up_weight, down_weight):
    n_expert, n_tensor = lax.axis_size("expert"), lax.axis_size("tensor")
    chips = n_expert // CORES
    rows = tokens.shape[0]
    depth, units = gate_weight.shape[1:]
    slots = expert_ids.shape[1]
    width = units // chips
    spot, level = lax.axis_index("expert"), lax.axis_index("tensor")
    q, c = spot // CORES, spot % CORES
    place = jnp.stack([q, c, level])

    def to_chip(value, step):
        pairs = [(s, s ^ (step * CORES)) for s in range(n_expert)]
        return lax.ppermute(value, "expert", pairs)

    def to_core(value):
        return lax.ppermute(value, "expert", [(s, s ^ 1) for s in range(n_expert)])

    def to_level(value, step):
        return lax.ppermute(value, "tensor", [(s, s ^ step) for s in range(n_tensor)])

    def to_owner(value, step):
        pairs = [
            (s * n_tensor + t, (s ^ ((t ^ step) * CORES)) * n_tensor + t)
            for s in range(n_expert)
            for t in range(n_tensor)
        ]
        return lax.ppermute(value, ("expert", "tensor"), pairs)

    def copies(value, send, bits):
        held = {0: value}
        for bit in bits:
            for step in sorted(held):
                held[step + bit] = send(held[step], bit)
        return [held[step] for step in range(len(held))]

    def level_sums(keep, send):
        terms, bit = [keep], 1
        while True:
            terms.append(to_level(send, bit))
            bit *= 2
            if bit == n_tensor:
                return terms
            send = sum(term[1::2].astype(jnp.float32) for term in terms).astype(jnp.bfloat16)
            terms = [term[::2] for term in terms]

    def blocks_of(weight):
        return [
            lax.dynamic_slice_in_dim(weight, (q ^ step) * width, width, 2)
            for step in range(1, chips)
        ]

    def chip_exchange(blocks):
        return [to_chip(block, step) for step, block in enumerate(blocks, 1)]

    def core_exchange(joined):
        pair = [joined, to_core(joined)]
        return [side.reshape(side.shape[0], chips * depth, width) for side in pair]

    routing = jnp.concatenate([expert_ids, gate_scores], axis=1).astype(jnp.bfloat16)
    routing = jnp.pad(routing, ((0, 0), (0, LANES - 2 * slots)))
    gate_same = chip_exchange(blocks_of(gate_weight))
    cut = cut_tokens(place, tokens, n_tensor, depth)
    cut = [cut[0]] + [to_level(cut[step], step) for step in range(1, n_tensor)]
    groups = group_tokens(place, routing, cut)

    gate_joined = join_blocks(place, gate_weight, after(gate_same, groups))
    gate_pair = core_exchange(gate_joined)
    groups = after(groups, gate_joined)
    bits = [1 << bit for bit in range(chips.bit_length() - 1)]
    toks = []
    for half in range(HALVES):
        turn = (half + 1) % len(bits)
        toks.append(copies(groups[half], to_chip, bits[turn:] + bits[:turn]))
    up_same = chip_exchange(after(blocks_of(up_weight), toks))

    def products(weights, parts):
        routings, sends = [], []
        for half in range(HALVES):
            left = after(toks[half], parts)
            *parts, routing = picked_sums(place, left, weights, slots)
            routings.append(routing)
            sends.append(parts)
        sums = [level_sums(*parts) for parts in sends]
        return routings, sums

    routings, gate_sums = products(gate_pair, place)
    up_joined = join_blocks(place, up_weight, after(up_same, [terms[:-1] for terms in gate_sums]))
    up_pair = core_exchange(up_joined)
    down_same = chip_exchange(after(blocks_of(down_weight), up_joined))
    _, up_sums = products(up_pair, gate_sums)
    hiddens = [
        hidden_rows(routings[half], gate_sums[half], up_sums[half], slots)
        for half in range(HALVES)
    ]
    down_joined = join_blocks(place, down_weight, after(down_same, hiddens[0]))
    down_pair = core_exchange(down_joined)

    backs = []
    bits = [1 << bit for bit in range(n_tensor.bit_length() - 1)]
    for half in range(HALVES):
        routing = routings[half]
        blocks = copies(hiddens[half], to_level, bits[::-1])
        total = 0.0
        for step in range(n_tensor):
            part = down_sums(routing, blocks[step], down_pair, step, slots)
            total = total + to_owner(part, step).astype(jnp.float32)
        total = total.astype(jnp.bfloat16).reshape(n_tensor, rows // HALVES, -1)
        for step in range(n_tensor):
            piece = lax.dynamic_index_in_dim(total, level ^ step, 0, keepdims=False)
            backs.append(to_level(piece, step) if step else piece)
    return finish(place, backs, n_tensor, depth)


def solution(mesh):
    return jax.shard_map(
        local,
        mesh=mesh,
        in_specs=(
            P(("expert", "tensor"), None),
            P("expert", None),
            P("expert", None),
            P(None, ("expert", "tensor"), None),
            P(None, ("expert", "tensor"), None),
            P(None, ("expert", "tensor"), None),
        ),
        out_specs=P(("expert", "tensor"), None),
        check_vma=False,
    )
```

time: 606 us -> 306 us (0.50)
  blocking collectives: 357 us -> 0 us
  starting transfers between devices: 0.35 us -> 86.3 us
  matrix products: 46.4 us -> 0 us
  Pallas kernels: 0 us -> 44.4 us
  local copies, waits for them, and re-layouts: 38.2 us -> 10.2 us
  between operations: 13.3 us -> 0.47 us
  waiting for transfers between devices: 150 us -> 161 us
    all_to_all x3 -> x0, blocking collectives: 357 us -> none  [the longest x1 159 us: local(): lax.all_to_all(gate_weight, 'tensor', split_axis=2, concat_axis=1, tiled=...]
    ppermute x0 -> x49, waiting for transfers between devices: none -> 161 us  [the longest x23 119 us: to_level(): lax.ppermute(value, 'tensor', [(s, s ^ step) for s in range(n_tensor)])]
    ppermute x0 -> x49, starting transfers between devices: none -> 86.3 us  [the longest x23 44.1 us: to_level(): lax.ppermute(value, 'tensor', [(s, s ^ step) for s in range(n_tensor)])]
    all_gather x4 -> x0, waiting for transfers between devices: 81 us -> none  [the longest x1 80.9 us: local(): lax.all_gather(served_down, 'expert', axis=1, tiled=True)]
    reduce_scatter x1 -> x0, waiting for transfers between devices: 68.6 us -> none  [local(): lax.psum_scatter(partial_sum.astype(jnp.bfloat16), 'tensor', scatter_dime...]
    dot_general x7 -> x0, matrix products: 46.4 us -> none  [the longest x3 17.9 us: local(): jnp.dot(gathered, full_gate[which], preferred_element_type=jnp.float32)]
    pallas_call x0 -> x20, Pallas kernels: none -> 44.4 us  [the longest x8 18.3 us: down_sums(): pl.pallas_call(functools.partial(down_kernel, step, slots), in_specs=[VME...]
    all_to_all x3 -> x0, local copies, waits for them, and re-layouts: 21.5 us -> none  [the longest x1 7.2 us: local(): lax.all_to_all(up_weight, 'tensor', split_axis=2, concat_axis=1, tiled=True)]
  transfers between devices with their start and end apart: 5 -> 49, of which waited for: 2 -> 19; matrix products, arithmetic and copies ran while one was open for 12% -> 1% of each run, Pallas kernels for 0% -> 11%
where the time goes in v5:
time: 306 us; the launch traced here: 305 us
  waiting for transfers between devices  161 us (53%)
  starting transfers between devices  86.3 us (28%)
  Pallas kernels  44.4 us (15%)
  local copies, waits for them, and re-layouts  10.2 us (3%)
    ppermute x23, waiting for transfers between devices, to_level(): lax.ppermute(value, 'tensor', [(s, s ^ step) for s in range(n_tensor)])  119 us
    ppermute x23, starting transfers between devices, to_level(): lax.ppermute(value, 'tensor', [(s, s ^ step) for s in range(n_tensor)])  44.1 us
    ppermute x15, waiting for transfers between devices, to_chip(): return lax.ppermute(value, 'expert', pairs)  37.6 us
    ppermute x8, starting transfers between devices, to_owner(): return lax.ppermute(value, ('expert', 'tensor'), pairs)  24.3 us
    pallas_call x8, Pallas kernels, down_sums(): pl.pallas_call(functools.partial(down_kernel, step, slots), in_specs=[VME...  18.3 us
    ppermute x15, starting transfers between devices, to_chip(): return lax.ppermute(value, 'expert', pairs)  17.7 us
    pallas_call x4, Pallas kernels, picked_sums(): pl.pallas_call(functools.partial(pick_kernel, chips), in_specs=[SMEM_SPEC...  16.3 us
    unnamed x26, local copies, waits for them, and re-layouts  6.29 us
  transfers between devices with their start and end apart: 49, of which 19 were waited for; matrix products, arithmetic and copies ran while one was open for 1% of the time, Pallas kernels for 11%

profile of v5, /device:TPU:0, one launch (start us, length us, event | category | flops | bytes accessed | tf_op | source)
XLA Modules:
  0.0 304.7 jit_solution(8866166561119417096)
XLA Ops:
  0.0 3.0 constant_dynamic-slice_fusion.6
  3.0 3.0 collective-permute-start.3
  13.2 2.6 collective-permute-start.1
  15.8 6.8 %collective-permute-done.refs_1_ = bf16[64,1792]{1,0:T(8,128)(2,1)S(1)} collective-permute-done((bf16[64,1792]{1,0:T(8,128)(2,1)S(1)}, bf16[64,1792]{1,0:T(8,128)(2,1)S(1)}, u32[]{:S(2)}, u32[]{:S(2)}) %collective-permute-start) | collective-permute-done | bytes 229408 | tf_op jit(solution)/shard_map/ppermute | solution.py:296
  23.3 2.6 collective-permute-start.2
  26.1 5.4 %collective-permute-done.2.refs_3_ = bf16[64,1792]{1,0:T(8,128)(2,1)} collective-permute-done((bf16[64,1792]{1,0:T(8,128)(2,1)}, bf16[64,1792]{1,0:T(8,128)(2,1)}, u32[]{:S(2)}, u32[]{:S(2)}) %collective-permute-start.2) | collective-permute-done | bytes 229408 | tf_op jit(solution)/shard_map/ppermute | solution.py:296
  34.5 3.4 %collective-permute-done.4.refs_1_ = bf16[3,224,512]{2,1,0:T(8,128)(2,1)} collective-permute-done((bf16[3,224,512]{2,1,0:T(8,128)(2,1)}, bf16[3,224,512]{2,1,0:T(8,128)(2,1)}, u32[]{:S(2)}, u32[]{:S(2)}) %collective-permute-start.4) | collective-permute-done | bytes 688160 | tf_op jit(solution)/shard_map/ppermute | solution.py:290
  38.0 2.2 shard_map.66
  44.3 10.0 %collective-permute-done.12.refs_1_ = bf16[128,1920]{1,0:T(8,128)(2,1)S(1)} collective-permute-done((bf16[128,1920]{1,0:T(8,128)(2,1)S(1)}, bf16[128,1920]{1,0:T(8,128)(2,1)S(1)}, u32[]{:S(2)}, u32[]{:S(2)}) %collective-permute-start.12) | collective-permute-done | bytes 491552 | tf_op jit(solution)/shard_map/ppermute | solution.py:290
  56.6 9.5 %collective-permute-done.13.refs_2_ = bf16[128,1920]{1,0:T(8,128)(2,1)S(1)} collective-permute-done((bf16[128,1920]{1,0:T(8,128)(2,1)S(1)}, bf16[128,1920]{1,0:T(8,128)(2,1)S(1)}, u32[]{:S(2)}, u32[]{:S(2)}) %collective-permute-start.13) | collective-permute-done | bytes 491552 | tf_op jit(solution)/shard_map/ppermute | solution.py:290
  66.1 9.8 %collective-permute-done.14.refs_3_ = bf16[128,1920]{1,0:T(8,128)(2,1)S(1)} collective-permute-done((bf16[128,1920]{1,0:T(8,128)(2,1)S(1)}, bf16[128,1920]{1,0:T(8,128)(2,1)S(1)}, u32[]{:S(2)}, u32[]{:S(2)}) %collective-permute-start.14) | collective-permute-done | bytes 491552 | tf_op jit(solution)/shard_map/ppermute | solution.py:290
  79.4 4.1 %shard_map.67 = (bf16[2,128,1024]{2,1,0:T(8,128)(2,1)S(1)}, bf16[2,128,1024]{2,1,0:T(8,128)(2,1)S(1)}, bf16[4,128,128]{2,1,0:T(8,128)(2,1)S(1)}) custom-call(s32[3]{0:T(128)S(1)} %pad_add_fusion.place_ref, bf16[128,1920]{1,0:T(8,128)(2,1)S(1)} %get-tuple-element.78.refs_0_, bf16[128,1920]{1,0:T(8,128)(2,1)S(1)} %collective-permute-done.6.refs_1_, ...), custom_call_target="tpu_custom_call" | custom-call | flops 2818572288 | bytes 8388608 | tf_op jit(solution)/shard_map/pallas_call | solution.py:195
  83.4 4.1 %shard_map.68 = (bf16[2,128,1024]{2,1,0:T(8,128)(2,1)S(1)}, bf16[2,128,1024]{2,1,0:T(8,128)(2,1)S(1)}, bf16[4,128,128]{2,1,0:T(8,128)(2,1)S(1)}) custom-call(s32[3]{0:T(128)S(1)} %pad_add_fusion.place_ref, bf16[128,1920]{1,0:T(8,128)(2,1)S(1)} %get-tuple-element.97.refs_0_, bf16[128,1920]{1,0:T(8,128)(2,1)S(1)} %collective-permute-done.12.refs_1_, ...), custom_call_target="tpu_custom_call" | custom-call | flops 2818572288 | bytes 8388608 | tf_op jit(solution)/shard_map/pallas_call | solution.py:195
  89.7 12.8 %collective-permute-done.15 = bf16[2,128,1024]{2,1,0:T(8,128)(2,1)S(1)} collective-permute-done((bf16[2,128,1024]{2,1,0:T(8,128)(2,1)S(1)}, bf16[2,128,1024]{2,1,0:T(8,128)(2,1)S(1)}, u32[]{:S(2)}, u32[]{:S(2)}) %collective-permute-start.15) | collective-permute-done | bytes 524320 | tf_op jit(solution)/shard_map/ppermute | solution.py:296
  102.5 8.7 %collective-permute-done.10 = bf16[2,128,1024]{2,1,0:T(8,128)(2,1)S(1)} collective-permute-done((bf16[2,128,1024]{2,1,0:T(8,128)(2,1)S(1)}, bf16[2,128,1024]{2,1,0:T(8,128)(2,1)S(1)}, u32[]{:S(2)}, u32[]{:S(2)}) %collective-permute-start.10) | collective-permute-done | bytes 524320 | tf_op jit(solution)/shard_map/ppermute | solution.py:296
  112.3 2.7 collective-permute-start.16
  115.4 18.2 %collective-permute-done.16.refs_2_ = bf16[1,128,1024]{2,1,0:T(8,128)(2,1)S(1)} collective-permute-done((bf16[1,128,1024]{2,1,0:T(8,128)(2,1)S(1)}, bf16[1,128,1024]{2,1,0:T(8,128)(2,1)S(1)}, u32[]{:S(2)}, u32[]{:S(2)}) %collective-permute-start.16) | collective-permute-done | bytes 262176 | tf_op jit(solution)/shard_map/ppermute | solution.py:296
  133.6 5.2 %collective-permute-done.11.refs_2_ = bf16[1,128,1024]{2,1,0:T(8,128)(2,1)S(1)} collective-permute-done((bf16[1,128,1024]{2,1,0:T(8,128)(2,1)S(1)}, bf16[1,128,1024]{2,1,0:T(8,128)(2,1)S(1)}, u32[]{:S(2)}, u32[]{:S(2)}) %collective-permute-start.11) | collective-permute-done | bytes 262176 | tf_op jit(solution)/shard_map/ppermute | solution.py:296
  138.8 4.1 %shard_map.70 = (bf16[2,128,1024]{2,1,0:T(8,128)(2,1)S(1)}, bf16[2,128,1024]{2,1,0:T(8,128)(2,1)S(1)}, bf16[4,128,128]{2,1,0:T(8,128)(2,1)}) custom-call(s32[3]{0:T(128)S(1)} %pad_add_fusion.place_ref, bf16[128,1920]{1,0:T(8,128)(2,1)S(1)} %get-tuple-element.78.refs_0_, bf16[128,1920]{1,0:T(8,128)(2,1)S(1)} %collective-permute-done.6.refs_1_, ...), custom_call_target="tpu_custom_call" | custom-call | flops 2818572288 | bytes 8388608 | tf_op jit(solution)/shard_map/pallas_call | solution.py:195
  147.5 9.0 %collective-permute-done.21 = bf16[2,128,1024]{2,1,0:T(8,128)(2,1)S(1)} collective-permute-done((bf16[2,128,1024]{2,1,0:T(8,128)(2,1)S(1)}, bf16[2,128,1024]{2,1,0:T(8,128)(2,1)S(1)}, u32[]{:S(2)}, u32[]{:S(2)}) %collective-permute-start.21) | collective-permute-done | bytes 524320 | tf_op jit(solution)/shard_map/ppermute | solution.py:296
  156.6 2.7 collective-permute-start.22
  159.4 11.6 %collective-permute-done.22.refs_5_ = bf16[1,128,1024]{2,1,0:T(8,128)(2,1)S(1)} collective-permute-done((bf16[1,128,1024]{2,1,0:T(8,128)(2,1)S(1)}, bf16[1,128,1024]{2,1,0:T(8,128)(2,1)S(1)}, u32[]{:S(2)}, u32[]{:S(2)}) %collective-permute-start.22) | collective-permute-done | bytes 262176 | tf_op jit(solution)/shard_map/ppermute | solution.py:296
  171.4 4.9 %collective-permute-done.24.refs_1_ = bf16[3,224,512]{2,1,0:T(8,128)(2,1)S(1)} collective-permute-done((bf16[3,224,512]{2,1,0:T(8,128)(2,1)S(1)}, bf16[3,224,512]{2,1,0:T(8,128)(2,1)S(1)}, u32[]{:S(2)}, u32[]{:S(2)}) %collective-permute-start.24) | collective-permute-done | bytes 688160 | tf_op jit(solution)/shard_map/ppermute | solution.py:290
  177.6 4.1 %shard_map.77 = (bf16[2,128,1024]{2,1,0:T(8,128)(2,1)S(1)}, bf16[2,128,1024]{2,1,0:T(8,128)(2,1)S(1)}, bf16[4,128,128]{2,1,0:T(8,128)(2,1)}) custom-call(s32[3]{0:T(128)S(1)} %pad_add_fusion.place_ref, bf16[128,1920]{1,0:T(8,128)(2,1)S(1)} %get-tuple-element.97.refs_0_, bf16[128,1920]{1,0:T(8,128)(2,1)S(1)} %collective-permute-done.12.refs_1_, ...), custom_call_target="tpu_custom_call" | custom-call | flops 2818572288 | bytes 8388608 | tf_op jit(solution)/shard_map/pallas_call | solution.py:195
  183.0 13.0 %collective-permute-done.37 = bf16[2,128,1024]{2,1,0:T(8,128)(2,1)S(1)} collective-permute-done((bf16[2,128,1024]{2,1,0:T(8,128)(2,1)S(1)}, bf16[2,128,1024]{2,1,0:T(8,128)(2,1)S(1)}, u32[]{:S(2)}, u32[]{:S(2)}) %collective-permute-start.37) | collective-permute-done | bytes 524320 | tf_op jit(solution)/shard_map/ppermute | solution.py:296
  196.1 3.4 %collective-permute-start.38 = (bf16[1,128,1024]{2,1,0:T(8,128)(2,1)S(1)}, bf16[1,128,1024]{2,1,0:T(8,128)(2,1)S(1)}, u32[]{:S(2)}, u32[]{:S(2)}) collective-permute-start(bf16[1,128,1024]{2,1,0:T(8,128)(2,1)S(1)} %add_convert_fusion.2), channel_id=1, source_target_pairs={{0,2},{1,3},{2,0},{3,1},{4,6},{5,7},{6,4},{7,5},{8,10},{9,11},{10,... | collective-permute-start | bytes 786440 | tf_op jit(solution)/shard_map/ppermute | solution.py:296
  199.6 11.7 %collective-permute-done.38.refs_5_ = bf16[1,128,1024]{2,1,0:T(8,128)(2,1)S(1)} collective-permute-done((bf16[1,128,1024]{2,1,0:T(8,128)(2,1)S(1)}, bf16[1,128,1024]{2,1,0:T(8,128)(2,1)S(1)}, u32[]{:S(2)}, u32[]{:S(2)}) %collective-permute-start.38) | collective-permute-done | bytes 262176 | tf_op jit(solution)/shard_map/ppermute | solution.py:296
  211.9 3.0 collective-permute-start.40
  214.8 10.5 %collective-permute-done.42.hid_ref = bf16[128,1024]{1,0:T(8,128)(2,1)S(1)} collective-permute-done((bf16[128,1024]{1,0:T(8,128)(2,1)S(1)}, bf16[128,1024]{1,0:T(8,128)(2,1)S(1)}, u32[]{:S(2)}, u32[]{:S(2)}) %collective-permute-start.42) | collective-permute-done | bytes 262176 | tf_op jit(solution)/shard_map/ppermute | solution.py:296
  228.5 2.5 shard_map.79
  231.0 5.0 %collective-permute-start.39 = (bf16[128,1792]{1,0:T(8,128)(2,1)}, bf16[128,1792]{1,0:T(8,128)(2,1)}, u32[]{:S(2)}, u32[]{:S(2)}) collective-permute-start(bf16[128,1792]{1,0:T(8,128)(2,1)} %shard_map.79), channel_id=1, source_target_pairs={{0,0},{1,9},{2,18},{3,27},{4,4},{5,13},{6,22},{7,31},{8,8},{9,1},{... | collective-permute-start | bytes 1376264 | tf_op jit(solution)/shard_map/ppermute | solution.py:304
  236.0 2.5 shard_map.80
  238.5 2.9 collective-permute-start.41
  241.4 2.4 shard_map.81
  243.8 2.5 collective-permute-start.43
  246.3 2.4 shard_map.82
  248.8 3.8 %collective-permute-start.45 = (bf16[128,1792]{1,0:T(8,128)(2,1)}, bf16[128,1792]{1,0:T(8,128)(2,1)}, u32[]{:S(2)}, u32[]{:S(2)}) collective-permute-start(bf16[128,1792]{1,0:T(8,128)(2,1)} %shard_map.82), channel_id=1, source_target_pairs={{0,24},{1,17},{2,10},{3,3},{4,28},{5,21},{6,14},{7,7},{8,16},{9,25... | collective-permute-start | bytes 1376264 | tf_op jit(solution)/shard_map/ppermute | solution.py:304
  252.6 2.1 collective-permute-start.32
  258.1 2.6 shard_map.75
  263.3 2.6 shard_map.76
  265.9 2.9 collective-permute-start.29
  268.9 2.5 collective-permute-start.31
  271.4 3.8 %collective-permute-start.33 = (bf16[128,1792]{1,0:T(8,128)(2,1)S(1)}, bf16[128,1792]{1,0:T(8,128)(2,1)S(1)}, u32[]{:S(2)}, u32[]{:S(2)}) collective-permute-start(bf16[128,1792]{1,0:T(8,128)(2,1)S(1)} %shard_map.76), channel_id=1, source_target_pairs={{0,24},{1,17},{2,10},{3,3},{4,28},{5,21},{6,14},{7,7},{8,16},{9,25... | collective-permute-start | bytes 1376264 | tf_op jit(solution)/shard_map/ppermute | solution.py:304
  277.0 7.7 %collective-permute-start.47 = (bf16[32,1792]{1,0:T(8,128)(2,1)S(1)}, bf16[32,1792]{1,0:T(8,128)(2,1)S(1)}, u32[]{:S(2)}, u32[]{:S(2)}) collective-permute-start(bf16[32,1792]{1,0:T(8,128)(2,1)S(1)} %get-tuple-element.113), channel_id=1, source_target_pairs={{0,2},{1,3},{2,0},{3,1},{4,6},{5,7},{6,4},{7,5},{8,10},{9,11},{10,... | collective-permute-start | bytes 344072 | tf_op jit(solution)/shard_map/ppermute | solution.py:296
  286.7 4.0 %collective-permute-done.31 = bf16[128,1792]{1,0:T(8,128)(2,1)S(1)} collective-permute-done((bf16[128,1792]{1,0:T(8,128)(2,1)S(1)}, bf16[128,1792]{1,0:T(8,128)(2,1)S(1)}, u32[]{:S(2)}, u32[]{:S(2)}) %collective-permute-start.31) | collective-permute-done | bytes 458784 | tf_op jit(solution)/shard_map/ppermute | solution.py:304
  291.0 2.9 collective-permute-start.34
  293.9 2.4 collective-permute-start.36
  297.4 5.5 %collective-permute-done.35.refs_2_ = bf16[32,1792]{1,0:T(8,128)(2,1)S(1)} collective-permute-done((bf16[32,1792]{1,0:T(8,128)(2,1)S(1)}, bf16[32,1792]{1,0:T(8,128)(2,1)S(1)}, u32[]{:S(2)}, u32[]{:S(2)}) %collective-permute-start.35) | collective-permute-done | bytes 114720 | tf_op jit(solution)/shard_map/ppermute | solution.py:296
  (121 shorter events, 49.3 us)
Async XLA Ops:
  3.0 31.5 %collective-permute-start.3 = (bf16[3,224,512]{2,1,0:T(8,128)(2,1)}, bf16[3,224,512]{2,1,0:T(8,128)(2,1)S(1)}, u32[]{:S(2)}, u32[]{:S(2)}) collective-permute-start(bf16[3,224,512]{2,1,0:T(8,128)(2,1)} %get-tuple-element.111), channel_id=1, source_target_pairs={{0,8},{4,12},{8,0},{12,4},{16,24},{20,28},{24,16},{28,20},{1,9},{5... | collective-permute-start | bytes 2064392 | tf_op jit(solution)/shard_map/ppermute | solution.py:290
  6.0 32.0 %collective-permute-start.4 = (bf16[3,224,512]{2,1,0:T(8,128)(2,1)}, bf16[3,224,512]{2,1,0:T(8,128)(2,1)}, u32[]{:S(2)}, u32[]{:S(2)}) collective-permute-start(bf16[3,224,512]{2,1,0:T(8,128)(2,1)} %get-tuple-element.110), channel_id=1, source_target_pairs={{0,16},{4,20},{8,24},{12,28},{16,0},{20,4},{24,8},{28,12},{1,17},{... | collective-permute-start | bytes 2064392 | tf_op jit(solution)/shard_map/ppermute | solution.py:290
  7.5 30.4 %collective-permute-start.5 = (bf16[3,224,512]{2,1,0:T(8,128)(2,1)}, bf16[3,224,512]{2,1,0:T(8,128)(2,1)}, u32[]{:S(2)}, u32[]{:S(2)}) collective-permute-start(bf16[3,224,512]{2,1,0:T(8,128)(2,1)} %get-tuple-element.109), channel_id=1, source_target_pairs={{0,24},{4,28},{8,16},{12,20},{16,8},{20,12},{24,0},{28,4},{1,25},{... | collective-permute-start | bytes 2064392 | tf_op jit(solution)/shard_map/ppermute | solution.py:290
  11.2 11.4 %collective-permute-start = (bf16[64,1792]{1,0:T(8,128)(2,1)S(1)}, bf16[64,1792]{1,0:T(8,128)(2,1)S(1)}, u32[]{:S(2)}, u32[]{:S(2)}) collective-permute-start(bf16[64,1792]{1,0:T(8,128)(2,1)S(1)} %get-tuple-element.55), channel_id=1, source_target_pairs={{0,1},{1,0},{2,3},{3,2},{4,5},{5,4},{6,7},{7,6},{8,9},{9,8},{10,11... | collective-permute-start | bytes 688136 | tf_op jit(solution)/shard_map/ppermute | solution.py:296
  13.2 12.9 %collective-permute-start.1 = (bf16[64,1792]{1,0:T(8,128)(2,1)}, bf16[64,1792]{1,0:T(8,128)(2,1)}, u32[]{:S(2)}, u32[]{:S(2)}) collective-permute-start(bf16[64,1792]{1,0:T(8,128)(2,1)} %get-tuple-element.56), channel_id=1, source_target_pairs={{0,2},{1,3},{2,0},{3,1},{4,6},{5,7},{6,4},{7,5},{8,10},{9,11},{10,... | collective-permute-start | bytes 688136 | tf_op jit(solution)/shard_map/ppermute | solution.py:296
  23.3 8.2 %collective-permute-start.2 = (bf16[64,1792]{1,0:T(8,128)(2,1)}, bf16[64,1792]{1,0:T(8,128)(2,1)}, u32[]{:S(2)}, u32[]{:S(2)}) collective-permute-start(bf16[64,1792]{1,0:T(8,128)(2,1)} %get-tuple-element.57), channel_id=1, source_target_pairs={{0,3},{1,2},{2,1},{3,0},{4,7},{5,6},{6,5},{7,4},{8,11},{9,10},{10,... | collective-permute-start | bytes 688136 | tf_op jit(solution)/shard_map/ppermute | solution.py:296
  40.1 39.2 %collective-permute-start.9 = (bf16[3,4,224,512]{3,2,1,0:T(8,128)(2,1)S(1)}, bf16[3,4,224,512]{3,2,1,0:T(8,128)(2,1)S(1)}, u32[]{:S(2)}, u32[]{:S(2)}) collective-permute-start(bf16[3,4,224,512]{3,2,1,0:T(8,128)(2,1)S(1)} %shard_map.66), channel_id=1, source_target_pairs={{0,4},{4,0},{8,12},{12,8},{16,20},{20,16},{24,28},{28,24},{1,5},{5... | collective-permute-start | bytes 8257544 | tf_op jit(solution)/shard_map/ppermute | solution.py:293
  40.2 14.1 %collective-permute-start.12 = (bf16[128,1920]{1,0:T(8,128)(2,1)S(1)}, bf16[128,1920]{1,0:T(8,128)(2,1)S(1)}, u32[]{:S(2)}, u32[]{:S(2)}) collective-permute-start(bf16[128,1920]{1,0:T(8,128)(2,1)S(1)} %get-tuple-element.97.refs_0_), channel_id=1, source_target_pairs={{0,8},{4,12},{8,0},{12,4},{16,24},{20,28},{24,16},{28,20},{1,9},{5... | collective-permute-start | bytes 1474568 | tf_op jit(solution)/shard_map/ppermute | solution.py:290
  41.5 14.3 %collective-permute-start.7 = (bf16[128,1920]{1,0:T(8,128)(2,1)S(1)}, bf16[128,1920]{1,0:T(8,128)(2,1)S(1)}, u32[]{:S(2)}, u32[]{:S(2)}) collective-permute-start(bf16[128,1920]{1,0:T(8,128)(2,1)S(1)} %get-tuple-element.78.refs_0_), channel_id=1, source_target_pairs={{0,16},{4,20},{8,24},{12,28},{16,0},{20,4},{24,8},{28,12},{1,17},{... | collective-permute-start | bytes 1474568 | tf_op jit(solution)/shard_map/ppermute | solution.py:290
  42.3 23.8 %collective-permute-start.13 = (bf16[128,1920]{1,0:T(8,128)(2,1)S(1)}, bf16[128,1920]{1,0:T(8,128)(2,1)S(1)}, u32[]{:S(2)}, u32[]{:S(2)}) collective-permute-start(bf16[128,1920]{1,0:T(8,128)(2,1)S(1)} %get-tuple-element.97.refs_0_), channel_id=1, source_target_pairs={{0,16},{4,20},{8,24},{12,28},{16,0},{20,4},{24,8},{28,12},{1,17},{... | collective-permute-start | bytes 1474568 | tf_op jit(solution)/shard_map/ppermute | solution.py:290
  43.5 22.6 %collective-permute-start.6 = (bf16[128,1920]{1,0:T(8,128)(2,1)S(1)}, bf16[128,1920]{1,0:T(8,128)(2,1)S(1)}, u32[]{:S(2)}, u32[]{:S(2)}) collective-permute-start(bf16[128,1920]{1,0:T(8,128)(2,1)S(1)} %get-tuple-element.78.refs_0_), channel_id=1, source_target_pairs={{0,8},{4,12},{8,0},{12,4},{16,24},{20,28},{24,16},{28,20},{1,9},{5... | collective-permute-start | bytes 1474568 | tf_op jit(solution)/shard_map/ppermute | solution.py:290
  54.3 21.6 %collective-permute-start.14 = (bf16[128,1920]{1,0:T(8,128)(2,1)S(1)}, bf16[128,1920]{1,0:T(8,128)(2,1)S(1)}, u32[]{:S(2)}, u32[]{:S(2)}) collective-permute-start(bf16[128,1920]{1,0:T(8,128)(2,1)S(1)} %collective-permute-done.12.refs_1_), channel_id=1, source_target_pairs={{0,16},{4,20},{8,24},{12,28},{16,0},{20,4},{24,8},{28,12},{1,17},{... | collective-permute-start | bytes 1474568 | tf_op jit(solution)/shard_map/ppermute | solution.py:290
  55.8 20.0 %collective-permute-start.8 = (bf16[128,1920]{1,0:T(8,128)(2,1)S(1)}, bf16[128,1920]{1,0:T(8,128)(2,1)S(1)}, u32[]{:S(2)}, u32[]{:S(2)}) collective-permute-start(bf16[128,1920]{1,0:T(8,128)(2,1)S(1)} %collective-permute-done.7.refs_2_), channel_id=1, source_target_pairs={{0,8},{4,12},{8,0},{12,4},{16,24},{20,28},{24,16},{28,20},{1,9},{5... | collective-permute-start | bytes 1474568 | tf_op jit(solution)/shard_map/ppermute | solution.py:290
  75.9 35.3 %collective-permute-start.17 = (bf16[3,224,512]{2,1,0:T(8,128)(2,1)S(1)}, bf16[3,224,512]{2,1,0:T(8,128)(2,1)S(1)}, u32[]{:S(2)}, u32[]{:S(2)}) collective-permute-start(bf16[3,224,512]{2,1,0:T(8,128)(2,1)S(1)} %get-tuple-element.82), channel_id=1, source_target_pairs={{0,8},{4,12},{8,0},{12,4},{16,24},{20,28},{24,16},{28,20},{1,9},{5... | collective-permute-start | bytes 2064392 | tf_op jit(solution)/shard_map/ppermute | solution.py:290
  76.7 34.5 %collective-permute-start.18 = (bf16[3,224,512]{2,1,0:T(8,128)(2,1)S(1)}, bf16[3,224,512]{2,1,0:T(8,128)(2,1)S(1)}, u32[]{:S(2)}, u32[]{:S(2)}) collective-permute-start(bf16[3,224,512]{2,1,0:T(8,128)(2,1)S(1)} %get-tuple-element.83), channel_id=1, source_target_pairs={{0,16},{4,20},{8,24},{12,28},{16,0},{20,4},{24,8},{28,12},{1,17},{... | collective-permute-start | bytes 2064392 | tf_op jit(solution)/shard_map/ppermute | solution.py:290
  78.2 33.0 %collective-permute-start.19 = (bf16[3,224,512]{2,1,0:T(8,128)(2,1)S(1)}, bf16[3,224,512]{2,1,0:T(8,128)(2,1)S(1)}, u32[]{:S(2)}, u32[]{:S(2)}) collective-permute-start(bf16[3,224,512]{2,1,0:T(8,128)(2,1)S(1)} %get-tuple-element.84), channel_id=1, source_target_pairs={{0,24},{4,28},{8,16},{12,20},{16,8},{20,12},{24,0},{28,4},{1,25},{... | collective-permute-start | bytes 2064392 | tf_op jit(solution)/shard_map/ppermute | solution.py:290
  87.5 14.9 %collective-permute-start.15 = (bf16[2,128,1024]{2,1,0:T(8,128)(2,1)S(1)}, bf16[2,128,1024]{2,1,0:T(8,128)(2,1)S(1)}, u32[]{:S(2)}, u32[]{:S(2)}) collective-permute-start(bf16[2,128,1024]{2,1,0:T(8,128)(2,1)S(1)} %get-tuple-element.77), channel_id=1, source_target_pairs={{0,1},{1,0},{2,3},{3,2},{4,5},{5,4},{6,7},{7,6},{8,9},{9,8},{10,11... | collective-permute-start | bytes 1572872 | tf_op jit(solution)/shard_map/ppermute | solution.py:296
  89.2 22.0 %collective-permute-start.10 = (bf16[2,128,1024]{2,1,0:T(8,128)(2,1)S(1)}, bf16[2,128,1024]{2,1,0:T(8,128)(2,1)S(1)}, u32[]{:S(2)}, u32[]{:S(2)}) collective-permute-start(bf16[2,128,1024]{2,1,0:T(8,128)(2,1)S(1)} %get-tuple-element.70), channel_id=1, source_target_pairs={{0,1},{1,0},{2,3},{3,2},{4,5},{5,4},{6,7},{7,6},{8,9},{9,8},{10,11... | collective-permute-start | bytes 1572872 | tf_op jit(solution)/shard_map/ppermute | solution.py:296
  112.1 26.7 %collective-permute-start.20 = (bf16[3,4,224,512]{3,2,1,0:T(8,128)(2,1)S(1)}, bf16[3,4,224,512]{3,2,1,0:T(8,128)(2,1)S(1)}, u32[]{:S(2)}, u32[]{:S(2)}) collective-permute-start(bf16[3,4,224,512]{3,2,1,0:T(8,128)(2,1)S(1)} %shard_map.69), channel_id=1, source_target_pairs={{0,4},{4,0},{8,12},{12,8},{16,20},{20,16},{24,28},{28,24},{1,5},{5... | collective-permute-start | bytes 8257544 | tf_op jit(solution)/shard_map/ppermute | solution.py:293
  112.3 21.3 %collective-permute-start.16 = (bf16[1,128,1024]{2,1,0:T(8,128)(2,1)S(1)}, bf16[1,128,1024]{2,1,0:T(8,128)(2,1)S(1)}, u32[]{:S(2)}, u32[]{:S(2)}) collective-permute-start(bf16[1,128,1024]{2,1,0:T(8,128)(2,1)S(1)} %add_convert_fusion.4), channel_id=1, source_target_pairs={{0,2},{1,3},{2,0},{3,1},{4,6},{5,7},{6,4},{7,5},{8,10},{9,11},{10,... | collective-permute-start | bytes 786440 | tf_op jit(solution)/shard_map/ppermute | solution.py:296
  115.0 23.8 %collective-permute-start.11 = (bf16[1,128,1024]{2,1,0:T(8,128)(2,1)S(1)}, bf16[1,128,1024]{2,1,0:T(8,128)(2,1)S(1)}, u32[]{:S(2)}, u32[]{:S(2)}) collective-permute-start(bf16[1,128,1024]{2,1,0:T(8,128)(2,1)S(1)} %add_convert_fusion.5), channel_id=1, source_target_pairs={{0,2},{1,3},{2,0},{3,1},{4,6},{5,7},{6,4},{7,5},{8,10},{9,11},{10,... | collective-permute-start | bytes 786440 | tf_op jit(solution)/shard_map/ppermute | solution.py:296
  142.9 13.6 %collective-permute-start.21 = (bf16[2,128,1024]{2,1,0:T(8,128)(2,1)S(1)}, bf16[2,128,1024]{2,1,0:T(8,128)(2,1)S(1)}, u32[]{:S(2)}, u32[]{:S(2)}) collective-permute-start(bf16[2,128,1024]{2,1,0:T(8,128)(2,1)S(1)} %get-tuple-element.89), channel_id=1, source_target_pairs={{0,1},{1,0},{2,3},{3,2},{4,5},{5,4},{6,7},{7,6},{8,9},{9,8},{10,11... | collective-permute-start | bytes 1572872 | tf_op jit(solution)/shard_map/ppermute | solution.py:296
  143.9 27.5 %collective-permute-start.23 = (bf16[3,224,512]{2,1,0:T(8,128)(2,1)S(1)}, bf16[3,224,512]{2,1,0:T(8,128)(2,1)S(1)}, u32[]{:S(2)}, u32[]{:S(2)}) collective-permute-start(bf16[3,224,512]{2,1,0:T(8,128)(2,1)S(1)} %get-tuple-element.90), channel_id=1, source_target_pairs={{0,8},{4,12},{8,0},{12,4},{16,24},{20,28},{24,16},{28,20},{1,9},{5... | collective-permute-start | bytes 2064392 | tf_op jit(solution)/shard_map/ppermute | solution.py:290
  144.8 31.6 %collective-permute-start.24 = (bf16[3,224,512]{2,1,0:T(8,128)(2,1)S(1)}, bf16[3,224,512]{2,1,0:T(8,128)(2,1)S(1)}, u32[]{:S(2)}, u32[]{:S(2)}) collective-permute-start(bf16[3,224,512]{2,1,0:T(8,128)(2,1)S(1)} %get-tuple-element.91), channel_id=1, source_target_pairs={{0,16},{4,20},{8,24},{12,28},{16,0},{20,4},{24,8},{28,12},{1,17},{... | collective-permute-start | bytes 2064392 | tf_op jit(solution)/shard_map/ppermute | solution.py:290
  146.3 30.1 %collective-permute-start.25 = (bf16[3,224,512]{2,1,0:T(8,128)(2,1)S(1)}, bf16[3,224,512]{2,1,0:T(8,128)(2,1)S(1)}, u32[]{:S(2)}, u32[]{:S(2)}) collective-permute-start(bf16[3,224,512]{2,1,0:T(8,128)(2,1)S(1)} %get-tuple-element.92), channel_id=1, source_target_pairs={{0,24},{4,28},{8,16},{12,20},{16,8},{20,12},{24,0},{28,4},{1,25},{... | collective-permute-start | bytes 2064392 | tf_op jit(solution)/shard_map/ppermute | solution.py:290
  156.6 14.4 %collective-permute-start.22 = (bf16[1,128,1024]{2,1,0:T(8,128)(2,1)S(1)}, bf16[1,128,1024]{2,1,0:T(8,128)(2,1)S(1)}, u32[]{:S(2)}, u32[]{:S(2)}) collective-permute-start(bf16[1,128,1024]{2,1,0:T(8,128)(2,1)S(1)} %add_convert_fusion.3), channel_id=1, source_target_pairs={{0,2},{1,3},{2,0},{3,1},{4,6},{5,7},{6,4},{7,5},{8,10},{9,11},{10,... | collective-permute-start | bytes 786440 | tf_op jit(solution)/shard_map/ppermute | solution.py:296
  177.5 51.0 %collective-permute-start.26 = (bf16[3,4,224,512]{3,2,1,0:T(8,128)(2,1)S(1)}, bf16[3,4,224,512]{3,2,1,0:T(8,128)(2,1)S(1)}, u32[]{:S(2)}, u32[]{:S(2)}) collective-permute-start(bf16[3,4,224,512]{3,2,1,0:T(8,128)(2,1)S(1)} %shard_map.72), channel_id=1, source_target_pairs={{0,4},{4,0},{8,12},{12,8},{16,20},{20,16},{24,28},{28,24},{1,5},{5... | collective-permute-start | bytes 8257544 | tf_op jit(solution)/shard_map/ppermute | solution.py:293
  181.6 14.4 %collective-permute-start.37 = (bf16[2,128,1024]{2,1,0:T(8,128)(2,1)S(1)}, bf16[2,128,1024]{2,1,0:T(8,128)(2,1)S(1)}, u32[]{:S(2)}, u32[]{:S(2)}) collective-permute-start(bf16[2,128,1024]{2,1,0:T(8,128)(2,1)S(1)} %get-tuple-element.102), channel_id=1, source_target_pairs={{0,1},{1,0},{2,3},{3,2},{4,5},{5,4},{6,7},{7,6},{8,9},{9,8},{10,11... | collective-permute-start | bytes 1572872 | tf_op jit(solution)/shard_map/ppermute | solution.py:296
  196.1 15.2 %collective-permute-start.38 = (bf16[1,128,1024]{2,1,0:T(8,128)(2,1)S(1)}, bf16[1,128,1024]{2,1,0:T(8,128)(2,1)S(1)}, u32[]{:S(2)}, u32[]{:S(2)}) collective-permute-start(bf16[1,128,1024]{2,1,0:T(8,128)(2,1)S(1)} %add_convert_fusion.2), channel_id=1, source_target_pairs={{0,2},{1,3},{2,0},{3,1},{4,6},{5,7},{6,4},{7,5},{8,10},{9,11},{10,... | collective-permute-start | bytes 786440 | tf_op jit(solution)/shard_map/ppermute | solution.py:296
  211.8 13.5 %collective-permute-start.42 = (bf16[128,1024]{1,0:T(8,128)(2,1)S(1)}, bf16[128,1024]{1,0:T(8,128)(2,1)S(1)}, u32[]{:S(2)}, u32[]{:S(2)}) collective-permute-start(bf16[128,1024]{1,0:T(8,128)(2,1)S(1)} %shard_map.78.hid_ref), channel_id=1, source_target_pairs={{0,2},{1,3},{2,0},{3,1},{4,6},{5,7},{6,4},{7,5},{8,10},{9,11},{10,... | collective-permute-start | bytes 786440 | tf_op jit(solution)/shard_map/ppermute | solution.py:296
  211.9 24.1 %collective-permute-start.40 = (bf16[128,1024]{1,0:T(8,128)(2,1)S(1)}, bf16[128,1024]{1,0:T(8,128)(2,1)S(1)}, u32[]{:S(2)}, u32[]{:S(2)}) collective-permute-start(bf16[128,1024]{1,0:T(8,128)(2,1)S(1)} %shard_map.78.hid_ref), channel_id=1, source_target_pairs={{0,1},{1,0},{2,3},{3,2},{4,5},{5,4},{6,7},{7,6},{8,9},{9,8},{10,11... | collective-permute-start | bytes 786440 | tf_op jit(solution)/shard_map/ppermute | solution.py:296
  225.3 18.5 %collective-permute-start.44 = (bf16[128,1024]{1,0:T(8,128)(2,1)S(1)}, bf16[128,1024]{1,0:T(8,128)(2,1)S(1)}, u32[]{:S(2)}, u32[]{:S(2)}) collective-permute-start(bf16[128,1024]{1,0:T(8,128)(2,1)S(1)} %collective-permute-done.42.hid_ref), channel_id=1, source_target_pairs={{0,1},{1,0},{2,3},{3,2},{4,5},{5,4},{6,7},{7,6},{8,9},{9,8},{10,11... | collective-permute-start | bytes 786440 | tf_op jit(solution)/shard_map/ppermute | solution.py:296
  225.3 23.5 %collective-permute-start.28 = (bf16[128,1024]{1,0:T(8,128)(2,1)S(1)}, bf16[128,1024]{1,0:T(8,128)(2,1)S(1)}, u32[]{:S(2)}, u32[]{:S(2)}) collective-permute-start(bf16[128,1024]{1,0:T(8,128)(2,1)S(1)} %shard_map.71.hid_ref), channel_id=1, source_target_pairs={{0,1},{1,0},{2,3},{3,2},{4,5},{5,4},{6,7},{7,6},{8,9},{9,8},{10,11... | collective-permute-start | bytes 786440 | tf_op jit(solution)/shard_map/ppermute | solution.py:296
  227.3 25.2 %collective-permute-start.30 = (bf16[128,1024]{1,0:T(8,128)(2,1)S(1)}, bf16[128,1024]{1,0:T(8,128)(2,1)}, u32[]{:S(2)}, u32[]{:S(2)}) collective-permute-start(bf16[128,1024]{1,0:T(8,128)(2,1)S(1)} %shard_map.71.hid_ref), channel_id=1, source_target_pairs={{0,2},{1,3},{2,0},{3,1},{4,6},{5,7},{6,4},{7,5},{8,10},{9,11},{10,... | collective-permute-start | bytes 786440 | tf_op jit(solution)/shard_map/ppermute | solution.py:296
  231.0 35.0 %collective-permute-start.39 = (bf16[128,1792]{1,0:T(8,128)(2,1)}, bf16[128,1792]{1,0:T(8,128)(2,1)}, u32[]{:S(2)}, u32[]{:S(2)}) collective-permute-start(bf16[128,1792]{1,0:T(8,128)(2,1)} %shard_map.79), channel_id=1, source_target_pairs={{0,0},{1,9},{2,18},{3,27},{4,4},{5,13},{6,22},{7,31},{8,8},{9,1},{... | collective-permute-start | bytes 1376264 | tf_op jit(solution)/shard_map/ppermute | solution.py:304
  238.5 30.4 %collective-permute-start.41 = (bf16[128,1792]{1,0:T(8,128)(2,1)}, bf16[128,1792]{1,0:T(8,128)(2,1)}, u32[]{:S(2)}, u32[]{:S(2)}) collective-permute-start(bf16[128,1792]{1,0:T(8,128)(2,1)} %shard_map.80), channel_id=1, source_target_pairs={{0,8},{1,1},{2,26},{3,19},{4,12},{5,5},{6,30},{7,23},{8,0},{9,9},{... | collective-permute-start | bytes 1376264 | tf_op jit(solution)/shard_map/ppermute | solution.py:304
  243.8 27.6 %collective-permute-start.43 = (bf16[128,1792]{1,0:T(8,128)(2,1)}, bf16[128,1792]{1,0:T(8,128)(2,1)}, u32[]{:S(2)}, u32[]{:S(2)}) collective-permute-start(bf16[128,1792]{1,0:T(8,128)(2,1)} %shard_map.81), channel_id=1, source_target_pairs={{0,16},{1,25},{2,2},{3,11},{4,20},{5,29},{6,6},{7,15},{8,24},{9,17... | collective-permute-start | bytes 1376264 | tf_op jit(solution)/shard_map/ppermute | solution.py:304
  248.8 26.4 %collective-permute-start.45 = (bf16[128,1792]{1,0:T(8,128)(2,1)}, bf16[128,1792]{1,0:T(8,128)(2,1)}, u32[]{:S(2)}, u32[]{:S(2)}) collective-permute-start(bf16[128,1792]{1,0:T(8,128)(2,1)} %shard_map.82), channel_id=1, source_target_pairs={{0,24},{1,17},{2,10},{3,3},{4,28},{5,21},{6,14},{7,7},{8,16},{9,25... | collective-permute-start | bytes 1376264 | tf_op jit(solution)/shard_map/ppermute | solution.py:304
  252.6 9.8 %collective-permute-start.32 = (bf16[128,1024]{1,0:T(8,128)(2,1)}, bf16[128,1024]{1,0:T(8,128)(2,1)}, u32[]{:S(2)}, u32[]{:S(2)}) collective-permute-start(bf16[128,1024]{1,0:T(8,128)(2,1)} %collective-permute-done.30.hid_ref), channel_id=1, source_target_pairs={{0,1},{1,0},{2,3},{3,2},{4,5},{5,4},{6,7},{7,6},{8,9},{9,8},{10,11... | collective-permute-start | bytes 786440 | tf_op jit(solution)/shard_map/ppermute | solution.py:296
  262.4 14.6 %collective-permute-start.27 = (bf16[128,1792]{1,0:T(8,128)(2,1)S(1)}, bf16[128,1792]{1,0:T(8,128)(2,1)S(1)}, u32[]{:S(2)}, u32[]{:S(2)}) collective-permute-start(bf16[128,1792]{1,0:T(8,128)(2,1)S(1)} %shard_map.73), channel_id=1, source_target_pairs={{0,0},{1,9},{2,18},{3,27},{4,4},{5,13},{6,22},{7,31},{8,8},{9,1},{... | collective-permute-start | bytes 1376264 | tf_op jit(solution)/shard_map/ppermute | solution.py:304
  265.9 18.8 %collective-permute-start.29 = (bf16[128,1792]{1,0:T(8,128)(2,1)S(1)}, bf16[128,1792]{1,0:T(8,128)(2,1)S(1)}, u32[]{:S(2)}, u32[]{:S(2)}) collective-permute-start(bf16[128,1792]{1,0:T(8,128)(2,1)S(1)} %shard_map.74), channel_id=1, source_target_pairs={{0,8},{1,1},{2,26},{3,19},{4,12},{5,5},{6,30},{7,23},{8,0},{9,9},{... | collective-permute-start | bytes 1376264 | tf_op jit(solution)/shard_map/ppermute | solution.py:304
  268.9 21.9 %collective-permute-start.31 = (bf16[128,1792]{1,0:T(8,128)(2,1)S(1)}, bf16[128,1792]{1,0:T(8,128)(2,1)S(1)}, u32[]{:S(2)}, u32[]{:S(2)}) collective-permute-start(bf16[128,1792]{1,0:T(8,128)(2,1)S(1)} %shard_map.75), channel_id=1, source_target_pairs={{0,16},{1,25},{2,2},{3,11},{4,20},{5,29},{6,6},{7,15},{8,24},{9,17... | collective-permute-start | bytes 1376264 | tf_op jit(solution)/shard_map/ppermute | solution.py:304
  271.4 19.3 %collective-permute-start.33 = (bf16[128,1792]{1,0:T(8,128)(2,1)S(1)}, bf16[128,1792]{1,0:T(8,128)(2,1)S(1)}, u32[]{:S(2)}, u32[]{:S(2)}) collective-permute-start(bf16[128,1792]{1,0:T(8,128)(2,1)S(1)} %shard_map.76), channel_id=1, source_target_pairs={{0,24},{1,17},{2,10},{3,3},{4,28},{5,21},{6,14},{7,7},{8,16},{9,25... | collective-permute-start | bytes 1376264 | tf_op jit(solution)/shard_map/ppermute | solution.py:304
  276.9 16.9 %collective-permute-start.46 = (bf16[32,1792]{1,0:T(8,128)(2,1)S(1)}, bf16[32,1792]{1,0:T(8,128)(2,1)S(1)}, u32[]{:S(2)}, u32[]{:S(2)}) collective-permute-start(bf16[32,1792]{1,0:T(8,128)(2,1)S(1)} %get-tuple-element.114), channel_id=1, source_target_pairs={{0,1},{1,0},{2,3},{3,2},{4,5},{5,4},{6,7},{7,6},{8,9},{9,8},{10,11... | collective-permute-start | bytes 344072 | tf_op jit(solution)/shard_map/ppermute | solution.py:296
  277.0 19.3 %collective-permute-start.47 = (bf16[32,1792]{1,0:T(8,128)(2,1)S(1)}, bf16[32,1792]{1,0:T(8,128)(2,1)S(1)}, u32[]{:S(2)}, u32[]{:S(2)}) collective-permute-start(bf16[32,1792]{1,0:T(8,128)(2,1)S(1)} %get-tuple-element.113), channel_id=1, source_target_pairs={{0,2},{1,3},{2,0},{3,1},{4,6},{5,7},{6,4},{7,5},{8,10},{9,11},{10,... | collective-permute-start | bytes 344072 | tf_op jit(solution)/shard_map/ppermute | solution.py:296
  284.7 11.6 %collective-permute-start.48 = (bf16[32,1792]{1,0:T(8,128)(2,1)S(1)}, bf16[32,1792]{1,0:T(8,128)(2,1)S(1)}, u32[]{:S(2)}, u32[]{:S(2)}) collective-permute-start(bf16[32,1792]{1,0:T(8,128)(2,1)S(1)} %get-tuple-element.112), channel_id=1, source_target_pairs={{0,3},{1,2},{2,1},{3,0},{4,7},{5,6},{6,5},{7,4},{8,11},{9,10},{10,... | collective-permute-start | bytes 344072 | tf_op jit(solution)/shard_map/ppermute | solution.py:296
  293.9 9.0 %collective-permute-start.35 = (bf16[32,1792]{1,0:T(8,128)(2,1)S(1)}, bf16[32,1792]{1,0:T(8,128)(2,1)S(1)}, u32[]{:S(2)}, u32[]{:S(2)}) collective-permute-start(bf16[32,1792]{1,0:T(8,128)(2,1)S(1)} %get-tuple-element.117), channel_id=1, source_target_pairs={{0,2},{1,3},{2,0},{3,1},{4,6},{5,7},{6,4},{7,5},{8,10},{9,11},{10,... | collective-permute-start | bytes 344072 | tf_op jit(solution)/shard_map/ppermute | solution.py:296
  293.9 9.0 %collective-permute-start.36 = (bf16[32,1792]{1,0:T(8,128)(2,1)S(1)}, bf16[32,1792]{1,0:T(8,128)(2,1)S(1)}, u32[]{:S(2)}, u32[]{:S(2)}) collective-permute-start(bf16[32,1792]{1,0:T(8,128)(2,1)S(1)} %get-tuple-element.116), channel_id=1, source_target_pairs={{0,3},{1,2},{2,1},{3,0},{4,7},{5,6},{6,5},{7,4},{8,11},{9,10},{10,... | collective-permute-start | bytes 344072 | tf_op jit(solution)/shard_map/ppermute | solution.py:296
  (14 other events, 146.1 us)

commit v6 on v5

--- a/solution.py
+++ b/solution.py
@@ -303,22 +303,26 @@
         ]
         return lax.ppermute(value, ("expert", "tensor"), pairs)
 
-    def copies(value, send, bits):
+    def copies(value, send, bits, behind=()):
         held = {0: value}
         for bit in bits:
             for step in sorted(held):
-                held[step + bit] = send(held[step], bit)
+                held[step + bit] = send(after(held[step], behind), bit)
+            behind = ()
         return [held[step] for step in range(len(held))]
 
-    def level_sums(keep, send):
-        terms, bit = [keep], 1
+    def level_sums(keep, send, behind):
+        terms, marks, bit = [keep], [], 1
+        send = after(send, behind[:1])
         while True:
             terms.append(to_level(send, bit))
             bit *= 2
             if bit == n_tensor:
-                return terms
+                return terms, marks + [terms[-1]]
             send = sum(term[1::2].astype(jnp.float32) for term in terms).astype(jnp.bfloat16)
             terms = [term[::2] for term in terms]
+            send = after(send, behind[len(marks) + 1 : len(marks) + 2])
+            marks.append(send)
 
     def blocks_of(weight):
         return [
@@ -342,41 +346,46 @@
 
     gate_joined = join_blocks(place, gate_weight, after(gate_same, groups))
     gate_pair = core_exchange(gate_joined)
-    groups = after(groups, gate_joined)
     bits = [1 << bit for bit in range(chips.bit_length() - 1)]
     toks = []
     for half in range(HALVES):
         turn = (half + 1) % len(bits)
         toks.append(copies(groups[half], to_chip, bits[turn:] + bits[:turn]))
-    up_same = chip_exchange(after(blocks_of(up_weight), toks))
-
-    def products(weights, parts):
-        routings, sends = [], []
+    near = [tok[bit] for tok in toks for bit in bits]
+    up_same = chip_exchange(after(blocks_of(up_weight), near))
+
+    def products(weights, before, late):
+        sums, routings, parts = [], [], []
+        behind = before[-1][1] if before else []
         for half in range(HALVES):
-            left = after(toks[half], parts)
-            *parts, routing = picked_sums(place, left, weights, slots)
+            others = [parts, behind[:1], [marks for _, marks in before[half : half + 1]]]
+            others += late if half else []
+            *parts, routing = picked_sums(place, after(toks[half], others), weights, slots)
+            terms, behind = level_sums(*parts, behind)
+            sums.append((terms, behind))
             routings.append(routing)
-            sends.append(parts)
-        sums = [level_sums(*parts) for parts in sends]
-        return routings, sums
-
-    routings, gate_sums = products(gate_pair, place)
-    up_joined = join_blocks(place, up_weight, after(up_same, [terms[:-1] for terms in gate_sums]))
+        return sums, routings
+
+    gate_sums, routings = products(gate_pair, [], up_same[: chips // 2])
+    up_joined = join_blocks(place, up_weight, after(up_same, gate_sums[-1][1][0]))
     up_pair = core_exchange(up_joined)
     down_same = chip_exchange(after(blocks_of(down_weight), up_joined))
-    _, up_sums = products(up_pair, gate_sums)
-    hiddens = [
-        hidden_rows(routings[half], gate_sums[half], up_sums[half], slots)
-        for half in range(HALVES)
-    ]
-    down_joined = join_blocks(place, down_weight, after(down_same, hiddens[0]))
-    down_pair = core_exchange(down_joined)
-
-    backs = []
+    up_sums, _ = products(up_pair, gate_sums, [])
+    hiddens, near, far = [], [], up_sums[-1][1][-1]
     bits = [1 << bit for bit in range(n_tensor.bit_length() - 1)]
     for half in range(HALVES):
-        routing = routings[half]
-        blocks = copies(hiddens[half], to_level, bits[::-1])
+        up_terms = after(up_sums[half][0], [up_sums[-1][1][0], near])
+        hidden = hidden_rows(routings[half], gate_sums[half][0], up_terms, slots)
+        hiddens.append(copies(hidden, to_level, bits[::-1], far))
+        near, far = hiddens[-1][1], hiddens[-1][n_tensor // 2]
+    down_joined = join_blocks(place, down_weight, after(down_same, [h[0] for h in hiddens]))
+    down_pair = core_exchange(down_joined)
+
+    backs, part = [], []
+    for half in range(HALVES):
+        routing, blocks = routings[half], after(hiddens[half], part)
+        if half + 1 < HALVES:
+            blocks[-1] = after(blocks[-1], hiddens[half + 1][n_tensor // 2])
         total = 0.0
         for step in range(n_tensor):
             part = down_sums(routing, blocks[step], down_pair, step, slots)

time: 306 us -> 313 us (1.023)
  waiting for transfers between devices: 161 us -> 176 us
  starting transfers between devices: 86.3 us -> 80 us
    ppermute x15, waiting for transfers between devices: 37.6 us -> 50.1 us  [to_chip(): return lax.ppermute(value, 'expert', pairs)]
    ppermute x23, waiting for transfers between devices: 119 us -> 108 us  [to_level(): lax.ppermute(value, 'tensor', [(s, s ^ step) for s in range(n_tensor)])]
    ppermute x8, waiting for transfers between devices: 4.07 us -> 12.9 us  [to_owner(): return lax.ppermute(value, ('expert', 'tensor'), pairs)]
    ppermute x23, starting transfers between devices: 44.1 us -> 36.1 us  [to_level(): lax.ppermute(value, 'tensor', [(s, s ^ step) for s in range(n_tensor)])]
    ppermute x3, waiting for transfers between devices: 0.01 us -> 5.09 us  [to_core(): return lax.ppermute(value, 'expert', [(s, s ^ 1) for s in range(n_expert)])]
    unnamed x26 -> x30, local copies, waits for them, and re-layouts: 6.29 us -> 7.71 us
  transfers between devices with their start and end apart: 49 -> 49, of which waited for: 19 -> 23; matrix products, arithmetic and copies ran while one was open for 1% -> 1% of each run, Pallas kernels for 11% -> 7%
where the time goes in v6:
time: 313 us
  waiting for transfers between devices  176 us (56%)
  starting transfers between devices  80 us (26%)
  Pallas kernels  42.3 us (14%)
  local copies, waits for them, and re-layouts  11.6 us (4%)
    ppermute x23, waiting for transfers between devices, to_level(): lax.ppermute(value, 'tensor', [(s, s ^ step) for s in range(n_tensor)])  108 us
    ppermute x15, waiting for transfers between devices, to_chip(): return lax.ppermute(value, 'expert', pairs)  50.1 us
    ppermute x23, starting transfers between devices, to_level(): lax.ppermute(value, 'tensor', [(s, s ^ step) for s in range(n_tensor)])  36.1 us
    ppermute x8, starting transfers between devices, to_owner(): return lax.ppermute(value, ('expert', 'tensor'), pairs)  24.9 us
    ppermute x15, starting transfers between devices, to_chip(): return lax.ppermute(value, 'expert', pairs)  18.7 us
    pallas_call x8, Pallas kernels, down_sums(): pl.pallas_call(functools.partial(down_kernel, step, slots), in_specs=[VME...  16.3 us
    pallas_call x4, Pallas kernels, picked_sums(): pl.pallas_call(functools.partial(pick_kernel, chips), in_specs=[SMEM_SPEC...  16.2 us
    ppermute x8, waiting for transfers between devices, to_owner(): return lax.ppermute(value, ('expert', 'tensor'), pairs)  12.9 us
  transfers between devices with their start and end apart: 49, of which 23 were waited for; matrix products, arithmetic and copies ran while one was open for 1% of the time, Pallas kernels for 7%

profile of v6, /device:TPU:0, one launch (start us, length us, event | category | flops | bytes accessed | tf_op | source)
XLA Modules:
  0.0 312.6 jit_solution(5256506360476915481)
XLA Ops:
  0.0 3.0 constant_dynamic-slice_fusion.6
  3.0 3.0 collective-permute-start.6
  13.2 2.6 collective-permute-start.1
  15.8 6.8 %collective-permute-done.refs_1_ = bf16[64,1792]{1,0:T(8,128)(2,1)S(1)} collective-permute-done((bf16[64,1792]{1,0:T(8,128)(2,1)S(1)}, bf16[64,1792]{1,0:T(8,128)(2,1)S(1)}, u32[]{:S(2)}, u32[]{:S(2)}) %collective-permute-start) | collective-permute-done | bytes 229408 | tf_op jit(solution)/shard_map/ppermute | solution.py:296
  23.2 2.6 collective-permute-start.2
  26.1 5.4 %collective-permute-done.2.refs_3_ = bf16[64,1792]{1,0:T(8,128)(2,1)} collective-permute-done((bf16[64,1792]{1,0:T(8,128)(2,1)}, bf16[64,1792]{1,0:T(8,128)(2,1)}, u32[]{:S(2)}, u32[]{:S(2)}) %collective-permute-start.2) | collective-permute-done | bytes 229408 | tf_op jit(solution)/shard_map/ppermute | solution.py:296
  34.5 3.4 %collective-permute-done.7.refs_1_ = bf16[3,224,512]{2,1,0:T(8,128)(2,1)} collective-permute-done((bf16[3,224,512]{2,1,0:T(8,128)(2,1)}, bf16[3,224,512]{2,1,0:T(8,128)(2,1)}, u32[]{:S(2)}, u32[]{:S(2)}) %collective-permute-start.7) | collective-permute-done | bytes 688160 | tf_op jit(solution)/shard_map/ppermute | solution.py:290
  37.9 2.1 shard_map.66
  42.2 11.5 %collective-permute-done.4.refs_2_ = bf16[128,1920]{1,0:T(8,128)(2,1)S(1)} collective-permute-done((bf16[128,1920]{1,0:T(8,128)(2,1)S(1)}, bf16[128,1920]{1,0:T(8,128)(2,1)S(1)}, u32[]{:S(2)}, u32[]{:S(2)}) %collective-permute-start.4) | collective-permute-done | bytes 491552 | tf_op jit(solution)/shard_map/ppermute | solution.py:290
  57.3 10.6 %collective-permute-done.5.refs_3_ = bf16[128,1920]{1,0:T(8,128)(2,1)S(1)} collective-permute-done((bf16[128,1920]{1,0:T(8,128)(2,1)S(1)}, bf16[128,1920]{1,0:T(8,128)(2,1)S(1)}, u32[]{:S(2)}, u32[]{:S(2)}) %collective-permute-start.5) | collective-permute-done | bytes 491552 | tf_op jit(solution)/shard_map/ppermute | solution.py:290
  67.9 4.1 %shard_map.67 = (bf16[2,128,1024]{2,1,0:T(8,128)(2,1)S(1)}, bf16[2,128,1024]{2,1,0:T(8,128)(2,1)S(1)}, bf16[4,128,128]{2,1,0:T(8,128)(2,1)S(1)}) custom-call(s32[3]{0:T(128)S(1)} %pad_add_fusion.place_ref, bf16[128,1920]{1,0:T(8,128)(2,1)S(1)} %get-tuple-element.101.refs_0_, bf16[128,1920]{1,0:T(8,128)(2,1)S(1)} %collective-permute-done.3.refs_1_, ...), custom_call_target="tpu_custom_call" | custom-call | flops 2818572288 | bytes 8388608 | tf_op jit(solution)/shard_map/pallas_call | solution.py:195
  73.8 3.2 %collective-permute-done.12.refs_1_ = bf16[128,1920]{1,0:T(8,128)(2,1)S(1)} collective-permute-done((bf16[128,1920]{1,0:T(8,128)(2,1)S(1)}, bf16[128,1920]{1,0:T(8,128)(2,1)S(1)}, u32[]{:S(2)}, u32[]{:S(2)}) %collective-permute-start.12) | collective-permute-done | bytes 491552 | tf_op jit(solution)/shard_map/ppermute | solution.py:290
  80.3 2.9 collective-permute-done.10
  83.3 21.3 %collective-permute-done.14.refs_3_ = bf16[128,1920]{1,0:T(8,128)(2,1)S(1)} collective-permute-done((bf16[128,1920]{1,0:T(8,128)(2,1)S(1)}, bf16[128,1920]{1,0:T(8,128)(2,1)S(1)}, u32[]{:S(2)}, u32[]{:S(2)}) %collective-permute-start.14) | collective-permute-done | bytes 491552 | tf_op jit(solution)/shard_map/ppermute | solution.py:290
  104.7 4.1 %shard_map.68 = (bf16[2,128,1024]{2,1,0:T(8,128)(2,1)S(1)}, bf16[2,128,1024]{2,1,0:T(8,128)(2,1)S(1)}, bf16[4,128,128]{2,1,0:T(8,128)(2,1)S(1)}) custom-call(s32[3]{0:T(128)S(1)} %pad_add_fusion.place_ref, bf16[128,1920]{1,0:T(8,128)(2,1)S(1)} %get-tuple-element.113.refs_0_, bf16[128,1920]{1,0:T(8,128)(2,1)S(1)} %collective-permute-done.12.refs_1_, ...), custom_call_target="tpu_custom_call" | custom-call | flops 2818572288 | bytes 8388608 | tf_op jit(solution)/shard_map/pallas_call | solution.py:195
  112.1 2.6 collective-permute-start.11
  114.7 11.1 %collective-permute-done.17 = bf16[2,128,1024]{2,1,0:T(8,128)(2,1)S(1)} collective-permute-done((bf16[2,128,1024]{2,1,0:T(8,128)(2,1)S(1)}, bf16[2,128,1024]{2,1,0:T(8,128)(2,1)S(1)}, u32[]{:S(2)}, u32[]{:S(2)}) %collective-permute-start.17) | collective-permute-done | bytes 524320 | tf_op jit(solution)/shard_map/ppermute | solution.py:296
  127.1 5.1 %collective-permute-done.19 = bf16[3,4,224,512]{3,2,1,0:T(8,128)(2,1)S(1)} collective-permute-done((bf16[3,4,224,512]{3,2,1,0:T(8,128)(2,1)S(1)}, bf16[3,4,224,512]{3,2,1,0:T(8,128)(2,1)S(1)}, u32[]{:S(2)}, u32[]{:S(2)}) %collective-permute-start.19) | collective-permute-done | bytes 2752544 | tf_op jit(solution)/shard_map/ppermute | solution.py:293
  132.2 4.1 %shard_map.70 = (bf16[2,128,1024]{2,1,0:T(8,128)(2,1)S(1)}, bf16[2,128,1024]{2,1,0:T(8,128)(2,1)S(1)}, bf16[4,128,128]{2,1,0:T(8,128)(2,1)}) custom-call(s32[3]{0:T(128)S(1)} %pad_add_fusion.place_ref, bf16[128,1920]{1,0:T(8,128)(2,1)S(1)} %get-tuple-element.101.refs_0_, bf16[128,1920]{1,0:T(8,128)(2,1)S(1)} %collective-permute-done.3.refs_1_, ...), custom_call_target="tpu_custom_call" | custom-call | flops 2818572288 | bytes 8388608 | tf_op jit(solution)/shard_map/pallas_call | solution.py:195
  136.2 2.6 collective-permute-start.20
  140.5 16.2 %collective-permute-done.20 = bf16[2,128,1024]{2,1,0:T(8,128)(2,1)S(1)} collective-permute-done((bf16[2,128,1024]{2,1,0:T(8,128)(2,1)S(1)}, bf16[2,128,1024]{2,1,0:T(8,128)(2,1)S(1)}, u32[]{:S(2)}, u32[]{:S(2)}) %collective-permute-start.20) | collective-permute-done | bytes 524320 | tf_op jit(solution)/shard_map/ppermute | solution.py:296
  156.7 4.1 %shard_map.71 = (bf16[2,128,1024]{2,1,0:T(8,128)(2,1)S(1)}, bf16[2,128,1024]{2,1,0:T(8,128)(2,1)S(1)}, bf16[4,128,128]{2,1,0:T(8,128)(2,1)}) custom-call(s32[3]{0:T(128)S(1)} %pad_add_fusion.place_ref, bf16[128,1920]{1,0:T(8,128)(2,1)S(1)} %get-tuple-element.113.refs_0_, bf16[128,1920]{1,0:T(8,128)(2,1)S(1)} %collective-permute-done.12.refs_1_, ...), custom_call_target="tpu_custom_call" | custom-call | flops 2818572288 | bytes 8388608 | tf_op jit(solution)/shard_map/pallas_call | solution.py:195
  168.2 11.8 %collective-permute-done.23 = bf16[2,128,1024]{2,1,0:T(8,128)(2,1)S(1)} collective-permute-done((bf16[2,128,1024]{2,1,0:T(8,128)(2,1)S(1)}, bf16[2,128,1024]{2,1,0:T(8,128)(2,1)S(1)}, u32[]{:S(2)}, u32[]{:S(2)}) %collective-permute-start.23) | collective-permute-done | bytes 524320 | tf_op jit(solution)/shard_map/ppermute | solution.py:296
  180.5 2.2 collective-permute-start.24
  183.7 8.4 %collective-permute-done.24.hid_ref = bf16[128,1024]{1,0:T(8,128)(2,1)S(1)} collective-permute-done((bf16[128,1024]{1,0:T(8,128)(2,1)S(1)}, bf16[128,1024]{1,0:T(8,128)(2,1)S(1)}, u32[]{:S(2)}, u32[]{:S(2)}) %collective-permute-start.24) | collective-permute-done | bytes 262176 | tf_op jit(solution)/shard_map/ppermute | solution.py:296
  192.1 3.4 %collective-permute-done.25.refs_5_ = bf16[1,128,1024]{2,1,0:T(8,128)(2,1)S(1)} collective-permute-done((bf16[1,128,1024]{2,1,0:T(8,128)(2,1)S(1)}, bf16[1,128,1024]{2,1,0:T(8,128)(2,1)S(1)}, u32[]{:S(2)}, u32[]{:S(2)}) %collective-permute-start.25) | collective-permute-done | bytes 262176 | tf_op jit(solution)/shard_map/ppermute | solution.py:296
  197.5 13.8 %collective-permute-done.26.hid_ref = bf16[128,1024]{1,0:T(8,128)(2,1)S(1)} collective-permute-done((bf16[128,1024]{1,0:T(8,128)(2,1)S(1)}, bf16[128,1024]{1,0:T(8,128)(2,1)S(1)}, u32[]{:S(2)}, u32[]{:S(2)}) %collective-permute-start.26) | collective-permute-done | bytes 262176 | tf_op jit(solution)/shard_map/ppermute | solution.py:296
  211.3 2.8 collective-permute-start.27
  214.8 11.0 %collective-permute-done.35.hid_ref = bf16[128,1024]{1,0:T(8,128)(2,1)S(1)} collective-permute-done((bf16[128,1024]{1,0:T(8,128)(2,1)S(1)}, bf16[128,1024]{1,0:T(8,128)(2,1)S(1)}, u32[]{:S(2)}, u32[]{:S(2)}) %collective-permute-start.35) | collective-permute-done | bytes 262176 | tf_op jit(solution)/shard_map/ppermute | solution.py:296
  229.2 3.2 %collective-permute-done.40.hid_ref = bf16[128,1024]{1,0:T(8,128)(2,1)S(1)} collective-permute-done((bf16[128,1024]{1,0:T(8,128)(2,1)S(1)}, bf16[128,1024]{1,0:T(8,128)(2,1)S(1)}, u32[]{:S(2)}, u32[]{:S(2)}) %collective-permute-start.40) | collective-permute-done | bytes 262176 | tf_op jit(solution)/shard_map/ppermute | solution.py:296
  232.4 4.8 %collective-permute-done.41.hid_ref = bf16[128,1024]{1,0:T(8,128)(2,1)S(1)} collective-permute-done((bf16[128,1024]{1,0:T(8,128)(2,1)S(1)}, bf16[128,1024]{1,0:T(8,128)(2,1)S(1)}, u32[]{:S(2)}, u32[]{:S(2)}) %collective-permute-start.41) | collective-permute-done | bytes 262176 | tf_op jit(solution)/shard_map/ppermute | solution.py:296
  237.2 2.4 shard_map.79
  239.7 5.1 %collective-permute-start.42 = (bf16[128,1792]{1,0:T(8,128)(2,1)}, bf16[128,1792]{1,0:T(8,128)(2,1)}, u32[]{:S(2)}, u32[]{:S(2)}) collective-permute-start(bf16[128,1792]{1,0:T(8,128)(2,1)} %shard_map.79), channel_id=1, source_target_pairs={{0,0},{1,9},{2,18},{3,27},{4,4},{5,13},{6,22},{7,31},{8,8},{9,1},{... | collective-permute-start | bytes 1376264 | tf_op jit(solution)/shard_map/ppermute | solution.py:304
  244.7 2.4 shard_map.80
  247.1 2.9 collective-permute-start.43
  250.1 2.4 shard_map.81
  252.5 3.4 %collective-permute-start.44 = (bf16[128,1792]{1,0:T(8,128)(2,1)}, bf16[128,1792]{1,0:T(8,128)(2,1)}, u32[]{:S(2)}, u32[]{:S(2)}) collective-permute-start(bf16[128,1792]{1,0:T(8,128)(2,1)} %shard_map.81), channel_id=1, source_target_pairs={{0,16},{1,25},{2,2},{3,11},{4,20},{5,29},{6,6},{7,15},{8,24},{9,17... | collective-permute-start | bytes 1376264 | tf_op jit(solution)/shard_map/ppermute | solution.py:304
  255.9 2.4 shard_map.82
  258.4 3.1 collective-permute-start.45
  261.5 3.7 %collective-permute-start.36 = (bf16[128,1792]{1,0:T(8,128)(2,1)}, bf16[128,1792]{1,0:T(8,128)(2,1)S(1)}, u32[]{:S(2)}, u32[]{:S(2)}) collective-permute-start(bf16[128,1792]{1,0:T(8,128)(2,1)} %copy-done.6), channel_id=1, source_target_pairs={{0,24},{1,17},{2,10},{3,3},{4,28},{5,21},{6,14},{7,7},{8,16},{9,25... | collective-permute-start | bytes 1376264 | tf_op jit(solution)/shard_map/ppermute | solution.py:304
  272.6 3.0 collective-permute-start.33
  275.6 10.5 %collective-permute-done.44 = bf16[128,1792]{1,0:T(8,128)(2,1)} collective-permute-done((bf16[128,1792]{1,0:T(8,128)(2,1)}, bf16[128,1792]{1,0:T(8,128)(2,1)}, u32[]{:S(2)}, u32[]{:S(2)}) %collective-permute-start.44) | collective-permute-done | bytes 458784 | tf_op jit(solution)/shard_map/ppermute | solution.py:304
  286.1 3.2 %collective-permute-start.34 = (bf16[128,1792]{1,0:T(8,128)(2,1)S(1)}, bf16[128,1792]{1,0:T(8,128)(2,1)S(1)}, u32[]{:S(2)}, u32[]{:S(2)}) collective-permute-start(bf16[128,1792]{1,0:T(8,128)(2,1)S(1)} %shard_map.77), channel_id=1, source_target_pairs={{0,16},{1,25},{2,2},{3,11},{4,20},{5,29},{6,6},{7,15},{8,24},{9,17... | collective-permute-start | bytes 1376264 | tf_op jit(solution)/shard_map/ppermute | solution.py:304
  291.1 3.0 collective-permute-start.47
  295.4 2.4 collective-permute-done.34
  298.9 3.7 %collective-permute-start.39 = (bf16[32,1792]{1,0:T(8,128)(2,1)S(1)}, bf16[32,1792]{1,0:T(8,128)(2,1)S(1)}, u32[]{:S(2)}, u32[]{:S(2)}) collective-permute-start(bf16[32,1792]{1,0:T(8,128)(2,1)S(1)} %get-tuple-element.158), channel_id=1, source_target_pairs={{0,3},{1,2},{2,1},{3,0},{4,7},{5,6},{6,5},{7,4},{8,11},{9,10},{10,... | collective-permute-start | bytes 344072 | tf_op jit(solution)/shard_map/ppermute | solution.py:296
  302.6 2.4 collective-permute-done.37.refs_1_
  305.0 5.7 %collective-permute-done.38.refs_2_ = bf16[32,1792]{1,0:T(8,128)(2,1)S(1)} collective-permute-done((bf16[32,1792]{1,0:T(8,128)(2,1)S(1)}, bf16[32,1792]{1,0:T(8,128)(2,1)S(1)}, u32[]{:S(2)}, u32[]{:S(2)}) %collective-permute-start.38) | collective-permute-done | bytes 114720 | tf_op jit(solution)/shard_map/ppermute | solution.py:296
  (125 shorter events, 56.8 us)
Async XLA Ops:
  3.0 31.5 %collective-permute-start.6 = (bf16[3,224,512]{2,1,0:T(8,128)(2,1)}, bf16[3,224,512]{2,1,0:T(8,128)(2,1)S(1)}, u32[]{:S(2)}, u32[]{:S(2)}) collective-permute-start(bf16[3,224,512]{2,1,0:T(8,128)(2,1)} %get-tuple-element.153), channel_id=1, source_target_pairs={{0,8},{4,12},{8,0},{12,4},{16,24},{20,28},{24,16},{28,20},{1,9},{5... | collective-permute-start | bytes 2064392 | tf_op jit(solution)/shard_map/ppermute | solution.py:290
  6.0 32.0 %collective-permute-start.7 = (bf16[3,224,512]{2,1,0:T(8,128)(2,1)}, bf16[3,224,512]{2,1,0:T(8,128)(2,1)}, u32[]{:S(2)}, u32[]{:S(2)}) collective-permute-start(bf16[3,224,512]{2,1,0:T(8,128)(2,1)} %get-tuple-element.152), channel_id=1, source_target_pairs={{0,16},{4,20},{8,24},{12,28},{16,0},{20,4},{24,8},{28,12},{1,17},{... | collective-permute-start | bytes 2064392 | tf_op jit(solution)/shard_map/ppermute | solution.py:290
  7.5 30.4 %collective-permute-start.8 = (bf16[3,224,512]{2,1,0:T(8,128)(2,1)}, bf16[3,224,512]{2,1,0:T(8,128)(2,1)}, u32[]{:S(2)}, u32[]{:S(2)}) collective-permute-start(bf16[3,224,512]{2,1,0:T(8,128)(2,1)} %get-tuple-element.151), channel_id=1, source_target_pairs={{0,24},{4,28},{8,16},{12,20},{16,8},{20,12},{24,0},{28,4},{1,25},{... | collective-permute-start | bytes 2064392 | tf_op jit(solution)/shard_map/ppermute | solution.py:290
  11.1 11.4 %collective-permute-start = (bf16[64,1792]{1,0:T(8,128)(2,1)S(1)}, bf16[64,1792]{1,0:T(8,128)(2,1)S(1)}, u32[]{:S(2)}, u32[]{:S(2)}) collective-permute-start(bf16[64,1792]{1,0:T(8,128)(2,1)S(1)} %get-tuple-element.76), channel_id=1, source_target_pairs={{0,1},{1,0},{2,3},{3,2},{4,5},{5,4},{6,7},{7,6},{8,9},{9,8},{10,11... | collective-permute-start | bytes 688136 | tf_op jit(solution)/shard_map/ppermute | solution.py:296
  13.2 12.9 %collective-permute-start.1 = (bf16[64,1792]{1,0:T(8,128)(2,1)}, bf16[64,1792]{1,0:T(8,128)(2,1)}, u32[]{:S(2)}, u32[]{:S(2)}) collective-permute-start(bf16[64,1792]{1,0:T(8,128)(2,1)} %get-tuple-element.77), channel_id=1, source_target_pairs={{0,2},{1,3},{2,0},{3,1},{4,6},{5,7},{6,4},{7,5},{8,10},{9,11},{10,... | collective-permute-start | bytes 688136 | tf_op jit(solution)/shard_map/ppermute | solution.py:296
  23.2 8.2 %collective-permute-start.2 = (bf16[64,1792]{1,0:T(8,128)(2,1)}, bf16[64,1792]{1,0:T(8,128)(2,1)}, u32[]{:S(2)}, u32[]{:S(2)}) collective-permute-start(bf16[64,1792]{1,0:T(8,128)(2,1)} %get-tuple-element.78), channel_id=1, source_target_pairs={{0,3},{1,2},{2,1},{3,0},{4,7},{5,6},{6,5},{7,4},{8,11},{9,10},{10,... | collective-permute-start | bytes 688136 | tf_op jit(solution)/shard_map/ppermute | solution.py:296
  40.0 27.9 %collective-permute-start.9 = (bf16[3,4,224,512]{3,2,1,0:T(8,128)(2,1)S(1)}, bf16[3,4,224,512]{3,2,1,0:T(8,128)(2,1)S(1)}, u32[]{:S(2)}, u32[]{:S(2)}) collective-permute-start(bf16[3,4,224,512]{3,2,1,0:T(8,128)(2,1)S(1)} %shard_map.66), channel_id=1, source_target_pairs={{0,4},{4,0},{8,12},{12,8},{16,20},{20,16},{24,28},{28,24},{1,5},{5... | collective-permute-start | bytes 8257544 | tf_op jit(solution)/shard_map/ppermute | solution.py:293
  40.1 13.6 %collective-permute-start.4 = (bf16[128,1920]{1,0:T(8,128)(2,1)S(1)}, bf16[128,1920]{1,0:T(8,128)(2,1)S(1)}, u32[]{:S(2)}, u32[]{:S(2)}) collective-permute-start(bf16[128,1920]{1,0:T(8,128)(2,1)S(1)} %get-tuple-element.101.refs_0_), channel_id=1, source_target_pairs={{0,16},{4,20},{8,24},{12,28},{16,0},{20,4},{24,8},{28,12},{1,17},{... | collective-permute-start | bytes 1474568 | tf_op jit(solution)/shard_map/ppermute | solution.py:290
  41.7 15.6 %collective-permute-start.3 = (bf16[128,1920]{1,0:T(8,128)(2,1)S(1)}, bf16[128,1920]{1,0:T(8,128)(2,1)S(1)}, u32[]{:S(2)}, u32[]{:S(2)}) collective-permute-start(bf16[128,1920]{1,0:T(8,128)(2,1)S(1)} %get-tuple-element.101.refs_0_), channel_id=1, source_target_pairs={{0,8},{4,12},{8,0},{12,4},{16,24},{20,28},{24,16},{28,20},{1,9},{5... | collective-permute-start | bytes 1474568 | tf_op jit(solution)/shard_map/ppermute | solution.py:290
  53.7 14.1 %collective-permute-start.5 = (bf16[128,1920]{1,0:T(8,128)(2,1)S(1)}, bf16[128,1920]{1,0:T(8,128)(2,1)S(1)}, u32[]{:S(2)}, u32[]{:S(2)}) collective-permute-start(bf16[128,1920]{1,0:T(8,128)(2,1)S(1)} %collective-permute-done.4.refs_2_), channel_id=1, source_target_pairs={{0,8},{4,12},{8,0},{12,4},{16,24},{20,28},{24,16},{28,20},{1,9},{5... | collective-permute-start | bytes 1474568 | tf_op jit(solution)/shard_map/ppermute | solution.py:290
  55.0 22.1 %collective-permute-start.12 = (bf16[128,1920]{1,0:T(8,128)(2,1)S(1)}, bf16[128,1920]{1,0:T(8,128)(2,1)S(1)}, u32[]{:S(2)}, u32[]{:S(2)}) collective-permute-start(bf16[128,1920]{1,0:T(8,128)(2,1)S(1)} %get-tuple-element.113.refs_0_), channel_id=1, source_target_pairs={{0,8},{4,12},{8,0},{12,4},{16,24},{20,28},{24,16},{28,20},{1,9},{5... | collective-permute-start | bytes 1474568 | tf_op jit(solution)/shard_map/ppermute | solution.py:290
  55.8 21.3 %collective-permute-start.13 = (bf16[128,1920]{1,0:T(8,128)(2,1)S(1)}, bf16[128,1920]{1,0:T(8,128)(2,1)S(1)}, u32[]{:S(2)}, u32[]{:S(2)}) collective-permute-start(bf16[128,1920]{1,0:T(8,128)(2,1)S(1)} %get-tuple-element.113.refs_0_), channel_id=1, source_target_pairs={{0,16},{4,20},{8,24},{12,28},{16,0},{20,4},{24,8},{28,12},{1,17},{... | collective-permute-start | bytes 1474568 | tf_op jit(solution)/shard_map/ppermute | solution.py:290
  71.9 11.3 %collective-permute-start.10 = (bf16[2,128,1024]{2,1,0:T(8,128)(2,1)S(1)}, bf16[2,128,1024]{2,1,0:T(8,128)(2,1)S(1)}, u32[]{:S(2)}, u32[]{:S(2)}) collective-permute-start(bf16[2,128,1024]{2,1,0:T(8,128)(2,1)S(1)} %get-tuple-element.90), channel_id=1, source_target_pairs={{0,1},{1,0},{2,3},{3,2},{4,5},{5,4},{6,7},{7,6},{8,9},{9,8},{10,11... | collective-permute-start | bytes 1572872 | tf_op jit(solution)/shard_map/ppermute | solution.py:296
  77.1 27.6 %collective-permute-start.15 = (bf16[3,224,512]{2,1,0:T(8,128)(2,1)S(1)}, bf16[3,224,512]{2,1,0:T(8,128)(2,1)S(1)}, u32[]{:S(2)}, u32[]{:S(2)}) collective-permute-start(bf16[3,224,512]{2,1,0:T(8,128)(2,1)S(1)} %get-tuple-element.91), channel_id=1, source_target_pairs={{0,8},{4,12},{8,0},{12,4},{16,24},{20,28},{24,16},{28,20},{1,9},{5... | collective-permute-start | bytes 2064392 | tf_op jit(solution)/shard_map/ppermute | solution.py:290
  78.3 26.4 %collective-permute-start.16 = (bf16[3,224,512]{2,1,0:T(8,128)(2,1)S(1)}, bf16[3,224,512]{2,1,0:T(8,128)(2,1)S(1)}, u32[]{:S(2)}, u32[]{:S(2)}) collective-permute-start(bf16[3,224,512]{2,1,0:T(8,128)(2,1)S(1)} %get-tuple-element.92), channel_id=1, source_target_pairs={{0,16},{4,20},{8,24},{12,28},{16,0},{20,4},{24,8},{28,12},{1,17},{... | collective-permute-start | bytes 2064392 | tf_op jit(solution)/shard_map/ppermute | solution.py:290
  79.1 25.5 %collective-permute-start.14 = (bf16[128,1920]{1,0:T(8,128)(2,1)S(1)}, bf16[128,1920]{1,0:T(8,128)(2,1)S(1)}, u32[]{:S(2)}, u32[]{:S(2)}) collective-permute-start(bf16[128,1920]{1,0:T(8,128)(2,1)S(1)} %collective-permute-done.12.refs_1_), channel_id=1, source_target_pairs={{0,16},{4,20},{8,24},{12,28},{16,0},{20,4},{24,8},{28,12},{1,17},{... | collective-permute-start | bytes 1474568 | tf_op jit(solution)/shard_map/ppermute | solution.py:290
  108.7 17.1 %collective-permute-start.17 = (bf16[2,128,1024]{2,1,0:T(8,128)(2,1)S(1)}, bf16[2,128,1024]{2,1,0:T(8,128)(2,1)S(1)}, u32[]{:S(2)}, u32[]{:S(2)}) collective-permute-start(bf16[2,128,1024]{2,1,0:T(8,128)(2,1)S(1)} %get-tuple-element.99), channel_id=1, source_target_pairs={{0,1},{1,0},{2,3},{3,2},{4,5},{5,4},{6,7},{7,6},{8,9},{9,8},{10,11... | collective-permute-start | bytes 1572872 | tf_op jit(solution)/shard_map/ppermute | solution.py:296
  110.4 15.5 %collective-permute-start.18 = (bf16[3,224,512]{2,1,0:T(8,128)(2,1)S(1)}, bf16[3,224,512]{2,1,0:T(8,128)(2,1)S(1)}, u32[]{:S(2)}, u32[]{:S(2)}) collective-permute-start(bf16[3,224,512]{2,1,0:T(8,128)(2,1)S(1)} %get-tuple-element.105), channel_id=1, source_target_pairs={{0,24},{4,28},{8,16},{12,20},{16,8},{20,12},{24,0},{28,4},{1,25},{... | collective-permute-start | bytes 2064392 | tf_op jit(solution)/shard_map/ppermute | solution.py:290
  112.1 13.8 %collective-permute-start.11 = (bf16[1,128,1024]{2,1,0:T(8,128)(2,1)S(1)}, bf16[1,128,1024]{2,1,0:T(8,128)(2,1)S(1)}, u32[]{:S(2)}, u32[]{:S(2)}) collective-permute-start(bf16[1,128,1024]{2,1,0:T(8,128)(2,1)S(1)} %add_convert_fusion.5), channel_id=1, source_target_pairs={{0,2},{1,3},{2,0},{3,1},{4,6},{5,7},{6,4},{7,5},{8,10},{9,11},{10,... | collective-permute-start | bytes 786440 | tf_op jit(solution)/shard_map/ppermute | solution.py:296
  136.2 20.4 %collective-permute-start.20 = (bf16[2,128,1024]{2,1,0:T(8,128)(2,1)S(1)}, bf16[2,128,1024]{2,1,0:T(8,128)(2,1)S(1)}, u32[]{:S(2)}, u32[]{:S(2)}) collective-permute-start(bf16[2,128,1024]{2,1,0:T(8,128)(2,1)S(1)} %get-tuple-element.111), channel_id=1, source_target_pairs={{0,1},{1,0},{2,3},{3,2},{4,5},{5,4},{6,7},{7,6},{8,9},{9,8},{10,11... | collective-permute-start | bytes 1572872 | tf_op jit(solution)/shard_map/ppermute | solution.py:296
  138.8 17.9 %collective-permute-start.21 = (bf16[1,128,1024]{2,1,0:T(8,128)(2,1)S(1)}, bf16[1,128,1024]{2,1,0:T(8,128)(2,1)S(1)}, u32[]{:S(2)}, u32[]{:S(2)}) collective-permute-start(bf16[1,128,1024]{2,1,0:T(8,128)(2,1)S(1)} %add_convert_fusion.4), channel_id=1, source_target_pairs={{0,2},{1,3},{2,0},{3,1},{4,6},{5,7},{6,4},{7,5},{8,10},{9,11},{10,... | collective-permute-start | bytes 786440 | tf_op jit(solution)/shard_map/ppermute | solution.py:296
  160.8 19.1 %collective-permute-start.23 = (bf16[2,128,1024]{2,1,0:T(8,128)(2,1)S(1)}, bf16[2,128,1024]{2,1,0:T(8,128)(2,1)S(1)}, u32[]{:S(2)}, u32[]{:S(2)}) collective-permute-start(bf16[2,128,1024]{2,1,0:T(8,128)(2,1)S(1)} %get-tuple-element.119), channel_id=1, source_target_pairs={{0,1},{1,0},{2,3},{3,2},{4,5},{5,4},{6,7},{7,6},{8,9},{9,8},{10,11... | collective-permute-start | bytes 1572872 | tf_op jit(solution)/shard_map/ppermute | solution.py:296
  162.8 33.2 %collective-permute-start.28 = (bf16[3,224,512]{2,1,0:T(8,128)(2,1)S(1)}, bf16[3,224,512]{2,1,0:T(8,128)(2,1)S(1)}, u32[]{:S(2)}, u32[]{:S(2)}) collective-permute-start(bf16[3,224,512]{2,1,0:T(8,128)(2,1)S(1)} %get-tuple-element.126), channel_id=1, source_target_pairs={{0,8},{4,12},{8,0},{12,4},{16,24},{20,28},{24,16},{28,20},{1,9},{5... | collective-permute-start | bytes 2064392 | tf_op jit(solution)/shard_map/ppermute | solution.py:290
  163.7 32.3 %collective-permute-start.29 = (bf16[3,224,512]{2,1,0:T(8,128)(2,1)S(1)}, bf16[3,224,512]{2,1,0:T(8,128)(2,1)S(1)}, u32[]{:S(2)}, u32[]{:S(2)}) collective-permute-start(bf16[3,224,512]{2,1,0:T(8,128)(2,1)S(1)} %get-tuple-element.127), channel_id=1, source_target_pairs={{0,16},{4,20},{8,24},{12,28},{16,0},{20,4},{24,8},{28,12},{1,17},{... | collective-permute-start | bytes 2064392 | tf_op jit(solution)/shard_map/ppermute | solution.py:290
  165.2 30.8 %collective-permute-start.30 = (bf16[3,224,512]{2,1,0:T(8,128)(2,1)S(1)}, bf16[3,224,512]{2,1,0:T(8,128)(2,1)S(1)}, u32[]{:S(2)}, u32[]{:S(2)}) collective-permute-start(bf16[3,224,512]{2,1,0:T(8,128)(2,1)S(1)} %get-tuple-element.128), channel_id=1, source_target_pairs={{0,24},{4,28},{8,16},{12,20},{16,8},{20,12},{24,0},{28,4},{1,25},{... | collective-permute-start | bytes 2064392 | tf_op jit(solution)/shard_map/ppermute | solution.py:290
  166.4 13.6 %collective-permute-start.22 = (bf16[1,128,1024]{2,1,0:T(8,128)(2,1)S(1)}, bf16[1,128,1024]{2,1,0:T(8,128)(2,1)S(1)}, u32[]{:S(2)}, u32[]{:S(2)}) collective-permute-start(bf16[1,128,1024]{2,1,0:T(8,128)(2,1)S(1)} %add_convert_fusion.3), channel_id=1, source_target_pairs={{0,2},{1,3},{2,0},{3,1},{4,6},{5,7},{6,4},{7,5},{8,10},{9,11},{10,... | collective-permute-start | bytes 786440 | tf_op jit(solution)/shard_map/ppermute | solution.py:296
  180.5 11.6 %collective-permute-start.24 = (bf16[128,1024]{1,0:T(8,128)(2,1)S(1)}, bf16[128,1024]{1,0:T(8,128)(2,1)S(1)}, u32[]{:S(2)}, u32[]{:S(2)}) collective-permute-start(bf16[128,1024]{1,0:T(8,128)(2,1)S(1)} %shard_map.72.hid_ref), channel_id=1, source_target_pairs={{0,1},{1,0},{2,3},{3,2},{4,5},{5,4},{6,7},{7,6},{8,9},{9,8},{10,11... | collective-permute-start | bytes 786440 | tf_op jit(solution)/shard_map/ppermute | solution.py:296
  182.7 12.9 %collective-permute-start.25 = (bf16[1,128,1024]{2,1,0:T(8,128)(2,1)S(1)}, bf16[1,128,1024]{2,1,0:T(8,128)(2,1)S(1)}, u32[]{:S(2)}, u32[]{:S(2)}) collective-permute-start(bf16[1,128,1024]{2,1,0:T(8,128)(2,1)S(1)} %add_convert_fusion.2), channel_id=1, source_target_pairs={{0,2},{1,3},{2,0},{3,1},{4,6},{5,7},{6,4},{7,5},{8,10},{9,11},{10,... | collective-permute-start | bytes 786440 | tf_op jit(solution)/shard_map/ppermute | solution.py:296
  197.0 29.8 %collective-permute-start.31 = (bf16[3,4,224,512]{3,2,1,0:T(8,128)(2,1)S(1)}, bf16[3,4,224,512]{3,2,1,0:T(8,128)(2,1)S(1)}, u32[]{:S(2)}, u32[]{:S(2)}) collective-permute-start(bf16[3,4,224,512]{3,2,1,0:T(8,128)(2,1)S(1)} %shard_map.74), channel_id=1, source_target_pairs={{0,4},{4,0},{8,12},{12,8},{16,20},{20,16},{24,28},{28,24},{1,5},{5... | collective-permute-start | bytes 8257544 | tf_op jit(solution)/shard_map/ppermute | solution.py:293
  197.1 14.2 %collective-permute-start.26 = (bf16[128,1024]{1,0:T(8,128)(2,1)S(1)}, bf16[128,1024]{1,0:T(8,128)(2,1)S(1)}, u32[]{:S(2)}, u32[]{:S(2)}) collective-permute-start(bf16[128,1024]{1,0:T(8,128)(2,1)S(1)} %shard_map.72.hid_ref), channel_id=1, source_target_pairs={{0,2},{1,3},{2,0},{3,1},{4,6},{5,7},{6,4},{7,5},{8,10},{9,11},{10,... | collective-permute-start | bytes 786440 | tf_op jit(solution)/shard_map/ppermute | solution.py:296
  211.3 14.5 %collective-permute-start.35 = (bf16[128,1024]{1,0:T(8,128)(2,1)S(1)}, bf16[128,1024]{1,0:T(8,128)(2,1)S(1)}, u32[]{:S(2)}, u32[]{:S(2)}) collective-permute-start(bf16[128,1024]{1,0:T(8,128)(2,1)S(1)} %shard_map.73.hid_ref), channel_id=1, source_target_pairs={{0,2},{1,3},{2,0},{3,1},{4,6},{5,7},{6,4},{7,5},{8,10},{9,11},{10,... | collective-permute-start | bytes 786440 | tf_op jit(solution)/shard_map/ppermute | solution.py:296
  211.3 15.5 %collective-permute-start.27 = (bf16[128,1024]{1,0:T(8,128)(2,1)S(1)}, bf16[128,1024]{1,0:T(8,128)(2,1)S(1)}, u32[]{:S(2)}, u32[]{:S(2)}) collective-permute-start(bf16[128,1024]{1,0:T(8,128)(2,1)S(1)} %collective-permute-done.26.hid_ref), channel_id=1, source_target_pairs={{0,1},{1,0},{2,3},{3,2},{4,5},{5,4},{6,7},{7,6},{8,9},{9,8},{10,11... | collective-permute-start | bytes 786440 | tf_op jit(solution)/shard_map/ppermute | solution.py:296
  214.8 17.6 %collective-permute-start.40 = (bf16[128,1024]{1,0:T(8,128)(2,1)S(1)}, bf16[128,1024]{1,0:T(8,128)(2,1)S(1)}, u32[]{:S(2)}, u32[]{:S(2)}) collective-permute-start(bf16[128,1024]{1,0:T(8,128)(2,1)S(1)} %shard_map.73.hid_ref), channel_id=1, source_target_pairs={{0,1},{1,0},{2,3},{3,2},{4,5},{5,4},{6,7},{7,6},{8,9},{9,8},{10,11... | collective-permute-start | bytes 786440 | tf_op jit(solution)/shard_map/ppermute | solution.py:296
  225.8 11.4 %collective-permute-start.41 = (bf16[128,1024]{1,0:T(8,128)(2,1)S(1)}, bf16[128,1024]{1,0:T(8,128)(2,1)S(1)}, u32[]{:S(2)}, u32[]{:S(2)}) collective-permute-start(bf16[128,1024]{1,0:T(8,128)(2,1)S(1)} %collective-permute-done.35.hid_ref), channel_id=1, source_target_pairs={{0,1},{1,0},{2,3},{3,2},{4,5},{5,4},{6,7},{7,6},{8,9},{9,8},{10,11... | collective-permute-start | bytes 786440 | tf_op jit(solution)/shard_map/ppermute | solution.py:296
  239.7 32.2 %collective-permute-start.42 = (bf16[128,1792]{1,0:T(8,128)(2,1)}, bf16[128,1792]{1,0:T(8,128)(2,1)}, u32[]{:S(2)}, u32[]{:S(2)}) collective-permute-start(bf16[128,1792]{1,0:T(8,128)(2,1)} %shard_map.79), channel_id=1, source_target_pairs={{0,0},{1,9},{2,18},{3,27},{4,4},{5,13},{6,22},{7,31},{8,8},{9,1},{... | collective-permute-start | bytes 1376264 | tf_op jit(solution)/shard_map/ppermute | solution.py:304
  247.1 25.5 %collective-permute-start.43 = (bf16[128,1792]{1,0:T(8,128)(2,1)}, bf16[128,1792]{1,0:T(8,128)(2,1)}, u32[]{:S(2)}, u32[]{:S(2)}) collective-permute-start(bf16[128,1792]{1,0:T(8,128)(2,1)} %shard_map.80), channel_id=1, source_target_pairs={{0,8},{1,1},{2,26},{3,19},{4,12},{5,5},{6,30},{7,23},{8,0},{9,9},{... | collective-permute-start | bytes 1376264 | tf_op jit(solution)/shard_map/ppermute | solution.py:304
  252.5 33.5 %collective-permute-start.44 = (bf16[128,1792]{1,0:T(8,128)(2,1)}, bf16[128,1792]{1,0:T(8,128)(2,1)}, u32[]{:S(2)}, u32[]{:S(2)}) collective-permute-start(bf16[128,1792]{1,0:T(8,128)(2,1)} %shard_map.81), channel_id=1, source_target_pairs={{0,16},{1,25},{2,2},{3,11},{4,20},{5,29},{6,6},{7,15},{8,24},{9,17... | collective-permute-start | bytes 1376264 | tf_op jit(solution)/shard_map/ppermute | solution.py:304
  258.4 30.9 %collective-permute-start.45 = (bf16[128,1792]{1,0:T(8,128)(2,1)}, bf16[128,1792]{1,0:T(8,128)(2,1)}, u32[]{:S(2)}, u32[]{:S(2)}) collective-permute-start(bf16[128,1792]{1,0:T(8,128)(2,1)} %shard_map.82), channel_id=1, source_target_pairs={{0,24},{1,17},{2,10},{3,3},{4,28},{5,21},{6,14},{7,7},{8,16},{9,25... | collective-permute-start | bytes 1376264 | tf_op jit(solution)/shard_map/ppermute | solution.py:304
  261.5 36.4 %collective-permute-start.36 = (bf16[128,1792]{1,0:T(8,128)(2,1)}, bf16[128,1792]{1,0:T(8,128)(2,1)S(1)}, u32[]{:S(2)}, u32[]{:S(2)}) collective-permute-start(bf16[128,1792]{1,0:T(8,128)(2,1)} %copy-done.6), channel_id=1, source_target_pairs={{0,24},{1,17},{2,10},{3,3},{4,28},{5,21},{6,14},{7,7},{8,16},{9,25... | collective-permute-start | bytes 1376264 | tf_op jit(solution)/shard_map/ppermute | solution.py:304
  271.9 19.1 %collective-permute-start.32 = (bf16[128,1792]{1,0:T(8,128)(2,1)S(1)}, bf16[128,1792]{1,0:T(8,128)(2,1)S(1)}, u32[]{:S(2)}, u32[]{:S(2)}) collective-permute-start(bf16[128,1792]{1,0:T(8,128)(2,1)S(1)} %shard_map.75), channel_id=1, source_target_pairs={{0,0},{1,9},{2,18},{3,27},{4,4},{5,13},{6,22},{7,31},{8,8},{9,1},{... | collective-permute-start | bytes 1376264 | tf_op jit(solution)/shard_map/ppermute | solution.py:304
  272.6 21.5 %collective-permute-start.33 = (bf16[128,1792]{1,0:T(8,128)(2,1)S(1)}, bf16[128,1792]{1,0:T(8,128)(2,1)S(1)}, u32[]{:S(2)}, u32[]{:S(2)}) collective-permute-start(bf16[128,1792]{1,0:T(8,128)(2,1)S(1)} %shard_map.76), channel_id=1, source_target_pairs={{0,8},{1,1},{2,26},{3,19},{4,12},{5,5},{6,30},{7,23},{8,0},{9,9},{... | collective-permute-start | bytes 1376264 | tf_op jit(solution)/shard_map/ppermute | solution.py:304
  286.1 11.8 %collective-permute-start.34 = (bf16[128,1792]{1,0:T(8,128)(2,1)S(1)}, bf16[128,1792]{1,0:T(8,128)(2,1)S(1)}, u32[]{:S(2)}, u32[]{:S(2)}) collective-permute-start(bf16[128,1792]{1,0:T(8,128)(2,1)S(1)} %shard_map.77), channel_id=1, source_target_pairs={{0,16},{1,25},{2,2},{3,11},{4,20},{5,29},{6,6},{7,15},{8,24},{9,17... | collective-permute-start | bytes 1376264 | tf_op jit(solution)/shard_map/ppermute | solution.py:304
  291.0 7.9 %collective-permute-start.46 = (bf16[32,1792]{1,0:T(8,128)(2,1)S(1)}, bf16[32,1792]{1,0:T(8,128)(2,1)S(1)}, u32[]{:S(2)}, u32[]{:S(2)}) collective-permute-start(bf16[32,1792]{1,0:T(8,128)(2,1)S(1)} %get-tuple-element.156), channel_id=1, source_target_pairs={{0,1},{1,0},{2,3},{3,2},{4,5},{5,4},{6,7},{7,6},{8,9},{9,8},{10,11... | collective-permute-start | bytes 344072 | tf_op jit(solution)/shard_map/ppermute | solution.py:296
  291.1 11.6 %collective-permute-start.47 = (bf16[32,1792]{1,0:T(8,128)(2,1)S(1)}, bf16[32,1792]{1,0:T(8,128)(2,1)S(1)}, u32[]{:S(2)}, u32[]{:S(2)}) collective-permute-start(bf16[32,1792]{1,0:T(8,128)(2,1)S(1)} %get-tuple-element.155), channel_id=1, source_target_pairs={{0,2},{1,3},{2,0},{3,1},{4,6},{5,7},{6,4},{7,5},{8,10},{9,11},{10,... | collective-permute-start | bytes 344072 | tf_op jit(solution)/shard_map/ppermute | solution.py:296
  294.1 8.5 %collective-permute-start.48 = (bf16[32,1792]{1,0:T(8,128)(2,1)S(1)}, bf16[32,1792]{1,0:T(8,128)(2,1)S(1)}, u32[]{:S(2)}, u32[]{:S(2)}) collective-permute-start(bf16[32,1792]{1,0:T(8,128)(2,1)S(1)} %get-tuple-element.154), channel_id=1, source_target_pairs={{0,3},{1,2},{2,1},{3,0},{4,7},{5,6},{6,5},{7,4},{8,11},{9,10},{10,... | collective-permute-start | bytes 344072 | tf_op jit(solution)/shard_map/ppermute | solution.py:296
  298.2 6.8 %collective-permute-start.37 = (bf16[32,1792]{1,0:T(8,128)(2,1)S(1)}, bf16[32,1792]{1,0:T(8,128)(2,1)S(1)}, u32[]{:S(2)}, u32[]{:S(2)}) collective-permute-start(bf16[32,1792]{1,0:T(8,128)(2,1)S(1)} %get-tuple-element.160), channel_id=1, source_target_pairs={{0,1},{1,0},{2,3},{3,2},{4,5},{5,4},{6,7},{7,6},{8,9},{9,8},{10,11... | collective-permute-start | bytes 344072 | tf_op jit(solution)/shard_map/ppermute | solution.py:296
  298.2 12.5 %collective-permute-start.38 = (bf16[32,1792]{1,0:T(8,128)(2,1)S(1)}, bf16[32,1792]{1,0:T(8,128)(2,1)S(1)}, u32[]{:S(2)}, u32[]{:S(2)}) collective-permute-start(bf16[32,1792]{1,0:T(8,128)(2,1)S(1)} %get-tuple-element.159), channel_id=1, source_target_pairs={{0,2},{1,3},{2,0},{3,1},{4,6},{5,7},{6,4},{7,5},{8,10},{9,11},{10,... | collective-permute-start | bytes 344072 | tf_op jit(solution)/shard_map/ppermute | solution.py:296
  298.9 11.9 %collective-permute-start.39 = (bf16[32,1792]{1,0:T(8,128)(2,1)S(1)}, bf16[32,1792]{1,0:T(8,128)(2,1)S(1)}, u32[]{:S(2)}, u32[]{:S(2)}) collective-permute-start(bf16[32,1792]{1,0:T(8,128)(2,1)S(1)} %get-tuple-element.158), channel_id=1, source_target_pairs={{0,3},{1,2},{2,1},{3,0},{4,7},{5,6},{6,5},{7,4},{8,11},{9,10},{10,... | collective-permute-start | bytes 344072 | tf_op jit(solution)/shard_map/ppermute | solution.py:296
  (16 other events, 145.0 us)

commit v7 on v5

--- a/solution.py
+++ b/solution.py
@@ -152,15 +152,19 @@
 
 
 def pick_kernel(chips, place_ref, *refs):
-    toks, refs = refs[:chips], refs[chips:]
-    weights, (keep_ref, send_ref, routing_ref, left) = refs[:CORES], refs[CORES:]
+    toks, refs = refs[: chips * HALVES], refs[chips * HALVES :]
+    weights, (*outs, routing_ref, left, ids_ref) = refs[:CORES], refs[CORES:]
     experts, depth, width = weights[0].shape
     rows = toks[0].shape[0]
-    for step, tok in enumerate(toks):
-        block = jnp.bitwise_xor(step, place_ref[2])
-        left[rows_of(block, rows), :] = tok[:, : CORES * depth]
-        routing_ref[block] = tok[:, CORES * depth :]
-    slots = keep_ref.shape[2] // width
+    for index, tok in enumerate(toks):
+        chip, half = index // HALVES, index % HALVES
+        routing_ref[index * rows : (index + 1) * rows, :] = tok[:, CORES * depth :]
+        block = jnp.bitwise_xor(chip, place_ref[2]) if len(outs) > 1 else chip
+        target = rows_of(block * HALVES + half, rows)
+        left[target, :] = tok[:, : CORES * depth]
+        ids_ref[target, :] = tok[:, CORES * depth :]
+    rows *= HALVES
+    slots = outs[0].shape[-1] // width
     tile = min(TILE, width)
     for start in range(0, width, tile):
         sums = []
@@ -174,30 +178,34 @@
                 )
                 total = term if total is None else total + term
             sums.append(total)
-        for step in range(chips):
-            out_ref = (keep_ref, send_ref)[step % 2]
-            ids = routing_ref[step].astype(jnp.float32)
-            for slot in range(slots):
-                chosen = ids[:, slot : slot + 1]
-                picked = sums[0][step * rows : (step + 1) * rows]
-                for which in range(1, experts):
-                    other = sums[which][step * rows : (step + 1) * rows]
-                    picked = jnp.where(chosen == which, other, picked)
-                first = slot * width + start
-                out_ref[step // 2, :, first : first + tile] = picked.astype(out_ref.dtype)
-
-
-def picked_sums(place, toks, weights, slots):
-    chips, rows = len(toks), toks[0].shape[0]
+        ids = ids_ref[...].astype(jnp.float32)
+        for slot in range(slots):
+            chosen = ids[:, slot : slot + 1]
+            picked = sums[0]
+            for which in range(1, experts):
+                picked = jnp.where(chosen == which, sums[which], picked)
+            picked = picked.astype(left.dtype)
+            first = slot * width + start
+            for step in range(chips):
+                part = picked[step * rows : (step + 1) * rows]
+                out_ref = outs[step % len(outs)]
+                out_ref[step // len(outs), :, first : first + tile] = part
+
+
+def picked_sums(place, toks, weights, slots, split):
     experts, depth, width = weights[0].shape
-    wide = CORES * depth
+    wide, chips = CORES * depth, len(toks) // HALVES
+    rows = HALVES * toks[0].shape[0]
     count = chips * rows
     return pl.pallas_call(
         functools.partial(pick_kernel, chips),
-        in_specs=[SMEM_SPEC] + [VMEM_SPEC] * (chips + CORES),
-        out_specs=[VMEM_SPEC] * 3,
-        out_shape=[bf16(chips // 2, rows, slots * width)] * 2 + [bf16(chips, rows, LANES)],
-        scratch_shapes=[pltpu.VMEM((count, wide), jnp.bfloat16)],
+        in_specs=[SMEM_SPEC] + [VMEM_SPEC] * (len(toks) + CORES),
+        out_specs=[VMEM_SPEC] * (split + 1),
+        out_shape=[bf16(chips // split, rows, slots * width)] * split + [bf16(count, LANES)],
+        scratch_shapes=[
+            pltpu.VMEM((count, wide), jnp.bfloat16),
+            pltpu.VMEM((count, LANES), jnp.bfloat16),
+        ],
         cost_estimate=cost(
             2 * count * wide * width * experts,
             count * wide + experts * wide * width + count * slots * width,
@@ -206,39 +214,43 @@
     )(place, *toks, *weights)
 
 
-def hidden_kernel(terms, slots, routing_ref, *refs):
-    gates, ups, out_ref = refs[:terms], refs[terms : 2 * terms], refs[2 * terms]
-    scores = routing_ref[0].astype(jnp.float32)[:, slots : 2 * slots]
+def hidden_kernel(slots, place_ref, routing_ref, up_ref, *refs):
+    gates, out_ref = refs[:-1], refs[-1]
+    rows, wide = out_ref.shape
+    scores = routing_ref[rows_of(place_ref[2], rows), :].astype(jnp.float32)
+    scores = scores[:, slots : 2 * slots]
     combine = scores / jnp.sum(scores, axis=1, keepdims=True)
-    width = out_ref.shape[1] // slots
+    width = wide // slots
     for slot in range(slots):
         columns = slice(slot * width, (slot + 1) * width)
         gate_sum = sum(ref[0, :, columns].astype(jnp.float32) for ref in gates)
-        up_sum = sum(ref[0, :, columns].astype(jnp.float32) for ref in ups)
+        up_sum = up_ref[:, columns].astype(jnp.float32)
         value = gate_sum / (1.0 + jnp.exp(-gate_sum)) * up_sum * combine[:, slot : slot + 1]
         out_ref[:, columns] = value.astype(out_ref.dtype)
 
 
-def hidden_rows(routing, gates, ups, slots):
-    return pl.pallas_call(
-        functools.partial(hidden_kernel, len(gates), slots),
-        in_specs=[VMEM_SPEC] * (1 + 2 * len(gates)),
+def hidden_rows(place, routing, gate_terms, up_sum, slots):
+    return pl.pallas_call(
+        functools.partial(hidden_kernel, slots),
+        in_specs=[SMEM_SPEC] + [VMEM_SPEC] * (2 + len(gate_terms)),
         out_specs=VMEM_SPEC,
-        out_shape=bf16(*gates[0].shape[1:]),
-        compiler_params=PARAMS,
-    )(routing, *gates, *ups)
-
-
-def down_kernel(step, slots, routing_ref, hid_ref, *refs):
+        out_shape=bf16(*up_sum.shape),
+        compiler_params=PARAMS,
+    )(place, routing, up_sum, *gate_terms)
+
+
+def down_kernel(step, part, parts, slots, place_ref, routing_ref, hid_ref, *refs):
     weights, (out_ref,) = refs[:CORES], refs[CORES:]
     experts, depth, width = weights[0].shape
-    ids = routing_ref[step].astype(jnp.float32)
+    rows = hid_ref.shape[0]
+    block = jnp.bitwise_xor(place_ref[2], step) * parts + part
+    ids = routing_ref[rows_of(block, rows), :].astype(jnp.float32)
     lefts = []
     for which in range(experts):
-        mine = jnp.zeros((hid_ref.shape[0], width), jnp.float32)
+        mine = jnp.zeros((rows, width), jnp.float32)
         for slot in range(slots):
-            part = hid_ref[:, slot * width : (slot + 1) * width].astype(jnp.float32)
-            mine = jnp.where(ids[:, slot : slot + 1] == which, part, mine)
+            value = hid_ref[:, slot * width : (slot + 1) * width].astype(jnp.float32)
+            mine = jnp.where(ids[:, slot : slot + 1] == which, value, mine)
         lefts.append(mine.astype(hid_ref.dtype))
     for side, weight in enumerate(weights):
         total = None
@@ -253,13 +265,13 @@
         out_ref[:, side * depth : (side + 1) * depth] = total.astype(out_ref.dtype)
 
 
-def down_sums(routing, hidden, weights, step, slots):
+def down_sums(place, routing, hidden, weights, step, part, parts, slots):
     rows = hidden.shape[0]
     experts, depth, width = weights[0].shape
     wide = CORES * depth
     return pl.pallas_call(
-        functools.partial(down_kernel, step, slots),
-        in_specs=[VMEM_SPEC] * (2 + CORES),
+        functools.partial(down_kernel, step, part, parts, slots),
+        in_specs=[SMEM_SPEC] + [VMEM_SPEC] * (2 + CORES),
         out_specs=VMEM_SPEC,
         out_shape=bf16(rows, wide),
         cost_estimate=cost(
@@ -267,7 +279,7 @@
             rows * slots * width + experts * wide * width + rows * wide,
         ),
         compiler_params=PARAMS,
-    )(routing, hidden, *weights)
+    )(place, routing, hidden, *weights)
 
 
 def after(values, others):
@@ -310,16 +322,6 @@
                 held[step + bit] = send(held[step], bit)
         return [held[step] for step in range(len(held))]
 
-    def level_sums(keep, send):
-        terms, bit = [keep], 1
-        while True:
-            terms.append(to_level(send, bit))
-            bit *= 2
-            if bit == n_tensor:
-                return terms
-            send = sum(term[1::2].astype(jnp.float32) for term in terms).astype(jnp.bfloat16)
-            terms = [term[::2] for term in terms]
-
     def blocks_of(weight):
         return [
             lax.dynamic_slice_in_dim(weight, (q ^ step) * width, width, 2)
@@ -348,43 +350,56 @@
     for half in range(HALVES):
         turn = (half + 1) % len(bits)
         toks.append(copies(groups[half], to_chip, bits[turn:] + bits[:turn]))
+
+    left = [toks[half][step] for step in range(chips) for half in range(HALVES)]
     up_same = chip_exchange(after(blocks_of(up_weight), toks))
-
-    def products(weights, parts):
-        routings, sends = [], []
-        for half in range(HALVES):
-            left = after(toks[half], parts)
-            *parts, routing = picked_sums(place, left, weights, slots)
-            routings.append(routing)
-            sends.append(parts)
-        sums = [level_sums(*parts) for parts in sends]
-        return routings, sums
-
-    routings, gate_sums = products(gate_pair, place)
-    up_joined = join_blocks(place, up_weight, after(up_same, [terms[:-1] for terms in gate_sums]))
+    keep, send, routing = picked_sums(place, left, gate_pair, slots, 2)
+    gate_terms, bit = [keep], 1
+    while True:
+        gate_terms.append(to_level(send, bit))
+        bit *= 2
+        if bit == n_tensor:
+            break
+        send = sum(term[1::2].astype(jnp.float32) for term in gate_terms).astype(jnp.bfloat16)
+        gate_terms = [term[::2] for term in gate_terms]
+    up_joined = join_blocks(place, up_weight, after(up_same, send))
     up_pair = core_exchange(up_joined)
     down_same = chip_exchange(after(blocks_of(down_weight), up_joined))
-    _, up_sums = products(up_pair, gate_sums)
-    hiddens = [
-        hidden_rows(routings[half], gate_sums[half], up_sums[half], slots)
-        for half in range(HALVES)
-    ]
-    down_joined = join_blocks(place, down_weight, after(down_same, hiddens[0]))
+    left = after(left, gate_terms[-1])
+    part, _ = picked_sums(place, left, up_pair, slots, 1)
+    part = part.reshape(-1, part.shape[2])
+    up_sum = lax.psum_scatter(part, "tensor", scatter_dimension=0, tiled=True)
+    down_joined = join_blocks(place, down_weight, after(down_same, up_sum))
     down_pair = core_exchange(down_joined)
-
-    backs = []
-    bits = [1 << bit for bit in range(n_tensor.bit_length() - 1)]
+    hidden = hidden_rows(place, routing, gate_terms, up_sum, slots)
+
+    count = hidden.shape[0] // HALVES
+    blocks, bit = {0: hidden}, n_tensor // 2
+    while bit:
+        for step in sorted(blocks):
+            if step + bit < n_tensor - 1:
+                blocks[step + bit] = to_level(blocks[step], bit)
+        bit //= 2
+    last = [blocks[n_tensor - 2][half * count : (half + 1) * count] for half in range(HALVES)]
+    last = [to_level(value, 1) for value in last]
+    blocks[n_tensor - 2] = after(blocks[n_tensor - 2], last[0])
+    terms, part = [[] for _ in range(HALVES)], []
+    for step in range(n_tensor - 1):
+        block = after(blocks[step], part)
+        part = down_sums(place, routing, block, down_pair, step, 0, 1, slots)
+        term = to_owner(part, step)
+        for half in range(HALVES):
+            terms[half].append(term[half * count : (half + 1) * count])
+    backs, step, total = [], n_tensor - 1, []
     for half in range(HALVES):
-        routing = routings[half]
-        blocks = copies(hiddens[half], to_level, bits[::-1])
-        total = 0.0
-        for step in range(n_tensor):
-            part = down_sums(routing, blocks[step], down_pair, step, slots)
-            total = total + to_owner(part, step).astype(jnp.float32)
+        block = after(last[half], part)
+        part = down_sums(place, routing, block, down_pair, step, half, HALVES, slots)
+        terms[half].append(to_owner(part, step))
+        total = sum(term.astype(jnp.float32) for term in after(terms[half], total))
         total = total.astype(jnp.bfloat16).reshape(n_tensor, rows // HALVES, -1)
-        for step in range(n_tensor):
-            piece = lax.dynamic_index_in_dim(total, level ^ step, 0, keepdims=False)
-            backs.append(to_level(piece, step) if step else piece)
+        for other in range(n_tensor):
+            piece = lax.dynamic_index_in_dim(total, level ^ other, 0, keepdims=False)
+            backs.append(to_level(piece, other) if other else piece)
     return finish(place, backs, n_tensor, depth)
 
 

time: 306 us -> 330 us (1.078)
  waiting for transfers between devices: 161 us -> 184 us
  starting transfers between devices: 86.3 us -> 66.9 us
  between operations: 0.47 us -> 13.8 us
  local copies, waits for them, and re-layouts: 10.2 us -> 22.8 us
  Pallas kernels: 44.4 us -> 39.7 us
    ppermute x23 -> x15, waiting for transfers between devices: 119 us -> 78.6 us  [to_level(): lax.ppermute(value, 'tensor', [(s, s ^ step) for s in range(n_tensor)])]
    ppermute x15, waiting for transfers between devices: 37.6 us -> 71.3 us  [to_chip(): return lax.ppermute(value, 'expert', pairs)]
    ppermute x8 -> x5, waiting for transfers between devices: 4.07 us -> 25.2 us  [to_owner(): return lax.ppermute(value, ('expert', 'tensor'), pairs)]
    ppermute x23 -> x15, starting transfers between devices: 44.1 us -> 27.3 us  [to_level(): lax.ppermute(value, 'tensor', [(s, s ^ step) for s in range(n_tensor)])]
    unnamed x26 -> x50, local copies, waits for them, and re-layouts: 6.29 us -> 15.6 us
    reduce_scatter x0 -> x1, waiting for transfers between devices: none -> 8.04 us  [local(): up_sum = lax.psum_scatter(part, 'tensor', scatter_dimension=0, tiled=True)]
    pallas_call x10 -> x6, Pallas kernels: 19.2 us -> 15.5 us  [the longest x5 14.3 us: down_sums(): pl.pallas_call(functools.partial(down_kernel, step, part, parts, slots),...]
    ppermute x8 -> x5, starting transfers between devices: 24.3 us -> 22 us  [to_owner(): return lax.ppermute(value, ('expert', 'tensor'), pairs)]
  transfers between devices with their start and end apart: 49 -> 39, of which waited for: 19 -> 20; matrix products, arithmetic and copies ran while one was open for 1% -> 1% of each run, Pallas kernels for 11% -> 6%
where the time goes in v7:
time: 330 us; the launch traced here: 328 us
  waiting for transfers between devices  184 us (56%)
  starting transfers between devices  66.9 us (20%)
  Pallas kernels  39.7 us (12%)
  local copies, waits for them, and re-layouts  22.8 us (7%)
  between operations  13.8 us (4%)
    ppermute x15, waiting for transfers between devices, to_level(): lax.ppermute(value, 'tensor', [(s, s ^ step) for s in range(n_tensor)])  78.6 us
    ppermute x15, waiting for transfers between devices, to_chip(): return lax.ppermute(value, 'expert', pairs)  71.3 us
    ppermute x15, starting transfers between devices, to_level(): lax.ppermute(value, 'tensor', [(s, s ^ step) for s in range(n_tensor)])  27.3 us
    ppermute x5, waiting for transfers between devices, to_owner(): return lax.ppermute(value, ('expert', 'tensor'), pairs)  25.2 us
    ppermute x5, starting transfers between devices, to_owner(): return lax.ppermute(value, ('expert', 'tensor'), pairs)  22 us
    ppermute x15, starting transfers between devices, to_chip(): return lax.ppermute(value, 'expert', pairs)  17.4 us
    unnamed x50, local copies, waits for them, and re-layouts  15.6 us
    pallas_call x2, Pallas kernels, picked_sums(): pl.pallas_call(functools.partial(pick_kernel, chips), in_specs=[SMEM_SPEC...  15.4 us
  transfers between devices with their start and end apart: 39, of which 20 were waited for; matrix products, arithmetic and copies ran while one was open for 1% of the time, Pallas kernels for 6%

profile of v7, /device:TPU:0, one launch (start us, length us, event | category | flops | bytes accessed | tf_op | source)
XLA Modules:
  0.0 328.4 jit_solution(8358634139979679682)
XLA Ops:
  6.5 3.0 constant_dynamic-slice_fusion.6
  9.6 2.9 collective-permute-start.3
  12.5 1.5 collective-permute-start.4
  15.3 1.7 shard_map.64
  17.7 2.1 collective-permute-start
  19.7 2.6 collective-permute-start.1
  22.3 6.8 %collective-permute-done.refs_1_ = bf16[64,1792]{1,0:T(8,128)(2,1)S(1)} collective-permute-done((bf16[64,1792]{1,0:T(8,128)(2,1)S(1)}, bf16[64,1792]{1,0:T(8,128)(2,1)S(1)}, u32[]{:S(2)}, u32[]{:S(2)}) %collective-permute-start) | collective-permute-done | bytes 229408 | tf_op jit(solution)/shard_map/ppermute | solution.py:308
  29.8 2.6 collective-permute-start.2
  32.6 5.4 %collective-permute-done.2.refs_3_ = bf16[64,1792]{1,0:T(8,128)(2,1)} collective-permute-done((bf16[64,1792]{1,0:T(8,128)(2,1)}, bf16[64,1792]{1,0:T(8,128)(2,1)}, u32[]{:S(2)}, u32[]{:S(2)}) %collective-permute-start.2) | collective-permute-done | bytes 229408 | tf_op jit(solution)/shard_map/ppermute | solution.py:308
  41.0 3.4 %collective-permute-done.4.refs_1_ = bf16[3,224,512]{2,1,0:T(8,128)(2,1)} collective-permute-done((bf16[3,224,512]{2,1,0:T(8,128)(2,1)}, bf16[3,224,512]{2,1,0:T(8,128)(2,1)}, u32[]{:S(2)}, u32[]{:S(2)}) %collective-permute-start.4) | collective-permute-done | bytes 688160 | tf_op jit(solution)/shard_map/ppermute | solution.py:302
  44.5 2.1 shard_map.66
  46.6 1.6 collective-permute-start.8
  50.8 10.0 %collective-permute-done.8.refs_4_ = bf16[128,1920]{1,0:T(8,128)(2,1)S(1)} collective-permute-done((bf16[128,1920]{1,0:T(8,128)(2,1)S(1)}, bf16[128,1920]{1,0:T(8,128)(2,1)S(1)}, u32[]{:S(2)}, u32[]{:S(2)}) %collective-permute-start.8) | collective-permute-done | bytes 491552 | tf_op jit(solution)/shard_map/ppermute | solution.py:302
  62.8 10.0 %collective-permute-done.6.refs_2_ = bf16[128,1920]{1,0:T(8,128)(2,1)S(1)} collective-permute-done((bf16[128,1920]{1,0:T(8,128)(2,1)S(1)}, bf16[128,1920]{1,0:T(8,128)(2,1)S(1)}, u32[]{:S(2)}, u32[]{:S(2)}) %collective-permute-start.6) | collective-permute-done | bytes 491552 | tf_op jit(solution)/shard_map/ppermute | solution.py:302
  72.8 9.8 %collective-permute-done.10.refs_6_ = bf16[128,1920]{1,0:T(8,128)(2,1)S(1)} collective-permute-done((bf16[128,1920]{1,0:T(8,128)(2,1)S(1)}, bf16[128,1920]{1,0:T(8,128)(2,1)S(1)}, u32[]{:S(2)}, u32[]{:S(2)}) %collective-permute-start.10) | collective-permute-done | bytes 491552 | tf_op jit(solution)/shard_map/ppermute | solution.py:302
  82.6 7.5 %shard_map.67 = (bf16[2,256,1024]{2,1,0:T(8,128)(2,1)S(1)}, bf16[2,256,1024]{2,1,0:T(8,128)(2,1)S(1)}, bf16[1024,128]{1,0:T(8,128)(2,1)S(1)}) custom-call(s32[3]{0:T(128)S(1)} %pad_add_fusion.place_ref, bf16[128,1920]{1,0:T(8,128)(2,1)S(1)} %get-tuple-element.67.refs_0_, bf16[128,1920]{1,0:T(8,128)(2,1)S(1)} %get-tuple-element.68.refs_1_, ...), custom_call_target="tpu_custom_call" | custom-call | flops 5637144576 | bytes 11272192 | tf_op jit(solution)/shard_map/pallas_call | solution.py:200
  90.1 1.6 collective-permute-start.13
  93.8 1.8 collective-permute-start.17
  95.5 19.0 %collective-permute-done.13 = bf16[2,256,1024]{2,1,0:T(8,128)(2,1)S(1)} collective-permute-done((bf16[2,256,1024]{2,1,0:T(8,128)(2,1)S(1)}, bf16[2,256,1024]{2,1,0:T(8,128)(2,1)S(1)}, u32[]{:S(2)}, u32[]{:S(2)}) %collective-permute-start.13) | collective-permute-done | bytes 1048608 | tf_op jit(solution)/shard_map/ppermute | solution.py:308
  114.8 9.1 %collective-permute-done.16.refs_1_ = bf16[3,224,512]{2,1,0:T(8,128)(2,1)S(1)} collective-permute-done((bf16[3,224,512]{2,1,0:T(8,128)(2,1)S(1)}, bf16[3,224,512]{2,1,0:T(8,128)(2,1)S(1)}, u32[]{:S(2)}, u32[]{:S(2)}) %collective-permute-start.16) | collective-permute-done | bytes 688160 | tf_op jit(solution)/shard_map/ppermute | solution.py:302
  124.9 2.2 collective-permute-start.14
  127.1 24.1 %collective-permute-done.14.refs_2_ = bf16[1,256,1024]{2,1,0:T(8,128)(2,1)S(1)} collective-permute-done((bf16[1,256,1024]{2,1,0:T(8,128)(2,1)S(1)}, bf16[1,256,1024]{2,1,0:T(8,128)(2,1)S(1)}, u32[]{:S(2)}, u32[]{:S(2)}) %collective-permute-start.14) | collective-permute-done | bytes 524320 | tf_op jit(solution)/shard_map/ppermute | solution.py:308
  151.2 8.0 %shard_map.69 = (bf16[4,256,1024]{2,1,0:T(8,128)(2,1)S(1)}, bf16[1024,128]{1,0:T(8,128)(2,1)}) custom-call(s32[3]{0:T(128)S(1)} %pad_add_fusion.place_ref, bf16[128,1920]{1,0:T(8,128)(2,1)S(1)} %get-tuple-element.67.refs_0_, bf16[128,1920]{1,0:T(8,128)(2,1)S(1)} %get-tuple-element.68.refs_1_, bf16[128,1920]{1,0:T(8,128)(2,1)S(1)} %collective-permute-done.6.refs_2_, ...), custom_call_target="tpu_custom_call" | custom-call | flops 5637144576 | bytes 11272192 | tf_op jit(solution)/shard_map/pallas_call | solution.py:200
  162.6 1.8 collective-permute-start.21
  164.3 14.8 %collective-permute-done.19.refs_0_ = bf16[3,224,512]{2,1,0:T(8,128)(2,1)S(1)} collective-permute-done((bf16[3,224,512]{2,1,0:T(8,128)(2,1)S(1)}, bf16[3,224,512]{2,1,0:T(8,128)(2,1)S(1)}, u32[]{:S(2)}, u32[]{:S(2)}) %collective-permute-start.19) | collective-permute-done | bytes 688160 | tf_op jit(solution)/shard_map/ppermute | solution.py:302
  180.0 13.8 %collective-permute-done.20.refs_1_ = bf16[3,224,512]{2,1,0:T(8,128)(2,1)S(1)} collective-permute-done((bf16[3,224,512]{2,1,0:T(8,128)(2,1)S(1)}, bf16[3,224,512]{2,1,0:T(8,128)(2,1)S(1)}, u32[]{:S(2)}, u32[]{:S(2)}) %collective-permute-start.20) | collective-permute-done | bytes 688160 | tf_op jit(solution)/shard_map/ppermute | solution.py:302
  195.5 8.0 %reduce-scatter.2.cloned.1.call-done.up_ref = bf16[256,1024]{1,0:T(8,128)(2,1)} async-done(((bf16[1024,1024]{1,0:T(8,128)(2,1)}), bf16[256,1024]{1,0:T(8,128)(2,1)}) %reduce-scatter.2.cloned.1.call-update) | async-done | bytes 524304 | tf_op jit(solution)/shard_map/reduce_scatter | solution.py:371
  203.6 1.8 copy-done.5
  211.6 1.8 collective-permute-start.26
  215.0 3.3 %shard_map.72 = bf16[256,1792]{1,0:T(8,128)(2,1)} custom-call(s32[3]{0:T(128)S(1)} %pad_add_fusion.place_ref, bf16[1024,128]{1,0:T(8,128)(2,1)S(1)} %get-tuple-element.64.routing_ref, bf16[256,1024]{1,0:T(8,128)(2,1)S(1)} %shard_map.70.hid_ref, bf16[3,896,512]{2,1,0:T(8,128)(2,1)S(1)} %bitcast.28, bf16[3,896,512]{2,1,0:T(8,128)(2,1)S(1)} %bitcast.33), custom_call_target="tpu_custom_call" | custom-call | flops 1409286144 | bytes 6946816 | tf_op jit(solution)/shard_map/pallas_call | solution.py:272
  218.3 8.4 %collective-permute-start.23 = (bf16[256,1792]{1,0:T(8,128)(2,1)}, bf16[256,1792]{1,0:T(8,128)(2,1)}, u32[]{:S(2)}, u32[]{:S(2)}) collective-permute-start(bf16[256,1792]{1,0:T(8,128)(2,1)} %shard_map.72), channel_id=1, source_target_pairs={{0,0},{1,9},{2,18},{3,27},{4,4},{5,13},{6,22},{7,31},{8,8},{9,1},{... | collective-permute-start | bytes 2752520 | tf_op jit(solution)/shard_map/ppermute | solution.py:316
  226.6 10.0 %collective-permute-done.26.hid_ref = bf16[256,1024]{1,0:T(8,128)(2,1)S(1)} collective-permute-done((bf16[256,1024]{1,0:T(8,128)(2,1)S(1)}, bf16[256,1024]{1,0:T(8,128)(2,1)S(1)}, u32[]{:S(2)}, u32[]{:S(2)}) %collective-permute-start.26) | collective-permute-done | bytes 524320 | tf_op jit(solution)/shard_map/ppermute | solution.py:308
  238.2 3.3 %shard_map.73 = bf16[256,1792]{1,0:T(8,128)(2,1)} custom-call(s32[3]{0:T(128)S(1)} %pad_add_fusion.place_ref, bf16[1024,128]{1,0:T(8,128)(2,1)S(1)} %get-tuple-element.64.routing_ref, bf16[256,1024]{1,0:T(8,128)(2,1)S(1)} %collective-permute-done.24.hid_ref, bf16[3,896,512]{2,1,0:T(8,128)(2,1)S(1)} %bitcast.29, bf16[3,896,512]{2,1,0:T(8,128)(2,1)S(1)} %bitcast.34), custom_call_target="tpu_custom_call" | custom-call | flops 1409286144 | bytes 6946816 | tf_op jit(solution)/shard_map/pallas_call | solution.py:272
  241.6 3.4 %collective-permute-start.25 = (bf16[256,1792]{1,0:T(8,128)(2,1)}, bf16[256,1792]{1,0:T(8,128)(2,1)}, u32[]{:S(2)}, u32[]{:S(2)}) collective-permute-start(bf16[256,1792]{1,0:T(8,128)(2,1)} %shard_map.73), channel_id=1, source_target_pairs={{0,8},{1,1},{2,26},{3,19},{4,12},{5,5},{6,30},{7,23},{8,0},{9,9},{... | collective-permute-start | bytes 2752520 | tf_op jit(solution)/shard_map/ppermute | solution.py:316
  244.9 6.3 %collective-permute-start.33 = (bf16[128,1024]{1,0:T(8,128)(2,1)}, bf16[128,1024]{1,0:T(8,128)(2,1)}, u32[]{:S(2)}, u32[]{:S(2)}) collective-permute-start(bf16[128,1024]{1,0:T(8,128)(2,1)} %get-tuple-element.116), channel_id=1, source_target_pairs={{0,1},{1,0},{2,3},{3,2},{4,5},{5,4},{6,7},{7,6},{8,9},{9,8},{10,11... | collective-permute-start | bytes 786440 | tf_op jit(solution)/shard_map/ppermute | solution.py:308
  251.3 1.8 copy-done.1
  253.0 2.4 shard_map.74
  255.4 3.5 %collective-permute-start.28 = (bf16[256,1792]{1,0:T(8,128)(2,1)S(1)}, bf16[256,1792]{1,0:T(8,128)(2,1)S(1)}, u32[]{:S(2)}, u32[]{:S(2)}) collective-permute-start(bf16[256,1792]{1,0:T(8,128)(2,1)S(1)} %shard_map.74), channel_id=1, source_target_pairs={{0,16},{1,25},{2,2},{3,11},{4,20},{5,29},{6,6},{7,15},{8,24},{9,17... | collective-permute-start | bytes 2752520 | tf_op jit(solution)/shard_map/ppermute | solution.py:316
  259.0 2.6 shard_map.75
  261.6 3.4 %collective-permute-start.29 = (bf16[128,1792]{1,0:T(8,128)(2,1)S(1)}, bf16[128,1792]{1,0:T(8,128)(2,1)S(1)}, u32[]{:S(2)}, u32[]{:S(2)}) collective-permute-start(bf16[128,1792]{1,0:T(8,128)(2,1)S(1)} %shard_map.75), channel_id=1, source_target_pairs={{0,24},{1,17},{2,10},{3,3},{4,28},{5,21},{6,14},{7,7},{8,16},{9,25... | collective-permute-start | bytes 1376264 | tf_op jit(solution)/shard_map/ppermute | solution.py:316
  265.0 2.6 shard_map.76
  267.6 3.4 %collective-permute-start.34 = (bf16[128,1792]{1,0:T(8,128)(2,1)S(1)}, bf16[128,1792]{1,0:T(8,128)(2,1)S(1)}, u32[]{:S(2)}, u32[]{:S(2)}) collective-permute-start(bf16[128,1792]{1,0:T(8,128)(2,1)S(1)} %shard_map.76), channel_id=1, source_target_pairs={{0,24},{1,17},{2,10},{3,3},{4,28},{5,21},{6,14},{7,7},{8,16},{9,25... | collective-permute-start | bytes 1376264 | tf_op jit(solution)/shard_map/ppermute | solution.py:316
  273.5 25.2 %collective-permute-done.28 = bf16[256,1792]{1,0:T(8,128)(2,1)S(1)} collective-permute-done((bf16[256,1792]{1,0:T(8,128)(2,1)S(1)}, bf16[256,1792]{1,0:T(8,128)(2,1)S(1)}, u32[]{:S(2)}, u32[]{:S(2)}) %collective-permute-start.28) | collective-permute-done | bytes 917536 | tf_op jit(solution)/shard_map/ppermute | solution.py:316
  299.2 4.3 %collective-permute-start.32 = (bf16[32,1792]{1,0:T(8,128)(2,1)S(1)}, bf16[32,1792]{1,0:T(8,128)(2,1)S(1)}, u32[]{:S(2)}, u32[]{:S(2)}) collective-permute-start(bf16[32,1792]{1,0:T(8,128)(2,1)S(1)} %get-tuple-element.122), channel_id=1, source_target_pairs={{0,3},{1,2},{2,1},{3,0},{4,7},{5,6},{6,5},{7,4},{8,11},{9,10},{10,... | collective-permute-start | bytes 344072 | tf_op jit(solution)/shard_map/ppermute | solution.py:308
  305.5 2.7 collective-permute-start.37
  308.2 6.5 %collective-permute-done.31.refs_2_ = bf16[32,1792]{1,0:T(8,128)(2,1)S(1)} collective-permute-done((bf16[32,1792]{1,0:T(8,128)(2,1)S(1)}, bf16[32,1792]{1,0:T(8,128)(2,1)S(1)}, u32[]{:S(2)}, u32[]{:S(2)}) %collective-permute-start.31) | collective-permute-done | bytes 114720 | tf_op jit(solution)/shard_map/ppermute | solution.py:308
  314.8 4.9 %collective-permute-done.36.refs_6_ = bf16[32,1792]{1,0:T(8,128)(2,1)S(1)} collective-permute-done((bf16[32,1792]{1,0:T(8,128)(2,1)S(1)}, bf16[32,1792]{1,0:T(8,128)(2,1)S(1)}, u32[]{:S(2)}, u32[]{:S(2)}) %collective-permute-start.36) | collective-permute-done | bytes 114720 | tf_op jit(solution)/shard_map/ppermute | solution.py:308
  319.7 1.9 shard_map.77
  (115 shorter events, 34.0 us)
Async XLA Ops:
  6.5 25.9 %copy-start.23 = (s32[256,2]{0,1:T(2,128)S(1)}, s32[256,2]{0,1:T(2,128)}, u32[]{:S(2)}) copy-start(s32[256,2]{0,1:T(2,128)} %param.8) | copy-start | bytes 6148
  6.5 25.9 %copy-start.24 = (s32[256,2]{0,1:T(2,128)S(1)}, s32[256,2]{0,1:T(2,128)}, u32[]{:S(2)}) copy-start(s32[256,2]{0,1:T(2,128)} %param.7) | copy-start | bytes 6148
  6.5 197.0 %reduce-scatter.2.cloned.1.call-start = ((), (), s32[]{:S(2)}) async-start(), calls=%async_computation.1 | async-start | bytes 2621440 | tf_op jit(solution)/shard_map/reduce_scatter | solution.py:371
  6.5 37.9 %copy-start.2 = (bf16[3,224,2048]{2,1,0:T(8,128)(2,1)S(1)}, bf16[3,224,2048]{2,1,0:T(8,128)(2,1)}, u32[]{:S(2)}) copy-start(bf16[3,224,2048]{2,1,0:T(8,128)(2,1)} %own_ref.3) | copy-start | bytes 8257540
  9.6 31.4 %collective-permute-start.3 = (bf16[3,224,512]{2,1,0:T(8,128)(2,1)}, bf16[3,224,512]{2,1,0:T(8,128)(2,1)S(1)}, u32[]{:S(2)}, u32[]{:S(2)}) collective-permute-start(bf16[3,224,512]{2,1,0:T(8,128)(2,1)} %get-tuple-element.109), channel_id=1, source_target_pairs={{0,8},{4,12},{8,0},{12,4},{16,24},{20,28},{24,16},{28,20},{1,9},{5... | collective-permute-start | bytes 2064392 | tf_op jit(solution)/shard_map/ppermute | solution.py:302
  12.5 32.0 %collective-permute-start.4 = (bf16[3,224,512]{2,1,0:T(8,128)(2,1)}, bf16[3,224,512]{2,1,0:T(8,128)(2,1)}, u32[]{:S(2)}, u32[]{:S(2)}) collective-permute-start(bf16[3,224,512]{2,1,0:T(8,128)(2,1)} %get-tuple-element.108), channel_id=1, source_target_pairs={{0,16},{4,20},{8,24},{12,28},{16,0},{20,4},{24,8},{28,12},{1,17},{... | collective-permute-start | bytes 2064392 | tf_op jit(solution)/shard_map/ppermute | solution.py:302
  14.0 30.4 %collective-permute-start.5 = (bf16[3,224,512]{2,1,0:T(8,128)(2,1)}, bf16[3,224,512]{2,1,0:T(8,128)(2,1)}, u32[]{:S(2)}, u32[]{:S(2)}) collective-permute-start(bf16[3,224,512]{2,1,0:T(8,128)(2,1)} %get-tuple-element.107), channel_id=1, source_target_pairs={{0,24},{4,28},{8,16},{12,20},{16,8},{20,12},{24,0},{28,4},{1,25},{... | collective-permute-start | bytes 2064392 | tf_op jit(solution)/shard_map/ppermute | solution.py:302
  17.7 11.4 %collective-permute-start = (bf16[64,1792]{1,0:T(8,128)(2,1)S(1)}, bf16[64,1792]{1,0:T(8,128)(2,1)S(1)}, u32[]{:S(2)}, u32[]{:S(2)}) collective-permute-start(bf16[64,1792]{1,0:T(8,128)(2,1)S(1)} %get-tuple-element.54), channel_id=1, source_target_pairs={{0,1},{1,0},{2,3},{3,2},{4,5},{5,4},{6,7},{7,6},{8,9},{9,8},{10,11... | collective-permute-start | bytes 688136 | tf_op jit(solution)/shard_map/ppermute | solution.py:308
  19.7 12.9 %collective-permute-start.1 = (bf16[64,1792]{1,0:T(8,128)(2,1)}, bf16[64,1792]{1,0:T(8,128)(2,1)}, u32[]{:S(2)}, u32[]{:S(2)}) collective-permute-start(bf16[64,1792]{1,0:T(8,128)(2,1)} %get-tuple-element.55), channel_id=1, source_target_pairs={{0,2},{1,3},{2,0},{3,1},{4,6},{5,7},{6,4},{7,5},{8,10},{9,11},{10,... | collective-permute-start | bytes 688136 | tf_op jit(solution)/shard_map/ppermute | solution.py:308
  29.8 8.2 %collective-permute-start.2 = (bf16[64,1792]{1,0:T(8,128)(2,1)}, bf16[64,1792]{1,0:T(8,128)(2,1)}, u32[]{:S(2)}, u32[]{:S(2)}) collective-permute-start(bf16[64,1792]{1,0:T(8,128)(2,1)} %get-tuple-element.56), channel_id=1, source_target_pairs={{0,3},{1,2},{2,1},{3,0},{4,7},{5,6},{6,5},{7,4},{8,11},{9,10},{10,... | collective-permute-start | bytes 688136 | tf_op jit(solution)/shard_map/ppermute | solution.py:308
  46.6 36.0 %collective-permute-start.12 = (bf16[3,4,224,512]{3,2,1,0:T(8,128)(2,1)S(1)}, bf16[3,4,224,512]{3,2,1,0:T(8,128)(2,1)S(1)}, u32[]{:S(2)}, u32[]{:S(2)}) collective-permute-start(bf16[3,4,224,512]{3,2,1,0:T(8,128)(2,1)S(1)} %shard_map.66), channel_id=1, source_target_pairs={{0,4},{4,0},{8,12},{12,8},{16,20},{20,16},{24,28},{28,24},{1,5},{5... | collective-permute-start | bytes 8257544 | tf_op jit(solution)/shard_map/ppermute | solution.py:305
  46.6 14.1 %collective-permute-start.8 = (bf16[128,1920]{1,0:T(8,128)(2,1)S(1)}, bf16[128,1920]{1,0:T(8,128)(2,1)S(1)}, u32[]{:S(2)}, u32[]{:S(2)}) collective-permute-start(bf16[128,1920]{1,0:T(8,128)(2,1)S(1)} %get-tuple-element.67.refs_0_), channel_id=1, source_target_pairs={{0,16},{4,20},{8,24},{12,28},{16,0},{20,4},{24,8},{28,12},{1,17},{... | collective-permute-start | bytes 1474568 | tf_op jit(solution)/shard_map/ppermute | solution.py:302
  48.2 14.1 %collective-permute-start.7 = (bf16[128,1920]{1,0:T(8,128)(2,1)S(1)}, bf16[128,1920]{1,0:T(8,128)(2,1)S(1)}, u32[]{:S(2)}, u32[]{:S(2)}) collective-permute-start(bf16[128,1920]{1,0:T(8,128)(2,1)S(1)} %get-tuple-element.68.refs_1_), channel_id=1, source_target_pairs={{0,8},{4,12},{8,0},{12,4},{16,24},{20,28},{24,16},{28,20},{1,9},{5... | collective-permute-start | bytes 1474568 | tf_op jit(solution)/shard_map/ppermute | solution.py:302
  48.8 24.1 %collective-permute-start.6 = (bf16[128,1920]{1,0:T(8,128)(2,1)S(1)}, bf16[128,1920]{1,0:T(8,128)(2,1)S(1)}, u32[]{:S(2)}, u32[]{:S(2)}) collective-permute-start(bf16[128,1920]{1,0:T(8,128)(2,1)S(1)} %get-tuple-element.67.refs_0_), channel_id=1, source_target_pairs={{0,8},{4,12},{8,0},{12,4},{16,24},{20,28},{24,16},{28,20},{1,9},{5... | collective-permute-start | bytes 1474568 | tf_op jit(solution)/shard_map/ppermute | solution.py:302
  50.2 22.6 %collective-permute-start.9 = (bf16[128,1920]{1,0:T(8,128)(2,1)S(1)}, bf16[128,1920]{1,0:T(8,128)(2,1)S(1)}, u32[]{:S(2)}, u32[]{:S(2)}) collective-permute-start(bf16[128,1920]{1,0:T(8,128)(2,1)S(1)} %get-tuple-element.68.refs_1_), channel_id=1, source_target_pairs={{0,16},{4,20},{8,24},{12,28},{16,0},{20,4},{24,8},{28,12},{1,17},{... | collective-permute-start | bytes 1474568 | tf_op jit(solution)/shard_map/ppermute | solution.py:302
  60.7 21.9 %collective-permute-start.10 = (bf16[128,1920]{1,0:T(8,128)(2,1)S(1)}, bf16[128,1920]{1,0:T(8,128)(2,1)S(1)}, u32[]{:S(2)}, u32[]{:S(2)}) collective-permute-start(bf16[128,1920]{1,0:T(8,128)(2,1)S(1)} %collective-permute-done.8.refs_4_), channel_id=1, source_target_pairs={{0,8},{4,12},{8,0},{12,4},{16,24},{20,28},{24,16},{28,20},{1,9},{5... | collective-permute-start | bytes 1474568 | tf_op jit(solution)/shard_map/ppermute | solution.py:302
  62.3 20.3 %collective-permute-start.11 = (bf16[128,1920]{1,0:T(8,128)(2,1)S(1)}, bf16[128,1920]{1,0:T(8,128)(2,1)S(1)}, u32[]{:S(2)}, u32[]{:S(2)}) collective-permute-start(bf16[128,1920]{1,0:T(8,128)(2,1)S(1)} %collective-permute-done.7.refs_3_), channel_id=1, source_target_pairs={{0,16},{4,20},{8,24},{12,28},{16,0},{20,4},{24,8},{28,12},{1,17},{... | collective-permute-start | bytes 1474568 | tf_op jit(solution)/shard_map/ppermute | solution.py:302
  82.6 9.1 %copy-start.3 = (bf16[3,224,2048]{2,1,0:T(8,128)(2,1)S(1)}, bf16[3,224,2048]{2,1,0:T(8,128)(2,1)}, u32[]{:S(2)}) copy-start(bf16[3,224,2048]{2,1,0:T(8,128)(2,1)} %own_ref.4) | copy-start | bytes 8257540
  90.1 24.7 %copy-start.7 = (bf16[2,256,1024]{2,1,0:T(8,128)(2,1)}, bf16[2,256,1024]{2,1,0:T(8,128)(2,1)S(1)}, u32[]{:S(2)}) copy-start(bf16[2,256,1024]{2,1,0:T(8,128)(2,1)S(1)} %get-tuple-element.65) | copy-start | bytes 3145732
  90.1 24.5 %collective-permute-start.13 = (bf16[2,256,1024]{2,1,0:T(8,128)(2,1)S(1)}, bf16[2,256,1024]{2,1,0:T(8,128)(2,1)S(1)}, u32[]{:S(2)}, u32[]{:S(2)}) collective-permute-start(bf16[2,256,1024]{2,1,0:T(8,128)(2,1)S(1)} %get-tuple-element.66), channel_id=1, source_target_pairs={{0,1},{1,0},{2,3},{3,2},{4,5},{5,4},{6,7},{7,6},{8,9},{9,8},{10,11... | collective-permute-start | bytes 3145736 | tf_op jit(solution)/shard_map/ppermute | solution.py:308
  92.0 22.8 %collective-permute-start.15 = (bf16[3,224,512]{2,1,0:T(8,128)(2,1)S(1)}, bf16[3,224,512]{2,1,0:T(8,128)(2,1)S(1)}, u32[]{:S(2)}, u32[]{:S(2)}) collective-permute-start(bf16[3,224,512]{2,1,0:T(8,128)(2,1)S(1)} %get-tuple-element.75), channel_id=1, source_target_pairs={{0,8},{4,12},{8,0},{12,4},{16,24},{20,28},{24,16},{28,20},{1,9},{5... | collective-permute-start | bytes 2064392 | tf_op jit(solution)/shard_map/ppermute | solution.py:302
  93.0 30.9 %collective-permute-start.16 = (bf16[3,224,512]{2,1,0:T(8,128)(2,1)S(1)}, bf16[3,224,512]{2,1,0:T(8,128)(2,1)S(1)}, u32[]{:S(2)}, u32[]{:S(2)}) collective-permute-start(bf16[3,224,512]{2,1,0:T(8,128)(2,1)S(1)} %get-tuple-element.76), channel_id=1, source_target_pairs={{0,16},{4,20},{8,24},{12,28},{16,0},{20,4},{24,8},{28,12},{1,17},{... | collective-permute-start | bytes 2064392 | tf_op jit(solution)/shard_map/ppermute | solution.py:302
  93.8 30.2 %collective-permute-start.17 = (bf16[3,224,512]{2,1,0:T(8,128)(2,1)S(1)}, bf16[3,224,512]{2,1,0:T(8,128)(2,1)S(1)}, u32[]{:S(2)}, u32[]{:S(2)}) collective-permute-start(bf16[3,224,512]{2,1,0:T(8,128)(2,1)S(1)} %get-tuple-element.77), channel_id=1, source_target_pairs={{0,24},{4,28},{8,16},{12,20},{16,8},{20,12},{24,0},{28,4},{1,25},{... | collective-permute-start | bytes 2064392 | tf_op jit(solution)/shard_map/ppermute | solution.py:302
  114.5 10.3 %copy-start.21 = (bf16[2,256,1024]{2,1,0:T(8,128)(2,1)}, bf16[2,256,1024]{2,1,0:T(8,128)(2,1)S(1)}, u32[]{:S(2)}) copy-start(bf16[2,256,1024]{2,1,0:T(8,128)(2,1)S(1)} %collective-permute-done.13) | copy-start | bytes 3145732
  124.9 26.4 %collective-permute-start.18 = (bf16[3,4,224,512]{3,2,1,0:T(8,128)(2,1)S(1)}, bf16[3,4,224,512]{3,2,1,0:T(8,128)(2,1)S(1)}, u32[]{:S(2)}, u32[]{:S(2)}) collective-permute-start(bf16[3,4,224,512]{3,2,1,0:T(8,128)(2,1)S(1)} %shard_map.68), channel_id=1, source_target_pairs={{0,4},{4,0},{8,12},{12,8},{16,20},{20,16},{24,28},{28,24},{1,5},{5... | collective-permute-start | bytes 8257544 | tf_op jit(solution)/shard_map/ppermute | solution.py:305
  124.9 26.3 %collective-permute-start.14 = (bf16[1,256,1024]{2,1,0:T(8,128)(2,1)S(1)}, bf16[1,256,1024]{2,1,0:T(8,128)(2,1)S(1)}, u32[]{:S(2)}, u32[]{:S(2)}) collective-permute-start(bf16[1,256,1024]{2,1,0:T(8,128)(2,1)S(1)} %add_convert_fusion), channel_id=1, source_target_pairs={{0,2},{1,3},{2,0},{3,1},{4,6},{5,7},{6,4},{7,5},{8,10},{9,11},{10,... | collective-permute-start | bytes 1572872 | tf_op jit(solution)/shard_map/ppermute | solution.py:308
  151.2 9.3 %copy-start.4 = (bf16[3,224,2048]{2,1,0:T(8,128)(2,1)S(1)}, bf16[3,224,2048]{2,1,0:T(8,128)(2,1)}, u32[]{:S(2)}) copy-start(bf16[3,224,2048]{2,1,0:T(8,128)(2,1)} %own_ref.5) | copy-start | bytes 8257540
  160.8 18.4 %collective-permute-start.19 = (bf16[3,224,512]{2,1,0:T(8,128)(2,1)S(1)}, bf16[3,224,512]{2,1,0:T(8,128)(2,1)S(1)}, u32[]{:S(2)}, u32[]{:S(2)}) collective-permute-start(bf16[3,224,512]{2,1,0:T(8,128)(2,1)S(1)} %get-tuple-element.82), channel_id=1, source_target_pairs={{0,8},{4,12},{8,0},{12,4},{16,24},{20,28},{24,16},{28,20},{1,9},{5... | collective-permute-start | bytes 2064392 | tf_op jit(solution)/shard_map/ppermute | solution.py:302
  161.9 31.9 %collective-permute-start.20 = (bf16[3,224,512]{2,1,0:T(8,128)(2,1)S(1)}, bf16[3,224,512]{2,1,0:T(8,128)(2,1)S(1)}, u32[]{:S(2)}, u32[]{:S(2)}) collective-permute-start(bf16[3,224,512]{2,1,0:T(8,128)(2,1)S(1)} %get-tuple-element.83), channel_id=1, source_target_pairs={{0,16},{4,20},{8,24},{12,28},{16,0},{20,4},{24,8},{28,12},{1,17},{... | collective-permute-start | bytes 2064392 | tf_op jit(solution)/shard_map/ppermute | solution.py:302
  162.6 32.1 %collective-permute-start.21 = (bf16[3,224,512]{2,1,0:T(8,128)(2,1)S(1)}, bf16[3,224,512]{2,1,0:T(8,128)(2,1)S(1)}, u32[]{:S(2)}, u32[]{:S(2)}) collective-permute-start(bf16[3,224,512]{2,1,0:T(8,128)(2,1)S(1)} %get-tuple-element.84), channel_id=1, source_target_pairs={{0,24},{4,28},{8,16},{12,20},{16,8},{20,12},{24,0},{28,4},{1,25},{... | collective-permute-start | bytes 2064392 | tf_op jit(solution)/shard_map/ppermute | solution.py:302
  209.8 5.2 %collective-permute-start.22 = (bf16[3,4,224,512]{3,2,1,0:T(8,128)(2,1)S(1)}, bf16[3,4,224,512]{3,2,1,0:T(8,128)(2,1)S(1)}, u32[]{:S(2)}, u32[]{:S(2)}) collective-permute-start(bf16[3,4,224,512]{3,2,1,0:T(8,128)(2,1)S(1)} %shard_map.71), channel_id=1, source_target_pairs={{0,4},{4,0},{8,12},{12,8},{16,20},{20,16},{24,28},{28,24},{1,5},{5... | collective-permute-start | bytes 8257544 | tf_op jit(solution)/shard_map/ppermute | solution.py:305
  211.6 25.1 %collective-permute-start.26 = (bf16[256,1024]{1,0:T(8,128)(2,1)S(1)}, bf16[256,1024]{1,0:T(8,128)(2,1)S(1)}, u32[]{:S(2)}, u32[]{:S(2)}) collective-permute-start(bf16[256,1024]{1,0:T(8,128)(2,1)S(1)} %shard_map.70.hid_ref), channel_id=1, source_target_pairs={{0,2},{1,3},{2,0},{3,1},{4,6},{5,7},{6,4},{7,5},{8,10},{9,11},{10,... | collective-permute-start | bytes 1572872 | tf_op jit(solution)/shard_map/ppermute | solution.py:308
  213.4 24.9 %collective-permute-start.24 = (bf16[256,1024]{1,0:T(8,128)(2,1)S(1)}, bf16[256,1024]{1,0:T(8,128)(2,1)S(1)}, u32[]{:S(2)}, u32[]{:S(2)}) collective-permute-start(bf16[256,1024]{1,0:T(8,128)(2,1)S(1)} %shard_map.70.hid_ref), channel_id=1, source_target_pairs={{0,1},{1,0},{2,3},{3,2},{4,5},{5,4},{6,7},{7,6},{8,9},{9,8},{10,11... | collective-permute-start | bytes 1572872 | tf_op jit(solution)/shard_map/ppermute | solution.py:308
  215.0 23.3 %copy-start = (bf16[3,4,224,512]{3,2,1,0:T(8,128)(2,1)}, bf16[3,4,224,512]{3,2,1,0:T(8,128)(2,1)S(1)}, u32[]{:S(2)}) copy-start(bf16[3,4,224,512]{3,2,1,0:T(8,128)(2,1)S(1)} %collective-permute-done.22) | copy-start | bytes 8257540
  218.3 52.7 %collective-permute-start.23 = (bf16[256,1792]{1,0:T(8,128)(2,1)}, bf16[256,1792]{1,0:T(8,128)(2,1)}, u32[]{:S(2)}, u32[]{:S(2)}) collective-permute-start(bf16[256,1792]{1,0:T(8,128)(2,1)} %shard_map.72), channel_id=1, source_target_pairs={{0,0},{1,9},{2,18},{3,27},{4,4},{5,13},{6,22},{7,31},{8,8},{9,1},{... | collective-permute-start | bytes 2752520 | tf_op jit(solution)/shard_map/ppermute | solution.py:316
  237.5 13.7 %collective-permute-start.27 = (bf16[128,1024]{1,0:T(8,128)(2,1)}, bf16[128,1024]{1,0:T(8,128)(2,1)}, u32[]{:S(2)}, u32[]{:S(2)}) collective-permute-start(bf16[128,1024]{1,0:T(8,128)(2,1)} %get-tuple-element.117), channel_id=1, source_target_pairs={{0,1},{1,0},{2,3},{3,2},{4,5},{5,4},{6,7},{7,6},{8,9},{9,8},{10,11... | collective-permute-start | bytes 786440 | tf_op jit(solution)/shard_map/ppermute | solution.py:308
  241.6 30.7 %collective-permute-start.25 = (bf16[256,1792]{1,0:T(8,128)(2,1)}, bf16[256,1792]{1,0:T(8,128)(2,1)}, u32[]{:S(2)}, u32[]{:S(2)}) collective-permute-start(bf16[256,1792]{1,0:T(8,128)(2,1)} %shard_map.73), channel_id=1, source_target_pairs={{0,8},{1,1},{2,26},{3,19},{4,12},{5,5},{6,30},{7,23},{8,0},{9,9},{... | collective-permute-start | bytes 2752520 | tf_op jit(solution)/shard_map/ppermute | solution.py:316
  244.9 20.1 %collective-permute-start.33 = (bf16[128,1024]{1,0:T(8,128)(2,1)}, bf16[128,1024]{1,0:T(8,128)(2,1)}, u32[]{:S(2)}, u32[]{:S(2)}) collective-permute-start(bf16[128,1024]{1,0:T(8,128)(2,1)} %get-tuple-element.116), channel_id=1, source_target_pairs={{0,1},{1,0},{2,3},{3,2},{4,5},{5,4},{6,7},{7,6},{8,9},{9,8},{10,11... | collective-permute-start | bytes 786440 | tf_op jit(solution)/shard_map/ppermute | solution.py:308
  251.3 1.8 copy-start.1
  255.4 43.2 %collective-permute-start.28 = (bf16[256,1792]{1,0:T(8,128)(2,1)S(1)}, bf16[256,1792]{1,0:T(8,128)(2,1)S(1)}, u32[]{:S(2)}, u32[]{:S(2)}) collective-permute-start(bf16[256,1792]{1,0:T(8,128)(2,1)S(1)} %shard_map.74), channel_id=1, source_target_pairs={{0,16},{1,25},{2,2},{3,11},{4,20},{5,29},{6,6},{7,15},{8,24},{9,17... | collective-permute-start | bytes 2752520 | tf_op jit(solution)/shard_map/ppermute | solution.py:316
  261.6 37.1 %collective-permute-start.29 = (bf16[128,1792]{1,0:T(8,128)(2,1)S(1)}, bf16[128,1792]{1,0:T(8,128)(2,1)S(1)}, u32[]{:S(2)}, u32[]{:S(2)}) collective-permute-start(bf16[128,1792]{1,0:T(8,128)(2,1)S(1)} %shard_map.75), channel_id=1, source_target_pairs={{0,24},{1,17},{2,10},{3,3},{4,28},{5,21},{6,14},{7,7},{8,16},{9,25... | collective-permute-start | bytes 1376264 | tf_op jit(solution)/shard_map/ppermute | solution.py:316
  267.6 35.8 %collective-permute-start.34 = (bf16[128,1792]{1,0:T(8,128)(2,1)S(1)}, bf16[128,1792]{1,0:T(8,128)(2,1)S(1)}, u32[]{:S(2)}, u32[]{:S(2)}) collective-permute-start(bf16[128,1792]{1,0:T(8,128)(2,1)S(1)} %shard_map.76), channel_id=1, source_target_pairs={{0,24},{1,17},{2,10},{3,3},{4,28},{5,21},{6,14},{7,7},{8,16},{9,25... | collective-permute-start | bytes 1376264 | tf_op jit(solution)/shard_map/ppermute | solution.py:316
  299.0 6.5 %collective-permute-start.30 = (bf16[32,1792]{1,0:T(8,128)(2,1)S(1)}, bf16[32,1792]{1,0:T(8,128)(2,1)S(1)}, u32[]{:S(2)}, u32[]{:S(2)}) collective-permute-start(bf16[32,1792]{1,0:T(8,128)(2,1)S(1)} %get-tuple-element.124), channel_id=1, source_target_pairs={{0,1},{1,0},{2,3},{3,2},{4,5},{5,4},{6,7},{7,6},{8,9},{9,8},{10,11... | collective-permute-start | bytes 344072 | tf_op jit(solution)/shard_map/ppermute | solution.py:308
  299.1 15.6 %collective-permute-start.31 = (bf16[32,1792]{1,0:T(8,128)(2,1)S(1)}, bf16[32,1792]{1,0:T(8,128)(2,1)S(1)}, u32[]{:S(2)}, u32[]{:S(2)}) collective-permute-start(bf16[32,1792]{1,0:T(8,128)(2,1)S(1)} %get-tuple-element.123), channel_id=1, source_target_pairs={{0,2},{1,3},{2,0},{3,1},{4,6},{5,7},{6,4},{7,5},{8,10},{9,11},{10,... | collective-permute-start | bytes 344072 | tf_op jit(solution)/shard_map/ppermute | solution.py:308
  299.2 15.6 %collective-permute-start.32 = (bf16[32,1792]{1,0:T(8,128)(2,1)S(1)}, bf16[32,1792]{1,0:T(8,128)(2,1)S(1)}, u32[]{:S(2)}, u32[]{:S(2)}) collective-permute-start(bf16[32,1792]{1,0:T(8,128)(2,1)S(1)} %get-tuple-element.122), channel_id=1, source_target_pairs={{0,3},{1,2},{2,1},{3,0},{4,7},{5,6},{6,5},{7,4},{8,11},{9,10},{10,... | collective-permute-start | bytes 344072 | tf_op jit(solution)/shard_map/ppermute | solution.py:308
  303.8 11.0 %collective-permute-start.35 = (bf16[32,1792]{1,0:T(8,128)(2,1)S(1)}, bf16[32,1792]{1,0:T(8,128)(2,1)S(1)}, u32[]{:S(2)}, u32[]{:S(2)}) collective-permute-start(bf16[32,1792]{1,0:T(8,128)(2,1)S(1)} %get-tuple-element.120), channel_id=1, source_target_pairs={{0,1},{1,0},{2,3},{3,2},{4,5},{5,4},{6,7},{7,6},{8,9},{9,8},{10,11... | collective-permute-start | bytes 344072 | tf_op jit(solution)/shard_map/ppermute | solution.py:308
  303.8 15.8 %collective-permute-start.36 = (bf16[32,1792]{1,0:T(8,128)(2,1)S(1)}, bf16[32,1792]{1,0:T(8,128)(2,1)S(1)}, u32[]{:S(2)}, u32[]{:S(2)}) collective-permute-start(bf16[32,1792]{1,0:T(8,128)(2,1)S(1)} %get-tuple-element.119), channel_id=1, source_target_pairs={{0,2},{1,3},{2,0},{3,1},{4,6},{5,7},{6,4},{7,5},{8,10},{9,11},{10,... | collective-permute-start | bytes 344072 | tf_op jit(solution)/shard_map/ppermute | solution.py:308
  305.5 14.2 %collective-permute-start.37 = (bf16[32,1792]{1,0:T(8,128)(2,1)S(1)}, bf16[32,1792]{1,0:T(8,128)(2,1)S(1)}, u32[]{:S(2)}, u32[]{:S(2)}) collective-permute-start(bf16[32,1792]{1,0:T(8,128)(2,1)S(1)} %get-tuple-element.118), channel_id=1, source_target_pairs={{0,3},{1,2},{2,1},{3,0},{4,7},{5,6},{6,5},{7,4},{8,11},{9,10},{10,... | collective-permute-start | bytes 344072 | tf_op jit(solution)/shard_map/ppermute | solution.py:308
  (16 other events, 17.8 us)
Sparse Core Ops, SparseCore 0:
  160.6 42.8 reduce-scatter.1

commit v8 on v5

--- a/solution.py
+++ b/solution.py
@@ -151,16 +151,15 @@
     )(place, own, *pieces)
 
 
-def pick_kernel(chips, place_ref, *refs):
-    toks, refs = refs[:chips], refs[chips:]
-    weights, (keep_ref, send_ref, routing_ref, left) = refs[:CORES], refs[CORES:]
+def pick_kernel(tokens, *refs):
+    toks, refs = refs[:tokens], refs[tokens:]
+    weights, (out_ref, routing_ref, left) = refs[:CORES], refs[CORES:]
     experts, depth, width = weights[0].shape
     rows = toks[0].shape[0]
     for step, tok in enumerate(toks):
-        block = jnp.bitwise_xor(step, place_ref[2])
-        left[rows_of(block, rows), :] = tok[:, : CORES * depth]
-        routing_ref[block] = tok[:, CORES * depth :]
-    slots = keep_ref.shape[2] // width
+        left[step * rows : (step + 1) * rows, :] = tok[:, : CORES * depth]
+        routing_ref[step * rows : (step + 1) * rows, :] = tok[:, CORES * depth :]
+    slots = out_ref.shape[1] // width
     tile = min(TILE, width)
     for start in range(0, width, tile):
         sums = []
@@ -174,100 +173,106 @@
                 )
                 total = term if total is None else total + term
             sums.append(total)
-        for step in range(chips):
-            out_ref = (keep_ref, send_ref)[step % 2]
-            ids = routing_ref[step].astype(jnp.float32)
-            for slot in range(slots):
-                chosen = ids[:, slot : slot + 1]
-                picked = sums[0][step * rows : (step + 1) * rows]
-                for which in range(1, experts):
-                    other = sums[which][step * rows : (step + 1) * rows]
-                    picked = jnp.where(chosen == which, other, picked)
-                first = slot * width + start
-                out_ref[step // 2, :, first : first + tile] = picked.astype(out_ref.dtype)
-
-
-def picked_sums(place, toks, weights, slots):
-    chips, rows = len(toks), toks[0].shape[0]
+        ids = routing_ref[...].astype(jnp.float32)
+        for slot in range(slots):
+            chosen = ids[:, slot : slot + 1]
+            picked = sums[0]
+            for which in range(1, experts):
+                picked = jnp.where(chosen == which, sums[which], picked)
+            first = slot * width + start
+            out_ref[:, first : first + tile] = picked.astype(out_ref.dtype)
+
+
+def picked_sums(toks, weights, slots):
     experts, depth, width = weights[0].shape
     wide = CORES * depth
-    count = chips * rows
-    return pl.pallas_call(
-        functools.partial(pick_kernel, chips),
-        in_specs=[SMEM_SPEC] + [VMEM_SPEC] * (chips + CORES),
-        out_specs=[VMEM_SPEC] * 3,
-        out_shape=[bf16(chips // 2, rows, slots * width)] * 2 + [bf16(chips, rows, LANES)],
+    count = len(toks) * toks[0].shape[0]
+    return pl.pallas_call(
+        functools.partial(pick_kernel, len(toks)),
+        in_specs=[VMEM_SPEC] * (len(toks) + CORES),
+        out_specs=[VMEM_SPEC] * 2,
+        out_shape=[bf16(count, slots * width), bf16(count, LANES)],
         scratch_shapes=[pltpu.VMEM((count, wide), jnp.bfloat16)],
         cost_estimate=cost(
             2 * count * wide * width * experts,
             count * wide + experts * wide * width + count * slots * width,
         ),
         compiler_params=PARAMS,
-    )(place, *toks, *weights)
-
-
-def hidden_kernel(terms, slots, routing_ref, *refs):
-    gates, ups, out_ref = refs[:terms], refs[terms : 2 * terms], refs[2 * terms]
-    scores = routing_ref[0].astype(jnp.float32)[:, slots : 2 * slots]
-    combine = scores / jnp.sum(scores, axis=1, keepdims=True)
-    width = out_ref.shape[1] // slots
-    for slot in range(slots):
-        columns = slice(slot * width, (slot + 1) * width)
-        gate_sum = sum(ref[0, :, columns].astype(jnp.float32) for ref in gates)
-        up_sum = sum(ref[0, :, columns].astype(jnp.float32) for ref in ups)
-        value = gate_sum / (1.0 + jnp.exp(-gate_sum)) * up_sum * combine[:, slot : slot + 1]
-        out_ref[:, columns] = value.astype(out_ref.dtype)
-
-
-def hidden_rows(routing, gates, ups, slots):
-    return pl.pallas_call(
-        functools.partial(hidden_kernel, len(gates), slots),
-        in_specs=[VMEM_SPEC] * (1 + 2 * len(gates)),
-        out_specs=VMEM_SPEC,
-        out_shape=bf16(*gates[0].shape[1:]),
-        compiler_params=PARAMS,
-    )(routing, *gates, *ups)
-
-
-def down_kernel(step, slots, routing_ref, hid_ref, *refs):
-    weights, (out_ref,) = refs[:CORES], refs[CORES:]
+    )(*toks, *weights)
+
+
+def hidden_kernel(slots, place_ref, routing_ref, gate_ref, up_ref, *outs):
+    rows, wide = outs[0].shape
+    width = wide // slots
+    for half, out_ref in enumerate(outs):
+        target = slice(half * rows, (half + 1) * rows)
+        scores = routing_ref[rows_of(place_ref[2] * HALVES + half, rows), :]
+        scores = scores.astype(jnp.float32)[:, slots : 2 * slots]
+        combine = scores / jnp.sum(scores, axis=1, keepdims=True)
+        for slot in range(slots):
+            columns = slice(slot * width, (slot + 1) * width)
+            gate_sum = gate_ref[target, columns].astype(jnp.float32)
+            up_sum = up_ref[target, columns].astype(jnp.float32)
+            value = gate_sum / (1.0 + jnp.exp(-gate_sum)) * up_sum * combine[:, slot : slot + 1]
+            out_ref[:, columns] = value.astype(out_ref.dtype)
+
+
+def hidden_rows(place, routing, gate_sum, up_sum, slots):
+    rows, wide = gate_sum.shape
+    return pl.pallas_call(
+        functools.partial(hidden_kernel, slots),
+        in_specs=[SMEM_SPEC] + [VMEM_SPEC] * 3,
+        out_specs=[VMEM_SPEC] * HALVES,
+        out_shape=[bf16(rows // HALVES, wide)] * HALVES,
+        compiler_params=PARAMS,
+    )(place, routing, gate_sum, up_sum)
+
+
+def down_kernel(half, slots, levels, place_ref, routing_ref, *refs):
+    hids, refs = refs[:levels], refs[levels:]
+    weights, (*outs, left) = refs[:CORES], refs[CORES:]
     experts, depth, width = weights[0].shape
-    ids = routing_ref[step].astype(jnp.float32)
-    lefts = []
-    for which in range(experts):
-        mine = jnp.zeros((hid_ref.shape[0], width), jnp.float32)
-        for slot in range(slots):
-            part = hid_ref[:, slot * width : (slot + 1) * width].astype(jnp.float32)
-            mine = jnp.where(ids[:, slot : slot + 1] == which, part, mine)
-        lefts.append(mine.astype(hid_ref.dtype))
+    rows = hids[0].shape[0]
+    for step, hid_ref in enumerate(hids):
+        block = jnp.bitwise_xor(place_ref[2], step)
+        ids = routing_ref[rows_of(block * HALVES + half, rows), :].astype(jnp.float32)
+        for which in range(experts):
+            mine = jnp.zeros((rows, width), jnp.float32)
+            for slot in range(slots):
+                value = hid_ref[:, slot * width : (slot + 1) * width].astype(jnp.float32)
+                mine = jnp.where(ids[:, slot : slot + 1] == which, value, mine)
+            left[which, rows_of(block, rows), :] = mine.astype(left.dtype)
     for side, weight in enumerate(weights):
         total = None
         for which in range(experts):
             term = lax.dot_general(
-                lefts[which],
+                left[which],
                 weight[which],
                 (((1,), (1,)), ((), ())),
                 preferred_element_type=jnp.float32,
             )
             total = term if total is None else total + term
-        out_ref[:, side * depth : (side + 1) * depth] = total.astype(out_ref.dtype)
-
-
-def down_sums(routing, hidden, weights, step, slots):
-    rows = hidden.shape[0]
+        for step, out_ref in enumerate(outs):
+            part = total[step * rows : (step + 1) * rows]
+            out_ref[:, side * depth : (side + 1) * depth] = part.astype(out_ref.dtype)
+
+
+def down_sums(place, routing, hids, weights, half, slots):
+    rows, levels = hids[0].shape[0], len(hids)
     experts, depth, width = weights[0].shape
-    wide = CORES * depth
-    return pl.pallas_call(
-        functools.partial(down_kernel, step, slots),
-        in_specs=[VMEM_SPEC] * (2 + CORES),
-        out_specs=VMEM_SPEC,
-        out_shape=bf16(rows, wide),
+    wide, count = CORES * depth, levels * rows
+    return pl.pallas_call(
+        functools.partial(down_kernel, half, slots, levels),
+        in_specs=[SMEM_SPEC] + [VMEM_SPEC] * (1 + levels + CORES),
+        out_specs=[VMEM_SPEC] * levels,
+        out_shape=[bf16(rows, wide)] * levels,
+        scratch_shapes=[pltpu.VMEM((experts, count, width), jnp.bfloat16)],
         cost_estimate=cost(
-            2 * rows * wide * width * experts,
-            rows * slots * width + experts * wide * width + rows * wide,
+            2 * count * wide * width * experts,
+            count * slots * width + experts * wide * width + count * wide,
         ),
         compiler_params=PARAMS,
-    )(routing, hidden, *weights)
+    )(place, routing, *hids, *weights)
 
 
 def after(values, others):
@@ -295,30 +300,13 @@
     def to_level(value, step):
         return lax.ppermute(value, "tensor", [(s, s ^ step) for s in range(n_tensor)])
 
-    def to_owner(value, step):
-        pairs = [
-            (s * n_tensor + t, (s ^ ((t ^ step) * CORES)) * n_tensor + t)
-            for s in range(n_expert)
-            for t in range(n_tensor)
-        ]
-        return lax.ppermute(value, ("expert", "tensor"), pairs)
-
-    def copies(value, send, bits):
+    def copies(value, send, bits, behind=()):
         held = {0: value}
         for bit in bits:
             for step in sorted(held):
-                held[step + bit] = send(held[step], bit)
+                held[step + bit] = send(after(held[step], behind), bit)
+            behind = ()
         return [held[step] for step in range(len(held))]
-
-    def level_sums(keep, send):
-        terms, bit = [keep], 1
-        while True:
-            terms.append(to_level(send, bit))
-            bit *= 2
-            if bit == n_tensor:
-                return terms
-            send = sum(term[1::2].astype(jnp.float32) for term in terms).astype(jnp.bfloat16)
-            terms = [term[::2] for term in terms]
 
     def blocks_of(weight):
         return [
@@ -348,43 +336,36 @@
     for half in range(HALVES):
         turn = (half + 1) % len(bits)
         toks.append(copies(groups[half], to_chip, bits[turn:] + bits[:turn]))
+
+    def reduced(part):
+        return lax.psum_scatter(part, "tensor", scatter_dimension=0, tiled=True)
+
+    left = [toks[half][step] for step in range(chips) for half in range(HALVES)]
     up_same = chip_exchange(after(blocks_of(up_weight), toks))
-
-    def products(weights, parts):
-        routings, sends = [], []
-        for half in range(HALVES):
-            left = after(toks[half], parts)
-            *parts, routing = picked_sums(place, left, weights, slots)
-            routings.append(routing)
-            sends.append(parts)
-        sums = [level_sums(*parts) for parts in sends]
-        return routings, sums
-
-    routings, gate_sums = products(gate_pair, place)
-    up_joined = join_blocks(place, up_weight, after(up_same, [terms[:-1] for terms in gate_sums]))
+    part, routing = picked_sums(left, gate_pair, slots)
+    gate_sum = reduced(part)
+    up_joined = join_blocks(place, up_weight, after(up_same, gate_sum))
     up_pair = core_exchange(up_joined)
     down_same = chip_exchange(after(blocks_of(down_weight), up_joined))
-    _, up_sums = products(up_pair, gate_sums)
-    hiddens = [
-        hidden_rows(routings[half], gate_sums[half], up_sums[half], slots)
-        for half in range(HALVES)
-    ]
-    down_joined = join_blocks(place, down_weight, after(down_same, hiddens[0]))
+    part, _ = picked_sums(left, up_pair, slots)
+    up_sum = reduced(part)
+    hidden = hidden_rows(place, routing, gate_sum, up_sum, slots)
+    down_joined = join_blocks(place, down_weight, after(down_same, hidden))
     down_pair = core_exchange(down_joined)
 
-    backs = []
+    backs, far = [], ()
     bits = [1 << bit for bit in range(n_tensor.bit_length() - 1)]
     for half in range(HALVES):
-        routing = routings[half]
-        blocks = copies(hiddens[half], to_level, bits[::-1])
-        total = 0.0
-        for step in range(n_tensor):
-            part = down_sums(routing, blocks[step], down_pair, step, slots)
-            total = total + to_owner(part, step).astype(jnp.float32)
+        hids = copies(hidden[half], to_level, bits[::-1], far)
+        far = [hids[bit] for bit in bits]
+        parts = down_sums(place, routing, hids, down_pair, half, slots)
+        total = parts[0].astype(jnp.float32)
+        for step in range(1, chips):
+            total = total + to_chip(parts[step], step).astype(jnp.float32)
         total = total.astype(jnp.bfloat16).reshape(n_tensor, rows // HALVES, -1)
-        for step in range(n_tensor):
-            piece = lax.dynamic_index_in_dim(total, level ^ step, 0, keepdims=False)
-            backs.append(to_level(piece, step) if step else piece)
+        for other in range(n_tensor):
+            piece = lax.dynamic_index_in_dim(total, level ^ other, 0, keepdims=False)
+            backs.append(to_level(piece, other) if other else piece)
     return finish(place, backs, n_tensor, depth)
 
 

time: 306 us -> 301 us (0.984)
  starting transfers between devices: 86.3 us -> 50 us
  waiting for transfers between devices: 161 us -> 176 us
  between operations: 0.47 us -> 13.9 us
  local copies, waits for them, and re-layouts: 10.2 us -> 23.4 us
  Pallas kernels: 44.4 us -> 34.8 us
    ppermute x23 -> x15, waiting for transfers between devices: 119 us -> 45.5 us  [to_level(): lax.ppermute(value, 'tensor', [(s, s ^ step) for s in range(n_tensor)])]
    reduce_scatter x0 -> x2, waiting for transfers between devices: none -> 48.5 us  [reduced(): return lax.psum_scatter(part, 'tensor', scatter_dimension=0, tiled=True)]
    ppermute x15 -> x21, waiting for transfers between devices: 37.6 us -> 77.4 us  [to_chip(): return lax.ppermute(value, 'expert', pairs)]
    ppermute x8 -> x0, starting transfers between devices: 24.3 us -> none  [to_owner(): return lax.ppermute(value, ('expert', 'tensor'), pairs)]
    ppermute x23 -> x15, starting transfers between devices: 44.1 us -> 25.1 us  [to_level(): lax.ppermute(value, 'tensor', [(s, s ^ step) for s in range(n_tensor)])]
    unnamed x26 -> x84, local copies, waits for them, and re-layouts: 6.29 us -> 18.5 us
    pallas_call x14 -> x5, Pallas kernels: 35.5 us -> 24.9 us  [the longest x2 13.4 us: picked_sums(): pl.pallas_call(functools.partial(pick_kernel, len(toks)), in_specs=[VMEM_...]
    ppermute x15 -> x21, starting transfers between devices: 17.7 us -> 24.5 us  [to_chip(): return lax.ppermute(value, 'expert', pairs)]
  transfers between devices with their start and end apart: 49 -> 41, of which waited for: 19 -> 23; matrix products, arithmetic and copies ran while one was open for 1% -> 1% of each run, Pallas kernels for 11% -> 5%
where the time goes in v8:
time: 301 us; the launch traced here: 300 us
  waiting for transfers between devices  176 us (58%)
  starting transfers between devices  50 us (17%)
  Pallas kernels  34.8 us (12%)
  local copies, waits for them, and re-layouts  23.4 us (8%)
  between operations  13.9 us (5%)
    ppermute x21, waiting for transfers between devices, to_chip(): return lax.ppermute(value, 'expert', pairs)  77.4 us
    reduce_scatter x2, waiting for transfers between devices, reduced(): return lax.psum_scatter(part, 'tensor', scatter_dimension=0, tiled=True)  48.5 us
    ppermute x15, waiting for transfers between devices, to_level(): lax.ppermute(value, 'tensor', [(s, s ^ step) for s in range(n_tensor)])  45.5 us
    ppermute x15, starting transfers between devices, to_level(): lax.ppermute(value, 'tensor', [(s, s ^ step) for s in range(n_tensor)])  25.1 us
    ppermute x21, starting transfers between devices, to_chip(): return lax.ppermute(value, 'expert', pairs)  24.5 us
    unnamed x84, local copies, waits for them, and re-layouts  18.5 us
    pallas_call x2, Pallas kernels, picked_sums(): pl.pallas_call(functools.partial(pick_kernel, len(toks)), in_specs=[VMEM_...  13.4 us
    pallas_call x2, Pallas kernels, down_sums(): pl.pallas_call(functools.partial(down_kernel, half, slots, levels), in_sp...  9.6 us
  transfers between devices with their start and end apart: 41, of which 23 were waited for; matrix products, arithmetic and copies ran while one was open for 1% of the time, Pallas kernels for 5%

profile of v8, /device:TPU:0, one launch (start us, length us, event | category | flops | bytes accessed | tf_op | source)
XLA Modules:
  0.0 300.3 jit_solution(5869104841095365866)
XLA Ops:
  6.5 3.0 %constant_dynamic-slice_fusion.6 = (bf16[3,224,512]{2,1,0:T(8,128)(2,1)}, bf16[3,224,512]{2,1,0:T(8,128)(2,1)}, bf16[3,224,512]{2,1,0:T(8,128)(2,1)}) fusion(bf16[3,224,2048]{2,1,0:T(8,128)(2,1)} %own_ref.3, s32[]{:T(128)S(6)} %select_n.47, s32[]{:T(128)S(6)} %select_n.46, s32[]{:T(128)S(6)} %select_n.45), kind=kLoop, calls=%fused_computation.16 | loop fusion | bytes 4128780 | tf_op jit(solution)/shard_map/dynamic_slice | solution.py:313
  9.6 2.9 collective-permute-start.3
  12.5 1.5 collective-permute-start.4
  15.3 1.7 shard_map.64
  17.7 2.1 collective-permute-start
  19.8 2.6 collective-permute-start.1
  22.3 6.8 %collective-permute-done.refs_1_ = bf16[64,1792]{1,0:T(8,128)(2,1)S(1)} collective-permute-done((bf16[64,1792]{1,0:T(8,128)(2,1)S(1)}, bf16[64,1792]{1,0:T(8,128)(2,1)S(1)}, u32[]{:S(2)}, u32[]{:S(2)}) %collective-permute-start) | collective-permute-done | bytes 229408 | tf_op jit(solution)/shard_map/ppermute | solution.py:301
  29.8 2.6 collective-permute-start.2
  32.7 5.4 %collective-permute-done.2.refs_3_ = bf16[64,1792]{1,0:T(8,128)(2,1)} collective-permute-done((bf16[64,1792]{1,0:T(8,128)(2,1)}, bf16[64,1792]{1,0:T(8,128)(2,1)}, u32[]{:S(2)}, u32[]{:S(2)}) %collective-permute-start.2) | collective-permute-done | bytes 229408 | tf_op jit(solution)/shard_map/ppermute | solution.py:301
  41.1 3.4 %collective-permute-done.4.refs_1_ = bf16[3,224,512]{2,1,0:T(8,128)(2,1)} collective-permute-done((bf16[3,224,512]{2,1,0:T(8,128)(2,1)}, bf16[3,224,512]{2,1,0:T(8,128)(2,1)}, u32[]{:S(2)}, u32[]{:S(2)}) %collective-permute-start.4) | collective-permute-done | bytes 688160 | tf_op jit(solution)/shard_map/ppermute | solution.py:295
  44.5 2.1 shard_map.66
  46.6 1.6 collective-permute-start.8
  48.8 1.5 collective-permute-start.6
  50.8 10.0 %collective-permute-done.8.refs_4_ = bf16[128,1920]{1,0:T(8,128)(2,1)S(1)} collective-permute-done((bf16[128,1920]{1,0:T(8,128)(2,1)S(1)}, bf16[128,1920]{1,0:T(8,128)(2,1)S(1)}, u32[]{:S(2)}, u32[]{:S(2)}) %collective-permute-start.8) | collective-permute-done | bytes 491552 | tf_op jit(solution)/shard_map/ppermute | solution.py:295
  62.8 10.0 %collective-permute-done.6.refs_2_ = bf16[128,1920]{1,0:T(8,128)(2,1)S(1)} collective-permute-done((bf16[128,1920]{1,0:T(8,128)(2,1)S(1)}, bf16[128,1920]{1,0:T(8,128)(2,1)S(1)}, u32[]{:S(2)}, u32[]{:S(2)}) %collective-permute-start.6) | collective-permute-done | bytes 491552 | tf_op jit(solution)/shard_map/ppermute | solution.py:295
  72.8 9.8 %collective-permute-done.10.refs_6_ = bf16[128,1920]{1,0:T(8,128)(2,1)S(1)} collective-permute-done((bf16[128,1920]{1,0:T(8,128)(2,1)S(1)}, bf16[128,1920]{1,0:T(8,128)(2,1)S(1)}, u32[]{:S(2)}, u32[]{:S(2)}) %collective-permute-start.10) | collective-permute-done | bytes 491552 | tf_op jit(solution)/shard_map/ppermute | solution.py:295
  82.6 6.7 %shard_map.67 = (bf16[1024,1024]{1,0:T(8,128)(2,1)S(1)}, bf16[1024,128]{1,0:T(8,128)(2,1)S(1)}) custom-call(bf16[128,1920]{1,0:T(8,128)(2,1)S(1)} %get-tuple-element.51.refs_0_, bf16[128,1920]{1,0:T(8,128)(2,1)S(1)} %get-tuple-element.52.refs_1_, bf16[128,1920]{1,0:T(8,128)(2,1)S(1)} %collective-permute-done.6.refs_2_, ...), custom_call_target="tpu_custom_call" | custom-call | flops 5637144576 | bytes 11272192 | tf_op jit(solution)/shard_map/pallas_call | solution.py:190
  93.8 1.8 collective-permute-start.15
  95.6 14.9 %collective-permute-done.13.refs_0_ = bf16[3,224,512]{2,1,0:T(8,128)(2,1)S(1)} collective-permute-done((bf16[3,224,512]{2,1,0:T(8,128)(2,1)S(1)}, bf16[3,224,512]{2,1,0:T(8,128)(2,1)S(1)}, u32[]{:S(2)}, u32[]{:S(2)}) %collective-permute-start.13) | collective-permute-done | bytes 688160 | tf_op jit(solution)/shard_map/ppermute | solution.py:295
  110.4 13.3 %collective-permute-done.14.refs_1_ = bf16[3,224,512]{2,1,0:T(8,128)(2,1)S(1)} collective-permute-done((bf16[3,224,512]{2,1,0:T(8,128)(2,1)S(1)}, bf16[3,224,512]{2,1,0:T(8,128)(2,1)S(1)}, u32[]{:S(2)}, u32[]{:S(2)}) %collective-permute-start.14) | collective-permute-done | bytes 688160 | tf_op jit(solution)/shard_map/ppermute | solution.py:295
  125.5 10.0 %reduce-scatter.3.cloned.1.call-done.gate_ref = bf16[256,1024]{1,0:T(8,128)(2,1)} async-done(((bf16[1024,1024]{1,0:T(8,128)(2,1)}), bf16[256,1024]{1,0:T(8,128)(2,1)}) %reduce-scatter.3.cloned.1.call-update) | async-done | bytes 524304 | tf_op jit(solution)/shard_map/reduce_scatter | solution.py:341
  138.8 5.1 %collective-permute-done.16 = bf16[3,4,224,512]{3,2,1,0:T(8,128)(2,1)S(1)} collective-permute-done((bf16[3,4,224,512]{3,2,1,0:T(8,128)(2,1)S(1)}, bf16[3,4,224,512]{3,2,1,0:T(8,128)(2,1)S(1)}, u32[]{:S(2)}, u32[]{:S(2)}) %collective-permute-start.16) | collective-permute-done | bytes 2752544 | tf_op jit(solution)/shard_map/ppermute | solution.py:298
  144.0 6.7 %shard_map.69 = (bf16[1024,1024]{1,0:T(8,128)(2,1)S(1)}, bf16[1024,128]{1,0:T(8,128)(2,1)}) custom-call(bf16[128,1920]{1,0:T(8,128)(2,1)S(1)} %copy-done.25, bf16[128,1920]{1,0:T(8,128)(2,1)S(1)} %copy-done.27, bf16[128,1920]{1,0:T(8,128)(2,1)S(1)} %copy-done.33, bf16[128,1920]{1,0:T(8,128)(2,1)S(1)} %copy-done.31, bf16[128,1920]{1,0:T(8,128)(2,1)S(1)} %copy-done.29, ...), custom_call_target="tpu_custom_call" | custom-call | flops 5637144576 | bytes 11272192 | tf_op jit(solution)/shard_map/pallas_call | solution.py:190
  153.4 1.5 collective-permute-start.20
  154.9 1.5 collective-permute-start.21
  156.9 38.4 %reduce-scatter.5.cloned.1.call-done.up_ref = bf16[256,1024]{1,0:T(8,128)(2,1)} async-done(((bf16[1024,1024]{1,0:T(8,128)(2,1)}), bf16[256,1024]{1,0:T(8,128)(2,1)}) %reduce-scatter.5.cloned.1.call-update) | async-done | bytes 524304 | tf_op jit(solution)/shard_map/reduce_scatter | solution.py:341
  198.4 1.8 shard_map.70
  200.3 2.3 shard_map.71
  202.7 2.0 collective-permute-start.18
  204.8 12.2 %collective-permute-done.17.refs_1_ = bf16[128,1024]{1,0:T(8,128)(2,1)S(1)} collective-permute-done((bf16[128,1024]{1,0:T(8,128)(2,1)S(1)}, bf16[128,1024]{1,0:T(8,128)(2,1)S(1)}, u32[]{:S(2)}, u32[]{:S(2)}) %collective-permute-start.17) | collective-permute-done | bytes 262176 | tf_op jit(solution)/shard_map/ppermute | solution.py:301
  218.3 3.2 %collective-permute-start.19 = (bf16[128,1024]{1,0:T(8,128)(2,1)S(1)}, bf16[128,1024]{1,0:T(8,128)(2,1)S(1)}, u32[]{:S(2)}, u32[]{:S(2)}) collective-permute-start(bf16[128,1024]{1,0:T(8,128)(2,1)S(1)} %collective-permute-done.18.refs_2_), channel_id=1, source_target_pairs={{0,1},{1,0},{2,3},{3,2},{4,5},{5,4},{6,7},{7,6},{8,9},{9,8},{10,11... | collective-permute-start | bytes 786440 | tf_op jit(solution)/shard_map/ppermute | solution.py:301
  221.5 10.2 %collective-permute-done.31.refs_2_ = bf16[128,1024]{1,0:T(8,128)(2,1)S(1)} collective-permute-done((bf16[128,1024]{1,0:T(8,128)(2,1)}, bf16[128,1024]{1,0:T(8,128)(2,1)S(1)}, u32[]{:S(2)}, u32[]{:S(2)}) %collective-permute-start.31) | collective-permute-done | bytes 262176 | tf_op jit(solution)/shard_map/ppermute | solution.py:301
  233.0 4.6 %shard_map.72 = (bf16[128,1792]{1,0:T(8,128)(2,1)S(1)}, bf16[128,1792]{1,0:T(8,128)(2,1)S(1)}, bf16[128,1792]{1,0:T(8,128)(2,1)S(1)}, bf16[128,1792]{1,0:T(8,128)(2,1)S(1)}) custom-call(s32[3]{0:T(128)S(1)} %pad_add_fusion.place_ref, bf16[1024,128]{1,0:T(8,128)(2,1)S(1)} %copy-done.16, bf16[128,1024]{1,0:T(8,128)(2,1)S(1)} %get-tuple-element.62.refs_0_, ...), custom_call_target="tpu_custom_call" | custom-call | flops 2818572288 | bytes 8388608 | tf_op jit(solution)/shard_map/pallas_call | solution.py:264
  237.6 2.5 collective-permute-start.26
  241.2 1.6 collective-permute-done.32.refs_3_
  242.8 1.8 copy-done.4
  244.6 1.8 copy-done.23
  246.4 5.0 %shard_map.73 = (bf16[128,1792]{1,0:T(8,128)(2,1)S(1)}, bf16[128,1792]{1,0:T(8,128)(2,1)S(1)}, bf16[128,1792]{1,0:T(8,128)(2,1)S(1)}, bf16[128,1792]{1,0:T(8,128)(2,1)S(1)}) custom-call(s32[3]{0:T(128)S(1)} %pad_add_fusion.place_ref, bf16[1024,128]{1,0:T(8,128)(2,1)S(1)} %copy-done.17, bf16[128,1024]{1,0:T(8,128)(2,1)} %get-tuple-element.74.refs_0_, ...), custom_call_target="tpu_custom_call" | custom-call | flops 2818572288 | bytes 8388608 | tf_op jit(solution)/shard_map/pallas_call | solution.py:264
  251.4 2.5 collective-permute-start.35
  255.0 7.1 %collective-permute-done.25 = bf16[128,1792]{1,0:T(8,128)(2,1)} collective-permute-done((bf16[128,1792]{1,0:T(8,128)(2,1)S(1)}, bf16[128,1792]{1,0:T(8,128)(2,1)}, u32[]{:S(2)}, u32[]{:S(2)}) %collective-permute-start.25) | collective-permute-done | bytes 458784 | tf_op jit(solution)/shard_map/ppermute | solution.py:295
  264.3 2.7 collective-permute-start.28
  267.0 4.7 %collective-permute-done.35 = bf16[128,1792]{1,0:T(8,128)(2,1)S(1)} collective-permute-done((bf16[128,1792]{1,0:T(8,128)(2,1)S(1)}, bf16[128,1792]{1,0:T(8,128)(2,1)S(1)}, u32[]{:S(2)}, u32[]{:S(2)}) %collective-permute-start.35) | collective-permute-done | bytes 458784 | tf_op jit(solution)/shard_map/ppermute | solution.py:295
  271.8 2.9 collective-permute-start.29
  274.7 3.8 %collective-permute-done.34 = bf16[128,1792]{1,0:T(8,128)(2,1)S(1)} collective-permute-done((bf16[128,1792]{1,0:T(8,128)(2,1)S(1)}, bf16[128,1792]{1,0:T(8,128)(2,1)S(1)}, u32[]{:S(2)}, u32[]{:S(2)}) %collective-permute-start.34) | collective-permute-done | bytes 458784 | tf_op jit(solution)/shard_map/ppermute | solution.py:295
  280.1 2.4 collective-permute-start.37
  283.7 2.7 collective-permute-done.36.refs_5_
  286.5 5.2 %collective-permute-done.38.refs_7_ = bf16[32,1792]{1,0:T(8,128)(2,1)S(1)} collective-permute-done((bf16[32,1792]{1,0:T(8,128)(2,1)S(1)}, bf16[32,1792]{1,0:T(8,128)(2,1)S(1)}, u32[]{:S(2)}, u32[]{:S(2)}) %collective-permute-start.38) | collective-permute-done | bytes 114720 | tf_op jit(solution)/shard_map/ppermute | solution.py:301
  291.6 1.9 shard_map.74
  (144 shorter events, 34.9 us)
Async XLA Ops:
  6.5 129.0 %reduce-scatter.3.cloned.1.call-start = ((), (), s32[]{:S(2)}) async-start(), calls=%async_computation.2 | async-start | bytes 2621440 | tf_op jit(solution)/shard_map/reduce_scatter | solution.py:341
  6.5 37.9 %copy-start = (bf16[3,224,2048]{2,1,0:T(8,128)(2,1)S(1)}, bf16[3,224,2048]{2,1,0:T(8,128)(2,1)}, u32[]{:S(2)}) copy-start(bf16[3,224,2048]{2,1,0:T(8,128)(2,1)} %own_ref.3) | copy-start | bytes 8257540
  9.6 31.5 %collective-permute-start.3 = (bf16[3,224,512]{2,1,0:T(8,128)(2,1)}, bf16[3,224,512]{2,1,0:T(8,128)(2,1)S(1)}, u32[]{:S(2)}, u32[]{:S(2)}) collective-permute-start(bf16[3,224,512]{2,1,0:T(8,128)(2,1)} %get-tuple-element.87), channel_id=1, source_target_pairs={{0,8},{4,12},{8,0},{12,4},{16,24},{20,28},{24,16},{28,20},{1,9},{5... | collective-permute-start | bytes 2064392 | tf_op jit(solution)/shard_map/ppermute | solution.py:295
  12.5 32.0 %collective-permute-start.4 = (bf16[3,224,512]{2,1,0:T(8,128)(2,1)}, bf16[3,224,512]{2,1,0:T(8,128)(2,1)}, u32[]{:S(2)}, u32[]{:S(2)}) collective-permute-start(bf16[3,224,512]{2,1,0:T(8,128)(2,1)} %get-tuple-element.86), channel_id=1, source_target_pairs={{0,16},{4,20},{8,24},{12,28},{16,0},{20,4},{24,8},{28,12},{1,17},{... | collective-permute-start | bytes 2064392 | tf_op jit(solution)/shard_map/ppermute | solution.py:295
  14.0 30.4 %collective-permute-start.5 = (bf16[3,224,512]{2,1,0:T(8,128)(2,1)}, bf16[3,224,512]{2,1,0:T(8,128)(2,1)}, u32[]{:S(2)}, u32[]{:S(2)}) collective-permute-start(bf16[3,224,512]{2,1,0:T(8,128)(2,1)} %get-tuple-element.85), channel_id=1, source_target_pairs={{0,24},{4,28},{8,16},{12,20},{16,8},{20,12},{24,0},{28,4},{1,25},{... | collective-permute-start | bytes 2064392 | tf_op jit(solution)/shard_map/ppermute | solution.py:295
  17.7 11.4 %collective-permute-start = (bf16[64,1792]{1,0:T(8,128)(2,1)S(1)}, bf16[64,1792]{1,0:T(8,128)(2,1)S(1)}, u32[]{:S(2)}, u32[]{:S(2)}) collective-permute-start(bf16[64,1792]{1,0:T(8,128)(2,1)S(1)} %get-tuple-element.43), channel_id=1, source_target_pairs={{0,1},{1,0},{2,3},{3,2},{4,5},{5,4},{6,7},{7,6},{8,9},{9,8},{10,11... | collective-permute-start | bytes 688136 | tf_op jit(solution)/shard_map/ppermute | solution.py:301
  19.8 12.9 %collective-permute-start.1 = (bf16[64,1792]{1,0:T(8,128)(2,1)}, bf16[64,1792]{1,0:T(8,128)(2,1)}, u32[]{:S(2)}, u32[]{:S(2)}) collective-permute-start(bf16[64,1792]{1,0:T(8,128)(2,1)} %get-tuple-element.44), channel_id=1, source_target_pairs={{0,2},{1,3},{2,0},{3,1},{4,6},{5,7},{6,4},{7,5},{8,10},{9,11},{10,... | collective-permute-start | bytes 688136 | tf_op jit(solution)/shard_map/ppermute | solution.py:301
  29.8 8.2 %collective-permute-start.2 = (bf16[64,1792]{1,0:T(8,128)(2,1)}, bf16[64,1792]{1,0:T(8,128)(2,1)}, u32[]{:S(2)}, u32[]{:S(2)}) collective-permute-start(bf16[64,1792]{1,0:T(8,128)(2,1)} %get-tuple-element.45), channel_id=1, source_target_pairs={{0,3},{1,2},{2,1},{3,0},{4,7},{5,6},{6,5},{7,4},{8,11},{9,10},{10,... | collective-permute-start | bytes 688136 | tf_op jit(solution)/shard_map/ppermute | solution.py:301
  41.1 41.5 %copy-start.24 = (bf16[128,1920]{1,0:T(8,128)(2,1)}, bf16[128,1920]{1,0:T(8,128)(2,1)S(1)}, u32[]{:S(2)}) copy-start(bf16[128,1920]{1,0:T(8,128)(2,1)S(1)} %get-tuple-element.51.refs_0_) | copy-start | bytes 1474564
  41.1 41.5 %copy-start.26 = (bf16[128,1920]{1,0:T(8,128)(2,1)}, bf16[128,1920]{1,0:T(8,128)(2,1)S(1)}, u32[]{:S(2)}) copy-start(bf16[128,1920]{1,0:T(8,128)(2,1)S(1)} %get-tuple-element.52.refs_1_) | copy-start | bytes 1474564
  46.6 36.0 %collective-permute-start.12 = (bf16[3,4,224,512]{3,2,1,0:T(8,128)(2,1)S(1)}, bf16[3,4,224,512]{3,2,1,0:T(8,128)(2,1)S(1)}, u32[]{:S(2)}, u32[]{:S(2)}) collective-permute-start(bf16[3,4,224,512]{3,2,1,0:T(8,128)(2,1)S(1)} %shard_map.66), channel_id=1, source_target_pairs={{0,4},{4,0},{8,12},{12,8},{16,20},{20,16},{24,28},{28,24},{1,5},{5... | collective-permute-start | bytes 8257544 | tf_op jit(solution)/shard_map/ppermute | solution.py:298
  46.6 14.1 %collective-permute-start.8 = (bf16[128,1920]{1,0:T(8,128)(2,1)S(1)}, bf16[128,1920]{1,0:T(8,128)(2,1)S(1)}, u32[]{:S(2)}, u32[]{:S(2)}) collective-permute-start(bf16[128,1920]{1,0:T(8,128)(2,1)S(1)} %get-tuple-element.51.refs_0_), channel_id=1, source_target_pairs={{0,16},{4,20},{8,24},{12,28},{16,0},{20,4},{24,8},{28,12},{1,17},{... | collective-permute-start | bytes 1474568 | tf_op jit(solution)/shard_map/ppermute | solution.py:295
  48.2 14.1 %collective-permute-start.7 = (bf16[128,1920]{1,0:T(8,128)(2,1)S(1)}, bf16[128,1920]{1,0:T(8,128)(2,1)S(1)}, u32[]{:S(2)}, u32[]{:S(2)}) collective-permute-start(bf16[128,1920]{1,0:T(8,128)(2,1)S(1)} %get-tuple-element.52.refs_1_), channel_id=1, source_target_pairs={{0,8},{4,12},{8,0},{12,4},{16,24},{20,28},{24,16},{28,20},{1,9},{5... | collective-permute-start | bytes 1474568 | tf_op jit(solution)/shard_map/ppermute | solution.py:295
  48.8 24.1 %collective-permute-start.6 = (bf16[128,1920]{1,0:T(8,128)(2,1)S(1)}, bf16[128,1920]{1,0:T(8,128)(2,1)S(1)}, u32[]{:S(2)}, u32[]{:S(2)}) collective-permute-start(bf16[128,1920]{1,0:T(8,128)(2,1)S(1)} %get-tuple-element.51.refs_0_), channel_id=1, source_target_pairs={{0,8},{4,12},{8,0},{12,4},{16,24},{20,28},{24,16},{28,20},{1,9},{5... | collective-permute-start | bytes 1474568 | tf_op jit(solution)/shard_map/ppermute | solution.py:295
  50.3 22.6 %collective-permute-start.9 = (bf16[128,1920]{1,0:T(8,128)(2,1)S(1)}, bf16[128,1920]{1,0:T(8,128)(2,1)S(1)}, u32[]{:S(2)}, u32[]{:S(2)}) collective-permute-start(bf16[128,1920]{1,0:T(8,128)(2,1)S(1)} %get-tuple-element.52.refs_1_), channel_id=1, source_target_pairs={{0,16},{4,20},{8,24},{12,28},{16,0},{20,4},{24,8},{28,12},{1,17},{... | collective-permute-start | bytes 1474568 | tf_op jit(solution)/shard_map/ppermute | solution.py:295
  60.7 28.6 %copy-start.28 = (bf16[128,1920]{1,0:T(8,128)(2,1)}, bf16[128,1920]{1,0:T(8,128)(2,1)S(1)}, u32[]{:S(2)}) copy-start(bf16[128,1920]{1,0:T(8,128)(2,1)S(1)} %collective-permute-done.8.refs_4_) | copy-start | bytes 1474564
  60.7 21.9 %collective-permute-start.10 = (bf16[128,1920]{1,0:T(8,128)(2,1)S(1)}, bf16[128,1920]{1,0:T(8,128)(2,1)S(1)}, u32[]{:S(2)}, u32[]{:S(2)}) collective-permute-start(bf16[128,1920]{1,0:T(8,128)(2,1)S(1)} %collective-permute-done.8.refs_4_), channel_id=1, source_target_pairs={{0,8},{4,12},{8,0},{12,4},{16,24},{20,28},{24,16},{28,20},{1,9},{5... | collective-permute-start | bytes 1474568 | tf_op jit(solution)/shard_map/ppermute | solution.py:295
  62.3 27.1 %copy-start.30 = (bf16[128,1920]{1,0:T(8,128)(2,1)}, bf16[128,1920]{1,0:T(8,128)(2,1)S(1)}, u32[]{:S(2)}) copy-start(bf16[128,1920]{1,0:T(8,128)(2,1)S(1)} %collective-permute-done.7.refs_3_) | copy-start | bytes 1474564
  62.3 20.3 %collective-permute-start.11 = (bf16[128,1920]{1,0:T(8,128)(2,1)S(1)}, bf16[128,1920]{1,0:T(8,128)(2,1)S(1)}, u32[]{:S(2)}, u32[]{:S(2)}) collective-permute-start(bf16[128,1920]{1,0:T(8,128)(2,1)S(1)} %collective-permute-done.7.refs_3_), channel_id=1, source_target_pairs={{0,16},{4,20},{8,24},{12,28},{16,0},{20,4},{24,8},{28,12},{1,17},{... | collective-permute-start | bytes 1474568 | tf_op jit(solution)/shard_map/ppermute | solution.py:295
  91.5 103.9 %reduce-scatter.5.cloned.1.call-start = ((), (), s32[]{:S(2)}) async-start(), calls=%async_computation.3 | async-start | bytes 2621440 | tf_op jit(solution)/shard_map/reduce_scatter | solution.py:341
  92.0 18.4 %collective-permute-start.13 = (bf16[3,224,512]{2,1,0:T(8,128)(2,1)S(1)}, bf16[3,224,512]{2,1,0:T(8,128)(2,1)S(1)}, u32[]{:S(2)}, u32[]{:S(2)}) collective-permute-start(bf16[3,224,512]{2,1,0:T(8,128)(2,1)S(1)} %get-tuple-element.55), channel_id=1, source_target_pairs={{0,8},{4,12},{8,0},{12,4},{16,24},{20,28},{24,16},{28,20},{1,9},{5... | collective-permute-start | bytes 2064392 | tf_op jit(solution)/shard_map/ppermute | solution.py:295
  92.6 31.1 %collective-permute-start.14 = (bf16[3,224,512]{2,1,0:T(8,128)(2,1)S(1)}, bf16[3,224,512]{2,1,0:T(8,128)(2,1)S(1)}, u32[]{:S(2)}, u32[]{:S(2)}) collective-permute-start(bf16[3,224,512]{2,1,0:T(8,128)(2,1)S(1)} %get-tuple-element.56), channel_id=1, source_target_pairs={{0,16},{4,20},{8,24},{12,28},{16,0},{20,4},{24,8},{28,12},{1,17},{... | collective-permute-start | bytes 2064392 | tf_op jit(solution)/shard_map/ppermute | solution.py:295
  93.8 30.8 %collective-permute-start.15 = (bf16[3,224,512]{2,1,0:T(8,128)(2,1)S(1)}, bf16[3,224,512]{2,1,0:T(8,128)(2,1)S(1)}, u32[]{:S(2)}, u32[]{:S(2)}) collective-permute-start(bf16[3,224,512]{2,1,0:T(8,128)(2,1)S(1)} %get-tuple-element.57), channel_id=1, source_target_pairs={{0,24},{4,28},{8,16},{12,20},{16,8},{20,12},{24,0},{28,4},{1,25},{... | collective-permute-start | bytes 2064392 | tf_op jit(solution)/shard_map/ppermute | solution.py:295
  138.7 5.2 %collective-permute-start.16 = (bf16[3,4,224,512]{3,2,1,0:T(8,128)(2,1)S(1)}, bf16[3,4,224,512]{3,2,1,0:T(8,128)(2,1)S(1)}, u32[]{:S(2)}, u32[]{:S(2)}) collective-permute-start(bf16[3,4,224,512]{3,2,1,0:T(8,128)(2,1)S(1)} %shard_map.68), channel_id=1, source_target_pairs={{0,4},{4,0},{8,12},{12,8},{16,20},{20,16},{24,28},{28,24},{1,5},{5... | collective-permute-start | bytes 8257544 | tf_op jit(solution)/shard_map/ppermute | solution.py:298
  153.4 46.8 %collective-permute-start.20 = (bf16[3,224,512]{2,1,0:T(8,128)(2,1)}, bf16[3,224,512]{2,1,0:T(8,128)(2,1)S(1)}, u32[]{:S(2)}, u32[]{:S(2)}) collective-permute-start(bf16[3,224,512]{2,1,0:T(8,128)(2,1)} %get-tuple-element.63), channel_id=1, source_target_pairs={{0,8},{4,12},{8,0},{12,4},{16,24},{20,28},{24,16},{28,20},{1,9},{5... | collective-permute-start | bytes 2064392 | tf_op jit(solution)/shard_map/ppermute | solution.py:295
  154.9 45.3 %collective-permute-start.21 = (bf16[3,224,512]{2,1,0:T(8,128)(2,1)}, bf16[3,224,512]{2,1,0:T(8,128)(2,1)}, u32[]{:S(2)}, u32[]{:S(2)}) collective-permute-start(bf16[3,224,512]{2,1,0:T(8,128)(2,1)} %get-tuple-element.64), channel_id=1, source_target_pairs={{0,16},{4,20},{8,24},{12,28},{16,0},{20,4},{24,8},{28,12},{1,17},{... | collective-permute-start | bytes 2064392 | tf_op jit(solution)/shard_map/ppermute | solution.py:295
  156.4 43.9 %collective-permute-start.22 = (bf16[3,224,512]{2,1,0:T(8,128)(2,1)}, bf16[3,224,512]{2,1,0:T(8,128)(2,1)}, u32[]{:S(2)}, u32[]{:S(2)}) collective-permute-start(bf16[3,224,512]{2,1,0:T(8,128)(2,1)} %get-tuple-element.65), channel_id=1, source_target_pairs={{0,24},{4,28},{8,16},{12,20},{16,8},{20,12},{24,0},{28,4},{1,25},{... | collective-permute-start | bytes 2064392 | tf_op jit(solution)/shard_map/ppermute | solution.py:295
  200.2 32.7 %copy-start.16 = (bf16[1024,128]{1,0:T(8,128)(2,1)S(1)}, bf16[1024,128]{1,0:T(8,128)(2,1)}, u32[]{:S(2)}) copy-start(bf16[1024,128]{1,0:T(8,128)(2,1)} %copy-done.14) | copy-start | bytes 786436
  202.6 35.0 %copy-start.3 = (bf16[3,4,224,512]{3,2,1,0:T(8,128)(2,1)}, bf16[3,4,224,512]{3,2,1,0:T(8,128)(2,1)S(1)}, u32[]{:S(2)}) copy-start(bf16[3,4,224,512]{3,2,1,0:T(8,128)(2,1)S(1)} %shard_map.71) | copy-start | bytes 8257540
  202.6 30.4 %collective-permute-start.23 = (bf16[3,4,224,512]{3,2,1,0:T(8,128)(2,1)S(1)}, bf16[3,4,224,512]{3,2,1,0:T(8,128)(2,1)S(1)}, u32[]{:S(2)}, u32[]{:S(2)}) collective-permute-start(bf16[3,4,224,512]{3,2,1,0:T(8,128)(2,1)S(1)} %shard_map.71), channel_id=1, source_target_pairs={{0,4},{4,0},{8,12},{12,8},{16,20},{20,16},{24,28},{28,24},{1,5},{5... | collective-permute-start | bytes 8257544 | tf_op jit(solution)/shard_map/ppermute | solution.py:298
  202.6 14.3 %collective-permute-start.17 = (bf16[128,1024]{1,0:T(8,128)(2,1)S(1)}, bf16[128,1024]{1,0:T(8,128)(2,1)S(1)}, u32[]{:S(2)}, u32[]{:S(2)}) collective-permute-start(bf16[128,1024]{1,0:T(8,128)(2,1)S(1)} %get-tuple-element.62.refs_0_), channel_id=1, source_target_pairs={{0,1},{1,0},{2,3},{3,2},{4,5},{5,4},{6,7},{7,6},{8,9},{9,8},{10,11... | collective-permute-start | bytes 786440 | tf_op jit(solution)/shard_map/ppermute | solution.py:301
  202.7 14.3 %collective-permute-start.18 = (bf16[128,1024]{1,0:T(8,128)(2,1)S(1)}, bf16[128,1024]{1,0:T(8,128)(2,1)S(1)}, u32[]{:S(2)}, u32[]{:S(2)}) collective-permute-start(bf16[128,1024]{1,0:T(8,128)(2,1)S(1)} %get-tuple-element.62.refs_0_), channel_id=1, source_target_pairs={{0,2},{1,3},{2,0},{3,1},{4,6},{5,7},{6,4},{7,5},{8,10},{9,11},{10,... | collective-permute-start | bytes 786440 | tf_op jit(solution)/shard_map/ppermute | solution.py:301
  217.0 14.7 %collective-permute-start.31 = (bf16[128,1024]{1,0:T(8,128)(2,1)}, bf16[128,1024]{1,0:T(8,128)(2,1)S(1)}, u32[]{:S(2)}, u32[]{:S(2)}) collective-permute-start(bf16[128,1024]{1,0:T(8,128)(2,1)} %get-tuple-element.74.refs_0_), channel_id=1, source_target_pairs={{0,2},{1,3},{2,0},{3,1},{4,6},{5,7},{6,4},{7,5},{8,10},{9,11},{10,... | collective-permute-start | bytes 786440 | tf_op jit(solution)/shard_map/ppermute | solution.py:301
  218.3 14.7 %collective-permute-start.19 = (bf16[128,1024]{1,0:T(8,128)(2,1)S(1)}, bf16[128,1024]{1,0:T(8,128)(2,1)S(1)}, u32[]{:S(2)}, u32[]{:S(2)}) collective-permute-start(bf16[128,1024]{1,0:T(8,128)(2,1)S(1)} %collective-permute-done.18.refs_2_), channel_id=1, source_target_pairs={{0,1},{1,0},{2,3},{3,2},{4,5},{5,4},{6,7},{7,6},{8,9},{9,8},{10,11... | collective-permute-start | bytes 786440 | tf_op jit(solution)/shard_map/ppermute | solution.py:301
  221.4 19.8 %collective-permute-start.30 = (bf16[128,1024]{1,0:T(8,128)(2,1)}, bf16[128,1024]{1,0:T(8,128)(2,1)S(1)}, u32[]{:S(2)}, u32[]{:S(2)}) collective-permute-start(bf16[128,1024]{1,0:T(8,128)(2,1)} %get-tuple-element.74.refs_0_), channel_id=1, source_target_pairs={{0,1},{1,0},{2,3},{3,2},{4,5},{5,4},{6,7},{7,6},{8,9},{9,8},{10,11... | collective-permute-start | bytes 786440 | tf_op jit(solution)/shard_map/ppermute | solution.py:301
  231.7 11.1 %collective-permute-start.32 = (bf16[128,1024]{1,0:T(8,128)(2,1)S(1)}, bf16[128,1024]{1,0:T(8,128)(2,1)S(1)}, u32[]{:S(2)}, u32[]{:S(2)}) collective-permute-start(bf16[128,1024]{1,0:T(8,128)(2,1)S(1)} %collective-permute-done.31.refs_2_), channel_id=1, source_target_pairs={{0,1},{1,0},{2,3},{3,2},{4,5},{5,4},{6,7},{7,6},{8,9},{9,8},{10,11... | collective-permute-start | bytes 786440 | tf_op jit(solution)/shard_map/ppermute | solution.py:301
  237.6 16.8 %collective-permute-start.26 = (bf16[128,1792]{1,0:T(8,128)(2,1)S(1)}, bf16[128,1792]{1,0:T(8,128)(2,1)S(1)}, u32[]{:S(2)}, u32[]{:S(2)}) collective-permute-start(bf16[128,1792]{1,0:T(8,128)(2,1)S(1)} %get-tuple-element.73), channel_id=1, source_target_pairs={{0,24},{4,28},{8,16},{12,20},{16,8},{20,12},{24,0},{28,4},{1,25},{... | collective-permute-start | bytes 1376264 | tf_op jit(solution)/shard_map/ppermute | solution.py:295
  240.1 22.0 %collective-permute-start.25 = (bf16[128,1792]{1,0:T(8,128)(2,1)S(1)}, bf16[128,1792]{1,0:T(8,128)(2,1)}, u32[]{:S(2)}, u32[]{:S(2)}) collective-permute-start(bf16[128,1792]{1,0:T(8,128)(2,1)S(1)} %get-tuple-element.72), channel_id=1, source_target_pairs={{0,16},{4,20},{8,24},{12,28},{16,0},{20,4},{24,8},{28,12},{1,17},{... | collective-permute-start | bytes 1376264 | tf_op jit(solution)/shard_map/ppermute | solution.py:295
  240.6 21.5 %collective-permute-start.24 = (bf16[128,1792]{1,0:T(8,128)(2,1)S(1)}, bf16[128,1792]{1,0:T(8,128)(2,1)}, u32[]{:S(2)}, u32[]{:S(2)}) collective-permute-start(bf16[128,1792]{1,0:T(8,128)(2,1)S(1)} %get-tuple-element.71), channel_id=1, source_target_pairs={{0,8},{4,12},{8,0},{12,4},{16,24},{20,28},{24,16},{28,20},{1,9},{5... | collective-permute-start | bytes 1376264 | tf_op jit(solution)/shard_map/ppermute | solution.py:295
  251.4 20.4 %collective-permute-start.35 = (bf16[128,1792]{1,0:T(8,128)(2,1)S(1)}, bf16[128,1792]{1,0:T(8,128)(2,1)S(1)}, u32[]{:S(2)}, u32[]{:S(2)}) collective-permute-start(bf16[128,1792]{1,0:T(8,128)(2,1)S(1)} %get-tuple-element.78), channel_id=1, source_target_pairs={{0,24},{4,28},{8,16},{12,20},{16,8},{20,12},{24,0},{28,4},{1,25},{... | collective-permute-start | bytes 1376264 | tf_op jit(solution)/shard_map/ppermute | solution.py:295
  253.9 24.6 %collective-permute-start.34 = (bf16[128,1792]{1,0:T(8,128)(2,1)S(1)}, bf16[128,1792]{1,0:T(8,128)(2,1)S(1)}, u32[]{:S(2)}, u32[]{:S(2)}) collective-permute-start(bf16[128,1792]{1,0:T(8,128)(2,1)S(1)} %get-tuple-element.77), channel_id=1, source_target_pairs={{0,16},{4,20},{8,24},{12,28},{16,0},{20,4},{24,8},{28,12},{1,17},{... | collective-permute-start | bytes 1376264 | tf_op jit(solution)/shard_map/ppermute | solution.py:295
  254.4 24.2 %collective-permute-start.33 = (bf16[128,1792]{1,0:T(8,128)(2,1)S(1)}, bf16[128,1792]{1,0:T(8,128)(2,1)S(1)}, u32[]{:S(2)}, u32[]{:S(2)}) collective-permute-start(bf16[128,1792]{1,0:T(8,128)(2,1)S(1)} %get-tuple-element.76), channel_id=1, source_target_pairs={{0,8},{4,12},{8,0},{12,4},{16,24},{20,28},{24,16},{28,20},{1,9},{5... | collective-permute-start | bytes 1376264 | tf_op jit(solution)/shard_map/ppermute | solution.py:295
  263.5 19.0 %collective-permute-start.27 = (bf16[32,1792]{1,0:T(8,128)(2,1)S(1)}, bf16[32,1792]{1,0:T(8,128)(2,1)S(1)}, u32[]{:S(2)}, u32[]{:S(2)}) collective-permute-start(bf16[32,1792]{1,0:T(8,128)(2,1)S(1)} %get-tuple-element.94), channel_id=1, source_target_pairs={{0,1},{1,0},{2,3},{3,2},{4,5},{5,4},{6,7},{7,6},{8,9},{9,8},{10,11... | collective-permute-start | bytes 344072 | tf_op jit(solution)/shard_map/ppermute | solution.py:301
  264.3 19.3 %collective-permute-start.28 = (bf16[32,1792]{1,0:T(8,128)(2,1)S(1)}, bf16[32,1792]{1,0:T(8,128)(2,1)S(1)}, u32[]{:S(2)}, u32[]{:S(2)}) collective-permute-start(bf16[32,1792]{1,0:T(8,128)(2,1)S(1)} %get-tuple-element.93), channel_id=1, source_target_pairs={{0,2},{1,3},{2,0},{3,1},{4,6},{5,7},{6,4},{7,5},{8,10},{9,11},{10,... | collective-permute-start | bytes 344072 | tf_op jit(solution)/shard_map/ppermute | solution.py:301
  271.8 11.9 %collective-permute-start.29 = (bf16[32,1792]{1,0:T(8,128)(2,1)S(1)}, bf16[32,1792]{1,0:T(8,128)(2,1)S(1)}, u32[]{:S(2)}, u32[]{:S(2)}) collective-permute-start(bf16[32,1792]{1,0:T(8,128)(2,1)S(1)} %get-tuple-element.92), channel_id=1, source_target_pairs={{0,3},{1,2},{2,1},{3,0},{4,7},{5,6},{6,5},{7,4},{8,11},{9,10},{10,... | collective-permute-start | bytes 344072 | tf_op jit(solution)/shard_map/ppermute | solution.py:301
  278.9 7.5 %collective-permute-start.36 = (bf16[32,1792]{1,0:T(8,128)(2,1)S(1)}, bf16[32,1792]{1,0:T(8,128)(2,1)S(1)}, u32[]{:S(2)}, u32[]{:S(2)}) collective-permute-start(bf16[32,1792]{1,0:T(8,128)(2,1)S(1)} %get-tuple-element.90), channel_id=1, source_target_pairs={{0,1},{1,0},{2,3},{3,2},{4,5},{5,4},{6,7},{7,6},{8,9},{9,8},{10,11... | collective-permute-start | bytes 344072 | tf_op jit(solution)/shard_map/ppermute | solution.py:301
  280.1 6.3 %collective-permute-start.37 = (bf16[32,1792]{1,0:T(8,128)(2,1)S(1)}, bf16[32,1792]{1,0:T(8,128)(2,1)S(1)}, u32[]{:S(2)}, u32[]{:S(2)}) collective-permute-start(bf16[32,1792]{1,0:T(8,128)(2,1)S(1)} %get-tuple-element.89), channel_id=1, source_target_pairs={{0,2},{1,3},{2,0},{3,1},{4,6},{5,7},{6,4},{7,5},{8,10},{9,11},{10,... | collective-permute-start | bytes 344072 | tf_op jit(solution)/shard_map/ppermute | solution.py:301
  282.5 9.2 %collective-permute-start.38 = (bf16[32,1792]{1,0:T(8,128)(2,1)S(1)}, bf16[32,1792]{1,0:T(8,128)(2,1)S(1)}, u32[]{:S(2)}, u32[]{:S(2)}) collective-permute-start(bf16[32,1792]{1,0:T(8,128)(2,1)S(1)} %get-tuple-element.88), channel_id=1, source_target_pairs={{0,3},{1,2},{2,1},{3,0},{4,7},{5,6},{6,5},{7,4},{8,11},{9,10},{10,... | collective-permute-start | bytes 344072 | tf_op jit(solution)/shard_map/ppermute | solution.py:301
  (35 other events, 198.1 us)
Sparse Core Ops, SparseCore 0:
  91.6 43.8 reduce-scatter.2
  152.2 43.1 reduce-scatter.4

commit v9 on v6

--- a/solution.py
+++ b/solution.py
@@ -229,45 +229,51 @@
     )(routing, *gates, *ups)
 
 
-def down_kernel(step, slots, routing_ref, hid_ref, *refs):
-    weights, (out_ref,) = refs[:CORES], refs[CORES:]
+def down_kernel(slots, levels, place_ref, routing_ref, *refs):
+    hids, refs = refs[:levels], refs[levels:]
+    weights, (*outs, left) = refs[:CORES], refs[CORES:]
     experts, depth, width = weights[0].shape
-    ids = routing_ref[step].astype(jnp.float32)
-    lefts = []
-    for which in range(experts):
-        mine = jnp.zeros((hid_ref.shape[0], width), jnp.float32)
-        for slot in range(slots):
-            part = hid_ref[:, slot * width : (slot + 1) * width].astype(jnp.float32)
-            mine = jnp.where(ids[:, slot : slot + 1] == which, part, mine)
-        lefts.append(mine.astype(hid_ref.dtype))
+    rows = hids[0].shape[0]
+    for step, hid_ref in enumerate(hids):
+        block = jnp.bitwise_xor(place_ref[2], step)
+        ids = routing_ref[step].astype(jnp.float32)
+        for which in range(experts):
+            mine = jnp.zeros((rows, width), jnp.float32)
+            for slot in range(slots):
+                value = hid_ref[:, slot * width : (slot + 1) * width].astype(jnp.float32)
+                mine = jnp.where(ids[:, slot : slot + 1] == which, value, mine)
+            left[which, rows_of(block, rows), :] = mine.astype(left.dtype)
     for side, weight in enumerate(weights):
         total = None
         for which in range(experts):
             term = lax.dot_general(
-                lefts[which],
+                left[which],
                 weight[which],
                 (((1,), (1,)), ((), ())),
                 preferred_element_type=jnp.float32,
             )
             total = term if total is None else total + term
-        out_ref[:, side * depth : (side + 1) * depth] = total.astype(out_ref.dtype)
-
-
-def down_sums(routing, hidden, weights, step, slots):
-    rows = hidden.shape[0]
+        for step, out_ref in enumerate(outs):
+            part = total[step * rows : (step + 1) * rows]
+            out_ref[:, side * depth : (side + 1) * depth] = part.astype(out_ref.dtype)
+
+
+def down_sums(place, routing, hids, weights, slots):
+    rows, levels = hids[0].shape[0], len(hids)
     experts, depth, width = weights[0].shape
-    wide = CORES * depth
-    return pl.pallas_call(
-        functools.partial(down_kernel, step, slots),
-        in_specs=[VMEM_SPEC] * (2 + CORES),
-        out_specs=VMEM_SPEC,
-        out_shape=bf16(rows, wide),
+    wide, count = CORES * depth, levels * rows
+    return pl.pallas_call(
+        functools.partial(down_kernel, slots, levels),
+        in_specs=[SMEM_SPEC] + [VMEM_SPEC] * (1 + levels + CORES),
+        out_specs=[VMEM_SPEC] * levels,
+        out_shape=[bf16(rows, wide)] * levels,
+        scratch_shapes=[pltpu.VMEM((experts, count, width), jnp.bfloat16)],
         cost_estimate=cost(
-            2 * rows * wide * width * experts,
-            rows * slots * width + experts * wide * width + rows * wide,
+            2 * count * wide * width * experts,
+            count * slots * width + experts * wide * width + count * wide,
         ),
         compiler_params=PARAMS,
-    )(routing, hidden, *weights)
+    )(place, routing, *hids, *weights)
 
 
 def after(values, others):
@@ -294,14 +300,6 @@
 
     def to_level(value, step):
         return lax.ppermute(value, "tensor", [(s, s ^ step) for s in range(n_tensor)])
-
-    def to_owner(value, step):
-        pairs = [
-            (s * n_tensor + t, (s ^ ((t ^ step) * CORES)) * n_tensor + t)
-            for s in range(n_expert)
-            for t in range(n_tensor)
-        ]
-        return lax.ppermute(value, ("expert", "tensor"), pairs)
 
     def copies(value, send, bits, behind=()):
         held = {0: value}
@@ -351,26 +349,26 @@
     for half in range(HALVES):
         turn = (half + 1) % len(bits)
         toks.append(copies(groups[half], to_chip, bits[turn:] + bits[:turn]))
-    near = [tok[bit] for tok in toks for bit in bits]
-    up_same = chip_exchange(after(blocks_of(up_weight), near))
-
-    def products(weights, before, late):
-        sums, routings, parts = [], [], []
-        behind = before[-1][1] if before else []
+    up_blocks = blocks_of(up_weight)
+    toks = after(toks, up_blocks)
+    up_same = chip_exchange(after(up_blocks, toks))
+
+    def products(weights, behind, parts):
+        sums, routings = [], []
         for half in range(HALVES):
-            others = [parts, behind[:1], [marks for _, marks in before[half : half + 1]]]
-            others += late if half else []
-            *parts, routing = picked_sums(place, after(toks[half], others), weights, slots)
+            left = after(toks[half], parts)
+            *parts, routing = picked_sums(place, left, weights, slots)
             terms, behind = level_sums(*parts, behind)
             sums.append((terms, behind))
             routings.append(routing)
         return sums, routings
 
-    gate_sums, routings = products(gate_pair, [], up_same[: chips // 2])
+    gate_sums, routings = products(gate_pair, [], [])
     up_joined = join_blocks(place, up_weight, after(up_same, gate_sums[-1][1][0]))
     up_pair = core_exchange(up_joined)
     down_same = chip_exchange(after(blocks_of(down_weight), up_joined))
-    up_sums, _ = products(up_pair, gate_sums, [])
+    up_sums, _ = products(up_pair, [], gate_sums[-1][1])
+
     hiddens, near, far = [], [], up_sums[-1][1][-1]
     bits = [1 << bit for bit in range(n_tensor.bit_length() - 1)]
     for half in range(HALVES):
@@ -380,20 +378,17 @@
         near, far = hiddens[-1][1], hiddens[-1][n_tensor // 2]
     down_joined = join_blocks(place, down_weight, after(down_same, [h[0] for h in hiddens]))
     down_pair = core_exchange(down_joined)
-
-    backs, part = [], []
+    backs, parts = [], []
     for half in range(HALVES):
-        routing, blocks = routings[half], after(hiddens[half], part)
-        if half + 1 < HALVES:
-            blocks[-1] = after(blocks[-1], hiddens[half + 1][n_tensor // 2])
-        total = 0.0
-        for step in range(n_tensor):
-            part = down_sums(routing, blocks[step], down_pair, step, slots)
-            total = total + to_owner(part, step).astype(jnp.float32)
+        hids = after(hiddens[half], parts)
+        parts = down_sums(place, routings[half], hids, down_pair, slots)
+        total = parts[0].astype(jnp.float32)
+        for step in range(1, chips):
+            total = total + to_chip(parts[step], step).astype(jnp.float32)
         total = total.astype(jnp.bfloat16).reshape(n_tensor, rows // HALVES, -1)
-        for step in range(n_tensor):
-            piece = lax.dynamic_index_in_dim(total, level ^ step, 0, keepdims=False)
-            backs.append(to_level(piece, step) if step else piece)
+        for other in range(n_tensor):
+            piece = lax.dynamic_index_in_dim(total, level ^ other, 0, keepdims=False)
+            backs.append(to_level(piece, other) if other else piece)
     return finish(place, backs, n_tensor, depth)
 
 

time: 313 us -> 297 us (0.949)
  starting transfers between devices: 80 us -> 58.9 us
  waiting for transfers between devices: 176 us -> 190 us
  Pallas kernels: 42.3 us -> 36.3 us
  local copies, waits for them, and re-layouts: 11.6 us -> 8.36 us
    ppermute x15 -> x21, waiting for transfers between devices: 50.1 us -> 75.8 us  [to_chip(): return lax.ppermute(value, 'expert', pairs)]
    ppermute x8 -> x0, starting transfers between devices: 24.9 us -> none  [to_owner(): return lax.ppermute(value, ('expert', 'tensor'), pairs)]
    ppermute x8 -> x0, waiting for transfers between devices: 12.9 us -> none  [to_owner(): return lax.ppermute(value, ('expert', 'tensor'), pairs)]
    ppermute x15 -> x21, starting transfers between devices: 18.7 us -> 26 us  [to_chip(): return lax.ppermute(value, 'expert', pairs)]
    ppermute x23, waiting for transfers between devices: 108 us -> 114 us  [to_level(): lax.ppermute(value, 'tensor', [(s, s ^ step) for s in range(n_tensor)])]
    pallas_call x8 -> x2, Pallas kernels: 16.3 us -> 10 us  [down_sums(): pl.pallas_call(functools.partial(down_kernel, slots, levels), in_specs=[S...]
    ppermute x3, waiting for transfers between devices: 5.09 us -> 0.01 us  [to_core(): return lax.ppermute(value, 'expert', [(s, s ^ 1) for s in range(n_expert)])]
    ppermute x23, starting transfers between devices: 36.1 us -> 32.6 us  [to_level(): lax.ppermute(value, 'tensor', [(s, s ^ step) for s in range(n_tensor)])]
  transfers between devices with their start and end apart: 49 -> 47, of which waited for: 23 -> 28; matrix products, arithmetic and copies ran while one was open for 1% -> 1% of each run, Pallas kernels for 7% -> 6%
where the time goes in v9:
time: 297 us; the launch traced here: 296 us
  waiting for transfers between devices  190 us (64%)
  starting transfers between devices  58.9 us (20%)
  Pallas kernels  36.3 us (12%)
  local copies, waits for them, and re-layouts  8.36 us (3%)
    ppermute x23, waiting for transfers between devices, to_level(): lax.ppermute(value, 'tensor', [(s, s ^ step) for s in range(n_tensor)])  114 us
    ppermute x21, waiting for transfers between devices, to_chip(): return lax.ppermute(value, 'expert', pairs)  75.8 us
    ppermute x23, starting transfers between devices, to_level(): lax.ppermute(value, 'tensor', [(s, s ^ step) for s in range(n_tensor)])  32.6 us
    ppermute x21, starting transfers between devices, to_chip(): return lax.ppermute(value, 'expert', pairs)  26 us
    pallas_call x4, Pallas kernels, picked_sums(): pl.pallas_call(functools.partial(pick_kernel, chips), in_specs=[SMEM_SPEC...  16.3 us
    pallas_call x2, Pallas kernels, down_sums(): pl.pallas_call(functools.partial(down_kernel, slots, levels), in_specs=[S...  10 us
  transfers between devices with their start and end apart: 47, of which 28 were waited for; matrix products, arithmetic and copies ran while one was open for 1% of the time, Pallas kernels for 6%

profile of v9, /device:TPU:0, one launch (start us, length us, event | category | flops | bytes accessed | tf_op | source)
XLA Modules:
  0.0 296.4 jit_solution(17511919213367234939)
XLA Ops:
  0.0 3.0 %constant_dynamic-slice_fusion.3 = (bf16[3,224,512]{2,1,0:T(8,128)(2,1)}, bf16[3,224,512]{2,1,0:T(8,128)(2,1)}, bf16[3,224,512]{2,1,0:T(8,128)(2,1)}) fusion(bf16[3,224,2048]{2,1,0:T(8,128)(2,1)} %own_ref.3, s32[]{:T(128)S(6)} %select_n.47, s32[]{:T(128)S(6)} %select_n.46, s32[]{:T(128)S(6)} %select_n.45), kind=kLoop, calls=%fused_computation.17 | loop fusion | bytes 4128780 | tf_op jit(solution)/shard_map/dynamic_slice | solution.py:327
  3.0 3.0 %collective-permute-start.10 = (bf16[3,224,512]{2,1,0:T(8,128)(2,1)}, bf16[3,224,512]{2,1,0:T(8,128)(2,1)S(1)}, u32[]{:S(2)}, u32[]{:S(2)}) collective-permute-start(bf16[3,224,512]{2,1,0:T(8,128)(2,1)} %get-tuple-element.175), channel_id=1, source_target_pairs={{0,16},{4,20},{8,24},{12,28},{16,0},{20,4},{24,8},{28,12},{1,17},{... | collective-permute-start | bytes 2064392 | tf_op jit(solution)/shard_map/ppermute | solution.py:296
  8.8 1.7 shard_map.64
  11.2 2.1 collective-permute-start
  13.2 2.6 collective-permute-start.1
  15.8 6.8 %collective-permute-done.refs_1_ = bf16[64,1792]{1,0:T(8,128)(2,1)S(1)} collective-permute-done((bf16[64,1792]{1,0:T(8,128)(2,1)S(1)}, bf16[64,1792]{1,0:T(8,128)(2,1)S(1)}, u32[]{:S(2)}, u32[]{:S(2)}) %collective-permute-start) | collective-permute-done | bytes 229408 | tf_op jit(solution)/shard_map/ppermute | solution.py:302
  23.2 2.6 collective-permute-start.2
  26.1 5.4 %collective-permute-done.2.refs_3_ = bf16[64,1792]{1,0:T(8,128)(2,1)} collective-permute-done((bf16[64,1792]{1,0:T(8,128)(2,1)}, bf16[64,1792]{1,0:T(8,128)(2,1)}, u32[]{:S(2)}, u32[]{:S(2)}) %collective-permute-start.2) | collective-permute-done | bytes 229408 | tf_op jit(solution)/shard_map/ppermute | solution.py:302
  34.5 1.9 collective-permute-done.10.refs_1_
  37.8 2.2 shard_map.66
  40.0 1.8 collective-permute-start.4
  44.1 10.0 %collective-permute-done.4.refs_2_ = bf16[128,1920]{1,0:T(8,128)(2,1)S(1)} collective-permute-done((bf16[128,1920]{1,0:T(8,128)(2,1)S(1)}, bf16[128,1920]{1,0:T(8,128)(2,1)S(1)}, u32[]{:S(2)}, u32[]{:S(2)}) %collective-permute-start.4) | collective-permute-done | bytes 491552 | tf_op jit(solution)/shard_map/ppermute | solution.py:296
  54.1 1.7 collective-permute-start.5
  57.6 8.8 %collective-permute-done.3.refs_1_ = bf16[128,1920]{1,0:T(8,128)(2,1)S(1)} collective-permute-done((bf16[128,1920]{1,0:T(8,128)(2,1)S(1)}, bf16[128,1920]{1,0:T(8,128)(2,1)S(1)}, u32[]{:S(2)}, u32[]{:S(2)}) %collective-permute-start.3) | collective-permute-done | bytes 491552 | tf_op jit(solution)/shard_map/ppermute | solution.py:296
  66.4 9.8 %collective-permute-done.5.refs_3_ = bf16[128,1920]{1,0:T(8,128)(2,1)S(1)} collective-permute-done((bf16[128,1920]{1,0:T(8,128)(2,1)S(1)}, bf16[128,1920]{1,0:T(8,128)(2,1)S(1)}, u32[]{:S(2)}, u32[]{:S(2)}) %collective-permute-start.5) | collective-permute-done | bytes 491552 | tf_op jit(solution)/shard_map/ppermute | solution.py:296
  76.2 4.1 %shard_map.67 = (bf16[2,128,1024]{2,1,0:T(8,128)(2,1)S(1)}, bf16[2,128,1024]{2,1,0:T(8,128)(2,1)S(1)}, bf16[4,128,128]{2,1,0:T(8,128)(2,1)S(1)}) custom-call(s32[3]{0:T(128)S(1)} %pad_add_fusion.place_ref, bf16[128,1920]{1,0:T(8,128)(2,1)S(1)} %get-tuple-element.120.refs_0_, bf16[128,1920]{1,0:T(8,128)(2,1)S(1)} %collective-permute-done.3.refs_1_, ...), custom_call_target="tpu_custom_call" | custom-call | flops 2818572288 | bytes 8388608 | tf_op jit(solution)/shard_map/pallas_call | solution.py:195
  81.9 4.1 %shard_map.68 = (bf16[2,128,1024]{2,1,0:T(8,128)(2,1)S(1)}, bf16[2,128,1024]{2,1,0:T(8,128)(2,1)S(1)}, bf16[4,128,128]{2,1,0:T(8,128)(2,1)S(1)}) custom-call(s32[3]{0:T(128)S(1)} %pad_add_fusion.place_ref, bf16[128,1920]{1,0:T(8,128)(2,1)S(1)} %get-tuple-element.132.refs_0_, bf16[128,1920]{1,0:T(8,128)(2,1)S(1)} %collective-permute-done.6.refs_1_, ...), custom_call_target="tpu_custom_call" | custom-call | flops 2818572288 | bytes 8388608 | tf_op jit(solution)/shard_map/pallas_call | solution.py:195
  86.0 7.5 %collective-permute-done.13 = bf16[2,128,1024]{2,1,0:T(8,128)(2,1)S(1)} collective-permute-done((bf16[2,128,1024]{2,1,0:T(8,128)(2,1)S(1)}, bf16[2,128,1024]{2,1,0:T(8,128)(2,1)S(1)}, u32[]{:S(2)}, u32[]{:S(2)}) %collective-permute-start.13) | collective-permute-done | bytes 524320 | tf_op jit(solution)/shard_map/ppermute | solution.py:302
  98.7 2.6 collective-permute-start.14
  101.3 10.2 %collective-permute-done.15 = bf16[2,128,1024]{2,1,0:T(8,128)(2,1)S(1)} collective-permute-done((bf16[2,128,1024]{2,1,0:T(8,128)(2,1)S(1)}, bf16[2,128,1024]{2,1,0:T(8,128)(2,1)S(1)}, u32[]{:S(2)}, u32[]{:S(2)}) %collective-permute-start.15) | collective-permute-done | bytes 524320 | tf_op jit(solution)/shard_map/ppermute | solution.py:302
  111.6 2.0 collective-permute-done.17.refs_0_
  113.6 13.1 %collective-permute-done.18.refs_1_ = bf16[3,224,512]{2,1,0:T(8,128)(2,1)S(1)} collective-permute-done((bf16[3,224,512]{2,1,0:T(8,128)(2,1)S(1)}, bf16[3,224,512]{2,1,0:T(8,128)(2,1)S(1)}, u32[]{:S(2)}, u32[]{:S(2)}) %collective-permute-start.18) | collective-permute-done | bytes 688160 | tf_op jit(solution)/shard_map/ppermute | solution.py:296
  127.8 2.7 collective-permute-start.16
  130.5 12.5 %collective-permute-done.16.refs_2_ = bf16[1,128,1024]{2,1,0:T(8,128)(2,1)S(1)} collective-permute-done((bf16[1,128,1024]{2,1,0:T(8,128)(2,1)S(1)}, bf16[1,128,1024]{2,1,0:T(8,128)(2,1)S(1)}, u32[]{:S(2)}, u32[]{:S(2)}) %collective-permute-start.16) | collective-permute-done | bytes 262176 | tf_op jit(solution)/shard_map/ppermute | solution.py:302
  143.0 4.1 %shard_map.70 = (bf16[2,128,1024]{2,1,0:T(8,128)(2,1)S(1)}, bf16[2,128,1024]{2,1,0:T(8,128)(2,1)S(1)}, bf16[4,128,128]{2,1,0:T(8,128)(2,1)}) custom-call(s32[3]{0:T(128)S(1)} %pad_add_fusion.place_ref, bf16[128,1920]{1,0:T(8,128)(2,1)S(1)} %get-tuple-element.120.refs_0_, bf16[128,1920]{1,0:T(8,128)(2,1)S(1)} %collective-permute-done.3.refs_1_, ...), custom_call_target="tpu_custom_call" | custom-call | flops 2818572288 | bytes 8388608 | tf_op jit(solution)/shard_map/pallas_call | solution.py:195
  147.1 4.1 %shard_map.71 = (bf16[2,128,1024]{2,1,0:T(8,128)(2,1)S(1)}, bf16[2,128,1024]{2,1,0:T(8,128)(2,1)S(1)}, bf16[4,128,128]{2,1,0:T(8,128)(2,1)}) custom-call(s32[3]{0:T(128)S(1)} %pad_add_fusion.place_ref, bf16[128,1920]{1,0:T(8,128)(2,1)S(1)} %get-tuple-element.132.refs_0_, bf16[128,1920]{1,0:T(8,128)(2,1)S(1)} %collective-permute-done.6.refs_1_, ...), custom_call_target="tpu_custom_call" | custom-call | flops 2818572288 | bytes 8388608 | tf_op jit(solution)/shard_map/pallas_call | solution.py:195
  151.2 9.8 %collective-permute-done.21 = bf16[2,128,1024]{2,1,0:T(8,128)(2,1)S(1)} collective-permute-done((bf16[2,128,1024]{2,1,0:T(8,128)(2,1)S(1)}, bf16[2,128,1024]{2,1,0:T(8,128)(2,1)S(1)}, u32[]{:S(2)}, u32[]{:S(2)}) %collective-permute-start.21) | collective-permute-done | bytes 524320 | tf_op jit(solution)/shard_map/ppermute | solution.py:302
  163.5 1.8 collective-permute-start.30
  165.2 2.5 collective-permute-start.22
  167.8 12.0 %collective-permute-done.23 = bf16[2,128,1024]{2,1,0:T(8,128)(2,1)S(1)} collective-permute-done((bf16[2,128,1024]{2,1,0:T(8,128)(2,1)S(1)}, bf16[2,128,1024]{2,1,0:T(8,128)(2,1)S(1)}, u32[]{:S(2)}, u32[]{:S(2)}) %collective-permute-start.23) | collective-permute-done | bytes 524320 | tf_op jit(solution)/shard_map/ppermute | solution.py:302
  182.8 9.5 %collective-permute-done.24.refs_1_ = bf16[128,1024]{1,0:T(8,128)(2,1)S(1)} collective-permute-done((bf16[128,1024]{1,0:T(8,128)(2,1)S(1)}, bf16[128,1024]{1,0:T(8,128)(2,1)S(1)}, u32[]{:S(2)}, u32[]{:S(2)}) %collective-permute-start.24) | collective-permute-done | bytes 262176 | tf_op jit(solution)/shard_map/ppermute | solution.py:302
  192.3 1.8 collective-permute-done.25.refs_5_
  196.3 14.5 %collective-permute-done.26.refs_2_ = bf16[128,1024]{1,0:T(8,128)(2,1)S(1)} collective-permute-done((bf16[128,1024]{1,0:T(8,128)(2,1)S(1)}, bf16[128,1024]{1,0:T(8,128)(2,1)S(1)}, u32[]{:S(2)}, u32[]{:S(2)}) %collective-permute-start.26) | collective-permute-done | bytes 262176 | tf_op jit(solution)/shard_map/ppermute | solution.py:302
  210.8 2.1 collective-permute-start.27
  213.0 11.7 %collective-permute-done.39.refs_2_ = bf16[128,1024]{1,0:T(8,128)(2,1)S(1)} collective-permute-done((bf16[128,1024]{1,0:T(8,128)(2,1)S(1)}, bf16[128,1024]{1,0:T(8,128)(2,1)S(1)}, u32[]{:S(2)}, u32[]{:S(2)}) %collective-permute-start.39) | collective-permute-done | bytes 262176 | tf_op jit(solution)/shard_map/ppermute | solution.py:302
  225.7 4.7 %shard_map.75 = (bf16[128,1792]{1,0:T(8,128)(2,1)S(1)}, bf16[128,1792]{1,0:T(8,128)(2,1)S(1)}, bf16[128,1792]{1,0:T(8,128)(2,1)S(1)}, bf16[128,1792]{1,0:T(8,128)(2,1)S(1)}) custom-call(s32[3]{0:T(128)S(1)} %pad_add_fusion.place_ref, bf16[4,128,128]{2,1,0:T(8,128)(2,1)S(1)} %get-tuple-element.105.routing_ref, bf16[128,1024]{1,0:T(8,128)(2,1)S(1)} %shard_map.72.refs_0_, ...), custom_call_target="tpu_custom_call" | custom-call | flops 2818572288 | bytes 8388608 | tf_op jit(solution)/shard_map/pallas_call | solution.py:265
  231.3 4.7 %collective-permute-done.40.refs_3_ = bf16[128,1024]{1,0:T(8,128)(2,1)S(1)} collective-permute-done((bf16[128,1024]{1,0:T(8,128)(2,1)S(1)}, bf16[128,1024]{1,0:T(8,128)(2,1)S(1)}, u32[]{:S(2)}, u32[]{:S(2)}) %collective-permute-start.40) | collective-permute-done | bytes 262176 | tf_op jit(solution)/shard_map/ppermute | solution.py:302
  236.1 5.4 %shard_map.76 = (bf16[128,1792]{1,0:T(8,128)(2,1)S(1)}, bf16[128,1792]{1,0:T(8,128)(2,1)}, bf16[128,1792]{1,0:T(8,128)(2,1)S(1)}, bf16[128,1792]{1,0:T(8,128)(2,1)S(1)}) custom-call(s32[3]{0:T(128)S(1)} %pad_add_fusion.place_ref, bf16[4,128,128]{2,1,0:T(8,128)(2,1)S(1)} %get-tuple-element.151.routing_ref, bf16[128,1024]{1,0:T(8,128)(2,1)S(1)} %shard_map.73.refs_0_, ...), custom_call_target="tpu_custom_call" | custom-call | flops 2818572288 | bytes 8388608 | tf_op jit(solution)/shard_map/pallas_call | solution.py:265
  247.1 8.1 %collective-permute-done.41 = bf16[128,1792]{1,0:T(8,128)(2,1)} collective-permute-done((bf16[128,1792]{1,0:T(8,128)(2,1)}, bf16[128,1792]{1,0:T(8,128)(2,1)}, u32[]{:S(2)}, u32[]{:S(2)}) %collective-permute-start.41) | collective-permute-done | bytes 458784 | tf_op jit(solution)/shard_map/ppermute | solution.py:296
  256.8 9.4 %collective-permute-done.42 = bf16[128,1792]{1,0:T(8,128)(2,1)} collective-permute-done((bf16[128,1792]{1,0:T(8,128)(2,1)S(1)}, bf16[128,1792]{1,0:T(8,128)(2,1)}, u32[]{:S(2)}, u32[]{:S(2)}) %collective-permute-start.42) | collective-permute-done | bytes 458784 | tf_op jit(solution)/shard_map/ppermute | solution.py:296
  267.8 2.2 collective-permute-start.45
  270.0 4.8 %collective-permute-done.32 = bf16[128,1792]{1,0:T(8,128)(2,1)S(1)} collective-permute-done((bf16[128,1792]{1,0:T(8,128)(2,1)S(1)}, bf16[128,1792]{1,0:T(8,128)(2,1)S(1)}, u32[]{:S(2)}, u32[]{:S(2)}) %collective-permute-start.32) | collective-permute-done | bytes 458784 | tf_op jit(solution)/shard_map/ppermute | solution.py:296
  274.8 2.2 collective-permute-start.46
  277.1 6.6 %collective-permute-done.33 = bf16[128,1792]{1,0:T(8,128)(2,1)S(1)} collective-permute-done((bf16[128,1792]{1,0:T(8,128)(2,1)S(1)}, bf16[128,1792]{1,0:T(8,128)(2,1)S(1)}, u32[]{:S(2)}, u32[]{:S(2)}) %collective-permute-start.33) | collective-permute-done | bytes 458784 | tf_op jit(solution)/shard_map/ppermute | solution.py:296
  284.0 2.1 collective-permute-start.36
  286.1 2.3 collective-permute-start.37
  289.5 4.9 %collective-permute-done.36.refs_2_ = bf16[32,1792]{1,0:T(8,128)(2,1)S(1)} collective-permute-done((bf16[32,1792]{1,0:T(8,128)(2,1)S(1)}, bf16[32,1792]{1,0:T(8,128)(2,1)S(1)}, u32[]{:S(2)}, u32[]{:S(2)}) %collective-permute-start.36) | collective-permute-done | bytes 114720 | tf_op jit(solution)/shard_map/ppermute | solution.py:302
  294.5 1.9 shard_map.77
  (105 shorter events, 41.2 us)
Async XLA Ops:
  0.0 37.8 %copy-start = (bf16[3,224,2048]{2,1,0:T(8,128)(2,1)S(1)}, bf16[3,224,2048]{2,1,0:T(8,128)(2,1)}, u32[]{:S(2)}) copy-start(bf16[3,224,2048]{2,1,0:T(8,128)(2,1)} %own_ref.3) | copy-start | bytes 8257540
  3.0 33.4 %collective-permute-start.10 = (bf16[3,224,512]{2,1,0:T(8,128)(2,1)}, bf16[3,224,512]{2,1,0:T(8,128)(2,1)S(1)}, u32[]{:S(2)}, u32[]{:S(2)}) collective-permute-start(bf16[3,224,512]{2,1,0:T(8,128)(2,1)} %get-tuple-element.175), channel_id=1, source_target_pairs={{0,16},{4,20},{8,24},{12,28},{16,0},{20,4},{24,8},{28,12},{1,17},{... | collective-permute-start | bytes 2064392 | tf_op jit(solution)/shard_map/ppermute | solution.py:296
  6.0 30.4 %collective-permute-start.11 = (bf16[3,224,512]{2,1,0:T(8,128)(2,1)}, bf16[3,224,512]{2,1,0:T(8,128)(2,1)}, u32[]{:S(2)}, u32[]{:S(2)}) collective-permute-start(bf16[3,224,512]{2,1,0:T(8,128)(2,1)} %get-tuple-element.174), channel_id=1, source_target_pairs={{0,24},{4,28},{8,16},{12,20},{16,8},{20,12},{24,0},{28,4},{1,25},{... | collective-permute-start | bytes 2064392 | tf_op jit(solution)/shard_map/ppermute | solution.py:296
  7.4 30.3 %collective-permute-start.9 = (bf16[3,224,512]{2,1,0:T(8,128)(2,1)}, bf16[3,224,512]{2,1,0:T(8,128)(2,1)}, u32[]{:S(2)}, u32[]{:S(2)}) collective-permute-start(bf16[3,224,512]{2,1,0:T(8,128)(2,1)} %get-tuple-element.176), channel_id=1, source_target_pairs={{0,8},{4,12},{8,0},{12,4},{16,24},{20,28},{24,16},{28,20},{1,9},{5... | collective-permute-start | bytes 2064392 | tf_op jit(solution)/shard_map/ppermute | solution.py:296
  11.2 11.4 %collective-permute-start = (bf16[64,1792]{1,0:T(8,128)(2,1)S(1)}, bf16[64,1792]{1,0:T(8,128)(2,1)S(1)}, u32[]{:S(2)}, u32[]{:S(2)}) collective-permute-start(bf16[64,1792]{1,0:T(8,128)(2,1)S(1)} %get-tuple-element.89), channel_id=1, source_target_pairs={{0,1},{1,0},{2,3},{3,2},{4,5},{5,4},{6,7},{7,6},{8,9},{9,8},{10,11... | collective-permute-start | bytes 688136 | tf_op jit(solution)/shard_map/ppermute | solution.py:302
  13.2 12.9 %collective-permute-start.1 = (bf16[64,1792]{1,0:T(8,128)(2,1)}, bf16[64,1792]{1,0:T(8,128)(2,1)}, u32[]{:S(2)}, u32[]{:S(2)}) collective-permute-start(bf16[64,1792]{1,0:T(8,128)(2,1)} %get-tuple-element.90), channel_id=1, source_target_pairs={{0,2},{1,3},{2,0},{3,1},{4,6},{5,7},{6,4},{7,5},{8,10},{9,11},{10,... | collective-permute-start | bytes 688136 | tf_op jit(solution)/shard_map/ppermute | solution.py:302
  23.2 8.2 %collective-permute-start.2 = (bf16[64,1792]{1,0:T(8,128)(2,1)}, bf16[64,1792]{1,0:T(8,128)(2,1)}, u32[]{:S(2)}, u32[]{:S(2)}) collective-permute-start(bf16[64,1792]{1,0:T(8,128)(2,1)} %get-tuple-element.91), channel_id=1, source_target_pairs={{0,3},{1,2},{2,1},{3,0},{4,7},{5,6},{6,5},{7,4},{8,11},{9,10},{10,... | collective-permute-start | bytes 688136 | tf_op jit(solution)/shard_map/ppermute | solution.py:302
  39.9 36.2 %collective-permute-start.12 = (bf16[3,4,224,512]{3,2,1,0:T(8,128)(2,1)S(1)}, bf16[3,4,224,512]{3,2,1,0:T(8,128)(2,1)S(1)}, u32[]{:S(2)}, u32[]{:S(2)}) collective-permute-start(bf16[3,4,224,512]{3,2,1,0:T(8,128)(2,1)S(1)} %shard_map.66), channel_id=1, source_target_pairs={{0,4},{4,0},{8,12},{12,8},{16,20},{20,16},{24,28},{28,24},{1,5},{5... | collective-permute-start | bytes 8257544 | tf_op jit(solution)/shard_map/ppermute | solution.py:299
  40.0 14.1 %collective-permute-start.4 = (bf16[128,1920]{1,0:T(8,128)(2,1)S(1)}, bf16[128,1920]{1,0:T(8,128)(2,1)S(1)}, u32[]{:S(2)}, u32[]{:S(2)}) collective-permute-start(bf16[128,1920]{1,0:T(8,128)(2,1)S(1)} %get-tuple-element.120.refs_0_), channel_id=1, source_target_pairs={{0,16},{4,20},{8,24},{12,28},{16,0},{20,4},{24,8},{28,12},{1,17},{... | collective-permute-start | bytes 1474568 | tf_op jit(solution)/shard_map/ppermute | solution.py:296
  41.8 14.1 %collective-permute-start.6 = (bf16[128,1920]{1,0:T(8,128)(2,1)S(1)}, bf16[128,1920]{1,0:T(8,128)(2,1)S(1)}, u32[]{:S(2)}, u32[]{:S(2)}) collective-permute-start(bf16[128,1920]{1,0:T(8,128)(2,1)S(1)} %get-tuple-element.132.refs_0_), channel_id=1, source_target_pairs={{0,8},{4,12},{8,0},{12,4},{16,24},{20,28},{24,16},{28,20},{1,9},{5... | collective-permute-start | bytes 1474568 | tf_op jit(solution)/shard_map/ppermute | solution.py:296
  43.3 23.1 %collective-permute-start.3 = (bf16[128,1920]{1,0:T(8,128)(2,1)S(1)}, bf16[128,1920]{1,0:T(8,128)(2,1)S(1)}, u32[]{:S(2)}, u32[]{:S(2)}) collective-permute-start(bf16[128,1920]{1,0:T(8,128)(2,1)S(1)} %get-tuple-element.120.refs_0_), channel_id=1, source_target_pairs={{0,8},{4,12},{8,0},{12,4},{16,24},{20,28},{24,16},{28,20},{1,9},{5... | collective-permute-start | bytes 1474568 | tf_op jit(solution)/shard_map/ppermute | solution.py:296
  43.8 22.6 %collective-permute-start.7 = (bf16[128,1920]{1,0:T(8,128)(2,1)S(1)}, bf16[128,1920]{1,0:T(8,128)(2,1)S(1)}, u32[]{:S(2)}, u32[]{:S(2)}) collective-permute-start(bf16[128,1920]{1,0:T(8,128)(2,1)S(1)} %get-tuple-element.132.refs_0_), channel_id=1, source_target_pairs={{0,16},{4,20},{8,24},{12,28},{16,0},{20,4},{24,8},{28,12},{1,17},{... | collective-permute-start | bytes 1474568 | tf_op jit(solution)/shard_map/ppermute | solution.py:296
  54.1 22.1 %collective-permute-start.5 = (bf16[128,1920]{1,0:T(8,128)(2,1)S(1)}, bf16[128,1920]{1,0:T(8,128)(2,1)S(1)}, u32[]{:S(2)}, u32[]{:S(2)}) collective-permute-start(bf16[128,1920]{1,0:T(8,128)(2,1)S(1)} %collective-permute-done.4.refs_2_), channel_id=1, source_target_pairs={{0,8},{4,12},{8,0},{12,4},{16,24},{20,28},{24,16},{28,20},{1,9},{5... | collective-permute-start | bytes 1474568 | tf_op jit(solution)/shard_map/ppermute | solution.py:296
  55.9 20.3 %collective-permute-start.8 = (bf16[128,1920]{1,0:T(8,128)(2,1)S(1)}, bf16[128,1920]{1,0:T(8,128)(2,1)S(1)}, u32[]{:S(2)}, u32[]{:S(2)}) collective-permute-start(bf16[128,1920]{1,0:T(8,128)(2,1)S(1)} %collective-permute-done.6.refs_1_), channel_id=1, source_target_pairs={{0,16},{4,20},{8,24},{12,28},{16,0},{20,4},{24,8},{28,12},{1,17},{... | collective-permute-start | bytes 1474568 | tf_op jit(solution)/shard_map/ppermute | solution.py:296
  80.2 13.2 %collective-permute-start.13 = (bf16[2,128,1024]{2,1,0:T(8,128)(2,1)S(1)}, bf16[2,128,1024]{2,1,0:T(8,128)(2,1)S(1)}, u32[]{:S(2)}, u32[]{:S(2)}) collective-permute-start(bf16[2,128,1024]{2,1,0:T(8,128)(2,1)S(1)} %get-tuple-element.107), channel_id=1, source_target_pairs={{0,1},{1,0},{2,3},{3,2},{4,5},{5,4},{6,7},{7,6},{8,9},{9,8},{10,11... | collective-permute-start | bytes 1572872 | tf_op jit(solution)/shard_map/ppermute | solution.py:302
  93.5 17.9 %collective-permute-start.15 = (bf16[2,128,1024]{2,1,0:T(8,128)(2,1)S(1)}, bf16[2,128,1024]{2,1,0:T(8,128)(2,1)S(1)}, u32[]{:S(2)}, u32[]{:S(2)}) collective-permute-start(bf16[2,128,1024]{2,1,0:T(8,128)(2,1)S(1)} %get-tuple-element.118), channel_id=1, source_target_pairs={{0,1},{1,0},{2,3},{3,2},{4,5},{5,4},{6,7},{7,6},{8,9},{9,8},{10,11... | collective-permute-start | bytes 1572872 | tf_op jit(solution)/shard_map/ppermute | solution.py:302
  95.2 18.4 %collective-permute-start.17 = (bf16[3,224,512]{2,1,0:T(8,128)(2,1)S(1)}, bf16[3,224,512]{2,1,0:T(8,128)(2,1)S(1)}, u32[]{:S(2)}, u32[]{:S(2)}) collective-permute-start(bf16[3,224,512]{2,1,0:T(8,128)(2,1)S(1)} %get-tuple-element.124), channel_id=1, source_target_pairs={{0,8},{4,12},{8,0},{12,4},{16,24},{20,28},{24,16},{28,20},{1,9},{5... | collective-permute-start | bytes 2064392 | tf_op jit(solution)/shard_map/ppermute | solution.py:296
  96.7 29.9 %collective-permute-start.18 = (bf16[3,224,512]{2,1,0:T(8,128)(2,1)S(1)}, bf16[3,224,512]{2,1,0:T(8,128)(2,1)S(1)}, u32[]{:S(2)}, u32[]{:S(2)}) collective-permute-start(bf16[3,224,512]{2,1,0:T(8,128)(2,1)S(1)} %get-tuple-element.125), channel_id=1, source_target_pairs={{0,16},{4,20},{8,24},{12,28},{16,0},{20,4},{24,8},{28,12},{1,17},{... | collective-permute-start | bytes 2064392 | tf_op jit(solution)/shard_map/ppermute | solution.py:296
  97.3 29.3 %collective-permute-start.19 = (bf16[3,224,512]{2,1,0:T(8,128)(2,1)S(1)}, bf16[3,224,512]{2,1,0:T(8,128)(2,1)S(1)}, u32[]{:S(2)}, u32[]{:S(2)}) collective-permute-start(bf16[3,224,512]{2,1,0:T(8,128)(2,1)S(1)} %get-tuple-element.126), channel_id=1, source_target_pairs={{0,24},{4,28},{8,16},{12,20},{16,8},{20,12},{24,0},{28,4},{1,25},{... | collective-permute-start | bytes 2064392 | tf_op jit(solution)/shard_map/ppermute | solution.py:296
  98.7 12.9 %collective-permute-start.14 = (bf16[1,128,1024]{2,1,0:T(8,128)(2,1)S(1)}, bf16[1,128,1024]{2,1,0:T(8,128)(2,1)S(1)}, u32[]{:S(2)}, u32[]{:S(2)}) collective-permute-start(bf16[1,128,1024]{2,1,0:T(8,128)(2,1)S(1)} %add_convert_fusion.5), channel_id=1, source_target_pairs={{0,2},{1,3},{2,0},{3,1},{4,6},{5,7},{6,4},{7,5},{8,10},{9,11},{10,... | collective-permute-start | bytes 786440 | tf_op jit(solution)/shard_map/ppermute | solution.py:302
  127.7 15.2 %collective-permute-start.20 = (bf16[3,4,224,512]{3,2,1,0:T(8,128)(2,1)S(1)}, bf16[3,4,224,512]{3,2,1,0:T(8,128)(2,1)S(1)}, u32[]{:S(2)}, u32[]{:S(2)}) collective-permute-start(bf16[3,4,224,512]{3,2,1,0:T(8,128)(2,1)S(1)} %shard_map.69), channel_id=1, source_target_pairs={{0,4},{4,0},{8,12},{12,8},{16,20},{20,16},{24,28},{28,24},{1,5},{5... | collective-permute-start | bytes 8257544 | tf_op jit(solution)/shard_map/ppermute | solution.py:299
  127.8 15.1 %collective-permute-start.16 = (bf16[1,128,1024]{2,1,0:T(8,128)(2,1)S(1)}, bf16[1,128,1024]{2,1,0:T(8,128)(2,1)S(1)}, u32[]{:S(2)}, u32[]{:S(2)}) collective-permute-start(bf16[1,128,1024]{2,1,0:T(8,128)(2,1)S(1)} %add_convert_fusion.4), channel_id=1, source_target_pairs={{0,2},{1,3},{2,0},{3,1},{4,6},{5,7},{6,4},{7,5},{8,10},{9,11},{10,... | collective-permute-start | bytes 786440 | tf_op jit(solution)/shard_map/ppermute | solution.py:302
  147.0 14.0 %collective-permute-start.21 = (bf16[2,128,1024]{2,1,0:T(8,128)(2,1)S(1)}, bf16[2,128,1024]{2,1,0:T(8,128)(2,1)S(1)}, u32[]{:S(2)}, u32[]{:S(2)}) collective-permute-start(bf16[2,128,1024]{2,1,0:T(8,128)(2,1)S(1)} %get-tuple-element.131), channel_id=1, source_target_pairs={{0,1},{1,0},{2,3},{3,2},{4,5},{5,4},{6,7},{7,6},{8,9},{9,8},{10,11... | collective-permute-start | bytes 1572872 | tf_op jit(solution)/shard_map/ppermute | solution.py:302
  161.1 18.7 %collective-permute-start.23 = (bf16[2,128,1024]{2,1,0:T(8,128)(2,1)S(1)}, bf16[2,128,1024]{2,1,0:T(8,128)(2,1)S(1)}, u32[]{:S(2)}, u32[]{:S(2)}) collective-permute-start(bf16[2,128,1024]{2,1,0:T(8,128)(2,1)S(1)} %get-tuple-element.138), channel_id=1, source_target_pairs={{0,1},{1,0},{2,3},{3,2},{4,5},{5,4},{6,7},{7,6},{8,9},{9,8},{10,11... | collective-permute-start | bytes 1572872 | tf_op jit(solution)/shard_map/ppermute | solution.py:302
  161.7 32.9 %collective-permute-start.28 = (bf16[3,224,512]{2,1,0:T(8,128)(2,1)S(1)}, bf16[3,224,512]{2,1,0:T(8,128)(2,1)S(1)}, u32[]{:S(2)}, u32[]{:S(2)}) collective-permute-start(bf16[3,224,512]{2,1,0:T(8,128)(2,1)S(1)} %get-tuple-element.148), channel_id=1, source_target_pairs={{0,8},{4,12},{8,0},{12,4},{16,24},{20,28},{24,16},{28,20},{1,9},{5... | collective-permute-start | bytes 2064392 | tf_op jit(solution)/shard_map/ppermute | solution.py:296
  162.3 32.3 %collective-permute-start.29 = (bf16[3,224,512]{2,1,0:T(8,128)(2,1)S(1)}, bf16[3,224,512]{2,1,0:T(8,128)(2,1)S(1)}, u32[]{:S(2)}, u32[]{:S(2)}) collective-permute-start(bf16[3,224,512]{2,1,0:T(8,128)(2,1)S(1)} %get-tuple-element.149), channel_id=1, source_target_pairs={{0,16},{4,20},{8,24},{12,28},{16,0},{20,4},{24,8},{28,12},{1,17},{... | collective-permute-start | bytes 2064392 | tf_op jit(solution)/shard_map/ppermute | solution.py:296
  163.5 31.1 %collective-permute-start.30 = (bf16[3,224,512]{2,1,0:T(8,128)(2,1)S(1)}, bf16[3,224,512]{2,1,0:T(8,128)(2,1)S(1)}, u32[]{:S(2)}, u32[]{:S(2)}) collective-permute-start(bf16[3,224,512]{2,1,0:T(8,128)(2,1)S(1)} %get-tuple-element.150), channel_id=1, source_target_pairs={{0,24},{4,28},{8,16},{12,20},{16,8},{20,12},{24,0},{28,4},{1,25},{... | collective-permute-start | bytes 2064392 | tf_op jit(solution)/shard_map/ppermute | solution.py:296
  165.2 14.7 %collective-permute-start.22 = (bf16[1,128,1024]{2,1,0:T(8,128)(2,1)S(1)}, bf16[1,128,1024]{2,1,0:T(8,128)(2,1)S(1)}, u32[]{:S(2)}, u32[]{:S(2)}) collective-permute-start(bf16[1,128,1024]{2,1,0:T(8,128)(2,1)S(1)} %add_convert_fusion.3), channel_id=1, source_target_pairs={{0,2},{1,3},{2,0},{3,1},{4,6},{5,7},{6,4},{7,5},{8,10},{9,11},{10,... | collective-permute-start | bytes 786440 | tf_op jit(solution)/shard_map/ppermute | solution.py:302
  180.3 12.0 %collective-permute-start.24 = (bf16[128,1024]{1,0:T(8,128)(2,1)S(1)}, bf16[128,1024]{1,0:T(8,128)(2,1)S(1)}, u32[]{:S(2)}, u32[]{:S(2)}) collective-permute-start(bf16[128,1024]{1,0:T(8,128)(2,1)S(1)} %shard_map.72.refs_0_), channel_id=1, source_target_pairs={{0,1},{1,0},{2,3},{3,2},{4,5},{5,4},{6,7},{7,6},{8,9},{9,8},{10,11... | collective-permute-start | bytes 786440 | tf_op jit(solution)/shard_map/ppermute | solution.py:302
  181.2 12.9 %collective-permute-start.25 = (bf16[1,128,1024]{2,1,0:T(8,128)(2,1)S(1)}, bf16[1,128,1024]{2,1,0:T(8,128)(2,1)S(1)}, u32[]{:S(2)}, u32[]{:S(2)}) collective-permute-start(bf16[1,128,1024]{2,1,0:T(8,128)(2,1)S(1)} %add_convert_fusion.2), channel_id=1, source_target_pairs={{0,2},{1,3},{2,0},{3,1},{4,6},{5,7},{6,4},{7,5},{8,10},{9,11},{10,... | collective-permute-start | bytes 786440 | tf_op jit(solution)/shard_map/ppermute | solution.py:302
  195.7 30.0 %collective-permute-start.31 = (bf16[3,4,224,512]{3,2,1,0:T(8,128)(2,1)S(1)}, bf16[3,4,224,512]{3,2,1,0:T(8,128)(2,1)S(1)}, u32[]{:S(2)}, u32[]{:S(2)}) collective-permute-start(bf16[3,4,224,512]{3,2,1,0:T(8,128)(2,1)S(1)} %shard_map.74), channel_id=1, source_target_pairs={{0,4},{4,0},{8,12},{12,8},{16,20},{20,16},{24,28},{28,24},{1,5},{5... | collective-permute-start | bytes 8257544 | tf_op jit(solution)/shard_map/ppermute | solution.py:299
  195.8 15.0 %collective-permute-start.26 = (bf16[128,1024]{1,0:T(8,128)(2,1)S(1)}, bf16[128,1024]{1,0:T(8,128)(2,1)S(1)}, u32[]{:S(2)}, u32[]{:S(2)}) collective-permute-start(bf16[128,1024]{1,0:T(8,128)(2,1)S(1)} %shard_map.72.refs_0_), channel_id=1, source_target_pairs={{0,2},{1,3},{2,0},{3,1},{4,6},{5,7},{6,4},{7,5},{8,10},{9,11},{10,... | collective-permute-start | bytes 786440 | tf_op jit(solution)/shard_map/ppermute | solution.py:302
  210.8 13.8 %collective-permute-start.39 = (bf16[128,1024]{1,0:T(8,128)(2,1)S(1)}, bf16[128,1024]{1,0:T(8,128)(2,1)S(1)}, u32[]{:S(2)}, u32[]{:S(2)}) collective-permute-start(bf16[128,1024]{1,0:T(8,128)(2,1)S(1)} %shard_map.73.refs_0_), channel_id=1, source_target_pairs={{0,2},{1,3},{2,0},{3,1},{4,6},{5,7},{6,4},{7,5},{8,10},{9,11},{10,... | collective-permute-start | bytes 786440 | tf_op jit(solution)/shard_map/ppermute | solution.py:302
  210.8 14.9 %collective-permute-start.27 = (bf16[128,1024]{1,0:T(8,128)(2,1)S(1)}, bf16[128,1024]{1,0:T(8,128)(2,1)S(1)}, u32[]{:S(2)}, u32[]{:S(2)}) collective-permute-start(bf16[128,1024]{1,0:T(8,128)(2,1)S(1)} %collective-permute-done.26.refs_2_), channel_id=1, source_target_pairs={{0,1},{1,0},{2,3},{3,2},{4,5},{5,4},{6,7},{7,6},{8,9},{9,8},{10,11... | collective-permute-start | bytes 786440 | tf_op jit(solution)/shard_map/ppermute | solution.py:302
  213.0 18.4 %collective-permute-start.38 = (bf16[128,1024]{1,0:T(8,128)(2,1)S(1)}, bf16[128,1024]{1,0:T(8,128)(2,1)S(1)}, u32[]{:S(2)}, u32[]{:S(2)}) collective-permute-start(bf16[128,1024]{1,0:T(8,128)(2,1)S(1)} %shard_map.73.refs_0_), channel_id=1, source_target_pairs={{0,1},{1,0},{2,3},{3,2},{4,5},{5,4},{6,7},{7,6},{8,9},{9,8},{10,11... | collective-permute-start | bytes 786440 | tf_op jit(solution)/shard_map/ppermute | solution.py:302
  224.7 11.4 %collective-permute-start.40 = (bf16[128,1024]{1,0:T(8,128)(2,1)S(1)}, bf16[128,1024]{1,0:T(8,128)(2,1)S(1)}, u32[]{:S(2)}, u32[]{:S(2)}) collective-permute-start(bf16[128,1024]{1,0:T(8,128)(2,1)S(1)} %collective-permute-done.39.refs_2_), channel_id=1, source_target_pairs={{0,1},{1,0},{2,3},{3,2},{4,5},{5,4},{6,7},{7,6},{8,9},{9,8},{10,11... | collective-permute-start | bytes 786440 | tf_op jit(solution)/shard_map/ppermute | solution.py:302
  241.4 13.8 %collective-permute-start.41 = (bf16[128,1792]{1,0:T(8,128)(2,1)}, bf16[128,1792]{1,0:T(8,128)(2,1)}, u32[]{:S(2)}, u32[]{:S(2)}) collective-permute-start(bf16[128,1792]{1,0:T(8,128)(2,1)} %get-tuple-element.168), channel_id=1, source_target_pairs={{0,8},{4,12},{8,0},{12,4},{16,24},{20,28},{24,16},{28,20},{1,9},{5... | collective-permute-start | bytes 1376264 | tf_op jit(solution)/shard_map/ppermute | solution.py:296
  242.8 23.4 %collective-permute-start.42 = (bf16[128,1792]{1,0:T(8,128)(2,1)S(1)}, bf16[128,1792]{1,0:T(8,128)(2,1)}, u32[]{:S(2)}, u32[]{:S(2)}) collective-permute-start(bf16[128,1792]{1,0:T(8,128)(2,1)S(1)} %get-tuple-element.169), channel_id=1, source_target_pairs={{0,16},{4,20},{8,24},{12,28},{16,0},{20,4},{24,8},{28,12},{1,17},{... | collective-permute-start | bytes 1376264 | tf_op jit(solution)/shard_map/ppermute | solution.py:296
  243.6 22.6 %collective-permute-start.43 = (bf16[128,1792]{1,0:T(8,128)(2,1)S(1)}, bf16[128,1792]{1,0:T(8,128)(2,1)}, u32[]{:S(2)}, u32[]{:S(2)}) collective-permute-start(bf16[128,1792]{1,0:T(8,128)(2,1)S(1)} %get-tuple-element.170), channel_id=1, source_target_pairs={{0,24},{4,28},{8,16},{12,20},{16,8},{20,12},{24,0},{28,4},{1,25},{... | collective-permute-start | bytes 1376264 | tf_op jit(solution)/shard_map/ppermute | solution.py:296
  244.9 29.9 %collective-permute-start.32 = (bf16[128,1792]{1,0:T(8,128)(2,1)S(1)}, bf16[128,1792]{1,0:T(8,128)(2,1)S(1)}, u32[]{:S(2)}, u32[]{:S(2)}) collective-permute-start(bf16[128,1792]{1,0:T(8,128)(2,1)S(1)} %get-tuple-element.159), channel_id=1, source_target_pairs={{0,8},{4,12},{8,0},{12,4},{16,24},{20,28},{24,16},{28,20},{1,9},{5... | collective-permute-start | bytes 1376264 | tf_op jit(solution)/shard_map/ppermute | solution.py:296
  246.3 37.4 %collective-permute-start.33 = (bf16[128,1792]{1,0:T(8,128)(2,1)S(1)}, bf16[128,1792]{1,0:T(8,128)(2,1)S(1)}, u32[]{:S(2)}, u32[]{:S(2)}) collective-permute-start(bf16[128,1792]{1,0:T(8,128)(2,1)S(1)} %get-tuple-element.160), channel_id=1, source_target_pairs={{0,16},{4,20},{8,24},{12,28},{16,0},{20,4},{24,8},{28,12},{1,17},{... | collective-permute-start | bytes 1376264 | tf_op jit(solution)/shard_map/ppermute | solution.py:296
  255.2 28.4 %collective-permute-start.34 = (bf16[128,1792]{1,0:T(8,128)(2,1)S(1)}, bf16[128,1792]{1,0:T(8,128)(2,1)S(1)}, u32[]{:S(2)}, u32[]{:S(2)}) collective-permute-start(bf16[128,1792]{1,0:T(8,128)(2,1)S(1)} %get-tuple-element.161), channel_id=1, source_target_pairs={{0,24},{4,28},{8,16},{12,20},{16,8},{20,12},{24,0},{28,4},{1,25},{... | collective-permute-start | bytes 1376264 | tf_op jit(solution)/shard_map/ppermute | solution.py:296
  267.7 18.3 %collective-permute-start.44 = (bf16[32,1792]{1,0:T(8,128)(2,1)S(1)}, bf16[32,1792]{1,0:T(8,128)(2,1)S(1)}, u32[]{:S(2)}, u32[]{:S(2)}) collective-permute-start(bf16[32,1792]{1,0:T(8,128)(2,1)S(1)} %get-tuple-element.182), channel_id=1, source_target_pairs={{0,1},{1,0},{2,3},{3,2},{4,5},{5,4},{6,7},{7,6},{8,9},{9,8},{10,11... | collective-permute-start | bytes 344072 | tf_op jit(solution)/shard_map/ppermute | solution.py:302
  267.8 20.6 %collective-permute-start.45 = (bf16[32,1792]{1,0:T(8,128)(2,1)S(1)}, bf16[32,1792]{1,0:T(8,128)(2,1)S(1)}, u32[]{:S(2)}, u32[]{:S(2)}) collective-permute-start(bf16[32,1792]{1,0:T(8,128)(2,1)S(1)} %get-tuple-element.181), channel_id=1, source_target_pairs={{0,2},{1,3},{2,0},{3,1},{4,6},{5,7},{6,4},{7,5},{8,10},{9,11},{10,... | collective-permute-start | bytes 344072 | tf_op jit(solution)/shard_map/ppermute | solution.py:302
  274.8 13.6 %collective-permute-start.46 = (bf16[32,1792]{1,0:T(8,128)(2,1)S(1)}, bf16[32,1792]{1,0:T(8,128)(2,1)S(1)}, u32[]{:S(2)}, u32[]{:S(2)}) collective-permute-start(bf16[32,1792]{1,0:T(8,128)(2,1)S(1)} %get-tuple-element.180), channel_id=1, source_target_pairs={{0,3},{1,2},{2,1},{3,0},{4,7},{5,6},{6,5},{7,4},{8,11},{9,10},{10,... | collective-permute-start | bytes 344072 | tf_op jit(solution)/shard_map/ppermute | solution.py:302
  283.9 5.6 %collective-permute-start.35 = (bf16[32,1792]{1,0:T(8,128)(2,1)S(1)}, bf16[32,1792]{1,0:T(8,128)(2,1)S(1)}, u32[]{:S(2)}, u32[]{:S(2)}) collective-permute-start(bf16[32,1792]{1,0:T(8,128)(2,1)S(1)} %get-tuple-element.186), channel_id=1, source_target_pairs={{0,1},{1,0},{2,3},{3,2},{4,5},{5,4},{6,7},{7,6},{8,9},{9,8},{10,11... | collective-permute-start | bytes 344072 | tf_op jit(solution)/shard_map/ppermute | solution.py:302
  284.0 10.5 %collective-permute-start.36 = (bf16[32,1792]{1,0:T(8,128)(2,1)S(1)}, bf16[32,1792]{1,0:T(8,128)(2,1)S(1)}, u32[]{:S(2)}, u32[]{:S(2)}) collective-permute-start(bf16[32,1792]{1,0:T(8,128)(2,1)S(1)} %get-tuple-element.185), channel_id=1, source_target_pairs={{0,2},{1,3},{2,0},{3,1},{4,6},{5,7},{6,4},{7,5},{8,10},{9,11},{10,... | collective-permute-start | bytes 344072 | tf_op jit(solution)/shard_map/ppermute | solution.py:302
  286.1 8.4 %collective-permute-start.37 = (bf16[32,1792]{1,0:T(8,128)(2,1)S(1)}, bf16[32,1792]{1,0:T(8,128)(2,1)S(1)}, u32[]{:S(2)}, u32[]{:S(2)}) collective-permute-start(bf16[32,1792]{1,0:T(8,128)(2,1)S(1)} %get-tuple-element.184), channel_id=1, source_target_pairs={{0,3},{1,2},{2,1},{3,0},{4,7},{5,6},{6,5},{7,4},{8,11},{9,10},{10,... | collective-permute-start | bytes 344072 | tf_op jit(solution)/shard_map/ppermute | solution.py:302
  (9 other events, 90.1 us)

commit v10 on v9

--- a/solution.py
+++ b/solution.py
@@ -342,13 +342,14 @@
     cut = [cut[0]] + [to_level(cut[step], step) for step in range(1, n_tensor)]
     groups = group_tokens(place, routing, cut)
 
-    gate_joined = join_blocks(place, gate_weight, after(gate_same, groups))
-    gate_pair = core_exchange(gate_joined)
     bits = [1 << bit for bit in range(chips.bit_length() - 1)]
     toks = []
     for half in range(HALVES):
         turn = (half + 1) % len(bits)
         toks.append(copies(groups[half], to_chip, bits[turn:] + bits[:turn]))
+    near = [tok[bit] for tok in toks for bit in bits]
+    gate_joined = join_blocks(place, gate_weight, after(gate_same, near))
+    gate_pair = core_exchange(gate_joined)
     up_blocks = blocks_of(up_weight)
     toks = after(toks, up_blocks)
     up_same = chip_exchange(after(up_blocks, toks))
@@ -364,27 +365,26 @@
         return sums, routings
 
     gate_sums, routings = products(gate_pair, [], [])
-    up_joined = join_blocks(place, up_weight, after(up_same, gate_sums[-1][1][0]))
+    up_joined = join_blocks(place, up_weight, after(up_same, gate_sums[-1][1]))
     up_pair = core_exchange(up_joined)
     down_same = chip_exchange(after(blocks_of(down_weight), up_joined))
     up_sums, _ = products(up_pair, [], gate_sums[-1][1])
 
-    hiddens, near, far = [], [], up_sums[-1][1][-1]
+    hiddens, near, far = [], [], ()
     bits = [1 << bit for bit in range(n_tensor.bit_length() - 1)]
     for half in range(HALVES):
         up_terms = after(up_sums[half][0], [up_sums[-1][1][0], near])
         hidden = hidden_rows(routings[half], gate_sums[half][0], up_terms, slots)
         hiddens.append(copies(hidden, to_level, bits[::-1], far))
-        near, far = hiddens[-1][1], hiddens[-1][n_tensor // 2]
-    down_joined = join_blocks(place, down_weight, after(down_same, [h[0] for h in hiddens]))
+        near, far = hiddens[-1][1], [hiddens[0][n_tensor // 2]]
+    down_joined = join_blocks(place, down_weight, after(down_same, [hiddens[-1][0], far[0]]))
     down_pair = core_exchange(down_joined)
-    backs, parts = [], []
+    backs, parts, got = [], [], []
     for half in range(HALVES):
-        hids = after(hiddens[half], parts)
+        hids = after(hiddens[half], parts or hiddens[-1][1])
         parts = down_sums(place, routings[half], hids, down_pair, slots)
-        total = parts[0].astype(jnp.float32)
-        for step in range(1, chips):
-            total = total + to_chip(parts[step], step).astype(jnp.float32)
+        got = [to_chip(part, step) for step, part in enumerate(after(parts, got)) if step]
+        total = sum(part.astype(jnp.float32) for part in [parts[0], *got])
         total = total.astype(jnp.bfloat16).reshape(n_tensor, rows // HALVES, -1)
         for other in range(n_tensor):
             piece = lax.dynamic_index_in_dim(total, level ^ other, 0, keepdims=False)

time: 297 us -> 280 us (0.943)
  waiting for transfers between devices: 190 us -> 166 us
  local copies, waits for them, and re-layouts: 8.36 us -> 12.7 us
    ppermute x23, waiting for transfers between devices: 114 us -> 98.4 us  [to_level(): lax.ppermute(value, 'tensor', [(s, s ^ step) for s in range(n_tensor)])]
    ppermute x21, waiting for transfers between devices: 75.8 us -> 62.3 us  [to_chip(): return lax.ppermute(value, 'expert', pairs)]
    ppermute x3, waiting for transfers between devices: 0.01 us -> 5.09 us  [to_core(): return lax.ppermute(value, 'expert', [(s, s ^ 1) for s in range(n_expert)])]
    unnamed x20 -> x32, local copies, waits for them, and re-layouts: 4.47 us -> 8.81 us
  transfers between devices with their start and end apart: 47 -> 47, of which waited for: 28 -> 26; matrix products, arithmetic and copies ran while one was open for 1% -> 1% of each run, Pallas kernels for 6% -> 8%
where the time goes in v10:
time: 280 us
  waiting for transfers between devices  166 us (59%)
  starting transfers between devices  61.8 us (22%)
  Pallas kernels  37 us (13%)
  local copies, waits for them, and re-layouts  12.7 us (5%)
    ppermute x23, waiting for transfers between devices, to_level(): lax.ppermute(value, 'tensor', [(s, s ^ step) for s in range(n_tensor)])  98.4 us
    ppermute x21, waiting for transfers between devices, to_chip(): return lax.ppermute(value, 'expert', pairs)  62.3 us
    ppermute x23, starting transfers between devices, to_level(): lax.ppermute(value, 'tensor', [(s, s ^ step) for s in range(n_tensor)])  34 us
    ppermute x21, starting transfers between devices, to_chip(): return lax.ppermute(value, 'expert', pairs)  27.5 us
    pallas_call x4, Pallas kernels, picked_sums(): pl.pallas_call(functools.partial(pick_kernel, chips), in_specs=[SMEM_SPEC...  16.3 us
    pallas_call x2, Pallas kernels, down_sums(): pl.pallas_call(functools.partial(down_kernel, slots, levels), in_specs=[S...  10.8 us
    unnamed x32, local copies, waits for them, and re-layouts  8.81 us
  transfers between devices with their start and end apart: 47, of which 26 were waited for; matrix products, arithmetic and copies ran while one was open for 1% of the time, Pallas kernels for 8%

profile of v10, /device:TPU:0, one launch (start us, length us, event | category | flops | bytes accessed | tf_op | source)
XLA Modules:
  0.0 279.7 jit_solution(12480208625352493544)
XLA Ops:
  0.0 3.0 %constant_dynamic-slice_fusion.3 = (bf16[3,224,512]{2,1,0:T(8,128)(2,1)}, bf16[3,224,512]{2,1,0:T(8,128)(2,1)}, bf16[3,224,512]{2,1,0:T(8,128)(2,1)}) fusion(bf16[3,224,2048]{2,1,0:T(8,128)(2,1)} %own_ref.3, s32[]{:T(128)S(6)} %select_n.47, s32[]{:T(128)S(6)} %select_n.46, s32[]{:T(128)S(6)} %select_n.45), kind=kLoop, calls=%fused_computation.17 | loop fusion | bytes 4128780 | tf_op jit(solution)/shard_map/dynamic_slice | solution.py:327
  3.0 3.0 %collective-permute-start.10 = (bf16[3,224,512]{2,1,0:T(8,128)(2,1)}, bf16[3,224,512]{2,1,0:T(8,128)(2,1)S(1)}, u32[]{:S(2)}, u32[]{:S(2)}) collective-permute-start(bf16[3,224,512]{2,1,0:T(8,128)(2,1)} %get-tuple-element.188), channel_id=1, source_target_pairs={{0,16},{4,20},{8,24},{12,28},{16,0},{20,4},{24,8},{28,12},{1,17},{... | collective-permute-start | bytes 2064392 | tf_op jit(solution)/shard_map/ppermute | solution.py:296
  8.7 1.7 shard_map.64
  12.7 2.6 collective-permute-start.1
  15.5 6.1 %collective-permute-done.refs_1_ = bf16[64,1792]{1,0:T(8,128)(2,1)S(1)} collective-permute-done((bf16[64,1792]{1,0:T(8,128)(2,1)S(1)}, bf16[64,1792]{1,0:T(8,128)(2,1)S(1)}, u32[]{:S(2)}, u32[]{:S(2)}) %collective-permute-start) | collective-permute-done | bytes 229408 | tf_op jit(solution)/shard_map/ppermute | solution.py:302
  22.8 9.5 %collective-permute-done.1.refs_2_ = bf16[64,1792]{1,0:T(8,128)(2,1)} collective-permute-done((bf16[64,1792]{1,0:T(8,128)(2,1)}, bf16[64,1792]{1,0:T(8,128)(2,1)}, u32[]{:S(2)}, u32[]{:S(2)}) %collective-permute-start.1) | collective-permute-done | bytes 229408 | tf_op jit(solution)/shard_map/ppermute | solution.py:302
  37.4 1.9 collective-permute-start.6
  40.8 8.7 %collective-permute-done.4.refs_2_ = bf16[128,1920]{1,0:T(8,128)(2,1)S(1)} collective-permute-done((bf16[128,1920]{1,0:T(8,128)(2,1)S(1)}, bf16[128,1920]{1,0:T(8,128)(2,1)S(1)}, u32[]{:S(2)}, u32[]{:S(2)}) %collective-permute-start.4) | collective-permute-done | bytes 491552 | tf_op jit(solution)/shard_map/ppermute | solution.py:296
  49.5 9.2 %collective-permute-done.6.refs_1_ = bf16[128,1920]{1,0:T(8,128)(2,1)S(1)} collective-permute-done((bf16[128,1920]{1,0:T(8,128)(2,1)S(1)}, bf16[128,1920]{1,0:T(8,128)(2,1)S(1)}, u32[]{:S(2)}, u32[]{:S(2)}) %collective-permute-start.6) | collective-permute-done | bytes 491552 | tf_op jit(solution)/shard_map/ppermute | solution.py:296
  58.7 2.0 shard_map.66
  60.8 1.8 collective-permute-start.5
  64.4 10.1 %collective-permute-done.5.refs_3_ = bf16[128,1920]{1,0:T(8,128)(2,1)S(1)} collective-permute-done((bf16[128,1920]{1,0:T(8,128)(2,1)S(1)}, bf16[128,1920]{1,0:T(8,128)(2,1)S(1)}, u32[]{:S(2)}, u32[]{:S(2)}) %collective-permute-start.5) | collective-permute-done | bytes 491552 | tf_op jit(solution)/shard_map/ppermute | solution.py:296
  75.9 4.1 %shard_map.67 = (bf16[2,128,1024]{2,1,0:T(8,128)(2,1)S(1)}, bf16[2,128,1024]{2,1,0:T(8,128)(2,1)S(1)}, bf16[4,128,128]{2,1,0:T(8,128)(2,1)S(1)}) custom-call(s32[3]{0:T(128)S(1)} %pad_add_fusion.place_ref, bf16[128,1920]{1,0:T(8,128)(2,1)S(1)} %get-tuple-element.128.refs_0_, bf16[128,1920]{1,0:T(8,128)(2,1)S(1)} %collective-permute-done.3.refs_1_, ...), custom_call_target="tpu_custom_call" | custom-call | flops 2818572288 | bytes 8388608 | tf_op jit(solution)/shard_map/pallas_call | solution.py:195
  80.0 2.0 collective-permute-start.13
  82.0 4.1 %shard_map.68 = (bf16[2,128,1024]{2,1,0:T(8,128)(2,1)S(1)}, bf16[2,128,1024]{2,1,0:T(8,128)(2,1)S(1)}, bf16[4,128,128]{2,1,0:T(8,128)(2,1)S(1)}) custom-call(s32[3]{0:T(128)S(1)} %pad_add_fusion.place_ref, bf16[128,1920]{1,0:T(8,128)(2,1)S(1)} %get-tuple-element.140.refs_0_, bf16[128,1920]{1,0:T(8,128)(2,1)S(1)} %collective-permute-done.6.refs_1_, ...), custom_call_target="tpu_custom_call" | custom-call | flops 2818572288 | bytes 8388608 | tf_op jit(solution)/shard_map/pallas_call | solution.py:195
  86.1 7.4 %collective-permute-done.13 = bf16[2,128,1024]{2,1,0:T(8,128)(2,1)S(1)} collective-permute-done((bf16[2,128,1024]{2,1,0:T(8,128)(2,1)S(1)}, bf16[2,128,1024]{2,1,0:T(8,128)(2,1)S(1)}, u32[]{:S(2)}, u32[]{:S(2)}) %collective-permute-start.13) | collective-permute-done | bytes 524320 | tf_op jit(solution)/shard_map/ppermute | solution.py:302
  93.6 1.8 collective-permute-start.15
  98.9 2.1 collective-permute-start.14
  101.0 10.8 %collective-permute-done.15 = bf16[2,128,1024]{2,1,0:T(8,128)(2,1)S(1)} collective-permute-done((bf16[2,128,1024]{2,1,0:T(8,128)(2,1)S(1)}, bf16[2,128,1024]{2,1,0:T(8,128)(2,1)S(1)}, u32[]{:S(2)}, u32[]{:S(2)}) %collective-permute-start.15) | collective-permute-done | bytes 524320 | tf_op jit(solution)/shard_map/ppermute | solution.py:302
  111.9 2.3 collective-permute-start.16
  114.2 12.5 %collective-permute-done.18.refs_1_ = bf16[3,224,512]{2,1,0:T(8,128)(2,1)S(1)} collective-permute-done((bf16[3,224,512]{2,1,0:T(8,128)(2,1)S(1)}, bf16[3,224,512]{2,1,0:T(8,128)(2,1)S(1)}, u32[]{:S(2)}, u32[]{:S(2)}) %collective-permute-start.18) | collective-permute-done | bytes 688160 | tf_op jit(solution)/shard_map/ppermute | solution.py:296
  127.9 5.1 %collective-permute-done.20 = bf16[3,4,224,512]{3,2,1,0:T(8,128)(2,1)S(1)} collective-permute-done((bf16[3,4,224,512]{3,2,1,0:T(8,128)(2,1)S(1)}, bf16[3,4,224,512]{3,2,1,0:T(8,128)(2,1)S(1)}, u32[]{:S(2)}, u32[]{:S(2)}) %collective-permute-start.20) | collective-permute-done | bytes 2752544 | tf_op jit(solution)/shard_map/ppermute | solution.py:299
  133.0 4.1 %shard_map.70 = (bf16[2,128,1024]{2,1,0:T(8,128)(2,1)S(1)}, bf16[2,128,1024]{2,1,0:T(8,128)(2,1)S(1)}, bf16[4,128,128]{2,1,0:T(8,128)(2,1)}) custom-call(s32[3]{0:T(128)S(1)} %pad_add_fusion.place_ref, bf16[128,1920]{1,0:T(8,128)(2,1)S(1)} %get-tuple-element.128.refs_0_, bf16[128,1920]{1,0:T(8,128)(2,1)S(1)} %collective-permute-done.3.refs_1_, ...), custom_call_target="tpu_custom_call" | custom-call | flops 2818572288 | bytes 8388608 | tf_op jit(solution)/shard_map/pallas_call | solution.py:195
  137.8 4.1 %shard_map.71 = (bf16[2,128,1024]{2,1,0:T(8,128)(2,1)S(1)}, bf16[2,128,1024]{2,1,0:T(8,128)(2,1)S(1)}, bf16[4,128,128]{2,1,0:T(8,128)(2,1)}) custom-call(s32[3]{0:T(128)S(1)} %pad_add_fusion.place_ref, bf16[128,1920]{1,0:T(8,128)(2,1)S(1)} %get-tuple-element.140.refs_0_, bf16[128,1920]{1,0:T(8,128)(2,1)S(1)} %collective-permute-done.6.refs_1_, ...), custom_call_target="tpu_custom_call" | custom-call | flops 2818572288 | bytes 8388608 | tf_op jit(solution)/shard_map/pallas_call | solution.py:195
  141.8 9.3 %collective-permute-done.21 = bf16[2,128,1024]{2,1,0:T(8,128)(2,1)S(1)} collective-permute-done((bf16[2,128,1024]{2,1,0:T(8,128)(2,1)S(1)}, bf16[2,128,1024]{2,1,0:T(8,128)(2,1)S(1)}, u32[]{:S(2)}, u32[]{:S(2)}) %collective-permute-start.21) | collective-permute-done | bytes 524320 | tf_op jit(solution)/shard_map/ppermute | solution.py:302
  151.9 2.6 collective-permute-start.22
  156.6 1.8 collective-permute-start.31
  158.4 11.7 %collective-permute-done.23 = bf16[2,128,1024]{2,1,0:T(8,128)(2,1)S(1)} collective-permute-done((bf16[2,128,1024]{2,1,0:T(8,128)(2,1)S(1)}, bf16[2,128,1024]{2,1,0:T(8,128)(2,1)S(1)}, u32[]{:S(2)}, u32[]{:S(2)}) %collective-permute-start.23) | collective-permute-done | bytes 524320 | tf_op jit(solution)/shard_map/ppermute | solution.py:302
  170.6 1.9 collective-permute-start.24
  173.8 8.0 %collective-permute-done.24.refs_1_ = bf16[128,1024]{1,0:T(8,128)(2,1)S(1)} collective-permute-done((bf16[128,1024]{1,0:T(8,128)(2,1)S(1)}, bf16[128,1024]{1,0:T(8,128)(2,1)S(1)}, u32[]{:S(2)}, u32[]{:S(2)}) %collective-permute-start.24) | collective-permute-done | bytes 262176 | tf_op jit(solution)/shard_map/ppermute | solution.py:302
  181.9 1.8 collective-permute-start.25
  183.8 8.5 %collective-permute-done.27.refs_5_ = bf16[1,128,1024]{2,1,0:T(8,128)(2,1)S(1)} collective-permute-done((bf16[1,128,1024]{2,1,0:T(8,128)(2,1)S(1)}, bf16[1,128,1024]{2,1,0:T(8,128)(2,1)S(1)}, u32[]{:S(2)}, u32[]{:S(2)}) %collective-permute-start.27) | collective-permute-done | bytes 262176 | tf_op jit(solution)/shard_map/ppermute | solution.py:302
  192.7 3.9 %collective-permute-done.25.refs_2_ = bf16[128,1024]{1,0:T(8,128)(2,1)S(1)} collective-permute-done((bf16[128,1024]{1,0:T(8,128)(2,1)S(1)}, bf16[128,1024]{1,0:T(8,128)(2,1)S(1)}, u32[]{:S(2)}, u32[]{:S(2)}) %collective-permute-start.25) | collective-permute-done | bytes 262176 | tf_op jit(solution)/shard_map/ppermute | solution.py:302
  197.9 2.1 collective-permute-start.28
  200.1 12.1 %collective-permute-done.39.refs_2_ = bf16[128,1024]{1,0:T(8,128)(2,1)} collective-permute-done((bf16[128,1024]{1,0:T(8,128)(2,1)S(1)}, bf16[128,1024]{1,0:T(8,128)(2,1)}, u32[]{:S(2)}, u32[]{:S(2)}) %collective-permute-start.39) | collective-permute-done | bytes 262176 | tf_op jit(solution)/shard_map/ppermute | solution.py:302
  213.5 4.9 %collective-permute-done.26.refs_3_ = bf16[128,1024]{1,0:T(8,128)(2,1)S(1)} collective-permute-done((bf16[128,1024]{1,0:T(8,128)(2,1)S(1)}, bf16[128,1024]{1,0:T(8,128)(2,1)S(1)}, u32[]{:S(2)}, u32[]{:S(2)}) %collective-permute-start.26) | collective-permute-done | bytes 262176 | tf_op jit(solution)/shard_map/ppermute | solution.py:302
  218.4 5.7 %shard_map.75 = (bf16[128,1792]{1,0:T(8,128)(2,1)S(1)}, bf16[128,1792]{1,0:T(8,128)(2,1)}, bf16[128,1792]{1,0:T(8,128)(2,1)}, bf16[128,1792]{1,0:T(8,128)(2,1)}) custom-call(s32[3]{0:T(128)S(1)} %pad_add_fusion.place_ref, bf16[4,128,128]{2,1,0:T(8,128)(2,1)S(1)} %get-tuple-element.113.routing_ref, bf16[128,1024]{1,0:T(8,128)(2,1)S(1)} %shard_map.72.refs_0_, ...), custom_call_target="tpu_custom_call" | custom-call | flops 2818572288 | bytes 8388608 | tf_op jit(solution)/shard_map/pallas_call | solution.py:265
  228.5 1.8 copy-done.11
  231.2 5.1 %shard_map.76 = (bf16[128,1792]{1,0:T(8,128)(2,1)S(1)}, bf16[128,1792]{1,0:T(8,128)(2,1)S(1)}, bf16[128,1792]{1,0:T(8,128)(2,1)S(1)}, bf16[128,1792]{1,0:T(8,128)(2,1)S(1)}) custom-call(s32[3]{0:T(128)S(1)} %pad_add_fusion.place_ref, bf16[4,128,128]{2,1,0:T(8,128)(2,1)S(1)} %copy-done.9, bf16[128,1024]{1,0:T(8,128)(2,1)S(1)} %shard_map.73.refs_0_, ...), custom_call_target="tpu_custom_call" | custom-call | flops 2818572288 | bytes 8388608 | tf_op jit(solution)/shard_map/pallas_call | solution.py:265
  237.9 7.3 %collective-permute-done.34 = bf16[128,1792]{1,0:T(8,128)(2,1)} collective-permute-done((bf16[128,1792]{1,0:T(8,128)(2,1)}, bf16[128,1792]{1,0:T(8,128)(2,1)}, u32[]{:S(2)}, u32[]{:S(2)}) %collective-permute-start.34) | collective-permute-done | bytes 458784 | tf_op jit(solution)/shard_map/ppermute | solution.py:296
  251.9 2.5 collective-permute-start.37
  254.4 5.2 %collective-permute-done.41 = bf16[128,1792]{1,0:T(8,128)(2,1)S(1)} collective-permute-done((bf16[128,1792]{1,0:T(8,128)(2,1)S(1)}, bf16[128,1792]{1,0:T(8,128)(2,1)S(1)}, u32[]{:S(2)}, u32[]{:S(2)}) %collective-permute-start.41) | collective-permute-done | bytes 458784 | tf_op jit(solution)/shard_map/ppermute | solution.py:296
  259.6 2.5 collective-permute-start.38
  262.2 5.2 %collective-permute-done.42 = bf16[128,1792]{1,0:T(8,128)(2,1)S(1)} collective-permute-done((bf16[128,1792]{1,0:T(8,128)(2,1)S(1)}, bf16[128,1792]{1,0:T(8,128)(2,1)S(1)}, u32[]{:S(2)}, u32[]{:S(2)}) %collective-permute-start.42) | collective-permute-done | bytes 458784 | tf_op jit(solution)/shard_map/ppermute | solution.py:296
  269.0 2.2 collective-permute-start.45
  272.2 2.1 collective-permute-done.44.refs_5_
  274.2 2.2 collective-permute-done.45.refs_6_
  277.8 1.9 shard_map.77
  (117 shorter events, 47.3 us)
Async XLA Ops:
  3.0 34.4 %collective-permute-start.10 = (bf16[3,224,512]{2,1,0:T(8,128)(2,1)}, bf16[3,224,512]{2,1,0:T(8,128)(2,1)S(1)}, u32[]{:S(2)}, u32[]{:S(2)}) collective-permute-start(bf16[3,224,512]{2,1,0:T(8,128)(2,1)} %get-tuple-element.188), channel_id=1, source_target_pairs={{0,16},{4,20},{8,24},{12,28},{16,0},{20,4},{24,8},{28,12},{1,17},{... | collective-permute-start | bytes 2064392 | tf_op jit(solution)/shard_map/ppermute | solution.py:296
  6.0 33.3 %collective-permute-start.11 = (bf16[3,224,512]{2,1,0:T(8,128)(2,1)}, bf16[3,224,512]{2,1,0:T(8,128)(2,1)}, u32[]{:S(2)}, u32[]{:S(2)}) collective-permute-start(bf16[3,224,512]{2,1,0:T(8,128)(2,1)} %get-tuple-element.187), channel_id=1, source_target_pairs={{0,24},{4,28},{8,16},{12,20},{16,8},{20,12},{24,0},{28,4},{1,25},{... | collective-permute-start | bytes 2064392 | tf_op jit(solution)/shard_map/ppermute | solution.py:296
  11.1 10.5 %collective-permute-start = (bf16[64,1792]{1,0:T(8,128)(2,1)S(1)}, bf16[64,1792]{1,0:T(8,128)(2,1)S(1)}, u32[]{:S(2)}, u32[]{:S(2)}) collective-permute-start(bf16[64,1792]{1,0:T(8,128)(2,1)S(1)} %get-tuple-element.97), channel_id=1, source_target_pairs={{0,1},{1,0},{2,3},{3,2},{4,5},{5,4},{6,7},{7,6},{8,9},{9,8},{10,11... | collective-permute-start | bytes 688136 | tf_op jit(solution)/shard_map/ppermute | solution.py:302
  12.7 19.6 %collective-permute-start.1 = (bf16[64,1792]{1,0:T(8,128)(2,1)}, bf16[64,1792]{1,0:T(8,128)(2,1)}, u32[]{:S(2)}, u32[]{:S(2)}) collective-permute-start(bf16[64,1792]{1,0:T(8,128)(2,1)} %get-tuple-element.98), channel_id=1, source_target_pairs={{0,2},{1,3},{2,0},{3,1},{4,6},{5,7},{6,4},{7,5},{8,10},{9,11},{10,... | collective-permute-start | bytes 688136 | tf_op jit(solution)/shard_map/ppermute | solution.py:302
  15.3 17.0 %collective-permute-start.2 = (bf16[64,1792]{1,0:T(8,128)(2,1)}, bf16[64,1792]{1,0:T(8,128)(2,1)}, u32[]{:S(2)}, u32[]{:S(2)}) collective-permute-start(bf16[64,1792]{1,0:T(8,128)(2,1)} %get-tuple-element.99), channel_id=1, source_target_pairs={{0,3},{1,2},{2,1},{3,0},{4,7},{5,6},{6,5},{7,4},{8,11},{9,10},{10,... | collective-permute-start | bytes 688136 | tf_op jit(solution)/shard_map/ppermute | solution.py:302
  22.2 18.5 %collective-permute-start.9 = (bf16[3,224,512]{2,1,0:T(8,128)(2,1)}, bf16[3,224,512]{2,1,0:T(8,128)(2,1)}, u32[]{:S(2)}, u32[]{:S(2)}) collective-permute-start(bf16[3,224,512]{2,1,0:T(8,128)(2,1)} %get-tuple-element.189), channel_id=1, source_target_pairs={{0,8},{4,12},{8,0},{12,4},{16,24},{20,28},{24,16},{28,20},{1,9},{5... | collective-permute-start | bytes 2064392 | tf_op jit(solution)/shard_map/ppermute | solution.py:296
  35.3 14.2 %collective-permute-start.4 = (bf16[128,1920]{1,0:T(8,128)(2,1)S(1)}, bf16[128,1920]{1,0:T(8,128)(2,1)S(1)}, u32[]{:S(2)}, u32[]{:S(2)}) collective-permute-start(bf16[128,1920]{1,0:T(8,128)(2,1)S(1)} %get-tuple-element.128.refs_0_), channel_id=1, source_target_pairs={{0,16},{4,20},{8,24},{12,28},{16,0},{20,4},{24,8},{28,12},{1,17},{... | collective-permute-start | bytes 1474568 | tf_op jit(solution)/shard_map/ppermute | solution.py:296
  36.9 21.9 %collective-permute-start.3 = (bf16[128,1920]{1,0:T(8,128)(2,1)S(1)}, bf16[128,1920]{1,0:T(8,128)(2,1)S(1)}, u32[]{:S(2)}, u32[]{:S(2)}) collective-permute-start(bf16[128,1920]{1,0:T(8,128)(2,1)S(1)} %get-tuple-element.128.refs_0_), channel_id=1, source_target_pairs={{0,8},{4,12},{8,0},{12,4},{16,24},{20,28},{24,16},{28,20},{1,9},{5... | collective-permute-start | bytes 1474568 | tf_op jit(solution)/shard_map/ppermute | solution.py:296
  37.4 21.3 %collective-permute-start.6 = (bf16[128,1920]{1,0:T(8,128)(2,1)S(1)}, bf16[128,1920]{1,0:T(8,128)(2,1)S(1)}, u32[]{:S(2)}, u32[]{:S(2)}) collective-permute-start(bf16[128,1920]{1,0:T(8,128)(2,1)S(1)} %get-tuple-element.140.refs_0_), channel_id=1, source_target_pairs={{0,8},{4,12},{8,0},{12,4},{16,24},{20,28},{24,16},{28,20},{1,9},{5... | collective-permute-start | bytes 1474568 | tf_op jit(solution)/shard_map/ppermute | solution.py:296
  39.3 19.5 %collective-permute-start.7 = (bf16[128,1920]{1,0:T(8,128)(2,1)S(1)}, bf16[128,1920]{1,0:T(8,128)(2,1)S(1)}, u32[]{:S(2)}, u32[]{:S(2)}) collective-permute-start(bf16[128,1920]{1,0:T(8,128)(2,1)S(1)} %get-tuple-element.140.refs_0_), channel_id=1, source_target_pairs={{0,16},{4,20},{8,24},{12,28},{16,0},{20,4},{24,8},{28,12},{1,17},{... | collective-permute-start | bytes 1474568 | tf_op jit(solution)/shard_map/ppermute | solution.py:296
  60.8 15.1 %collective-permute-start.12 = (bf16[3,4,224,512]{3,2,1,0:T(8,128)(2,1)S(1)}, bf16[3,4,224,512]{3,2,1,0:T(8,128)(2,1)S(1)}, u32[]{:S(2)}, u32[]{:S(2)}) collective-permute-start(bf16[3,4,224,512]{3,2,1,0:T(8,128)(2,1)S(1)} %shard_map.66), channel_id=1, source_target_pairs={{0,4},{4,0},{8,12},{12,8},{16,20},{20,16},{24,28},{28,24},{1,5},{5... | collective-permute-start | bytes 8257544 | tf_op jit(solution)/shard_map/ppermute | solution.py:299
  60.8 13.6 %collective-permute-start.5 = (bf16[128,1920]{1,0:T(8,128)(2,1)S(1)}, bf16[128,1920]{1,0:T(8,128)(2,1)S(1)}, u32[]{:S(2)}, u32[]{:S(2)}) collective-permute-start(bf16[128,1920]{1,0:T(8,128)(2,1)S(1)} %collective-permute-done.4.refs_2_), channel_id=1, source_target_pairs={{0,8},{4,12},{8,0},{12,4},{16,24},{20,28},{24,16},{28,20},{1,9},{5... | collective-permute-start | bytes 1474568 | tf_op jit(solution)/shard_map/ppermute | solution.py:296
  62.6 13.3 %collective-permute-start.8 = (bf16[128,1920]{1,0:T(8,128)(2,1)S(1)}, bf16[128,1920]{1,0:T(8,128)(2,1)S(1)}, u32[]{:S(2)}, u32[]{:S(2)}) collective-permute-start(bf16[128,1920]{1,0:T(8,128)(2,1)S(1)} %collective-permute-done.6.refs_1_), channel_id=1, source_target_pairs={{0,16},{4,20},{8,24},{12,28},{16,0},{20,4},{24,8},{28,12},{1,17},{... | collective-permute-start | bytes 1474568 | tf_op jit(solution)/shard_map/ppermute | solution.py:296
  80.0 13.5 %collective-permute-start.13 = (bf16[2,128,1024]{2,1,0:T(8,128)(2,1)S(1)}, bf16[2,128,1024]{2,1,0:T(8,128)(2,1)S(1)}, u32[]{:S(2)}, u32[]{:S(2)}) collective-permute-start(bf16[2,128,1024]{2,1,0:T(8,128)(2,1)S(1)} %get-tuple-element.115), channel_id=1, source_target_pairs={{0,1},{1,0},{2,3},{3,2},{4,5},{5,4},{6,7},{7,6},{8,9},{9,8},{10,11... | collective-permute-start | bytes 1572872 | tf_op jit(solution)/shard_map/ppermute | solution.py:302
  86.1 106.2 %copy-start.8 = (bf16[4,128,128]{2,1,0:T(8,128)(2,1)}, bf16[4,128,128]{2,1,0:T(8,128)(2,1)S(1)}, u32[]{:S(2)}) copy-start(bf16[4,128,128]{2,1,0:T(8,128)(2,1)S(1)} %get-tuple-element.151.routing_ref) | copy-start | bytes 393220
  93.6 18.2 %collective-permute-start.15 = (bf16[2,128,1024]{2,1,0:T(8,128)(2,1)S(1)}, bf16[2,128,1024]{2,1,0:T(8,128)(2,1)S(1)}, u32[]{:S(2)}, u32[]{:S(2)}) collective-permute-start(bf16[2,128,1024]{2,1,0:T(8,128)(2,1)S(1)} %get-tuple-element.126), channel_id=1, source_target_pairs={{0,1},{1,0},{2,3},{3,2},{4,5},{5,4},{6,7},{7,6},{8,9},{9,8},{10,11... | collective-permute-start | bytes 1572872 | tf_op jit(solution)/shard_map/ppermute | solution.py:302
  95.4 18.8 %collective-permute-start.17 = (bf16[3,224,512]{2,1,0:T(8,128)(2,1)S(1)}, bf16[3,224,512]{2,1,0:T(8,128)(2,1)S(1)}, u32[]{:S(2)}, u32[]{:S(2)}) collective-permute-start(bf16[3,224,512]{2,1,0:T(8,128)(2,1)S(1)} %get-tuple-element.132), channel_id=1, source_target_pairs={{0,8},{4,12},{8,0},{12,4},{16,24},{20,28},{24,16},{28,20},{1,9},{5... | collective-permute-start | bytes 2064392 | tf_op jit(solution)/shard_map/ppermute | solution.py:296
  96.8 29.9 %collective-permute-start.18 = (bf16[3,224,512]{2,1,0:T(8,128)(2,1)S(1)}, bf16[3,224,512]{2,1,0:T(8,128)(2,1)S(1)}, u32[]{:S(2)}, u32[]{:S(2)}) collective-permute-start(bf16[3,224,512]{2,1,0:T(8,128)(2,1)S(1)} %get-tuple-element.133), channel_id=1, source_target_pairs={{0,16},{4,20},{8,24},{12,28},{16,0},{20,4},{24,8},{28,12},{1,17},{... | collective-permute-start | bytes 2064392 | tf_op jit(solution)/shard_map/ppermute | solution.py:296
  97.3 29.4 %collective-permute-start.19 = (bf16[3,224,512]{2,1,0:T(8,128)(2,1)S(1)}, bf16[3,224,512]{2,1,0:T(8,128)(2,1)S(1)}, u32[]{:S(2)}, u32[]{:S(2)}) collective-permute-start(bf16[3,224,512]{2,1,0:T(8,128)(2,1)S(1)} %get-tuple-element.134), channel_id=1, source_target_pairs={{0,24},{4,28},{8,16},{12,20},{16,8},{20,12},{24,0},{28,4},{1,25},{... | collective-permute-start | bytes 2064392 | tf_op jit(solution)/shard_map/ppermute | solution.py:296
  98.9 13.0 %collective-permute-start.14 = (bf16[1,128,1024]{2,1,0:T(8,128)(2,1)S(1)}, bf16[1,128,1024]{2,1,0:T(8,128)(2,1)S(1)}, u32[]{:S(2)}, u32[]{:S(2)}) collective-permute-start(bf16[1,128,1024]{2,1,0:T(8,128)(2,1)S(1)} %add_convert_fusion.5), channel_id=1, source_target_pairs={{0,2},{1,3},{2,0},{3,1},{4,6},{5,7},{6,4},{7,5},{8,10},{9,11},{10,... | collective-permute-start | bytes 786440 | tf_op jit(solution)/shard_map/ppermute | solution.py:302
  111.9 14.9 %collective-permute-start.16 = (bf16[1,128,1024]{2,1,0:T(8,128)(2,1)S(1)}, bf16[1,128,1024]{2,1,0:T(8,128)(2,1)S(1)}, u32[]{:S(2)}, u32[]{:S(2)}) collective-permute-start(bf16[1,128,1024]{2,1,0:T(8,128)(2,1)S(1)} %add_convert_fusion.4), channel_id=1, source_target_pairs={{0,2},{1,3},{2,0},{3,1},{4,6},{5,7},{6,4},{7,5},{8,10},{9,11},{10,... | collective-permute-start | bytes 786440 | tf_op jit(solution)/shard_map/ppermute | solution.py:302
  127.9 5.2 %collective-permute-start.20 = (bf16[3,4,224,512]{3,2,1,0:T(8,128)(2,1)S(1)}, bf16[3,4,224,512]{3,2,1,0:T(8,128)(2,1)S(1)}, u32[]{:S(2)}, u32[]{:S(2)}) collective-permute-start(bf16[3,4,224,512]{3,2,1,0:T(8,128)(2,1)S(1)} %shard_map.69), channel_id=1, source_target_pairs={{0,4},{4,0},{8,12},{12,8},{16,20},{20,16},{24,28},{28,24},{1,5},{5... | collective-permute-start | bytes 8257544 | tf_op jit(solution)/shard_map/ppermute | solution.py:299
  137.1 14.0 %collective-permute-start.21 = (bf16[2,128,1024]{2,1,0:T(8,128)(2,1)S(1)}, bf16[2,128,1024]{2,1,0:T(8,128)(2,1)S(1)}, u32[]{:S(2)}, u32[]{:S(2)}) collective-permute-start(bf16[2,128,1024]{2,1,0:T(8,128)(2,1)S(1)} %get-tuple-element.139), channel_id=1, source_target_pairs={{0,1},{1,0},{2,3},{3,2},{4,5},{5,4},{6,7},{7,6},{8,9},{9,8},{10,11... | collective-permute-start | bytes 1572872 | tf_op jit(solution)/shard_map/ppermute | solution.py:302
  151.2 18.8 %collective-permute-start.23 = (bf16[2,128,1024]{2,1,0:T(8,128)(2,1)S(1)}, bf16[2,128,1024]{2,1,0:T(8,128)(2,1)S(1)}, u32[]{:S(2)}, u32[]{:S(2)}) collective-permute-start(bf16[2,128,1024]{2,1,0:T(8,128)(2,1)S(1)} %get-tuple-element.146), channel_id=1, source_target_pairs={{0,1},{1,0},{2,3},{3,2},{4,5},{5,4},{6,7},{7,6},{8,9},{9,8},{10,11... | collective-permute-start | bytes 1572872 | tf_op jit(solution)/shard_map/ppermute | solution.py:302
  151.9 18.2 %collective-permute-start.22 = (bf16[1,128,1024]{2,1,0:T(8,128)(2,1)S(1)}, bf16[1,128,1024]{2,1,0:T(8,128)(2,1)S(1)}, u32[]{:S(2)}, u32[]{:S(2)}) collective-permute-start(bf16[1,128,1024]{2,1,0:T(8,128)(2,1)S(1)} %add_convert_fusion.3), channel_id=1, source_target_pairs={{0,2},{1,3},{2,0},{3,1},{4,6},{5,7},{6,4},{7,5},{8,10},{9,11},{10,... | collective-permute-start | bytes 786440 | tf_op jit(solution)/shard_map/ppermute | solution.py:302
  154.8 37.9 %collective-permute-start.29 = (bf16[3,224,512]{2,1,0:T(8,128)(2,1)S(1)}, bf16[3,224,512]{2,1,0:T(8,128)(2,1)S(1)}, u32[]{:S(2)}, u32[]{:S(2)}) collective-permute-start(bf16[3,224,512]{2,1,0:T(8,128)(2,1)S(1)} %get-tuple-element.159), channel_id=1, source_target_pairs={{0,8},{4,12},{8,0},{12,4},{16,24},{20,28},{24,16},{28,20},{1,9},{5... | collective-permute-start | bytes 2064392 | tf_op jit(solution)/shard_map/ppermute | solution.py:296
  155.5 37.2 %collective-permute-start.30 = (bf16[3,224,512]{2,1,0:T(8,128)(2,1)S(1)}, bf16[3,224,512]{2,1,0:T(8,128)(2,1)S(1)}, u32[]{:S(2)}, u32[]{:S(2)}) collective-permute-start(bf16[3,224,512]{2,1,0:T(8,128)(2,1)S(1)} %get-tuple-element.160), channel_id=1, source_target_pairs={{0,16},{4,20},{8,24},{12,28},{16,0},{20,4},{24,8},{28,12},{1,17},{... | collective-permute-start | bytes 2064392 | tf_op jit(solution)/shard_map/ppermute | solution.py:296
  156.6 36.2 %collective-permute-start.31 = (bf16[3,224,512]{2,1,0:T(8,128)(2,1)S(1)}, bf16[3,224,512]{2,1,0:T(8,128)(2,1)S(1)}, u32[]{:S(2)}, u32[]{:S(2)}) collective-permute-start(bf16[3,224,512]{2,1,0:T(8,128)(2,1)S(1)} %get-tuple-element.161), channel_id=1, source_target_pairs={{0,24},{4,28},{8,16},{12,20},{16,8},{20,12},{24,0},{28,4},{1,25},{... | collective-permute-start | bytes 2064392 | tf_op jit(solution)/shard_map/ppermute | solution.py:296
  170.6 11.3 %collective-permute-start.24 = (bf16[128,1024]{1,0:T(8,128)(2,1)S(1)}, bf16[128,1024]{1,0:T(8,128)(2,1)S(1)}, u32[]{:S(2)}, u32[]{:S(2)}) collective-permute-start(bf16[128,1024]{1,0:T(8,128)(2,1)S(1)} %shard_map.72.refs_0_), channel_id=1, source_target_pairs={{0,1},{1,0},{2,3},{3,2},{4,5},{5,4},{6,7},{7,6},{8,9},{9,8},{10,11... | collective-permute-start | bytes 786440 | tf_op jit(solution)/shard_map/ppermute | solution.py:302
  172.5 19.8 %collective-permute-start.27 = (bf16[1,128,1024]{2,1,0:T(8,128)(2,1)S(1)}, bf16[1,128,1024]{2,1,0:T(8,128)(2,1)S(1)}, u32[]{:S(2)}, u32[]{:S(2)}) collective-permute-start(bf16[1,128,1024]{2,1,0:T(8,128)(2,1)S(1)} %add_convert_fusion.2), channel_id=1, source_target_pairs={{0,2},{1,3},{2,0},{3,1},{4,6},{5,7},{6,4},{7,5},{8,10},{9,11},{10,... | collective-permute-start | bytes 786440 | tf_op jit(solution)/shard_map/ppermute | solution.py:302
  181.9 14.7 %collective-permute-start.25 = (bf16[128,1024]{1,0:T(8,128)(2,1)S(1)}, bf16[128,1024]{1,0:T(8,128)(2,1)S(1)}, u32[]{:S(2)}, u32[]{:S(2)}) collective-permute-start(bf16[128,1024]{1,0:T(8,128)(2,1)S(1)} %shard_map.72.refs_0_), channel_id=1, source_target_pairs={{0,2},{1,3},{2,0},{3,1},{4,6},{5,7},{6,4},{7,5},{8,10},{9,11},{10,... | collective-permute-start | bytes 786440 | tf_op jit(solution)/shard_map/ppermute | solution.py:302
  197.8 20.6 %collective-permute-start.32 = (bf16[3,4,224,512]{3,2,1,0:T(8,128)(2,1)S(1)}, bf16[3,4,224,512]{3,2,1,0:T(8,128)(2,1)S(1)}, u32[]{:S(2)}, u32[]{:S(2)}) collective-permute-start(bf16[3,4,224,512]{3,2,1,0:T(8,128)(2,1)S(1)} %shard_map.74), channel_id=1, source_target_pairs={{0,4},{4,0},{8,12},{12,8},{16,20},{20,16},{24,28},{28,24},{1,5},{5... | collective-permute-start | bytes 8257544 | tf_op jit(solution)/shard_map/ppermute | solution.py:299
  197.9 14.3 %collective-permute-start.39 = (bf16[128,1024]{1,0:T(8,128)(2,1)S(1)}, bf16[128,1024]{1,0:T(8,128)(2,1)}, u32[]{:S(2)}, u32[]{:S(2)}) collective-permute-start(bf16[128,1024]{1,0:T(8,128)(2,1)S(1)} %shard_map.73.refs_0_), channel_id=1, source_target_pairs={{0,2},{1,3},{2,0},{3,1},{4,6},{5,7},{6,4},{7,5},{8,10},{9,11},{10,... | collective-permute-start | bytes 786440 | tf_op jit(solution)/shard_map/ppermute | solution.py:302
  197.9 14.8 %collective-permute-start.28 = (bf16[128,1024]{1,0:T(8,128)(2,1)S(1)}, bf16[128,1024]{1,0:T(8,128)(2,1)S(1)}, u32[]{:S(2)}, u32[]{:S(2)}) collective-permute-start(bf16[128,1024]{1,0:T(8,128)(2,1)S(1)} %shard_map.73.refs_0_), channel_id=1, source_target_pairs={{0,1},{1,0},{2,3},{3,2},{4,5},{5,4},{6,7},{7,6},{8,9},{9,8},{10,11... | collective-permute-start | bytes 786440 | tf_op jit(solution)/shard_map/ppermute | solution.py:302
  200.1 18.3 %collective-permute-start.26 = (bf16[128,1024]{1,0:T(8,128)(2,1)S(1)}, bf16[128,1024]{1,0:T(8,128)(2,1)S(1)}, u32[]{:S(2)}, u32[]{:S(2)}) collective-permute-start(bf16[128,1024]{1,0:T(8,128)(2,1)S(1)} %collective-permute-done.25.refs_2_), channel_id=1, source_target_pairs={{0,1},{1,0},{2,3},{3,2},{4,5},{5,4},{6,7},{7,6},{8,9},{9,8},{10,11... | collective-permute-start | bytes 786440 | tf_op jit(solution)/shard_map/ppermute | solution.py:302
  212.2 15.4 %collective-permute-start.40 = (bf16[128,1024]{1,0:T(8,128)(2,1)}, bf16[128,1024]{1,0:T(8,128)(2,1)}, u32[]{:S(2)}, u32[]{:S(2)}) collective-permute-start(bf16[128,1024]{1,0:T(8,128)(2,1)} %collective-permute-done.39.refs_2_), channel_id=1, source_target_pairs={{0,1},{1,0},{2,3},{3,2},{4,5},{5,4},{6,7},{7,6},{8,9},{9,8},{10,11... | collective-permute-start | bytes 786440 | tf_op jit(solution)/shard_map/ppermute | solution.py:302
  224.1 13.8 %collective-permute-start.33 = (bf16[128,1792]{1,0:T(8,128)(2,1)}, bf16[128,1792]{1,0:T(8,128)(2,1)}, u32[]{:S(2)}, u32[]{:S(2)}) collective-permute-start(bf16[128,1792]{1,0:T(8,128)(2,1)} %get-tuple-element.169), channel_id=1, source_target_pairs={{0,8},{4,12},{8,0},{12,4},{16,24},{20,28},{24,16},{28,20},{1,9},{5... | collective-permute-start | bytes 1376264 | tf_op jit(solution)/shard_map/ppermute | solution.py:296
  224.9 20.3 %collective-permute-start.34 = (bf16[128,1792]{1,0:T(8,128)(2,1)}, bf16[128,1792]{1,0:T(8,128)(2,1)}, u32[]{:S(2)}, u32[]{:S(2)}) collective-permute-start(bf16[128,1792]{1,0:T(8,128)(2,1)} %get-tuple-element.170), channel_id=1, source_target_pairs={{0,16},{4,20},{8,24},{12,28},{16,0},{20,4},{24,8},{28,12},{1,17},{... | collective-permute-start | bytes 1376264 | tf_op jit(solution)/shard_map/ppermute | solution.py:296
  226.3 19.8 %collective-permute-start.35 = (bf16[128,1792]{1,0:T(8,128)(2,1)}, bf16[128,1792]{1,0:T(8,128)(2,1)}, u32[]{:S(2)}, u32[]{:S(2)}) collective-permute-start(bf16[128,1792]{1,0:T(8,128)(2,1)} %get-tuple-element.171), channel_id=1, source_target_pairs={{0,24},{4,28},{8,16},{12,20},{16,8},{20,12},{24,0},{28,4},{1,25},{... | collective-permute-start | bytes 1376264 | tf_op jit(solution)/shard_map/ppermute | solution.py:296
  246.2 13.5 %collective-permute-start.41 = (bf16[128,1792]{1,0:T(8,128)(2,1)S(1)}, bf16[128,1792]{1,0:T(8,128)(2,1)S(1)}, u32[]{:S(2)}, u32[]{:S(2)}) collective-permute-start(bf16[128,1792]{1,0:T(8,128)(2,1)S(1)} %get-tuple-element.181), channel_id=1, source_target_pairs={{0,8},{4,12},{8,0},{12,4},{16,24},{20,28},{24,16},{28,20},{1,9},{5... | collective-permute-start | bytes 1376264 | tf_op jit(solution)/shard_map/ppermute | solution.py:296
  247.4 20.0 %collective-permute-start.42 = (bf16[128,1792]{1,0:T(8,128)(2,1)S(1)}, bf16[128,1792]{1,0:T(8,128)(2,1)S(1)}, u32[]{:S(2)}, u32[]{:S(2)}) collective-permute-start(bf16[128,1792]{1,0:T(8,128)(2,1)S(1)} %get-tuple-element.182), channel_id=1, source_target_pairs={{0,16},{4,20},{8,24},{12,28},{16,0},{20,4},{24,8},{28,12},{1,17},{... | collective-permute-start | bytes 1376264 | tf_op jit(solution)/shard_map/ppermute | solution.py:296
  248.5 18.9 %collective-permute-start.43 = (bf16[128,1792]{1,0:T(8,128)(2,1)S(1)}, bf16[128,1792]{1,0:T(8,128)(2,1)S(1)}, u32[]{:S(2)}, u32[]{:S(2)}) collective-permute-start(bf16[128,1792]{1,0:T(8,128)(2,1)S(1)} %get-tuple-element.183), channel_id=1, source_target_pairs={{0,24},{4,28},{8,16},{12,20},{16,8},{20,12},{24,0},{28,4},{1,25},{... | collective-permute-start | bytes 1376264 | tf_op jit(solution)/shard_map/ppermute | solution.py:296
  251.3 19.9 %collective-permute-start.36 = (bf16[32,1792]{1,0:T(8,128)(2,1)S(1)}, bf16[32,1792]{1,0:T(8,128)(2,1)S(1)}, u32[]{:S(2)}, u32[]{:S(2)}) collective-permute-start(bf16[32,1792]{1,0:T(8,128)(2,1)S(1)} %get-tuple-element.199), channel_id=1, source_target_pairs={{0,1},{1,0},{2,3},{3,2},{4,5},{5,4},{6,7},{7,6},{8,9},{9,8},{10,11... | collective-permute-start | bytes 344072 | tf_op jit(solution)/shard_map/ppermute | solution.py:302
  251.9 20.2 %collective-permute-start.37 = (bf16[32,1792]{1,0:T(8,128)(2,1)S(1)}, bf16[32,1792]{1,0:T(8,128)(2,1)S(1)}, u32[]{:S(2)}, u32[]{:S(2)}) collective-permute-start(bf16[32,1792]{1,0:T(8,128)(2,1)S(1)} %get-tuple-element.198), channel_id=1, source_target_pairs={{0,2},{1,3},{2,0},{3,1},{4,6},{5,7},{6,4},{7,5},{8,10},{9,11},{10,... | collective-permute-start | bytes 344072 | tf_op jit(solution)/shard_map/ppermute | solution.py:302
  259.6 12.5 %collective-permute-start.38 = (bf16[32,1792]{1,0:T(8,128)(2,1)S(1)}, bf16[32,1792]{1,0:T(8,128)(2,1)S(1)}, u32[]{:S(2)}, u32[]{:S(2)}) collective-permute-start(bf16[32,1792]{1,0:T(8,128)(2,1)S(1)} %get-tuple-element.197), channel_id=1, source_target_pairs={{0,3},{1,2},{2,1},{3,0},{4,7},{5,6},{6,5},{7,4},{8,11},{9,10},{10,... | collective-permute-start | bytes 344072 | tf_op jit(solution)/shard_map/ppermute | solution.py:302
  267.7 6.5 %collective-permute-start.44 = (bf16[32,1792]{1,0:T(8,128)(2,1)S(1)}, bf16[32,1792]{1,0:T(8,128)(2,1)S(1)}, u32[]{:S(2)}, u32[]{:S(2)}) collective-permute-start(bf16[32,1792]{1,0:T(8,128)(2,1)S(1)} %get-tuple-element.195), channel_id=1, source_target_pairs={{0,1},{1,0},{2,3},{3,2},{4,5},{5,4},{6,7},{7,6},{8,9},{9,8},{10,11... | collective-permute-start | bytes 344072 | tf_op jit(solution)/shard_map/ppermute | solution.py:302
  269.0 7.4 %collective-permute-start.45 = (bf16[32,1792]{1,0:T(8,128)(2,1)S(1)}, bf16[32,1792]{1,0:T(8,128)(2,1)S(1)}, u32[]{:S(2)}, u32[]{:S(2)}) collective-permute-start(bf16[32,1792]{1,0:T(8,128)(2,1)S(1)} %get-tuple-element.194), channel_id=1, source_target_pairs={{0,2},{1,3},{2,0},{3,1},{4,6},{5,7},{6,4},{7,5},{8,10},{9,11},{10,... | collective-permute-start | bytes 344072 | tf_op jit(solution)/shard_map/ppermute | solution.py:302
  271.1 6.7 %collective-permute-start.46 = (bf16[32,1792]{1,0:T(8,128)(2,1)S(1)}, bf16[32,1792]{1,0:T(8,128)(2,1)S(1)}, u32[]{:S(2)}, u32[]{:S(2)}) collective-permute-start(bf16[32,1792]{1,0:T(8,128)(2,1)S(1)} %get-tuple-element.193), channel_id=1, source_target_pairs={{0,3},{1,2},{2,1},{3,0},{4,7},{5,6},{6,5},{7,4},{8,11},{9,10},{10,... | collective-permute-start | bytes 344072 | tf_op jit(solution)/shard_map/ppermute | solution.py:302
  (15 other events, 161.8 us)

commit v11 on v10

--- a/solution.py
+++ b/solution.py
@@ -301,12 +301,11 @@
     def to_level(value, step):
         return lax.ppermute(value, "tensor", [(s, s ^ step) for s in range(n_tensor)])
 
-    def copies(value, send, bits, behind=()):
-        held = {0: value}
+    def copies(held, send, bits):
+        held = dict(held)
         for bit in bits:
             for step in sorted(held):
-                held[step + bit] = send(after(held[step], behind), bit)
-            behind = ()
+                held[step + bit] = send(held[step], bit)
         return [held[step] for step in range(len(held))]
 
     def level_sums(keep, send, behind):
@@ -346,7 +345,7 @@
     toks = []
     for half in range(HALVES):
         turn = (half + 1) % len(bits)
-        toks.append(copies(groups[half], to_chip, bits[turn:] + bits[:turn]))
+        toks.append(copies({0: groups[half]}, to_chip, bits[turn:] + bits[:turn]))
     near = [tok[bit] for tok in toks for bit in bits]
     gate_joined = join_blocks(place, gate_weight, after(gate_same, near))
     gate_pair = core_exchange(gate_joined)
@@ -370,19 +369,22 @@
     down_same = chip_exchange(after(blocks_of(down_weight), up_joined))
     up_sums, _ = products(up_pair, [], gate_sums[-1][1])
 
-    hiddens, near, far = [], [], ()
-    bits = [1 << bit for bit in range(n_tensor.bit_length() - 1)]
+    held, first = [], [up_sums[-1][1][0]]
+    bits = [n_tensor >> bit for bit in range(1, n_tensor.bit_length())]
     for half in range(HALVES):
-        up_terms = after(up_sums[half][0], [up_sums[-1][1][0], near])
+        up_terms = after(up_sums[half][0], first)
         hidden = hidden_rows(routings[half], gate_sums[half][0], up_terms, slots)
-        hiddens.append(copies(hidden, to_level, bits[::-1], far))
-        near, far = hiddens[-1][1], [hiddens[0][n_tensor // 2]]
-    down_joined = join_blocks(place, down_weight, after(down_same, [hiddens[-1][0], far[0]]))
+        held.append({0: hidden, bits[0]: to_level(after(hidden, first[1:]), bits[0])})
+        if half == 0:
+            blocks = copies(held[0], to_level, bits[1:])
+            first = [first[0], blocks[1]]
+    down_joined = join_blocks(place, down_weight, after(down_same, [hidden, blocks[bits[0]]]))
     down_pair = core_exchange(down_joined)
-    backs, parts, got = [], [], []
+    backs, got = [], []
     for half in range(HALVES):
-        hids = after(hiddens[half], parts or hiddens[-1][1])
-        parts = down_sums(place, routings[half], hids, down_pair, slots)
+        if half:
+            blocks = copies(after(held[half], parts), to_level, bits[1:])
+        parts = down_sums(place, routings[half], blocks, down_pair, slots)
         got = [to_chip(part, step) for step, part in enumerate(after(parts, got)) if step]
         total = sum(part.astype(jnp.float32) for part in [parts[0], *got])
         total = total.astype(jnp.bfloat16).reshape(n_tensor, rows // HALVES, -1)

time: 280 us -> 275 us (0.982)
  waiting for transfers between devices: 166 us -> 160 us
    ppermute x21, waiting for transfers between devices: 62.3 us -> 55.5 us  [to_chip(): return lax.ppermute(value, 'expert', pairs)]
    unnamed x32 -> x28, local copies, waits for them, and re-layouts: 8.81 us -> 7.17 us
  transfers between devices with their start and end apart: 47 -> 47, of which waited for: 26 -> 23; matrix products, arithmetic and copies ran while one was open for 1% -> 1% of each run, Pallas kernels for 8% -> 8%
where the time goes in v11:
time: 275 us; the launch traced here: 274 us
  waiting for transfers between devices  160 us (58%)
  starting transfers between devices  63.2 us (23%)
  Pallas kernels  37.1 us (13%)
  local copies, waits for them, and re-layouts  11.1 us (4%)
    ppermute x23, waiting for transfers between devices, to_level(): lax.ppermute(value, 'tensor', [(s, s ^ step) for s in range(n_tensor)])  99.8 us
    ppermute x21, waiting for transfers between devices, to_chip(): return lax.ppermute(value, 'expert', pairs)  55.5 us
    ppermute x23, starting transfers between devices, to_level(): lax.ppermute(value, 'tensor', [(s, s ^ step) for s in range(n_tensor)])  35.5 us
    ppermute x21, starting transfers between devices, to_chip(): return lax.ppermute(value, 'expert', pairs)  27.5 us
    pallas_call x4, Pallas kernels, picked_sums(): pl.pallas_call(functools.partial(pick_kernel, chips), in_specs=[SMEM_SPEC...  16.3 us
    pallas_call x2, Pallas kernels, down_sums(): pl.pallas_call(functools.partial(down_kernel, slots, levels), in_specs=[S...  10.9 us
    unnamed x28, local copies, waits for them, and re-layouts  7.17 us
  transfers between devices with their start and end apart: 47, of which 23 were waited for; matrix products, arithmetic and copies ran while one was open for 1% of the time, Pallas kernels for 8%

profile of v11, /device:TPU:0, one launch (start us, length us, event | category | flops | bytes accessed | tf_op | source)
XLA Modules:
  0.0 274.3 jit_solution(14929725855187052966)
XLA Ops:
  0.0 3.0 %constant_dynamic-slice_fusion.3 = (bf16[3,224,512]{2,1,0:T(8,128)(2,1)}, bf16[3,224,512]{2,1,0:T(8,128)(2,1)}, bf16[3,224,512]{2,1,0:T(8,128)(2,1)}) fusion(bf16[3,224,2048]{2,1,0:T(8,128)(2,1)} %own_ref.3, s32[]{:T(128)S(6)} %select_n.47, s32[]{:T(128)S(6)} %select_n.46, s32[]{:T(128)S(6)} %select_n.45), kind=kLoop, calls=%fused_computation.17 | loop fusion | bytes 4128780 | tf_op jit(solution)/shard_map/dynamic_slice | solution.py:326
  3.0 3.0 %collective-permute-start.10 = (bf16[3,224,512]{2,1,0:T(8,128)(2,1)}, bf16[3,224,512]{2,1,0:T(8,128)(2,1)S(1)}, u32[]{:S(2)}, u32[]{:S(2)}) collective-permute-start(bf16[3,224,512]{2,1,0:T(8,128)(2,1)} %get-tuple-element.176), channel_id=1, source_target_pairs={{0,16},{4,20},{8,24},{12,28},{16,0},{20,4},{24,8},{28,12},{1,17},{... | collective-permute-start | bytes 2064392 | tf_op jit(solution)/shard_map/ppermute | solution.py:296
  12.7 2.6 collective-permute-start.1
  15.5 6.1 %collective-permute-done.refs_1_ = bf16[64,1792]{1,0:T(8,128)(2,1)S(1)} collective-permute-done((bf16[64,1792]{1,0:T(8,128)(2,1)S(1)}, bf16[64,1792]{1,0:T(8,128)(2,1)S(1)}, u32[]{:S(2)}, u32[]{:S(2)}) %collective-permute-start) | collective-permute-done | bytes 229408 | tf_op jit(solution)/shard_map/ppermute | solution.py:302
  22.8 9.5 %collective-permute-done.1.refs_2_ = bf16[64,1792]{1,0:T(8,128)(2,1)} collective-permute-done((bf16[64,1792]{1,0:T(8,128)(2,1)}, bf16[64,1792]{1,0:T(8,128)(2,1)}, u32[]{:S(2)}, u32[]{:S(2)}) %collective-permute-start.1) | collective-permute-done | bytes 229408 | tf_op jit(solution)/shard_map/ppermute | solution.py:302
  37.4 1.8 collective-permute-start.6
  40.8 8.7 %collective-permute-done.4.refs_2_ = bf16[128,1920]{1,0:T(8,128)(2,1)S(1)} collective-permute-done((bf16[128,1920]{1,0:T(8,128)(2,1)S(1)}, bf16[128,1920]{1,0:T(8,128)(2,1)S(1)}, u32[]{:S(2)}, u32[]{:S(2)}) %collective-permute-start.4) | collective-permute-done | bytes 491552 | tf_op jit(solution)/shard_map/ppermute | solution.py:296
  49.5 9.2 %collective-permute-done.6.refs_1_ = bf16[128,1920]{1,0:T(8,128)(2,1)S(1)} collective-permute-done((bf16[128,1920]{1,0:T(8,128)(2,1)S(1)}, bf16[128,1920]{1,0:T(8,128)(2,1)S(1)}, u32[]{:S(2)}, u32[]{:S(2)}) %collective-permute-start.6) | collective-permute-done | bytes 491552 | tf_op jit(solution)/shard_map/ppermute | solution.py:296
  58.8 2.0 shard_map.66
  60.9 1.7 collective-permute-start.5
  64.3 10.2 %collective-permute-done.5.refs_3_ = bf16[128,1920]{1,0:T(8,128)(2,1)S(1)} collective-permute-done((bf16[128,1920]{1,0:T(8,128)(2,1)S(1)}, bf16[128,1920]{1,0:T(8,128)(2,1)S(1)}, u32[]{:S(2)}, u32[]{:S(2)}) %collective-permute-start.5) | collective-permute-done | bytes 491552 | tf_op jit(solution)/shard_map/ppermute | solution.py:296
  75.9 4.1 %shard_map.67 = (bf16[2,128,1024]{2,1,0:T(8,128)(2,1)S(1)}, bf16[2,128,1024]{2,1,0:T(8,128)(2,1)S(1)}, bf16[4,128,128]{2,1,0:T(8,128)(2,1)S(1)}) custom-call(s32[3]{0:T(128)S(1)} %pad_add_fusion.place_ref, bf16[128,1920]{1,0:T(8,128)(2,1)S(1)} %get-tuple-element.122.refs_0_, bf16[128,1920]{1,0:T(8,128)(2,1)S(1)} %collective-permute-done.3.refs_1_, ...), custom_call_target="tpu_custom_call" | custom-call | flops 2818572288 | bytes 8388608 | tf_op jit(solution)/shard_map/pallas_call | solution.py:195
  80.0 2.1 collective-permute-start.13
  82.0 4.1 %shard_map.68 = (bf16[2,128,1024]{2,1,0:T(8,128)(2,1)S(1)}, bf16[2,128,1024]{2,1,0:T(8,128)(2,1)S(1)}, bf16[4,128,128]{2,1,0:T(8,128)(2,1)S(1)}) custom-call(s32[3]{0:T(128)S(1)} %pad_add_fusion.place_ref, bf16[128,1920]{1,0:T(8,128)(2,1)S(1)} %get-tuple-element.134.refs_0_, bf16[128,1920]{1,0:T(8,128)(2,1)S(1)} %collective-permute-done.6.refs_1_, ...), custom_call_target="tpu_custom_call" | custom-call | flops 2818572288 | bytes 8388608 | tf_op jit(solution)/shard_map/pallas_call | solution.py:195
  86.1 7.4 %collective-permute-done.13 = bf16[2,128,1024]{2,1,0:T(8,128)(2,1)S(1)} collective-permute-done((bf16[2,128,1024]{2,1,0:T(8,128)(2,1)S(1)}, bf16[2,128,1024]{2,1,0:T(8,128)(2,1)S(1)}, u32[]{:S(2)}, u32[]{:S(2)}) %collective-permute-start.13) | collective-permute-done | bytes 524320 | tf_op jit(solution)/shard_map/ppermute | solution.py:302
  93.6 1.8 collective-permute-start.15
  98.9 2.1 collective-permute-start.14
  101.0 10.9 %collective-permute-done.15 = bf16[2,128,1024]{2,1,0:T(8,128)(2,1)S(1)} collective-permute-done((bf16[2,128,1024]{2,1,0:T(8,128)(2,1)S(1)}, bf16[2,128,1024]{2,1,0:T(8,128)(2,1)S(1)}, u32[]{:S(2)}, u32[]{:S(2)}) %collective-permute-start.15) | collective-permute-done | bytes 524320 | tf_op jit(solution)/shard_map/ppermute | solution.py:302
  111.9 2.3 collective-permute-start.16
  114.2 12.5 %collective-permute-done.18.refs_1_ = bf16[3,224,512]{2,1,0:T(8,128)(2,1)S(1)} collective-permute-done((bf16[3,224,512]{2,1,0:T(8,128)(2,1)S(1)}, bf16[3,224,512]{2,1,0:T(8,128)(2,1)S(1)}, u32[]{:S(2)}, u32[]{:S(2)}) %collective-permute-start.18) | collective-permute-done | bytes 688160 | tf_op jit(solution)/shard_map/ppermute | solution.py:296
  128.0 5.1 %collective-permute-done.20 = bf16[3,4,224,512]{3,2,1,0:T(8,128)(2,1)S(1)} collective-permute-done((bf16[3,4,224,512]{3,2,1,0:T(8,128)(2,1)S(1)}, bf16[3,4,224,512]{3,2,1,0:T(8,128)(2,1)S(1)}, u32[]{:S(2)}, u32[]{:S(2)}) %collective-permute-start.20) | collective-permute-done | bytes 2752544 | tf_op jit(solution)/shard_map/ppermute | solution.py:299
  133.0 4.1 %shard_map.70 = (bf16[2,128,1024]{2,1,0:T(8,128)(2,1)S(1)}, bf16[2,128,1024]{2,1,0:T(8,128)(2,1)S(1)}, bf16[4,128,128]{2,1,0:T(8,128)(2,1)}) custom-call(s32[3]{0:T(128)S(1)} %pad_add_fusion.place_ref, bf16[128,1920]{1,0:T(8,128)(2,1)S(1)} %get-tuple-element.122.refs_0_, bf16[128,1920]{1,0:T(8,128)(2,1)S(1)} %collective-permute-done.3.refs_1_, ...), custom_call_target="tpu_custom_call" | custom-call | flops 2818572288 | bytes 8388608 | tf_op jit(solution)/shard_map/pallas_call | solution.py:195
  137.8 4.1 %shard_map.71 = (bf16[2,128,1024]{2,1,0:T(8,128)(2,1)S(1)}, bf16[2,128,1024]{2,1,0:T(8,128)(2,1)S(1)}, bf16[4,128,128]{2,1,0:T(8,128)(2,1)}) custom-call(s32[3]{0:T(128)S(1)} %pad_add_fusion.place_ref, bf16[128,1920]{1,0:T(8,128)(2,1)S(1)} %get-tuple-element.134.refs_0_, bf16[128,1920]{1,0:T(8,128)(2,1)S(1)} %collective-permute-done.6.refs_1_, ...), custom_call_target="tpu_custom_call" | custom-call | flops 2818572288 | bytes 8388608 | tf_op jit(solution)/shard_map/pallas_call | solution.py:195
  141.9 9.3 %collective-permute-done.21 = bf16[2,128,1024]{2,1,0:T(8,128)(2,1)S(1)} collective-permute-done((bf16[2,128,1024]{2,1,0:T(8,128)(2,1)S(1)}, bf16[2,128,1024]{2,1,0:T(8,128)(2,1)S(1)}, u32[]{:S(2)}, u32[]{:S(2)}) %collective-permute-start.21) | collective-permute-done | bytes 524320 | tf_op jit(solution)/shard_map/ppermute | solution.py:302
  151.9 2.6 collective-permute-start.22
  156.6 1.8 collective-permute-start.29
  158.4 11.6 %collective-permute-done.23 = bf16[2,128,1024]{2,1,0:T(8,128)(2,1)S(1)} collective-permute-done((bf16[2,128,1024]{2,1,0:T(8,128)(2,1)S(1)}, bf16[2,128,1024]{2,1,0:T(8,128)(2,1)S(1)}, u32[]{:S(2)}, u32[]{:S(2)}) %collective-permute-start.23) | collective-permute-done | bytes 524320 | tf_op jit(solution)/shard_map/ppermute | solution.py:302
  170.6 1.9 collective-permute-start.24
  173.9 8.1 %collective-permute-done.24.refs_1_ = bf16[128,1024]{1,0:T(8,128)(2,1)S(1)} collective-permute-done((bf16[128,1024]{1,0:T(8,128)(2,1)S(1)}, bf16[128,1024]{1,0:T(8,128)(2,1)S(1)}, u32[]{:S(2)}, u32[]{:S(2)}) %collective-permute-start.24) | collective-permute-done | bytes 262176 | tf_op jit(solution)/shard_map/ppermute | solution.py:302
  183.8 8.4 %collective-permute-done.30.refs_5_ = bf16[1,128,1024]{2,1,0:T(8,128)(2,1)S(1)} collective-permute-done((bf16[1,128,1024]{2,1,0:T(8,128)(2,1)S(1)}, bf16[1,128,1024]{2,1,0:T(8,128)(2,1)S(1)}, u32[]{:S(2)}, u32[]{:S(2)}) %collective-permute-start.30) | collective-permute-done | bytes 262176 | tf_op jit(solution)/shard_map/ppermute | solution.py:302
  192.7 3.9 %collective-permute-done.25.refs_2_ = bf16[128,1024]{1,0:T(8,128)(2,1)S(1)} collective-permute-done((bf16[128,1024]{1,0:T(8,128)(2,1)S(1)}, bf16[128,1024]{1,0:T(8,128)(2,1)S(1)}, u32[]{:S(2)}, u32[]{:S(2)}) %collective-permute-start.25) | collective-permute-done | bytes 262176 | tf_op jit(solution)/shard_map/ppermute | solution.py:302
  197.9 2.1 collective-permute-start.38
  200.0 11.1 %collective-permute-done.26.refs_3_ = bf16[128,1024]{1,0:T(8,128)(2,1)S(1)} collective-permute-done((bf16[128,1024]{1,0:T(8,128)(2,1)S(1)}, bf16[128,1024]{1,0:T(8,128)(2,1)S(1)}, u32[]{:S(2)}, u32[]{:S(2)}) %collective-permute-start.26) | collective-permute-done | bytes 262176 | tf_op jit(solution)/shard_map/ppermute | solution.py:302
  211.1 5.7 %shard_map.75 = (bf16[128,1792]{1,0:T(8,128)(2,1)S(1)}, bf16[128,1792]{1,0:T(8,128)(2,1)}, bf16[128,1792]{1,0:T(8,128)(2,1)}, bf16[128,1792]{1,0:T(8,128)(2,1)}) custom-call(s32[3]{0:T(128)S(1)} %pad_add_fusion.place_ref, bf16[4,128,128]{2,1,0:T(8,128)(2,1)S(1)} %get-tuple-element.107.routing_ref, bf16[128,1024]{1,0:T(8,128)(2,1)S(1)} %shard_map.72.refs_0_, ...), custom_call_target="tpu_custom_call" | custom-call | flops 2818572288 | bytes 8388608 | tf_op jit(solution)/shard_map/pallas_call | solution.py:265
  216.8 2.0 collective-permute-start.40
  222.3 3.8 %collective-permute-done.39.refs_1_ = bf16[128,1024]{1,0:T(8,128)(2,1)} collective-permute-done((bf16[128,1024]{1,0:T(8,128)(2,1)S(1)}, bf16[128,1024]{1,0:T(8,128)(2,1)}, u32[]{:S(2)}, u32[]{:S(2)}) %collective-permute-start.39) | collective-permute-done | bytes 262176 | tf_op jit(solution)/shard_map/ppermute | solution.py:302
  226.1 4.4 %collective-permute-done.40.refs_3_ = bf16[128,1024]{1,0:T(8,128)(2,1)} collective-permute-done((bf16[128,1024]{1,0:T(8,128)(2,1)}, bf16[128,1024]{1,0:T(8,128)(2,1)}, u32[]{:S(2)}, u32[]{:S(2)}) %collective-permute-start.40) | collective-permute-done | bytes 262176 | tf_op jit(solution)/shard_map/ppermute | solution.py:302
  231.4 1.8 copy-done.11
  233.2 5.2 %shard_map.76 = (bf16[128,1792]{1,0:T(8,128)(2,1)S(1)}, bf16[128,1792]{1,0:T(8,128)(2,1)S(1)}, bf16[128,1792]{1,0:T(8,128)(2,1)S(1)}, bf16[128,1792]{1,0:T(8,128)(2,1)S(1)}) custom-call(s32[3]{0:T(128)S(1)} %pad_add_fusion.place_ref, bf16[4,128,128]{2,1,0:T(8,128)(2,1)S(1)} %copy-done.9, bf16[128,1024]{1,0:T(8,128)(2,1)S(1)} %shard_map.73.refs_0_, ...), custom_call_target="tpu_custom_call" | custom-call | flops 2818572288 | bytes 8388608 | tf_op jit(solution)/shard_map/pallas_call | solution.py:265
  238.4 2.7 collective-permute-done.33
  246.6 2.6 collective-permute-start.36
  249.2 5.4 %collective-permute-done.41 = bf16[128,1792]{1,0:T(8,128)(2,1)S(1)} collective-permute-done((bf16[128,1792]{1,0:T(8,128)(2,1)S(1)}, bf16[128,1792]{1,0:T(8,128)(2,1)S(1)}, u32[]{:S(2)}, u32[]{:S(2)}) %collective-permute-start.41) | collective-permute-done | bytes 458784 | tf_op jit(solution)/shard_map/ppermute | solution.py:296
  254.6 2.3 collective-permute-start.37
  256.9 5.4 %collective-permute-done.42 = bf16[128,1792]{1,0:T(8,128)(2,1)S(1)} collective-permute-done((bf16[128,1792]{1,0:T(8,128)(2,1)S(1)}, bf16[128,1792]{1,0:T(8,128)(2,1)S(1)}, u32[]{:S(2)}, u32[]{:S(2)}) %collective-permute-start.42) | collective-permute-done | bytes 458784 | tf_op jit(solution)/shard_map/ppermute | solution.py:296
  263.3 2.3 collective-permute-start.45
  267.0 2.1 collective-permute-done.44.refs_5_
  269.1 3.3 %collective-permute-done.45.refs_6_ = bf16[32,1792]{1,0:T(8,128)(2,1)S(1)} collective-permute-done((bf16[32,1792]{1,0:T(8,128)(2,1)S(1)}, bf16[32,1792]{1,0:T(8,128)(2,1)S(1)}, u32[]{:S(2)}, u32[]{:S(2)}) %collective-permute-start.45) | collective-permute-done | bytes 114720 | tf_op jit(solution)/shard_map/ppermute | solution.py:302
  272.4 1.9 shard_map.77
  (113 shorter events, 44.1 us)
Async XLA Ops:
  3.0 34.4 %collective-permute-start.10 = (bf16[3,224,512]{2,1,0:T(8,128)(2,1)}, bf16[3,224,512]{2,1,0:T(8,128)(2,1)S(1)}, u32[]{:S(2)}, u32[]{:S(2)}) collective-permute-start(bf16[3,224,512]{2,1,0:T(8,128)(2,1)} %get-tuple-element.176), channel_id=1, source_target_pairs={{0,16},{4,20},{8,24},{12,28},{16,0},{20,4},{24,8},{28,12},{1,17},{... | collective-permute-start | bytes 2064392 | tf_op jit(solution)/shard_map/ppermute | solution.py:296
  6.0 33.3 %collective-permute-start.11 = (bf16[3,224,512]{2,1,0:T(8,128)(2,1)}, bf16[3,224,512]{2,1,0:T(8,128)(2,1)}, u32[]{:S(2)}, u32[]{:S(2)}) collective-permute-start(bf16[3,224,512]{2,1,0:T(8,128)(2,1)} %get-tuple-element.175), channel_id=1, source_target_pairs={{0,24},{4,28},{8,16},{12,20},{16,8},{20,12},{24,0},{28,4},{1,25},{... | collective-permute-start | bytes 2064392 | tf_op jit(solution)/shard_map/ppermute | solution.py:296
  11.1 10.5 %collective-permute-start = (bf16[64,1792]{1,0:T(8,128)(2,1)S(1)}, bf16[64,1792]{1,0:T(8,128)(2,1)S(1)}, u32[]{:S(2)}, u32[]{:S(2)}) collective-permute-start(bf16[64,1792]{1,0:T(8,128)(2,1)S(1)} %get-tuple-element.91), channel_id=1, source_target_pairs={{0,1},{1,0},{2,3},{3,2},{4,5},{5,4},{6,7},{7,6},{8,9},{9,8},{10,11... | collective-permute-start | bytes 688136 | tf_op jit(solution)/shard_map/ppermute | solution.py:302
  12.7 19.6 %collective-permute-start.1 = (bf16[64,1792]{1,0:T(8,128)(2,1)}, bf16[64,1792]{1,0:T(8,128)(2,1)}, u32[]{:S(2)}, u32[]{:S(2)}) collective-permute-start(bf16[64,1792]{1,0:T(8,128)(2,1)} %get-tuple-element.92), channel_id=1, source_target_pairs={{0,2},{1,3},{2,0},{3,1},{4,6},{5,7},{6,4},{7,5},{8,10},{9,11},{10,... | collective-permute-start | bytes 688136 | tf_op jit(solution)/shard_map/ppermute | solution.py:302
  15.3 17.0 %collective-permute-start.2 = (bf16[64,1792]{1,0:T(8,128)(2,1)}, bf16[64,1792]{1,0:T(8,128)(2,1)}, u32[]{:S(2)}, u32[]{:S(2)}) collective-permute-start(bf16[64,1792]{1,0:T(8,128)(2,1)} %get-tuple-element.93), channel_id=1, source_target_pairs={{0,3},{1,2},{2,1},{3,0},{4,7},{5,6},{6,5},{7,4},{8,11},{9,10},{10,... | collective-permute-start | bytes 688136 | tf_op jit(solution)/shard_map/ppermute | solution.py:302
  22.3 18.5 %collective-permute-start.9 = (bf16[3,224,512]{2,1,0:T(8,128)(2,1)}, bf16[3,224,512]{2,1,0:T(8,128)(2,1)}, u32[]{:S(2)}, u32[]{:S(2)}) collective-permute-start(bf16[3,224,512]{2,1,0:T(8,128)(2,1)} %get-tuple-element.177), channel_id=1, source_target_pairs={{0,8},{4,12},{8,0},{12,4},{16,24},{20,28},{24,16},{28,20},{1,9},{5... | collective-permute-start | bytes 2064392 | tf_op jit(solution)/shard_map/ppermute | solution.py:296
  35.3 14.2 %collective-permute-start.4 = (bf16[128,1920]{1,0:T(8,128)(2,1)S(1)}, bf16[128,1920]{1,0:T(8,128)(2,1)S(1)}, u32[]{:S(2)}, u32[]{:S(2)}) collective-permute-start(bf16[128,1920]{1,0:T(8,128)(2,1)S(1)} %get-tuple-element.122.refs_0_), channel_id=1, source_target_pairs={{0,16},{4,20},{8,24},{12,28},{16,0},{20,4},{24,8},{28,12},{1,17},{... | collective-permute-start | bytes 1474568 | tf_op jit(solution)/shard_map/ppermute | solution.py:296
  36.9 21.9 %collective-permute-start.3 = (bf16[128,1920]{1,0:T(8,128)(2,1)S(1)}, bf16[128,1920]{1,0:T(8,128)(2,1)S(1)}, u32[]{:S(2)}, u32[]{:S(2)}) collective-permute-start(bf16[128,1920]{1,0:T(8,128)(2,1)S(1)} %get-tuple-element.122.refs_0_), channel_id=1, source_target_pairs={{0,8},{4,12},{8,0},{12,4},{16,24},{20,28},{24,16},{28,20},{1,9},{5... | collective-permute-start | bytes 1474568 | tf_op jit(solution)/shard_map/ppermute | solution.py:296
  37.4 21.3 %collective-permute-start.6 = (bf16[128,1920]{1,0:T(8,128)(2,1)S(1)}, bf16[128,1920]{1,0:T(8,128)(2,1)S(1)}, u32[]{:S(2)}, u32[]{:S(2)}) collective-permute-start(bf16[128,1920]{1,0:T(8,128)(2,1)S(1)} %get-tuple-element.134.refs_0_), channel_id=1, source_target_pairs={{0,8},{4,12},{8,0},{12,4},{16,24},{20,28},{24,16},{28,20},{1,9},{5... | collective-permute-start | bytes 1474568 | tf_op jit(solution)/shard_map/ppermute | solution.py:296
  39.3 19.5 %collective-permute-start.7 = (bf16[128,1920]{1,0:T(8,128)(2,1)S(1)}, bf16[128,1920]{1,0:T(8,128)(2,1)S(1)}, u32[]{:S(2)}, u32[]{:S(2)}) collective-permute-start(bf16[128,1920]{1,0:T(8,128)(2,1)S(1)} %get-tuple-element.134.refs_0_), channel_id=1, source_target_pairs={{0,16},{4,20},{8,24},{12,28},{16,0},{20,4},{24,8},{28,12},{1,17},{... | collective-permute-start | bytes 1474568 | tf_op jit(solution)/shard_map/ppermute | solution.py:296
  60.8 15.1 %collective-permute-start.12 = (bf16[3,4,224,512]{3,2,1,0:T(8,128)(2,1)S(1)}, bf16[3,4,224,512]{3,2,1,0:T(8,128)(2,1)S(1)}, u32[]{:S(2)}, u32[]{:S(2)}) collective-permute-start(bf16[3,4,224,512]{3,2,1,0:T(8,128)(2,1)S(1)} %shard_map.66), channel_id=1, source_target_pairs={{0,4},{4,0},{8,12},{12,8},{16,20},{20,16},{24,28},{28,24},{1,5},{5... | collective-permute-start | bytes 8257544 | tf_op jit(solution)/shard_map/ppermute | solution.py:299
  60.9 13.6 %collective-permute-start.5 = (bf16[128,1920]{1,0:T(8,128)(2,1)S(1)}, bf16[128,1920]{1,0:T(8,128)(2,1)S(1)}, u32[]{:S(2)}, u32[]{:S(2)}) collective-permute-start(bf16[128,1920]{1,0:T(8,128)(2,1)S(1)} %collective-permute-done.4.refs_2_), channel_id=1, source_target_pairs={{0,8},{4,12},{8,0},{12,4},{16,24},{20,28},{24,16},{28,20},{1,9},{5... | collective-permute-start | bytes 1474568 | tf_op jit(solution)/shard_map/ppermute | solution.py:296
  62.6 13.3 %collective-permute-start.8 = (bf16[128,1920]{1,0:T(8,128)(2,1)S(1)}, bf16[128,1920]{1,0:T(8,128)(2,1)S(1)}, u32[]{:S(2)}, u32[]{:S(2)}) collective-permute-start(bf16[128,1920]{1,0:T(8,128)(2,1)S(1)} %collective-permute-done.6.refs_1_), channel_id=1, source_target_pairs={{0,16},{4,20},{8,24},{12,28},{16,0},{20,4},{24,8},{28,12},{1,17},{... | collective-permute-start | bytes 1474568 | tf_op jit(solution)/shard_map/ppermute | solution.py:296
  80.0 13.5 %collective-permute-start.13 = (bf16[2,128,1024]{2,1,0:T(8,128)(2,1)S(1)}, bf16[2,128,1024]{2,1,0:T(8,128)(2,1)S(1)}, u32[]{:S(2)}, u32[]{:S(2)}) collective-permute-start(bf16[2,128,1024]{2,1,0:T(8,128)(2,1)S(1)} %get-tuple-element.109), channel_id=1, source_target_pairs={{0,1},{1,0},{2,3},{3,2},{4,5},{5,4},{6,7},{7,6},{8,9},{9,8},{10,11... | collective-permute-start | bytes 1572872 | tf_op jit(solution)/shard_map/ppermute | solution.py:302
  86.1 106.1 %copy-start.8 = (bf16[4,128,128]{2,1,0:T(8,128)(2,1)}, bf16[4,128,128]{2,1,0:T(8,128)(2,1)S(1)}, u32[]{:S(2)}) copy-start(bf16[4,128,128]{2,1,0:T(8,128)(2,1)S(1)} %get-tuple-element.148.routing_ref) | copy-start | bytes 393220
  93.6 18.3 %collective-permute-start.15 = (bf16[2,128,1024]{2,1,0:T(8,128)(2,1)S(1)}, bf16[2,128,1024]{2,1,0:T(8,128)(2,1)S(1)}, u32[]{:S(2)}, u32[]{:S(2)}) collective-permute-start(bf16[2,128,1024]{2,1,0:T(8,128)(2,1)S(1)} %get-tuple-element.120), channel_id=1, source_target_pairs={{0,1},{1,0},{2,3},{3,2},{4,5},{5,4},{6,7},{7,6},{8,9},{9,8},{10,11... | collective-permute-start | bytes 1572872 | tf_op jit(solution)/shard_map/ppermute | solution.py:302
  95.4 18.8 %collective-permute-start.17 = (bf16[3,224,512]{2,1,0:T(8,128)(2,1)S(1)}, bf16[3,224,512]{2,1,0:T(8,128)(2,1)S(1)}, u32[]{:S(2)}, u32[]{:S(2)}) collective-permute-start(bf16[3,224,512]{2,1,0:T(8,128)(2,1)S(1)} %get-tuple-element.126), channel_id=1, source_target_pairs={{0,8},{4,12},{8,0},{12,4},{16,24},{20,28},{24,16},{28,20},{1,9},{5... | collective-permute-start | bytes 2064392 | tf_op jit(solution)/shard_map/ppermute | solution.py:296
  96.8 29.9 %collective-permute-start.18 = (bf16[3,224,512]{2,1,0:T(8,128)(2,1)S(1)}, bf16[3,224,512]{2,1,0:T(8,128)(2,1)S(1)}, u32[]{:S(2)}, u32[]{:S(2)}) collective-permute-start(bf16[3,224,512]{2,1,0:T(8,128)(2,1)S(1)} %get-tuple-element.127), channel_id=1, source_target_pairs={{0,16},{4,20},{8,24},{12,28},{16,0},{20,4},{24,8},{28,12},{1,17},{... | collective-permute-start | bytes 2064392 | tf_op jit(solution)/shard_map/ppermute | solution.py:296
  97.3 29.4 %collective-permute-start.19 = (bf16[3,224,512]{2,1,0:T(8,128)(2,1)S(1)}, bf16[3,224,512]{2,1,0:T(8,128)(2,1)S(1)}, u32[]{:S(2)}, u32[]{:S(2)}) collective-permute-start(bf16[3,224,512]{2,1,0:T(8,128)(2,1)S(1)} %get-tuple-element.128), channel_id=1, source_target_pairs={{0,24},{4,28},{8,16},{12,20},{16,8},{20,12},{24,0},{28,4},{1,25},{... | collective-permute-start | bytes 2064392 | tf_op jit(solution)/shard_map/ppermute | solution.py:296
  98.9 13.0 %collective-permute-start.14 = (bf16[1,128,1024]{2,1,0:T(8,128)(2,1)S(1)}, bf16[1,128,1024]{2,1,0:T(8,128)(2,1)S(1)}, u32[]{:S(2)}, u32[]{:S(2)}) collective-permute-start(bf16[1,128,1024]{2,1,0:T(8,128)(2,1)S(1)} %add_convert_fusion.5), channel_id=1, source_target_pairs={{0,2},{1,3},{2,0},{3,1},{4,6},{5,7},{6,4},{7,5},{8,10},{9,11},{10,... | collective-permute-start | bytes 786440 | tf_op jit(solution)/shard_map/ppermute | solution.py:302
  111.9 14.8 %collective-permute-start.16 = (bf16[1,128,1024]{2,1,0:T(8,128)(2,1)S(1)}, bf16[1,128,1024]{2,1,0:T(8,128)(2,1)S(1)}, u32[]{:S(2)}, u32[]{:S(2)}) collective-permute-start(bf16[1,128,1024]{2,1,0:T(8,128)(2,1)S(1)} %add_convert_fusion.4), channel_id=1, source_target_pairs={{0,2},{1,3},{2,0},{3,1},{4,6},{5,7},{6,4},{7,5},{8,10},{9,11},{10,... | collective-permute-start | bytes 786440 | tf_op jit(solution)/shard_map/ppermute | solution.py:302
  127.9 5.2 %collective-permute-start.20 = (bf16[3,4,224,512]{3,2,1,0:T(8,128)(2,1)S(1)}, bf16[3,4,224,512]{3,2,1,0:T(8,128)(2,1)S(1)}, u32[]{:S(2)}, u32[]{:S(2)}) collective-permute-start(bf16[3,4,224,512]{3,2,1,0:T(8,128)(2,1)S(1)} %shard_map.69), channel_id=1, source_target_pairs={{0,4},{4,0},{8,12},{12,8},{16,20},{20,16},{24,28},{28,24},{1,5},{5... | collective-permute-start | bytes 8257544 | tf_op jit(solution)/shard_map/ppermute | solution.py:299
  137.1 14.0 %collective-permute-start.21 = (bf16[2,128,1024]{2,1,0:T(8,128)(2,1)S(1)}, bf16[2,128,1024]{2,1,0:T(8,128)(2,1)S(1)}, u32[]{:S(2)}, u32[]{:S(2)}) collective-permute-start(bf16[2,128,1024]{2,1,0:T(8,128)(2,1)S(1)} %get-tuple-element.133), channel_id=1, source_target_pairs={{0,1},{1,0},{2,3},{3,2},{4,5},{5,4},{6,7},{7,6},{8,9},{9,8},{10,11... | collective-permute-start | bytes 1572872 | tf_op jit(solution)/shard_map/ppermute | solution.py:302
  151.2 18.8 %collective-permute-start.23 = (bf16[2,128,1024]{2,1,0:T(8,128)(2,1)S(1)}, bf16[2,128,1024]{2,1,0:T(8,128)(2,1)S(1)}, u32[]{:S(2)}, u32[]{:S(2)}) collective-permute-start(bf16[2,128,1024]{2,1,0:T(8,128)(2,1)S(1)} %get-tuple-element.140), channel_id=1, source_target_pairs={{0,1},{1,0},{2,3},{3,2},{4,5},{5,4},{6,7},{7,6},{8,9},{9,8},{10,11... | collective-permute-start | bytes 1572872 | tf_op jit(solution)/shard_map/ppermute | solution.py:302
  151.9 18.2 %collective-permute-start.22 = (bf16[1,128,1024]{2,1,0:T(8,128)(2,1)S(1)}, bf16[1,128,1024]{2,1,0:T(8,128)(2,1)S(1)}, u32[]{:S(2)}, u32[]{:S(2)}) collective-permute-start(bf16[1,128,1024]{2,1,0:T(8,128)(2,1)S(1)} %add_convert_fusion.3), channel_id=1, source_target_pairs={{0,2},{1,3},{2,0},{3,1},{4,6},{5,7},{6,4},{7,5},{8,10},{9,11},{10,... | collective-permute-start | bytes 786440 | tf_op jit(solution)/shard_map/ppermute | solution.py:302
  154.8 37.9 %collective-permute-start.27 = (bf16[3,224,512]{2,1,0:T(8,128)(2,1)S(1)}, bf16[3,224,512]{2,1,0:T(8,128)(2,1)S(1)}, u32[]{:S(2)}, u32[]{:S(2)}) collective-permute-start(bf16[3,224,512]{2,1,0:T(8,128)(2,1)S(1)} %get-tuple-element.145), channel_id=1, source_target_pairs={{0,8},{4,12},{8,0},{12,4},{16,24},{20,28},{24,16},{28,20},{1,9},{5... | collective-permute-start | bytes 2064392 | tf_op jit(solution)/shard_map/ppermute | solution.py:296
  155.5 37.1 %collective-permute-start.28 = (bf16[3,224,512]{2,1,0:T(8,128)(2,1)S(1)}, bf16[3,224,512]{2,1,0:T(8,128)(2,1)S(1)}, u32[]{:S(2)}, u32[]{:S(2)}) collective-permute-start(bf16[3,224,512]{2,1,0:T(8,128)(2,1)S(1)} %get-tuple-element.146), channel_id=1, source_target_pairs={{0,16},{4,20},{8,24},{12,28},{16,0},{20,4},{24,8},{28,12},{1,17},{... | collective-permute-start | bytes 2064392 | tf_op jit(solution)/shard_map/ppermute | solution.py:296
  156.6 36.1 %collective-permute-start.29 = (bf16[3,224,512]{2,1,0:T(8,128)(2,1)S(1)}, bf16[3,224,512]{2,1,0:T(8,128)(2,1)S(1)}, u32[]{:S(2)}, u32[]{:S(2)}) collective-permute-start(bf16[3,224,512]{2,1,0:T(8,128)(2,1)S(1)} %get-tuple-element.147), channel_id=1, source_target_pairs={{0,24},{4,28},{8,16},{12,20},{16,8},{20,12},{24,0},{28,4},{1,25},{... | collective-permute-start | bytes 2064392 | tf_op jit(solution)/shard_map/ppermute | solution.py:296
  170.6 11.4 %collective-permute-start.24 = (bf16[128,1024]{1,0:T(8,128)(2,1)S(1)}, bf16[128,1024]{1,0:T(8,128)(2,1)S(1)}, u32[]{:S(2)}, u32[]{:S(2)}) collective-permute-start(bf16[128,1024]{1,0:T(8,128)(2,1)S(1)} %shard_map.72.refs_0_), channel_id=1, source_target_pairs={{0,1},{1,0},{2,3},{3,2},{4,5},{5,4},{6,7},{7,6},{8,9},{9,8},{10,11... | collective-permute-start | bytes 786440 | tf_op jit(solution)/shard_map/ppermute | solution.py:302
  172.5 19.7 %collective-permute-start.30 = (bf16[1,128,1024]{2,1,0:T(8,128)(2,1)S(1)}, bf16[1,128,1024]{2,1,0:T(8,128)(2,1)S(1)}, u32[]{:S(2)}, u32[]{:S(2)}) collective-permute-start(bf16[1,128,1024]{2,1,0:T(8,128)(2,1)S(1)} %add_convert_fusion.2), channel_id=1, source_target_pairs={{0,2},{1,3},{2,0},{3,1},{4,6},{5,7},{6,4},{7,5},{8,10},{9,11},{10,... | collective-permute-start | bytes 786440 | tf_op jit(solution)/shard_map/ppermute | solution.py:302
  181.9 14.7 %collective-permute-start.25 = (bf16[128,1024]{1,0:T(8,128)(2,1)S(1)}, bf16[128,1024]{1,0:T(8,128)(2,1)S(1)}, u32[]{:S(2)}, u32[]{:S(2)}) collective-permute-start(bf16[128,1024]{1,0:T(8,128)(2,1)S(1)} %shard_map.72.refs_0_), channel_id=1, source_target_pairs={{0,2},{1,3},{2,0},{3,1},{4,6},{5,7},{6,4},{7,5},{8,10},{9,11},{10,... | collective-permute-start | bytes 786440 | tf_op jit(solution)/shard_map/ppermute | solution.py:302
  197.8 13.3 %collective-permute-start.31 = (bf16[3,4,224,512]{3,2,1,0:T(8,128)(2,1)S(1)}, bf16[3,4,224,512]{3,2,1,0:T(8,128)(2,1)S(1)}, u32[]{:S(2)}, u32[]{:S(2)}) collective-permute-start(bf16[3,4,224,512]{3,2,1,0:T(8,128)(2,1)S(1)} %shard_map.74), channel_id=1, source_target_pairs={{0,4},{4,0},{8,12},{12,8},{16,20},{20,16},{24,28},{28,24},{1,5},{5... | collective-permute-start | bytes 8257544 | tf_op jit(solution)/shard_map/ppermute | solution.py:299
  197.8 13.3 %collective-permute-start.26 = (bf16[128,1024]{1,0:T(8,128)(2,1)S(1)}, bf16[128,1024]{1,0:T(8,128)(2,1)S(1)}, u32[]{:S(2)}, u32[]{:S(2)}) collective-permute-start(bf16[128,1024]{1,0:T(8,128)(2,1)S(1)} %collective-permute-done.25.refs_2_), channel_id=1, source_target_pairs={{0,1},{1,0},{2,3},{3,2},{4,5},{5,4},{6,7},{7,6},{8,9},{9,8},{10,11... | collective-permute-start | bytes 786440 | tf_op jit(solution)/shard_map/ppermute | solution.py:302
  197.9 18.9 %collective-permute-start.38 = (bf16[128,1024]{1,0:T(8,128)(2,1)S(1)}, bf16[128,1024]{1,0:T(8,128)(2,1)}, u32[]{:S(2)}, u32[]{:S(2)}) collective-permute-start(bf16[128,1024]{1,0:T(8,128)(2,1)S(1)} %shard_map.73.refs_0_), channel_id=1, source_target_pairs={{0,2},{1,3},{2,0},{3,1},{4,6},{5,7},{6,4},{7,5},{8,10},{9,11},{10,... | collective-permute-start | bytes 786440 | tf_op jit(solution)/shard_map/ppermute | solution.py:302
  216.8 9.3 %collective-permute-start.39 = (bf16[128,1024]{1,0:T(8,128)(2,1)S(1)}, bf16[128,1024]{1,0:T(8,128)(2,1)}, u32[]{:S(2)}, u32[]{:S(2)}) collective-permute-start(bf16[128,1024]{1,0:T(8,128)(2,1)S(1)} %shard_map.73.refs_0_), channel_id=1, source_target_pairs={{0,1},{1,0},{2,3},{3,2},{4,5},{5,4},{6,7},{7,6},{8,9},{9,8},{10,11... | collective-permute-start | bytes 786440 | tf_op jit(solution)/shard_map/ppermute | solution.py:302
  216.8 13.7 %collective-permute-start.40 = (bf16[128,1024]{1,0:T(8,128)(2,1)}, bf16[128,1024]{1,0:T(8,128)(2,1)}, u32[]{:S(2)}, u32[]{:S(2)}) collective-permute-start(bf16[128,1024]{1,0:T(8,128)(2,1)} %collective-permute-done.38.refs_2_), channel_id=1, source_target_pairs={{0,1},{1,0},{2,3},{3,2},{4,5},{5,4},{6,7},{7,6},{8,9},{9,8},{10,11... | collective-permute-start | bytes 786440 | tf_op jit(solution)/shard_map/ppermute | solution.py:302
  218.8 19.6 %collective-permute-start.32 = (bf16[128,1792]{1,0:T(8,128)(2,1)}, bf16[128,1792]{1,0:T(8,128)(2,1)}, u32[]{:S(2)}, u32[]{:S(2)}) collective-permute-start(bf16[128,1792]{1,0:T(8,128)(2,1)} %get-tuple-element.159), channel_id=1, source_target_pairs={{0,8},{4,12},{8,0},{12,4},{16,24},{20,28},{24,16},{28,20},{1,9},{5... | collective-permute-start | bytes 1376264 | tf_op jit(solution)/shard_map/ppermute | solution.py:296
  219.6 21.5 %collective-permute-start.33 = (bf16[128,1792]{1,0:T(8,128)(2,1)}, bf16[128,1792]{1,0:T(8,128)(2,1)}, u32[]{:S(2)}, u32[]{:S(2)}) collective-permute-start(bf16[128,1792]{1,0:T(8,128)(2,1)} %get-tuple-element.160), channel_id=1, source_target_pairs={{0,16},{4,20},{8,24},{12,28},{16,0},{20,4},{24,8},{28,12},{1,17},{... | collective-permute-start | bytes 1376264 | tf_op jit(solution)/shard_map/ppermute | solution.py:296
  220.8 20.3 %collective-permute-start.34 = (bf16[128,1792]{1,0:T(8,128)(2,1)}, bf16[128,1792]{1,0:T(8,128)(2,1)}, u32[]{:S(2)}, u32[]{:S(2)}) collective-permute-start(bf16[128,1792]{1,0:T(8,128)(2,1)} %get-tuple-element.161), channel_id=1, source_target_pairs={{0,24},{4,28},{8,16},{12,20},{16,8},{20,12},{24,0},{28,4},{1,25},{... | collective-permute-start | bytes 1376264 | tf_op jit(solution)/shard_map/ppermute | solution.py:296
  241.1 13.5 %collective-permute-start.41 = (bf16[128,1792]{1,0:T(8,128)(2,1)S(1)}, bf16[128,1792]{1,0:T(8,128)(2,1)S(1)}, u32[]{:S(2)}, u32[]{:S(2)}) collective-permute-start(bf16[128,1792]{1,0:T(8,128)(2,1)S(1)} %get-tuple-element.169), channel_id=1, source_target_pairs={{0,8},{4,12},{8,0},{12,4},{16,24},{20,28},{24,16},{28,20},{1,9},{5... | collective-permute-start | bytes 1376264 | tf_op jit(solution)/shard_map/ppermute | solution.py:296
  242.4 19.9 %collective-permute-start.42 = (bf16[128,1792]{1,0:T(8,128)(2,1)S(1)}, bf16[128,1792]{1,0:T(8,128)(2,1)S(1)}, u32[]{:S(2)}, u32[]{:S(2)}) collective-permute-start(bf16[128,1792]{1,0:T(8,128)(2,1)S(1)} %get-tuple-element.170), channel_id=1, source_target_pairs={{0,16},{4,20},{8,24},{12,28},{16,0},{20,4},{24,8},{28,12},{1,17},{... | collective-permute-start | bytes 1376264 | tf_op jit(solution)/shard_map/ppermute | solution.py:296
  243.2 19.1 %collective-permute-start.43 = (bf16[128,1792]{1,0:T(8,128)(2,1)S(1)}, bf16[128,1792]{1,0:T(8,128)(2,1)S(1)}, u32[]{:S(2)}, u32[]{:S(2)}) collective-permute-start(bf16[128,1792]{1,0:T(8,128)(2,1)S(1)} %get-tuple-element.171), channel_id=1, source_target_pairs={{0,24},{4,28},{8,16},{12,20},{16,8},{20,12},{24,0},{28,4},{1,25},{... | collective-permute-start | bytes 1376264 | tf_op jit(solution)/shard_map/ppermute | solution.py:296
  246.2 19.3 %collective-permute-start.35 = (bf16[32,1792]{1,0:T(8,128)(2,1)S(1)}, bf16[32,1792]{1,0:T(8,128)(2,1)S(1)}, u32[]{:S(2)}, u32[]{:S(2)}) collective-permute-start(bf16[32,1792]{1,0:T(8,128)(2,1)S(1)} %get-tuple-element.187), channel_id=1, source_target_pairs={{0,1},{1,0},{2,3},{3,2},{4,5},{5,4},{6,7},{7,6},{8,9},{9,8},{10,11... | collective-permute-start | bytes 344072 | tf_op jit(solution)/shard_map/ppermute | solution.py:302
  246.6 20.4 %collective-permute-start.36 = (bf16[32,1792]{1,0:T(8,128)(2,1)S(1)}, bf16[32,1792]{1,0:T(8,128)(2,1)S(1)}, u32[]{:S(2)}, u32[]{:S(2)}) collective-permute-start(bf16[32,1792]{1,0:T(8,128)(2,1)S(1)} %get-tuple-element.186), channel_id=1, source_target_pairs={{0,2},{1,3},{2,0},{3,1},{4,6},{5,7},{6,4},{7,5},{8,10},{9,11},{10,... | collective-permute-start | bytes 344072 | tf_op jit(solution)/shard_map/ppermute | solution.py:302
  254.6 12.5 %collective-permute-start.37 = (bf16[32,1792]{1,0:T(8,128)(2,1)S(1)}, bf16[32,1792]{1,0:T(8,128)(2,1)S(1)}, u32[]{:S(2)}, u32[]{:S(2)}) collective-permute-start(bf16[32,1792]{1,0:T(8,128)(2,1)S(1)} %get-tuple-element.185), channel_id=1, source_target_pairs={{0,3},{1,2},{2,1},{3,0},{4,7},{5,6},{6,5},{7,4},{8,11},{9,10},{10,... | collective-permute-start | bytes 344072 | tf_op jit(solution)/shard_map/ppermute | solution.py:302
  262.6 6.6 %collective-permute-start.44 = (bf16[32,1792]{1,0:T(8,128)(2,1)S(1)}, bf16[32,1792]{1,0:T(8,128)(2,1)S(1)}, u32[]{:S(2)}, u32[]{:S(2)}) collective-permute-start(bf16[32,1792]{1,0:T(8,128)(2,1)S(1)} %get-tuple-element.183), channel_id=1, source_target_pairs={{0,1},{1,0},{2,3},{3,2},{4,5},{5,4},{6,7},{7,6},{8,9},{9,8},{10,11... | collective-permute-start | bytes 344072 | tf_op jit(solution)/shard_map/ppermute | solution.py:302
  263.3 9.1 %collective-permute-start.45 = (bf16[32,1792]{1,0:T(8,128)(2,1)S(1)}, bf16[32,1792]{1,0:T(8,128)(2,1)S(1)}, u32[]{:S(2)}, u32[]{:S(2)}) collective-permute-start(bf16[32,1792]{1,0:T(8,128)(2,1)S(1)} %get-tuple-element.182), channel_id=1, source_target_pairs={{0,2},{1,3},{2,0},{3,1},{4,6},{5,7},{6,4},{7,5},{8,10},{9,11},{10,... | collective-permute-start | bytes 344072 | tf_op jit(solution)/shard_map/ppermute | solution.py:302
  265.6 6.8 %collective-permute-start.46 = (bf16[32,1792]{1,0:T(8,128)(2,1)S(1)}, bf16[32,1792]{1,0:T(8,128)(2,1)S(1)}, u32[]{:S(2)}, u32[]{:S(2)}) collective-permute-start(bf16[32,1792]{1,0:T(8,128)(2,1)S(1)} %get-tuple-element.181), channel_id=1, source_target_pairs={{0,3},{1,2},{2,1},{3,0},{4,7},{5,6},{6,5},{7,4},{8,11},{9,10},{10,... | collective-permute-start | bytes 344072 | tf_op jit(solution)/shard_map/ppermute | solution.py:302
  (13 other events, 160.2 us)

commit v12 on v11

--- a/solution.py
+++ b/solution.py
@@ -7,7 +7,7 @@
 from jax.experimental.pallas import tpu as pltpu
 from jax.sharding import PartitionSpec as P
 
-VMEM_BYTES = 22 * 1024 * 1024
+VMEM_BYTES = 14 * 1024 * 1024
 CORES = 2
 HALVES = 2
 TILE = 256
@@ -237,22 +237,20 @@
     for step, hid_ref in enumerate(hids):
         block = jnp.bitwise_xor(place_ref[2], step)
         ids = routing_ref[step].astype(jnp.float32)
+        values = hid_ref[...].astype(jnp.float32)
+        values = [values[:, slot * width : (slot + 1) * width] for slot in range(slots)]
         for which in range(experts):
             mine = jnp.zeros((rows, width), jnp.float32)
             for slot in range(slots):
-                value = hid_ref[:, slot * width : (slot + 1) * width].astype(jnp.float32)
-                mine = jnp.where(ids[:, slot : slot + 1] == which, value, mine)
-            left[which, rows_of(block, rows), :] = mine.astype(left.dtype)
+                mine = jnp.where(ids[:, slot : slot + 1] == which, values[slot], mine)
+            left[rows_of(block, rows), which * width : (which + 1) * width] = mine.astype(
+                left.dtype
+            )
     for side, weight in enumerate(weights):
-        total = None
-        for which in range(experts):
-            term = lax.dot_general(
-                left[which],
-                weight[which],
-                (((1,), (1,)), ((), ())),
-                preferred_element_type=jnp.float32,
-            )
-            total = term if total is None else total + term
+        joined = jnp.concatenate([weight[which] for which in range(experts)], axis=1)
+        total = lax.dot_general(
+            left[...], joined, (((1,), (1,)), ((), ())), preferred_element_type=jnp.float32
+        )
         for step, out_ref in enumerate(outs):
             part = total[step * rows : (step + 1) * rows]
             out_ref[:, side * depth : (side + 1) * depth] = part.astype(out_ref.dtype)
@@ -267,7 +265,7 @@
         in_specs=[SMEM_SPEC] + [VMEM_SPEC] * (1 + levels + CORES),
         out_specs=[VMEM_SPEC] * levels,
         out_shape=[bf16(rows, wide)] * levels,
-        scratch_shapes=[pltpu.VMEM((experts, count, width), jnp.bfloat16)],
+        scratch_shapes=[pltpu.VMEM((count, experts * width), jnp.bfloat16)],
         cost_estimate=cost(
             2 * count * wide * width * experts,
             count * slots * width + experts * wide * width + count * wide,

time: 275 us -> 275 us (level)
  no operation moved by 1% of the time
where the time goes in v12:
time: 275 us; the launch traced here: 274 us
  waiting for transfers between devices  160 us (58%)
  starting transfers between devices  63.2 us (23%)
  Pallas kernels  37.1 us (13%)
  local copies, waits for them, and re-layouts  11.1 us (4%)
    ppermute x23, waiting for transfers between devices, to_level(): lax.ppermute(value, 'tensor', [(s, s ^ step) for s in range(n_tensor)])  99.7 us
    ppermute x21, waiting for transfers between devices, to_chip(): return lax.ppermute(value, 'expert', pairs)  55.5 us
    ppermute x23, starting transfers between devices, to_level(): lax.ppermute(value, 'tensor', [(s, s ^ step) for s in range(n_tensor)])  35.5 us
    ppermute x21, starting transfers between devices, to_chip(): return lax.ppermute(value, 'expert', pairs)  27.5 us
    pallas_call x4, Pallas kernels, picked_sums(): pl.pallas_call(functools.partial(pick_kernel, chips), in_specs=[SMEM_SPEC...  16.3 us
    pallas_call x2, Pallas kernels, down_sums(): pl.pallas_call(functools.partial(down_kernel, slots, levels), in_specs=[S...  10.9 us
    unnamed x28, local copies, waits for them, and re-layouts  7.17 us
  transfers between devices with their start and end apart: 47, of which 23 were waited for; matrix products, arithmetic and copies ran while one was open for 1% of the time, Pallas kernels for 8%

profile of v12, /device:TPU:0, one launch (start us, length us, event | category | flops | bytes accessed | tf_op | source)
XLA Modules:
  0.0 274.2 jit_solution(4736754664399051357)
XLA Ops:
  0.0 3.0 %constant_dynamic-slice_fusion.3 = (bf16[3,224,512]{2,1,0:T(8,128)(2,1)}, bf16[3,224,512]{2,1,0:T(8,128)(2,1)}, bf16[3,224,512]{2,1,0:T(8,128)(2,1)}) fusion(bf16[3,224,2048]{2,1,0:T(8,128)(2,1)} %own_ref.3, s32[]{:T(128)S(6)} %select_n.47, s32[]{:T(128)S(6)} %select_n.46, s32[]{:T(128)S(6)} %select_n.45), kind=kLoop, calls=%fused_computation.17 | loop fusion | bytes 4128780 | tf_op jit(solution)/shard_map/dynamic_slice | solution.py:324
  3.0 3.0 %collective-permute-start.10 = (bf16[3,224,512]{2,1,0:T(8,128)(2,1)}, bf16[3,224,512]{2,1,0:T(8,128)(2,1)S(1)}, u32[]{:S(2)}, u32[]{:S(2)}) collective-permute-start(bf16[3,224,512]{2,1,0:T(8,128)(2,1)} %get-tuple-element.176), channel_id=1, source_target_pairs={{0,16},{4,20},{8,24},{12,28},{16,0},{20,4},{24,8},{28,12},{1,17},{... | collective-permute-start | bytes 2064392 | tf_op jit(solution)/shard_map/ppermute | solution.py:294
  12.7 2.6 collective-permute-start.1
  15.5 6.1 %collective-permute-done.refs_1_ = bf16[64,1792]{1,0:T(8,128)(2,1)S(1)} collective-permute-done((bf16[64,1792]{1,0:T(8,128)(2,1)S(1)}, bf16[64,1792]{1,0:T(8,128)(2,1)S(1)}, u32[]{:S(2)}, u32[]{:S(2)}) %collective-permute-start) | collective-permute-done | bytes 229408 | tf_op jit(solution)/shard_map/ppermute | solution.py:300
  22.8 9.5 %collective-permute-done.1.refs_2_ = bf16[64,1792]{1,0:T(8,128)(2,1)} collective-permute-done((bf16[64,1792]{1,0:T(8,128)(2,1)}, bf16[64,1792]{1,0:T(8,128)(2,1)}, u32[]{:S(2)}, u32[]{:S(2)}) %collective-permute-start.1) | collective-permute-done | bytes 229408 | tf_op jit(solution)/shard_map/ppermute | solution.py:300
  37.4 1.8 collective-permute-start.6
  40.8 8.7 %collective-permute-done.4.refs_2_ = bf16[128,1920]{1,0:T(8,128)(2,1)S(1)} collective-permute-done((bf16[128,1920]{1,0:T(8,128)(2,1)S(1)}, bf16[128,1920]{1,0:T(8,128)(2,1)S(1)}, u32[]{:S(2)}, u32[]{:S(2)}) %collective-permute-start.4) | collective-permute-done | bytes 491552 | tf_op jit(solution)/shard_map/ppermute | solution.py:294
  49.5 9.2 %collective-permute-done.6.refs_1_ = bf16[128,1920]{1,0:T(8,128)(2,1)S(1)} collective-permute-done((bf16[128,1920]{1,0:T(8,128)(2,1)S(1)}, bf16[128,1920]{1,0:T(8,128)(2,1)S(1)}, u32[]{:S(2)}, u32[]{:S(2)}) %collective-permute-start.6) | collective-permute-done | bytes 491552 | tf_op jit(solution)/shard_map/ppermute | solution.py:294
  58.8 2.0 shard_map.66
  60.9 1.7 collective-permute-start.5
  64.3 10.2 %collective-permute-done.5.refs_3_ = bf16[128,1920]{1,0:T(8,128)(2,1)S(1)} collective-permute-done((bf16[128,1920]{1,0:T(8,128)(2,1)S(1)}, bf16[128,1920]{1,0:T(8,128)(2,1)S(1)}, u32[]{:S(2)}, u32[]{:S(2)}) %collective-permute-start.5) | collective-permute-done | bytes 491552 | tf_op jit(solution)/shard_map/ppermute | solution.py:294
  75.9 4.1 %shard_map.67 = (bf16[2,128,1024]{2,1,0:T(8,128)(2,1)S(1)}, bf16[2,128,1024]{2,1,0:T(8,128)(2,1)S(1)}, bf16[4,128,128]{2,1,0:T(8,128)(2,1)S(1)}) custom-call(s32[3]{0:T(128)S(1)} %pad_add_fusion.place_ref, bf16[128,1920]{1,0:T(8,128)(2,1)S(1)} %get-tuple-element.122.refs_0_, bf16[128,1920]{1,0:T(8,128)(2,1)S(1)} %collective-permute-done.3.refs_1_, ...), custom_call_target="tpu_custom_call" | custom-call | flops 2818572288 | bytes 8388608 | tf_op jit(solution)/shard_map/pallas_call | solution.py:195
  80.0 2.1 collective-permute-start.13
  82.0 4.1 %shard_map.68 = (bf16[2,128,1024]{2,1,0:T(8,128)(2,1)S(1)}, bf16[2,128,1024]{2,1,0:T(8,128)(2,1)S(1)}, bf16[4,128,128]{2,1,0:T(8,128)(2,1)S(1)}) custom-call(s32[3]{0:T(128)S(1)} %pad_add_fusion.place_ref, bf16[128,1920]{1,0:T(8,128)(2,1)S(1)} %get-tuple-element.134.refs_0_, bf16[128,1920]{1,0:T(8,128)(2,1)S(1)} %collective-permute-done.6.refs_1_, ...), custom_call_target="tpu_custom_call" | custom-call | flops 2818572288 | bytes 8388608 | tf_op jit(solution)/shard_map/pallas_call | solution.py:195
  86.1 7.4 %collective-permute-done.13 = bf16[2,128,1024]{2,1,0:T(8,128)(2,1)S(1)} collective-permute-done((bf16[2,128,1024]{2,1,0:T(8,128)(2,1)S(1)}, bf16[2,128,1024]{2,1,0:T(8,128)(2,1)S(1)}, u32[]{:S(2)}, u32[]{:S(2)}) %collective-permute-start.13) | collective-permute-done | bytes 524320 | tf_op jit(solution)/shard_map/ppermute | solution.py:300
  93.6 1.8 collective-permute-start.15
  98.9 2.1 collective-permute-start.14
  101.0 10.9 %collective-permute-done.15 = bf16[2,128,1024]{2,1,0:T(8,128)(2,1)S(1)} collective-permute-done((bf16[2,128,1024]{2,1,0:T(8,128)(2,1)S(1)}, bf16[2,128,1024]{2,1,0:T(8,128)(2,1)S(1)}, u32[]{:S(2)}, u32[]{:S(2)}) %collective-permute-start.15) | collective-permute-done | bytes 524320 | tf_op jit(solution)/shard_map/ppermute | solution.py:300
  111.9 2.3 collective-permute-start.16
  114.2 12.5 %collective-permute-done.18.refs_1_ = bf16[3,224,512]{2,1,0:T(8,128)(2,1)S(1)} collective-permute-done((bf16[3,224,512]{2,1,0:T(8,128)(2,1)S(1)}, bf16[3,224,512]{2,1,0:T(8,128)(2,1)S(1)}, u32[]{:S(2)}, u32[]{:S(2)}) %collective-permute-start.18) | collective-permute-done | bytes 688160 | tf_op jit(solution)/shard_map/ppermute | solution.py:294
  128.0 5.1 %collective-permute-done.20 = bf16[3,4,224,512]{3,2,1,0:T(8,128)(2,1)S(1)} collective-permute-done((bf16[3,4,224,512]{3,2,1,0:T(8,128)(2,1)S(1)}, bf16[3,4,224,512]{3,2,1,0:T(8,128)(2,1)S(1)}, u32[]{:S(2)}, u32[]{:S(2)}) %collective-permute-start.20) | collective-permute-done | bytes 2752544 | tf_op jit(solution)/shard_map/ppermute | solution.py:297
  133.1 4.1 %shard_map.70 = (bf16[2,128,1024]{2,1,0:T(8,128)(2,1)S(1)}, bf16[2,128,1024]{2,1,0:T(8,128)(2,1)S(1)}, bf16[4,128,128]{2,1,0:T(8,128)(2,1)}) custom-call(s32[3]{0:T(128)S(1)} %pad_add_fusion.place_ref, bf16[128,1920]{1,0:T(8,128)(2,1)S(1)} %get-tuple-element.122.refs_0_, bf16[128,1920]{1,0:T(8,128)(2,1)S(1)} %collective-permute-done.3.refs_1_, ...), custom_call_target="tpu_custom_call" | custom-call | flops 2818572288 | bytes 8388608 | tf_op jit(solution)/shard_map/pallas_call | solution.py:195
  137.8 4.1 %shard_map.71 = (bf16[2,128,1024]{2,1,0:T(8,128)(2,1)S(1)}, bf16[2,128,1024]{2,1,0:T(8,128)(2,1)S(1)}, bf16[4,128,128]{2,1,0:T(8,128)(2,1)}) custom-call(s32[3]{0:T(128)S(1)} %pad_add_fusion.place_ref, bf16[128,1920]{1,0:T(8,128)(2,1)S(1)} %get-tuple-element.134.refs_0_, bf16[128,1920]{1,0:T(8,128)(2,1)S(1)} %collective-permute-done.6.refs_1_, ...), custom_call_target="tpu_custom_call" | custom-call | flops 2818572288 | bytes 8388608 | tf_op jit(solution)/shard_map/pallas_call | solution.py:195
  141.9 9.3 %collective-permute-done.21 = bf16[2,128,1024]{2,1,0:T(8,128)(2,1)S(1)} collective-permute-done((bf16[2,128,1024]{2,1,0:T(8,128)(2,1)S(1)}, bf16[2,128,1024]{2,1,0:T(8,128)(2,1)S(1)}, u32[]{:S(2)}, u32[]{:S(2)}) %collective-permute-start.21) | collective-permute-done | bytes 524320 | tf_op jit(solution)/shard_map/ppermute | solution.py:300
  151.9 2.6 collective-permute-start.22
  156.6 1.8 collective-permute-start.29
  158.4 11.6 %collective-permute-done.23 = bf16[2,128,1024]{2,1,0:T(8,128)(2,1)S(1)} collective-permute-done((bf16[2,128,1024]{2,1,0:T(8,128)(2,1)S(1)}, bf16[2,128,1024]{2,1,0:T(8,128)(2,1)S(1)}, u32[]{:S(2)}, u32[]{:S(2)}) %collective-permute-start.23) | collective-permute-done | bytes 524320 | tf_op jit(solution)/shard_map/ppermute | solution.py:300
  170.6 1.9 collective-permute-start.24
  173.9 8.1 %collective-permute-done.24.refs_1_ = bf16[128,1024]{1,0:T(8,128)(2,1)S(1)} collective-permute-done((bf16[128,1024]{1,0:T(8,128)(2,1)S(1)}, bf16[128,1024]{1,0:T(8,128)(2,1)S(1)}, u32[]{:S(2)}, u32[]{:S(2)}) %collective-permute-start.24) | collective-permute-done | bytes 262176 | tf_op jit(solution)/shard_map/ppermute | solution.py:300
  183.8 8.4 %collective-permute-done.30.refs_5_ = bf16[1,128,1024]{2,1,0:T(8,128)(2,1)S(1)} collective-permute-done((bf16[1,128,1024]{2,1,0:T(8,128)(2,1)S(1)}, bf16[1,128,1024]{2,1,0:T(8,128)(2,1)S(1)}, u32[]{:S(2)}, u32[]{:S(2)}) %collective-permute-start.30) | collective-permute-done | bytes 262176 | tf_op jit(solution)/shard_map/ppermute | solution.py:300
  192.7 3.9 %collective-permute-done.25.refs_2_ = bf16[128,1024]{1,0:T(8,128)(2,1)S(1)} collective-permute-done((bf16[128,1024]{1,0:T(8,128)(2,1)S(1)}, bf16[128,1024]{1,0:T(8,128)(2,1)S(1)}, u32[]{:S(2)}, u32[]{:S(2)}) %collective-permute-start.25) | collective-permute-done | bytes 262176 | tf_op jit(solution)/shard_map/ppermute | solution.py:300
  197.9 2.1 collective-permute-start.38
  200.0 11.1 %collective-permute-done.26.refs_3_ = bf16[128,1024]{1,0:T(8,128)(2,1)S(1)} collective-permute-done((bf16[128,1024]{1,0:T(8,128)(2,1)S(1)}, bf16[128,1024]{1,0:T(8,128)(2,1)S(1)}, u32[]{:S(2)}, u32[]{:S(2)}) %collective-permute-start.26) | collective-permute-done | bytes 262176 | tf_op jit(solution)/shard_map/ppermute | solution.py:300
  211.1 5.7 %shard_map.75 = (bf16[128,1792]{1,0:T(8,128)(2,1)S(1)}, bf16[128,1792]{1,0:T(8,128)(2,1)}, bf16[128,1792]{1,0:T(8,128)(2,1)}, bf16[128,1792]{1,0:T(8,128)(2,1)}) custom-call(s32[3]{0:T(128)S(1)} %pad_add_fusion.place_ref, bf16[4,128,128]{2,1,0:T(8,128)(2,1)S(1)} %get-tuple-element.107.routing_ref, bf16[128,1024]{1,0:T(8,128)(2,1)S(1)} %shard_map.72.refs_0_, ...), custom_call_target="tpu_custom_call" | custom-call | flops 2818572288 | bytes 8388608 | tf_op jit(solution)/shard_map/pallas_call | solution.py:263
  216.8 2.0 collective-permute-start.40
  222.3 3.8 %collective-permute-done.39.refs_1_ = bf16[128,1024]{1,0:T(8,128)(2,1)} collective-permute-done((bf16[128,1024]{1,0:T(8,128)(2,1)S(1)}, bf16[128,1024]{1,0:T(8,128)(2,1)}, u32[]{:S(2)}, u32[]{:S(2)}) %collective-permute-start.39) | collective-permute-done | bytes 262176 | tf_op jit(solution)/shard_map/ppermute | solution.py:300
  226.1 4.4 %collective-permute-done.40.refs_3_ = bf16[128,1024]{1,0:T(8,128)(2,1)} collective-permute-done((bf16[128,1024]{1,0:T(8,128)(2,1)}, bf16[128,1024]{1,0:T(8,128)(2,1)}, u32[]{:S(2)}, u32[]{:S(2)}) %collective-permute-start.40) | collective-permute-done | bytes 262176 | tf_op jit(solution)/shard_map/ppermute | solution.py:300
  231.4 1.8 copy-done.11
  233.2 5.2 %shard_map.76 = (bf16[128,1792]{1,0:T(8,128)(2,1)S(1)}, bf16[128,1792]{1,0:T(8,128)(2,1)S(1)}, bf16[128,1792]{1,0:T(8,128)(2,1)S(1)}, bf16[128,1792]{1,0:T(8,128)(2,1)S(1)}) custom-call(s32[3]{0:T(128)S(1)} %pad_add_fusion.place_ref, bf16[4,128,128]{2,1,0:T(8,128)(2,1)S(1)} %copy-done.9, bf16[128,1024]{1,0:T(8,128)(2,1)S(1)} %shard_map.73.refs_0_, ...), custom_call_target="tpu_custom_call" | custom-call | flops 2818572288 | bytes 8388608 | tf_op jit(solution)/shard_map/pallas_call | solution.py:263
  238.4 2.7 collective-permute-done.33
  246.6 2.6 collective-permute-start.36
  249.2 5.4 %collective-permute-done.41 = bf16[128,1792]{1,0:T(8,128)(2,1)S(1)} collective-permute-done((bf16[128,1792]{1,0:T(8,128)(2,1)S(1)}, bf16[128,1792]{1,0:T(8,128)(2,1)S(1)}, u32[]{:S(2)}, u32[]{:S(2)}) %collective-permute-start.41) | collective-permute-done | bytes 458784 | tf_op jit(solution)/shard_map/ppermute | solution.py:294
  254.6 2.3 collective-permute-start.37
  256.9 5.4 %collective-permute-done.42 = bf16[128,1792]{1,0:T(8,128)(2,1)S(1)} collective-permute-done((bf16[128,1792]{1,0:T(8,128)(2,1)S(1)}, bf16[128,1792]{1,0:T(8,128)(2,1)S(1)}, u32[]{:S(2)}, u32[]{:S(2)}) %collective-permute-start.42) | collective-permute-done | bytes 458784 | tf_op jit(solution)/shard_map/ppermute | solution.py:294
  263.3 2.3 collective-permute-start.45
  267.1 2.1 collective-permute-done.44.refs_5_
  269.1 3.3 %collective-permute-done.45.refs_6_ = bf16[32,1792]{1,0:T(8,128)(2,1)S(1)} collective-permute-done((bf16[32,1792]{1,0:T(8,128)(2,1)S(1)}, bf16[32,1792]{1,0:T(8,128)(2,1)S(1)}, u32[]{:S(2)}, u32[]{:S(2)}) %collective-permute-start.45) | collective-permute-done | bytes 114720 | tf_op jit(solution)/shard_map/ppermute | solution.py:300
  272.4 1.9 shard_map.77
  (113 shorter events, 44.1 us)
Async XLA Ops:
  3.0 34.4 %collective-permute-start.10 = (bf16[3,224,512]{2,1,0:T(8,128)(2,1)}, bf16[3,224,512]{2,1,0:T(8,128)(2,1)S(1)}, u32[]{:S(2)}, u32[]{:S(2)}) collective-permute-start(bf16[3,224,512]{2,1,0:T(8,128)(2,1)} %get-tuple-element.176), channel_id=1, source_target_pairs={{0,16},{4,20},{8,24},{12,28},{16,0},{20,4},{24,8},{28,12},{1,17},{... | collective-permute-start | bytes 2064392 | tf_op jit(solution)/shard_map/ppermute | solution.py:294
  6.0 33.3 %collective-permute-start.11 = (bf16[3,224,512]{2,1,0:T(8,128)(2,1)}, bf16[3,224,512]{2,1,0:T(8,128)(2,1)}, u32[]{:S(2)}, u32[]{:S(2)}) collective-permute-start(bf16[3,224,512]{2,1,0:T(8,128)(2,1)} %get-tuple-element.175), channel_id=1, source_target_pairs={{0,24},{4,28},{8,16},{12,20},{16,8},{20,12},{24,0},{28,4},{1,25},{... | collective-permute-start | bytes 2064392 | tf_op jit(solution)/shard_map/ppermute | solution.py:294
  11.1 10.5 %collective-permute-start = (bf16[64,1792]{1,0:T(8,128)(2,1)S(1)}, bf16[64,1792]{1,0:T(8,128)(2,1)S(1)}, u32[]{:S(2)}, u32[]{:S(2)}) collective-permute-start(bf16[64,1792]{1,0:T(8,128)(2,1)S(1)} %get-tuple-element.91), channel_id=1, source_target_pairs={{0,1},{1,0},{2,3},{3,2},{4,5},{5,4},{6,7},{7,6},{8,9},{9,8},{10,11... | collective-permute-start | bytes 688136 | tf_op jit(solution)/shard_map/ppermute | solution.py:300
  12.7 19.6 %collective-permute-start.1 = (bf16[64,1792]{1,0:T(8,128)(2,1)}, bf16[64,1792]{1,0:T(8,128)(2,1)}, u32[]{:S(2)}, u32[]{:S(2)}) collective-permute-start(bf16[64,1792]{1,0:T(8,128)(2,1)} %get-tuple-element.92), channel_id=1, source_target_pairs={{0,2},{1,3},{2,0},{3,1},{4,6},{5,7},{6,4},{7,5},{8,10},{9,11},{10,... | collective-permute-start | bytes 688136 | tf_op jit(solution)/shard_map/ppermute | solution.py:300
  15.3 17.0 %collective-permute-start.2 = (bf16[64,1792]{1,0:T(8,128)(2,1)}, bf16[64,1792]{1,0:T(8,128)(2,1)}, u32[]{:S(2)}, u32[]{:S(2)}) collective-permute-start(bf16[64,1792]{1,0:T(8,128)(2,1)} %get-tuple-element.93), channel_id=1, source_target_pairs={{0,3},{1,2},{2,1},{3,0},{4,7},{5,6},{6,5},{7,4},{8,11},{9,10},{10,... | collective-permute-start | bytes 688136 | tf_op jit(solution)/shard_map/ppermute | solution.py:300
  22.3 18.5 %collective-permute-start.9 = (bf16[3,224,512]{2,1,0:T(8,128)(2,1)}, bf16[3,224,512]{2,1,0:T(8,128)(2,1)}, u32[]{:S(2)}, u32[]{:S(2)}) collective-permute-start(bf16[3,224,512]{2,1,0:T(8,128)(2,1)} %get-tuple-element.177), channel_id=1, source_target_pairs={{0,8},{4,12},{8,0},{12,4},{16,24},{20,28},{24,16},{28,20},{1,9},{5... | collective-permute-start | bytes 2064392 | tf_op jit(solution)/shard_map/ppermute | solution.py:294
  35.3 14.2 %collective-permute-start.4 = (bf16[128,1920]{1,0:T(8,128)(2,1)S(1)}, bf16[128,1920]{1,0:T(8,128)(2,1)S(1)}, u32[]{:S(2)}, u32[]{:S(2)}) collective-permute-start(bf16[128,1920]{1,0:T(8,128)(2,1)S(1)} %get-tuple-element.122.refs_0_), channel_id=1, source_target_pairs={{0,16},{4,20},{8,24},{12,28},{16,0},{20,4},{24,8},{28,12},{1,17},{... | collective-permute-start | bytes 1474568 | tf_op jit(solution)/shard_map/ppermute | solution.py:294
  36.9 21.9 %collective-permute-start.3 = (bf16[128,1920]{1,0:T(8,128)(2,1)S(1)}, bf16[128,1920]{1,0:T(8,128)(2,1)S(1)}, u32[]{:S(2)}, u32[]{:S(2)}) collective-permute-start(bf16[128,1920]{1,0:T(8,128)(2,1)S(1)} %get-tuple-element.122.refs_0_), channel_id=1, source_target_pairs={{0,8},{4,12},{8,0},{12,4},{16,24},{20,28},{24,16},{28,20},{1,9},{5... | collective-permute-start | bytes 1474568 | tf_op jit(solution)/shard_map/ppermute | solution.py:294
  37.4 21.3 %collective-permute-start.6 = (bf16[128,1920]{1,0:T(8,128)(2,1)S(1)}, bf16[128,1920]{1,0:T(8,128)(2,1)S(1)}, u32[]{:S(2)}, u32[]{:S(2)}) collective-permute-start(bf16[128,1920]{1,0:T(8,128)(2,1)S(1)} %get-tuple-element.134.refs_0_), channel_id=1, source_target_pairs={{0,8},{4,12},{8,0},{12,4},{16,24},{20,28},{24,16},{28,20},{1,9},{5... | collective-permute-start | bytes 1474568 | tf_op jit(solution)/shard_map/ppermute | solution.py:294
  39.3 19.5 %collective-permute-start.7 = (bf16[128,1920]{1,0:T(8,128)(2,1)S(1)}, bf16[128,1920]{1,0:T(8,128)(2,1)S(1)}, u32[]{:S(2)}, u32[]{:S(2)}) collective-permute-start(bf16[128,1920]{1,0:T(8,128)(2,1)S(1)} %get-tuple-element.134.refs_0_), channel_id=1, source_target_pairs={{0,16},{4,20},{8,24},{12,28},{16,0},{20,4},{24,8},{28,12},{1,17},{... | collective-permute-start | bytes 1474568 | tf_op jit(solution)/shard_map/ppermute | solution.py:294
  60.8 15.1 %collective-permute-start.12 = (bf16[3,4,224,512]{3,2,1,0:T(8,128)(2,1)S(1)}, bf16[3,4,224,512]{3,2,1,0:T(8,128)(2,1)S(1)}, u32[]{:S(2)}, u32[]{:S(2)}) collective-permute-start(bf16[3,4,224,512]{3,2,1,0:T(8,128)(2,1)S(1)} %shard_map.66), channel_id=1, source_target_pairs={{0,4},{4,0},{8,12},{12,8},{16,20},{20,16},{24,28},{28,24},{1,5},{5... | collective-permute-start | bytes 8257544 | tf_op jit(solution)/shard_map/ppermute | solution.py:297
  60.9 13.6 %collective-permute-start.5 = (bf16[128,1920]{1,0:T(8,128)(2,1)S(1)}, bf16[128,1920]{1,0:T(8,128)(2,1)S(1)}, u32[]{:S(2)}, u32[]{:S(2)}) collective-permute-start(bf16[128,1920]{1,0:T(8,128)(2,1)S(1)} %collective-permute-done.4.refs_2_), channel_id=1, source_target_pairs={{0,8},{4,12},{8,0},{12,4},{16,24},{20,28},{24,16},{28,20},{1,9},{5... | collective-permute-start | bytes 1474568 | tf_op jit(solution)/shard_map/ppermute | solution.py:294
  62.6 13.3 %collective-permute-start.8 = (bf16[128,1920]{1,0:T(8,128)(2,1)S(1)}, bf16[128,1920]{1,0:T(8,128)(2,1)S(1)}, u32[]{:S(2)}, u32[]{:S(2)}) collective-permute-start(bf16[128,1920]{1,0:T(8,128)(2,1)S(1)} %collective-permute-done.6.refs_1_), channel_id=1, source_target_pairs={{0,16},{4,20},{8,24},{12,28},{16,0},{20,4},{24,8},{28,12},{1,17},{... | collective-permute-start | bytes 1474568 | tf_op jit(solution)/shard_map/ppermute | solution.py:294
  80.0 13.5 %collective-permute-start.13 = (bf16[2,128,1024]{2,1,0:T(8,128)(2,1)S(1)}, bf16[2,128,1024]{2,1,0:T(8,128)(2,1)S(1)}, u32[]{:S(2)}, u32[]{:S(2)}) collective-permute-start(bf16[2,128,1024]{2,1,0:T(8,128)(2,1)S(1)} %get-tuple-element.109), channel_id=1, source_target_pairs={{0,1},{1,0},{2,3},{3,2},{4,5},{5,4},{6,7},{7,6},{8,9},{9,8},{10,11... | collective-permute-start | bytes 1572872 | tf_op jit(solution)/shard_map/ppermute | solution.py:300
  86.1 106.1 %copy-start.8 = (bf16[4,128,128]{2,1,0:T(8,128)(2,1)}, bf16[4,128,128]{2,1,0:T(8,128)(2,1)S(1)}, u32[]{:S(2)}) copy-start(bf16[4,128,128]{2,1,0:T(8,128)(2,1)S(1)} %get-tuple-element.148.routing_ref) | copy-start | bytes 393220
  93.6 18.3 %collective-permute-start.15 = (bf16[2,128,1024]{2,1,0:T(8,128)(2,1)S(1)}, bf16[2,128,1024]{2,1,0:T(8,128)(2,1)S(1)}, u32[]{:S(2)}, u32[]{:S(2)}) collective-permute-start(bf16[2,128,1024]{2,1,0:T(8,128)(2,1)S(1)} %get-tuple-element.120), channel_id=1, source_target_pairs={{0,1},{1,0},{2,3},{3,2},{4,5},{5,4},{6,7},{7,6},{8,9},{9,8},{10,11... | collective-permute-start | bytes 1572872 | tf_op jit(solution)/shard_map/ppermute | solution.py:300
  95.4 18.8 %collective-permute-start.17 = (bf16[3,224,512]{2,1,0:T(8,128)(2,1)S(1)}, bf16[3,224,512]{2,1,0:T(8,128)(2,1)S(1)}, u32[]{:S(2)}, u32[]{:S(2)}) collective-permute-start(bf16[3,224,512]{2,1,0:T(8,128)(2,1)S(1)} %get-tuple-element.126), channel_id=1, source_target_pairs={{0,8},{4,12},{8,0},{12,4},{16,24},{20,28},{24,16},{28,20},{1,9},{5... | collective-permute-start | bytes 2064392 | tf_op jit(solution)/shard_map/ppermute | solution.py:294
  96.8 29.9 %collective-permute-start.18 = (bf16[3,224,512]{2,1,0:T(8,128)(2,1)S(1)}, bf16[3,224,512]{2,1,0:T(8,128)(2,1)S(1)}, u32[]{:S(2)}, u32[]{:S(2)}) collective-permute-start(bf16[3,224,512]{2,1,0:T(8,128)(2,1)S(1)} %get-tuple-element.127), channel_id=1, source_target_pairs={{0,16},{4,20},{8,24},{12,28},{16,0},{20,4},{24,8},{28,12},{1,17},{... | collective-permute-start | bytes 2064392 | tf_op jit(solution)/shard_map/ppermute | solution.py:294
  97.3 29.4 %collective-permute-start.19 = (bf16[3,224,512]{2,1,0:T(8,128)(2,1)S(1)}, bf16[3,224,512]{2,1,0:T(8,128)(2,1)S(1)}, u32[]{:S(2)}, u32[]{:S(2)}) collective-permute-start(bf16[3,224,512]{2,1,0:T(8,128)(2,1)S(1)} %get-tuple-element.128), channel_id=1, source_target_pairs={{0,24},{4,28},{8,16},{12,20},{16,8},{20,12},{24,0},{28,4},{1,25},{... | collective-permute-start | bytes 2064392 | tf_op jit(solution)/shard_map/ppermute | solution.py:294
  98.9 13.0 %collective-permute-start.14 = (bf16[1,128,1024]{2,1,0:T(8,128)(2,1)S(1)}, bf16[1,128,1024]{2,1,0:T(8,128)(2,1)S(1)}, u32[]{:S(2)}, u32[]{:S(2)}) collective-permute-start(bf16[1,128,1024]{2,1,0:T(8,128)(2,1)S(1)} %add_convert_fusion.5), channel_id=1, source_target_pairs={{0,2},{1,3},{2,0},{3,1},{4,6},{5,7},{6,4},{7,5},{8,10},{9,11},{10,... | collective-permute-start | bytes 786440 | tf_op jit(solution)/shard_map/ppermute | solution.py:300
  111.9 14.8 %collective-permute-start.16 = (bf16[1,128,1024]{2,1,0:T(8,128)(2,1)S(1)}, bf16[1,128,1024]{2,1,0:T(8,128)(2,1)S(1)}, u32[]{:S(2)}, u32[]{:S(2)}) collective-permute-start(bf16[1,128,1024]{2,1,0:T(8,128)(2,1)S(1)} %add_convert_fusion.4), channel_id=1, source_target_pairs={{0,2},{1,3},{2,0},{3,1},{4,6},{5,7},{6,4},{7,5},{8,10},{9,11},{10,... | collective-permute-start | bytes 786440 | tf_op jit(solution)/shard_map/ppermute | solution.py:300
  127.9 5.2 %collective-permute-start.20 = (bf16[3,4,224,512]{3,2,1,0:T(8,128)(2,1)S(1)}, bf16[3,4,224,512]{3,2,1,0:T(8,128)(2,1)S(1)}, u32[]{:S(2)}, u32[]{:S(2)}) collective-permute-start(bf16[3,4,224,512]{3,2,1,0:T(8,128)(2,1)S(1)} %shard_map.69), channel_id=1, source_target_pairs={{0,4},{4,0},{8,12},{12,8},{16,20},{20,16},{24,28},{28,24},{1,5},{5... | collective-permute-start | bytes 8257544 | tf_op jit(solution)/shard_map/ppermute | solution.py:297
  137.1 14.0 %collective-permute-start.21 = (bf16[2,128,1024]{2,1,0:T(8,128)(2,1)S(1)}, bf16[2,128,1024]{2,1,0:T(8,128)(2,1)S(1)}, u32[]{:S(2)}, u32[]{:S(2)}) collective-permute-start(bf16[2,128,1024]{2,1,0:T(8,128)(2,1)S(1)} %get-tuple-element.133), channel_id=1, source_target_pairs={{0,1},{1,0},{2,3},{3,2},{4,5},{5,4},{6,7},{7,6},{8,9},{9,8},{10,11... | collective-permute-start | bytes 1572872 | tf_op jit(solution)/shard_map/ppermute | solution.py:300
  151.2 18.8 %collective-permute-start.23 = (bf16[2,128,1024]{2,1,0:T(8,128)(2,1)S(1)}, bf16[2,128,1024]{2,1,0:T(8,128)(2,1)S(1)}, u32[]{:S(2)}, u32[]{:S(2)}) collective-permute-start(bf16[2,128,1024]{2,1,0:T(8,128)(2,1)S(1)} %get-tuple-element.140), channel_id=1, source_target_pairs={{0,1},{1,0},{2,3},{3,2},{4,5},{5,4},{6,7},{7,6},{8,9},{9,8},{10,11... | collective-permute-start | bytes 1572872 | tf_op jit(solution)/shard_map/ppermute | solution.py:300
  151.9 18.2 %collective-permute-start.22 = (bf16[1,128,1024]{2,1,0:T(8,128)(2,1)S(1)}, bf16[1,128,1024]{2,1,0:T(8,128)(2,1)S(1)}, u32[]{:S(2)}, u32[]{:S(2)}) collective-permute-start(bf16[1,128,1024]{2,1,0:T(8,128)(2,1)S(1)} %add_convert_fusion.3), channel_id=1, source_target_pairs={{0,2},{1,3},{2,0},{3,1},{4,6},{5,7},{6,4},{7,5},{8,10},{9,11},{10,... | collective-permute-start | bytes 786440 | tf_op jit(solution)/shard_map/ppermute | solution.py:300
  154.8 37.9 %collective-permute-start.27 = (bf16[3,224,512]{2,1,0:T(8,128)(2,1)S(1)}, bf16[3,224,512]{2,1,0:T(8,128)(2,1)S(1)}, u32[]{:S(2)}, u32[]{:S(2)}) collective-permute-start(bf16[3,224,512]{2,1,0:T(8,128)(2,1)S(1)} %get-tuple-element.145), channel_id=1, source_target_pairs={{0,8},{4,12},{8,0},{12,4},{16,24},{20,28},{24,16},{28,20},{1,9},{5... | collective-permute-start | bytes 2064392 | tf_op jit(solution)/shard_map/ppermute | solution.py:294
  155.5 37.1 %collective-permute-start.28 = (bf16[3,224,512]{2,1,0:T(8,128)(2,1)S(1)}, bf16[3,224,512]{2,1,0:T(8,128)(2,1)S(1)}, u32[]{:S(2)}, u32[]{:S(2)}) collective-permute-start(bf16[3,224,512]{2,1,0:T(8,128)(2,1)S(1)} %get-tuple-element.146), channel_id=1, source_target_pairs={{0,16},{4,20},{8,24},{12,28},{16,0},{20,4},{24,8},{28,12},{1,17},{... | collective-permute-start | bytes 2064392 | tf_op jit(solution)/shard_map/ppermute | solution.py:294
  156.6 36.1 %collective-permute-start.29 = (bf16[3,224,512]{2,1,0:T(8,128)(2,1)S(1)}, bf16[3,224,512]{2,1,0:T(8,128)(2,1)S(1)}, u32[]{:S(2)}, u32[]{:S(2)}) collective-permute-start(bf16[3,224,512]{2,1,0:T(8,128)(2,1)S(1)} %get-tuple-element.147), channel_id=1, source_target_pairs={{0,24},{4,28},{8,16},{12,20},{16,8},{20,12},{24,0},{28,4},{1,25},{... | collective-permute-start | bytes 2064392 | tf_op jit(solution)/shard_map/ppermute | solution.py:294
  170.6 11.4 %collective-permute-start.24 = (bf16[128,1024]{1,0:T(8,128)(2,1)S(1)}, bf16[128,1024]{1,0:T(8,128)(2,1)S(1)}, u32[]{:S(2)}, u32[]{:S(2)}) collective-permute-start(bf16[128,1024]{1,0:T(8,128)(2,1)S(1)} %shard_map.72.refs_0_), channel_id=1, source_target_pairs={{0,1},{1,0},{2,3},{3,2},{4,5},{5,4},{6,7},{7,6},{8,9},{9,8},{10,11... | collective-permute-start | bytes 786440 | tf_op jit(solution)/shard_map/ppermute | solution.py:300
  172.5 19.7 %collective-permute-start.30 = (bf16[1,128,1024]{2,1,0:T(8,128)(2,1)S(1)}, bf16[1,128,1024]{2,1,0:T(8,128)(2,1)S(1)}, u32[]{:S(2)}, u32[]{:S(2)}) collective-permute-start(bf16[1,128,1024]{2,1,0:T(8,128)(2,1)S(1)} %add_convert_fusion.2), channel_id=1, source_target_pairs={{0,2},{1,3},{2,0},{3,1},{4,6},{5,7},{6,4},{7,5},{8,10},{9,11},{10,... | collective-permute-start | bytes 786440 | tf_op jit(solution)/shard_map/ppermute | solution.py:300
  181.9 14.7 %collective-permute-start.25 = (bf16[128,1024]{1,0:T(8,128)(2,1)S(1)}, bf16[128,1024]{1,0:T(8,128)(2,1)S(1)}, u32[]{:S(2)}, u32[]{:S(2)}) collective-permute-start(bf16[128,1024]{1,0:T(8,128)(2,1)S(1)} %shard_map.72.refs_0_), channel_id=1, source_target_pairs={{0,2},{1,3},{2,0},{3,1},{4,6},{5,7},{6,4},{7,5},{8,10},{9,11},{10,... | collective-permute-start | bytes 786440 | tf_op jit(solution)/shard_map/ppermute | solution.py:300
  197.8 13.3 %collective-permute-start.31 = (bf16[3,4,224,512]{3,2,1,0:T(8,128)(2,1)S(1)}, bf16[3,4,224,512]{3,2,1,0:T(8,128)(2,1)S(1)}, u32[]{:S(2)}, u32[]{:S(2)}) collective-permute-start(bf16[3,4,224,512]{3,2,1,0:T(8,128)(2,1)S(1)} %shard_map.74), channel_id=1, source_target_pairs={{0,4},{4,0},{8,12},{12,8},{16,20},{20,16},{24,28},{28,24},{1,5},{5... | collective-permute-start | bytes 8257544 | tf_op jit(solution)/shard_map/ppermute | solution.py:297
  197.8 13.3 %collective-permute-start.26 = (bf16[128,1024]{1,0:T(8,128)(2,1)S(1)}, bf16[128,1024]{1,0:T(8,128)(2,1)S(1)}, u32[]{:S(2)}, u32[]{:S(2)}) collective-permute-start(bf16[128,1024]{1,0:T(8,128)(2,1)S(1)} %collective-permute-done.25.refs_2_), channel_id=1, source_target_pairs={{0,1},{1,0},{2,3},{3,2},{4,5},{5,4},{6,7},{7,6},{8,9},{9,8},{10,11... | collective-permute-start | bytes 786440 | tf_op jit(solution)/shard_map/ppermute | solution.py:300
  197.9 18.9 %collective-permute-start.38 = (bf16[128,1024]{1,0:T(8,128)(2,1)S(1)}, bf16[128,1024]{1,0:T(8,128)(2,1)}, u32[]{:S(2)}, u32[]{:S(2)}) collective-permute-start(bf16[128,1024]{1,0:T(8,128)(2,1)S(1)} %shard_map.73.refs_0_), channel_id=1, source_target_pairs={{0,2},{1,3},{2,0},{3,1},{4,6},{5,7},{6,4},{7,5},{8,10},{9,11},{10,... | collective-permute-start | bytes 786440 | tf_op jit(solution)/shard_map/ppermute | solution.py:300
  216.8 9.3 %collective-permute-start.39 = (bf16[128,1024]{1,0:T(8,128)(2,1)S(1)}, bf16[128,1024]{1,0:T(8,128)(2,1)}, u32[]{:S(2)}, u32[]{:S(2)}) collective-permute-start(bf16[128,1024]{1,0:T(8,128)(2,1)S(1)} %shard_map.73.refs_0_), channel_id=1, source_target_pairs={{0,1},{1,0},{2,3},{3,2},{4,5},{5,4},{6,7},{7,6},{8,9},{9,8},{10,11... | collective-permute-start | bytes 786440 | tf_op jit(solution)/shard_map/ppermute | solution.py:300
  216.8 13.7 %collective-permute-start.40 = (bf16[128,1024]{1,0:T(8,128)(2,1)}, bf16[128,1024]{1,0:T(8,128)(2,1)}, u32[]{:S(2)}, u32[]{:S(2)}) collective-permute-start(bf16[128,1024]{1,0:T(8,128)(2,1)} %collective-permute-done.38.refs_2_), channel_id=1, source_target_pairs={{0,1},{1,0},{2,3},{3,2},{4,5},{5,4},{6,7},{7,6},{8,9},{9,8},{10,11... | collective-permute-start | bytes 786440 | tf_op jit(solution)/shard_map/ppermute | solution.py:300
  218.8 19.6 %collective-permute-start.32 = (bf16[128,1792]{1,0:T(8,128)(2,1)}, bf16[128,1792]{1,0:T(8,128)(2,1)}, u32[]{:S(2)}, u32[]{:S(2)}) collective-permute-start(bf16[128,1792]{1,0:T(8,128)(2,1)} %get-tuple-element.159), channel_id=1, source_target_pairs={{0,8},{4,12},{8,0},{12,4},{16,24},{20,28},{24,16},{28,20},{1,9},{5... | collective-permute-start | bytes 1376264 | tf_op jit(solution)/shard_map/ppermute | solution.py:294
  219.6 21.5 %collective-permute-start.33 = (bf16[128,1792]{1,0:T(8,128)(2,1)}, bf16[128,1792]{1,0:T(8,128)(2,1)}, u32[]{:S(2)}, u32[]{:S(2)}) collective-permute-start(bf16[128,1792]{1,0:T(8,128)(2,1)} %get-tuple-element.160), channel_id=1, source_target_pairs={{0,16},{4,20},{8,24},{12,28},{16,0},{20,4},{24,8},{28,12},{1,17},{... | collective-permute-start | bytes 1376264 | tf_op jit(solution)/shard_map/ppermute | solution.py:294
  220.8 20.3 %collective-permute-start.34 = (bf16[128,1792]{1,0:T(8,128)(2,1)}, bf16[128,1792]{1,0:T(8,128)(2,1)}, u32[]{:S(2)}, u32[]{:S(2)}) collective-permute-start(bf16[128,1792]{1,0:T(8,128)(2,1)} %get-tuple-element.161), channel_id=1, source_target_pairs={{0,24},{4,28},{8,16},{12,20},{16,8},{20,12},{24,0},{28,4},{1,25},{... | collective-permute-start | bytes 1376264 | tf_op jit(solution)/shard_map/ppermute | solution.py:294
  241.1 13.5 %collective-permute-start.41 = (bf16[128,1792]{1,0:T(8,128)(2,1)S(1)}, bf16[128,1792]{1,0:T(8,128)(2,1)S(1)}, u32[]{:S(2)}, u32[]{:S(2)}) collective-permute-start(bf16[128,1792]{1,0:T(8,128)(2,1)S(1)} %get-tuple-element.169), channel_id=1, source_target_pairs={{0,8},{4,12},{8,0},{12,4},{16,24},{20,28},{24,16},{28,20},{1,9},{5... | collective-permute-start | bytes 1376264 | tf_op jit(solution)/shard_map/ppermute | solution.py:294
  242.4 20.0 %collective-permute-start.42 = (bf16[128,1792]{1,0:T(8,128)(2,1)S(1)}, bf16[128,1792]{1,0:T(8,128)(2,1)S(1)}, u32[]{:S(2)}, u32[]{:S(2)}) collective-permute-start(bf16[128,1792]{1,0:T(8,128)(2,1)S(1)} %get-tuple-element.170), channel_id=1, source_target_pairs={{0,16},{4,20},{8,24},{12,28},{16,0},{20,4},{24,8},{28,12},{1,17},{... | collective-permute-start | bytes 1376264 | tf_op jit(solution)/shard_map/ppermute | solution.py:294
  243.2 19.1 %collective-permute-start.43 = (bf16[128,1792]{1,0:T(8,128)(2,1)S(1)}, bf16[128,1792]{1,0:T(8,128)(2,1)S(1)}, u32[]{:S(2)}, u32[]{:S(2)}) collective-permute-start(bf16[128,1792]{1,0:T(8,128)(2,1)S(1)} %get-tuple-element.171), channel_id=1, source_target_pairs={{0,24},{4,28},{8,16},{12,20},{16,8},{20,12},{24,0},{28,4},{1,25},{... | collective-permute-start | bytes 1376264 | tf_op jit(solution)/shard_map/ppermute | solution.py:294
  246.2 19.4 %collective-permute-start.35 = (bf16[32,1792]{1,0:T(8,128)(2,1)S(1)}, bf16[32,1792]{1,0:T(8,128)(2,1)S(1)}, u32[]{:S(2)}, u32[]{:S(2)}) collective-permute-start(bf16[32,1792]{1,0:T(8,128)(2,1)S(1)} %get-tuple-element.187), channel_id=1, source_target_pairs={{0,1},{1,0},{2,3},{3,2},{4,5},{5,4},{6,7},{7,6},{8,9},{9,8},{10,11... | collective-permute-start | bytes 344072 | tf_op jit(solution)/shard_map/ppermute | solution.py:300
  246.6 20.4 %collective-permute-start.36 = (bf16[32,1792]{1,0:T(8,128)(2,1)S(1)}, bf16[32,1792]{1,0:T(8,128)(2,1)S(1)}, u32[]{:S(2)}, u32[]{:S(2)}) collective-permute-start(bf16[32,1792]{1,0:T(8,128)(2,1)S(1)} %get-tuple-element.186), channel_id=1, source_target_pairs={{0,2},{1,3},{2,0},{3,1},{4,6},{5,7},{6,4},{7,5},{8,10},{9,11},{10,... | collective-permute-start | bytes 344072 | tf_op jit(solution)/shard_map/ppermute | solution.py:300
  254.6 12.5 %collective-permute-start.37 = (bf16[32,1792]{1,0:T(8,128)(2,1)S(1)}, bf16[32,1792]{1,0:T(8,128)(2,1)S(1)}, u32[]{:S(2)}, u32[]{:S(2)}) collective-permute-start(bf16[32,1792]{1,0:T(8,128)(2,1)S(1)} %get-tuple-element.185), channel_id=1, source_target_pairs={{0,3},{1,2},{2,1},{3,0},{4,7},{5,6},{6,5},{7,4},{8,11},{9,10},{10,... | collective-permute-start | bytes 344072 | tf_op jit(solution)/shard_map/ppermute | solution.py:300
  262.6 6.5 %collective-permute-start.44 = (bf16[32,1792]{1,0:T(8,128)(2,1)S(1)}, bf16[32,1792]{1,0:T(8,128)(2,1)S(1)}, u32[]{:S(2)}, u32[]{:S(2)}) collective-permute-start(bf16[32,1792]{1,0:T(8,128)(2,1)S(1)} %get-tuple-element.183), channel_id=1, source_target_pairs={{0,1},{1,0},{2,3},{3,2},{4,5},{5,4},{6,7},{7,6},{8,9},{9,8},{10,11... | collective-permute-start | bytes 344072 | tf_op jit(solution)/shard_map/ppermute | solution.py:300
  263.3 9.1 %collective-permute-start.45 = (bf16[32,1792]{1,0:T(8,128)(2,1)S(1)}, bf16[32,1792]{1,0:T(8,128)(2,1)S(1)}, u32[]{:S(2)}, u32[]{:S(2)}) collective-permute-start(bf16[32,1792]{1,0:T(8,128)(2,1)S(1)} %get-tuple-element.182), channel_id=1, source_target_pairs={{0,2},{1,3},{2,0},{3,1},{4,6},{5,7},{6,4},{7,5},{8,10},{9,11},{10,... | collective-permute-start | bytes 344072 | tf_op jit(solution)/shard_map/ppermute | solution.py:300
  265.6 6.8 %collective-permute-start.46 = (bf16[32,1792]{1,0:T(8,128)(2,1)S(1)}, bf16[32,1792]{1,0:T(8,128)(2,1)S(1)}, u32[]{:S(2)}, u32[]{:S(2)}) collective-permute-start(bf16[32,1792]{1,0:T(8,128)(2,1)S(1)} %get-tuple-element.181), channel_id=1, source_target_pairs={{0,3},{1,2},{2,1},{3,0},{4,7},{5,6},{6,5},{7,4},{8,11},{9,10},{10,... | collective-permute-start | bytes 344072 | tf_op jit(solution)/shard_map/ppermute | solution.py:300
  (13 other events, 160.2 us)

commit v13 on v12

--- a/solution.py
+++ b/solution.py
@@ -351,21 +351,23 @@
     toks = after(toks, up_blocks)
     up_same = chip_exchange(after(up_blocks, toks))
 
-    def products(weights, behind, parts):
-        sums, routings = [], []
+    def products(weights, chained, late):
+        sums, routings, parts, behind = [], [], [], []
         for half in range(HALVES):
-            left = after(toks[half], parts)
+            left = after(toks[half], [parts, late if half else []])
             *parts, routing = picked_sums(place, left, weights, slots)
-            terms, behind = level_sums(*parts, behind)
-            sums.append((terms, behind))
+            terms, marks = level_sums(*parts, behind)
+            behind = marks if chained else [(), *marks[1:]]
+            sums.append((terms, marks))
             routings.append(routing)
         return sums, routings
 
-    gate_sums, routings = products(gate_pair, [], [])
-    up_joined = join_blocks(place, up_weight, after(up_same, gate_sums[-1][1]))
+    gate_sums, routings = products(gate_pair, False, [])
+    ready = [gate_sums[0][1], gate_sums[-1][1][0]]
+    up_joined = join_blocks(place, up_weight, after(up_same, ready))
     up_pair = core_exchange(up_joined)
     down_same = chip_exchange(after(blocks_of(down_weight), up_joined))
-    up_sums, _ = products(up_pair, [], gate_sums[-1][1])
+    up_sums, _ = products(up_pair, True, gate_sums[-1][1])
 
     held, first = [], [up_sums[-1][1][0]]
     bits = [n_tensor >> bit for bit in range(1, n_tensor.bit_length())]

time: 275 us -> 271 us (0.985)
  waiting for transfers between devices: 160 us -> 155 us
    ppermute x21, waiting for transfers between devices: 55.5 us -> 51.8 us  [to_chip(): return lax.ppermute(value, 'expert', pairs)]
    ppermute x3, waiting for transfers between devices: 5.09 us -> 2.18 us  [to_core(): return lax.ppermute(value, 'expert', [(s, s ^ 1) for s in range(n_expert)])]
  transfers between devices with their start and end apart: 47 -> 47, of which waited for: 23 -> 28; matrix products, arithmetic and copies ran while one was open for 1% -> 1% of each run, Pallas kernels for 8% -> 10%
where the time goes in v13:
time: 271 us
  waiting for transfers between devices  155 us (57%)
  starting transfers between devices  65.2 us (24%)
  Pallas kernels  37.1 us (14%)
  local copies, waits for them, and re-layouts  11.1 us (4%)
    ppermute x23, waiting for transfers between devices, to_level(): lax.ppermute(value, 'tensor', [(s, s ^ step) for s in range(n_tensor)])  101 us
    ppermute x21, waiting for transfers between devices, to_chip(): return lax.ppermute(value, 'expert', pairs)  51.8 us
    ppermute x23, starting transfers between devices, to_level(): lax.ppermute(value, 'tensor', [(s, s ^ step) for s in range(n_tensor)])  37.5 us
    ppermute x21, starting transfers between devices, to_chip(): return lax.ppermute(value, 'expert', pairs)  27.5 us
    pallas_call x4, Pallas kernels, picked_sums(): pl.pallas_call(functools.partial(pick_kernel, chips), in_specs=[SMEM_SPEC...  16.3 us
    pallas_call x2, Pallas kernels, down_sums(): pl.pallas_call(functools.partial(down_kernel, slots, levels), in_specs=[S...  10.9 us
    unnamed x28, local copies, waits for them, and re-layouts  7.17 us
  transfers between devices with their start and end apart: 47, of which 28 were waited for; matrix products, arithmetic and copies ran while one was open for 1% of the time, Pallas kernels for 10%

profile of v13, /device:TPU:0, one launch (start us, length us, event | category | flops | bytes accessed | tf_op | source)
XLA Modules:
  0.0 271.1 jit_solution(2607218781579811617)
XLA Ops:
  0.0 3.0 %constant_dynamic-slice_fusion.3 = (bf16[3,224,512]{2,1,0:T(8,128)(2,1)}, bf16[3,224,512]{2,1,0:T(8,128)(2,1)}, bf16[3,224,512]{2,1,0:T(8,128)(2,1)}) fusion(bf16[3,224,2048]{2,1,0:T(8,128)(2,1)} %own_ref.3, s32[]{:T(128)S(6)} %select_n.47, s32[]{:T(128)S(6)} %select_n.46, s32[]{:T(128)S(6)} %select_n.45), kind=kLoop, calls=%fused_computation.17 | loop fusion | bytes 4128780 | tf_op jit(solution)/shard_map/dynamic_slice | solution.py:324
  3.0 3.0 %collective-permute-start.10 = (bf16[3,224,512]{2,1,0:T(8,128)(2,1)}, bf16[3,224,512]{2,1,0:T(8,128)(2,1)S(1)}, u32[]{:S(2)}, u32[]{:S(2)}) collective-permute-start(bf16[3,224,512]{2,1,0:T(8,128)(2,1)} %get-tuple-element.166), channel_id=1, source_target_pairs={{0,16},{4,20},{8,24},{12,28},{16,0},{20,4},{24,8},{28,12},{1,17},{... | collective-permute-start | bytes 2064392 | tf_op jit(solution)/shard_map/ppermute | solution.py:294
  12.7 2.6 collective-permute-start.1
  15.5 6.1 %collective-permute-done.refs_1_ = bf16[64,1792]{1,0:T(8,128)(2,1)S(1)} collective-permute-done((bf16[64,1792]{1,0:T(8,128)(2,1)S(1)}, bf16[64,1792]{1,0:T(8,128)(2,1)S(1)}, u32[]{:S(2)}, u32[]{:S(2)}) %collective-permute-start) | collective-permute-done | bytes 229408 | tf_op jit(solution)/shard_map/ppermute | solution.py:300
  22.8 9.5 %collective-permute-done.1.refs_2_ = bf16[64,1792]{1,0:T(8,128)(2,1)} collective-permute-done((bf16[64,1792]{1,0:T(8,128)(2,1)}, bf16[64,1792]{1,0:T(8,128)(2,1)}, u32[]{:S(2)}, u32[]{:S(2)}) %collective-permute-start.1) | collective-permute-done | bytes 229408 | tf_op jit(solution)/shard_map/ppermute | solution.py:300
  37.4 1.8 collective-permute-start.6
  41.0 10.4 %collective-permute-done.3.refs_1_ = bf16[128,1920]{1,0:T(8,128)(2,1)S(1)} collective-permute-done((bf16[128,1920]{1,0:T(8,128)(2,1)S(1)}, bf16[128,1920]{1,0:T(8,128)(2,1)S(1)}, u32[]{:S(2)}, u32[]{:S(2)}) %collective-permute-start.3) | collective-permute-done | bytes 491552 | tf_op jit(solution)/shard_map/ppermute | solution.py:294
  51.4 7.4 %collective-permute-done.6.refs_1_ = bf16[128,1920]{1,0:T(8,128)(2,1)S(1)} collective-permute-done((bf16[128,1920]{1,0:T(8,128)(2,1)S(1)}, bf16[128,1920]{1,0:T(8,128)(2,1)S(1)}, u32[]{:S(2)}, u32[]{:S(2)}) %collective-permute-start.6) | collective-permute-done | bytes 491552 | tf_op jit(solution)/shard_map/ppermute | solution.py:294
  58.8 2.0 shard_map.66
  64.3 10.2 %collective-permute-done.5.refs_3_ = bf16[128,1920]{1,0:T(8,128)(2,1)S(1)} collective-permute-done((bf16[128,1920]{1,0:T(8,128)(2,1)S(1)}, bf16[128,1920]{1,0:T(8,128)(2,1)S(1)}, u32[]{:S(2)}, u32[]{:S(2)}) %collective-permute-start.5) | collective-permute-done | bytes 491552 | tf_op jit(solution)/shard_map/ppermute | solution.py:294
  75.9 4.1 %shard_map.67 = (bf16[2,128,1024]{2,1,0:T(8,128)(2,1)S(1)}, bf16[2,128,1024]{2,1,0:T(8,128)(2,1)S(1)}, bf16[4,128,128]{2,1,0:T(8,128)(2,1)S(1)}) custom-call(s32[3]{0:T(128)S(1)} %pad_add_fusion.place_ref, bf16[128,1920]{1,0:T(8,128)(2,1)S(1)} %get-tuple-element.95.refs_0_, bf16[128,1920]{1,0:T(8,128)(2,1)S(1)} %collective-permute-done.3.refs_1_, ...), custom_call_target="tpu_custom_call" | custom-call | flops 2818572288 | bytes 8388608 | tf_op jit(solution)/shard_map/pallas_call | solution.py:195
  80.0 2.0 collective-permute-start.13
  82.0 4.1 %shard_map.68 = (bf16[2,128,1024]{2,1,0:T(8,128)(2,1)S(1)}, bf16[2,128,1024]{2,1,0:T(8,128)(2,1)S(1)}, bf16[4,128,128]{2,1,0:T(8,128)(2,1)S(1)}) custom-call(s32[3]{0:T(128)S(1)} %pad_add_fusion.place_ref, bf16[128,1920]{1,0:T(8,128)(2,1)S(1)} %get-tuple-element.124.refs_0_, bf16[128,1920]{1,0:T(8,128)(2,1)S(1)} %collective-permute-done.6.refs_1_, ...), custom_call_target="tpu_custom_call" | custom-call | flops 2818572288 | bytes 8388608 | tf_op jit(solution)/shard_map/pallas_call | solution.py:195
  89.7 5.2 %collective-permute-done.13 = bf16[2,128,1024]{2,1,0:T(8,128)(2,1)S(1)} collective-permute-done((bf16[2,128,1024]{2,1,0:T(8,128)(2,1)S(1)}, bf16[2,128,1024]{2,1,0:T(8,128)(2,1)S(1)}, u32[]{:S(2)}, u32[]{:S(2)}) %collective-permute-start.13) | collective-permute-done | bytes 524320 | tf_op jit(solution)/shard_map/ppermute | solution.py:300
  94.9 3.2 %collective-permute-start.14 = (bf16[1,128,1024]{2,1,0:T(8,128)(2,1)S(1)}, bf16[1,128,1024]{2,1,0:T(8,128)(2,1)S(1)}, u32[]{:S(2)}, u32[]{:S(2)}) collective-permute-start(bf16[1,128,1024]{2,1,0:T(8,128)(2,1)S(1)} %add_convert_fusion.5), channel_id=1, source_target_pairs={{0,2},{1,3},{2,0},{3,1},{4,6},{5,7},{6,4},{7,5},{8,10},{9,11},{10,... | collective-permute-start | bytes 786440 | tf_op jit(solution)/shard_map/ppermute | solution.py:300
  98.2 12.1 %collective-permute-done.18 = bf16[2,128,1024]{2,1,0:T(8,128)(2,1)S(1)} collective-permute-done((bf16[2,128,1024]{2,1,0:T(8,128)(2,1)S(1)}, bf16[2,128,1024]{2,1,0:T(8,128)(2,1)S(1)}, u32[]{:S(2)}, u32[]{:S(2)}) %collective-permute-start.18) | collective-permute-done | bytes 524320 | tf_op jit(solution)/shard_map/ppermute | solution.py:300
  110.3 6.4 %collective-permute-done.16.refs_1_ = bf16[3,224,512]{2,1,0:T(8,128)(2,1)S(1)} collective-permute-done((bf16[3,224,512]{2,1,0:T(8,128)(2,1)S(1)}, bf16[3,224,512]{2,1,0:T(8,128)(2,1)S(1)}, u32[]{:S(2)}, u32[]{:S(2)}) %collective-permute-start.16) | collective-permute-done | bytes 688160 | tf_op jit(solution)/shard_map/ppermute | solution.py:294
  119.5 2.9 %collective-permute-start.22 = (bf16[1,128,1024]{2,1,0:T(8,128)(2,1)S(1)}, bf16[1,128,1024]{2,1,0:T(8,128)(2,1)S(1)}, u32[]{:S(2)}, u32[]{:S(2)}) collective-permute-start(bf16[1,128,1024]{2,1,0:T(8,128)(2,1)S(1)} %add_convert_fusion.4), channel_id=1, source_target_pairs={{0,2},{1,3},{2,0},{3,1},{4,6},{5,7},{6,4},{7,5},{8,10},{9,11},{10,... | collective-permute-start | bytes 786440 | tf_op jit(solution)/shard_map/ppermute | solution.py:300
  122.4 2.2 collective-permute-done.19
  124.6 4.1 %shard_map.70 = (bf16[2,128,1024]{2,1,0:T(8,128)(2,1)S(1)}, bf16[2,128,1024]{2,1,0:T(8,128)(2,1)S(1)}, bf16[4,128,128]{2,1,0:T(8,128)(2,1)}) custom-call(s32[3]{0:T(128)S(1)} %pad_add_fusion.place_ref, bf16[128,1920]{1,0:T(8,128)(2,1)S(1)} %get-tuple-element.95.refs_0_, bf16[128,1920]{1,0:T(8,128)(2,1)S(1)} %collective-permute-done.3.refs_1_, ...), custom_call_target="tpu_custom_call" | custom-call | flops 2818572288 | bytes 8388608 | tf_op jit(solution)/shard_map/pallas_call | solution.py:195
  130.4 4.6 %collective-permute-done.22.refs_2_ = bf16[1,128,1024]{2,1,0:T(8,128)(2,1)S(1)} collective-permute-done((bf16[1,128,1024]{2,1,0:T(8,128)(2,1)S(1)}, bf16[1,128,1024]{2,1,0:T(8,128)(2,1)S(1)}, u32[]{:S(2)}, u32[]{:S(2)}) %collective-permute-start.22) | collective-permute-done | bytes 262176 | tf_op jit(solution)/shard_map/ppermute | solution.py:300
  135.1 4.1 %shard_map.71 = (bf16[2,128,1024]{2,1,0:T(8,128)(2,1)S(1)}, bf16[2,128,1024]{2,1,0:T(8,128)(2,1)S(1)}, bf16[4,128,128]{2,1,0:T(8,128)(2,1)}) custom-call(s32[3]{0:T(128)S(1)} %pad_add_fusion.place_ref, bf16[128,1920]{1,0:T(8,128)(2,1)S(1)} %get-tuple-element.124.refs_0_, bf16[128,1920]{1,0:T(8,128)(2,1)S(1)} %collective-permute-done.6.refs_1_, ...), custom_call_target="tpu_custom_call" | custom-call | flops 2818572288 | bytes 8388608 | tf_op jit(solution)/shard_map/pallas_call | solution.py:195
  139.1 7.0 %collective-permute-done.20 = bf16[2,128,1024]{2,1,0:T(8,128)(2,1)S(1)} collective-permute-done((bf16[2,128,1024]{2,1,0:T(8,128)(2,1)S(1)}, bf16[2,128,1024]{2,1,0:T(8,128)(2,1)S(1)}, u32[]{:S(2)}, u32[]{:S(2)}) %collective-permute-start.20) | collective-permute-done | bytes 524320 | tf_op jit(solution)/shard_map/ppermute | solution.py:300
  146.3 3.7 %collective-permute-start.21 = (bf16[1,128,1024]{2,1,0:T(8,128)(2,1)S(1)}, bf16[1,128,1024]{2,1,0:T(8,128)(2,1)S(1)}, u32[]{:S(2)}, u32[]{:S(2)}) collective-permute-start(bf16[1,128,1024]{2,1,0:T(8,128)(2,1)S(1)} %add_convert_fusion.3), channel_id=1, source_target_pairs={{0,2},{1,3},{2,0},{3,1},{4,6},{5,7},{6,4},{7,5},{8,10},{9,11},{10,... | collective-permute-start | bytes 786440 | tf_op jit(solution)/shard_map/ppermute | solution.py:300
  153.9 11.9 %collective-permute-done.23 = bf16[2,128,1024]{2,1,0:T(8,128)(2,1)S(1)} collective-permute-done((bf16[2,128,1024]{2,1,0:T(8,128)(2,1)S(1)}, bf16[2,128,1024]{2,1,0:T(8,128)(2,1)S(1)}, u32[]{:S(2)}, u32[]{:S(2)}) %collective-permute-start.23) | collective-permute-done | bytes 524320 | tf_op jit(solution)/shard_map/ppermute | solution.py:300
  166.3 1.9 collective-permute-start.24
  168.3 1.8 collective-permute-start.30
  170.1 8.4 %collective-permute-done.24.refs_1_ = bf16[128,1024]{1,0:T(8,128)(2,1)S(1)} collective-permute-done((bf16[128,1024]{1,0:T(8,128)(2,1)S(1)}, bf16[128,1024]{1,0:T(8,128)(2,1)S(1)}, u32[]{:S(2)}, u32[]{:S(2)}) %collective-permute-start.24) | collective-permute-done | bytes 262176 | tf_op jit(solution)/shard_map/ppermute | solution.py:300
  178.5 2.1 collective-permute-start.25
  180.7 8.5 %collective-permute-done.30.refs_5_ = bf16[1,128,1024]{2,1,0:T(8,128)(2,1)S(1)} collective-permute-done((bf16[1,128,1024]{2,1,0:T(8,128)(2,1)S(1)}, bf16[1,128,1024]{2,1,0:T(8,128)(2,1)S(1)}, u32[]{:S(2)}, u32[]{:S(2)}) %collective-permute-start.30) | collective-permute-done | bytes 262176 | tf_op jit(solution)/shard_map/ppermute | solution.py:300
  189.7 3.8 %collective-permute-done.25.refs_2_ = bf16[128,1024]{1,0:T(8,128)(2,1)S(1)} collective-permute-done((bf16[128,1024]{1,0:T(8,128)(2,1)S(1)}, bf16[128,1024]{1,0:T(8,128)(2,1)S(1)}, u32[]{:S(2)}, u32[]{:S(2)}) %collective-permute-start.25) | collective-permute-done | bytes 262176 | tf_op jit(solution)/shard_map/ppermute | solution.py:300
  194.8 2.3 collective-permute-start.38
  197.1 11.0 %collective-permute-done.26.refs_3_ = bf16[128,1024]{1,0:T(8,128)(2,1)S(1)} collective-permute-done((bf16[128,1024]{1,0:T(8,128)(2,1)S(1)}, bf16[128,1024]{1,0:T(8,128)(2,1)S(1)}, u32[]{:S(2)}, u32[]{:S(2)}) %collective-permute-start.26) | collective-permute-done | bytes 262176 | tf_op jit(solution)/shard_map/ppermute | solution.py:300
  208.2 5.7 %shard_map.75 = (bf16[128,1792]{1,0:T(8,128)(2,1)S(1)}, bf16[128,1792]{1,0:T(8,128)(2,1)}, bf16[128,1792]{1,0:T(8,128)(2,1)}, bf16[128,1792]{1,0:T(8,128)(2,1)}) custom-call(s32[3]{0:T(128)S(1)} %pad_add_fusion.place_ref, bf16[4,128,128]{2,1,0:T(8,128)(2,1)S(1)} %get-tuple-element.102.routing_ref, bf16[128,1024]{1,0:T(8,128)(2,1)S(1)} %shard_map.72.refs_0_, ...), custom_call_target="tpu_custom_call" | custom-call | flops 2818572288 | bytes 8388608 | tf_op jit(solution)/shard_map/pallas_call | solution.py:263
  213.9 2.0 collective-permute-start.40
  219.4 3.8 %collective-permute-done.39.refs_1_ = bf16[128,1024]{1,0:T(8,128)(2,1)} collective-permute-done((bf16[128,1024]{1,0:T(8,128)(2,1)S(1)}, bf16[128,1024]{1,0:T(8,128)(2,1)}, u32[]{:S(2)}, u32[]{:S(2)}) %collective-permute-start.39) | collective-permute-done | bytes 262176 | tf_op jit(solution)/shard_map/ppermute | solution.py:300
  223.2 4.4 %collective-permute-done.40.refs_3_ = bf16[128,1024]{1,0:T(8,128)(2,1)} collective-permute-done((bf16[128,1024]{1,0:T(8,128)(2,1)}, bf16[128,1024]{1,0:T(8,128)(2,1)}, u32[]{:S(2)}, u32[]{:S(2)}) %collective-permute-start.40) | collective-permute-done | bytes 262176 | tf_op jit(solution)/shard_map/ppermute | solution.py:300
  228.5 1.8 copy-done.11
  230.2 5.2 %shard_map.76 = (bf16[128,1792]{1,0:T(8,128)(2,1)S(1)}, bf16[128,1792]{1,0:T(8,128)(2,1)S(1)}, bf16[128,1792]{1,0:T(8,128)(2,1)S(1)}, bf16[128,1792]{1,0:T(8,128)(2,1)S(1)}) custom-call(s32[3]{0:T(128)S(1)} %pad_add_fusion.place_ref, bf16[4,128,128]{2,1,0:T(8,128)(2,1)S(1)} %copy-done.9, bf16[128,1024]{1,0:T(8,128)(2,1)S(1)} %shard_map.73.refs_0_, ...), custom_call_target="tpu_custom_call" | custom-call | flops 2818572288 | bytes 8388608 | tf_op jit(solution)/shard_map/pallas_call | solution.py:263
  235.5 1.8 collective-permute-done.33
  243.8 2.3 collective-permute-start.36
  246.0 5.7 %collective-permute-done.41 = bf16[128,1792]{1,0:T(8,128)(2,1)S(1)} collective-permute-done((bf16[128,1792]{1,0:T(8,128)(2,1)S(1)}, bf16[128,1792]{1,0:T(8,128)(2,1)S(1)}, u32[]{:S(2)}, u32[]{:S(2)}) %collective-permute-start.41) | collective-permute-done | bytes 458784 | tf_op jit(solution)/shard_map/ppermute | solution.py:294
  251.7 2.1 collective-permute-start.37
  253.8 5.9 %collective-permute-done.42 = bf16[128,1792]{1,0:T(8,128)(2,1)S(1)} collective-permute-done((bf16[128,1792]{1,0:T(8,128)(2,1)S(1)}, bf16[128,1792]{1,0:T(8,128)(2,1)S(1)}, u32[]{:S(2)}, u32[]{:S(2)}) %collective-permute-start.42) | collective-permute-done | bytes 458784 | tf_op jit(solution)/shard_map/ppermute | solution.py:294
  260.6 1.9 collective-permute-start.45
  262.6 1.8 collective-permute-start.46
  265.7 2.2 collective-permute-done.45.refs_6_
  269.3 1.9 shard_map.77
  (113 shorter events, 49.0 us)
Async XLA Ops:
  3.0 34.4 %collective-permute-start.10 = (bf16[3,224,512]{2,1,0:T(8,128)(2,1)}, bf16[3,224,512]{2,1,0:T(8,128)(2,1)S(1)}, u32[]{:S(2)}, u32[]{:S(2)}) collective-permute-start(bf16[3,224,512]{2,1,0:T(8,128)(2,1)} %get-tuple-element.166), channel_id=1, source_target_pairs={{0,16},{4,20},{8,24},{12,28},{16,0},{20,4},{24,8},{28,12},{1,17},{... | collective-permute-start | bytes 2064392 | tf_op jit(solution)/shard_map/ppermute | solution.py:294
  6.0 33.3 %collective-permute-start.11 = (bf16[3,224,512]{2,1,0:T(8,128)(2,1)}, bf16[3,224,512]{2,1,0:T(8,128)(2,1)}, u32[]{:S(2)}, u32[]{:S(2)}) collective-permute-start(bf16[3,224,512]{2,1,0:T(8,128)(2,1)} %get-tuple-element.165), channel_id=1, source_target_pairs={{0,24},{4,28},{8,16},{12,20},{16,8},{20,12},{24,0},{28,4},{1,25},{... | collective-permute-start | bytes 2064392 | tf_op jit(solution)/shard_map/ppermute | solution.py:294
  11.1 10.5 %collective-permute-start = (bf16[64,1792]{1,0:T(8,128)(2,1)S(1)}, bf16[64,1792]{1,0:T(8,128)(2,1)S(1)}, u32[]{:S(2)}, u32[]{:S(2)}) collective-permute-start(bf16[64,1792]{1,0:T(8,128)(2,1)S(1)} %get-tuple-element.86), channel_id=1, source_target_pairs={{0,1},{1,0},{2,3},{3,2},{4,5},{5,4},{6,7},{7,6},{8,9},{9,8},{10,11... | collective-permute-start | bytes 688136 | tf_op jit(solution)/shard_map/ppermute | solution.py:300
  12.7 19.6 %collective-permute-start.1 = (bf16[64,1792]{1,0:T(8,128)(2,1)}, bf16[64,1792]{1,0:T(8,128)(2,1)}, u32[]{:S(2)}, u32[]{:S(2)}) collective-permute-start(bf16[64,1792]{1,0:T(8,128)(2,1)} %get-tuple-element.87), channel_id=1, source_target_pairs={{0,2},{1,3},{2,0},{3,1},{4,6},{5,7},{6,4},{7,5},{8,10},{9,11},{10,... | collective-permute-start | bytes 688136 | tf_op jit(solution)/shard_map/ppermute | solution.py:300
  15.3 17.0 %collective-permute-start.2 = (bf16[64,1792]{1,0:T(8,128)(2,1)}, bf16[64,1792]{1,0:T(8,128)(2,1)}, u32[]{:S(2)}, u32[]{:S(2)}) collective-permute-start(bf16[64,1792]{1,0:T(8,128)(2,1)} %get-tuple-element.88), channel_id=1, source_target_pairs={{0,3},{1,2},{2,1},{3,0},{4,7},{5,6},{6,5},{7,4},{8,11},{9,10},{10,... | collective-permute-start | bytes 688136 | tf_op jit(solution)/shard_map/ppermute | solution.py:300
  22.3 18.7 %collective-permute-start.9 = (bf16[3,224,512]{2,1,0:T(8,128)(2,1)}, bf16[3,224,512]{2,1,0:T(8,128)(2,1)}, u32[]{:S(2)}, u32[]{:S(2)}) collective-permute-start(bf16[3,224,512]{2,1,0:T(8,128)(2,1)} %get-tuple-element.167), channel_id=1, source_target_pairs={{0,8},{4,12},{8,0},{12,4},{16,24},{20,28},{24,16},{28,20},{1,9},{5... | collective-permute-start | bytes 2064392 | tf_op jit(solution)/shard_map/ppermute | solution.py:294
  35.3 16.1 %collective-permute-start.3 = (bf16[128,1920]{1,0:T(8,128)(2,1)S(1)}, bf16[128,1920]{1,0:T(8,128)(2,1)S(1)}, u32[]{:S(2)}, u32[]{:S(2)}) collective-permute-start(bf16[128,1920]{1,0:T(8,128)(2,1)S(1)} %get-tuple-element.95.refs_0_), channel_id=1, source_target_pairs={{0,8},{4,12},{8,0},{12,4},{16,24},{20,28},{24,16},{28,20},{1,9},{5... | collective-permute-start | bytes 1474568 | tf_op jit(solution)/shard_map/ppermute | solution.py:294
  35.9 15.5 %collective-permute-start.4 = (bf16[128,1920]{1,0:T(8,128)(2,1)S(1)}, bf16[128,1920]{1,0:T(8,128)(2,1)S(1)}, u32[]{:S(2)}, u32[]{:S(2)}) collective-permute-start(bf16[128,1920]{1,0:T(8,128)(2,1)S(1)} %get-tuple-element.95.refs_0_), channel_id=1, source_target_pairs={{0,16},{4,20},{8,24},{12,28},{16,0},{20,4},{24,8},{28,12},{1,17},{... | collective-permute-start | bytes 1474568 | tf_op jit(solution)/shard_map/ppermute | solution.py:294
  37.4 21.3 %collective-permute-start.6 = (bf16[128,1920]{1,0:T(8,128)(2,1)S(1)}, bf16[128,1920]{1,0:T(8,128)(2,1)S(1)}, u32[]{:S(2)}, u32[]{:S(2)}) collective-permute-start(bf16[128,1920]{1,0:T(8,128)(2,1)S(1)} %get-tuple-element.124.refs_0_), channel_id=1, source_target_pairs={{0,8},{4,12},{8,0},{12,4},{16,24},{20,28},{24,16},{28,20},{1,9},{5... | collective-permute-start | bytes 1474568 | tf_op jit(solution)/shard_map/ppermute | solution.py:294
  39.3 19.5 %collective-permute-start.7 = (bf16[128,1920]{1,0:T(8,128)(2,1)S(1)}, bf16[128,1920]{1,0:T(8,128)(2,1)S(1)}, u32[]{:S(2)}, u32[]{:S(2)}) collective-permute-start(bf16[128,1920]{1,0:T(8,128)(2,1)S(1)} %get-tuple-element.124.refs_0_), channel_id=1, source_target_pairs={{0,16},{4,20},{8,24},{12,28},{16,0},{20,4},{24,8},{28,12},{1,17},{... | collective-permute-start | bytes 1474568 | tf_op jit(solution)/shard_map/ppermute | solution.py:294
  60.8 15.1 %collective-permute-start.12 = (bf16[3,4,224,512]{3,2,1,0:T(8,128)(2,1)S(1)}, bf16[3,4,224,512]{3,2,1,0:T(8,128)(2,1)S(1)}, u32[]{:S(2)}, u32[]{:S(2)}) collective-permute-start(bf16[3,4,224,512]{3,2,1,0:T(8,128)(2,1)S(1)} %shard_map.66), channel_id=1, source_target_pairs={{0,4},{4,0},{8,12},{12,8},{16,20},{20,16},{24,28},{28,24},{1,5},{5... | collective-permute-start | bytes 8257544 | tf_op jit(solution)/shard_map/ppermute | solution.py:297
  60.9 13.6 %collective-permute-start.5 = (bf16[128,1920]{1,0:T(8,128)(2,1)S(1)}, bf16[128,1920]{1,0:T(8,128)(2,1)S(1)}, u32[]{:S(2)}, u32[]{:S(2)}) collective-permute-start(bf16[128,1920]{1,0:T(8,128)(2,1)S(1)} %collective-permute-done.4.refs_2_), channel_id=1, source_target_pairs={{0,8},{4,12},{8,0},{12,4},{16,24},{20,28},{24,16},{28,20},{1,9},{5... | collective-permute-start | bytes 1474568 | tf_op jit(solution)/shard_map/ppermute | solution.py:294
  62.6 13.3 %collective-permute-start.8 = (bf16[128,1920]{1,0:T(8,128)(2,1)S(1)}, bf16[128,1920]{1,0:T(8,128)(2,1)S(1)}, u32[]{:S(2)}, u32[]{:S(2)}) collective-permute-start(bf16[128,1920]{1,0:T(8,128)(2,1)S(1)} %collective-permute-done.6.refs_1_), channel_id=1, source_target_pairs={{0,16},{4,20},{8,24},{12,28},{16,0},{20,4},{24,8},{28,12},{1,17},{... | collective-permute-start | bytes 1474568 | tf_op jit(solution)/shard_map/ppermute | solution.py:294
  80.0 14.9 %collective-permute-start.13 = (bf16[2,128,1024]{2,1,0:T(8,128)(2,1)S(1)}, bf16[2,128,1024]{2,1,0:T(8,128)(2,1)S(1)}, u32[]{:S(2)}, u32[]{:S(2)}) collective-permute-start(bf16[2,128,1024]{2,1,0:T(8,128)(2,1)S(1)} %get-tuple-element.104), channel_id=1, source_target_pairs={{0,1},{1,0},{2,3},{3,2},{4,5},{5,4},{6,7},{7,6},{8,9},{9,8},{10,11... | collective-permute-start | bytes 1572872 | tf_op jit(solution)/shard_map/ppermute | solution.py:300
  86.1 103.1 %copy-start.8 = (bf16[4,128,128]{2,1,0:T(8,128)(2,1)}, bf16[4,128,128]{2,1,0:T(8,128)(2,1)S(1)}, u32[]{:S(2)}) copy-start(bf16[4,128,128]{2,1,0:T(8,128)(2,1)S(1)} %get-tuple-element.138.routing_ref) | copy-start | bytes 393220
  86.1 24.2 %collective-permute-start.18 = (bf16[2,128,1024]{2,1,0:T(8,128)(2,1)S(1)}, bf16[2,128,1024]{2,1,0:T(8,128)(2,1)S(1)}, u32[]{:S(2)}, u32[]{:S(2)}) collective-permute-start(bf16[2,128,1024]{2,1,0:T(8,128)(2,1)S(1)} %get-tuple-element.117), channel_id=1, source_target_pairs={{0,1},{1,0},{2,3},{3,2},{4,5},{5,4},{6,7},{7,6},{8,9},{9,8},{10,11... | collective-permute-start | bytes 1572872 | tf_op jit(solution)/shard_map/ppermute | solution.py:300
  86.2 24.1 %collective-permute-start.15 = (bf16[3,224,512]{2,1,0:T(8,128)(2,1)S(1)}, bf16[3,224,512]{2,1,0:T(8,128)(2,1)S(1)}, u32[]{:S(2)}, u32[]{:S(2)}) collective-permute-start(bf16[3,224,512]{2,1,0:T(8,128)(2,1)S(1)} %get-tuple-element.109), channel_id=1, source_target_pairs={{0,8},{4,12},{8,0},{12,4},{16,24},{20,28},{24,16},{28,20},{1,9},{5... | collective-permute-start | bytes 2064392 | tf_op jit(solution)/shard_map/ppermute | solution.py:294
  86.8 30.0 %collective-permute-start.16 = (bf16[3,224,512]{2,1,0:T(8,128)(2,1)S(1)}, bf16[3,224,512]{2,1,0:T(8,128)(2,1)S(1)}, u32[]{:S(2)}, u32[]{:S(2)}) collective-permute-start(bf16[3,224,512]{2,1,0:T(8,128)(2,1)S(1)} %get-tuple-element.110), channel_id=1, source_target_pairs={{0,16},{4,20},{8,24},{12,28},{16,0},{20,4},{24,8},{28,12},{1,17},{... | collective-permute-start | bytes 2064392 | tf_op jit(solution)/shard_map/ppermute | solution.py:294
  88.3 30.0 %collective-permute-start.17 = (bf16[3,224,512]{2,1,0:T(8,128)(2,1)S(1)}, bf16[3,224,512]{2,1,0:T(8,128)(2,1)S(1)}, u32[]{:S(2)}, u32[]{:S(2)}) collective-permute-start(bf16[3,224,512]{2,1,0:T(8,128)(2,1)S(1)} %get-tuple-element.111), channel_id=1, source_target_pairs={{0,24},{4,28},{8,16},{12,20},{16,8},{20,12},{24,0},{28,4},{1,25},{... | collective-permute-start | bytes 2064392 | tf_op jit(solution)/shard_map/ppermute | solution.py:294
  94.9 15.4 %collective-permute-start.14 = (bf16[1,128,1024]{2,1,0:T(8,128)(2,1)S(1)}, bf16[1,128,1024]{2,1,0:T(8,128)(2,1)S(1)}, u32[]{:S(2)}, u32[]{:S(2)}) collective-permute-start(bf16[1,128,1024]{2,1,0:T(8,128)(2,1)S(1)} %add_convert_fusion.5), channel_id=1, source_target_pairs={{0,2},{1,3},{2,0},{3,1},{4,6},{5,7},{6,4},{7,5},{8,10},{9,11},{10,... | collective-permute-start | bytes 786440 | tf_op jit(solution)/shard_map/ppermute | solution.py:300
  119.4 5.2 %collective-permute-start.19 = (bf16[3,4,224,512]{3,2,1,0:T(8,128)(2,1)S(1)}, bf16[3,4,224,512]{3,2,1,0:T(8,128)(2,1)S(1)}, u32[]{:S(2)}, u32[]{:S(2)}) collective-permute-start(bf16[3,4,224,512]{3,2,1,0:T(8,128)(2,1)S(1)} %shard_map.69), channel_id=1, source_target_pairs={{0,4},{4,0},{8,12},{12,8},{16,20},{20,16},{24,28},{28,24},{1,5},{5... | collective-permute-start | bytes 8257544 | tf_op jit(solution)/shard_map/ppermute | solution.py:297
  119.5 15.5 %collective-permute-start.22 = (bf16[1,128,1024]{2,1,0:T(8,128)(2,1)S(1)}, bf16[1,128,1024]{2,1,0:T(8,128)(2,1)S(1)}, u32[]{:S(2)}, u32[]{:S(2)}) collective-permute-start(bf16[1,128,1024]{2,1,0:T(8,128)(2,1)S(1)} %add_convert_fusion.4), channel_id=1, source_target_pairs={{0,2},{1,3},{2,0},{3,1},{4,6},{5,7},{6,4},{7,5},{8,10},{9,11},{10,... | collective-permute-start | bytes 786440 | tf_op jit(solution)/shard_map/ppermute | solution.py:300
  128.7 17.5 %collective-permute-start.20 = (bf16[2,128,1024]{2,1,0:T(8,128)(2,1)S(1)}, bf16[2,128,1024]{2,1,0:T(8,128)(2,1)S(1)}, u32[]{:S(2)}, u32[]{:S(2)}) collective-permute-start(bf16[2,128,1024]{2,1,0:T(8,128)(2,1)S(1)} %get-tuple-element.123), channel_id=1, source_target_pairs={{0,1},{1,0},{2,3},{3,2},{4,5},{5,4},{6,7},{7,6},{8,9},{9,8},{10,11... | collective-permute-start | bytes 1572872 | tf_op jit(solution)/shard_map/ppermute | solution.py:300
  146.3 19.5 %collective-permute-start.23 = (bf16[2,128,1024]{2,1,0:T(8,128)(2,1)S(1)}, bf16[2,128,1024]{2,1,0:T(8,128)(2,1)S(1)}, u32[]{:S(2)}, u32[]{:S(2)}) collective-permute-start(bf16[2,128,1024]{2,1,0:T(8,128)(2,1)S(1)} %get-tuple-element.130), channel_id=1, source_target_pairs={{0,1},{1,0},{2,3},{3,2},{4,5},{5,4},{6,7},{7,6},{8,9},{9,8},{10,11... | collective-permute-start | bytes 1572872 | tf_op jit(solution)/shard_map/ppermute | solution.py:300
  146.3 19.5 %collective-permute-start.21 = (bf16[1,128,1024]{2,1,0:T(8,128)(2,1)S(1)}, bf16[1,128,1024]{2,1,0:T(8,128)(2,1)S(1)}, u32[]{:S(2)}, u32[]{:S(2)}) collective-permute-start(bf16[1,128,1024]{2,1,0:T(8,128)(2,1)S(1)} %add_convert_fusion.3), channel_id=1, source_target_pairs={{0,2},{1,3},{2,0},{3,1},{4,6},{5,7},{6,4},{7,5},{8,10},{9,11},{10,... | collective-permute-start | bytes 786440 | tf_op jit(solution)/shard_map/ppermute | solution.py:300
  150.3 39.4 %collective-permute-start.27 = (bf16[3,224,512]{2,1,0:T(8,128)(2,1)S(1)}, bf16[3,224,512]{2,1,0:T(8,128)(2,1)S(1)}, u32[]{:S(2)}, u32[]{:S(2)}) collective-permute-start(bf16[3,224,512]{2,1,0:T(8,128)(2,1)S(1)} %get-tuple-element.135), channel_id=1, source_target_pairs={{0,8},{4,12},{8,0},{12,4},{16,24},{20,28},{24,16},{28,20},{1,9},{5... | collective-permute-start | bytes 2064392 | tf_op jit(solution)/shard_map/ppermute | solution.py:294
  151.2 38.4 %collective-permute-start.28 = (bf16[3,224,512]{2,1,0:T(8,128)(2,1)S(1)}, bf16[3,224,512]{2,1,0:T(8,128)(2,1)S(1)}, u32[]{:S(2)}, u32[]{:S(2)}) collective-permute-start(bf16[3,224,512]{2,1,0:T(8,128)(2,1)S(1)} %get-tuple-element.136), channel_id=1, source_target_pairs={{0,16},{4,20},{8,24},{12,28},{16,0},{20,4},{24,8},{28,12},{1,17},{... | collective-permute-start | bytes 2064392 | tf_op jit(solution)/shard_map/ppermute | solution.py:294
  152.7 37.0 %collective-permute-start.29 = (bf16[3,224,512]{2,1,0:T(8,128)(2,1)S(1)}, bf16[3,224,512]{2,1,0:T(8,128)(2,1)S(1)}, u32[]{:S(2)}, u32[]{:S(2)}) collective-permute-start(bf16[3,224,512]{2,1,0:T(8,128)(2,1)S(1)} %get-tuple-element.137), channel_id=1, source_target_pairs={{0,24},{4,28},{8,16},{12,20},{16,8},{20,12},{24,0},{28,4},{1,25},{... | collective-permute-start | bytes 2064392 | tf_op jit(solution)/shard_map/ppermute | solution.py:294
  166.3 12.2 %collective-permute-start.24 = (bf16[128,1024]{1,0:T(8,128)(2,1)S(1)}, bf16[128,1024]{1,0:T(8,128)(2,1)S(1)}, u32[]{:S(2)}, u32[]{:S(2)}) collective-permute-start(bf16[128,1024]{1,0:T(8,128)(2,1)S(1)} %shard_map.72.refs_0_), channel_id=1, source_target_pairs={{0,1},{1,0},{2,3},{3,2},{4,5},{5,4},{6,7},{7,6},{8,9},{9,8},{10,11... | collective-permute-start | bytes 786440 | tf_op jit(solution)/shard_map/ppermute | solution.py:300
  168.3 20.9 %collective-permute-start.30 = (bf16[1,128,1024]{2,1,0:T(8,128)(2,1)S(1)}, bf16[1,128,1024]{2,1,0:T(8,128)(2,1)S(1)}, u32[]{:S(2)}, u32[]{:S(2)}) collective-permute-start(bf16[1,128,1024]{2,1,0:T(8,128)(2,1)S(1)} %add_convert_fusion.2), channel_id=1, source_target_pairs={{0,2},{1,3},{2,0},{3,1},{4,6},{5,7},{6,4},{7,5},{8,10},{9,11},{10,... | collective-permute-start | bytes 786440 | tf_op jit(solution)/shard_map/ppermute | solution.py:300
  178.5 15.0 %collective-permute-start.25 = (bf16[128,1024]{1,0:T(8,128)(2,1)S(1)}, bf16[128,1024]{1,0:T(8,128)(2,1)S(1)}, u32[]{:S(2)}, u32[]{:S(2)}) collective-permute-start(bf16[128,1024]{1,0:T(8,128)(2,1)S(1)} %shard_map.72.refs_0_), channel_id=1, source_target_pairs={{0,2},{1,3},{2,0},{3,1},{4,6},{5,7},{6,4},{7,5},{8,10},{9,11},{10,... | collective-permute-start | bytes 786440 | tf_op jit(solution)/shard_map/ppermute | solution.py:300
  194.7 13.5 %collective-permute-start.31 = (bf16[3,4,224,512]{3,2,1,0:T(8,128)(2,1)S(1)}, bf16[3,4,224,512]{3,2,1,0:T(8,128)(2,1)S(1)}, u32[]{:S(2)}, u32[]{:S(2)}) collective-permute-start(bf16[3,4,224,512]{3,2,1,0:T(8,128)(2,1)S(1)} %shard_map.74), channel_id=1, source_target_pairs={{0,4},{4,0},{8,12},{12,8},{16,20},{20,16},{24,28},{28,24},{1,5},{5... | collective-permute-start | bytes 8257544 | tf_op jit(solution)/shard_map/ppermute | solution.py:297
  194.8 13.4 %collective-permute-start.26 = (bf16[128,1024]{1,0:T(8,128)(2,1)S(1)}, bf16[128,1024]{1,0:T(8,128)(2,1)S(1)}, u32[]{:S(2)}, u32[]{:S(2)}) collective-permute-start(bf16[128,1024]{1,0:T(8,128)(2,1)S(1)} %collective-permute-done.25.refs_2_), channel_id=1, source_target_pairs={{0,1},{1,0},{2,3},{3,2},{4,5},{5,4},{6,7},{7,6},{8,9},{9,8},{10,11... | collective-permute-start | bytes 786440 | tf_op jit(solution)/shard_map/ppermute | solution.py:300
  194.8 19.0 %collective-permute-start.38 = (bf16[128,1024]{1,0:T(8,128)(2,1)S(1)}, bf16[128,1024]{1,0:T(8,128)(2,1)}, u32[]{:S(2)}, u32[]{:S(2)}) collective-permute-start(bf16[128,1024]{1,0:T(8,128)(2,1)S(1)} %shard_map.73.refs_0_), channel_id=1, source_target_pairs={{0,2},{1,3},{2,0},{3,1},{4,6},{5,7},{6,4},{7,5},{8,10},{9,11},{10,... | collective-permute-start | bytes 786440 | tf_op jit(solution)/shard_map/ppermute | solution.py:300
  213.8 9.3 %collective-permute-start.39 = (bf16[128,1024]{1,0:T(8,128)(2,1)S(1)}, bf16[128,1024]{1,0:T(8,128)(2,1)}, u32[]{:S(2)}, u32[]{:S(2)}) collective-permute-start(bf16[128,1024]{1,0:T(8,128)(2,1)S(1)} %shard_map.73.refs_0_), channel_id=1, source_target_pairs={{0,1},{1,0},{2,3},{3,2},{4,5},{5,4},{6,7},{7,6},{8,9},{9,8},{10,11... | collective-permute-start | bytes 786440 | tf_op jit(solution)/shard_map/ppermute | solution.py:300
  213.9 13.7 %collective-permute-start.40 = (bf16[128,1024]{1,0:T(8,128)(2,1)}, bf16[128,1024]{1,0:T(8,128)(2,1)}, u32[]{:S(2)}, u32[]{:S(2)}) collective-permute-start(bf16[128,1024]{1,0:T(8,128)(2,1)} %collective-permute-done.38.refs_2_), channel_id=1, source_target_pairs={{0,1},{1,0},{2,3},{3,2},{4,5},{5,4},{6,7},{7,6},{8,9},{9,8},{10,11... | collective-permute-start | bytes 786440 | tf_op jit(solution)/shard_map/ppermute | solution.py:300
  215.9 19.6 %collective-permute-start.32 = (bf16[128,1792]{1,0:T(8,128)(2,1)}, bf16[128,1792]{1,0:T(8,128)(2,1)}, u32[]{:S(2)}, u32[]{:S(2)}) collective-permute-start(bf16[128,1792]{1,0:T(8,128)(2,1)} %get-tuple-element.149), channel_id=1, source_target_pairs={{0,8},{4,12},{8,0},{12,4},{16,24},{20,28},{24,16},{28,20},{1,9},{5... | collective-permute-start | bytes 1376264 | tf_op jit(solution)/shard_map/ppermute | solution.py:294
  216.8 20.5 %collective-permute-start.33 = (bf16[128,1792]{1,0:T(8,128)(2,1)}, bf16[128,1792]{1,0:T(8,128)(2,1)}, u32[]{:S(2)}, u32[]{:S(2)}) collective-permute-start(bf16[128,1792]{1,0:T(8,128)(2,1)} %get-tuple-element.150), channel_id=1, source_target_pairs={{0,16},{4,20},{8,24},{12,28},{16,0},{20,4},{24,8},{28,12},{1,17},{... | collective-permute-start | bytes 1376264 | tf_op jit(solution)/shard_map/ppermute | solution.py:294
  218.2 20.1 %collective-permute-start.34 = (bf16[128,1792]{1,0:T(8,128)(2,1)}, bf16[128,1792]{1,0:T(8,128)(2,1)}, u32[]{:S(2)}, u32[]{:S(2)}) collective-permute-start(bf16[128,1792]{1,0:T(8,128)(2,1)} %get-tuple-element.151), channel_id=1, source_target_pairs={{0,24},{4,28},{8,16},{12,20},{16,8},{20,12},{24,0},{28,4},{1,25},{... | collective-permute-start | bytes 1376264 | tf_op jit(solution)/shard_map/ppermute | solution.py:294
  238.3 13.5 %collective-permute-start.41 = (bf16[128,1792]{1,0:T(8,128)(2,1)S(1)}, bf16[128,1792]{1,0:T(8,128)(2,1)S(1)}, u32[]{:S(2)}, u32[]{:S(2)}) collective-permute-start(bf16[128,1792]{1,0:T(8,128)(2,1)S(1)} %get-tuple-element.159), channel_id=1, source_target_pairs={{0,8},{4,12},{8,0},{12,4},{16,24},{20,28},{24,16},{28,20},{1,9},{5... | collective-permute-start | bytes 1376264 | tf_op jit(solution)/shard_map/ppermute | solution.py:294
  239.4 20.3 %collective-permute-start.42 = (bf16[128,1792]{1,0:T(8,128)(2,1)S(1)}, bf16[128,1792]{1,0:T(8,128)(2,1)S(1)}, u32[]{:S(2)}, u32[]{:S(2)}) collective-permute-start(bf16[128,1792]{1,0:T(8,128)(2,1)S(1)} %get-tuple-element.160), channel_id=1, source_target_pairs={{0,16},{4,20},{8,24},{12,28},{16,0},{20,4},{24,8},{28,12},{1,17},{... | collective-permute-start | bytes 1376264 | tf_op jit(solution)/shard_map/ppermute | solution.py:294
  240.6 19.1 %collective-permute-start.43 = (bf16[128,1792]{1,0:T(8,128)(2,1)S(1)}, bf16[128,1792]{1,0:T(8,128)(2,1)S(1)}, u32[]{:S(2)}, u32[]{:S(2)}) collective-permute-start(bf16[128,1792]{1,0:T(8,128)(2,1)S(1)} %get-tuple-element.161), channel_id=1, source_target_pairs={{0,24},{4,28},{8,16},{12,20},{16,8},{20,12},{24,0},{28,4},{1,25},{... | collective-permute-start | bytes 1376264 | tf_op jit(solution)/shard_map/ppermute | solution.py:294
  243.4 19.2 %collective-permute-start.35 = (bf16[32,1792]{1,0:T(8,128)(2,1)S(1)}, bf16[32,1792]{1,0:T(8,128)(2,1)S(1)}, u32[]{:S(2)}, u32[]{:S(2)}) collective-permute-start(bf16[32,1792]{1,0:T(8,128)(2,1)S(1)} %get-tuple-element.177), channel_id=1, source_target_pairs={{0,1},{1,0},{2,3},{3,2},{4,5},{5,4},{6,7},{7,6},{8,9},{9,8},{10,11... | collective-permute-start | bytes 344072 | tf_op jit(solution)/shard_map/ppermute | solution.py:300
  243.8 20.6 %collective-permute-start.36 = (bf16[32,1792]{1,0:T(8,128)(2,1)S(1)}, bf16[32,1792]{1,0:T(8,128)(2,1)S(1)}, u32[]{:S(2)}, u32[]{:S(2)}) collective-permute-start(bf16[32,1792]{1,0:T(8,128)(2,1)S(1)} %get-tuple-element.176), channel_id=1, source_target_pairs={{0,2},{1,3},{2,0},{3,1},{4,6},{5,7},{6,4},{7,5},{8,10},{9,11},{10,... | collective-permute-start | bytes 344072 | tf_op jit(solution)/shard_map/ppermute | solution.py:300
  251.7 12.7 %collective-permute-start.37 = (bf16[32,1792]{1,0:T(8,128)(2,1)S(1)}, bf16[32,1792]{1,0:T(8,128)(2,1)S(1)}, u32[]{:S(2)}, u32[]{:S(2)}) collective-permute-start(bf16[32,1792]{1,0:T(8,128)(2,1)S(1)} %get-tuple-element.175), channel_id=1, source_target_pairs={{0,3},{1,2},{2,1},{3,0},{4,7},{5,6},{6,5},{7,4},{8,11},{9,10},{10,... | collective-permute-start | bytes 344072 | tf_op jit(solution)/shard_map/ppermute | solution.py:300
  259.9 5.7 %collective-permute-start.44 = (bf16[32,1792]{1,0:T(8,128)(2,1)S(1)}, bf16[32,1792]{1,0:T(8,128)(2,1)S(1)}, u32[]{:S(2)}, u32[]{:S(2)}) collective-permute-start(bf16[32,1792]{1,0:T(8,128)(2,1)S(1)} %get-tuple-element.173), channel_id=1, source_target_pairs={{0,1},{1,0},{2,3},{3,2},{4,5},{5,4},{6,7},{7,6},{8,9},{9,8},{10,11... | collective-permute-start | bytes 344072 | tf_op jit(solution)/shard_map/ppermute | solution.py:300
  260.6 7.2 %collective-permute-start.45 = (bf16[32,1792]{1,0:T(8,128)(2,1)S(1)}, bf16[32,1792]{1,0:T(8,128)(2,1)S(1)}, u32[]{:S(2)}, u32[]{:S(2)}) collective-permute-start(bf16[32,1792]{1,0:T(8,128)(2,1)S(1)} %get-tuple-element.172), channel_id=1, source_target_pairs={{0,2},{1,3},{2,0},{3,1},{4,6},{5,7},{6,4},{7,5},{8,10},{9,11},{10,... | collective-permute-start | bytes 344072 | tf_op jit(solution)/shard_map/ppermute | solution.py:300
  262.6 6.7 %collective-permute-start.46 = (bf16[32,1792]{1,0:T(8,128)(2,1)S(1)}, bf16[32,1792]{1,0:T(8,128)(2,1)S(1)}, u32[]{:S(2)}, u32[]{:S(2)}) collective-permute-start(bf16[32,1792]{1,0:T(8,128)(2,1)S(1)} %get-tuple-element.171), channel_id=1, source_target_pairs={{0,3},{1,2},{2,1},{3,0},{4,7},{5,6},{6,5},{7,4},{8,11},{9,10},{10,... | collective-permute-start | bytes 344072 | tf_op jit(solution)/shard_map/ppermute | solution.py:300
  (13 other events, 158.4 us)

commit v14 on v13

--- a/solution.py
+++ b/solution.py
@@ -306,14 +306,16 @@
                 held[step + bit] = send(held[step], bit)
         return [held[step] for step in range(len(held))]
 
-    def level_sums(keep, send, behind):
+    def level_sums(keep, send, behind, pieces=1):
         terms, marks, bit = [keep], [], 1
         send = after(send, behind[:1])
         while True:
+            if 2 * bit == n_tensor:
+                got = [to_level(part, bit) for part in jnp.split(send, pieces, axis=1)]
+                terms.append(jnp.concatenate(got, axis=1) if pieces > 1 else got[0])
+                return terms, marks + [got]
             terms.append(to_level(send, bit))
             bit *= 2
-            if bit == n_tensor:
-                return terms, marks + [terms[-1]]
             send = sum(term[1::2].astype(jnp.float32) for term in terms).astype(jnp.bfloat16)
             terms = [term[::2] for term in terms]
             send = after(send, behind[len(marks) + 1 : len(marks) + 2])
@@ -356,14 +358,14 @@
         for half in range(HALVES):
             left = after(toks[half], [parts, late if half else []])
             *parts, routing = picked_sums(place, left, weights, slots)
-            terms, marks = level_sums(*parts, behind)
+            terms, marks = level_sums(*parts, behind, 1 if chained or not half else 2)
             behind = marks if chained else [(), *marks[1:]]
             sums.append((terms, marks))
             routings.append(routing)
         return sums, routings
 
     gate_sums, routings = products(gate_pair, False, [])
-    ready = [gate_sums[0][1], gate_sums[-1][1][0]]
+    ready = [gate_sums[0][1], gate_sums[-1][1][0], gate_sums[-1][1][-1][0]]
     up_joined = join_blocks(place, up_weight, after(up_same, ready))
     up_pair = core_exchange(up_joined)
     down_same = chip_exchange(after(blocks_of(down_weight), up_joined))

time: 271 us -> 274 us (1.011)
  waiting for transfers between devices: 155 us -> 160 us
    ppermute x3, waiting for transfers between devices: 2.18 us -> 5.09 us  [to_core(): return lax.ppermute(value, 'expert', [(s, s ^ 1) for s in range(n_expert)])]
    ppermute x23 -> x24, starting transfers between devices: 37.5 us -> 35.5 us  [to_level(): lax.ppermute(value, 'tensor', [(s, s ^ step) for s in range(n_tensor)])]
    ppermute x23 -> x24, waiting for transfers between devices: 101 us -> 103 us  [to_level(): lax.ppermute(value, 'tensor', [(s, s ^ step) for s in range(n_tensor)])]
  transfers between devices with their start and end apart: 47 -> 48, of which waited for: 28 -> 26; matrix products, arithmetic and copies ran while one was open for 1% -> 1% of each run, Pallas kernels for 10% -> 8%
where the time goes in v14:
time: 274 us
  waiting for transfers between devices  160 us (58%)
  starting transfers between devices  63.3 us (23%)
  Pallas kernels  37.1 us (14%)
  local copies, waits for them, and re-layouts  11.1 us (4%)
    ppermute x24, waiting for transfers between devices, to_level(): lax.ppermute(value, 'tensor', [(s, s ^ step) for s in range(n_tensor)])  103 us
    ppermute x21, waiting for transfers between devices, to_chip(): return lax.ppermute(value, 'expert', pairs)  51.5 us
    ppermute x24, starting transfers between devices, to_level(): lax.ppermute(value, 'tensor', [(s, s ^ step) for s in range(n_tensor)])  35.5 us
    ppermute x21, starting transfers between devices, to_chip(): return lax.ppermute(value, 'expert', pairs)  27.5 us
    pallas_call x4, Pallas kernels, picked_sums(): pl.pallas_call(functools.partial(pick_kernel, chips), in_specs=[SMEM_SPEC...  16.3 us
    pallas_call x2, Pallas kernels, down_sums(): pl.pallas_call(functools.partial(down_kernel, slots, levels), in_specs=[S...  10.9 us
    unnamed x28, local copies, waits for them, and re-layouts  7.14 us
  transfers between devices with their start and end apart: 48, of which 26 were waited for; matrix products, arithmetic and copies ran while one was open for 1% of the time, Pallas kernels for 8%

profile of v14, /device:TPU:0, one launch (start us, length us, event | category | flops | bytes accessed | tf_op | source)
XLA Modules:
  0.0 273.8 jit_solution(14152357708256300377)
XLA Ops:
  0.0 3.0 %constant_dynamic-slice_fusion.3 = (bf16[3,224,512]{2,1,0:T(8,128)(2,1)}, bf16[3,224,512]{2,1,0:T(8,128)(2,1)}, bf16[3,224,512]{2,1,0:T(8,128)(2,1)}) fusion(bf16[3,224,2048]{2,1,0:T(8,128)(2,1)} %own_ref.3, s32[]{:T(128)S(6)} %select_n.47, s32[]{:T(128)S(6)} %select_n.46, s32[]{:T(128)S(6)} %select_n.45), kind=kLoop, calls=%fused_computation.18 | loop fusion | bytes 4128780 | tf_op jit(solution)/shard_map/dynamic_slice | solution.py:326
  3.0 3.0 %collective-permute-start.10 = (bf16[3,224,512]{2,1,0:T(8,128)(2,1)}, bf16[3,224,512]{2,1,0:T(8,128)(2,1)S(1)}, u32[]{:S(2)}, u32[]{:S(2)}) collective-permute-start(bf16[3,224,512]{2,1,0:T(8,128)(2,1)} %get-tuple-element.166), channel_id=1, source_target_pairs={{0,16},{4,20},{8,24},{12,28},{16,0},{20,4},{24,8},{28,12},{1,17},{... | collective-permute-start | bytes 2064392 | tf_op jit(solution)/shard_map/ppermute | solution.py:294
  8.7 1.7 shard_map.64
  11.1 1.6 collective-permute-start
  12.7 2.6 collective-permute-start.1
  15.5 6.1 %collective-permute-done.refs_1_ = bf16[64,1792]{1,0:T(8,128)(2,1)S(1)} collective-permute-done((bf16[64,1792]{1,0:T(8,128)(2,1)S(1)}, bf16[64,1792]{1,0:T(8,128)(2,1)S(1)}, u32[]{:S(2)}, u32[]{:S(2)}) %collective-permute-start) | collective-permute-done | bytes 229408 | tf_op jit(solution)/shard_map/ppermute | solution.py:300
  22.8 9.5 %collective-permute-done.1.refs_2_ = bf16[64,1792]{1,0:T(8,128)(2,1)} collective-permute-done((bf16[64,1792]{1,0:T(8,128)(2,1)}, bf16[64,1792]{1,0:T(8,128)(2,1)}, u32[]{:S(2)}, u32[]{:S(2)}) %collective-permute-start.1) | collective-permute-done | bytes 229408 | tf_op jit(solution)/shard_map/ppermute | solution.py:300
  37.4 1.9 collective-permute-start.6
  40.9 10.4 %collective-permute-done.3.refs_1_ = bf16[128,1920]{1,0:T(8,128)(2,1)S(1)} collective-permute-done((bf16[128,1920]{1,0:T(8,128)(2,1)S(1)}, bf16[128,1920]{1,0:T(8,128)(2,1)S(1)}, u32[]{:S(2)}, u32[]{:S(2)}) %collective-permute-start.3) | collective-permute-done | bytes 491552 | tf_op jit(solution)/shard_map/ppermute | solution.py:294
  51.4 7.4 %collective-permute-done.6.refs_1_ = bf16[128,1920]{1,0:T(8,128)(2,1)S(1)} collective-permute-done((bf16[128,1920]{1,0:T(8,128)(2,1)S(1)}, bf16[128,1920]{1,0:T(8,128)(2,1)S(1)}, u32[]{:S(2)}, u32[]{:S(2)}) %collective-permute-start.6) | collective-permute-done | bytes 491552 | tf_op jit(solution)/shard_map/ppermute | solution.py:294
  58.7 2.0 shard_map.66
  60.8 1.8 collective-permute-start.5
  64.3 10.1 %collective-permute-done.5.refs_3_ = bf16[128,1920]{1,0:T(8,128)(2,1)S(1)} collective-permute-done((bf16[128,1920]{1,0:T(8,128)(2,1)S(1)}, bf16[128,1920]{1,0:T(8,128)(2,1)S(1)}, u32[]{:S(2)}, u32[]{:S(2)}) %collective-permute-start.5) | collective-permute-done | bytes 491552 | tf_op jit(solution)/shard_map/ppermute | solution.py:294
  75.9 4.1 %shard_map.67 = (bf16[2,128,1024]{2,1,0:T(8,128)(2,1)S(1)}, bf16[2,128,1024]{2,1,0:T(8,128)(2,1)S(1)}, bf16[4,128,128]{2,1,0:T(8,128)(2,1)S(1)}) custom-call(s32[3]{0:T(128)S(1)} %pad_add_fusion.place_ref, bf16[128,1920]{1,0:T(8,128)(2,1)S(1)} %get-tuple-element.95.refs_0_, bf16[128,1920]{1,0:T(8,128)(2,1)S(1)} %collective-permute-done.3.refs_1_, ...), custom_call_target="tpu_custom_call" | custom-call | flops 2818572288 | bytes 8388608 | tf_op jit(solution)/shard_map/pallas_call | solution.py:195
  80.0 2.0 collective-permute-start.13
  82.0 4.1 %shard_map.68 = (bf16[2,128,1024]{2,1,0:T(8,128)(2,1)S(1)}, bf16[2,128,1024]{2,1,0:T(8,128)(2,1)S(1)}, bf16[4,128,128]{2,1,0:T(8,128)(2,1)S(1)}) custom-call(s32[3]{0:T(128)S(1)} %pad_add_fusion.place_ref, bf16[128,1920]{1,0:T(8,128)(2,1)S(1)} %get-tuple-element.124.refs_0_, bf16[128,1920]{1,0:T(8,128)(2,1)S(1)} %collective-permute-done.6.refs_1_, ...), custom_call_target="tpu_custom_call" | custom-call | flops 2818572288 | bytes 8388608 | tf_op jit(solution)/shard_map/pallas_call | solution.py:195
  86.7 1.5 collective-permute-start.16
  89.7 5.2 %collective-permute-done.13 = bf16[2,128,1024]{2,1,0:T(8,128)(2,1)S(1)} collective-permute-done((bf16[2,128,1024]{2,1,0:T(8,128)(2,1)S(1)}, bf16[2,128,1024]{2,1,0:T(8,128)(2,1)S(1)}, u32[]{:S(2)}, u32[]{:S(2)}) %collective-permute-start.13) | collective-permute-done | bytes 524320 | tf_op jit(solution)/shard_map/ppermute | solution.py:300
  95.0 3.2 %collective-permute-start.14 = (bf16[1,128,1024]{2,1,0:T(8,128)(2,1)S(1)}, bf16[1,128,1024]{2,1,0:T(8,128)(2,1)S(1)}, u32[]{:S(2)}, u32[]{:S(2)}) collective-permute-start(bf16[1,128,1024]{2,1,0:T(8,128)(2,1)S(1)} %add_convert_fusion.5), channel_id=1, source_target_pairs={{0,2},{1,3},{2,0},{3,1},{4,6},{5,7},{6,4},{7,5},{8,10},{9,11},{10,... | collective-permute-start | bytes 786440 | tf_op jit(solution)/shard_map/ppermute | solution.py:300
  98.1 12.1 %collective-permute-done.18 = bf16[2,128,1024]{2,1,0:T(8,128)(2,1)S(1)} collective-permute-done((bf16[2,128,1024]{2,1,0:T(8,128)(2,1)S(1)}, bf16[2,128,1024]{2,1,0:T(8,128)(2,1)S(1)}, u32[]{:S(2)}, u32[]{:S(2)}) %collective-permute-start.18) | collective-permute-done | bytes 524320 | tf_op jit(solution)/shard_map/ppermute | solution.py:300
  110.3 2.6 collective-permute-start.19
  113.0 3.8 %collective-permute-done.16.refs_1_ = bf16[3,224,512]{2,1,0:T(8,128)(2,1)S(1)} collective-permute-done((bf16[3,224,512]{2,1,0:T(8,128)(2,1)S(1)}, bf16[3,224,512]{2,1,0:T(8,128)(2,1)S(1)}, u32[]{:S(2)}, u32[]{:S(2)}) %collective-permute-start.16) | collective-permute-done | bytes 688160 | tf_op jit(solution)/shard_map/ppermute | solution.py:294
  116.7 1.6 collective-permute-done.17.refs_2_
  120.0 5.1 %collective-permute-done.20 = bf16[3,4,224,512]{3,2,1,0:T(8,128)(2,1)S(1)} collective-permute-done((bf16[3,4,224,512]{3,2,1,0:T(8,128)(2,1)S(1)}, bf16[3,4,224,512]{3,2,1,0:T(8,128)(2,1)S(1)}, u32[]{:S(2)}, u32[]{:S(2)}) %collective-permute-start.20) | collective-permute-done | bytes 2752544 | tf_op jit(solution)/shard_map/ppermute | solution.py:297
  125.1 4.1 %shard_map.70 = (bf16[2,128,1024]{2,1,0:T(8,128)(2,1)S(1)}, bf16[2,128,1024]{2,1,0:T(8,128)(2,1)S(1)}, bf16[4,128,128]{2,1,0:T(8,128)(2,1)}) custom-call(s32[3]{0:T(128)S(1)} %pad_add_fusion.place_ref, bf16[128,1920]{1,0:T(8,128)(2,1)S(1)} %get-tuple-element.95.refs_0_, bf16[128,1920]{1,0:T(8,128)(2,1)S(1)} %collective-permute-done.3.refs_1_, ...), custom_call_target="tpu_custom_call" | custom-call | flops 2818572288 | bytes 8388608 | tf_op jit(solution)/shard_map/pallas_call | solution.py:195
  130.4 2.2 collective-permute-start.23
  132.6 12.1 %collective-permute-done.23 = bf16[1,64,1024]{2,1,0:T(8,128)(2,1)S(1)} collective-permute-done((bf16[1,64,1024]{2,1,0:T(8,128)(2,1)S(1)}, bf16[1,64,1024]{2,1,0:T(8,128)(2,1)S(1)}, u32[]{:S(2)}, u32[]{:S(2)}) %collective-permute-start.23) | collective-permute-done | bytes 131104 | tf_op jit(solution)/shard_map/ppermute | solution.py:300
  144.7 4.1 %shard_map.71 = (bf16[2,128,1024]{2,1,0:T(8,128)(2,1)S(1)}, bf16[2,128,1024]{2,1,0:T(8,128)(2,1)S(1)}, bf16[4,128,128]{2,1,0:T(8,128)(2,1)}) custom-call(s32[3]{0:T(128)S(1)} %pad_add_fusion.place_ref, bf16[128,1920]{1,0:T(8,128)(2,1)S(1)} %get-tuple-element.124.refs_0_, bf16[128,1920]{1,0:T(8,128)(2,1)S(1)} %collective-permute-done.6.refs_1_, ...), custom_call_target="tpu_custom_call" | custom-call | flops 2818572288 | bytes 8388608 | tf_op jit(solution)/shard_map/pallas_call | solution.py:195
  148.9 3.7 %collective-permute-start.24 = (bf16[2,128,1024]{2,1,0:T(8,128)(2,1)S(1)}, bf16[2,128,1024]{2,1,0:T(8,128)(2,1)S(1)}, u32[]{:S(2)}, u32[]{:S(2)}) collective-permute-start(bf16[2,128,1024]{2,1,0:T(8,128)(2,1)S(1)} %get-tuple-element.130), channel_id=1, source_target_pairs={{0,1},{1,0},{2,3},{3,2},{4,5},{5,4},{6,7},{7,6},{8,9},{9,8},{10,11... | collective-permute-start | bytes 1572872 | tf_op jit(solution)/shard_map/ppermute | solution.py:300
  156.5 13.1 %collective-permute-done.24 = bf16[2,128,1024]{2,1,0:T(8,128)(2,1)S(1)} collective-permute-done((bf16[2,128,1024]{2,1,0:T(8,128)(2,1)S(1)}, bf16[2,128,1024]{2,1,0:T(8,128)(2,1)S(1)}, u32[]{:S(2)}, u32[]{:S(2)}) %collective-permute-start.24) | collective-permute-done | bytes 524320 | tf_op jit(solution)/shard_map/ppermute | solution.py:300
  172.8 9.9 %collective-permute-done.25.refs_1_ = bf16[128,1024]{1,0:T(8,128)(2,1)S(1)} collective-permute-done((bf16[128,1024]{1,0:T(8,128)(2,1)S(1)}, bf16[128,1024]{1,0:T(8,128)(2,1)S(1)}, u32[]{:S(2)}, u32[]{:S(2)}) %collective-permute-start.25) | collective-permute-done | bytes 262176 | tf_op jit(solution)/shard_map/ppermute | solution.py:300
  184.6 11.1 %collective-permute-done.26.refs_2_ = bf16[128,1024]{1,0:T(8,128)(2,1)S(1)} collective-permute-done((bf16[128,1024]{1,0:T(8,128)(2,1)S(1)}, bf16[128,1024]{1,0:T(8,128)(2,1)S(1)}, u32[]{:S(2)}, u32[]{:S(2)}) %collective-permute-start.26) | collective-permute-done | bytes 262176 | tf_op jit(solution)/shard_map/ppermute | solution.py:300
  197.0 3.2 %collective-permute-start.39 = (bf16[128,1024]{1,0:T(8,128)(2,1)S(1)}, bf16[128,1024]{1,0:T(8,128)(2,1)}, u32[]{:S(2)}, u32[]{:S(2)}) collective-permute-start(bf16[128,1024]{1,0:T(8,128)(2,1)S(1)} %shard_map.73.refs_0_), channel_id=1, source_target_pairs={{0,2},{1,3},{2,0},{3,1},{4,6},{5,7},{6,4},{7,5},{8,10},{9,11},{10,... | collective-permute-start | bytes 786440 | tf_op jit(solution)/shard_map/ppermute | solution.py:300
  200.2 10.8 %collective-permute-done.27.refs_3_ = bf16[128,1024]{1,0:T(8,128)(2,1)S(1)} collective-permute-done((bf16[128,1024]{1,0:T(8,128)(2,1)S(1)}, bf16[128,1024]{1,0:T(8,128)(2,1)S(1)}, u32[]{:S(2)}, u32[]{:S(2)}) %collective-permute-start.27) | collective-permute-done | bytes 262176 | tf_op jit(solution)/shard_map/ppermute | solution.py:300
  211.1 5.7 %shard_map.75 = (bf16[128,1792]{1,0:T(8,128)(2,1)S(1)}, bf16[128,1792]{1,0:T(8,128)(2,1)}, bf16[128,1792]{1,0:T(8,128)(2,1)}, bf16[128,1792]{1,0:T(8,128)(2,1)}) custom-call(s32[3]{0:T(128)S(1)} %pad_add_fusion.place_ref, bf16[4,128,128]{2,1,0:T(8,128)(2,1)S(1)} %get-tuple-element.102.routing_ref, bf16[128,1024]{1,0:T(8,128)(2,1)S(1)} %shard_map.72.refs_0_, ...), custom_call_target="tpu_custom_call" | custom-call | flops 2818572288 | bytes 8388608 | tf_op jit(solution)/shard_map/pallas_call | solution.py:263
  216.8 2.0 collective-permute-start.41
  222.3 3.8 %collective-permute-done.40.refs_1_ = bf16[128,1024]{1,0:T(8,128)(2,1)} collective-permute-done((bf16[128,1024]{1,0:T(8,128)(2,1)S(1)}, bf16[128,1024]{1,0:T(8,128)(2,1)}, u32[]{:S(2)}, u32[]{:S(2)}) %collective-permute-start.40) | collective-permute-done | bytes 262176 | tf_op jit(solution)/shard_map/ppermute | solution.py:300
  226.1 4.4 %collective-permute-done.41.refs_3_ = bf16[128,1024]{1,0:T(8,128)(2,1)} collective-permute-done((bf16[128,1024]{1,0:T(8,128)(2,1)}, bf16[128,1024]{1,0:T(8,128)(2,1)}, u32[]{:S(2)}, u32[]{:S(2)}) %collective-permute-start.41) | collective-permute-done | bytes 262176 | tf_op jit(solution)/shard_map/ppermute | solution.py:300
  231.3 1.8 copy-done.11
  233.1 5.2 %shard_map.76 = (bf16[128,1792]{1,0:T(8,128)(2,1)S(1)}, bf16[128,1792]{1,0:T(8,128)(2,1)S(1)}, bf16[128,1792]{1,0:T(8,128)(2,1)S(1)}, bf16[128,1792]{1,0:T(8,128)(2,1)S(1)}) custom-call(s32[3]{0:T(128)S(1)} %pad_add_fusion.place_ref, bf16[4,128,128]{2,1,0:T(8,128)(2,1)S(1)} %copy-done.9, bf16[128,1024]{1,0:T(8,128)(2,1)S(1)} %shard_map.73.refs_0_, ...), custom_call_target="tpu_custom_call" | custom-call | flops 2818572288 | bytes 8388608 | tf_op jit(solution)/shard_map/pallas_call | solution.py:263
  238.4 2.7 collective-permute-done.34
  244.6 1.5 add_convert_fusion.1
  246.6 1.7 collective-permute-start.37
  248.3 6.2 %collective-permute-done.42 = bf16[128,1792]{1,0:T(8,128)(2,1)S(1)} collective-permute-done((bf16[128,1792]{1,0:T(8,128)(2,1)S(1)}, bf16[128,1792]{1,0:T(8,128)(2,1)S(1)}, u32[]{:S(2)}, u32[]{:S(2)}) %collective-permute-start.42) | collective-permute-done | bytes 458784 | tf_op jit(solution)/shard_map/ppermute | solution.py:294
  256.0 6.5 %collective-permute-done.43 = bf16[128,1792]{1,0:T(8,128)(2,1)S(1)} collective-permute-done((bf16[128,1792]{1,0:T(8,128)(2,1)S(1)}, bf16[128,1792]{1,0:T(8,128)(2,1)S(1)}, u32[]{:S(2)}, u32[]{:S(2)}) %collective-permute-start.43) | collective-permute-done | bytes 458784 | tf_op jit(solution)/shard_map/ppermute | solution.py:294
  265.0 2.3 collective-permute-start.47
  268.5 3.4 %collective-permute-done.46.refs_6_ = bf16[32,1792]{1,0:T(8,128)(2,1)S(1)} collective-permute-done((bf16[32,1792]{1,0:T(8,128)(2,1)S(1)}, bf16[32,1792]{1,0:T(8,128)(2,1)S(1)}, u32[]{:S(2)}, u32[]{:S(2)}) %collective-permute-start.46) | collective-permute-done | bytes 114720 | tf_op jit(solution)/shard_map/ppermute | solution.py:300
  272.0 1.9 shard_map.77
  (117 shorter events, 43.8 us)
Async XLA Ops:
  3.0 34.4 %collective-permute-start.10 = (bf16[3,224,512]{2,1,0:T(8,128)(2,1)}, bf16[3,224,512]{2,1,0:T(8,128)(2,1)S(1)}, u32[]{:S(2)}, u32[]{:S(2)}) collective-permute-start(bf16[3,224,512]{2,1,0:T(8,128)(2,1)} %get-tuple-element.166), channel_id=1, source_target_pairs={{0,16},{4,20},{8,24},{12,28},{16,0},{20,4},{24,8},{28,12},{1,17},{... | collective-permute-start | bytes 2064392 | tf_op jit(solution)/shard_map/ppermute | solution.py:294
  6.0 33.3 %collective-permute-start.11 = (bf16[3,224,512]{2,1,0:T(8,128)(2,1)}, bf16[3,224,512]{2,1,0:T(8,128)(2,1)}, u32[]{:S(2)}, u32[]{:S(2)}) collective-permute-start(bf16[3,224,512]{2,1,0:T(8,128)(2,1)} %get-tuple-element.165), channel_id=1, source_target_pairs={{0,24},{4,28},{8,16},{12,20},{16,8},{20,12},{24,0},{28,4},{1,25},{... | collective-permute-start | bytes 2064392 | tf_op jit(solution)/shard_map/ppermute | solution.py:294
  11.1 10.5 %collective-permute-start = (bf16[64,1792]{1,0:T(8,128)(2,1)S(1)}, bf16[64,1792]{1,0:T(8,128)(2,1)S(1)}, u32[]{:S(2)}, u32[]{:S(2)}) collective-permute-start(bf16[64,1792]{1,0:T(8,128)(2,1)S(1)} %get-tuple-element.86), channel_id=1, source_target_pairs={{0,1},{1,0},{2,3},{3,2},{4,5},{5,4},{6,7},{7,6},{8,9},{9,8},{10,11... | collective-permute-start | bytes 688136 | tf_op jit(solution)/shard_map/ppermute | solution.py:300
  12.7 19.6 %collective-permute-start.1 = (bf16[64,1792]{1,0:T(8,128)(2,1)}, bf16[64,1792]{1,0:T(8,128)(2,1)}, u32[]{:S(2)}, u32[]{:S(2)}) collective-permute-start(bf16[64,1792]{1,0:T(8,128)(2,1)} %get-tuple-element.87), channel_id=1, source_target_pairs={{0,2},{1,3},{2,0},{3,1},{4,6},{5,7},{6,4},{7,5},{8,10},{9,11},{10,... | collective-permute-start | bytes 688136 | tf_op jit(solution)/shard_map/ppermute | solution.py:300
  15.3 17.0 %collective-permute-start.2 = (bf16[64,1792]{1,0:T(8,128)(2,1)}, bf16[64,1792]{1,0:T(8,128)(2,1)}, u32[]{:S(2)}, u32[]{:S(2)}) collective-permute-start(bf16[64,1792]{1,0:T(8,128)(2,1)} %get-tuple-element.88), channel_id=1, source_target_pairs={{0,3},{1,2},{2,1},{3,0},{4,7},{5,6},{6,5},{7,4},{8,11},{9,10},{10,... | collective-permute-start | bytes 688136 | tf_op jit(solution)/shard_map/ppermute | solution.py:300
  22.2 18.7 %collective-permute-start.9 = (bf16[3,224,512]{2,1,0:T(8,128)(2,1)}, bf16[3,224,512]{2,1,0:T(8,128)(2,1)}, u32[]{:S(2)}, u32[]{:S(2)}) collective-permute-start(bf16[3,224,512]{2,1,0:T(8,128)(2,1)} %get-tuple-element.167), channel_id=1, source_target_pairs={{0,8},{4,12},{8,0},{12,4},{16,24},{20,28},{24,16},{28,20},{1,9},{5... | collective-permute-start | bytes 2064392 | tf_op jit(solution)/shard_map/ppermute | solution.py:294
  35.3 16.1 %collective-permute-start.3 = (bf16[128,1920]{1,0:T(8,128)(2,1)S(1)}, bf16[128,1920]{1,0:T(8,128)(2,1)S(1)}, u32[]{:S(2)}, u32[]{:S(2)}) collective-permute-start(bf16[128,1920]{1,0:T(8,128)(2,1)S(1)} %get-tuple-element.95.refs_0_), channel_id=1, source_target_pairs={{0,8},{4,12},{8,0},{12,4},{16,24},{20,28},{24,16},{28,20},{1,9},{5... | collective-permute-start | bytes 1474568 | tf_op jit(solution)/shard_map/ppermute | solution.py:294
  35.9 15.5 %collective-permute-start.4 = (bf16[128,1920]{1,0:T(8,128)(2,1)S(1)}, bf16[128,1920]{1,0:T(8,128)(2,1)S(1)}, u32[]{:S(2)}, u32[]{:S(2)}) collective-permute-start(bf16[128,1920]{1,0:T(8,128)(2,1)S(1)} %get-tuple-element.95.refs_0_), channel_id=1, source_target_pairs={{0,16},{4,20},{8,24},{12,28},{16,0},{20,4},{24,8},{28,12},{1,17},{... | collective-permute-start | bytes 1474568 | tf_op jit(solution)/shard_map/ppermute | solution.py:294
  37.4 21.3 %collective-permute-start.6 = (bf16[128,1920]{1,0:T(8,128)(2,1)S(1)}, bf16[128,1920]{1,0:T(8,128)(2,1)S(1)}, u32[]{:S(2)}, u32[]{:S(2)}) collective-permute-start(bf16[128,1920]{1,0:T(8,128)(2,1)S(1)} %get-tuple-element.124.refs_0_), channel_id=1, source_target_pairs={{0,8},{4,12},{8,0},{12,4},{16,24},{20,28},{24,16},{28,20},{1,9},{5... | collective-permute-start | bytes 1474568 | tf_op jit(solution)/shard_map/ppermute | solution.py:294
  39.3 19.5 %collective-permute-start.7 = (bf16[128,1920]{1,0:T(8,128)(2,1)S(1)}, bf16[128,1920]{1,0:T(8,128)(2,1)S(1)}, u32[]{:S(2)}, u32[]{:S(2)}) collective-permute-start(bf16[128,1920]{1,0:T(8,128)(2,1)S(1)} %get-tuple-element.124.refs_0_), channel_id=1, source_target_pairs={{0,16},{4,20},{8,24},{12,28},{16,0},{20,4},{24,8},{28,12},{1,17},{... | collective-permute-start | bytes 1474568 | tf_op jit(solution)/shard_map/ppermute | solution.py:294
  60.8 15.1 %collective-permute-start.12 = (bf16[3,4,224,512]{3,2,1,0:T(8,128)(2,1)S(1)}, bf16[3,4,224,512]{3,2,1,0:T(8,128)(2,1)S(1)}, u32[]{:S(2)}, u32[]{:S(2)}) collective-permute-start(bf16[3,4,224,512]{3,2,1,0:T(8,128)(2,1)S(1)} %shard_map.66), channel_id=1, source_target_pairs={{0,4},{4,0},{8,12},{12,8},{16,20},{20,16},{24,28},{28,24},{1,5},{5... | collective-permute-start | bytes 8257544 | tf_op jit(solution)/shard_map/ppermute | solution.py:297
  60.8 13.6 %collective-permute-start.5 = (bf16[128,1920]{1,0:T(8,128)(2,1)S(1)}, bf16[128,1920]{1,0:T(8,128)(2,1)S(1)}, u32[]{:S(2)}, u32[]{:S(2)}) collective-permute-start(bf16[128,1920]{1,0:T(8,128)(2,1)S(1)} %collective-permute-done.4.refs_2_), channel_id=1, source_target_pairs={{0,8},{4,12},{8,0},{12,4},{16,24},{20,28},{24,16},{28,20},{1,9},{5... | collective-permute-start | bytes 1474568 | tf_op jit(solution)/shard_map/ppermute | solution.py:294
  62.6 13.3 %collective-permute-start.8 = (bf16[128,1920]{1,0:T(8,128)(2,1)S(1)}, bf16[128,1920]{1,0:T(8,128)(2,1)S(1)}, u32[]{:S(2)}, u32[]{:S(2)}) collective-permute-start(bf16[128,1920]{1,0:T(8,128)(2,1)S(1)} %collective-permute-done.6.refs_1_), channel_id=1, source_target_pairs={{0,16},{4,20},{8,24},{12,28},{16,0},{20,4},{24,8},{28,12},{1,17},{... | collective-permute-start | bytes 1474568 | tf_op jit(solution)/shard_map/ppermute | solution.py:294
  80.0 14.9 %collective-permute-start.13 = (bf16[2,128,1024]{2,1,0:T(8,128)(2,1)S(1)}, bf16[2,128,1024]{2,1,0:T(8,128)(2,1)S(1)}, u32[]{:S(2)}, u32[]{:S(2)}) collective-permute-start(bf16[2,128,1024]{2,1,0:T(8,128)(2,1)S(1)} %get-tuple-element.104), channel_id=1, source_target_pairs={{0,1},{1,0},{2,3},{3,2},{4,5},{5,4},{6,7},{7,6},{8,9},{9,8},{10,11... | collective-permute-start | bytes 1572872 | tf_op jit(solution)/shard_map/ppermute | solution.py:300
  86.1 24.2 %collective-permute-start.18 = (bf16[2,128,1024]{2,1,0:T(8,128)(2,1)S(1)}, bf16[2,128,1024]{2,1,0:T(8,128)(2,1)S(1)}, u32[]{:S(2)}, u32[]{:S(2)}) collective-permute-start(bf16[2,128,1024]{2,1,0:T(8,128)(2,1)S(1)} %get-tuple-element.117), channel_id=1, source_target_pairs={{0,1},{1,0},{2,3},{3,2},{4,5},{5,4},{6,7},{7,6},{8,9},{9,8},{10,11... | collective-permute-start | bytes 1572872 | tf_op jit(solution)/shard_map/ppermute | solution.py:300
  86.2 26.7 %collective-permute-start.15 = (bf16[3,224,512]{2,1,0:T(8,128)(2,1)S(1)}, bf16[3,224,512]{2,1,0:T(8,128)(2,1)S(1)}, u32[]{:S(2)}, u32[]{:S(2)}) collective-permute-start(bf16[3,224,512]{2,1,0:T(8,128)(2,1)S(1)} %get-tuple-element.109), channel_id=1, source_target_pairs={{0,8},{4,12},{8,0},{12,4},{16,24},{20,28},{24,16},{28,20},{1,9},{5... | collective-permute-start | bytes 2064392 | tf_op jit(solution)/shard_map/ppermute | solution.py:294
  86.7 30.0 %collective-permute-start.16 = (bf16[3,224,512]{2,1,0:T(8,128)(2,1)S(1)}, bf16[3,224,512]{2,1,0:T(8,128)(2,1)S(1)}, u32[]{:S(2)}, u32[]{:S(2)}) collective-permute-start(bf16[3,224,512]{2,1,0:T(8,128)(2,1)S(1)} %get-tuple-element.110), channel_id=1, source_target_pairs={{0,16},{4,20},{8,24},{12,28},{16,0},{20,4},{24,8},{28,12},{1,17},{... | collective-permute-start | bytes 2064392 | tf_op jit(solution)/shard_map/ppermute | solution.py:294
  88.3 30.0 %collective-permute-start.17 = (bf16[3,224,512]{2,1,0:T(8,128)(2,1)S(1)}, bf16[3,224,512]{2,1,0:T(8,128)(2,1)S(1)}, u32[]{:S(2)}, u32[]{:S(2)}) collective-permute-start(bf16[3,224,512]{2,1,0:T(8,128)(2,1)S(1)} %get-tuple-element.111), channel_id=1, source_target_pairs={{0,24},{4,28},{8,16},{12,20},{16,8},{20,12},{24,0},{28,4},{1,25},{... | collective-permute-start | bytes 2064392 | tf_op jit(solution)/shard_map/ppermute | solution.py:294
  95.0 15.3 %collective-permute-start.14 = (bf16[1,128,1024]{2,1,0:T(8,128)(2,1)S(1)}, bf16[1,128,1024]{2,1,0:T(8,128)(2,1)S(1)}, u32[]{:S(2)}, u32[]{:S(2)}) collective-permute-start(bf16[1,128,1024]{2,1,0:T(8,128)(2,1)S(1)} %add_convert_fusion.5), channel_id=1, source_target_pairs={{0,2},{1,3},{2,0},{3,1},{4,6},{5,7},{6,4},{7,5},{8,10},{9,11},{10,... | collective-permute-start | bytes 786440 | tf_op jit(solution)/shard_map/ppermute | solution.py:300
  110.3 8.5 %collective-permute-start.19 = (bf16[1,64,1024]{2,1,0:T(8,128)(2,1)S(1)}, bf16[1,64,1024]{2,1,0:T(8,128)(2,1)S(1)}, u32[]{:S(2)}, u32[]{:S(2)}) collective-permute-start(bf16[1,64,1024]{2,1,0:T(8,128)(2,1)S(1)} %get-tuple-element.180), channel_id=1, source_target_pairs={{0,2},{1,3},{2,0},{3,1},{4,6},{5,7},{6,4},{7,5},{8,10},{9,11},{10,... | collective-permute-start | bytes 393224 | tf_op jit(solution)/shard_map/ppermute | solution.py:300
  119.9 5.2 %collective-permute-start.20 = (bf16[3,4,224,512]{3,2,1,0:T(8,128)(2,1)S(1)}, bf16[3,4,224,512]{3,2,1,0:T(8,128)(2,1)S(1)}, u32[]{:S(2)}, u32[]{:S(2)}) collective-permute-start(bf16[3,4,224,512]{3,2,1,0:T(8,128)(2,1)S(1)} %shard_map.69), channel_id=1, source_target_pairs={{0,4},{4,0},{8,12},{12,8},{16,20},{20,16},{24,28},{28,24},{1,5},{5... | collective-permute-start | bytes 8257544 | tf_op jit(solution)/shard_map/ppermute | solution.py:297
  129.2 19.6 %collective-permute-start.21 = (bf16[2,128,1024]{2,1,0:T(8,128)(2,1)S(1)}, bf16[2,128,1024]{2,1,0:T(8,128)(2,1)S(1)}, u32[]{:S(2)}, u32[]{:S(2)}) collective-permute-start(bf16[2,128,1024]{2,1,0:T(8,128)(2,1)S(1)} %get-tuple-element.123), channel_id=1, source_target_pairs={{0,1},{1,0},{2,3},{3,2},{4,5},{5,4},{6,7},{7,6},{8,9},{9,8},{10,11... | collective-permute-start | bytes 1572872 | tf_op jit(solution)/shard_map/ppermute | solution.py:300
  130.4 14.3 %collective-permute-start.23 = (bf16[1,64,1024]{2,1,0:T(8,128)(2,1)S(1)}, bf16[1,64,1024]{2,1,0:T(8,128)(2,1)S(1)}, u32[]{:S(2)}, u32[]{:S(2)}) collective-permute-start(bf16[1,64,1024]{2,1,0:T(8,128)(2,1)S(1)} %get-tuple-element.179), channel_id=1, source_target_pairs={{0,2},{1,3},{2,0},{3,1},{4,6},{5,7},{6,4},{7,5},{8,10},{9,11},{10,... | collective-permute-start | bytes 393224 | tf_op jit(solution)/shard_map/ppermute | solution.py:300
  148.9 20.7 %collective-permute-start.24 = (bf16[2,128,1024]{2,1,0:T(8,128)(2,1)S(1)}, bf16[2,128,1024]{2,1,0:T(8,128)(2,1)S(1)}, u32[]{:S(2)}, u32[]{:S(2)}) collective-permute-start(bf16[2,128,1024]{2,1,0:T(8,128)(2,1)S(1)} %get-tuple-element.130), channel_id=1, source_target_pairs={{0,1},{1,0},{2,3},{3,2},{4,5},{5,4},{6,7},{7,6},{8,9},{9,8},{10,11... | collective-permute-start | bytes 1572872 | tf_op jit(solution)/shard_map/ppermute | solution.py:300
  152.6 17.1 %collective-permute-start.22 = (bf16[1,128,1024]{2,1,0:T(8,128)(2,1)S(1)}, bf16[1,128,1024]{2,1,0:T(8,128)(2,1)S(1)}, u32[]{:S(2)}, u32[]{:S(2)}) collective-permute-start(bf16[1,128,1024]{2,1,0:T(8,128)(2,1)S(1)} %add_convert_fusion.3), channel_id=1, source_target_pairs={{0,2},{1,3},{2,0},{3,1},{4,6},{5,7},{6,4},{7,5},{8,10},{9,11},{10,... | collective-permute-start | bytes 786440 | tf_op jit(solution)/shard_map/ppermute | solution.py:300
  152.9 30.4 %collective-permute-start.28 = (bf16[3,224,512]{2,1,0:T(8,128)(2,1)S(1)}, bf16[3,224,512]{2,1,0:T(8,128)(2,1)S(1)}, u32[]{:S(2)}, u32[]{:S(2)}) collective-permute-start(bf16[3,224,512]{2,1,0:T(8,128)(2,1)S(1)} %get-tuple-element.135), channel_id=1, source_target_pairs={{0,8},{4,12},{8,0},{12,4},{16,24},{20,28},{24,16},{28,20},{1,9},{5... | collective-permute-start | bytes 2064392 | tf_op jit(solution)/shard_map/ppermute | solution.py:294
  153.7 30.8 %collective-permute-start.29 = (bf16[3,224,512]{2,1,0:T(8,128)(2,1)S(1)}, bf16[3,224,512]{2,1,0:T(8,128)(2,1)S(1)}, u32[]{:S(2)}, u32[]{:S(2)}) collective-permute-start(bf16[3,224,512]{2,1,0:T(8,128)(2,1)S(1)} %get-tuple-element.136), channel_id=1, source_target_pairs={{0,16},{4,20},{8,24},{12,28},{16,0},{20,4},{24,8},{28,12},{1,17},{... | collective-permute-start | bytes 2064392 | tf_op jit(solution)/shard_map/ppermute | solution.py:294
  155.3 29.3 %collective-permute-start.30 = (bf16[3,224,512]{2,1,0:T(8,128)(2,1)S(1)}, bf16[3,224,512]{2,1,0:T(8,128)(2,1)S(1)}, u32[]{:S(2)}, u32[]{:S(2)}) collective-permute-start(bf16[3,224,512]{2,1,0:T(8,128)(2,1)S(1)} %get-tuple-element.137), channel_id=1, source_target_pairs={{0,24},{4,28},{8,16},{12,20},{16,8},{20,12},{24,0},{28,4},{1,25},{... | collective-permute-start | bytes 2064392 | tf_op jit(solution)/shard_map/ppermute | solution.py:294
  170.1 12.6 %collective-permute-start.25 = (bf16[128,1024]{1,0:T(8,128)(2,1)S(1)}, bf16[128,1024]{1,0:T(8,128)(2,1)S(1)}, u32[]{:S(2)}, u32[]{:S(2)}) collective-permute-start(bf16[128,1024]{1,0:T(8,128)(2,1)S(1)} %shard_map.72.refs_0_), channel_id=1, source_target_pairs={{0,1},{1,0},{2,3},{3,2},{4,5},{5,4},{6,7},{7,6},{8,9},{9,8},{10,11... | collective-permute-start | bytes 786440 | tf_op jit(solution)/shard_map/ppermute | solution.py:300
  171.6 11.3 %collective-permute-start.31 = (bf16[1,128,1024]{2,1,0:T(8,128)(2,1)S(1)}, bf16[1,128,1024]{2,1,0:T(8,128)(2,1)S(1)}, u32[]{:S(2)}, u32[]{:S(2)}) collective-permute-start(bf16[1,128,1024]{2,1,0:T(8,128)(2,1)S(1)} %add_convert_fusion.2), channel_id=1, source_target_pairs={{0,2},{1,3},{2,0},{3,1},{4,6},{5,7},{6,4},{7,5},{8,10},{9,11},{10,... | collective-permute-start | bytes 786440 | tf_op jit(solution)/shard_map/ppermute | solution.py:300
  182.7 13.0 %collective-permute-start.26 = (bf16[128,1024]{1,0:T(8,128)(2,1)S(1)}, bf16[128,1024]{1,0:T(8,128)(2,1)S(1)}, u32[]{:S(2)}, u32[]{:S(2)}) collective-permute-start(bf16[128,1024]{1,0:T(8,128)(2,1)S(1)} %shard_map.72.refs_0_), channel_id=1, source_target_pairs={{0,2},{1,3},{2,0},{3,1},{4,6},{5,7},{6,4},{7,5},{8,10},{9,11},{10,... | collective-permute-start | bytes 786440 | tf_op jit(solution)/shard_map/ppermute | solution.py:300
  196.9 14.2 %collective-permute-start.32 = (bf16[3,4,224,512]{3,2,1,0:T(8,128)(2,1)S(1)}, bf16[3,4,224,512]{3,2,1,0:T(8,128)(2,1)S(1)}, u32[]{:S(2)}, u32[]{:S(2)}) collective-permute-start(bf16[3,4,224,512]{3,2,1,0:T(8,128)(2,1)S(1)} %shard_map.74), channel_id=1, source_target_pairs={{0,4},{4,0},{8,12},{12,8},{16,20},{20,16},{24,28},{28,24},{1,5},{5... | collective-permute-start | bytes 8257544 | tf_op jit(solution)/shard_map/ppermute | solution.py:297
  197.0 14.0 %collective-permute-start.27 = (bf16[128,1024]{1,0:T(8,128)(2,1)S(1)}, bf16[128,1024]{1,0:T(8,128)(2,1)S(1)}, u32[]{:S(2)}, u32[]{:S(2)}) collective-permute-start(bf16[128,1024]{1,0:T(8,128)(2,1)S(1)} %collective-permute-done.26.refs_2_), channel_id=1, source_target_pairs={{0,1},{1,0},{2,3},{3,2},{4,5},{5,4},{6,7},{7,6},{8,9},{9,8},{10,11... | collective-permute-start | bytes 786440 | tf_op jit(solution)/shard_map/ppermute | solution.py:300
  197.0 19.7 %collective-permute-start.39 = (bf16[128,1024]{1,0:T(8,128)(2,1)S(1)}, bf16[128,1024]{1,0:T(8,128)(2,1)}, u32[]{:S(2)}, u32[]{:S(2)}) collective-permute-start(bf16[128,1024]{1,0:T(8,128)(2,1)S(1)} %shard_map.73.refs_0_), channel_id=1, source_target_pairs={{0,2},{1,3},{2,0},{3,1},{4,6},{5,7},{6,4},{7,5},{8,10},{9,11},{10,... | collective-permute-start | bytes 786440 | tf_op jit(solution)/shard_map/ppermute | solution.py:300
  216.7 9.3 %collective-permute-start.40 = (bf16[128,1024]{1,0:T(8,128)(2,1)S(1)}, bf16[128,1024]{1,0:T(8,128)(2,1)}, u32[]{:S(2)}, u32[]{:S(2)}) collective-permute-start(bf16[128,1024]{1,0:T(8,128)(2,1)S(1)} %shard_map.73.refs_0_), channel_id=1, source_target_pairs={{0,1},{1,0},{2,3},{3,2},{4,5},{5,4},{6,7},{7,6},{8,9},{9,8},{10,11... | collective-permute-start | bytes 786440 | tf_op jit(solution)/shard_map/ppermute | solution.py:300
  216.8 13.7 %collective-permute-start.41 = (bf16[128,1024]{1,0:T(8,128)(2,1)}, bf16[128,1024]{1,0:T(8,128)(2,1)}, u32[]{:S(2)}, u32[]{:S(2)}) collective-permute-start(bf16[128,1024]{1,0:T(8,128)(2,1)} %collective-permute-done.39.refs_2_), channel_id=1, source_target_pairs={{0,1},{1,0},{2,3},{3,2},{4,5},{5,4},{6,7},{7,6},{8,9},{9,8},{10,11... | collective-permute-start | bytes 786440 | tf_op jit(solution)/shard_map/ppermute | solution.py:300
  218.8 19.6 %collective-permute-start.33 = (bf16[128,1792]{1,0:T(8,128)(2,1)}, bf16[128,1792]{1,0:T(8,128)(2,1)}, u32[]{:S(2)}, u32[]{:S(2)}) collective-permute-start(bf16[128,1792]{1,0:T(8,128)(2,1)} %get-tuple-element.149), channel_id=1, source_target_pairs={{0,8},{4,12},{8,0},{12,4},{16,24},{20,28},{24,16},{28,20},{1,9},{5... | collective-permute-start | bytes 1376264 | tf_op jit(solution)/shard_map/ppermute | solution.py:294
  219.6 21.5 %collective-permute-start.34 = (bf16[128,1792]{1,0:T(8,128)(2,1)}, bf16[128,1792]{1,0:T(8,128)(2,1)}, u32[]{:S(2)}, u32[]{:S(2)}) collective-permute-start(bf16[128,1792]{1,0:T(8,128)(2,1)} %get-tuple-element.150), channel_id=1, source_target_pairs={{0,16},{4,20},{8,24},{12,28},{16,0},{20,4},{24,8},{28,12},{1,17},{... | collective-permute-start | bytes 1376264 | tf_op jit(solution)/shard_map/ppermute | solution.py:294
  221.1 20.0 %collective-permute-start.35 = (bf16[128,1792]{1,0:T(8,128)(2,1)}, bf16[128,1792]{1,0:T(8,128)(2,1)}, u32[]{:S(2)}, u32[]{:S(2)}) collective-permute-start(bf16[128,1792]{1,0:T(8,128)(2,1)} %get-tuple-element.151), channel_id=1, source_target_pairs={{0,24},{4,28},{8,16},{12,20},{16,8},{20,12},{24,0},{28,4},{1,25},{... | collective-permute-start | bytes 1376264 | tf_op jit(solution)/shard_map/ppermute | solution.py:294
  241.1 13.5 %collective-permute-start.42 = (bf16[128,1792]{1,0:T(8,128)(2,1)S(1)}, bf16[128,1792]{1,0:T(8,128)(2,1)S(1)}, u32[]{:S(2)}, u32[]{:S(2)}) collective-permute-start(bf16[128,1792]{1,0:T(8,128)(2,1)S(1)} %get-tuple-element.159), channel_id=1, source_target_pairs={{0,8},{4,12},{8,0},{12,4},{16,24},{20,28},{24,16},{28,20},{1,9},{5... | collective-permute-start | bytes 1376264 | tf_op jit(solution)/shard_map/ppermute | solution.py:294
  242.3 20.2 %collective-permute-start.43 = (bf16[128,1792]{1,0:T(8,128)(2,1)S(1)}, bf16[128,1792]{1,0:T(8,128)(2,1)S(1)}, u32[]{:S(2)}, u32[]{:S(2)}) collective-permute-start(bf16[128,1792]{1,0:T(8,128)(2,1)S(1)} %get-tuple-element.160), channel_id=1, source_target_pairs={{0,16},{4,20},{8,24},{12,28},{16,0},{20,4},{24,8},{28,12},{1,17},{... | collective-permute-start | bytes 1376264 | tf_op jit(solution)/shard_map/ppermute | solution.py:294
  243.2 19.3 %collective-permute-start.44 = (bf16[128,1792]{1,0:T(8,128)(2,1)S(1)}, bf16[128,1792]{1,0:T(8,128)(2,1)S(1)}, u32[]{:S(2)}, u32[]{:S(2)}) collective-permute-start(bf16[128,1792]{1,0:T(8,128)(2,1)S(1)} %get-tuple-element.161), channel_id=1, source_target_pairs={{0,24},{4,28},{8,16},{12,20},{16,8},{20,12},{24,0},{28,4},{1,25},{... | collective-permute-start | bytes 1376264 | tf_op jit(solution)/shard_map/ppermute | solution.py:294
  246.2 18.8 %collective-permute-start.36 = (bf16[32,1792]{1,0:T(8,128)(2,1)S(1)}, bf16[32,1792]{1,0:T(8,128)(2,1)S(1)}, u32[]{:S(2)}, u32[]{:S(2)}) collective-permute-start(bf16[32,1792]{1,0:T(8,128)(2,1)S(1)} %get-tuple-element.177), channel_id=1, source_target_pairs={{0,1},{1,0},{2,3},{3,2},{4,5},{5,4},{6,7},{7,6},{8,9},{9,8},{10,11... | collective-permute-start | bytes 344072 | tf_op jit(solution)/shard_map/ppermute | solution.py:300
  246.6 20.7 %collective-permute-start.37 = (bf16[32,1792]{1,0:T(8,128)(2,1)S(1)}, bf16[32,1792]{1,0:T(8,128)(2,1)S(1)}, u32[]{:S(2)}, u32[]{:S(2)}) collective-permute-start(bf16[32,1792]{1,0:T(8,128)(2,1)S(1)} %get-tuple-element.176), channel_id=1, source_target_pairs={{0,2},{1,3},{2,0},{3,1},{4,6},{5,7},{6,4},{7,5},{8,10},{9,11},{10,... | collective-permute-start | bytes 344072 | tf_op jit(solution)/shard_map/ppermute | solution.py:300
  254.5 12.8 %collective-permute-start.38 = (bf16[32,1792]{1,0:T(8,128)(2,1)S(1)}, bf16[32,1792]{1,0:T(8,128)(2,1)S(1)}, u32[]{:S(2)}, u32[]{:S(2)}) collective-permute-start(bf16[32,1792]{1,0:T(8,128)(2,1)S(1)} %get-tuple-element.175), channel_id=1, source_target_pairs={{0,3},{1,2},{2,1},{3,0},{4,7},{5,6},{6,5},{7,4},{8,11},{9,10},{10,... | collective-permute-start | bytes 344072 | tf_op jit(solution)/shard_map/ppermute | solution.py:300
  262.8 5.7 %collective-permute-start.45 = (bf16[32,1792]{1,0:T(8,128)(2,1)S(1)}, bf16[32,1792]{1,0:T(8,128)(2,1)S(1)}, u32[]{:S(2)}, u32[]{:S(2)}) collective-permute-start(bf16[32,1792]{1,0:T(8,128)(2,1)S(1)} %get-tuple-element.173), channel_id=1, source_target_pairs={{0,1},{1,0},{2,3},{3,2},{4,5},{5,4},{6,7},{7,6},{8,9},{9,8},{10,11... | collective-permute-start | bytes 344072 | tf_op jit(solution)/shard_map/ppermute | solution.py:300
  263.5 8.5 %collective-permute-start.46 = (bf16[32,1792]{1,0:T(8,128)(2,1)S(1)}, bf16[32,1792]{1,0:T(8,128)(2,1)S(1)}, u32[]{:S(2)}, u32[]{:S(2)}) collective-permute-start(bf16[32,1792]{1,0:T(8,128)(2,1)S(1)} %get-tuple-element.172), channel_id=1, source_target_pairs={{0,2},{1,3},{2,0},{3,1},{4,6},{5,7},{6,4},{7,5},{8,10},{9,11},{10,... | collective-permute-start | bytes 344072 | tf_op jit(solution)/shard_map/ppermute | solution.py:300
  265.0 7.0 %collective-permute-start.47 = (bf16[32,1792]{1,0:T(8,128)(2,1)S(1)}, bf16[32,1792]{1,0:T(8,128)(2,1)S(1)}, u32[]{:S(2)}, u32[]{:S(2)}) collective-permute-start(bf16[32,1792]{1,0:T(8,128)(2,1)S(1)} %get-tuple-element.171), channel_id=1, source_target_pairs={{0,3},{1,2},{2,1},{3,0},{4,7},{5,6},{6,5},{7,4},{8,11},{9,10},{10,... | collective-permute-start | bytes 344072 | tf_op jit(solution)/shard_map/ppermute | solution.py:300
  (14 other events, 248.1 us)

commit v15 on v14

--- a/solution.py
+++ b/solution.py
@@ -356,7 +356,7 @@
     def products(weights, chained, late):
         sums, routings, parts, behind = [], [], [], []
         for half in range(HALVES):
-            left = after(toks[half], [parts, late if half else []])
+            left = after(toks[half], parts or late)
             *parts, routing = picked_sums(place, left, weights, slots)
             terms, marks = level_sums(*parts, behind, 1 if chained or not half else 2)
             behind = marks if chained else [(), *marks[1:]]

time: 274 us -> 271 us (0.989)
  waiting for transfers between devices: 160 us -> 156 us
    ppermute x3, waiting for transfers between devices: 5.09 us -> 0.01 us  [to_core(): return lax.ppermute(value, 'expert', [(s, s ^ 1) for s in range(n_expert)])]
  transfers between devices with their start and end apart: 48 -> 48, of which waited for: 26 -> 25; matrix products, arithmetic and copies ran while one was open for 1% -> 1% of each run, Pallas kernels for 8% -> 8%
where the time goes in v15:
time: 271 us; the launch traced here: 270 us
  waiting for transfers between devices  156 us (58%)
  starting transfers between devices  63.2 us (23%)
  Pallas kernels  37.1 us (14%)
  local copies, waits for them, and re-layouts  11.1 us (4%)
    ppermute x24, waiting for transfers between devices, to_level(): lax.ppermute(value, 'tensor', [(s, s ^ step) for s in range(n_tensor)])  106 us
    ppermute x21, waiting for transfers between devices, to_chip(): return lax.ppermute(value, 'expert', pairs)  50.5 us
    ppermute x24, starting transfers between devices, to_level(): lax.ppermute(value, 'tensor', [(s, s ^ step) for s in range(n_tensor)])  35.5 us
    ppermute x21, starting transfers between devices, to_chip(): return lax.ppermute(value, 'expert', pairs)  27.5 us
    pallas_call x4, Pallas kernels, picked_sums(): pl.pallas_call(functools.partial(pick_kernel, chips), in_specs=[SMEM_SPEC...  16.3 us
    pallas_call x2, Pallas kernels, down_sums(): pl.pallas_call(functools.partial(down_kernel, slots, levels), in_specs=[S...  10.9 us
    unnamed x28, local copies, waits for them, and re-layouts  7.14 us
  transfers between devices with their start and end apart: 48, of which 25 were waited for; matrix products, arithmetic and copies ran while one was open for 1% of the time, Pallas kernels for 8%

profile of v15, /device:TPU:0, one launch (start us, length us, event | category | flops | bytes accessed | tf_op | source)
XLA Modules:
  0.0 270.4 jit_solution(4129666819673905101)
XLA Ops:
  0.0 3.0 %constant_dynamic-slice_fusion.3 = (bf16[3,224,512]{2,1,0:T(8,128)(2,1)}, bf16[3,224,512]{2,1,0:T(8,128)(2,1)}, bf16[3,224,512]{2,1,0:T(8,128)(2,1)}) fusion(bf16[3,224,2048]{2,1,0:T(8,128)(2,1)} %own_ref.3, s32[]{:T(128)S(6)} %select_n.47, s32[]{:T(128)S(6)} %select_n.46, s32[]{:T(128)S(6)} %select_n.45), kind=kLoop, calls=%fused_computation.18 | loop fusion | bytes 4128780 | tf_op jit(solution)/shard_map/dynamic_slice | solution.py:326
  3.0 3.0 %collective-permute-start.10 = (bf16[3,224,512]{2,1,0:T(8,128)(2,1)}, bf16[3,224,512]{2,1,0:T(8,128)(2,1)S(1)}, u32[]{:S(2)}, u32[]{:S(2)}) collective-permute-start(bf16[3,224,512]{2,1,0:T(8,128)(2,1)} %get-tuple-element.174), channel_id=1, source_target_pairs={{0,16},{4,20},{8,24},{12,28},{16,0},{20,4},{24,8},{28,12},{1,17},{... | collective-permute-start | bytes 2064392 | tf_op jit(solution)/shard_map/ppermute | solution.py:294
  12.7 2.6 collective-permute-start.1
  15.5 6.1 %collective-permute-done.refs_1_ = bf16[64,1792]{1,0:T(8,128)(2,1)S(1)} collective-permute-done((bf16[64,1792]{1,0:T(8,128)(2,1)S(1)}, bf16[64,1792]{1,0:T(8,128)(2,1)S(1)}, u32[]{:S(2)}, u32[]{:S(2)}) %collective-permute-start) | collective-permute-done | bytes 229408 | tf_op jit(solution)/shard_map/ppermute | solution.py:300
  22.8 9.5 %collective-permute-done.1.refs_2_ = bf16[64,1792]{1,0:T(8,128)(2,1)} collective-permute-done((bf16[64,1792]{1,0:T(8,128)(2,1)}, bf16[64,1792]{1,0:T(8,128)(2,1)}, u32[]{:S(2)}, u32[]{:S(2)}) %collective-permute-start.1) | collective-permute-done | bytes 229408 | tf_op jit(solution)/shard_map/ppermute | solution.py:300
  37.4 1.9 collective-permute-start.6
  40.8 8.7 %collective-permute-done.4.refs_2_ = bf16[128,1920]{1,0:T(8,128)(2,1)S(1)} collective-permute-done((bf16[128,1920]{1,0:T(8,128)(2,1)S(1)}, bf16[128,1920]{1,0:T(8,128)(2,1)S(1)}, u32[]{:S(2)}, u32[]{:S(2)}) %collective-permute-start.4) | collective-permute-done | bytes 491552 | tf_op jit(solution)/shard_map/ppermute | solution.py:294
  49.5 9.2 %collective-permute-done.6.refs_1_ = bf16[128,1920]{1,0:T(8,128)(2,1)S(1)} collective-permute-done((bf16[128,1920]{1,0:T(8,128)(2,1)S(1)}, bf16[128,1920]{1,0:T(8,128)(2,1)S(1)}, u32[]{:S(2)}, u32[]{:S(2)}) %collective-permute-start.6) | collective-permute-done | bytes 491552 | tf_op jit(solution)/shard_map/ppermute | solution.py:294
  58.7 2.0 shard_map.66
  60.8 1.8 collective-permute-start.5
  64.4 10.1 %collective-permute-done.5.refs_3_ = bf16[128,1920]{1,0:T(8,128)(2,1)S(1)} collective-permute-done((bf16[128,1920]{1,0:T(8,128)(2,1)S(1)}, bf16[128,1920]{1,0:T(8,128)(2,1)S(1)}, u32[]{:S(2)}, u32[]{:S(2)}) %collective-permute-start.5) | collective-permute-done | bytes 491552 | tf_op jit(solution)/shard_map/ppermute | solution.py:294
  75.9 4.1 %shard_map.67 = (bf16[2,128,1024]{2,1,0:T(8,128)(2,1)S(1)}, bf16[2,128,1024]{2,1,0:T(8,128)(2,1)S(1)}, bf16[4,128,128]{2,1,0:T(8,128)(2,1)S(1)}) custom-call(s32[3]{0:T(128)S(1)} %pad_add_fusion.place_ref, bf16[128,1920]{1,0:T(8,128)(2,1)S(1)} %get-tuple-element.120.refs_0_, bf16[128,1920]{1,0:T(8,128)(2,1)S(1)} %collective-permute-done.3.refs_1_, ...), custom_call_target="tpu_custom_call" | custom-call | flops 2818572288 | bytes 8388608 | tf_op jit(solution)/shard_map/pallas_call | solution.py:195
  80.0 2.0 collective-permute-start.13
  82.0 4.1 %shard_map.68 = (bf16[2,128,1024]{2,1,0:T(8,128)(2,1)S(1)}, bf16[2,128,1024]{2,1,0:T(8,128)(2,1)S(1)}, bf16[4,128,128]{2,1,0:T(8,128)(2,1)S(1)}) custom-call(s32[3]{0:T(128)S(1)} %pad_add_fusion.place_ref, bf16[128,1920]{1,0:T(8,128)(2,1)S(1)} %get-tuple-element.132.refs_0_, bf16[128,1920]{1,0:T(8,128)(2,1)S(1)} %collective-permute-done.6.refs_1_, ...), custom_call_target="tpu_custom_call" | custom-call | flops 2818572288 | bytes 8388608 | tf_op jit(solution)/shard_map/pallas_call | solution.py:195
  89.7 5.2 %collective-permute-done.13 = bf16[2,128,1024]{2,1,0:T(8,128)(2,1)S(1)} collective-permute-done((bf16[2,128,1024]{2,1,0:T(8,128)(2,1)S(1)}, bf16[2,128,1024]{2,1,0:T(8,128)(2,1)S(1)}, u32[]{:S(2)}, u32[]{:S(2)}) %collective-permute-start.13) | collective-permute-done | bytes 524320 | tf_op jit(solution)/shard_map/ppermute | solution.py:300
  94.9 3.2 %collective-permute-start.14 = (bf16[1,128,1024]{2,1,0:T(8,128)(2,1)S(1)}, bf16[1,128,1024]{2,1,0:T(8,128)(2,1)S(1)}, u32[]{:S(2)}, u32[]{:S(2)}) collective-permute-start(bf16[1,128,1024]{2,1,0:T(8,128)(2,1)S(1)} %add_convert_fusion.5), channel_id=1, source_target_pairs={{0,2},{1,3},{2,0},{3,1},{4,6},{5,7},{6,4},{7,5},{8,10},{9,11},{10,... | collective-permute-start | bytes 786440 | tf_op jit(solution)/shard_map/ppermute | solution.py:300
  98.2 12.2 %collective-permute-done.15 = bf16[2,128,1024]{2,1,0:T(8,128)(2,1)S(1)} collective-permute-done((bf16[2,128,1024]{2,1,0:T(8,128)(2,1)S(1)}, bf16[2,128,1024]{2,1,0:T(8,128)(2,1)S(1)}, u32[]{:S(2)}, u32[]{:S(2)}) %collective-permute-start.15) | collective-permute-done | bytes 524320 | tf_op jit(solution)/shard_map/ppermute | solution.py:300
  110.5 2.6 collective-permute-start.16
  113.1 5.5 %collective-permute-done.19.refs_1_ = bf16[3,224,512]{2,1,0:T(8,128)(2,1)S(1)} collective-permute-done((bf16[3,224,512]{2,1,0:T(8,128)(2,1)S(1)}, bf16[3,224,512]{2,1,0:T(8,128)(2,1)S(1)}, u32[]{:S(2)}, u32[]{:S(2)}) %collective-permute-start.19) | collective-permute-done | bytes 688160 | tf_op jit(solution)/shard_map/ppermute | solution.py:294
  120.2 2.5 collective-permute-start.17
  122.7 7.1 %collective-permute-done.17 = bf16[1,64,1024]{2,1,0:T(8,128)(2,1)S(1)} collective-permute-done((bf16[1,64,1024]{2,1,0:T(8,128)(2,1)S(1)}, bf16[1,64,1024]{2,1,0:T(8,128)(2,1)S(1)}, u32[]{:S(2)}, u32[]{:S(2)}) %collective-permute-start.17) | collective-permute-done | bytes 131104 | tf_op jit(solution)/shard_map/ppermute | solution.py:300
  129.8 4.1 %shard_map.70 = (bf16[2,128,1024]{2,1,0:T(8,128)(2,1)S(1)}, bf16[2,128,1024]{2,1,0:T(8,128)(2,1)S(1)}, bf16[4,128,128]{2,1,0:T(8,128)(2,1)}) custom-call(s32[3]{0:T(128)S(1)} %pad_add_fusion.place_ref, bf16[128,1920]{1,0:T(8,128)(2,1)S(1)} %get-tuple-element.120.refs_0_, bf16[128,1920]{1,0:T(8,128)(2,1)S(1)} %collective-permute-done.3.refs_1_, ...), custom_call_target="tpu_custom_call" | custom-call | flops 2818572288 | bytes 8388608 | tf_op jit(solution)/shard_map/pallas_call | solution.py:195
  134.0 4.1 %shard_map.71 = (bf16[2,128,1024]{2,1,0:T(8,128)(2,1)S(1)}, bf16[2,128,1024]{2,1,0:T(8,128)(2,1)S(1)}, bf16[4,128,128]{2,1,0:T(8,128)(2,1)}) custom-call(s32[3]{0:T(128)S(1)} %pad_add_fusion.place_ref, bf16[128,1920]{1,0:T(8,128)(2,1)S(1)} %get-tuple-element.132.refs_0_, bf16[128,1920]{1,0:T(8,128)(2,1)S(1)} %collective-permute-done.6.refs_1_, ...), custom_call_target="tpu_custom_call" | custom-call | flops 2818572288 | bytes 8388608 | tf_op jit(solution)/shard_map/pallas_call | solution.py:195
  138.1 9.4 %collective-permute-done.22 = bf16[2,128,1024]{2,1,0:T(8,128)(2,1)S(1)} collective-permute-done((bf16[2,128,1024]{2,1,0:T(8,128)(2,1)S(1)}, bf16[2,128,1024]{2,1,0:T(8,128)(2,1)S(1)}, u32[]{:S(2)}, u32[]{:S(2)}) %collective-permute-start.22) | collective-permute-done | bytes 524320 | tf_op jit(solution)/shard_map/ppermute | solution.py:300
  147.9 2.9 %collective-permute-start.23 = (bf16[1,128,1024]{2,1,0:T(8,128)(2,1)S(1)}, bf16[1,128,1024]{2,1,0:T(8,128)(2,1)S(1)}, u32[]{:S(2)}, u32[]{:S(2)}) collective-permute-start(bf16[1,128,1024]{2,1,0:T(8,128)(2,1)S(1)} %add_convert_fusion.3), channel_id=1, source_target_pairs={{0,2},{1,3},{2,0},{3,1},{4,6},{5,7},{6,4},{7,5},{8,10},{9,11},{10,... | collective-permute-start | bytes 786440 | tf_op jit(solution)/shard_map/ppermute | solution.py:300
  154.7 11.1 %collective-permute-done.24 = bf16[2,128,1024]{2,1,0:T(8,128)(2,1)S(1)} collective-permute-done((bf16[2,128,1024]{2,1,0:T(8,128)(2,1)S(1)}, bf16[2,128,1024]{2,1,0:T(8,128)(2,1)S(1)}, u32[]{:S(2)}, u32[]{:S(2)}) %collective-permute-start.24) | collective-permute-done | bytes 524320 | tf_op jit(solution)/shard_map/ppermute | solution.py:300
  166.3 1.8 collective-permute-start.25
  169.6 8.5 %collective-permute-done.25.refs_1_ = bf16[128,1024]{1,0:T(8,128)(2,1)S(1)} collective-permute-done((bf16[128,1024]{1,0:T(8,128)(2,1)S(1)}, bf16[128,1024]{1,0:T(8,128)(2,1)S(1)}, u32[]{:S(2)}, u32[]{:S(2)}) %collective-permute-start.25) | collective-permute-done | bytes 262176 | tf_op jit(solution)/shard_map/ppermute | solution.py:300
  179.1 8.0 %collective-permute-done.31.refs_5_ = bf16[1,128,1024]{2,1,0:T(8,128)(2,1)S(1)} collective-permute-done((bf16[1,128,1024]{2,1,0:T(8,128)(2,1)S(1)}, bf16[1,128,1024]{2,1,0:T(8,128)(2,1)S(1)}, u32[]{:S(2)}, u32[]{:S(2)}) %collective-permute-start.31) | collective-permute-done | bytes 262176 | tf_op jit(solution)/shard_map/ppermute | solution.py:300
  187.6 4.4 %collective-permute-done.26.refs_2_ = bf16[128,1024]{1,0:T(8,128)(2,1)S(1)} collective-permute-done((bf16[128,1024]{1,0:T(8,128)(2,1)S(1)}, bf16[128,1024]{1,0:T(8,128)(2,1)S(1)}, u32[]{:S(2)}, u32[]{:S(2)}) %collective-permute-start.26) | collective-permute-done | bytes 262176 | tf_op jit(solution)/shard_map/ppermute | solution.py:300
  193.3 2.4 collective-permute-start.39
  195.8 11.1 %collective-permute-done.27.refs_3_ = bf16[128,1024]{1,0:T(8,128)(2,1)S(1)} collective-permute-done((bf16[128,1024]{1,0:T(8,128)(2,1)S(1)}, bf16[128,1024]{1,0:T(8,128)(2,1)S(1)}, u32[]{:S(2)}, u32[]{:S(2)}) %collective-permute-start.27) | collective-permute-done | bytes 262176 | tf_op jit(solution)/shard_map/ppermute | solution.py:300
  206.9 5.7 %shard_map.75 = (bf16[128,1792]{1,0:T(8,128)(2,1)S(1)}, bf16[128,1792]{1,0:T(8,128)(2,1)}, bf16[128,1792]{1,0:T(8,128)(2,1)}, bf16[128,1792]{1,0:T(8,128)(2,1)}) custom-call(s32[3]{0:T(128)S(1)} %pad_add_fusion.place_ref, bf16[4,128,128]{2,1,0:T(8,128)(2,1)S(1)} %get-tuple-element.106.routing_ref, bf16[128,1024]{1,0:T(8,128)(2,1)S(1)} %shard_map.72.refs_0_, ...), custom_call_target="tpu_custom_call" | custom-call | flops 2818572288 | bytes 8388608 | tf_op jit(solution)/shard_map/pallas_call | solution.py:263
  212.6 2.0 collective-permute-start.41
  214.6 2.0 collective-permute-start.33
  218.1 3.8 %collective-permute-done.40.refs_1_ = bf16[128,1024]{1,0:T(8,128)(2,1)} collective-permute-done((bf16[128,1024]{1,0:T(8,128)(2,1)S(1)}, bf16[128,1024]{1,0:T(8,128)(2,1)}, u32[]{:S(2)}, u32[]{:S(2)}) %collective-permute-start.40) | collective-permute-done | bytes 262176 | tf_op jit(solution)/shard_map/ppermute | solution.py:300
  221.9 4.4 %collective-permute-done.41.refs_3_ = bf16[128,1024]{1,0:T(8,128)(2,1)} collective-permute-done((bf16[128,1024]{1,0:T(8,128)(2,1)}, bf16[128,1024]{1,0:T(8,128)(2,1)}, u32[]{:S(2)}, u32[]{:S(2)}) %collective-permute-start.41) | collective-permute-done | bytes 262176 | tf_op jit(solution)/shard_map/ppermute | solution.py:300
  227.2 1.8 copy-done.11
  229.0 5.2 %shard_map.76 = (bf16[128,1792]{1,0:T(8,128)(2,1)S(1)}, bf16[128,1792]{1,0:T(8,128)(2,1)S(1)}, bf16[128,1792]{1,0:T(8,128)(2,1)S(1)}, bf16[128,1792]{1,0:T(8,128)(2,1)S(1)}) custom-call(s32[3]{0:T(128)S(1)} %pad_add_fusion.place_ref, bf16[4,128,128]{2,1,0:T(8,128)(2,1)S(1)} %copy-done.9, bf16[128,1024]{1,0:T(8,128)(2,1)S(1)} %shard_map.73.refs_0_, ...), custom_call_target="tpu_custom_call" | custom-call | flops 2818572288 | bytes 8388608 | tf_op jit(solution)/shard_map/pallas_call | solution.py:263
  234.2 3.7 %collective-permute-done.34 = bf16[128,1792]{1,0:T(8,128)(2,1)} collective-permute-done((bf16[128,1792]{1,0:T(8,128)(2,1)}, bf16[128,1792]{1,0:T(8,128)(2,1)}, u32[]{:S(2)}, u32[]{:S(2)}) %collective-permute-start.34) | collective-permute-done | bytes 458784 | tf_op jit(solution)/shard_map/ppermute | solution.py:294
  243.5 2.0 collective-permute-start.37
  245.4 6.0 %collective-permute-done.42 = bf16[128,1792]{1,0:T(8,128)(2,1)S(1)} collective-permute-done((bf16[128,1792]{1,0:T(8,128)(2,1)S(1)}, bf16[128,1792]{1,0:T(8,128)(2,1)S(1)}, u32[]{:S(2)}, u32[]{:S(2)}) %collective-permute-start.42) | collective-permute-done | bytes 458784 | tf_op jit(solution)/shard_map/ppermute | solution.py:294
  251.4 1.8 collective-permute-start.38
  253.2 5.8 %collective-permute-done.43 = bf16[128,1792]{1,0:T(8,128)(2,1)S(1)} collective-permute-done((bf16[128,1792]{1,0:T(8,128)(2,1)S(1)}, bf16[128,1792]{1,0:T(8,128)(2,1)S(1)}, u32[]{:S(2)}, u32[]{:S(2)}) %collective-permute-start.43) | collective-permute-done | bytes 458784 | tf_op jit(solution)/shard_map/ppermute | solution.py:294
  259.9 1.9 collective-permute-start.46
  261.8 1.9 collective-permute-start.47
  264.1 2.8 %collective-permute-done.46.refs_6_ = bf16[32,1792]{1,0:T(8,128)(2,1)S(1)} collective-permute-done((bf16[32,1792]{1,0:T(8,128)(2,1)S(1)}, bf16[32,1792]{1,0:T(8,128)(2,1)S(1)}, u32[]{:S(2)}, u32[]{:S(2)}) %collective-permute-start.46) | collective-permute-done | bytes 114720 | tf_op jit(solution)/shard_map/ppermute | solution.py:300
  268.5 1.9 shard_map.77
  (117 shorter events, 43.4 us)
Async XLA Ops:
  3.0 34.4 %collective-permute-start.10 = (bf16[3,224,512]{2,1,0:T(8,128)(2,1)}, bf16[3,224,512]{2,1,0:T(8,128)(2,1)S(1)}, u32[]{:S(2)}, u32[]{:S(2)}) collective-permute-start(bf16[3,224,512]{2,1,0:T(8,128)(2,1)} %get-tuple-element.174), channel_id=1, source_target_pairs={{0,16},{4,20},{8,24},{12,28},{16,0},{20,4},{24,8},{28,12},{1,17},{... | collective-permute-start | bytes 2064392 | tf_op jit(solution)/shard_map/ppermute | solution.py:294
  6.0 33.3 %collective-permute-start.11 = (bf16[3,224,512]{2,1,0:T(8,128)(2,1)}, bf16[3,224,512]{2,1,0:T(8,128)(2,1)}, u32[]{:S(2)}, u32[]{:S(2)}) collective-permute-start(bf16[3,224,512]{2,1,0:T(8,128)(2,1)} %get-tuple-element.173), channel_id=1, source_target_pairs={{0,24},{4,28},{8,16},{12,20},{16,8},{20,12},{24,0},{28,4},{1,25},{... | collective-permute-start | bytes 2064392 | tf_op jit(solution)/shard_map/ppermute | solution.py:294
  11.1 10.5 %collective-permute-start = (bf16[64,1792]{1,0:T(8,128)(2,1)S(1)}, bf16[64,1792]{1,0:T(8,128)(2,1)S(1)}, u32[]{:S(2)}, u32[]{:S(2)}) collective-permute-start(bf16[64,1792]{1,0:T(8,128)(2,1)S(1)} %get-tuple-element.90), channel_id=1, source_target_pairs={{0,1},{1,0},{2,3},{3,2},{4,5},{5,4},{6,7},{7,6},{8,9},{9,8},{10,11... | collective-permute-start | bytes 688136 | tf_op jit(solution)/shard_map/ppermute | solution.py:300
  12.7 19.6 %collective-permute-start.1 = (bf16[64,1792]{1,0:T(8,128)(2,1)}, bf16[64,1792]{1,0:T(8,128)(2,1)}, u32[]{:S(2)}, u32[]{:S(2)}) collective-permute-start(bf16[64,1792]{1,0:T(8,128)(2,1)} %get-tuple-element.91), channel_id=1, source_target_pairs={{0,2},{1,3},{2,0},{3,1},{4,6},{5,7},{6,4},{7,5},{8,10},{9,11},{10,... | collective-permute-start | bytes 688136 | tf_op jit(solution)/shard_map/ppermute | solution.py:300
  15.3 17.0 %collective-permute-start.2 = (bf16[64,1792]{1,0:T(8,128)(2,1)}, bf16[64,1792]{1,0:T(8,128)(2,1)}, u32[]{:S(2)}, u32[]{:S(2)}) collective-permute-start(bf16[64,1792]{1,0:T(8,128)(2,1)} %get-tuple-element.92), channel_id=1, source_target_pairs={{0,3},{1,2},{2,1},{3,0},{4,7},{5,6},{6,5},{7,4},{8,11},{9,10},{10,... | collective-permute-start | bytes 688136 | tf_op jit(solution)/shard_map/ppermute | solution.py:300
  22.2 18.6 %collective-permute-start.9 = (bf16[3,224,512]{2,1,0:T(8,128)(2,1)}, bf16[3,224,512]{2,1,0:T(8,128)(2,1)}, u32[]{:S(2)}, u32[]{:S(2)}) collective-permute-start(bf16[3,224,512]{2,1,0:T(8,128)(2,1)} %get-tuple-element.175), channel_id=1, source_target_pairs={{0,8},{4,12},{8,0},{12,4},{16,24},{20,28},{24,16},{28,20},{1,9},{5... | collective-permute-start | bytes 2064392 | tf_op jit(solution)/shard_map/ppermute | solution.py:294
  35.3 14.2 %collective-permute-start.4 = (bf16[128,1920]{1,0:T(8,128)(2,1)S(1)}, bf16[128,1920]{1,0:T(8,128)(2,1)S(1)}, u32[]{:S(2)}, u32[]{:S(2)}) collective-permute-start(bf16[128,1920]{1,0:T(8,128)(2,1)S(1)} %get-tuple-element.120.refs_0_), channel_id=1, source_target_pairs={{0,16},{4,20},{8,24},{12,28},{16,0},{20,4},{24,8},{28,12},{1,17},{... | collective-permute-start | bytes 1474568 | tf_op jit(solution)/shard_map/ppermute | solution.py:294
  36.9 21.9 %collective-permute-start.3 = (bf16[128,1920]{1,0:T(8,128)(2,1)S(1)}, bf16[128,1920]{1,0:T(8,128)(2,1)S(1)}, u32[]{:S(2)}, u32[]{:S(2)}) collective-permute-start(bf16[128,1920]{1,0:T(8,128)(2,1)S(1)} %get-tuple-element.120.refs_0_), channel_id=1, source_target_pairs={{0,8},{4,12},{8,0},{12,4},{16,24},{20,28},{24,16},{28,20},{1,9},{5... | collective-permute-start | bytes 1474568 | tf_op jit(solution)/shard_map/ppermute | solution.py:294
  37.4 21.3 %collective-permute-start.6 = (bf16[128,1920]{1,0:T(8,128)(2,1)S(1)}, bf16[128,1920]{1,0:T(8,128)(2,1)S(1)}, u32[]{:S(2)}, u32[]{:S(2)}) collective-permute-start(bf16[128,1920]{1,0:T(8,128)(2,1)S(1)} %get-tuple-element.132.refs_0_), channel_id=1, source_target_pairs={{0,8},{4,12},{8,0},{12,4},{16,24},{20,28},{24,16},{28,20},{1,9},{5... | collective-permute-start | bytes 1474568 | tf_op jit(solution)/shard_map/ppermute | solution.py:294
  39.3 19.5 %collective-permute-start.7 = (bf16[128,1920]{1,0:T(8,128)(2,1)S(1)}, bf16[128,1920]{1,0:T(8,128)(2,1)S(1)}, u32[]{:S(2)}, u32[]{:S(2)}) collective-permute-start(bf16[128,1920]{1,0:T(8,128)(2,1)S(1)} %get-tuple-element.132.refs_0_), channel_id=1, source_target_pairs={{0,16},{4,20},{8,24},{12,28},{16,0},{20,4},{24,8},{28,12},{1,17},{... | collective-permute-start | bytes 1474568 | tf_op jit(solution)/shard_map/ppermute | solution.py:294
  60.8 15.1 %collective-permute-start.12 = (bf16[3,4,224,512]{3,2,1,0:T(8,128)(2,1)S(1)}, bf16[3,4,224,512]{3,2,1,0:T(8,128)(2,1)S(1)}, u32[]{:S(2)}, u32[]{:S(2)}) collective-permute-start(bf16[3,4,224,512]{3,2,1,0:T(8,128)(2,1)S(1)} %shard_map.66), channel_id=1, source_target_pairs={{0,4},{4,0},{8,12},{12,8},{16,20},{20,16},{24,28},{28,24},{1,5},{5... | collective-permute-start | bytes 8257544 | tf_op jit(solution)/shard_map/ppermute | solution.py:297
  60.8 13.6 %collective-permute-start.5 = (bf16[128,1920]{1,0:T(8,128)(2,1)S(1)}, bf16[128,1920]{1,0:T(8,128)(2,1)S(1)}, u32[]{:S(2)}, u32[]{:S(2)}) collective-permute-start(bf16[128,1920]{1,0:T(8,128)(2,1)S(1)} %collective-permute-done.4.refs_2_), channel_id=1, source_target_pairs={{0,8},{4,12},{8,0},{12,4},{16,24},{20,28},{24,16},{28,20},{1,9},{5... | collective-permute-start | bytes 1474568 | tf_op jit(solution)/shard_map/ppermute | solution.py:294
  62.6 13.3 %collective-permute-start.8 = (bf16[128,1920]{1,0:T(8,128)(2,1)S(1)}, bf16[128,1920]{1,0:T(8,128)(2,1)S(1)}, u32[]{:S(2)}, u32[]{:S(2)}) collective-permute-start(bf16[128,1920]{1,0:T(8,128)(2,1)S(1)} %collective-permute-done.6.refs_1_), channel_id=1, source_target_pairs={{0,16},{4,20},{8,24},{12,28},{16,0},{20,4},{24,8},{28,12},{1,17},{... | collective-permute-start | bytes 1474568 | tf_op jit(solution)/shard_map/ppermute | solution.py:294
  80.0 14.9 %collective-permute-start.13 = (bf16[2,128,1024]{2,1,0:T(8,128)(2,1)S(1)}, bf16[2,128,1024]{2,1,0:T(8,128)(2,1)S(1)}, u32[]{:S(2)}, u32[]{:S(2)}) collective-permute-start(bf16[2,128,1024]{2,1,0:T(8,128)(2,1)S(1)} %get-tuple-element.108), channel_id=1, source_target_pairs={{0,1},{1,0},{2,3},{3,2},{4,5},{5,4},{6,7},{7,6},{8,9},{9,8},{10,11... | collective-permute-start | bytes 1572872 | tf_op jit(solution)/shard_map/ppermute | solution.py:300
  86.1 24.3 %collective-permute-start.15 = (bf16[2,128,1024]{2,1,0:T(8,128)(2,1)S(1)}, bf16[2,128,1024]{2,1,0:T(8,128)(2,1)S(1)}, u32[]{:S(2)}, u32[]{:S(2)}) collective-permute-start(bf16[2,128,1024]{2,1,0:T(8,128)(2,1)S(1)} %get-tuple-element.118), channel_id=1, source_target_pairs={{0,1},{1,0},{2,3},{3,2},{4,5},{5,4},{6,7},{7,6},{8,9},{9,8},{10,11... | collective-permute-start | bytes 1572872 | tf_op jit(solution)/shard_map/ppermute | solution.py:300
  86.2 26.9 %collective-permute-start.18 = (bf16[3,224,512]{2,1,0:T(8,128)(2,1)S(1)}, bf16[3,224,512]{2,1,0:T(8,128)(2,1)S(1)}, u32[]{:S(2)}, u32[]{:S(2)}) collective-permute-start(bf16[3,224,512]{2,1,0:T(8,128)(2,1)S(1)} %get-tuple-element.124), channel_id=1, source_target_pairs={{0,8},{4,12},{8,0},{12,4},{16,24},{20,28},{24,16},{28,20},{1,9},{5... | collective-permute-start | bytes 2064392 | tf_op jit(solution)/shard_map/ppermute | solution.py:294
  87.7 30.9 %collective-permute-start.19 = (bf16[3,224,512]{2,1,0:T(8,128)(2,1)S(1)}, bf16[3,224,512]{2,1,0:T(8,128)(2,1)S(1)}, u32[]{:S(2)}, u32[]{:S(2)}) collective-permute-start(bf16[3,224,512]{2,1,0:T(8,128)(2,1)S(1)} %get-tuple-element.125), channel_id=1, source_target_pairs={{0,16},{4,20},{8,24},{12,28},{16,0},{20,4},{24,8},{28,12},{1,17},{... | collective-permute-start | bytes 2064392 | tf_op jit(solution)/shard_map/ppermute | solution.py:294
  88.3 30.3 %collective-permute-start.20 = (bf16[3,224,512]{2,1,0:T(8,128)(2,1)S(1)}, bf16[3,224,512]{2,1,0:T(8,128)(2,1)S(1)}, u32[]{:S(2)}, u32[]{:S(2)}) collective-permute-start(bf16[3,224,512]{2,1,0:T(8,128)(2,1)S(1)} %get-tuple-element.126), channel_id=1, source_target_pairs={{0,24},{4,28},{8,16},{12,20},{16,8},{20,12},{24,0},{28,4},{1,25},{... | collective-permute-start | bytes 2064392 | tf_op jit(solution)/shard_map/ppermute | solution.py:294
  94.9 15.5 %collective-permute-start.14 = (bf16[1,128,1024]{2,1,0:T(8,128)(2,1)S(1)}, bf16[1,128,1024]{2,1,0:T(8,128)(2,1)S(1)}, u32[]{:S(2)}, u32[]{:S(2)}) collective-permute-start(bf16[1,128,1024]{2,1,0:T(8,128)(2,1)S(1)} %add_convert_fusion.5), channel_id=1, source_target_pairs={{0,2},{1,3},{2,0},{3,1},{4,6},{5,7},{6,4},{7,5},{8,10},{9,11},{10,... | collective-permute-start | bytes 786440 | tf_op jit(solution)/shard_map/ppermute | solution.py:300
  110.5 8.5 %collective-permute-start.16 = (bf16[1,64,1024]{2,1,0:T(8,128)(2,1)S(1)}, bf16[1,64,1024]{2,1,0:T(8,128)(2,1)S(1)}, u32[]{:S(2)}, u32[]{:S(2)}) collective-permute-start(bf16[1,64,1024]{2,1,0:T(8,128)(2,1)S(1)} %get-tuple-element.188), channel_id=1, source_target_pairs={{0,2},{1,3},{2,0},{3,1},{4,6},{5,7},{6,4},{7,5},{8,10},{9,11},{10,... | collective-permute-start | bytes 393224 | tf_op jit(solution)/shard_map/ppermute | solution.py:300
  120.1 9.7 %collective-permute-start.21 = (bf16[3,4,224,512]{3,2,1,0:T(8,128)(2,1)S(1)}, bf16[3,4,224,512]{3,2,1,0:T(8,128)(2,1)S(1)}, u32[]{:S(2)}, u32[]{:S(2)}) collective-permute-start(bf16[3,4,224,512]{3,2,1,0:T(8,128)(2,1)S(1)} %shard_map.69), channel_id=1, source_target_pairs={{0,4},{4,0},{8,12},{12,8},{16,20},{20,16},{24,28},{28,24},{1,5},{5... | collective-permute-start | bytes 8257544 | tf_op jit(solution)/shard_map/ppermute | solution.py:297
  120.2 9.6 %collective-permute-start.17 = (bf16[1,64,1024]{2,1,0:T(8,128)(2,1)S(1)}, bf16[1,64,1024]{2,1,0:T(8,128)(2,1)S(1)}, u32[]{:S(2)}, u32[]{:S(2)}) collective-permute-start(bf16[1,64,1024]{2,1,0:T(8,128)(2,1)S(1)} %get-tuple-element.187), channel_id=1, source_target_pairs={{0,2},{1,3},{2,0},{3,1},{4,6},{5,7},{6,4},{7,5},{8,10},{9,11},{10,... | collective-permute-start | bytes 393224 | tf_op jit(solution)/shard_map/ppermute | solution.py:300
  133.9 13.6 %collective-permute-start.22 = (bf16[2,128,1024]{2,1,0:T(8,128)(2,1)S(1)}, bf16[2,128,1024]{2,1,0:T(8,128)(2,1)S(1)}, u32[]{:S(2)}, u32[]{:S(2)}) collective-permute-start(bf16[2,128,1024]{2,1,0:T(8,128)(2,1)S(1)} %get-tuple-element.131), channel_id=1, source_target_pairs={{0,1},{1,0},{2,3},{3,2},{4,5},{5,4},{6,7},{7,6},{8,9},{9,8},{10,11... | collective-permute-start | bytes 1572872 | tf_op jit(solution)/shard_map/ppermute | solution.py:300
  147.5 18.3 %collective-permute-start.24 = (bf16[2,128,1024]{2,1,0:T(8,128)(2,1)S(1)}, bf16[2,128,1024]{2,1,0:T(8,128)(2,1)S(1)}, u32[]{:S(2)}, u32[]{:S(2)}) collective-permute-start(bf16[2,128,1024]{2,1,0:T(8,128)(2,1)S(1)} %get-tuple-element.138), channel_id=1, source_target_pairs={{0,1},{1,0},{2,3},{3,2},{4,5},{5,4},{6,7},{7,6},{8,9},{9,8},{10,11... | collective-permute-start | bytes 1572872 | tf_op jit(solution)/shard_map/ppermute | solution.py:300
  147.9 18.0 %collective-permute-start.23 = (bf16[1,128,1024]{2,1,0:T(8,128)(2,1)S(1)}, bf16[1,128,1024]{2,1,0:T(8,128)(2,1)S(1)}, u32[]{:S(2)}, u32[]{:S(2)}) collective-permute-start(bf16[1,128,1024]{2,1,0:T(8,128)(2,1)S(1)} %add_convert_fusion.3), channel_id=1, source_target_pairs={{0,2},{1,3},{2,0},{3,1},{4,6},{5,7},{6,4},{7,5},{8,10},{9,11},{10,... | collective-permute-start | bytes 786440 | tf_op jit(solution)/shard_map/ppermute | solution.py:300
  151.1 36.5 %collective-permute-start.28 = (bf16[3,224,512]{2,1,0:T(8,128)(2,1)S(1)}, bf16[3,224,512]{2,1,0:T(8,128)(2,1)S(1)}, u32[]{:S(2)}, u32[]{:S(2)}) collective-permute-start(bf16[3,224,512]{2,1,0:T(8,128)(2,1)S(1)} %get-tuple-element.143), channel_id=1, source_target_pairs={{0,8},{4,12},{8,0},{12,4},{16,24},{20,28},{24,16},{28,20},{1,9},{5... | collective-permute-start | bytes 2064392 | tf_op jit(solution)/shard_map/ppermute | solution.py:294
  152.0 35.6 %collective-permute-start.29 = (bf16[3,224,512]{2,1,0:T(8,128)(2,1)S(1)}, bf16[3,224,512]{2,1,0:T(8,128)(2,1)S(1)}, u32[]{:S(2)}, u32[]{:S(2)}) collective-permute-start(bf16[3,224,512]{2,1,0:T(8,128)(2,1)S(1)} %get-tuple-element.144), channel_id=1, source_target_pairs={{0,16},{4,20},{8,24},{12,28},{16,0},{20,4},{24,8},{28,12},{1,17},{... | collective-permute-start | bytes 2064392 | tf_op jit(solution)/shard_map/ppermute | solution.py:294
  153.7 33.9 %collective-permute-start.30 = (bf16[3,224,512]{2,1,0:T(8,128)(2,1)S(1)}, bf16[3,224,512]{2,1,0:T(8,128)(2,1)S(1)}, u32[]{:S(2)}, u32[]{:S(2)}) collective-permute-start(bf16[3,224,512]{2,1,0:T(8,128)(2,1)S(1)} %get-tuple-element.145), channel_id=1, source_target_pairs={{0,24},{4,28},{8,16},{12,20},{16,8},{20,12},{24,0},{28,4},{1,25},{... | collective-permute-start | bytes 2064392 | tf_op jit(solution)/shard_map/ppermute | solution.py:294
  166.3 11.8 %collective-permute-start.25 = (bf16[128,1024]{1,0:T(8,128)(2,1)S(1)}, bf16[128,1024]{1,0:T(8,128)(2,1)S(1)}, u32[]{:S(2)}, u32[]{:S(2)}) collective-permute-start(bf16[128,1024]{1,0:T(8,128)(2,1)S(1)} %shard_map.72.refs_0_), channel_id=1, source_target_pairs={{0,1},{1,0},{2,3},{3,2},{4,5},{5,4},{6,7},{7,6},{8,9},{9,8},{10,11... | collective-permute-start | bytes 786440 | tf_op jit(solution)/shard_map/ppermute | solution.py:300
  168.1 19.0 %collective-permute-start.31 = (bf16[1,128,1024]{2,1,0:T(8,128)(2,1)S(1)}, bf16[1,128,1024]{2,1,0:T(8,128)(2,1)S(1)}, u32[]{:S(2)}, u32[]{:S(2)}) collective-permute-start(bf16[1,128,1024]{2,1,0:T(8,128)(2,1)S(1)} %add_convert_fusion.2), channel_id=1, source_target_pairs={{0,2},{1,3},{2,0},{3,1},{4,6},{5,7},{6,4},{7,5},{8,10},{9,11},{10,... | collective-permute-start | bytes 786440 | tf_op jit(solution)/shard_map/ppermute | solution.py:300
  178.2 13.9 %collective-permute-start.26 = (bf16[128,1024]{1,0:T(8,128)(2,1)S(1)}, bf16[128,1024]{1,0:T(8,128)(2,1)S(1)}, u32[]{:S(2)}, u32[]{:S(2)}) collective-permute-start(bf16[128,1024]{1,0:T(8,128)(2,1)S(1)} %shard_map.72.refs_0_), channel_id=1, source_target_pairs={{0,2},{1,3},{2,0},{3,1},{4,6},{5,7},{6,4},{7,5},{8,10},{9,11},{10,... | collective-permute-start | bytes 786440 | tf_op jit(solution)/shard_map/ppermute | solution.py:300
  193.2 13.7 %collective-permute-start.32 = (bf16[3,4,224,512]{3,2,1,0:T(8,128)(2,1)S(1)}, bf16[3,4,224,512]{3,2,1,0:T(8,128)(2,1)S(1)}, u32[]{:S(2)}, u32[]{:S(2)}) collective-permute-start(bf16[3,4,224,512]{3,2,1,0:T(8,128)(2,1)S(1)} %shard_map.74), channel_id=1, source_target_pairs={{0,4},{4,0},{8,12},{12,8},{16,20},{20,16},{24,28},{28,24},{1,5},{5... | collective-permute-start | bytes 8257544 | tf_op jit(solution)/shard_map/ppermute | solution.py:297
  193.3 13.6 %collective-permute-start.27 = (bf16[128,1024]{1,0:T(8,128)(2,1)S(1)}, bf16[128,1024]{1,0:T(8,128)(2,1)S(1)}, u32[]{:S(2)}, u32[]{:S(2)}) collective-permute-start(bf16[128,1024]{1,0:T(8,128)(2,1)S(1)} %collective-permute-done.26.refs_2_), channel_id=1, source_target_pairs={{0,1},{1,0},{2,3},{3,2},{4,5},{5,4},{6,7},{7,6},{8,9},{9,8},{10,11... | collective-permute-start | bytes 786440 | tf_op jit(solution)/shard_map/ppermute | solution.py:300
  193.3 19.2 %collective-permute-start.39 = (bf16[128,1024]{1,0:T(8,128)(2,1)S(1)}, bf16[128,1024]{1,0:T(8,128)(2,1)}, u32[]{:S(2)}, u32[]{:S(2)}) collective-permute-start(bf16[128,1024]{1,0:T(8,128)(2,1)S(1)} %shard_map.73.refs_0_), channel_id=1, source_target_pairs={{0,2},{1,3},{2,0},{3,1},{4,6},{5,7},{6,4},{7,5},{8,10},{9,11},{10,... | collective-permute-start | bytes 786440 | tf_op jit(solution)/shard_map/ppermute | solution.py:300
  212.6 9.3 %collective-permute-start.40 = (bf16[128,1024]{1,0:T(8,128)(2,1)S(1)}, bf16[128,1024]{1,0:T(8,128)(2,1)}, u32[]{:S(2)}, u32[]{:S(2)}) collective-permute-start(bf16[128,1024]{1,0:T(8,128)(2,1)S(1)} %shard_map.73.refs_0_), channel_id=1, source_target_pairs={{0,1},{1,0},{2,3},{3,2},{4,5},{5,4},{6,7},{7,6},{8,9},{9,8},{10,11... | collective-permute-start | bytes 786440 | tf_op jit(solution)/shard_map/ppermute | solution.py:300
  212.6 13.7 %collective-permute-start.41 = (bf16[128,1024]{1,0:T(8,128)(2,1)}, bf16[128,1024]{1,0:T(8,128)(2,1)}, u32[]{:S(2)}, u32[]{:S(2)}) collective-permute-start(bf16[128,1024]{1,0:T(8,128)(2,1)} %collective-permute-done.39.refs_2_), channel_id=1, source_target_pairs={{0,1},{1,0},{2,3},{3,2},{4,5},{5,4},{6,7},{7,6},{8,9},{9,8},{10,11... | collective-permute-start | bytes 786440 | tf_op jit(solution)/shard_map/ppermute | solution.py:300
  214.6 19.6 %collective-permute-start.33 = (bf16[128,1792]{1,0:T(8,128)(2,1)}, bf16[128,1792]{1,0:T(8,128)(2,1)}, u32[]{:S(2)}, u32[]{:S(2)}) collective-permute-start(bf16[128,1792]{1,0:T(8,128)(2,1)} %get-tuple-element.157), channel_id=1, source_target_pairs={{0,8},{4,12},{8,0},{12,4},{16,24},{20,28},{24,16},{28,20},{1,9},{5... | collective-permute-start | bytes 1376264 | tf_op jit(solution)/shard_map/ppermute | solution.py:294
  216.6 21.4 %collective-permute-start.34 = (bf16[128,1792]{1,0:T(8,128)(2,1)}, bf16[128,1792]{1,0:T(8,128)(2,1)}, u32[]{:S(2)}, u32[]{:S(2)}) collective-permute-start(bf16[128,1792]{1,0:T(8,128)(2,1)} %get-tuple-element.158), channel_id=1, source_target_pairs={{0,16},{4,20},{8,24},{12,28},{16,0},{20,4},{24,8},{28,12},{1,17},{... | collective-permute-start | bytes 1376264 | tf_op jit(solution)/shard_map/ppermute | solution.py:294
  217.4 20.5 %collective-permute-start.35 = (bf16[128,1792]{1,0:T(8,128)(2,1)}, bf16[128,1792]{1,0:T(8,128)(2,1)}, u32[]{:S(2)}, u32[]{:S(2)}) collective-permute-start(bf16[128,1792]{1,0:T(8,128)(2,1)} %get-tuple-element.159), channel_id=1, source_target_pairs={{0,24},{4,28},{8,16},{12,20},{16,8},{20,12},{24,0},{28,4},{1,25},{... | collective-permute-start | bytes 1376264 | tf_op jit(solution)/shard_map/ppermute | solution.py:294
  238.0 13.5 %collective-permute-start.42 = (bf16[128,1792]{1,0:T(8,128)(2,1)S(1)}, bf16[128,1792]{1,0:T(8,128)(2,1)S(1)}, u32[]{:S(2)}, u32[]{:S(2)}) collective-permute-start(bf16[128,1792]{1,0:T(8,128)(2,1)S(1)} %get-tuple-element.167), channel_id=1, source_target_pairs={{0,8},{4,12},{8,0},{12,4},{16,24},{20,28},{24,16},{28,20},{1,9},{5... | collective-permute-start | bytes 1376264 | tf_op jit(solution)/shard_map/ppermute | solution.py:294
  238.7 20.3 %collective-permute-start.43 = (bf16[128,1792]{1,0:T(8,128)(2,1)S(1)}, bf16[128,1792]{1,0:T(8,128)(2,1)S(1)}, u32[]{:S(2)}, u32[]{:S(2)}) collective-permute-start(bf16[128,1792]{1,0:T(8,128)(2,1)S(1)} %get-tuple-element.168), channel_id=1, source_target_pairs={{0,16},{4,20},{8,24},{12,28},{16,0},{20,4},{24,8},{28,12},{1,17},{... | collective-permute-start | bytes 1376264 | tf_op jit(solution)/shard_map/ppermute | solution.py:294
  240.0 19.0 %collective-permute-start.44 = (bf16[128,1792]{1,0:T(8,128)(2,1)S(1)}, bf16[128,1792]{1,0:T(8,128)(2,1)S(1)}, u32[]{:S(2)}, u32[]{:S(2)}) collective-permute-start(bf16[128,1792]{1,0:T(8,128)(2,1)S(1)} %get-tuple-element.169), channel_id=1, source_target_pairs={{0,24},{4,28},{8,16},{12,20},{16,8},{20,12},{24,0},{28,4},{1,25},{... | collective-permute-start | bytes 1376264 | tf_op jit(solution)/shard_map/ppermute | solution.py:294
  243.0 18.8 %collective-permute-start.36 = (bf16[32,1792]{1,0:T(8,128)(2,1)S(1)}, bf16[32,1792]{1,0:T(8,128)(2,1)S(1)}, u32[]{:S(2)}, u32[]{:S(2)}) collective-permute-start(bf16[32,1792]{1,0:T(8,128)(2,1)S(1)} %get-tuple-element.185), channel_id=1, source_target_pairs={{0,1},{1,0},{2,3},{3,2},{4,5},{5,4},{6,7},{7,6},{8,9},{9,8},{10,11... | collective-permute-start | bytes 344072 | tf_op jit(solution)/shard_map/ppermute | solution.py:300
  243.5 20.2 %collective-permute-start.37 = (bf16[32,1792]{1,0:T(8,128)(2,1)S(1)}, bf16[32,1792]{1,0:T(8,128)(2,1)S(1)}, u32[]{:S(2)}, u32[]{:S(2)}) collective-permute-start(bf16[32,1792]{1,0:T(8,128)(2,1)S(1)} %get-tuple-element.184), channel_id=1, source_target_pairs={{0,2},{1,3},{2,0},{3,1},{4,6},{5,7},{6,4},{7,5},{8,10},{9,11},{10,... | collective-permute-start | bytes 344072 | tf_op jit(solution)/shard_map/ppermute | solution.py:300
  251.4 12.3 %collective-permute-start.38 = (bf16[32,1792]{1,0:T(8,128)(2,1)S(1)}, bf16[32,1792]{1,0:T(8,128)(2,1)S(1)}, u32[]{:S(2)}, u32[]{:S(2)}) collective-permute-start(bf16[32,1792]{1,0:T(8,128)(2,1)S(1)} %get-tuple-element.183), channel_id=1, source_target_pairs={{0,3},{1,2},{2,1},{3,0},{4,7},{5,6},{6,5},{7,4},{8,11},{9,10},{10,... | collective-permute-start | bytes 344072 | tf_op jit(solution)/shard_map/ppermute | solution.py:300
  259.2 4.9 %collective-permute-start.45 = (bf16[32,1792]{1,0:T(8,128)(2,1)S(1)}, bf16[32,1792]{1,0:T(8,128)(2,1)S(1)}, u32[]{:S(2)}, u32[]{:S(2)}) collective-permute-start(bf16[32,1792]{1,0:T(8,128)(2,1)S(1)} %get-tuple-element.181), channel_id=1, source_target_pairs={{0,1},{1,0},{2,3},{3,2},{4,5},{5,4},{6,7},{7,6},{8,9},{9,8},{10,11... | collective-permute-start | bytes 344072 | tf_op jit(solution)/shard_map/ppermute | solution.py:300
  259.9 6.9 %collective-permute-start.46 = (bf16[32,1792]{1,0:T(8,128)(2,1)S(1)}, bf16[32,1792]{1,0:T(8,128)(2,1)S(1)}, u32[]{:S(2)}, u32[]{:S(2)}) collective-permute-start(bf16[32,1792]{1,0:T(8,128)(2,1)S(1)} %get-tuple-element.180), channel_id=1, source_target_pairs={{0,2},{1,3},{2,0},{3,1},{4,6},{5,7},{6,4},{7,5},{8,10},{9,11},{10,... | collective-permute-start | bytes 344072 | tf_op jit(solution)/shard_map/ppermute | solution.py:300
  261.8 6.7 %collective-permute-start.47 = (bf16[32,1792]{1,0:T(8,128)(2,1)S(1)}, bf16[32,1792]{1,0:T(8,128)(2,1)S(1)}, u32[]{:S(2)}, u32[]{:S(2)}) collective-permute-start(bf16[32,1792]{1,0:T(8,128)(2,1)S(1)} %get-tuple-element.179), channel_id=1, source_target_pairs={{0,3},{1,2},{2,1},{3,0},{4,7},{5,6},{6,5},{7,4},{8,11},{9,10},{10,... | collective-permute-start | bytes 344072 | tf_op jit(solution)/shard_map/ppermute | solution.py:300
  (14 other events, 261.3 us)
